TPU v7x, 32 devices: a whole 2x2x4 slice. The times are simulated.
32 devices in a mesh: dp: 2 (over core), expert: 16 (over z, y, x).
Axes of the slice: x: 2, y: 2, z: 4, core: 2. Of those that a mesh axis runs over, the one named last changes fastest.
Arguments:
- tokens: bfloat16 [4096, 2048], P(('dp', 'expert')), parts along dimension 0, may hold values from -6 to 6
- cotangent: bfloat16 [4096, 2048], P(('dp', 'expert')), parts along dimension 0, may hold values from -6 to 6
- expert_ids: int32 [4096, 10], P(('dp', 'expert')), parts along dimension 0, may hold values from 0 to 31, all different within a row; in each aligned block of 128 rows (0 to 127, 128 to 255, ...) at most 48 rows name the same one
- probs: float32 [4096, 10], P(('dp', 'expert')), parts along dimension 0, may hold values from 0.05 to 0.5
- gate_weight: bfloat16 [64, 2048, 256], P(('dp', 'expert')), parts along dimension 0, may hold values from -0.125 to 0.125
- up_weight: bfloat16 [64, 2048, 256], P(('dp', 'expert')), parts along dimension 0, may hold values from -0.125 to 0.125
- down_weight: bfloat16 [64, 256, 2048], P(('dp', 'expert')), parts along dimension 0, may hold values from -0.375 to 0.375
Outputs:
- mixed: float32 [4096, 2048], P(('dp', 'expert')), parts along dimension 0
- input_grad: float32 [4096, 2048], P(('dp', 'expert')), parts along dimension 0
There are 2 independent parts, one for each index of `dp`. A program takes and returns all parts, laid end to end along the dimension named above; each array names one. Nothing has to cross between parts.
Inputs may be any that keep to these rules, and one draw needn't show every extreme that they name: `expert_ids`: each row names 10 different experts. Within the 128 rows of one device no expert is named by more than 48 rows, and in some of these blocks one expert is named by exactly 48 rows; loads across experts are skewed.
All inputs are finite; a program needn't handle non-finite values.
Results may differ from a plain program's by a relative error of at most 0.0041.
Values may be sent and summed in bfloat16 or wider, within the bound.
No kernel may reach another device: no remote copies, remote signals or barrier semaphores. Data moves between devices by JAX's collectives and lax.ppermute only.
A program may use at most 128 MiB of HBM per device.

v0:
```python
import jax
import jax.numpy as jnp
from jax import lax
from jax.sharding import PartitionSpec as P


def route_slots(expert_ids, local_count, device_count, capacity):
    experts = local_count * device_count
    row_count = expert_ids.shape[0] * expert_ids.shape[1]
    flat_ids = expert_ids.reshape(row_count)
    sort_order = jnp.argsort(flat_ids, stable=True)
    labels = lax.broadcasted_iota(jnp.int32, (1, experts), 1)
    counts = jnp.sum((flat_ids[:, None] == labels).astype(jnp.int32), axis=0)
    starts = jnp.cumsum(counts) - counts
    sorted_ids = flat_ids[sort_order]
    rank_within = jnp.arange(row_count, dtype=jnp.int32) - starts[sorted_ids]
    owner = sorted_ids // local_count
    local_slot = sorted_ids % local_count
    target = local_slot * (device_count * capacity) + owner * capacity + rank_within
    source_of = jnp.full((experts * capacity,), row_count, jnp.int32).at[target].set(sort_order)
    target_of = jnp.zeros((row_count,), jnp.int32).at[sort_order].set(target)
    return (source_of, target_of)


def pack_rows(values, source_of, top_count, local_count):
    token_count = values.shape[0]
    with_zero = jnp.concatenate([values, jnp.zeros((1, values.shape[1]), values.dtype)], axis=0)
    token_index = jnp.minimum(source_of // top_count, token_count)
    picked = with_zero[token_index]
    return picked.reshape(local_count, -1, values.shape[1])


def forward_part(received, gate_weight, up_weight, down_weight):
    gate_pre = jnp.einsum("erd,edh->erh", received, gate_weight, preferred_element_type=jnp.float32)
    up_pre = jnp.einsum("erd,edh->erh", received, up_weight, preferred_element_type=jnp.float32)
    sigmoid_gate = jax.nn.sigmoid(gate_pre)
    activ = (gate_pre * sigmoid_gate * up_pre).astype(jnp.bfloat16)
    expert_out = jnp.einsum("erh,ehd->erd", activ, down_weight, preferred_element_type=jnp.float32)
    return (expert_out.astype(jnp.bfloat16), gate_pre, up_pre, sigmoid_gate)


def backward_part(grad_rows, gate_pre, up_pre, sigmoid_gate, gate_weight, up_weight, down_weight):
    grad_act = jnp.einsum(
        "erd,ehd->erh", grad_rows, down_weight, preferred_element_type=jnp.float32
    )
    grad_gate = (grad_act * up_pre * sigmoid_gate * (1.0 + gate_pre * (1.0 - sigmoid_gate))).astype(
        jnp.bfloat16
    )
    grad_up = (grad_act * gate_pre * sigmoid_gate).astype(jnp.bfloat16)
    joined_grad = jnp.concatenate([grad_gate, grad_up], axis=2)
    joined_weight = jnp.concatenate([gate_weight, up_weight], axis=2)
    expert_back = jnp.einsum(
        "erh,edh->erd", joined_grad, joined_weight, preferred_element_type=jnp.float32
    )
    return expert_back.astype(jnp.bfloat16)


def combine_rows(returned, target_of, probs):
    token_count, top_count = probs.shape
    flat_back = returned.reshape(-1, returned.shape[2])
    picked = flat_back[target_of].reshape(token_count, top_count, returned.shape[2])
    return jnp.sum(picked.astype(jnp.float32) * probs[:, :, None], axis=1)


def on_device(tokens, cotangent, expert_ids, probs, gate_weight, up_weight, down_weight):
    local_count = gate_weight.shape[0]
    device_count = lax.axis_size("expert")
    experts = local_count * device_count
    token_count, top_count = expert_ids.shape
    row_count = token_count * top_count
    capacity = row_count * 6 // (5 * experts)
    source_of, target_of = route_slots(expert_ids, local_count, device_count, capacity)
    send_rows = pack_rows(tokens, source_of, top_count, local_count)
    send_grads = pack_rows(cotangent, source_of, top_count, local_count)
    received = lax.all_to_all(send_rows, "expert", split_axis=1, concat_axis=1, tiled=True)
    expert_out, gate_pre, up_pre, sigmoid_gate = forward_part(
        received, gate_weight, up_weight, down_weight
    )
    returned_out = lax.all_to_all(expert_out, "expert", split_axis=1, concat_axis=1, tiled=True)
    received_grads = lax.all_to_all(send_grads, "expert", split_axis=1, concat_axis=1, tiled=True)
    expert_back = backward_part(
        received_grads, gate_pre, up_pre, sigmoid_gate, gate_weight, up_weight, down_weight
    )
    returned_back = lax.all_to_all(expert_back, "expert", split_axis=1, concat_axis=1, tiled=True)
    mixed = combine_rows(returned_out, target_of, probs)
    input_grad = combine_rows(returned_back, target_of, probs)
    return (mixed, input_grad)


def solution(mesh):
    in_specs = (
        P(("dp", "expert"), None),
        P(("dp", "expert"), None),
        P(("dp", "expert"), None),
        P(("dp", "expert"), None),
        P(("dp", "expert"), None, None),
        P(("dp", "expert"), None, None),
        P(("dp", "expert"), None, None),
    )
    out_specs = (P(("dp", "expert"), None), P(("dp", "expert"), None))
    return jax.shard_map(
        on_device, mesh=mesh, in_specs=in_specs, out_specs=out_specs, check_vma=False
    )
```

profile of v0, /device:TPU:14, one launch (start us, length us, event | category | flops | bytes accessed | tf_op | source)
XLA Modules:
  0.0 729.2 jit_solution(1461152085628898170)
XLA Ops:
  0.6 0.0 copy-start
  0.6 0.9 copy.38
  1.6 0.1 reshape.163
  1.7 0.1 convert_reduce_fusion
  1.9 0.1 copy.39
  2.0 0.1 reduce-window.9
  2.0 0.1 reduce.1
  2.1 0.7 fusion.35
  2.9 0.7 fusion.34
  3.6 5.0 sort.17
  8.6 0.0 copy-start.2
  8.7 7.1 gather_fusion
  15.7 4.4 fusion.23
  20.2 0.4 compare_reduce_fusion.24
  20.5 15.7 %fusion.16 = (s32[1280]{0:T(1024)S(1)}, s32[1280]{0:T(1024)S(1)}) fusion(s32[1280]{0:T(1024)S(1)} %gather_fusion, pred[1280]{0:T(1024)(128)(4,1)S(1)} %get-tuple-element.30, pred[1280]{0:T(1024)(128)(4,1)S(1)} %get-tuple-element.29, pred[1280]{0:T(1024)(128)(4,1)S(1)} %get-tuple-element.28, pred[1280]{0:T(1024)(128)(4,1)S(1)} %get-tuple-element.27, ...), kind=kLoop, calls=%fused_computation.80 | loop fusion | flops 62720 | bytes 52580 | tf_op jit(solution)/shard_map/add | solution.py:19
  36.3 0.1 fusion.24
  36.3 5.2 scatter_custom_fusion
  41.6 0.0 copy-done.2
  41.7 7.1 gather_fusion.1
  48.8 12.6 %copy.40 = bf16[2,768,2048]{2,0,1:T(2,128)(2,1)} copy(bf16[2,768,2048]{2,1,0:T(8,128)(2,1)} %bitcast.44) | data formatting | bytes 12582912 | tf_op jit(solution)/shard_map/reshape | solution.py:30
  61.4 0.0 copy-start.3
  61.4 7.3 all-to-all-start
  68.7 0.0 copy-done.3
  68.7 7.0 gather_fusion.3
  75.8 12.6 %copy.49 = bf16[2,768,2048]{2,0,1:T(2,128)(2,1)} copy(bf16[2,768,2048]{2,1,0:T(8,128)(2,1)} %bitcast.43) | data formatting | bytes 12582912 | tf_op jit(solution)/shard_map/reshape | solution.py:30
  88.4 122.0 %all-to-all-done = bf16[2,768,2048]{2,0,1:T(2,128)(2,1)} async-done(((bf16[2,768,2048]{2,0,1:T(2,128)(2,1)}), bf16[2,768,2048]{2,0,1:T(2,128)(2,1)}, u32[]{:S(2)}, u32[]{:S(2)}) %all-to-all-start) | async-done | bytes 6291488 | tf_op jit(solution)/shard_map/all_to_all | solution.py:75
  210.4 6.8 all-to-all-start.2
  217.2 6.9 fusion.2
  224.2 131.4 %all-to-all-done.2 = bf16[2,768,2048]{2,0,1:T(2,128)(2,1)} async-done(((bf16[2,768,2048]{2,0,1:T(2,128)(2,1)}), bf16[2,768,2048]{2,0,1:T(2,128)(2,1)}, u32[]{:S(2)}, u32[]{:S(2)}) %all-to-all-start.2) | async-done | bytes 6291488 | tf_op jit(solution)/shard_map/all_to_all | solution.py:80
  355.6 0.0 copy-done
  355.6 0.0 copy-start.6
  355.6 0.0 copy-start.7
  355.6 7.2 fusion
  362.8 0.0 copy-done.6
  362.8 0.0 copy-done.7
  362.8 6.7 multiply_convert_fusion.1
  369.5 2.0 convolution_convert_fusion.1
  371.5 19.0 %copy.46 = bf16[2,768,2048]{2,0,1:T(2,128)(2,1)} copy(bf16[2,768,2048]{2,1,0:T(8,128)(2,1)S(1)} %convolution_convert_fusion.1) | data formatting | bytes 12582912 | tf_op jit(solution)/shard_map/convert_element_type | solution.py:39
  390.5 0.0 copy-start.5
  390.5 5.4 all-to-all-start.1
  395.9 0.0 copy-done.5
  395.9 5.5 convolution_convert_fusion
  401.4 18.8 %copy.52 = bf16[2,768,2048]{2,0,1:T(2,128)(2,1)} copy(bf16[2,768,2048]{2,1,0:T(8,128)(2,1)S(1)} %convolution_convert_fusion) | data formatting | bytes 12582912 | tf_op jit(solution)/shard_map/convert_element_type | solution.py:55
  420.2 0.0 copy-start.4
  420.2 115.2 %all-to-all-done.1 = bf16[2,768,2048]{2,0,1:T(2,128)(2,1)} async-done(((bf16[2,768,2048]{2,0,1:T(2,128)(2,1)}), bf16[2,768,2048]{2,0,1:T(2,128)(2,1)}, u32[]{:S(2)}, u32[]{:S(2)}) %all-to-all-start.1) | async-done | bytes 6291488 | tf_op jit(solution)/shard_map/all_to_all | solution.py:79
  535.4 5.1 all-to-all-start.3
  540.5 5.2 scatter_custom_fusion.1
  545.8 0.0 copy-done.4
  545.8 0.1 copy.48
  545.9 8.3 %copy.47 = bf16[2,768,2048]{2,1,0:T(8,128)(2,1)} copy(bf16[2,768,2048]{2,0,1:T(2,128)(2,1)} %all-to-all-done.1) | data formatting | bytes 12582912 | tf_op jit(solution)/shard_map/all_to_all | solution.py:79
  554.3 14.7 %gather_fusion.2 = bf16[1280,2048]{1,0:T(8,128)(2,1)} fusion(bf16[1536,2048]{1,0:T(8,128)(2,1)} %bitcast.42, s32[2048]{0:T(1024)S(1)} %pad_clamp_fusion), kind=kCustom, calls=%fused_computation.2 | custom fusion | bytes 10490880 | tf_op jit(solution)/shard_map/gather | solution.py:61
  568.9 10.4 %reshape.170 = f32[128,10,2048]{2,1,0:T(8,128)} reshape(bf16[1280,2048]{1,0:T(8,128)(2,1)} %gather_fusion.2) | data formatting | bytes 15728640 | tf_op jit(solution)/shard_map/convert_element_type | solution.py:62
  579.3 101.1 %all-to-all-done.3 = bf16[2,768,2048]{2,0,1:T(2,128)(2,1)} async-done(((bf16[2,768,2048]{2,0,1:T(2,128)(2,1)}), bf16[2,768,2048]{2,0,1:T(2,128)(2,1)}, u32[]{:S(2)}, u32[]{:S(2)}) %all-to-all-start.3) | async-done | bytes 6291488 | tf_op jit(solution)/shard_map/all_to_all | solution.py:84
  680.4 8.3 %copy.53 = bf16[2,768,2048]{2,1,0:T(8,128)(2,1)} copy(bf16[2,768,2048]{2,0,1:T(2,128)(2,1)} %all-to-all-done.3) | data formatting | bytes 12582912 | tf_op jit(solution)/shard_map/all_to_all | solution.py:84
  688.8 14.4 %gather_fusion.4 = bf16[1280,2048]{1,0:T(8,128)(2,1)} fusion(bf16[1536,2048]{1,0:T(8,128)(2,1)} %bitcast.41, s32[2048]{0:T(1024)S(1)} %pad_clamp_fusion), kind=kCustom, calls=%fused_computation.4 | custom fusion | bytes 10490880 | tf_op jit(solution)/shard_map/gather | solution.py:61
  703.2 10.4 %reshape.171 = f32[128,10,2048]{2,1,0:T(8,128)} reshape(bf16[1280,2048]{1,0:T(8,128)(2,1)} %gather_fusion.4) | data formatting | bytes 15728640 | tf_op jit(solution)/shard_map/convert_element_type | solution.py:62
  713.6 0.0 copy-start.1
  713.6 15.2 %multiply_reduce_fusion = (f32[128,2048]{1,0:T(8,128)}, f32[128,2048]{1,0:T(8,128)}) fusion(f32[128,10,2048]{2,1,0:T(8,128)} %reshape.171, f32[128,10]{1,0:T(8,128)S(1)} %copy.48, f32[128,10,2048]{2,1,0:T(8,128)} %reshape.170), kind=kLoop, calls=%fused_computation.7 | loop fusion | flops 9961472 | bytes 23073792 | tf_op jit(solution)/shard_map/reduce_sum | solution.py:62
  728.8 0.0 copy-done.1
  (10 shorter events, 0.2 us)
Async XLA Ops:
  0.6 354.9 %copy-start = (bf16[2,256,2048]{2,1,0:T(8,128)(2,1)S(1)}, bf16[2,256,2048]{2,1,0:T(8,128)(2,1)}, u32[]{:S(2)}) copy-start(bf16[2,256,2048]{2,1,0:T(8,128)(2,1)} %param.13) | copy-start | bytes 6291460
  8.6 33.0 %copy-start.2 = (bf16[128,2048]{1,0:T(8,128)(2,1)S(1)}, bf16[128,2048]{1,0:T(8,128)(2,1)}, u32[]{:S(2)}) copy-start(bf16[128,2048]{1,0:T(8,128)(2,1)} %param.7) | copy-start | bytes 1572868
  61.4 7.3 copy-start.3
  61.4 149.0 %all-to-all-start = ((bf16[2,768,2048]{2,0,1:T(2,128)(2,1)}), bf16[2,768,2048]{2,0,1:T(2,128)(2,1)}, u32[]{:S(2)}, u32[]{:S(2)}) async-start(bf16[2,768,2048]{2,0,1:T(2,128)(2,1)} %copy.40), calls=%async_computation | async-start | bytes 12582912 | tf_op jit(solution)/shard_map/all_to_all | solution.py:75
  210.4 145.2 %all-to-all-start.2 = ((bf16[2,768,2048]{2,0,1:T(2,128)(2,1)}), bf16[2,768,2048]{2,0,1:T(2,128)(2,1)}, u32[]{:S(2)}, u32[]{:S(2)}) async-start(bf16[2,768,2048]{2,0,1:T(2,128)(2,1)} %copy.49), calls=%async_computation.2 | async-start | bytes 12582912 | tf_op jit(solution)/shard_map/all_to_all | solution.py:80
  355.6 7.2 copy-start.6
  355.6 7.2 copy-start.7
  390.5 5.4 copy-start.5
  390.5 144.9 %all-to-all-start.1 = ((bf16[2,768,2048]{2,0,1:T(2,128)(2,1)}), bf16[2,768,2048]{2,0,1:T(2,128)(2,1)}, u32[]{:S(2)}, u32[]{:S(2)}) async-start(bf16[2,768,2048]{2,0,1:T(2,128)(2,1)} %copy.46), calls=%async_computation.1 | async-start | bytes 12582912 | tf_op jit(solution)/shard_map/all_to_all | solution.py:79
  420.2 125.6 %copy-start.4 = (f32[128,10]{0,1:T(8,128)S(1)}, f32[128,10]{0,1:T(8,128)}, u32[]{:S(2)}) copy-start(f32[128,10]{0,1:T(8,128)} %param.10) | copy-start | bytes 15364
  535.4 145.0 %all-to-all-start.3 = ((bf16[2,768,2048]{2,0,1:T(2,128)(2,1)}), bf16[2,768,2048]{2,0,1:T(2,128)(2,1)}, u32[]{:S(2)}, u32[]{:S(2)}) async-start(bf16[2,768,2048]{2,0,1:T(2,128)(2,1)} %copy.52), calls=%async_computation.3 | async-start | bytes 12582912 | tf_op jit(solution)/shard_map/all_to_all | solution.py:84
  713.6 15.2 %copy-start.1 = (bf16[2,256,2048]{2,1,0:T(8,128)(2,1)S(1)}, bf16[2,256,2048]{2,1,0:T(8,128)(2,1)}, u32[]{:S(2)}) copy-start(bf16[2,256,2048]{2,1,0:T(8,128)(2,1)} %param.13) | copy-start | bytes 6291460
where the time goes:
time: 736 us; the launch traced here: 729 us
  waiting for transfers between devices  470 us (64%)
  local copies, waits for them, and re-layouts  164 us (22%)
  other arithmetic  41.1 us (6%)
  matrix products  28.4 us (4%)
  starting transfers between devices  24.6 us (3%)
    all_to_all x1, waiting for transfers between devices, on_device(): lax.all_to_all(send_grads, 'expert', split_axis=1, concat_axis=1, tiled=T...  131 us
    all_to_all x1, waiting for transfers between devices, on_device(): lax.all_to_all(send_rows, 'expert', split_axis=1, concat_axis=1, tiled=True)  122 us
    all_to_all x1, waiting for transfers between devices, on_device(): lax.all_to_all(expert_out, 'expert', split_axis=1, concat_axis=1, tiled=T...  115 us
    all_to_all x1, waiting for transfers between devices, on_device(): lax.all_to_all(expert_back, 'expert', split_axis=1, concat_axis=1, tiled=...  101 us
    gather x2, local copies, waits for them, and re-layouts, combine_rows(): flat_back[target_of].reshape(token_count, top_count, returned.shape[2])  29.1 us
    reshape x2, local copies, waits for them, and re-layouts, pack_rows(): return picked.reshape(local_count, -1, values.shape[1])  25.3 us
    convert_element_type x2, local copies, waits for them, and re-layouts, combine_rows(): return jnp.sum(picked.astype(jnp.float32) * probs[:, :, None], axis=1)  20.8 us
    convert_element_type x1, local copies, waits for them, and re-layouts, forward_part(): return (expert_out.astype(jnp.bfloat16), gate_pre, up_pre, sigmoid_gate)  19 us
  transfers between devices with their start and end apart: 4, of which 4 were waited for; matrix products, arithmetic and copies ran while one was open for 12% of the time, Pallas kernels for 0%

commit v1 on v0

--- a/solution.py
+++ b/solution.py
@@ -1,7 +1,170 @@
+import functools
+
 import jax
 import jax.numpy as jnp
 from jax import lax
+from jax.experimental import pallas as pl
+from jax.experimental.pallas import tpu as pltpu
 from jax.sharding import PartitionSpec as P
+
+VMEM_BYTES = 48 * 2**20
+
+
+def forward_kernel(first, *refs):
+    if first:
+        rows_ref, weight_ref, gate_ref, up_ref, down_ref, mixed_ref, by_gate_ref, by_up_ref = refs
+        mixed = None
+    else:
+        rows_ref, weight_ref, gate_ref, up_ref, down_ref, so_far_ref, mixed_ref, by_gate_ref, by_up_ref = refs
+        mixed = so_far_ref[...]
+    local_count, _, hidden = gate_ref.shape
+    rows = rows_ref[...]
+    for e in range(local_count):
+        cut = slice(e * hidden, (e + 1) * hidden)
+        gate_pre = jnp.dot(rows, gate_ref[e], preferred_element_type=jnp.float32)
+        up_pre = jnp.dot(rows, up_ref[e], preferred_element_type=jnp.float32)
+        sig = jax.nn.sigmoid(gate_pre)
+        silu = gate_pre * sig
+        activ = (silu * up_pre).astype(jnp.bfloat16)
+        by_gate_ref[:, cut] = up_pre * sig * (1.0 + gate_pre * (1.0 - sig))
+        by_up_ref[:, cut] = silu
+        out = jnp.dot(activ, down_ref[e], preferred_element_type=jnp.float32)
+        out = out.astype(jnp.bfloat16).astype(jnp.float32) * weight_ref[:, e : e + 1]
+        mixed = out if mixed is None else mixed + out
+    mixed_ref[...] = mixed.astype(mixed_ref.dtype)
+
+
+def backward_kernel(first, *refs):
+    if first:
+        grads_ref, weight_ref, by_gate_ref, by_up_ref, gate_ref, up_ref, down_ref, back_ref = refs
+        total = None
+    else:
+        grads_ref, weight_ref, by_gate_ref, by_up_ref, gate_ref, up_ref, down_ref, so_far_ref, back_ref = refs
+        total = so_far_ref[...]
+    local_count, _, hidden = gate_ref.shape
+    grads = grads_ref[...]
+    nt = (((1,), (1,)), ((), ()))
+    for e in range(local_count):
+        cut = slice(e * hidden, (e + 1) * hidden)
+        grad_act = lax.dot_general(grads, down_ref[e], nt, preferred_element_type=jnp.float32)
+        grad_gate = (grad_act * by_gate_ref[:, cut]).astype(jnp.bfloat16)
+        grad_up = (grad_act * by_up_ref[:, cut]).astype(jnp.bfloat16)
+        back = lax.dot_general(grad_gate, gate_ref[e], nt, preferred_element_type=jnp.float32)
+        back += lax.dot_general(grad_up, up_ref[e], nt, preferred_element_type=jnp.float32)
+        back = back.astype(jnp.bfloat16).astype(jnp.float32) * weight_ref[:, e : e + 1]
+        total = back if total is None else total + back
+    back_ref[...] = total.astype(back_ref.dtype)
+
+
+def row_tile(rows):
+    return 256 if rows % 256 == 0 else rows
+
+
+def whole(array):
+    return pl.BlockSpec(array.shape, lambda i: (0,) * array.ndim)
+
+
+def tiled(tile, columns):
+    return pl.BlockSpec((tile, columns), lambda i: (i, 0))
+
+
+def forward_dense(rows, weight, gate_weight, up_weight, down_weight, so_far=None):
+    count, width = rows.shape
+    experts, _, hidden = gate_weight.shape
+    tile = row_tile(count)
+    first = so_far is None
+    sum_type = jnp.float32 if first else jnp.bfloat16
+    return pl.pallas_call(
+        functools.partial(forward_kernel, first),
+        grid=(count // tile,),
+        in_specs=[
+            tiled(tile, width),
+            tiled(tile, experts),
+            whole(gate_weight),
+            whole(up_weight),
+            whole(down_weight),
+        ]
+        + ([] if first else [tiled(tile, width)]),
+        out_specs=[tiled(tile, width), tiled(tile, experts * hidden), tiled(tile, experts * hidden)],
+        out_shape=[
+            jax.ShapeDtypeStruct((count, width), sum_type),
+            jax.ShapeDtypeStruct((count, experts * hidden), jnp.float32),
+            jax.ShapeDtypeStruct((count, experts * hidden), jnp.float32),
+        ],
+        compiler_params=pltpu.CompilerParams(vmem_limit_bytes=VMEM_BYTES),
+        cost_estimate=pl.CostEstimate(
+            flops=6 * count * experts * width * hidden,
+            bytes_accessed=6 * count * width + 8 * count * experts * hidden + 6 * gate_weight.size,
+            transcendentals=count * experts * hidden,
+        ),
+        name="forward_dense",
+    )(rows, weight, gate_weight, up_weight, down_weight, *([] if first else [so_far]))
+
+
+def backward_dense(grads, weight, by_gate, by_up, gate_weight, up_weight, down_weight, so_far=None):
+    count, width = grads.shape
+    experts, _, hidden = gate_weight.shape
+    tile = row_tile(count)
+    first = so_far is None
+    sum_type = jnp.float32 if first else jnp.bfloat16
+    return pl.pallas_call(
+        functools.partial(backward_kernel, first),
+        grid=(count // tile,),
+        in_specs=[
+            tiled(tile, width),
+            tiled(tile, experts),
+            tiled(tile, experts * hidden),
+            tiled(tile, experts * hidden),
+            whole(gate_weight),
+            whole(up_weight),
+            whole(down_weight),
+        ]
+        + ([] if first else [tiled(tile, width)]),
+        out_specs=tiled(tile, width),
+        out_shape=jax.ShapeDtypeStruct((count, width), sum_type),
+        compiler_params=pltpu.CompilerParams(vmem_limit_bytes=VMEM_BYTES),
+        cost_estimate=pl.CostEstimate(
+            flops=6 * count * experts * width * hidden,
+            bytes_accessed=6 * count * width + 8 * count * experts * hidden + 6 * gate_weight.size,
+            transcendentals=0,
+        ),
+        name="backward_dense",
+    )(grads, weight, by_gate, by_up, gate_weight, up_weight, down_weight, *([] if first else [so_far]))
+
+
+def on_device_dense(tokens, cotangent, expert_ids, probs, gate_weight, up_weight, down_weight):
+    local_count = gate_weight.shape[0]
+    devices = lax.axis_size("expert")
+    experts = local_count * devices
+    teams = [list(range(side, devices, 2)) for side in range(2)]
+    pairs = [(d, d ^ 1) for d in range(devices)]
+    labels = lax.broadcasted_iota(jnp.int32, (1, 1, experts), 2)
+    weight = jnp.sum(jnp.where(expert_ids[:, :, None] == labels, probs[:, :, None], 0.0), axis=1)
+
+    def gather(values):
+        return lax.all_gather(values, "expert", axis_index_groups=teams, axis=0, tiled=True)
+
+    def reduce(values):
+        summed = lax.psum_scatter(
+            values, "expert", scatter_dimension=0, axis_index_groups=teams, tiled=True
+        )
+        return summed.astype(jnp.float32)
+
+    other = [lax.ppermute(w, "expert", pairs) for w in (gate_weight, up_weight, down_weight)]
+    all_rows = gather(tokens)
+    all_weight = gather(weight)
+    all_grads = gather(cotangent)
+    me = lax.axis_index("expert")
+    own_weight = lax.dynamic_slice_in_dim(all_weight, me * local_count, local_count, axis=1)
+    other_weight = lax.dynamic_slice_in_dim(all_weight, (me ^ 1) * local_count, local_count, axis=1)
+    own = (gate_weight, up_weight, down_weight)
+    mixed, by_gate, by_up = forward_dense(all_rows, own_weight, *own)
+    back = backward_dense(all_grads, own_weight, by_gate, by_up, *own)
+    mixed, by_gate, by_up = forward_dense(all_rows, other_weight, *other, so_far=mixed)
+    mixed = reduce(mixed)
+    back = backward_dense(all_grads, other_weight, by_gate, by_up, *other, so_far=back)
+    back = reduce(back)
+    return (mixed, back)
 
 
 def route_slots(expert_ids, local_count, device_count, capacity):
@@ -62,7 +225,7 @@
     return jnp.sum(picked.astype(jnp.float32) * probs[:, :, None], axis=1)
 
 
-def on_device(tokens, cotangent, expert_ids, probs, gate_weight, up_weight, down_weight):
+def on_device_routed(tokens, cotangent, expert_ids, probs, gate_weight, up_weight, down_weight):
     local_count = gate_weight.shape[0]
     device_count = lax.axis_size("expert")
     experts = local_count * device_count
@@ -87,6 +250,13 @@
     return (mixed, input_grad)
 
 
+def on_device(tokens, cotangent, expert_ids, probs, gate_weight, up_weight, down_weight):
+    devices = lax.axis_size("expert")
+    dense = devices % 2 == 0 and devices <= 2 * expert_ids.shape[1]
+    body = on_device_dense if dense else on_device_routed
+    return body(tokens, cotangent, expert_ids, probs, gate_weight, up_weight, down_weight)
+
+
 def solution(mesh):
     in_specs = (
         P(("dp", "expert"), None),

time: 736 us -> 354 us (0.48)
  the two profiles are of different devices: /device:TPU:14 before, /device:TPU:0 now
where the time goes in v1:
time: 354 us
  waiting for transfers between devices  234 us (66%)
  Pallas kernels  55.4 us (16%)
  blocking collectives  33.3 us (9%)
  between operations  13.8 us (4%)
  local copies, waits for them, and re-layouts  7.58 us (2%)
  starting transfers between devices  5.19 us (1%)
  other arithmetic  4.97 us (1%)
    reduce_scatter x2, waiting for transfers between devices, reduce(): lax.psum_scatter(values, 'expert', scatter_dimension=0, axis_index_groups...  147 us
    all_gather x2, waiting for transfers between devices, gather(): lax.all_gather(values, 'expert', axis_index_groups=teams, axis=0, tiled=T...  43.1 us
    ppermute x3, waiting for transfers between devices, on_device_dense(): lax.ppermute(w, 'expert', pairs)  42.1 us
    all_gather x1, blocking collectives, gather(): lax.all_gather(values, 'expert', axis_index_groups=teams, axis=0, tiled=T...  33.3 us
    pallas_call x2, Pallas kernels, backward_dense(): pl.pallas_call(functools.partial(backward_kernel, first), grid=(count //...  29.1 us
    pallas_call x2, Pallas kernels, forward_dense(): pl.pallas_call(functools.partial(forward_kernel, first), grid=(count // t...  26.3 us
    unnamed x12, local copies, waits for them, and re-layouts  7.14 us
  transfers between devices with their start and end apart: 7, of which 5 were waited for; matrix products, arithmetic and copies ran while one was open for 1% of the time, Pallas kernels for 16%

profile of v1, /device:TPU:0, one launch (start us, length us, event | category | flops | bytes accessed | tf_op | source)
XLA Modules:
  0.0 353.8 jit_solution(2132381781013986852)
XLA Ops:
  7.2 0.0 all-gather.3.cloned.1.call-start
  7.2 0.7 all-gather.3.cloned.1.call-update
  7.9 0.0 all-gather.5.cloned.1.call-start
  7.9 0.7 all-gather.5.cloned.1.call-update
  8.6 0.0 reduce-scatter.3.cloned.1.call-start
  8.7 3.0 collective-permute-start
  11.7 0.1 collective-permute-start.1
  11.8 1.9 collective-permute-start.2
  13.7 0.7 select_reduce_fusion
  14.5 0.1 copy.11
  14.6 33.3 %all_gather.10 = f32[1024,32]{1,0:T(8,128)S(1)} all-gather(f32[128,32]{1,0:T(8,128)S(1)} %copy.11), channel_id=1, replica_groups={{0,2,4,6,8,10,12,14},{1,3,5,7,9,11,13,15},{16,18,20,22,24,26,28,30},{17..., dimensions={0}, use_global_device_ids=true | all-gather | bytes 147456 | tf_op jit(solution)/shard_map/all_gather | solution.py:145
  47.9 0.3 constant_dynamic-slice_fusion
  48.2 41.7 %all-gather.3.cloned.1.call-done.refs_0_ = bf16[1024,2048]{1,0:T(8,128)(2,1)} async-done(((bf16[128,2048]{1,0:T(8,128)(2,1)}), bf16[1024,2048]{1,0:T(8,128)(2,1)}) %all-gather.3.cloned.1.call-update) | async-done | bytes 4194320 | tf_op jit(solution)/shard_map/all_gather | solution.py:145
  89.9 12.9 %forward_dense.2 = (f32[1024,2048]{1,0:T(8,128)}, f32[1024,512]{1,0:T(8,128)S(1)}, f32[1024,512]{1,0:T(8,128)S(1)}) custom-call(bf16[1024,2048]{1,0:T(8,128)(2,1)} %all-gather.3.cloned.1.call-done.refs_0_, f32[1024,2]{1,0:T(8,128)S(1)} %get-tuple-element.14.refs_1_, bf16[2,2048,256]{2,1,0:T(8,128)(2,1)} %refs_4_.3, bf16[2,2048,256]{2,1,0:T(8,128)(2,1)} %refs_5_.1, ...), custom_call_target="tpu_custom_call" | custom-call | flops 6442450944 | bytes 23068672 | tf_op jit(solution)/shard_map/forward_dense/pallas_call | solution.py:77
  102.8 0.0 copy-start.2
  102.8 1.3 copy-done.2
  104.1 0.0 copy-start.4
  104.1 1.3 copy-done.4
  105.4 0.0 collective-permute-done.refs_2_.refs_4_
  105.5 0.0 collective-permute-done.1.refs_3_.refs_5_
  105.5 42.1 %collective-permute-done.2.refs_4_.refs_6_ = bf16[2,256,2048]{2,1,0:T(8,128)(2,1)} collective-permute-done((bf16[2,256,2048]{2,1,0:T(8,128)(2,1)}, bf16[2,256,2048]{2,1,0:T(8,128)(2,1)}, u32[]{:S(2)}, u32[]{:S(2)}) %collective-permute-start.2) | collective-permute-done | bytes 2097184 | tf_op jit(solution)/shard_map/ppermute | solution.py:153
  147.5 13.4 %forward_dense.3 = (bf16[1024,2048]{1,0:T(8,128)(2,1)}, f32[1024,512]{1,0:T(8,128)S(1)}, f32[1024,512]{1,0:T(8,128)S(1)}) custom-call(bf16[1024,2048]{1,0:T(8,128)(2,1)} %all-gather.3.cloned.1.call-done.refs_0_, f32[1024,2]{1,0:T(8,128)S(1)} %get-tuple-element.15.refs_1_, bf16[2,2048,256]{2,1,0:T(8,128)(2,1)} %collective-permute-done.refs_2_.refs_4_, ...), custom_call_target="tpu_custom_call" | custom-call | flops 6442450944 | bytes 23068672 | tf_op jit(solution)/shard_map/forward_dense/pallas_call | solution.py:77
  161.0 0.0 copy-start
  161.0 1.3 copy-done
  162.3 0.0 reduce-scatter.3.cloned.1.call-update
  162.3 0.0 reduce-scatter.5.cloned.1.call-start
  162.3 1.4 all-gather.5.cloned.1.call-done.refs_0_
  163.7 0.0 copy-start.3
  163.7 1.6 copy-done.3
  165.3 0.0 copy-start.5
  165.3 1.6 copy-done.5
  166.9 0.0 copy-start.1
  166.9 14.4 %backward_dense.2.refs_7_ = f32[1024,2048]{1,0:T(8,128)} custom-call(bf16[1024,2048]{1,0:T(8,128)(2,1)} %all-gather.5.cloned.1.call-done.refs_0_, f32[1024,2]{1,0:T(8,128)S(1)} %get-tuple-element.14.refs_1_, f32[1024,512]{1,0:T(8,128)S(1)} %copy-done.3, f32[1024,512]{1,0:T(8,128)S(1)} %copy-done.5, bf16[2,2048,256]{2,1,0:T(8,128)(2,1)} %refs_4_.3, ...), custom_call_target="tpu_custom_call" | custom-call | flops 6442450944 | bytes 23068672 | tf_op jit(solution)/shard_map/backward_dense/pallas_call | solution.py:110
  181.3 0.0 copy-done.1
  181.3 14.7 %backward_dense.3 = bf16[1024,2048]{1,0:T(8,128)(2,1)} custom-call(bf16[1024,2048]{1,0:T(8,128)(2,1)} %all-gather.5.cloned.1.call-done.refs_0_, f32[1024,2]{1,0:T(8,128)S(1)} %get-tuple-element.15.refs_1_, f32[1024,512]{1,0:T(8,128)S(1)} %get-tuple-element.10.refs_2_, f32[1024,512]{1,0:T(8,128)S(1)} %copy-done.1, ...), custom_call_target="tpu_custom_call" | custom-call | flops 6442450944 | bytes 23068672 | tf_op jit(solution)/shard_map/backward_dense/pallas_call | solution.py:110
  196.0 0.0 reduce-scatter.5.cloned.1.call-update
  196.1 57.5 %reduce-scatter.3.cloned.1.call-done = bf16[128,2048]{1,0:T(8,128)(2,1)} async-done(((bf16[1024,2048]{1,0:T(8,128)(2,1)}), bf16[128,2048]{1,0:T(8,128)(2,1)}) %reduce-scatter.3.cloned.1.call-update) | async-done | bytes 524304 | tf_op jit(solution)/shard_map/reduce_scatter | solution.py:148
  253.6 2.1 convert_element_type.6
  255.7 89.5 %reduce-scatter.5.cloned.1.call-done = bf16[128,2048]{1,0:T(8,128)(2,1)} async-done(((bf16[1024,2048]{1,0:T(8,128)(2,1)}), bf16[128,2048]{1,0:T(8,128)(2,1)}) %reduce-scatter.5.cloned.1.call-update) | async-done | bytes 524304 | tf_op jit(solution)/shard_map/reduce_scatter | solution.py:148
  345.2 2.1 convert_element_type.7
Async XLA Ops:
  7.2 82.8 %all-gather.3.cloned.1.call-start = ((), (), s32[]{:S(2)}) async-start(), calls=%async_computation.2 | async-start | bytes 4718592 | tf_op jit(solution)/shard_map/all_gather | solution.py:145
  7.9 155.8 %all-gather.5.cloned.1.call-start = ((), (), s32[]{:S(2)}) async-start(), calls=%async_computation.4 | async-start | bytes 4718592 | tf_op jit(solution)/shard_map/all_gather | solution.py:145
  8.6 244.9 %reduce-scatter.3.cloned.1.call-start = ((), (), s32[]{:S(2)}) async-start(), calls=%async_computation.3 | async-start | bytes 4718592 | tf_op jit(solution)/shard_map/reduce_scatter | solution.py:148
  8.7 96.8 %collective-permute-start = (bf16[2,2048,256]{2,1,0:T(8,128)(2,1)}, bf16[2,2048,256]{2,1,0:T(8,128)(2,1)}, u32[]{:S(2)}, u32[]{:S(2)}) collective-permute-start(bf16[2,2048,256]{2,1,0:T(8,128)(2,1)} %refs_4_.3), channel_id=1, source_target_pairs={{0,1},{1,0},{2,3},{3,2},{4,5},{5,4},{6,7},{7,6},{8,9},{9,8},{10,11... | collective-permute-start | bytes 6291464 | tf_op jit(solution)/shard_map/ppermute | solution.py:153
  11.7 93.8 %collective-permute-start.1 = (bf16[2,2048,256]{2,1,0:T(8,128)(2,1)}, bf16[2,2048,256]{2,1,0:T(8,128)(2,1)}, u32[]{:S(2)}, u32[]{:S(2)}) collective-permute-start(bf16[2,2048,256]{2,1,0:T(8,128)(2,1)} %refs_5_.1), channel_id=1, source_target_pairs={{0,1},{1,0},{2,3},{3,2},{4,5},{5,4},{6,7},{7,6},{8,9},{9,8},{10,11... | collective-permute-start | bytes 6291464 | tf_op jit(solution)/shard_map/ppermute | solution.py:153
  11.8 135.7 %collective-permute-start.2 = (bf16[2,256,2048]{2,1,0:T(8,128)(2,1)}, bf16[2,256,2048]{2,1,0:T(8,128)(2,1)}, u32[]{:S(2)}, u32[]{:S(2)}) collective-permute-start(bf16[2,256,2048]{2,1,0:T(8,128)(2,1)} %refs_6_.1), channel_id=1, source_target_pairs={{0,1},{1,0},{2,3},{3,2},{4,5},{5,4},{6,7},{7,6},{8,9},{9,8},{10,11... | collective-permute-start | bytes 6291464 | tf_op jit(solution)/shard_map/ppermute | solution.py:153
  102.8 1.3 copy-start.2
  104.1 1.3 copy-start.4
  161.0 1.3 copy-start
  162.3 182.9 %reduce-scatter.5.cloned.1.call-start = ((), (), s32[]{:S(2)}) async-start(), calls=%async_computation.5 | async-start | bytes 4718592 | tf_op jit(solution)/shard_map/reduce_scatter | solution.py:148
  163.7 1.6 copy-start.3
  165.3 1.6 copy-start.5
  166.9 14.4 %copy-start.1 = (f32[1024,512]{1,0:T(8,128)S(1)}, f32[1024,512]{1,0:T(8,128)}, u32[]{:S(2)}) copy-start(f32[1024,512]{1,0:T(8,128)} %copy-done) | copy-start | bytes 6291460
Sparse Core Ops, SparseCore 0:
  10.1 79.7 all-gather.2
  92.0 71.6 all-gather.4
  167.4 86.1 reduce-scatter.2
  257.5 87.6 reduce-scatter.4

commit v2 on v0

--- a/solution.py
+++ b/solution.py
@@ -1,7 +1,244 @@
 import jax
 import jax.numpy as jnp
 from jax import lax
+from jax.experimental import pallas as pl
+from jax.experimental.pallas import tpu as pltpu
 from jax.sharding import PartitionSpec as P
+
+VMEM_BYTES = 48 * 2**20
+CHUNKS = 4
+
+
+def hidden_kernel(rows_ref, gate_ref, up_ref, activ_ref, by_gate_ref, by_up_ref):
+    experts, _, hidden = gate_ref.shape
+    rows = rows_ref[...]
+    for e in range(experts):
+        cut = slice(e * hidden, (e + 1) * hidden)
+        gate_pre = jnp.dot(rows, gate_ref[e], preferred_element_type=jnp.float32)
+        up_pre = jnp.dot(rows, up_ref[e], preferred_element_type=jnp.float32)
+        sig = jax.nn.sigmoid(gate_pre)
+        silu = gate_pre * sig
+        activ_ref[:, cut] = (silu * up_pre).astype(jnp.bfloat16)
+        by_gate_ref[:, cut] = up_pre * sig * (1.0 + gate_pre * (1.0 - sig))
+        by_up_ref[:, cut] = silu
+
+
+def split_store(total, keep_ref, send_ref):
+    @pl.when(pl.program_id(0) == 0)
+    def _():
+        send_ref[...] = total.astype(send_ref.dtype)
+
+    @pl.when(pl.program_id(0) == 1)
+    def _():
+        keep_ref[...] = total
+
+
+def mix_kernel(weight_ref, own_ref, other_ref, own_down_ref, other_down_ref, keep_ref, send_ref):
+    experts, hidden, _ = own_down_ref.shape
+    total = None
+    for side, (activ_ref, down_ref) in enumerate(((own_ref, own_down_ref), (other_ref, other_down_ref))):
+        for e in range(experts):
+            cut = slice(e * hidden, (e + 1) * hidden)
+            at = side * experts + e
+            out = jnp.dot(activ_ref[:, cut], down_ref[e], preferred_element_type=jnp.float32)
+            out = out.astype(jnp.bfloat16).astype(jnp.float32) * weight_ref[:, at : at + 1]
+            total = out if total is None else total + out
+    split_store(total, keep_ref, send_ref)
+
+
+def back_kernel(weight_ref, *refs):
+    keep_ref, send_ref = refs[-2:]
+    experts, _, hidden = refs[2].shape
+    nt = (((1,), (1,)), ((), ()))
+    total = None
+    for side in range(2):
+        by_gate_ref, by_up_ref, gate_ref, up_ref = refs[4 * side : 4 * side + 4]
+        for e in range(experts):
+            cut = slice(e * hidden, (e + 1) * hidden)
+            at = side * experts + e
+            back = lax.dot_general(by_gate_ref[:, cut], gate_ref[e], nt, preferred_element_type=jnp.float32)
+            back += lax.dot_general(by_up_ref[:, cut], up_ref[e], nt, preferred_element_type=jnp.float32)
+            back = back.astype(jnp.bfloat16).astype(jnp.float32) * weight_ref[:, at : at + 1]
+            total = back if total is None else total + back
+    split_store(total, keep_ref, send_ref)
+
+
+def hidden_forward(rows, gate_weight, up_weight):
+    count = rows.shape[0]
+    experts, width, hidden = gate_weight.shape
+    tile = 256 if count % 256 == 0 else count
+    columns = experts * hidden
+    weights = pl.BlockSpec((experts, width, hidden), lambda i: (0, 0, 0))
+    out = pl.BlockSpec((tile, columns), lambda i: (i, 0))
+    return pl.pallas_call(
+        hidden_kernel,
+        grid=(count // tile,),
+        in_specs=[pl.BlockSpec((tile, width), lambda i: (i, 0)), weights, weights],
+        out_specs=[out, out, out],
+        out_shape=[
+            jax.ShapeDtypeStruct((count, columns), jnp.bfloat16),
+            jax.ShapeDtypeStruct((count, columns), jnp.float32),
+            jax.ShapeDtypeStruct((count, columns), jnp.float32),
+        ],
+        compiler_params=pltpu.CompilerParams(vmem_limit_bytes=VMEM_BYTES),
+        cost_estimate=pl.CostEstimate(
+            flops=4 * count * width * columns,
+            bytes_accessed=2 * count * width + 10 * count * columns + 4 * gate_weight.size,
+            transcendentals=count * columns,
+        ),
+        name="hidden_forward",
+    )(rows, gate_weight, up_weight)
+
+
+def halves_call(kernel, name, count, columns, flops, in_specs, operands):
+    half = count // 2
+    return pl.pallas_call(
+        kernel,
+        grid=(2,),
+        in_specs=in_specs,
+        out_specs=[pl.BlockSpec((half, columns), lambda i: (0, 0))] * 2,
+        out_shape=[
+            jax.ShapeDtypeStruct((half, columns), jnp.float32),
+            jax.ShapeDtypeStruct((half, columns), jnp.bfloat16),
+        ],
+        compiler_params=pltpu.CompilerParams(vmem_limit_bytes=VMEM_BYTES),
+        cost_estimate=pl.CostEstimate(
+            flops=flops,
+            bytes_accessed=sum(2 * x.size for x in operands) // 2 + 6 * half * columns,
+            transcendentals=0,
+        ),
+        name=name,
+    )(*operands)
+
+
+def half_rows(array):
+    return pl.BlockSpec((array.shape[0] // 2, array.shape[1]), lambda i: (1 - i, 0))
+
+
+def mix_columns(weight, own, other, own_down, other_down, at):
+    experts, hidden, columns = other_down.shape
+    count = own.shape[0]
+    specs = [
+        half_rows(weight),
+        half_rows(own),
+        half_rows(other),
+        pl.BlockSpec((experts, hidden, columns), lambda i: (0, 0, at)),
+        pl.BlockSpec((experts, hidden, columns), lambda i: (0, 0, 0)),
+    ]
+    flops = 4 * count * experts * hidden * columns
+    return halves_call(
+        mix_kernel, "mix_columns", count, columns, flops, specs, (weight, own, other, own_down, other_down)
+    )
+
+
+def back_columns(weight, own, own_weights, other, other_weights, at, columns):
+    experts, _, hidden = own_weights[0].shape
+    count = weight.shape[0]
+    weights = pl.BlockSpec((experts, columns, hidden), lambda i: (0, at, 0))
+    specs = [half_rows(weight)]
+    for grads in (own, other):
+        specs += [half_rows(grads[0]), half_rows(grads[1]), weights, weights]
+    flops = 8 * count * experts * hidden * columns
+    return halves_call(
+        back_kernel,
+        "back_columns",
+        count,
+        columns,
+        flops,
+        specs,
+        (weight, *own, *own_weights, *other, *other_weights),
+    )
+
+
+def on_device_dense(tokens, cotangent, expert_ids, probs, gate_weight, up_weight, down_weight):
+    local_count, hidden, width = down_weight.shape
+    devices = lax.axis_size("expert")
+    layers = devices // 4
+    experts = local_count * devices
+    block = tokens.shape[0]
+    columns = width // CHUNKS
+    me = lax.axis_index("expert")
+
+    def after(values, *others):
+        return lax.optimization_barrier((values, *others))[0]
+
+    def to_twin(values):
+        return lax.ppermute(values, "expert", [(d, d ^ 1) for d in range(devices)])
+
+    def to_side(values):
+        return lax.ppermute(values, "expert", [(d, d ^ 2) for d in range(devices)])
+
+    def to_layer(values, step):
+        return lax.ppermute(values, "expert", [(d, (d + 4 * step) % devices) for d in range(devices)])
+
+    def gather(values):
+        near = [values] + [to_layer(values, -k) for k in range(1, layers)]
+        return near, jnp.concatenate(near + [to_side(v) for v in near], axis=0)
+
+    def reduce_start(keep, send):
+        come = to_side(send).astype(jnp.float32)
+        total = keep + come
+        own = total[:block]
+        return [own] + [
+            to_layer(total[k * block : (k + 1) * block].astype(jnp.bfloat16), k) for k in range(1, layers)
+        ]
+
+    def reduce_end(parts):
+        return jnp.concatenate([sum(p.astype(jnp.float32) for p in part) for part in parts], axis=1)
+
+    labels = lax.broadcasted_iota(jnp.int32, (1, 1, experts), 2)
+    weight = jnp.sum(jnp.where(expert_ids[:, :, None] == labels, probs[:, :, None], 0.0), axis=1)
+    first = lax.reduce_precision(weight, 8, 7)
+    second = lax.reduce_precision(weight - first, 8, 7)
+    third = weight - first - second
+    spare = jnp.zeros((block, -3 * experts % 128), jnp.bfloat16)
+    terms = [t.astype(jnp.bfloat16) for t in (first, second, third)]
+    rows = jnp.concatenate([tokens] + terms + [spare], axis=1)
+
+    near, all_rows = gather(rows)
+    other_gate = to_twin(gate_weight)
+    other_up = to_twin(up_weight)
+    other_down = []
+    for c in range(CHUNKS):
+        piece = down_weight[:, :, c * columns : (c + 1) * columns]
+        other_down.append(to_twin(after(piece, other_gate if 2 * c < CHUNKS else other_up)))
+    _, all_grads = gather(after(cotangent, near[layers // 2]))
+
+    terms = [
+        all_rows[:, width + t * experts : width + (t + 1) * experts].astype(jnp.float32) for t in range(3)
+    ]
+    all_weight = terms[0] + terms[1] + terms[2]
+    weight = jnp.concatenate(
+        [
+            lax.dynamic_slice_in_dim(all_weight, owner * local_count, local_count, axis=1)
+            for owner in (me, me ^ 1)
+        ],
+        axis=1,
+    )
+
+    def grad_act(grads, down):
+        flat = down.reshape(local_count * hidden, down.shape[2])
+        return lax.dot_general(grads, flat, (((1,), (1,)), ((), ())), preferred_element_type=jnp.float32)
+
+    activ, by_gate, by_up = hidden_forward(all_rows, gate_weight, up_weight)
+    other_activ, other_by_gate, other_by_up = hidden_forward(all_rows, other_gate, other_up)
+    grad = grad_act(all_grads, down_weight)
+    own_grads = [(grad * by).astype(jnp.bfloat16) for by in (by_gate, by_up)]
+    mixed = []
+    other_grad = None
+    for c in range(CHUNKS):
+        keep, send = mix_columns(weight, activ, other_activ, down_weight, other_down[c], c)
+        mixed.append(reduce_start(keep, send))
+        term = grad_act(all_grads[:, c * columns : (c + 1) * columns], other_down[c])
+        other_grad = term if other_grad is None else other_grad + term
+    other_grads = [(other_grad * by).astype(jnp.bfloat16) for by in (other_by_gate, other_by_up)]
+    back = []
+    for c in range(CHUNKS):
+        keep, send = back_columns(
+            weight, own_grads, (gate_weight, up_weight), other_grads, (other_gate, other_up), c, columns
+        )
+        back.append(reduce_start(keep, send))
+    return (reduce_end(mixed), reduce_end(back))
 
 
 def route_slots(expert_ids, local_count, device_count, capacity):
@@ -62,7 +299,7 @@
     return jnp.sum(picked.astype(jnp.float32) * probs[:, :, None], axis=1)
 
 
-def on_device(tokens, cotangent, expert_ids, probs, gate_weight, up_weight, down_weight):
+def on_device_routed(tokens, cotangent, expert_ids, probs, gate_weight, up_weight, down_weight):
     local_count = gate_weight.shape[0]
     device_count = lax.axis_size("expert")
     experts = local_count * device_count
@@ -87,6 +324,13 @@
     return (mixed, input_grad)
 
 
+def on_device(tokens, cotangent, expert_ids, probs, gate_weight, up_weight, down_weight):
+    devices = lax.axis_size("expert")
+    dense = devices % 4 == 0 and devices <= 2 * expert_ids.shape[1]
+    body = on_device_dense if dense else on_device_routed
+    return body(tokens, cotangent, expert_ids, probs, gate_weight, up_weight, down_weight)
+
+
 def solution(mesh):
     in_specs = (
         P(("dp", "expert"), None),

time: 736 us -> 355 us (0.48)
  the two profiles are of different devices: /device:TPU:14 before, /device:TPU:0 now
where the time goes in v2:
time: 355 us; the launch traced here: 354 us
  waiting for transfers between devices  202 us (57%)
  starting transfers between devices  71.9 us (20%)
  Pallas kernels  46.5 us (13%)
  local copies, waits for them, and re-layouts  15.1 us (4%)
  matrix products  9.03 us (3%)
  other arithmetic  7.69 us (2%)
    ppermute x30, waiting for transfers between devices, to_layer(): lax.ppermute(values, 'expert', [(d, (d + 4 * step) % devices) for d in ra...  114 us
    ppermute x16, waiting for transfers between devices, to_side(): return lax.ppermute(values, 'expert', [(d, d ^ 2) for d in range(devices)])  73.4 us
    ppermute x30, starting transfers between devices, to_layer(): lax.ppermute(values, 'expert', [(d, (d + 4 * step) % devices) for d in ra...  42.7 us
    pallas_call x8, Pallas kernels, halves_call(): pl.pallas_call(kernel, grid=(2,), in_specs=in_specs, out_specs=[pl.BlockS...  30.9 us
    ppermute x16, starting transfers between devices, to_side(): return lax.ppermute(values, 'expert', [(d, d ^ 2) for d in range(devices)])  21.7 us
    pallas_call x2, Pallas kernels, hidden_forward(): pl.pallas_call(hidden_kernel, grid=(count // tile,), in_specs=[pl.BlockSp...  15.6 us
    ppermute x6, waiting for transfers between devices, to_twin(): return lax.ppermute(values, 'expert', [(d, d ^ 1) for d in range(devices)])  14.9 us
    unnamed x34, local copies, waits for them, and re-layouts  9.31 us
  transfers between devices with their start and end apart: 52, of which 23 were waited for; matrix products, arithmetic and copies ran while one was open for 8% of the time, Pallas kernels for 13%

profile of v2, /device:TPU:0, one launch (start us, length us, event | category | flops | bytes accessed | tf_op | source)
XLA Modules:
  0.0 353.8 jit_solution(10545619260721708393)
XLA Ops:
  2.9 5.1 %collective-permute-start = (bf16[128,2176]{1,0:T(8,128)(2,1)S(1)}, bf16[128,2176]{1,0:T(8,128)(2,1)S(1)}, u32[]{:S(2)}, u32[]{:S(2)}) collective-permute-start(bf16[128,2176]{1,0:T(8,128)(2,1)S(1)} %concatenate.18), channel_id=1, source_target_pairs={{0,12},{1,13},{2,14},{3,15},{4,0},{5,1},{6,2},{7,3},{8,4},{9,5},{1... | collective-permute-start | bytes 1671176 | tf_op jit(solution)/shard_map/ppermute | solution.py:172
  9.0 1.5 collective-permute-start.3
  10.5 1.5 collective-permute-start.7
  12.0 2.9 fusion.35
  15.8 39.8 %collective-permute-done.1 = bf16[128,2176]{1,0:T(8,128)(2,1)S(1)} collective-permute-done((bf16[128,2176]{1,0:T(8,128)(2,1)S(1)}, bf16[128,2176]{1,0:T(8,128)(2,1)S(1)}, u32[]{:S(2)}, u32[]{:S(2)}) %collective-permute-start.1) | collective-permute-done | bytes 557088 | tf_op jit(solution)/shard_map/ppermute | solution.py:172
  55.6 1.8 collective-permute-start.8
  59.9 2.0 collective-permute-start.31
  62.8 8.6 %collective-permute-done.29 = bf16[128,2048]{1,0:T(8,128)(2,1)S(1)} collective-permute-done((bf16[128,2048]{1,0:T(8,128)(2,1)S(1)}, bf16[128,2048]{1,0:T(8,128)(2,1)S(1)}, u32[]{:S(2)}, u32[]{:S(2)}) %collective-permute-start.29) | collective-permute-done | bytes 524320 | tf_op jit(solution)/shard_map/ppermute | solution.py:172
  71.4 1.5 collective-permute-start.32
  73.0 28.2 %collective-permute-done.30 = bf16[128,2048]{1,0:T(8,128)(2,1)} collective-permute-done((bf16[128,2048]{1,0:T(8,128)(2,1)S(1)}, bf16[128,2048]{1,0:T(8,128)(2,1)}, u32[]{:S(2)}, u32[]{:S(2)}) %collective-permute-start.30) | collective-permute-done | bytes 524320 | tf_op jit(solution)/shard_map/ppermute | solution.py:172
  101.2 1.5 collective-permute-start.4
  105.5 1.6 collective-permute-start.6
  107.1 9.7 %collective-permute-done.4 = bf16[128,2176]{1,0:T(8,128)(2,1)S(1)} collective-permute-done((bf16[128,2176]{1,0:T(8,128)(2,1)S(1)}, bf16[128,2176]{1,0:T(8,128)(2,1)S(1)}, u32[]{:S(2)}, u32[]{:S(2)}) %collective-permute-start.4) | collective-permute-done | bytes 557088 | tf_op jit(solution)/shard_map/ppermute | solution.py:169
  116.8 1.5 collective-permute-start.33
  119.1 9.6 %collective-permute-done.5 = bf16[128,2176]{1,0:T(8,128)(2,1)S(1)} collective-permute-done((bf16[128,2176]{1,0:T(8,128)(2,1)S(1)}, bf16[128,2176]{1,0:T(8,128)(2,1)S(1)}, u32[]{:S(2)}, u32[]{:S(2)}) %collective-permute-start.5) | collective-permute-done | bytes 557088 | tf_op jit(solution)/shard_map/ppermute | solution.py:169
  128.7 1.5 collective-permute-start.34
  131.1 9.6 %collective-permute-done.6 = bf16[128,2176]{1,0:T(8,128)(2,1)S(1)} collective-permute-done((bf16[128,2176]{1,0:T(8,128)(2,1)S(1)}, bf16[128,2176]{1,0:T(8,128)(2,1)S(1)}, u32[]{:S(2)}, u32[]{:S(2)}) %collective-permute-start.6) | collective-permute-done | bytes 557088 | tf_op jit(solution)/shard_map/ppermute | solution.py:169
  140.6 1.5 collective-permute-start.35
  143.0 7.8 %hidden_forward.2 = (bf16[1024,512]{1,0:T(8,128)(2,1)S(1)}, f32[1024,512]{1,0:T(8,128)S(1)}, f32[1024,512]{1,0:T(8,128)S(1)}) custom-call(bf16[1024,2176]{1,0:T(8,128)(2,1)} %constant_dynamic-update-slice_fusion.rows_ref, bf16[2,2048,256]{2,1,0:T(8,128)(2,1)} %refs_2_.7, bf16[2,2048,256]{2,1,0:T(8,128)(2,1)} %refs_3_.7), custom_call_target="tpu_custom_call" | custom-call | flops 4294967296 | bytes 13631488 | tf_op jit(solution)/shard_map/hidden_forward/pallas_call | solution.py:73
  150.8 1.5 convert_add_fusion.8
  152.9 10.2 %collective-permute-done.34 = bf16[128,2048]{1,0:T(8,128)(2,1)S(1)} collective-permute-done((bf16[128,2048]{1,0:T(8,128)(2,1)}, bf16[128,2048]{1,0:T(8,128)(2,1)S(1)}, u32[]{:S(2)}, u32[]{:S(2)}) %collective-permute-start.34) | collective-permute-done | bytes 524320 | tf_op jit(solution)/shard_map/ppermute | solution.py:169
  163.1 7.9 %collective-permute-done.35 = bf16[128,2048]{1,0:T(8,128)(2,1)S(1)} collective-permute-done((bf16[128,2048]{1,0:T(8,128)(2,1)}, bf16[128,2048]{1,0:T(8,128)(2,1)S(1)}, u32[]{:S(2)}, u32[]{:S(2)}) %collective-permute-start.35) | collective-permute-done | bytes 524320 | tf_op jit(solution)/shard_map/ppermute | solution.py:169
  171.1 1.7 collective-permute-start.24
  173.2 2.4 multiply_convert_fusion.2
  175.6 1.7 collective-permute-start.14
  177.7 7.8 %hidden_forward.3 = (bf16[1024,512]{1,0:T(8,128)(2,1)S(1)}, f32[1024,512]{1,0:T(8,128)S(1)}, f32[1024,512]{1,0:T(8,128)S(1)}) custom-call(bf16[1024,2176]{1,0:T(8,128)(2,1)} %constant_dynamic-update-slice_fusion.rows_ref, bf16[2,2048,256]{2,1,0:T(8,128)(2,1)} %collective-permute-done.7.gate_ref.refs_6_, bf16[2,2048,256]{2,1,0:T(8,128)(2,1)} %copy-done.5), custom_call_target="tpu_custom_call" | custom-call | flops 4294967296 | bytes 13631488 | tf_op jit(solution)/shard_map/hidden_forward/pallas_call | solution.py:73
  186.3 3.4 mix_columns.7
  190.7 1.5 collective-permute-start.25
  192.2 5.3 %collective-permute-done.19.other_down_ref = bf16[2,256,512]{2,1,0:T(8,128)(2,1)S(1)} collective-permute-done((bf16[2,256,512]{2,1,0:T(8,128)(2,1)}, bf16[2,256,512]{2,1,0:T(8,128)(2,1)S(1)}, u32[]{:S(2)}, u32[]{:S(2)}) %collective-permute-start.19) | collective-permute-done | bytes 524320 | tf_op jit(solution)/shard_map/ppermute | solution.py:166
  197.5 3.4 mix_columns.6
  200.9 1.5 collective-permute-start.20
  202.4 6.3 %collective-permute-done.14.other_down_ref = bf16[2,256,512]{2,1,0:T(8,128)(2,1)S(1)} collective-permute-done((bf16[2,256,512]{2,1,0:T(8,128)(2,1)S(1)}, bf16[2,256,512]{2,1,0:T(8,128)(2,1)S(1)}, u32[]{:S(2)}, u32[]{:S(2)}) %collective-permute-start.14) | collective-permute-done | bytes 524320 | tf_op jit(solution)/shard_map/ppermute | solution.py:166
  208.7 3.4 mix_columns.5
  212.1 1.5 collective-permute-start.15
  213.7 2.6 collective-permute-done.9.other_down_ref
  216.3 2.6 mix_columns.4
  219.0 1.6 collective-permute-start.10
  220.5 2.0 fusion.4
  222.5 2.0 fusion.8
  225.2 2.0 multiply_convert_fusion
  227.2 4.5 %back_columns.7 = (f32[512,512]{1,0:T(8,128)S(1)}, bf16[512,512]{1,0:T(8,128)(2,1)S(1)}) custom-call(f32[1024,4]{1,0:T(8,128)S(1)} %pad_maximum_fusion.2.weight_ref, bf16[1024,512]{1,0:T(8,128)(2,1)S(1)} %get-tuple-element.75.refs_0_, bf16[1024,512]{1,0:T(8,128)(2,1)S(1)} %get-tuple-element.74.refs_1_, bf16[2,2048,256]{2,1,0:T(8,128)(2,1)} %refs_2_.7, ...), custom_call_target="tpu_custom_call" | custom-call | flops 2147483648 | bytes 7868416 | tf_op jit(solution)/shard_map/back_columns/pallas_call | solution.py:95
  232.5 4.5 %back_columns.6 = (f32[512,512]{1,0:T(8,128)S(1)}, bf16[512,512]{1,0:T(8,128)(2,1)S(1)}) custom-call(f32[1024,4]{1,0:T(8,128)S(1)} %pad_maximum_fusion.2.weight_ref, bf16[1024,512]{1,0:T(8,128)(2,1)S(1)} %get-tuple-element.75.refs_0_, bf16[1024,512]{1,0:T(8,128)(2,1)S(1)} %get-tuple-element.74.refs_1_, bf16[2,2048,256]{2,1,0:T(8,128)(2,1)} %refs_2_.7, ...), custom_call_target="tpu_custom_call" | custom-call | flops 2147483648 | bytes 7868416 | tf_op jit(solution)/shard_map/back_columns/pallas_call | solution.py:95
  237.0 4.5 %back_columns.5 = (f32[512,512]{1,0:T(8,128)S(1)}, bf16[512,512]{1,0:T(8,128)(2,1)S(1)}) custom-call(f32[1024,4]{1,0:T(8,128)S(1)} %pad_maximum_fusion.2.weight_ref, bf16[1024,512]{1,0:T(8,128)(2,1)S(1)} %get-tuple-element.75.refs_0_, bf16[1024,512]{1,0:T(8,128)(2,1)S(1)} %get-tuple-element.74.refs_1_, bf16[2,2048,256]{2,1,0:T(8,128)(2,1)} %refs_2_.7, ...), custom_call_target="tpu_custom_call" | custom-call | flops 2147483648 | bytes 7868416 | tf_op jit(solution)/shard_map/back_columns/pallas_call | solution.py:95
  241.5 4.6 %back_columns.4 = (f32[512,512]{1,0:T(8,128)S(1)}, bf16[512,512]{1,0:T(8,128)(2,1)S(1)}) custom-call(f32[1024,4]{1,0:T(8,128)S(1)} %pad_maximum_fusion.2.weight_ref, bf16[1024,512]{1,0:T(8,128)(2,1)S(1)} %get-tuple-element.75.refs_0_, bf16[1024,512]{1,0:T(8,128)(2,1)S(1)} %get-tuple-element.74.refs_1_, bf16[2,2048,256]{2,1,0:T(8,128)(2,1)} %refs_2_.7, ...), custom_call_target="tpu_custom_call" | custom-call | flops 2147483648 | bytes 7868416 | tf_op jit(solution)/shard_map/back_columns/pallas_call | solution.py:95
  246.1 1.3 collective-permute-start.44
  249.8 1.3 collective-permute-start.36
  252.0 9.0 %collective-permute-done.44 = bf16[512,512]{1,0:T(8,128)(2,1)S(1)} collective-permute-done((bf16[512,512]{1,0:T(8,128)(2,1)S(1)}, bf16[512,512]{1,0:T(8,128)(2,1)S(1)}, u32[]{:S(2)}, u32[]{:S(2)}) %collective-permute-start.44) | collective-permute-done | bytes 524320 | tf_op jit(solution)/shard_map/ppermute | solution.py:169
  261.3 11.0 %collective-permute-done.40 = bf16[512,512]{1,0:T(8,128)(2,1)S(1)} collective-permute-done((bf16[512,512]{1,0:T(8,128)(2,1)S(1)}, bf16[512,512]{1,0:T(8,128)(2,1)S(1)}, u32[]{:S(2)}, u32[]{:S(2)}) %collective-permute-start.40) | collective-permute-done | bytes 524320 | tf_op jit(solution)/shard_map/ppermute | solution.py:169
  272.5 6.5 %collective-permute-done.36 = bf16[512,512]{1,0:T(8,128)(2,1)S(1)} collective-permute-done((bf16[512,512]{1,0:T(8,128)(2,1)S(1)}, bf16[512,512]{1,0:T(8,128)(2,1)S(1)}, u32[]{:S(2)}, u32[]{:S(2)}) %collective-permute-start.36) | collective-permute-done | bytes 524320 | tf_op jit(solution)/shard_map/ppermute | solution.py:169
  279.3 3.8 %collective-permute-start.18 = (bf16[128,512]{1,0:T(8,128)(2,1)S(1)}, bf16[128,512]{1,0:T(8,128)(2,1)S(1)}, u32[]{:S(2)}, u32[]{:S(2)}) collective-permute-start(bf16[128,512]{1,0:T(8,128)(2,1)S(1)} %get-tuple-element.96), channel_id=1, source_target_pairs={{0,12},{1,13},{2,14},{3,15},{4,0},{5,1},{6,2},{7,3},{8,4},{9,5},{1... | collective-permute-start | bytes 393224 | tf_op jit(solution)/shard_map/ppermute | solution.py:172
  284.5 11.1 %collective-permute-done.22 = bf16[128,512]{1,0:T(8,128)(2,1)S(1)} collective-permute-done((bf16[128,512]{1,0:T(8,128)(2,1)S(1)}, bf16[128,512]{1,0:T(8,128)(2,1)S(1)}, u32[]{:S(2)}, u32[]{:S(2)}) %collective-permute-start.22) | collective-permute-done | bytes 131104 | tf_op jit(solution)/shard_map/ppermute | solution.py:172
  296.1 2.8 collective-permute-start.11
  298.9 2.3 collective-permute-done.17
  301.3 6.0 %collective-permute-start.50 = (bf16[128,512]{1,0:T(8,128)(2,1)S(1)}, bf16[128,512]{1,0:T(8,128)(2,1)S(1)}, u32[]{:S(2)}, u32[]{:S(2)}) collective-permute-start(bf16[128,512]{1,0:T(8,128)(2,1)S(1)} %get-tuple-element.91), channel_id=1, source_target_pairs={{0,8},{1,9},{2,10},{3,11},{4,12},{5,13},{6,14},{7,15},{8,0},{9,1},... | collective-permute-start | bytes 393224 | tf_op jit(solution)/shard_map/ppermute | solution.py:172
  307.4 4.2 %collective-permute-start.49 = (bf16[128,512]{1,0:T(8,128)(2,1)S(1)}, bf16[128,512]{1,0:T(8,128)(2,1)S(1)}, u32[]{:S(2)}, u32[]{:S(2)}) collective-permute-start(bf16[128,512]{1,0:T(8,128)(2,1)S(1)} %get-tuple-element.89), channel_id=1, source_target_pairs={{0,4},{1,5},{2,6},{3,7},{4,8},{5,9},{6,10},{7,11},{8,12},{9,13},{1... | collective-permute-start | bytes 393224 | tf_op jit(solution)/shard_map/ppermute | solution.py:172
  311.5 6.6 %collective-permute-done.12 = bf16[128,512]{1,0:T(8,128)(2,1)S(1)} collective-permute-done((bf16[128,512]{1,0:T(8,128)(2,1)S(1)}, bf16[128,512]{1,0:T(8,128)(2,1)S(1)}, u32[]{:S(2)}, u32[]{:S(2)}) %collective-permute-start.12) | collective-permute-done | bytes 131104 | tf_op jit(solution)/shard_map/ppermute | solution.py:172
  319.6 1.9 collective-permute-start.45
  321.5 2.3 collective-permute-done.50
  323.9 5.9 %collective-permute-start.42 = (bf16[128,512]{1,0:T(8,128)(2,1)S(1)}, bf16[128,512]{1,0:T(8,128)(2,1)S(1)}, u32[]{:S(2)}, u32[]{:S(2)}) collective-permute-start(bf16[128,512]{1,0:T(8,128)(2,1)S(1)} %get-tuple-element.85), channel_id=1, source_target_pairs={{0,8},{1,9},{2,10},{3,11},{4,12},{5,13},{6,14},{7,15},{8,0},{9,1},... | collective-permute-start | bytes 393224 | tf_op jit(solution)/shard_map/ppermute | solution.py:172
  329.8 4.4 %collective-permute-start.41 = (bf16[128,512]{1,0:T(8,128)(2,1)S(1)}, bf16[128,512]{1,0:T(8,128)(2,1)S(1)}, u32[]{:S(2)}, u32[]{:S(2)}) collective-permute-start(bf16[128,512]{1,0:T(8,128)(2,1)S(1)} %get-tuple-element.83), channel_id=1, source_target_pairs={{0,4},{1,5},{2,6},{3,7},{4,8},{5,9},{6,10},{7,11},{8,12},{9,13},{1... | collective-permute-start | bytes 393224 | tf_op jit(solution)/shard_map/ppermute | solution.py:172
  334.2 6.5 %collective-permute-done.46 = bf16[128,512]{1,0:T(8,128)(2,1)S(1)} collective-permute-done((bf16[128,512]{1,0:T(8,128)(2,1)S(1)}, bf16[128,512]{1,0:T(8,128)(2,1)S(1)}, u32[]{:S(2)}, u32[]{:S(2)}) %collective-permute-start.46) | collective-permute-done | bytes 131104 | tf_op jit(solution)/shard_map/ppermute | solution.py:172
  341.1 3.0 collective-permute-start.37
  344.1 2.3 collective-permute-done.42
  347.5 5.2 %collective-permute-done.38 = bf16[128,512]{1,0:T(8,128)(2,1)S(1)} collective-permute-done((bf16[128,512]{1,0:T(8,128)(2,1)S(1)}, bf16[128,512]{1,0:T(8,128)(2,1)S(1)}, u32[]{:S(2)}, u32[]{:S(2)}) %collective-permute-start.38) | collective-permute-done | bytes 131104 | tf_op jit(solution)/shard_map/ppermute | solution.py:172
  (128 shorter events, 27.7 us)
Async XLA Ops:
  0.6 56.7 %copy-start.8 = (bf16[128,2048]{1,0:T(8,128)(2,1)S(1)}, bf16[128,2048]{1,0:T(8,128)(2,1)}, u32[]{:S(2)}) copy-start(bf16[128,2048]{1,0:T(8,128)(2,1)} %param.8) | copy-start | bytes 1572868
  2.9 54.5 %collective-permute-start = (bf16[128,2176]{1,0:T(8,128)(2,1)S(1)}, bf16[128,2176]{1,0:T(8,128)(2,1)S(1)}, u32[]{:S(2)}, u32[]{:S(2)}) collective-permute-start(bf16[128,2176]{1,0:T(8,128)(2,1)S(1)} %concatenate.18), channel_id=1, source_target_pairs={{0,12},{1,13},{2,14},{3,15},{4,0},{5,1},{6,2},{7,3},{8,4},{9,5},{1... | collective-permute-start | bytes 1671176 | tf_op jit(solution)/shard_map/ppermute | solution.py:172
  8.0 47.6 %collective-permute-start.1 = (bf16[128,2176]{1,0:T(8,128)(2,1)S(1)}, bf16[128,2176]{1,0:T(8,128)(2,1)S(1)}, u32[]{:S(2)}, u32[]{:S(2)}) collective-permute-start(bf16[128,2176]{1,0:T(8,128)(2,1)S(1)} %concatenate.18), channel_id=1, source_target_pairs={{0,8},{1,9},{2,10},{3,11},{4,12},{5,13},{6,14},{7,15},{8,0},{9,1},... | collective-permute-start | bytes 1671176 | tf_op jit(solution)/shard_map/ppermute | solution.py:172
  8.0 51.1 %collective-permute-start.2 = (bf16[128,2176]{1,0:T(8,128)(2,1)S(1)}, bf16[128,2176]{1,0:T(8,128)(2,1)S(1)}, u32[]{:S(2)}, u32[]{:S(2)}) collective-permute-start(bf16[128,2176]{1,0:T(8,128)(2,1)S(1)} %concatenate.18), channel_id=1, source_target_pairs={{0,4},{1,5},{2,6},{3,7},{4,8},{5,9},{6,10},{7,11},{8,12},{9,13},{1... | collective-permute-start | bytes 1671176 | tf_op jit(solution)/shard_map/ppermute | solution.py:172
  9.0 50.9 %collective-permute-start.3 = (bf16[128,2176]{1,0:T(8,128)(2,1)S(1)}, bf16[128,2176]{1,0:T(8,128)(2,1)S(1)}, u32[]{:S(2)}, u32[]{:S(2)}) collective-permute-start(bf16[128,2176]{1,0:T(8,128)(2,1)S(1)} %concatenate.18), channel_id=1, source_target_pairs={{0,2},{1,3},{2,0},{3,1},{4,6},{5,7},{6,4},{7,5},{8,10},{9,11},{10,... | collective-permute-start | bytes 1671176 | tf_op jit(solution)/shard_map/ppermute | solution.py:169
  10.5 165.1 %collective-permute-start.7 = (bf16[2,2048,256]{2,1,0:T(8,128)(2,1)}, bf16[2,2048,256]{2,1,0:T(8,128)(2,1)}, u32[]{:S(2)}, u32[]{:S(2)}) collective-permute-start(bf16[2,2048,256]{2,1,0:T(8,128)(2,1)} %refs_2_.7), channel_id=1, source_target_pairs={{0,1},{1,0},{2,3},{3,2},{4,5},{5,4},{6,7},{7,6},{8,9},{9,8},{10,11... | collective-permute-start | bytes 6291464 | tf_op jit(solution)/shard_map/ppermute | solution.py:166
  55.6 115.5 %collective-permute-start.8 = (bf16[2,2048,256]{2,1,0:T(8,128)(2,1)}, bf16[2,2048,256]{2,1,0:T(8,128)(2,1)S(1)}, u32[]{:S(2)}, u32[]{:S(2)}) collective-permute-start(bf16[2,2048,256]{2,1,0:T(8,128)(2,1)} %refs_3_.7), channel_id=1, source_target_pairs={{0,1},{1,0},{2,3},{3,2},{4,5},{5,4},{6,7},{7,6},{8,9},{9,8},{10,11... | collective-permute-start | bytes 6291464 | tf_op jit(solution)/shard_map/ppermute | solution.py:166
  57.4 14.0 %collective-permute-start.29 = (bf16[128,2048]{1,0:T(8,128)(2,1)S(1)}, bf16[128,2048]{1,0:T(8,128)(2,1)S(1)}, u32[]{:S(2)}, u32[]{:S(2)}) collective-permute-start(bf16[128,2048]{1,0:T(8,128)(2,1)S(1)} %copy-done.8), channel_id=1, source_target_pairs={{0,12},{1,13},{2,14},{3,15},{4,0},{5,1},{6,2},{7,3},{8,4},{9,5},{1... | collective-permute-start | bytes 1572872 | tf_op jit(solution)/shard_map/ppermute | solution.py:172
  59.1 42.1 %collective-permute-start.30 = (bf16[128,2048]{1,0:T(8,128)(2,1)S(1)}, bf16[128,2048]{1,0:T(8,128)(2,1)}, u32[]{:S(2)}, u32[]{:S(2)}) collective-permute-start(bf16[128,2048]{1,0:T(8,128)(2,1)S(1)} %copy-done.8), channel_id=1, source_target_pairs={{0,8},{1,9},{2,10},{3,11},{4,12},{5,13},{6,14},{7,15},{8,0},{9,1},... | collective-permute-start | bytes 1572872 | tf_op jit(solution)/shard_map/ppermute | solution.py:172
  59.9 43.9 %collective-permute-start.31 = (bf16[128,2048]{1,0:T(8,128)(2,1)S(1)}, bf16[128,2048]{1,0:T(8,128)(2,1)}, u32[]{:S(2)}, u32[]{:S(2)}) collective-permute-start(bf16[128,2048]{1,0:T(8,128)(2,1)S(1)} %copy-done.8), channel_id=1, source_target_pairs={{0,4},{1,5},{2,6},{3,7},{4,8},{5,9},{6,10},{7,11},{8,12},{9,13},{1... | collective-permute-start | bytes 1572872 | tf_op jit(solution)/shard_map/ppermute | solution.py:172
  71.4 34.1 %collective-permute-start.32 = (bf16[128,2048]{1,0:T(8,128)(2,1)S(1)}, bf16[128,2048]{1,0:T(8,128)(2,1)S(1)}, u32[]{:S(2)}, u32[]{:S(2)}) collective-permute-start(bf16[128,2048]{1,0:T(8,128)(2,1)S(1)} %copy-done.8), channel_id=1, source_target_pairs={{0,2},{1,3},{2,0},{3,1},{4,6},{5,7},{6,4},{7,5},{8,10},{9,11},{10,... | collective-permute-start | bytes 1572872 | tf_op jit(solution)/shard_map/ppermute | solution.py:169
  101.2 15.6 %collective-permute-start.4 = (bf16[128,2176]{1,0:T(8,128)(2,1)S(1)}, bf16[128,2176]{1,0:T(8,128)(2,1)S(1)}, u32[]{:S(2)}, u32[]{:S(2)}) collective-permute-start(bf16[128,2176]{1,0:T(8,128)(2,1)S(1)} %collective-permute-done), channel_id=1, source_target_pairs={{0,2},{1,3},{2,0},{3,1},{4,6},{5,7},{6,4},{7,5},{8,10},{9,11},{10,... | collective-permute-start | bytes 1671176 | tf_op jit(solution)/shard_map/ppermute | solution.py:169
  103.8 24.9 %collective-permute-start.5 = (bf16[128,2176]{1,0:T(8,128)(2,1)S(1)}, bf16[128,2176]{1,0:T(8,128)(2,1)S(1)}, u32[]{:S(2)}, u32[]{:S(2)}) collective-permute-start(bf16[128,2176]{1,0:T(8,128)(2,1)S(1)} %collective-permute-done.1), channel_id=1, source_target_pairs={{0,2},{1,3},{2,0},{3,1},{4,6},{5,7},{6,4},{7,5},{8,10},{9,11},{10,... | collective-permute-start | bytes 1671176 | tf_op jit(solution)/shard_map/ppermute | solution.py:169
  105.5 35.1 %collective-permute-start.6 = (bf16[128,2176]{1,0:T(8,128)(2,1)S(1)}, bf16[128,2176]{1,0:T(8,128)(2,1)S(1)}, u32[]{:S(2)}, u32[]{:S(2)}) collective-permute-start(bf16[128,2176]{1,0:T(8,128)(2,1)S(1)} %collective-permute-done.2), channel_id=1, source_target_pairs={{0,2},{1,3},{2,0},{3,1},{4,6},{5,7},{6,4},{7,5},{8,10},{9,11},{10,... | collective-permute-start | bytes 1671176 | tf_op jit(solution)/shard_map/ppermute | solution.py:169
  116.8 36.1 %collective-permute-start.33 = (bf16[128,2048]{1,0:T(8,128)(2,1)S(1)}, bf16[128,2048]{1,0:T(8,128)(2,1)S(1)}, u32[]{:S(2)}, u32[]{:S(2)}) collective-permute-start(bf16[128,2048]{1,0:T(8,128)(2,1)S(1)} %collective-permute-done.29), channel_id=1, source_target_pairs={{0,2},{1,3},{2,0},{3,1},{4,6},{5,7},{6,4},{7,5},{8,10},{9,11},{10,... | collective-permute-start | bytes 1572872 | tf_op jit(solution)/shard_map/ppermute | solution.py:169
  128.7 34.4 %collective-permute-start.34 = (bf16[128,2048]{1,0:T(8,128)(2,1)}, bf16[128,2048]{1,0:T(8,128)(2,1)S(1)}, u32[]{:S(2)}, u32[]{:S(2)}) collective-permute-start(bf16[128,2048]{1,0:T(8,128)(2,1)} %collective-permute-done.30), channel_id=1, source_target_pairs={{0,2},{1,3},{2,0},{3,1},{4,6},{5,7},{6,4},{7,5},{8,10},{9,11},{10,... | collective-permute-start | bytes 1572872 | tf_op jit(solution)/shard_map/ppermute | solution.py:169
  140.6 30.4 %collective-permute-start.35 = (bf16[128,2048]{1,0:T(8,128)(2,1)}, bf16[128,2048]{1,0:T(8,128)(2,1)S(1)}, u32[]{:S(2)}, u32[]{:S(2)}) collective-permute-start(bf16[128,2048]{1,0:T(8,128)(2,1)} %collective-permute-done.31), channel_id=1, source_target_pairs={{0,2},{1,3},{2,0},{3,1},{4,6},{5,7},{6,4},{7,5},{8,10},{9,11},{10,... | collective-permute-start | bytes 1572872 | tf_op jit(solution)/shard_map/ppermute | solution.py:169
  150.8 22.4 %copy-start.4 = (bf16[2,256,2048]{2,1,0:T(8,128)(2,1)S(1)}, bf16[2,256,2048]{2,1,0:T(8,128)(2,1)}, u32[]{:S(2)}) copy-start(bf16[2,256,2048]{2,1,0:T(8,128)(2,1)} %own_down_ref.7) | copy-start | bytes 6291460
  171.1 4.5 %copy-start.6 = (bf16[1024,2048]{1,0:T(8,128)(2,1)}, bf16[1024,2048]{1,0:T(8,128)(2,1)S(1)}, u32[]{:S(2)}) copy-start(bf16[1024,2048]{1,0:T(8,128)(2,1)S(1)} %constant_dynamic-update-slice_fusion.8) | copy-start | bytes 12582916
  171.1 2.1 copy-start.5
  171.1 15.1 %collective-permute-start.24 = (bf16[2,256,512]{2,1,0:T(8,128)(2,1)}, bf16[2,256,512]{2,1,0:T(8,128)(2,1)S(1)}, u32[]{:S(2)}, u32[]{:S(2)}) collective-permute-start(bf16[2,256,512]{2,1,0:T(8,128)(2,1)} %get-tuple-element.40), channel_id=1, source_target_pairs={{0,1},{1,0},{2,3},{3,2},{4,5},{5,4},{6,7},{7,6},{8,9},{9,8},{10,11... | collective-permute-start | bytes 1572872 | tf_op jit(solution)/shard_map/ppermute | solution.py:166
  172.8 24.7 %collective-permute-start.19 = (bf16[2,256,512]{2,1,0:T(8,128)(2,1)}, bf16[2,256,512]{2,1,0:T(8,128)(2,1)S(1)}, u32[]{:S(2)}, u32[]{:S(2)}) collective-permute-start(bf16[2,256,512]{2,1,0:T(8,128)(2,1)} %get-tuple-element.37), channel_id=1, source_target_pairs={{0,1},{1,0},{2,3},{3,2},{4,5},{5,4},{6,7},{7,6},{8,9},{9,8},{10,11... | collective-permute-start | bytes 1572872 | tf_op jit(solution)/shard_map/ppermute | solution.py:166
  173.2 2.4 copy-start.9
  175.6 33.1 %collective-permute-start.14 = (bf16[2,256,512]{2,1,0:T(8,128)(2,1)S(1)}, bf16[2,256,512]{2,1,0:T(8,128)(2,1)S(1)}, u32[]{:S(2)}, u32[]{:S(2)}) collective-permute-start(bf16[2,256,512]{2,1,0:T(8,128)(2,1)S(1)} %copy-done.9), channel_id=1, source_target_pairs={{0,1},{1,0},{2,3},{3,2},{4,5},{5,4},{6,7},{7,6},{8,9},{9,8},{10,11... | collective-permute-start | bytes 1572872 | tf_op jit(solution)/shard_map/ppermute | solution.py:166
  177.3 39.0 %collective-permute-start.9 = (bf16[2,256,512]{2,1,0:T(8,128)(2,1)}, bf16[2,256,512]{2,1,0:T(8,128)(2,1)S(1)}, u32[]{:S(2)}, u32[]{:S(2)}) collective-permute-start(bf16[2,256,512]{2,1,0:T(8,128)(2,1)} %get-tuple-element.31), channel_id=1, source_target_pairs={{0,1},{1,0},{2,3},{3,2},{4,5},{5,4},{6,7},{7,6},{8,9},{9,8},{10,11... | collective-permute-start | bytes 1572872 | tf_op jit(solution)/shard_map/ppermute | solution.py:166
  189.7 1.0 copy-start.2
  190.7 55.4 %collective-permute-start.25 = (bf16[512,512]{1,0:T(8,128)(2,1)}, bf16[512,512]{1,0:T(8,128)(2,1)}, u32[]{:S(2)}, u32[]{:S(2)}) collective-permute-start(bf16[512,512]{1,0:T(8,128)(2,1)} %get-tuple-element.42), channel_id=1, source_target_pairs={{0,2},{1,3},{2,0},{3,1},{4,6},{5,7},{6,4},{7,5},{8,10},{9,11},{10,... | collective-permute-start | bytes 1572872 | tf_op jit(solution)/shard_map/ppermute | solution.py:169
  200.9 18.0 %copy-start = (f32[512,512]{1,0:T(8,128)}, f32[512,512]{1,0:T(8,128)S(1)}, u32[]{:S(2)}) copy-start(f32[512,512]{1,0:T(8,128)S(1)} %get-tuple-element.38) | copy-start | bytes 3145732
  200.9 47.7 %collective-permute-start.20 = (bf16[512,512]{1,0:T(8,128)(2,1)}, bf16[512,512]{1,0:T(8,128)(2,1)S(1)}, u32[]{:S(2)}, u32[]{:S(2)}) collective-permute-start(bf16[512,512]{1,0:T(8,128)(2,1)} %get-tuple-element.39), channel_id=1, source_target_pairs={{0,2},{1,3},{2,0},{3,1},{4,6},{5,7},{6,4},{7,5},{8,10},{9,11},{10,... | collective-permute-start | bytes 1572872 | tf_op jit(solution)/shard_map/ppermute | solution.py:169
  212.1 37.6 %collective-permute-start.15 = (bf16[512,512]{1,0:T(8,128)(2,1)}, bf16[512,512]{1,0:T(8,128)(2,1)S(1)}, u32[]{:S(2)}, u32[]{:S(2)}) collective-permute-start(bf16[512,512]{1,0:T(8,128)(2,1)} %get-tuple-element.36), channel_id=1, source_target_pairs={{0,2},{1,3},{2,0},{3,1},{4,6},{5,7},{6,4},{7,5},{8,10},{9,11},{10,... | collective-permute-start | bytes 1572872 | tf_op jit(solution)/shard_map/ppermute | solution.py:169
  219.0 5.5 %copy-start.7 = (bf16[1024,2048]{1,0:T(8,128)(2,1)S(1)}, bf16[1024,2048]{1,0:T(8,128)(2,1)}, u32[]{:S(2)}) copy-start(bf16[1024,2048]{1,0:T(8,128)(2,1)} %copy-done.6) | copy-start | bytes 12582916
  219.0 32.4 %collective-permute-start.10 = (bf16[512,512]{1,0:T(8,128)(2,1)S(1)}, bf16[512,512]{1,0:T(8,128)(2,1)S(1)}, u32[]{:S(2)}, u32[]{:S(2)}) collective-permute-start(bf16[512,512]{1,0:T(8,128)(2,1)S(1)} %get-tuple-element.33), channel_id=1, source_target_pairs={{0,2},{1,3},{2,0},{3,1},{4,6},{5,7},{6,4},{7,5},{8,10},{9,11},{10,... | collective-permute-start | bytes 1572872 | tf_op jit(solution)/shard_map/ppermute | solution.py:169
  231.7 20.0 %collective-permute-start.48 = (bf16[512,512]{1,0:T(8,128)(2,1)S(1)}, bf16[512,512]{1,0:T(8,128)(2,1)S(1)}, u32[]{:S(2)}, u32[]{:S(2)}) collective-permute-start(bf16[512,512]{1,0:T(8,128)(2,1)S(1)} %get-tuple-element.55), channel_id=1, source_target_pairs={{0,2},{1,3},{2,0},{3,1},{4,6},{5,7},{6,4},{7,5},{8,10},{9,11},{10,... | collective-permute-start | bytes 1572872 | tf_op jit(solution)/shard_map/ppermute | solution.py:169
  241.5 5.9 %copy-start.3 = (f32[512,512]{1,0:T(8,128)S(1)}, f32[512,512]{1,0:T(8,128)}, u32[]{:S(2)}) copy-start(f32[512,512]{1,0:T(8,128)} %copy-done.2) | copy-start | bytes 3145732
  246.1 3.5 copy-start.1
  246.1 14.9 %collective-permute-start.44 = (bf16[512,512]{1,0:T(8,128)(2,1)S(1)}, bf16[512,512]{1,0:T(8,128)(2,1)S(1)}, u32[]{:S(2)}, u32[]{:S(2)}) collective-permute-start(bf16[512,512]{1,0:T(8,128)(2,1)S(1)} %get-tuple-element.53), channel_id=1, source_target_pairs={{0,2},{1,3},{2,0},{3,1},{4,6},{5,7},{6,4},{7,5},{8,10},{9,11},{10,... | collective-permute-start | bytes 1572872 | tf_op jit(solution)/shard_map/ppermute | solution.py:169
  248.7 23.6 %collective-permute-start.40 = (bf16[512,512]{1,0:T(8,128)(2,1)S(1)}, bf16[512,512]{1,0:T(8,128)(2,1)S(1)}, u32[]{:S(2)}, u32[]{:S(2)}) collective-permute-start(bf16[512,512]{1,0:T(8,128)(2,1)S(1)} %get-tuple-element.51), channel_id=1, source_target_pairs={{0,2},{1,3},{2,0},{3,1},{4,6},{5,7},{6,4},{7,5},{8,10},{9,11},{10,... | collective-permute-start | bytes 1572872 | tf_op jit(solution)/shard_map/ppermute | solution.py:169
  249.8 29.2 %collective-permute-start.36 = (bf16[512,512]{1,0:T(8,128)(2,1)S(1)}, bf16[512,512]{1,0:T(8,128)(2,1)S(1)}, u32[]{:S(2)}, u32[]{:S(2)}) collective-permute-start(bf16[512,512]{1,0:T(8,128)(2,1)S(1)} %get-tuple-element.49), channel_id=1, source_target_pairs={{0,2},{1,3},{2,0},{3,1},{4,6},{5,7},{6,4},{7,5},{8,10},{9,11},{10,... | collective-permute-start | bytes 1572872 | tf_op jit(solution)/shard_map/ppermute | solution.py:169
  251.3 27.9 %collective-permute-start.28 = (bf16[128,512]{1,0:T(8,128)(2,1)S(1)}, bf16[128,512]{1,0:T(8,128)(2,1)S(1)}, u32[]{:S(2)}, u32[]{:S(2)}) collective-permute-start(bf16[128,512]{1,0:T(8,128)(2,1)S(1)} %get-tuple-element.102), channel_id=1, source_target_pairs={{0,12},{1,13},{2,14},{3,15},{4,0},{5,1},{6,2},{7,3},{8,4},{9,5},{1... | collective-permute-start | bytes 393224 | tf_op jit(solution)/shard_map/ppermute | solution.py:172
  251.7 27.7 %collective-permute-start.27 = (bf16[128,512]{1,0:T(8,128)(2,1)S(1)}, bf16[128,512]{1,0:T(8,128)(2,1)S(1)}, u32[]{:S(2)}, u32[]{:S(2)}) collective-permute-start(bf16[128,512]{1,0:T(8,128)(2,1)S(1)} %get-tuple-element.103), channel_id=1, source_target_pairs={{0,8},{1,9},{2,10},{3,11},{4,12},{5,13},{6,14},{7,15},{8,0},{9,1},... | collective-permute-start | bytes 393224 | tf_op jit(solution)/shard_map/ppermute | solution.py:172
  261.0 22.1 %collective-permute-start.26 = (bf16[128,512]{1,0:T(8,128)(2,1)S(1)}, bf16[128,512]{1,0:T(8,128)(2,1)S(1)}, u32[]{:S(2)}, u32[]{:S(2)}) collective-permute-start(bf16[128,512]{1,0:T(8,128)(2,1)S(1)} %get-tuple-element.101), channel_id=1, source_target_pairs={{0,4},{1,5},{2,6},{3,7},{4,8},{5,9},{6,10},{7,11},{8,12},{9,13},{1... | collective-permute-start | bytes 393224 | tf_op jit(solution)/shard_map/ppermute | solution.py:172
  272.3 12.1 %collective-permute-start.23 = (bf16[128,512]{1,0:T(8,128)(2,1)S(1)}, bf16[128,512]{1,0:T(8,128)(2,1)S(1)}, u32[]{:S(2)}, u32[]{:S(2)}) collective-permute-start(bf16[128,512]{1,0:T(8,128)(2,1)S(1)} %get-tuple-element.99), channel_id=1, source_target_pairs={{0,12},{1,13},{2,14},{3,15},{4,0},{5,1},{6,2},{7,3},{8,4},{9,5},{1... | collective-permute-start | bytes 393224 | tf_op jit(solution)/shard_map/ppermute | solution.py:172
  279.0 16.6 %collective-permute-start.22 = (bf16[128,512]{1,0:T(8,128)(2,1)S(1)}, bf16[128,512]{1,0:T(8,128)(2,1)S(1)}, u32[]{:S(2)}, u32[]{:S(2)}) collective-permute-start(bf16[128,512]{1,0:T(8,128)(2,1)S(1)} %get-tuple-element.100), channel_id=1, source_target_pairs={{0,8},{1,9},{2,10},{3,11},{4,12},{5,13},{6,14},{7,15},{8,0},{9,1},... | collective-permute-start | bytes 393224 | tf_op jit(solution)/shard_map/ppermute | solution.py:172
  279.2 16.3 %collective-permute-start.21 = (bf16[128,512]{1,0:T(8,128)(2,1)S(1)}, bf16[128,512]{1,0:T(8,128)(2,1)S(1)}, u32[]{:S(2)}, u32[]{:S(2)}) collective-permute-start(bf16[128,512]{1,0:T(8,128)(2,1)S(1)} %get-tuple-element.98), channel_id=1, source_target_pairs={{0,4},{1,5},{2,6},{3,7},{4,8},{5,9},{6,10},{7,11},{8,12},{9,13},{1... | collective-permute-start | bytes 393224 | tf_op jit(solution)/shard_map/ppermute | solution.py:172
  279.3 16.8 %collective-permute-start.18 = (bf16[128,512]{1,0:T(8,128)(2,1)S(1)}, bf16[128,512]{1,0:T(8,128)(2,1)S(1)}, u32[]{:S(2)}, u32[]{:S(2)}) collective-permute-start(bf16[128,512]{1,0:T(8,128)(2,1)S(1)} %get-tuple-element.96), channel_id=1, source_target_pairs={{0,12},{1,13},{2,14},{3,15},{4,0},{5,1},{6,2},{7,3},{8,4},{9,5},{1... | collective-permute-start | bytes 393224 | tf_op jit(solution)/shard_map/ppermute | solution.py:172
  283.1 18.2 %collective-permute-start.17 = (bf16[128,512]{1,0:T(8,128)(2,1)S(1)}, bf16[128,512]{1,0:T(8,128)(2,1)S(1)}, u32[]{:S(2)}, u32[]{:S(2)}) collective-permute-start(bf16[128,512]{1,0:T(8,128)(2,1)S(1)} %get-tuple-element.97), channel_id=1, source_target_pairs={{0,8},{1,9},{2,10},{3,11},{4,12},{5,13},{6,14},{7,15},{8,0},{9,1},... | collective-permute-start | bytes 393224 | tf_op jit(solution)/shard_map/ppermute | solution.py:172
  284.3 17.0 %collective-permute-start.16 = (bf16[128,512]{1,0:T(8,128)(2,1)S(1)}, bf16[128,512]{1,0:T(8,128)(2,1)S(1)}, u32[]{:S(2)}, u32[]{:S(2)}) collective-permute-start(bf16[128,512]{1,0:T(8,128)(2,1)S(1)} %get-tuple-element.95), channel_id=1, source_target_pairs={{0,4},{1,5},{2,6},{3,7},{4,8},{5,9},{6,10},{7,11},{8,12},{9,13},{1... | collective-permute-start | bytes 393224 | tf_op jit(solution)/shard_map/ppermute | solution.py:172
  295.6 11.8 %collective-permute-start.13 = (bf16[128,512]{1,0:T(8,128)(2,1)S(1)}, bf16[128,512]{1,0:T(8,128)(2,1)S(1)}, u32[]{:S(2)}, u32[]{:S(2)}) collective-permute-start(bf16[128,512]{1,0:T(8,128)(2,1)S(1)} %get-tuple-element.93), channel_id=1, source_target_pairs={{0,12},{1,13},{2,14},{3,15},{4,0},{5,1},{6,2},{7,3},{8,4},{9,5},{1... | collective-permute-start | bytes 393224 | tf_op jit(solution)/shard_map/ppermute | solution.py:172
  295.6 22.5 %collective-permute-start.12 = (bf16[128,512]{1,0:T(8,128)(2,1)S(1)}, bf16[128,512]{1,0:T(8,128)(2,1)S(1)}, u32[]{:S(2)}, u32[]{:S(2)}) collective-permute-start(bf16[128,512]{1,0:T(8,128)(2,1)S(1)} %get-tuple-element.94), channel_id=1, source_target_pairs={{0,8},{1,9},{2,10},{3,11},{4,12},{5,13},{6,14},{7,15},{8,0},{9,1},... | collective-permute-start | bytes 393224 | tf_op jit(solution)/shard_map/ppermute | solution.py:172
  296.1 22.0 %collective-permute-start.11 = (bf16[128,512]{1,0:T(8,128)(2,1)S(1)}, bf16[128,512]{1,0:T(8,128)(2,1)S(1)}, u32[]{:S(2)}, u32[]{:S(2)}) collective-permute-start(bf16[128,512]{1,0:T(8,128)(2,1)S(1)} %get-tuple-element.92), channel_id=1, source_target_pairs={{0,4},{1,5},{2,6},{3,7},{4,8},{5,9},{6,10},{7,11},{8,12},{9,13},{1... | collective-permute-start | bytes 393224 | tf_op jit(solution)/shard_map/ppermute | solution.py:172
  301.3 18.3 %collective-permute-start.51 = (bf16[128,512]{1,0:T(8,128)(2,1)S(1)}, bf16[128,512]{1,0:T(8,128)(2,1)S(1)}, u32[]{:S(2)}, u32[]{:S(2)}) collective-permute-start(bf16[128,512]{1,0:T(8,128)(2,1)S(1)} %get-tuple-element.90), channel_id=1, source_target_pairs={{0,12},{1,13},{2,14},{3,15},{4,0},{5,1},{6,2},{7,3},{8,4},{9,5},{1... | collective-permute-start | bytes 393224 | tf_op jit(solution)/shard_map/ppermute | solution.py:172
  301.3 22.5 %collective-permute-start.50 = (bf16[128,512]{1,0:T(8,128)(2,1)S(1)}, bf16[128,512]{1,0:T(8,128)(2,1)S(1)}, u32[]{:S(2)}, u32[]{:S(2)}) collective-permute-start(bf16[128,512]{1,0:T(8,128)(2,1)S(1)} %get-tuple-element.91), channel_id=1, source_target_pairs={{0,8},{1,9},{2,10},{3,11},{4,12},{5,13},{6,14},{7,15},{8,0},{9,1},... | collective-permute-start | bytes 393224 | tf_op jit(solution)/shard_map/ppermute | solution.py:172
  307.4 16.5 %collective-permute-start.49 = (bf16[128,512]{1,0:T(8,128)(2,1)S(1)}, bf16[128,512]{1,0:T(8,128)(2,1)S(1)}, u32[]{:S(2)}, u32[]{:S(2)}) collective-permute-start(bf16[128,512]{1,0:T(8,128)(2,1)S(1)} %get-tuple-element.89), channel_id=1, source_target_pairs={{0,4},{1,5},{2,6},{3,7},{4,8},{5,9},{6,10},{7,11},{8,12},{9,13},{1... | collective-permute-start | bytes 393224 | tf_op jit(solution)/shard_map/ppermute | solution.py:172
  318.1 11.7 %collective-permute-start.47 = (bf16[128,512]{1,0:T(8,128)(2,1)S(1)}, bf16[128,512]{1,0:T(8,128)(2,1)S(1)}, u32[]{:S(2)}, u32[]{:S(2)}) collective-permute-start(bf16[128,512]{1,0:T(8,128)(2,1)S(1)} %get-tuple-element.87), channel_id=1, source_target_pairs={{0,12},{1,13},{2,14},{3,15},{4,0},{5,1},{6,2},{7,3},{8,4},{9,5},{1... | collective-permute-start | bytes 393224 | tf_op jit(solution)/shard_map/ppermute | solution.py:172
  318.1 22.5 %collective-permute-start.46 = (bf16[128,512]{1,0:T(8,128)(2,1)S(1)}, bf16[128,512]{1,0:T(8,128)(2,1)S(1)}, u32[]{:S(2)}, u32[]{:S(2)}) collective-permute-start(bf16[128,512]{1,0:T(8,128)(2,1)S(1)} %get-tuple-element.88), channel_id=1, source_target_pairs={{0,8},{1,9},{2,10},{3,11},{4,12},{5,13},{6,14},{7,15},{8,0},{9,1},... | collective-permute-start | bytes 393224 | tf_op jit(solution)/shard_map/ppermute | solution.py:172
  319.6 21.1 %collective-permute-start.45 = (bf16[128,512]{1,0:T(8,128)(2,1)S(1)}, bf16[128,512]{1,0:T(8,128)(2,1)S(1)}, u32[]{:S(2)}, u32[]{:S(2)}) collective-permute-start(bf16[128,512]{1,0:T(8,128)(2,1)S(1)} %get-tuple-element.86), channel_id=1, source_target_pairs={{0,4},{1,5},{2,6},{3,7},{4,8},{5,9},{6,10},{7,11},{8,12},{9,13},{1... | collective-permute-start | bytes 393224 | tf_op jit(solution)/shard_map/ppermute | solution.py:172
  323.8 17.2 %collective-permute-start.43 = (bf16[128,512]{1,0:T(8,128)(2,1)S(1)}, bf16[128,512]{1,0:T(8,128)(2,1)S(1)}, u32[]{:S(2)}, u32[]{:S(2)}) collective-permute-start(bf16[128,512]{1,0:T(8,128)(2,1)S(1)} %get-tuple-element.84), channel_id=1, source_target_pairs={{0,12},{1,13},{2,14},{3,15},{4,0},{5,1},{6,2},{7,3},{8,4},{9,5},{1... | collective-permute-start | bytes 393224 | tf_op jit(solution)/shard_map/ppermute | solution.py:172
  323.9 22.5 %collective-permute-start.42 = (bf16[128,512]{1,0:T(8,128)(2,1)S(1)}, bf16[128,512]{1,0:T(8,128)(2,1)S(1)}, u32[]{:S(2)}, u32[]{:S(2)}) collective-permute-start(bf16[128,512]{1,0:T(8,128)(2,1)S(1)} %get-tuple-element.85), channel_id=1, source_target_pairs={{0,8},{1,9},{2,10},{3,11},{4,12},{5,13},{6,14},{7,15},{8,0},{9,1},... | collective-permute-start | bytes 393224 | tf_op jit(solution)/shard_map/ppermute | solution.py:172
  329.8 16.6 %collective-permute-start.41 = (bf16[128,512]{1,0:T(8,128)(2,1)S(1)}, bf16[128,512]{1,0:T(8,128)(2,1)S(1)}, u32[]{:S(2)}, u32[]{:S(2)}) collective-permute-start(bf16[128,512]{1,0:T(8,128)(2,1)S(1)} %get-tuple-element.83), channel_id=1, source_target_pairs={{0,4},{1,5},{2,6},{3,7},{4,8},{5,9},{6,10},{7,11},{8,12},{9,13},{1... | collective-permute-start | bytes 393224 | tf_op jit(solution)/shard_map/ppermute | solution.py:172
  340.7 6.8 %collective-permute-start.39 = (bf16[128,512]{1,0:T(8,128)(2,1)S(1)}, bf16[128,512]{1,0:T(8,128)(2,1)S(1)}, u32[]{:S(2)}, u32[]{:S(2)}) collective-permute-start(bf16[128,512]{1,0:T(8,128)(2,1)S(1)} %get-tuple-element.81), channel_id=1, source_target_pairs={{0,12},{1,13},{2,14},{3,15},{4,0},{5,1},{6,2},{7,3},{8,4},{9,5},{1... | collective-permute-start | bytes 393224 | tf_op jit(solution)/shard_map/ppermute | solution.py:172
  340.7 12.0 %collective-permute-start.38 = (bf16[128,512]{1,0:T(8,128)(2,1)S(1)}, bf16[128,512]{1,0:T(8,128)(2,1)S(1)}, u32[]{:S(2)}, u32[]{:S(2)}) collective-permute-start(bf16[128,512]{1,0:T(8,128)(2,1)S(1)} %get-tuple-element.82), channel_id=1, source_target_pairs={{0,8},{1,9},{2,10},{3,11},{4,12},{5,13},{6,14},{7,15},{8,0},{9,1},... | collective-permute-start | bytes 393224 | tf_op jit(solution)/shard_map/ppermute | solution.py:172
  341.1 11.7 %collective-permute-start.37 = (bf16[128,512]{1,0:T(8,128)(2,1)S(1)}, bf16[128,512]{1,0:T(8,128)(2,1)S(1)}, u32[]{:S(2)}, u32[]{:S(2)}) collective-permute-start(bf16[128,512]{1,0:T(8,128)(2,1)S(1)} %get-tuple-element.80), channel_id=1, source_target_pairs={{0,4},{1,5},{2,6},{3,7},{4,8},{5,9},{6,10},{7,11},{8,12},{9,13},{1... | collective-permute-start | bytes 393224 | tf_op jit(solution)/shard_map/ppermute | solution.py:172

commit v3 on v2

--- a/solution.py
+++ b/solution.py
@@ -6,7 +6,6 @@
 from jax.sharding import PartitionSpec as P
 
 VMEM_BYTES = 48 * 2**20
-CHUNKS = 4
 
 
 def hidden_kernel(rows_ref, gate_ref, up_ref, activ_ref, by_gate_ref, by_up_ref):
@@ -150,41 +149,46 @@
     )
 
 
+def cut_columns(width, eighths):
+    eighth = width // 8
+    return [(lo * eighth, hi * eighth) for lo, hi in eighths]
+
+
+def join_columns(chunks, parts):
+    return jnp.concatenate([part for _, part in sorted(zip(chunks, parts), key=lambda p: p[0])], axis=1)
+
+
+def after(values, *others):
+    return lax.optimization_barrier((values, *others))[0]
+
+
+class Queue:
+    def __init__(self, depth):
+        self.depth = depth
+        self.results = []
+
+    def send(self, values, pairs, *others):
+        waits = list(others) + self.results[: max(0, len(self.results) - self.depth + 1)]
+        if waits:
+            values = after(values, *waits)
+        self.results.append(lax.ppermute(values, "expert", pairs))
+        return self.results[-1]
+
+
 def on_device_dense(tokens, cotangent, expert_ids, probs, gate_weight, up_weight, down_weight):
     local_count, hidden, width = down_weight.shape
     devices = lax.axis_size("expert")
     layers = devices // 4
     experts = local_count * devices
     block = tokens.shape[0]
-    columns = width // CHUNKS
+    chunks = cut_columns(width, ((4, 8), (0, 3), (3, 4)))
+    back_chunks = cut_columns(width, ((0, 3), (3, 6), (6, 8)))
     me = lax.axis_index("expert")
-
-    def after(values, *others):
-        return lax.optimization_barrier((values, *others))[0]
-
-    def to_twin(values):
-        return lax.ppermute(values, "expert", [(d, d ^ 1) for d in range(devices)])
-
-    def to_side(values):
-        return lax.ppermute(values, "expert", [(d, d ^ 2) for d in range(devices)])
-
-    def to_layer(values, step):
-        return lax.ppermute(values, "expert", [(d, (d + 4 * step) % devices) for d in range(devices)])
-
-    def gather(values):
-        near = [values] + [to_layer(values, -k) for k in range(1, layers)]
-        return near, jnp.concatenate(near + [to_side(v) for v in near], axis=0)
-
-    def reduce_start(keep, send):
-        come = to_side(send).astype(jnp.float32)
-        total = keep + come
-        own = total[:block]
-        return [own] + [
-            to_layer(total[k * block : (k + 1) * block].astype(jnp.bfloat16), k) for k in range(1, layers)
-        ]
-
-    def reduce_end(parts):
-        return jnp.concatenate([sum(p.astype(jnp.float32) for p in part) for part in parts], axis=1)
+    to_twin = [(d, d ^ 1) for d in range(devices)]
+    to_side = [(d, d ^ 2) for d in range(devices)]
+    to_layer = [[(d, (d + 4 * k) % devices) for d in range(devices)] for k in range(layers)]
+    hops = sorted(range(1, layers), key=lambda k: min(k, layers - k))
+    twins, sides, across = Queue(2), Queue(2), Queue(2)
 
     labels = lax.broadcasted_iota(jnp.int32, (1, 1, experts), 2)
     weight = jnp.sum(jnp.where(expert_ids[:, :, None] == labels, probs[:, :, None], 0.0), axis=1)
@@ -195,14 +199,27 @@
     terms = [t.astype(jnp.bfloat16) for t in (first, second, third)]
     rows = jnp.concatenate([tokens] + terms + [spare], axis=1)
 
-    near, all_rows = gather(rows)
-    other_gate = to_twin(gate_weight)
-    other_up = to_twin(up_weight)
-    other_down = []
-    for c in range(CHUNKS):
-        piece = down_weight[:, :, c * columns : (c + 1) * columns]
-        other_down.append(to_twin(after(piece, other_gate if 2 * c < CHUNKS else other_up)))
-    _, all_grads = gather(after(cotangent, near[layers // 2]))
+    other_gate = twins.send(gate_weight, to_twin)
+    near_rows, far_rows = {0: rows}, {}
+    near_grads, far_grads = {0: cotangent}, {}
+    for k in hops:
+        near_rows[k] = across.send(rows, to_layer[-k])
+    for k in hops:
+        near_grads[k] = across.send(cotangent, to_layer[-k])
+    early = [0] + hops[:-1]
+    for k in early:
+        far_rows[k] = sides.send(near_rows[k], to_side)
+    other_up = twins.send(up_weight, to_twin, far_rows[early[-1]])
+    far_grads[0] = sides.send(cotangent, to_side)
+    far_rows[hops[-1]] = sides.send(near_rows[hops[-1]], to_side)
+    for k in hops:
+        far_grads[k] = sides.send(near_grads[k], to_side)
+    all_rows = jnp.concatenate(
+        [near_rows[k] for k in range(layers)] + [far_rows[k] for k in range(layers)], axis=0
+    )
+    all_grads = jnp.concatenate(
+        [near_grads[k] for k in range(layers)] + [far_grads[k] for k in range(layers)], axis=0
+    )
 
     terms = [
         all_rows[:, width + t * experts : width + (t + 1) * experts].astype(jnp.float32) for t in range(3)
@@ -220,25 +237,44 @@
         flat = down.reshape(local_count * hidden, down.shape[2])
         return lax.dot_general(grads, flat, (((1,), (1,)), ((), ())), preferred_element_type=jnp.float32)
 
+    def reduce(keep, send):
+        total = keep + sides.send(send, to_side).astype(jnp.float32)
+        parts = [total[:block]]
+        for k in hops:
+            piece = total[k * block : (k + 1) * block].astype(jnp.bfloat16)
+            parts.append(across.send(piece, to_layer[k]))
+        return sum(p.astype(jnp.float32) for p in parts)
+
     activ, by_gate, by_up = hidden_forward(all_rows, gate_weight, up_weight)
     other_activ, other_by_gate, other_by_up = hidden_forward(all_rows, other_gate, other_up)
     grad = grad_act(all_grads, down_weight)
     own_grads = [(grad * by).astype(jnp.bfloat16) for by in (by_gate, by_up)]
     mixed = []
     other_grad = None
-    for c in range(CHUNKS):
-        keep, send = mix_columns(weight, activ, other_activ, down_weight, other_down[c], c)
-        mixed.append(reduce_start(keep, send))
-        term = grad_act(all_grads[:, c * columns : (c + 1) * columns], other_down[c])
+    other_down = [
+        twins.send(down_weight[:, :, lo:hi], to_twin, far_rows[hops[-1]]) for lo, hi in chunks[:2]
+    ]
+    last = other_activ
+    for c, (lo, hi) in enumerate(chunks):
+        down = after(other_down[c], last)
+        halves = mix_columns(weight, activ, other_activ, down_weight, down, lo // (hi - lo))
+        last = halves[1]
+        mixed.append(reduce(*halves))
+        for ahead in chunks[c + 2 : c + 3]:
+            other_down.append(twins.send(down_weight[:, :, ahead[0] : ahead[1]], to_twin, last))
+        term = grad_act(all_grads[:, lo:hi], down)
         other_grad = term if other_grad is None else other_grad + term
     other_grads = [(other_grad * by).astype(jnp.bfloat16) for by in (other_by_gate, other_by_up)]
+    own_weights, other_weights = (gate_weight, up_weight), (other_gate, other_up)
     back = []
-    for c in range(CHUNKS):
-        keep, send = back_columns(
-            weight, own_grads, (gate_weight, up_weight), other_grads, (other_gate, other_up), c, columns
+    for lo, hi in back_chunks:
+        columns = hi - lo
+        halves = back_columns(
+            after(weight, last), own_grads, own_weights, other_grads, other_weights, lo // columns, columns
         )
-        back.append(reduce_start(keep, send))
-    return (reduce_end(mixed), reduce_end(back))
+        last = halves[1]
+        back.append(reduce(*halves))
+    return (join_columns(chunks, mixed), join_columns(back_chunks, back))
 
 
 def route_slots(expert_ids, local_count, device_count, capacity):

time: 355 us -> 304 us (0.86)
  waiting for transfers between devices: 202 us -> 148 us
  local copies, waits for them, and re-layouts: 15.1 us -> 21.4 us
  starting transfers between devices: 71.9 us -> 66.9 us
    ppermute x52 -> x43, waiting for transfers between devices: 202 us -> 148 us  [send(): self.results.append(lax.ppermute(values, 'expert', pairs))]
    ppermute x52 -> x43, starting transfers between devices: 71.9 us -> 66.9 us  [send(): self.results.append(lax.ppermute(values, 'expert', pairs))]
    unnamed x34 -> x42, local copies, waits for them, and re-layouts: 9.31 us -> 13.7 us
    dot_general x5 -> x4, matrix products: 9.03 us -> 11.3 us  [grad_act(): lax.dot_general(grads, flat, (((1,), (1,)), ((), ())), preferred_element_...]
    pallas_call x8 -> x6, Pallas kernels: 30.9 us -> 30.4 us  [halves_call(): pl.pallas_call(kernel, grid=(2,), in_specs=in_specs, out_specs=[pl.BlockS...]
  transfers between devices with their start and end apart: 52 -> 43, of which waited for: 23 -> 23; matrix products, arithmetic and copies ran while one was open for 8% -> 11% of each run, Pallas kernels for 13% -> 15%
where the time goes in v3:
time: 304 us; the launch traced here: 303 us
  waiting for transfers between devices  148 us (49%)
  starting transfers between devices  66.9 us (22%)
  Pallas kernels  46 us (15%)
  local copies, waits for them, and re-layouts  21.4 us (7%)
  matrix products  11.3 us (4%)
  other arithmetic  7.79 us (3%)
    ppermute x43, waiting for transfers between devices, send(): self.results.append(lax.ppermute(values, 'expert', pairs))  148 us
    ppermute x43, starting transfers between devices, send(): self.results.append(lax.ppermute(values, 'expert', pairs))  66.9 us
    pallas_call x6, Pallas kernels, halves_call(): pl.pallas_call(kernel, grid=(2,), in_specs=in_specs, out_specs=[pl.BlockS...  30.4 us
    pallas_call x2, Pallas kernels, hidden_forward(): pl.pallas_call(hidden_kernel, grid=(count // tile,), in_specs=[pl.BlockSp...  15.6 us
    unnamed x42, local copies, waits for them, and re-layouts  13.7 us
    dot_general x4, matrix products, grad_act(): lax.dot_general(grads, flat, (((1,), (1,)), ((), ())), preferred_element_...  11.3 us
  transfers between devices with their start and end apart: 43, of which 23 were waited for; matrix products, arithmetic and copies ran while one was open for 11% of the time, Pallas kernels for 15%

profile of v3, /device:TPU:0, one launch (start us, length us, event | category | flops | bytes accessed | tf_op | source)
XLA Modules:
  0.0 302.8 jit_solution(4197488192126377448)
XLA Ops:
  1.8 1.2 concatenate.18
  3.0 3.1 %collective-permute-start.2 = (bf16[128,2176]{1,0:T(8,128)(2,1)S(1)}, bf16[128,2176]{1,0:T(8,128)(2,1)S(1)}, u32[]{:S(2)}, u32[]{:S(2)}) collective-permute-start(bf16[128,2176]{1,0:T(8,128)(2,1)S(1)} %concatenate.18), channel_id=1, source_target_pairs={{0,4},{1,5},{2,6},{3,7},{4,8},{5,9},{6,10},{7,11},{8,12},{9,13},{1... | collective-permute-start | bytes 1671176 | tf_op jit(solution)/shard_map/ppermute | solution.py:174
  6.0 2.1 collective-permute-start
  8.1 1.7 collective-permute-start.3
  9.8 1.5 collective-permute-start.7
  12.3 2.1 slice.120
  16.3 5.3 %collective-permute-done.2 = bf16[128,2176]{1,0:T(8,128)(2,1)S(1)} collective-permute-done((bf16[128,2176]{1,0:T(8,128)(2,1)S(1)}, bf16[128,2176]{1,0:T(8,128)(2,1)S(1)}, u32[]{:S(2)}, u32[]{:S(2)}) %collective-permute-start.2) | collective-permute-done | bytes 557088 | tf_op jit(solution)/shard_map/ppermute | solution.py:174
  21.6 10.6 %collective-permute-done = bf16[128,2176]{1,0:T(8,128)(2,1)} collective-permute-done((bf16[128,2176]{1,0:T(8,128)(2,1)S(1)}, bf16[128,2176]{1,0:T(8,128)(2,1)}, u32[]{:S(2)}, u32[]{:S(2)}) %collective-permute-start) | collective-permute-done | bytes 557088 | tf_op jit(solution)/shard_map/ppermute | solution.py:174
  32.2 2.2 collective-permute-start.12
  35.5 1.6 collective-permute-start.5
  38.0 1.9 constant_dynamic-update-slice_fusion.6
  39.9 7.2 %collective-permute-done.12 = bf16[128,2048]{1,0:T(8,128)(2,1)S(1)} collective-permute-done((bf16[128,2048]{1,0:T(8,128)(2,1)}, bf16[128,2048]{1,0:T(8,128)(2,1)S(1)}, u32[]{:S(2)}, u32[]{:S(2)}) %collective-permute-start.12) | collective-permute-done | bytes 524320 | tf_op jit(solution)/shard_map/ppermute | solution.py:174
  47.2 4.0 %collective-permute-done.5 = bf16[128,2176]{1,0:T(8,128)(2,1)S(1)} collective-permute-done((bf16[128,2176]{1,0:T(8,128)(2,1)S(1)}, bf16[128,2176]{1,0:T(8,128)(2,1)S(1)}, u32[]{:S(2)}, u32[]{:S(2)}) %collective-permute-start.5) | collective-permute-done | bytes 557088 | tf_op jit(solution)/shard_map/ppermute | solution.py:174
  51.2 19.5 %collective-permute-done.1 = bf16[128,2176]{1,0:T(8,128)(2,1)S(1)} collective-permute-done((bf16[128,2176]{1,0:T(8,128)(2,1)S(1)}, bf16[128,2176]{1,0:T(8,128)(2,1)S(1)}, u32[]{:S(2)}, u32[]{:S(2)}) %collective-permute-start.1) | collective-permute-done | bytes 557088 | tf_op jit(solution)/shard_map/ppermute | solution.py:174
  70.7 2.9 collective-permute-start.16
  73.5 1.5 collective-permute-start.11
  77.3 1.9 constant_dynamic-update-slice_fusion.3
  80.0 8.4 %collective-permute-done.11 = bf16[128,2048]{1,0:T(8,128)(2,1)S(1)} collective-permute-done((bf16[128,2048]{1,0:T(8,128)(2,1)S(1)}, bf16[128,2048]{1,0:T(8,128)(2,1)S(1)}, u32[]{:S(2)}, u32[]{:S(2)}) %collective-permute-start.11) | collective-permute-done | bytes 524320 | tf_op jit(solution)/shard_map/ppermute | solution.py:174
  88.4 1.5 collective-permute-start.8
  89.9 17.9 %collective-permute-done.16 = bf16[128,2048]{1,0:T(8,128)(2,1)S(1)} collective-permute-done((bf16[128,2048]{1,0:T(8,128)(2,1)S(1)}, bf16[128,2048]{1,0:T(8,128)(2,1)S(1)}, u32[]{:S(2)}, u32[]{:S(2)}) %collective-permute-start.16) | collective-permute-done | bytes 524320 | tf_op jit(solution)/shard_map/ppermute | solution.py:174
  107.8 1.5 collective-permute-start.13
  110.5 1.3 copy-done.12
  112.6 7.8 %hidden_forward.2 = (bf16[1024,512]{1,0:T(8,128)(2,1)S(1)}, f32[1024,512]{1,0:T(8,128)S(1)}, f32[1024,512]{1,0:T(8,128)S(1)}) custom-call(bf16[1024,2176]{1,0:T(8,128)(2,1)} %constant_dynamic-update-slice_fusion.rows_ref, bf16[2,2048,256]{2,1,0:T(8,128)(2,1)} %refs_2_.5, bf16[2,2048,256]{2,1,0:T(8,128)(2,1)} %refs_3_.5), custom_call_target="tpu_custom_call" | custom-call | flops 4294967296 | bytes 13631488 | tf_op jit(solution)/shard_map/hidden_forward/pallas_call | solution.py:72
  121.6 1.5 collective-permute-start.17
  123.1 1.4 convert_add_fusion.6
  125.7 1.6 collective-permute-start.10
  128.1 8.3 %collective-permute-done.17 = bf16[128,2048]{1,0:T(8,128)(2,1)S(1)} collective-permute-done((bf16[128,2048]{1,0:T(8,128)(2,1)S(1)}, bf16[128,2048]{1,0:T(8,128)(2,1)S(1)}, u32[]{:S(2)}, u32[]{:S(2)}) %collective-permute-start.17) | collective-permute-done | bytes 524320 | tf_op jit(solution)/shard_map/ppermute | solution.py:174
  137.3 8.4 %collective-permute-done.15 = bf16[128,2048]{1,0:T(8,128)(2,1)S(1)} collective-permute-done((bf16[128,2048]{1,0:T(8,128)(2,1)S(1)}, bf16[128,2048]{1,0:T(8,128)(2,1)S(1)}, u32[]{:S(2)}, u32[]{:S(2)}) %collective-permute-start.15) | collective-permute-done | bytes 524320 | tf_op jit(solution)/shard_map/ppermute | solution.py:174
  146.6 4.5 %multiply_convert_fusion.2 = (bf16[1024,512]{1,0:T(8,128)(2,1)S(1)}, bf16[1024,512]{1,0:T(8,128)(2,1)S(1)}) fusion(f32[1024,512]{1,0:T(8,128)S(1)} %get-tuple-element.103, f32[1024,512]{1,0:T(8,128)S(1)} %get-tuple-element.102, bf16[1024,2048]{1,0:T(8,128)(2,1)} %constant_dynamic-update-slice_fusion.8, bf16[512,2048]{1,0:T(8,128)(2,1)S(1)} %bitcast.9), kind=kOutput, calls=%fused_computation.5 | convolution fusion | flops 2149580800 | bytes 12582912 | tf_op jit(solution)/shard_map/dot_general | solution.py:238
  151.2 1.6 collective-permute-start.9
  152.7 7.8 %hidden_forward.3 = (bf16[1024,512]{1,0:T(8,128)(2,1)S(1)}, f32[1024,512]{1,0:T(8,128)S(1)}, f32[1024,512]{1,0:T(8,128)S(1)}) custom-call(bf16[1024,2176]{1,0:T(8,128)(2,1)} %constant_dynamic-update-slice_fusion.rows_ref, bf16[2,2048,256]{2,1,0:T(8,128)(2,1)} %collective-permute-done.7.gate_ref.refs_6_, ...), custom_call_target="tpu_custom_call" | custom-call | flops 4294967296 | bytes 13631488 | tf_op jit(solution)/shard_map/hidden_forward/pallas_call | solution.py:72
  160.6 6.0 %mix_columns.3 = (f32[512,1024]{1,0:T(8,128)}, bf16[512,1024]{1,0:T(8,128)(2,1)}) custom-call(f32[1024,4]{1,0:T(8,128)S(1)} %pad_maximum_fusion.2.weight_ref, bf16[1024,512]{1,0:T(8,128)(2,1)S(1)} %get-tuple-element.67.own_ref, bf16[1024,512]{1,0:T(8,128)(2,1)S(1)} %get-tuple-element.69.other_ref, bf16[2,256,2048]{2,1,0:T(8,128)(2,1)} %own_down_ref.5, ...), custom_call_target="tpu_custom_call" | custom-call | flops 2147483648 | bytes 5771264 | tf_op jit(solution)/shard_map/mix_columns/pallas_call | solution.py:94
  167.1 2.6 fusion
  169.7 1.5 collective-permute-start.19
  171.2 3.8 %collective-permute-done.9.other_down_ref = bf16[2,256,768]{2,1,0:T(8,128)(2,1)S(1)} collective-permute-done((bf16[2,256,768]{2,1,0:T(8,128)(2,1)}, bf16[2,256,768]{2,1,0:T(8,128)(2,1)S(1)}, u32[]{:S(2)}, u32[]{:S(2)}) %collective-permute-start.9) | collective-permute-done | bytes 786464 | tf_op jit(solution)/shard_map/ppermute | solution.py:174
  175.0 4.3 %mix_columns.4 = (f32[512,768]{1,0:T(8,128)S(1)}, bf16[512,768]{1,0:T(8,128)(2,1)}) custom-call(f32[1024,4]{1,0:T(8,128)S(1)} %pad_maximum_fusion.2.weight_ref, bf16[1024,512]{1,0:T(8,128)(2,1)S(1)} %get-tuple-element.67.own_ref, bf16[1024,512]{1,0:T(8,128)(2,1)S(1)} %get-tuple-element.69.other_ref, bf16[2,256,2048]{2,1,0:T(8,128)(2,1)} %own_down_ref.5, ...), custom_call_target="tpu_custom_call" | custom-call | flops 1610612736 | bytes 4853760 | tf_op jit(solution)/shard_map/mix_columns/pallas_call | solution.py:94
  181.5 1.6 collective-permute-start.18
  183.1 2.4 fusion.2
  185.5 1.8 multiply_convert_fusion
  187.3 7.6 %back_columns.3 = (f32[512,768]{1,0:T(8,128)}, bf16[512,768]{1,0:T(8,128)(2,1)S(1)}) custom-call(f32[1024,4]{1,0:T(8,128)S(1)} %pad_maximum_fusion.2.weight_ref, bf16[1024,512]{1,0:T(8,128)(2,1)S(1)} %get-tuple-element.141.refs_0_, bf16[1024,512]{1,0:T(8,128)(2,1)S(1)} %get-tuple-element.140.refs_1_, bf16[2,2048,256]{2,1,0:T(8,128)(2,1)} %refs_2_.5, ...), custom_call_target="tpu_custom_call" | custom-call | flops 3221225472 | bytes 8654848 | tf_op jit(solution)/shard_map/back_columns/pallas_call | solution.py:94
  196.1 1.8 fusion.26
  198.4 1.2 collective-permute-start.27
  199.6 6.9 %back_columns.4 = (f32[512,768]{1,0:T(8,128)}, bf16[512,768]{1,0:T(8,128)(2,1)S(1)}) custom-call(f32[1024,4]{1,0:T(8,128)S(1)} %pad_maximum_fusion.2.weight_ref, bf16[1024,512]{1,0:T(8,128)(2,1)S(1)} %get-tuple-element.141.refs_0_, bf16[1024,512]{1,0:T(8,128)(2,1)S(1)} %get-tuple-element.140.refs_1_, bf16[2,2048,256]{2,1,0:T(8,128)(2,1)} %refs_2_.5, ...), custom_call_target="tpu_custom_call" | custom-call | flops 3221225472 | bytes 8654848 | tf_op jit(solution)/shard_map/back_columns/pallas_call | solution.py:94
  206.5 4.6 %back_columns.5 = (f32[512,512]{1,0:T(8,128)S(1)}, bf16[512,512]{1,0:T(8,128)(2,1)S(1)}) custom-call(f32[1024,4]{1,0:T(8,128)S(1)} %pad_maximum_fusion.2.weight_ref, bf16[1024,512]{1,0:T(8,128)(2,1)S(1)} %get-tuple-element.141.refs_0_, bf16[1024,512]{1,0:T(8,128)(2,1)S(1)} %get-tuple-element.140.refs_1_, bf16[2,2048,256]{2,1,0:T(8,128)(2,1)} %refs_2_.5, ...), custom_call_target="tpu_custom_call" | custom-call | flops 2147483648 | bytes 7868416 | tf_op jit(solution)/shard_map/back_columns/pallas_call | solution.py:94
  211.1 3.8 %collective-permute-start.21 = (bf16[128,1024]{1,0:T(8,128)(2,1)S(1)}, bf16[128,1024]{1,0:T(8,128)(2,1)S(1)}, u32[]{:S(2)}, u32[]{:S(2)}) collective-permute-start(bf16[128,1024]{1,0:T(8,128)(2,1)S(1)} %get-tuple-element.88), channel_id=1, source_target_pairs={{0,12},{1,13},{2,14},{3,15},{4,0},{5,1},{6,2},{7,3},{8,4},{9,5},{1... | collective-permute-start | bytes 786440 | tf_op jit(solution)/shard_map/ppermute | solution.py:174
  215.5 6.0 %collective-permute-done.21 = bf16[128,1024]{1,0:T(8,128)(2,1)S(1)} collective-permute-done((bf16[128,1024]{1,0:T(8,128)(2,1)S(1)}, bf16[128,1024]{1,0:T(8,128)(2,1)S(1)}, u32[]{:S(2)}, u32[]{:S(2)}) %collective-permute-start.21) | collective-permute-done | bytes 262176 | tf_op jit(solution)/shard_map/ppermute | solution.py:174
  221.5 2.5 collective-permute-start.22
  224.7 6.6 %collective-permute-done.23 = bf16[128,1024]{1,0:T(8,128)(2,1)S(1)} collective-permute-done((bf16[128,1024]{1,0:T(8,128)(2,1)S(1)}, bf16[128,1024]{1,0:T(8,128)(2,1)S(1)}, u32[]{:S(2)}, u32[]{:S(2)}) %collective-permute-start.23) | collective-permute-done | bytes 262176 | tf_op jit(solution)/shard_map/ppermute | solution.py:174
  231.3 1.2 collective-permute-start.24
  233.0 6.9 %collective-permute-start.25 = (bf16[128,768]{1,0:T(8,128)(2,1)S(1)}, bf16[128,768]{1,0:T(8,128)(2,1)S(1)}, u32[]{:S(2)}, u32[]{:S(2)}) collective-permute-start(bf16[128,768]{1,0:T(8,128)(2,1)S(1)} %get-tuple-element.92), channel_id=1, source_target_pairs={{0,8},{1,9},{2,10},{3,11},{4,12},{5,13},{6,14},{7,15},{8,0},{9,1},... | collective-permute-start | bytes 589832 | tf_op jit(solution)/shard_map/ppermute | solution.py:174
  240.0 7.0 %collective-permute-done.25 = bf16[128,768]{1,0:T(8,128)(2,1)S(1)} collective-permute-done((bf16[128,768]{1,0:T(8,128)(2,1)S(1)}, bf16[128,768]{1,0:T(8,128)(2,1)S(1)}, u32[]{:S(2)}, u32[]{:S(2)}) %collective-permute-start.25) | collective-permute-done | bytes 196640 | tf_op jit(solution)/shard_map/ppermute | solution.py:174
  248.0 2.0 collective-permute-start.29
  250.1 5.5 %collective-permute-done.30 = bf16[128,256]{1,0:T(8,128)(2,1)S(1)} collective-permute-done((bf16[128,256]{1,0:T(8,128)(2,1)S(1)}, bf16[128,256]{1,0:T(8,128)(2,1)S(1)}, u32[]{:S(2)}, u32[]{:S(2)}) %collective-permute-start.30) | collective-permute-done | bytes 65568 | tf_op jit(solution)/shard_map/ppermute | solution.py:174
  256.0 1.8 collective-permute-start.32
  257.8 2.0 collective-permute-start.33
  260.6 3.7 %collective-permute-done.32 = bf16[128,768]{1,0:T(8,128)(2,1)S(1)} collective-permute-done((bf16[128,768]{1,0:T(8,128)(2,1)S(1)}, bf16[128,768]{1,0:T(8,128)(2,1)S(1)}, u32[]{:S(2)}, u32[]{:S(2)}) %collective-permute-start.32) | collective-permute-done | bytes 196640 | tf_op jit(solution)/shard_map/ppermute | solution.py:174
  264.3 3.0 %collective-permute-start.34 = (bf16[128,768]{1,0:T(8,128)(2,1)S(1)}, bf16[128,768]{1,0:T(8,128)(2,1)S(1)}, u32[]{:S(2)}, u32[]{:S(2)}) collective-permute-start(bf16[128,768]{1,0:T(8,128)(2,1)S(1)} %get-tuple-element.111), channel_id=1, source_target_pairs={{0,8},{1,9},{2,10},{3,11},{4,12},{5,13},{6,14},{7,15},{8,0},{9,1},... | collective-permute-start | bytes 589832 | tf_op jit(solution)/shard_map/ppermute | solution.py:174
  269.4 9.1 %collective-permute-done.34 = bf16[128,768]{1,0:T(8,128)(2,1)S(1)} collective-permute-done((bf16[128,768]{1,0:T(8,128)(2,1)S(1)}, bf16[128,768]{1,0:T(8,128)(2,1)S(1)}, u32[]{:S(2)}, u32[]{:S(2)}) %collective-permute-start.34) | collective-permute-done | bytes 196640 | tf_op jit(solution)/shard_map/ppermute | solution.py:174
  278.6 2.5 collective-permute-start.38
  281.8 7.3 %collective-permute-done.37 = bf16[128,768]{1,0:T(8,128)(2,1)S(1)} collective-permute-done((bf16[128,768]{1,0:T(8,128)(2,1)S(1)}, bf16[128,768]{1,0:T(8,128)(2,1)S(1)}, u32[]{:S(2)}, u32[]{:S(2)}) %collective-permute-start.37) | collective-permute-done | bytes 196640 | tf_op jit(solution)/shard_map/ppermute | solution.py:174
  289.0 3.7 %collective-permute-start.40 = (bf16[128,512]{1,0:T(8,128)(2,1)S(1)}, bf16[128,512]{1,0:T(8,128)(2,1)S(1)}, u32[]{:S(2)}, u32[]{:S(2)}) collective-permute-start(bf16[128,512]{1,0:T(8,128)(2,1)S(1)} %get-tuple-element.123), channel_id=1, source_target_pairs={{0,4},{1,5},{2,6},{3,7},{4,8},{5,9},{6,10},{7,11},{8,12},{9,13},{1... | collective-permute-start | bytes 393224 | tf_op jit(solution)/shard_map/ppermute | solution.py:174
  293.0 2.8 collective-permute-done.40
  295.8 2.1 collective-permute-start.42
  298.0 3.6 %collective-permute-done.42 = bf16[128,512]{1,0:T(8,128)(2,1)S(1)} collective-permute-done((bf16[128,512]{1,0:T(8,128)(2,1)S(1)}, bf16[128,512]{1,0:T(8,128)(2,1)S(1)}, u32[]{:S(2)}, u32[]{:S(2)}) %collective-permute-start.42) | collective-permute-done | bytes 131104 | tf_op jit(solution)/shard_map/ppermute | solution.py:174
  (111 shorter events, 28.7 us)
Async XLA Ops:
  0.6 13.7 %copy-start.1 = (bf16[2,256,2048]{2,1,0:T(8,128)(2,1)S(1)}, bf16[2,256,2048]{2,1,0:T(8,128)(2,1)}, u32[]{:S(2)}) copy-start(bf16[2,256,2048]{2,1,0:T(8,128)(2,1)} %own_down_ref.5) | copy-start | bytes 6291460
  3.0 18.6 %collective-permute-start.2 = (bf16[128,2176]{1,0:T(8,128)(2,1)S(1)}, bf16[128,2176]{1,0:T(8,128)(2,1)S(1)}, u32[]{:S(2)}, u32[]{:S(2)}) collective-permute-start(bf16[128,2176]{1,0:T(8,128)(2,1)S(1)} %concatenate.18), channel_id=1, source_target_pairs={{0,4},{1,5},{2,6},{3,7},{4,8},{5,9},{6,10},{7,11},{8,12},{9,13},{1... | collective-permute-start | bytes 1671176 | tf_op jit(solution)/shard_map/ppermute | solution.py:174
  6.0 26.1 %collective-permute-start = (bf16[128,2176]{1,0:T(8,128)(2,1)S(1)}, bf16[128,2176]{1,0:T(8,128)(2,1)}, u32[]{:S(2)}, u32[]{:S(2)}) collective-permute-start(bf16[128,2176]{1,0:T(8,128)(2,1)S(1)} %concatenate.18), channel_id=1, source_target_pairs={{0,12},{1,13},{2,14},{3,15},{4,0},{5,1},{6,2},{7,3},{8,4},{9,5},{1... | collective-permute-start | bytes 1671176 | tf_op jit(solution)/shard_map/ppermute | solution.py:174
  8.1 27.4 %collective-permute-start.3 = (bf16[128,2176]{1,0:T(8,128)(2,1)S(1)}, bf16[128,2176]{1,0:T(8,128)(2,1)}, u32[]{:S(2)}, u32[]{:S(2)}) collective-permute-start(bf16[128,2176]{1,0:T(8,128)(2,1)S(1)} %concatenate.18), channel_id=1, source_target_pairs={{0,2},{1,3},{2,0},{3,1},{4,6},{5,7},{6,4},{7,5},{8,10},{9,11},{10,... | collective-permute-start | bytes 1671176 | tf_op jit(solution)/shard_map/ppermute | solution.py:174
  9.8 115.8 %collective-permute-start.7 = (bf16[2,2048,256]{2,1,0:T(8,128)(2,1)}, bf16[2,2048,256]{2,1,0:T(8,128)(2,1)}, u32[]{:S(2)}, u32[]{:S(2)}) collective-permute-start(bf16[2,2048,256]{2,1,0:T(8,128)(2,1)} %refs_2_.5), channel_id=1, source_target_pairs={{0,1},{1,0},{2,3},{3,2},{4,5},{5,4},{6,7},{7,6},{8,9},{9,8},{10,11... | collective-permute-start | bytes 6291464 | tf_op jit(solution)/shard_map/ppermute | solution.py:174
  15.4 55.3 %copy-start.11 = (bf16[128,2048]{1,0:T(8,128)(2,1)S(1)}, bf16[128,2048]{1,0:T(8,128)(2,1)}, u32[]{:S(2)}) copy-start(bf16[128,2048]{1,0:T(8,128)(2,1)} %param.8) | copy-start | bytes 1572868
  15.4 73.0 %copy-start.5 = (bf16[2,2048,256]{2,1,0:T(8,128)(2,1)S(1)}, bf16[2,2048,256]{2,1,0:T(8,128)(2,1)}, u32[]{:S(2)}) copy-start(bf16[2,2048,256]{2,1,0:T(8,128)(2,1)} %refs_3_.5) | copy-start | bytes 6291460
  32.2 15.0 %collective-permute-start.12 = (bf16[128,2048]{1,0:T(8,128)(2,1)}, bf16[128,2048]{1,0:T(8,128)(2,1)S(1)}, u32[]{:S(2)}, u32[]{:S(2)}) collective-permute-start(bf16[128,2048]{1,0:T(8,128)(2,1)} %param.8), channel_id=1, source_target_pairs={{0,12},{1,13},{2,14},{3,15},{4,0},{5,1},{6,2},{7,3},{8,4},{9,5},{1... | collective-permute-start | bytes 1572872 | tf_op jit(solution)/shard_map/ppermute | solution.py:174
  35.5 15.6 %collective-permute-start.5 = (bf16[128,2176]{1,0:T(8,128)(2,1)S(1)}, bf16[128,2176]{1,0:T(8,128)(2,1)S(1)}, u32[]{:S(2)}, u32[]{:S(2)}) collective-permute-start(bf16[128,2176]{1,0:T(8,128)(2,1)S(1)} %collective-permute-done.2), channel_id=1, source_target_pairs={{0,2},{1,3},{2,0},{3,1},{4,6},{5,7},{6,4},{7,5},{8,10},{9,11},{10,... | collective-permute-start | bytes 1671176 | tf_op jit(solution)/shard_map/ppermute | solution.py:174
  37.1 33.5 %collective-permute-start.1 = (bf16[128,2176]{1,0:T(8,128)(2,1)S(1)}, bf16[128,2176]{1,0:T(8,128)(2,1)S(1)}, u32[]{:S(2)}, u32[]{:S(2)}) collective-permute-start(bf16[128,2176]{1,0:T(8,128)(2,1)S(1)} %concatenate.18), channel_id=1, source_target_pairs={{0,8},{1,9},{2,10},{3,11},{4,12},{5,13},{6,14},{7,15},{8,0},{9,1},... | collective-permute-start | bytes 1671176 | tf_op jit(solution)/shard_map/ppermute | solution.py:174
  37.5 36.1 %collective-permute-start.4 = (bf16[128,2176]{1,0:T(8,128)(2,1)}, bf16[128,2176]{1,0:T(8,128)(2,1)S(1)}, u32[]{:S(2)}, u32[]{:S(2)}) collective-permute-start(bf16[128,2176]{1,0:T(8,128)(2,1)} %collective-permute-done), channel_id=1, source_target_pairs={{0,2},{1,3},{2,0},{3,1},{4,6},{5,7},{6,4},{7,5},{8,10},{9,11},{10,... | collective-permute-start | bytes 1671176 | tf_op jit(solution)/shard_map/ppermute | solution.py:174
  70.7 38.7 %collective-permute-start.14 = (bf16[128,2048]{1,0:T(8,128)(2,1)S(1)}, bf16[128,2048]{1,0:T(8,128)(2,1)S(1)}, u32[]{:S(2)}, u32[]{:S(2)}) collective-permute-start(bf16[128,2048]{1,0:T(8,128)(2,1)S(1)} %copy-done.11), channel_id=1, source_target_pairs={{0,4},{1,5},{2,6},{3,7},{4,8},{5,9},{6,10},{7,11},{8,12},{9,13},{1... | collective-permute-start | bytes 1572872 | tf_op jit(solution)/shard_map/ppermute | solution.py:174
  70.7 37.2 %collective-permute-start.16 = (bf16[128,2048]{1,0:T(8,128)(2,1)S(1)}, bf16[128,2048]{1,0:T(8,128)(2,1)S(1)}, u32[]{:S(2)}, u32[]{:S(2)}) collective-permute-start(bf16[128,2048]{1,0:T(8,128)(2,1)S(1)} %copy-done.11), channel_id=1, source_target_pairs={{0,8},{1,9},{2,10},{3,11},{4,12},{5,13},{6,14},{7,15},{8,0},{9,1},... | collective-permute-start | bytes 1572872 | tf_op jit(solution)/shard_map/ppermute | solution.py:174
  73.5 14.9 %collective-permute-start.11 = (bf16[128,2048]{1,0:T(8,128)(2,1)S(1)}, bf16[128,2048]{1,0:T(8,128)(2,1)S(1)}, u32[]{:S(2)}, u32[]{:S(2)}) collective-permute-start(bf16[128,2048]{1,0:T(8,128)(2,1)S(1)} %copy-done.11), channel_id=1, source_target_pairs={{0,2},{1,3},{2,0},{3,1},{4,6},{5,7},{6,4},{7,5},{8,10},{9,11},{10,... | collective-permute-start | bytes 1572872 | tf_op jit(solution)/shard_map/ppermute | solution.py:174
  75.1 34.5 %collective-permute-start.6 = (bf16[128,2176]{1,0:T(8,128)(2,1)S(1)}, bf16[128,2176]{1,0:T(8,128)(2,1)S(1)}, u32[]{:S(2)}, u32[]{:S(2)}) collective-permute-start(bf16[128,2176]{1,0:T(8,128)(2,1)S(1)} %collective-permute-done.1), channel_id=1, source_target_pairs={{0,2},{1,3},{2,0},{3,1},{4,6},{5,7},{6,4},{7,5},{8,10},{9,11},{10,... | collective-permute-start | bytes 1671176 | tf_op jit(solution)/shard_map/ppermute | solution.py:174
  88.4 62.8 %collective-permute-start.8 = (bf16[2,2048,256]{2,1,0:T(8,128)(2,1)S(1)}, bf16[2,2048,256]{2,1,0:T(8,128)(2,1)}, u32[]{:S(2)}, u32[]{:S(2)}) collective-permute-start(bf16[2,2048,256]{2,1,0:T(8,128)(2,1)S(1)} %copy-done.5), channel_id=1, source_target_pairs={{0,1},{1,0},{2,3},{3,2},{4,5},{5,4},{6,7},{7,6},{8,9},{9,8},{10,11... | collective-permute-start | bytes 6291464 | tf_op jit(solution)/shard_map/ppermute | solution.py:174
  107.8 13.7 %collective-permute-start.13 = (bf16[128,2048]{1,0:T(8,128)(2,1)S(1)}, bf16[128,2048]{1,0:T(8,128)(2,1)S(1)}, u32[]{:S(2)}, u32[]{:S(2)}) collective-permute-start(bf16[128,2048]{1,0:T(8,128)(2,1)S(1)} %collective-permute-done.12), channel_id=1, source_target_pairs={{0,2},{1,3},{2,0},{3,1},{4,6},{5,7},{6,4},{7,5},{8,10},{9,11},{10,... | collective-permute-start | bytes 1572872 | tf_op jit(solution)/shard_map/ppermute | solution.py:174
  109.5 2.3 copy-start.12
  120.4 5.2 %copy-start.10 = (bf16[2,256,1024]{2,1,0:T(8,128)(2,1)S(1)}, bf16[2,256,1024]{2,1,0:T(8,128)(2,1)}, u32[]{:S(2)}) copy-start(bf16[2,256,1024]{2,1,0:T(8,128)(2,1)} %slice.121) | copy-start | bytes 3145732
  121.6 14.9 %collective-permute-start.17 = (bf16[128,2048]{1,0:T(8,128)(2,1)S(1)}, bf16[128,2048]{1,0:T(8,128)(2,1)S(1)}, u32[]{:S(2)}, u32[]{:S(2)}) collective-permute-start(bf16[128,2048]{1,0:T(8,128)(2,1)S(1)} %collective-permute-done.16), channel_id=1, source_target_pairs={{0,2},{1,3},{2,0},{3,1},{4,6},{5,7},{6,4},{7,5},{8,10},{9,11},{10,... | collective-permute-start | bytes 1572872 | tf_op jit(solution)/shard_map/ppermute | solution.py:174
  124.5 21.3 %collective-permute-start.15 = (bf16[128,2048]{1,0:T(8,128)(2,1)S(1)}, bf16[128,2048]{1,0:T(8,128)(2,1)S(1)}, u32[]{:S(2)}, u32[]{:S(2)}) collective-permute-start(bf16[128,2048]{1,0:T(8,128)(2,1)S(1)} %collective-permute-done.14), channel_id=1, source_target_pairs={{0,2},{1,3},{2,0},{3,1},{4,6},{5,7},{6,4},{7,5},{8,10},{9,11},{10,... | collective-permute-start | bytes 1572872 | tf_op jit(solution)/shard_map/ppermute | solution.py:174
  125.7 34.9 %collective-permute-start.10 = (bf16[2,256,1024]{2,1,0:T(8,128)(2,1)S(1)}, bf16[2,256,1024]{2,1,0:T(8,128)(2,1)S(1)}, u32[]{:S(2)}, u32[]{:S(2)}) collective-permute-start(bf16[2,256,1024]{2,1,0:T(8,128)(2,1)S(1)} %copy-done.10), channel_id=1, source_target_pairs={{0,1},{1,0},{2,3},{3,2},{4,5},{5,4},{6,7},{7,6},{8,9},{9,8},{10,11... | collective-permute-start | bytes 3145736 | tf_op jit(solution)/shard_map/ppermute | solution.py:174
  151.2 23.8 %collective-permute-start.9 = (bf16[2,256,768]{2,1,0:T(8,128)(2,1)}, bf16[2,256,768]{2,1,0:T(8,128)(2,1)S(1)}, u32[]{:S(2)}, u32[]{:S(2)}) collective-permute-start(bf16[2,256,768]{2,1,0:T(8,128)(2,1)} %slice.120), channel_id=1, source_target_pairs={{0,1},{1,0},{2,3},{3,2},{4,5},{5,4},{6,7},{7,6},{8,9},{9,8},{10,11... | collective-permute-start | bytes 2359304 | tf_op jit(solution)/shard_map/ppermute | solution.py:174
  160.5 6.5 %copy-start.13 = (bf16[1024,2048]{1,0:T(8,128)(2,1)S(1)}, bf16[1024,2048]{1,0:T(8,128)(2,1)}, u32[]{:S(2)}) copy-start(bf16[1024,2048]{1,0:T(8,128)(2,1)} %constant_dynamic-update-slice_fusion.8) | copy-start | bytes 12582916
  166.5 13.9 %collective-permute-start.26 = (bf16[2,256,256]{2,1,0:T(8,128)(2,1)S(1)}, bf16[2,256,256]{2,1,0:T(8,128)(2,1)S(1)}, u32[]{:S(2)}, u32[]{:S(2)}) collective-permute-start(bf16[2,256,256]{2,1,0:T(8,128)(2,1)S(1)} %slice.129), channel_id=1, source_target_pairs={{0,1},{1,0},{2,3},{3,2},{4,5},{5,4},{6,7},{7,6},{8,9},{9,8},{10,11... | collective-permute-start | bytes 786440 | tf_op jit(solution)/shard_map/ppermute | solution.py:174
  169.7 10.8 %copy-start.2 = (bf16[2,256,2048]{2,1,0:T(8,128)(2,1)S(1)}, bf16[2,256,2048]{2,1,0:T(8,128)(2,1)}, u32[]{:S(2)}) copy-start(bf16[2,256,2048]{2,1,0:T(8,128)(2,1)} %own_down_ref.5) | copy-start | bytes 6291460
  169.7 26.4 %collective-permute-start.19 = (bf16[512,1024]{1,0:T(8,128)(2,1)}, bf16[512,1024]{1,0:T(8,128)(2,1)}, u32[]{:S(2)}, u32[]{:S(2)}) collective-permute-start(bf16[512,1024]{1,0:T(8,128)(2,1)} %get-tuple-element.86), channel_id=1, source_target_pairs={{0,2},{1,3},{2,0},{3,1},{4,6},{5,7},{6,4},{7,5},{8,10},{9,11},{10,... | collective-permute-start | bytes 3145736 | tf_op jit(solution)/shard_map/ppermute | solution.py:174
  179.3 1.2 copy-start.3
  180.5 5.1 %copy-start.7 = (f32[1024,512]{1,0:T(8,128)S(1)}, f32[1024,512]{1,0:T(8,128)}, u32[]{:S(2)}) copy-start(f32[1024,512]{1,0:T(8,128)} %fusion) | copy-start | bytes 6291460
  181.5 33.8 %collective-permute-start.18 = (bf16[512,768]{1,0:T(8,128)(2,1)}, bf16[512,768]{1,0:T(8,128)(2,1)S(1)}, u32[]{:S(2)}, u32[]{:S(2)}) collective-permute-start(bf16[512,768]{1,0:T(8,128)(2,1)} %get-tuple-element.84), channel_id=1, source_target_pairs={{0,2},{1,3},{2,0},{3,1},{4,6},{5,7},{6,4},{7,5},{8,10},{9,11},{10,... | collective-permute-start | bytes 2359304 | tf_op jit(solution)/shard_map/ppermute | solution.py:174
  187.3 12.3 %copy-start = (bf16[1024,512]{1,0:T(8,128)(2,1)}, bf16[1024,512]{1,0:T(8,128)(2,1)S(1)}, u32[]{:S(2)}) copy-start(bf16[1024,512]{1,0:T(8,128)(2,1)S(1)} %get-tuple-element.138.refs_5_) | copy-start | bytes 3145732
  187.3 8.8 %copy-start.6 = (f32[512,1024]{1,0:T(8,128)S(1)}, f32[512,1024]{1,0:T(8,128)}, u32[]{:S(2)}) copy-start(f32[512,1024]{1,0:T(8,128)} %get-tuple-element.85) | copy-start | bytes 6291460
  197.9 17.0 %collective-permute-start.20 = (bf16[128,1024]{1,0:T(8,128)(2,1)S(1)}, bf16[128,1024]{1,0:T(8,128)(2,1)S(1)}, u32[]{:S(2)}, u32[]{:S(2)}) collective-permute-start(bf16[128,1024]{1,0:T(8,128)(2,1)S(1)} %get-tuple-element.87), channel_id=1, source_target_pairs={{0,4},{1,5},{2,6},{3,7},{4,8},{5,9},{6,10},{7,11},{8,12},{9,13},{1... | collective-permute-start | bytes 786440 | tf_op jit(solution)/shard_map/ppermute | solution.py:174
  198.4 16.8 %collective-permute-start.27 = (bf16[512,256]{1,0:T(8,128)(2,1)S(1)}, bf16[512,256]{1,0:T(8,128)(2,1)S(1)}, u32[]{:S(2)}, u32[]{:S(2)}) collective-permute-start(bf16[512,256]{1,0:T(8,128)(2,1)S(1)} %get-tuple-element.97), channel_id=1, source_target_pairs={{0,2},{1,3},{2,0},{3,1},{4,6},{5,7},{6,4},{7,5},{8,10},{9,11},{10,... | collective-permute-start | bytes 786440 | tf_op jit(solution)/shard_map/ppermute | solution.py:174
  206.5 8.8 %copy-start.4 = (f32[512,768]{1,0:T(8,128)S(1)}, f32[512,768]{1,0:T(8,128)}, u32[]{:S(2)}) copy-start(f32[512,768]{1,0:T(8,128)} %copy-done.3) | copy-start | bytes 4718596
  211.1 10.4 %collective-permute-start.21 = (bf16[128,1024]{1,0:T(8,128)(2,1)S(1)}, bf16[128,1024]{1,0:T(8,128)(2,1)S(1)}, u32[]{:S(2)}, u32[]{:S(2)}) collective-permute-start(bf16[128,1024]{1,0:T(8,128)(2,1)S(1)} %get-tuple-element.88), channel_id=1, source_target_pairs={{0,12},{1,13},{2,14},{3,15},{4,0},{5,1},{6,2},{7,3},{8,4},{9,5},{1... | collective-permute-start | bytes 786440 | tf_op jit(solution)/shard_map/ppermute | solution.py:174
  214.9 16.4 %collective-permute-start.23 = (bf16[128,1024]{1,0:T(8,128)(2,1)S(1)}, bf16[128,1024]{1,0:T(8,128)(2,1)S(1)}, u32[]{:S(2)}, u32[]{:S(2)}) collective-permute-start(bf16[128,1024]{1,0:T(8,128)(2,1)S(1)} %get-tuple-element.90), channel_id=1, source_target_pairs={{0,8},{1,9},{2,10},{3,11},{4,12},{5,13},{6,14},{7,15},{8,0},{9,1},... | collective-permute-start | bytes 786440 | tf_op jit(solution)/shard_map/ppermute | solution.py:174
  215.3 40.4 %copy-start.9 = (f32[512,768]{1,0:T(8,128)S(1)}, f32[512,768]{1,0:T(8,128)}, u32[]{:S(2)}) copy-start(f32[512,768]{1,0:T(8,128)} %get-tuple-element.106) | copy-start | bytes 4718596
  221.5 11.5 %collective-permute-start.22 = (bf16[128,768]{1,0:T(8,128)(2,1)S(1)}, bf16[128,768]{1,0:T(8,128)(2,1)S(1)}, u32[]{:S(2)}, u32[]{:S(2)}) collective-permute-start(bf16[128,768]{1,0:T(8,128)(2,1)S(1)} %get-tuple-element.89), channel_id=1, source_target_pairs={{0,4},{1,5},{2,6},{3,7},{4,8},{5,9},{6,10},{7,11},{8,12},{9,13},{1... | collective-permute-start | bytes 589832 | tf_op jit(solution)/shard_map/ppermute | solution.py:174
  224.0 31.7 %collective-permute-start.31 = (bf16[512,768]{1,0:T(8,128)(2,1)S(1)}, bf16[512,768]{1,0:T(8,128)(2,1)S(1)}, u32[]{:S(2)}, u32[]{:S(2)}) collective-permute-start(bf16[512,768]{1,0:T(8,128)(2,1)S(1)} %get-tuple-element.108), channel_id=1, source_target_pairs={{0,2},{1,3},{2,0},{3,1},{4,6},{5,7},{6,4},{7,5},{8,10},{9,11},{10,... | collective-permute-start | bytes 2359304 | tf_op jit(solution)/shard_map/ppermute | solution.py:174
  231.3 8.6 %collective-permute-start.24 = (bf16[128,768]{1,0:T(8,128)(2,1)S(1)}, bf16[128,768]{1,0:T(8,128)(2,1)S(1)}, u32[]{:S(2)}, u32[]{:S(2)}) collective-permute-start(bf16[128,768]{1,0:T(8,128)(2,1)S(1)} %get-tuple-element.91), channel_id=1, source_target_pairs={{0,12},{1,13},{2,14},{3,15},{4,0},{5,1},{6,2},{7,3},{8,4},{9,5},{1... | collective-permute-start | bytes 589832 | tf_op jit(solution)/shard_map/ppermute | solution.py:174
  232.5 27.9 %collective-permute-start.35 = (bf16[512,768]{1,0:T(8,128)(2,1)S(1)}, bf16[512,768]{1,0:T(8,128)(2,1)S(1)}, u32[]{:S(2)}, u32[]{:S(2)}) collective-permute-start(bf16[512,768]{1,0:T(8,128)(2,1)S(1)} %get-tuple-element.115), channel_id=1, source_target_pairs={{0,2},{1,3},{2,0},{3,1},{4,6},{5,7},{6,4},{7,5},{8,10},{9,11},{10,... | collective-permute-start | bytes 2359304 | tf_op jit(solution)/shard_map/ppermute | solution.py:174
  233.0 14.0 %collective-permute-start.25 = (bf16[128,768]{1,0:T(8,128)(2,1)S(1)}, bf16[128,768]{1,0:T(8,128)(2,1)S(1)}, u32[]{:S(2)}, u32[]{:S(2)}) collective-permute-start(bf16[128,768]{1,0:T(8,128)(2,1)S(1)} %get-tuple-element.92), channel_id=1, source_target_pairs={{0,8},{1,9},{2,10},{3,11},{4,12},{5,13},{6,14},{7,15},{8,0},{9,1},... | collective-permute-start | bytes 589832 | tf_op jit(solution)/shard_map/ppermute | solution.py:174
  239.9 7.1 %collective-permute-start.28 = (bf16[128,256]{1,0:T(8,128)(2,1)S(1)}, bf16[128,256]{1,0:T(8,128)(2,1)S(1)}, u32[]{:S(2)}, u32[]{:S(2)}) collective-permute-start(bf16[128,256]{1,0:T(8,128)(2,1)S(1)} %get-tuple-element.98), channel_id=1, source_target_pairs={{0,4},{1,5},{2,6},{3,7},{4,8},{5,9},{6,10},{7,11},{8,12},{9,13},{1... | collective-permute-start | bytes 196616 | tf_op jit(solution)/shard_map/ppermute | solution.py:174
  240.0 20.4 %copy-start.8 = (f32[512,768]{1,0:T(8,128)S(1)}, f32[512,768]{1,0:T(8,128)}, u32[]{:S(2)}) copy-start(f32[512,768]{1,0:T(8,128)} %get-tuple-element.113) | copy-start | bytes 4718596
  247.0 8.7 %collective-permute-start.30 = (bf16[128,256]{1,0:T(8,128)(2,1)S(1)}, bf16[128,256]{1,0:T(8,128)(2,1)S(1)}, u32[]{:S(2)}, u32[]{:S(2)}) collective-permute-start(bf16[128,256]{1,0:T(8,128)(2,1)S(1)} %get-tuple-element.100), channel_id=1, source_target_pairs={{0,8},{1,9},{2,10},{3,11},{4,12},{5,13},{6,14},{7,15},{8,0},{9,1},... | collective-permute-start | bytes 196616 | tf_op jit(solution)/shard_map/ppermute | solution.py:174
  248.0 7.6 %collective-permute-start.29 = (bf16[128,256]{1,0:T(8,128)(2,1)S(1)}, bf16[128,256]{1,0:T(8,128)(2,1)S(1)}, u32[]{:S(2)}, u32[]{:S(2)}) collective-permute-start(bf16[128,256]{1,0:T(8,128)(2,1)S(1)} %get-tuple-element.99), channel_id=1, source_target_pairs={{0,12},{1,13},{2,14},{3,15},{4,0},{5,1},{6,2},{7,3},{8,4},{9,5},{1... | collective-permute-start | bytes 196616 | tf_op jit(solution)/shard_map/ppermute | solution.py:174
  256.0 8.3 %collective-permute-start.32 = (bf16[128,768]{1,0:T(8,128)(2,1)S(1)}, bf16[128,768]{1,0:T(8,128)(2,1)S(1)}, u32[]{:S(2)}, u32[]{:S(2)}) collective-permute-start(bf16[128,768]{1,0:T(8,128)(2,1)S(1)} %get-tuple-element.109), channel_id=1, source_target_pairs={{0,4},{1,5},{2,6},{3,7},{4,8},{5,9},{6,10},{7,11},{8,12},{9,13},{1... | collective-permute-start | bytes 589832 | tf_op jit(solution)/shard_map/ppermute | solution.py:174
  257.8 9.9 %collective-permute-start.33 = (bf16[128,768]{1,0:T(8,128)(2,1)S(1)}, bf16[128,768]{1,0:T(8,128)(2,1)S(1)}, u32[]{:S(2)}, u32[]{:S(2)}) collective-permute-start(bf16[128,768]{1,0:T(8,128)(2,1)S(1)} %get-tuple-element.110), channel_id=1, source_target_pairs={{0,12},{1,13},{2,14},{3,15},{4,0},{5,1},{6,2},{7,3},{8,4},{9,5},{1... | collective-permute-start | bytes 589832 | tf_op jit(solution)/shard_map/ppermute | solution.py:174
  259.9 21.6 %collective-permute-start.39 = (bf16[512,512]{1,0:T(8,128)(2,1)S(1)}, bf16[512,512]{1,0:T(8,128)(2,1)S(1)}, u32[]{:S(2)}, u32[]{:S(2)}) collective-permute-start(bf16[512,512]{1,0:T(8,128)(2,1)S(1)} %get-tuple-element.122), channel_id=1, source_target_pairs={{0,2},{1,3},{2,0},{3,1},{4,6},{5,7},{6,4},{7,5},{8,10},{9,11},{10,... | collective-permute-start | bytes 1572872 | tf_op jit(solution)/shard_map/ppermute | solution.py:174
  264.3 14.2 %collective-permute-start.34 = (bf16[128,768]{1,0:T(8,128)(2,1)S(1)}, bf16[128,768]{1,0:T(8,128)(2,1)S(1)}, u32[]{:S(2)}, u32[]{:S(2)}) collective-permute-start(bf16[128,768]{1,0:T(8,128)(2,1)S(1)} %get-tuple-element.111), channel_id=1, source_target_pairs={{0,8},{1,9},{2,10},{3,11},{4,12},{5,13},{6,14},{7,15},{8,0},{9,1},... | collective-permute-start | bytes 589832 | tf_op jit(solution)/shard_map/ppermute | solution.py:174
  267.8 10.8 %collective-permute-start.36 = (bf16[128,768]{1,0:T(8,128)(2,1)S(1)}, bf16[128,768]{1,0:T(8,128)(2,1)S(1)}, u32[]{:S(2)}, u32[]{:S(2)}) collective-permute-start(bf16[128,768]{1,0:T(8,128)(2,1)S(1)} %get-tuple-element.116), channel_id=1, source_target_pairs={{0,4},{1,5},{2,6},{3,7},{4,8},{5,9},{6,10},{7,11},{8,12},{9,13},{1... | collective-permute-start | bytes 589832 | tf_op jit(solution)/shard_map/ppermute | solution.py:174
  278.6 14.3 %collective-permute-start.38 = (bf16[128,768]{1,0:T(8,128)(2,1)S(1)}, bf16[128,768]{1,0:T(8,128)(2,1)S(1)}, u32[]{:S(2)}, u32[]{:S(2)}) collective-permute-start(bf16[128,768]{1,0:T(8,128)(2,1)S(1)} %get-tuple-element.118), channel_id=1, source_target_pairs={{0,8},{1,9},{2,10},{3,11},{4,12},{5,13},{6,14},{7,15},{8,0},{9,1},... | collective-permute-start | bytes 589832 | tf_op jit(solution)/shard_map/ppermute | solution.py:174
  281.1 8.0 %collective-permute-start.37 = (bf16[128,768]{1,0:T(8,128)(2,1)S(1)}, bf16[128,768]{1,0:T(8,128)(2,1)S(1)}, u32[]{:S(2)}, u32[]{:S(2)}) collective-permute-start(bf16[128,768]{1,0:T(8,128)(2,1)S(1)} %get-tuple-element.117), channel_id=1, source_target_pairs={{0,12},{1,13},{2,14},{3,15},{4,0},{5,1},{6,2},{7,3},{8,4},{9,5},{1... | collective-permute-start | bytes 589832 | tf_op jit(solution)/shard_map/ppermute | solution.py:174
  289.0 6.8 %collective-permute-start.40 = (bf16[128,512]{1,0:T(8,128)(2,1)S(1)}, bf16[128,512]{1,0:T(8,128)(2,1)S(1)}, u32[]{:S(2)}, u32[]{:S(2)}) collective-permute-start(bf16[128,512]{1,0:T(8,128)(2,1)S(1)} %get-tuple-element.123), channel_id=1, source_target_pairs={{0,4},{1,5},{2,6},{3,7},{4,8},{5,9},{6,10},{7,11},{8,12},{9,13},{1... | collective-permute-start | bytes 393224 | tf_op jit(solution)/shard_map/ppermute | solution.py:174
  292.8 5.2 %collective-permute-start.41 = (bf16[128,512]{1,0:T(8,128)(2,1)S(1)}, bf16[128,512]{1,0:T(8,128)(2,1)S(1)}, u32[]{:S(2)}, u32[]{:S(2)}) collective-permute-start(bf16[128,512]{1,0:T(8,128)(2,1)S(1)} %get-tuple-element.124), channel_id=1, source_target_pairs={{0,12},{1,13},{2,14},{3,15},{4,0},{5,1},{6,2},{7,3},{8,4},{9,5},{1... | collective-permute-start | bytes 393224 | tf_op jit(solution)/shard_map/ppermute | solution.py:174
  295.8 5.9 %collective-permute-start.42 = (bf16[128,512]{1,0:T(8,128)(2,1)S(1)}, bf16[128,512]{1,0:T(8,128)(2,1)S(1)}, u32[]{:S(2)}, u32[]{:S(2)}) collective-permute-start(bf16[128,512]{1,0:T(8,128)(2,1)S(1)} %get-tuple-element.125), channel_id=1, source_target_pairs={{0,8},{1,9},{2,10},{3,11},{4,12},{5,13},{6,14},{7,15},{8,0},{9,1},... | collective-permute-start | bytes 393224 | tf_op jit(solution)/shard_map/ppermute | solution.py:174

commit v4 on v0

--- a/solution.py
+++ b/solution.py
@@ -1,7 +1,248 @@
 import jax
 import jax.numpy as jnp
 from jax import lax
+from jax.experimental import pallas as pl
+from jax.experimental.pallas import tpu as pltpu
 from jax.sharding import PartitionSpec as P
+
+VMEM_BYTES = 48 * 2**20
+AT_ONCE = pl.CostEstimate(flops=1, bytes_accessed=1, transcendentals=0)
+
+
+def hidden_kernel(rows_ref, weight_ref, gate_ref, up_ref, activ_ref, by_ref):
+    experts, _, hidden = gate_ref.shape
+    rows = rows_ref[...]
+    for e in range(experts):
+        cut = slice(e * hidden, (e + 1) * hidden)
+        cut_up = slice((experts + e) * hidden, (experts + e + 1) * hidden)
+        gate_pre = jnp.dot(rows, gate_ref[e], preferred_element_type=jnp.float32)
+        up_pre = jnp.dot(rows, up_ref[e], preferred_element_type=jnp.float32)
+        sig = jax.nn.sigmoid(gate_pre)
+        factor = sig * weight_ref[:, e : e + 1]
+        silu = gate_pre * factor
+        activ_ref[:, cut] = (silu * up_pre).astype(jnp.bfloat16)
+        by_ref[:, cut] = up_pre * factor * (1.0 + gate_pre * (1.0 - sig))
+        by_ref[:, cut_up] = silu
+
+
+def hidden_forward(rows, weight, gate_weight, up_weight):
+    count = rows.shape[0]
+    experts, width, hidden = gate_weight.shape
+    tile = 256 if count % 256 == 0 else count
+    columns = experts * hidden
+    weights = pl.BlockSpec((experts, width, hidden), lambda i: (0, 0, 0))
+    return pl.pallas_call(
+        hidden_kernel,
+        grid=(count // tile,),
+        in_specs=[
+            pl.BlockSpec((tile, width), lambda i: (i, 0)),
+            pl.BlockSpec((tile, experts), lambda i: (i, 0)),
+            weights,
+            weights,
+        ],
+        out_specs=[
+            pl.BlockSpec((tile, columns), lambda i: (i, 0)),
+            pl.BlockSpec((tile, 2 * columns), lambda i: (i, 0)),
+        ],
+        out_shape=[
+            jax.ShapeDtypeStruct((count, columns), jnp.bfloat16),
+            jax.ShapeDtypeStruct((count, 2 * columns), jnp.float32),
+        ],
+        compiler_params=pltpu.CompilerParams(vmem_limit_bytes=VMEM_BYTES),
+        cost_estimate=AT_ONCE,
+        name="hidden_forward",
+    )(rows, weight, gate_weight, up_weight)
+
+
+def columns_kernel(own_ref, other_ref, own_weight_ref, other_weight_ref, keep_ref, send_ref):
+    total = jnp.dot(own_ref[...], own_weight_ref[...], preferred_element_type=jnp.float32)
+    total += jnp.dot(other_ref[...], other_weight_ref[...], preferred_element_type=jnp.float32)
+
+    @pl.when(pl.program_id(0) == 0)
+    def _():
+        send_ref[...] = total.astype(send_ref.dtype)
+
+    @pl.when(pl.program_id(0) == 1)
+    def _():
+        keep_ref[...] = total
+
+
+def sum_columns(name, own, other, own_weight, other_weight, own_at, other_at, columns):
+    half, depth = own.shape[0] // 2, own.shape[1]
+    rows = pl.BlockSpec((half, depth), lambda i: (1 - i, 0))
+    return pl.pallas_call(
+        columns_kernel,
+        grid=(2,),
+        in_specs=[
+            rows,
+            rows,
+            pl.BlockSpec((depth, columns), lambda i: (0, own_at)),
+            pl.BlockSpec((depth, columns), lambda i: (0, other_at)),
+        ],
+        out_specs=[pl.BlockSpec((half, columns), lambda i: (0, 0))] * 2,
+        out_shape=[
+            jax.ShapeDtypeStruct((half, columns), jnp.float32),
+            jax.ShapeDtypeStruct((half, columns), jnp.bfloat16),
+        ],
+        compiler_params=pltpu.CompilerParams(vmem_limit_bytes=VMEM_BYTES),
+        cost_estimate=AT_ONCE,
+        name=name,
+    )(own, other, own_weight, other_weight)
+
+
+def cut_columns(width, eighths):
+    eighth = width // 8
+    return [(lo * eighth, hi * eighth) for lo, hi in eighths]
+
+
+def join_columns(chunks, parts):
+    return jnp.concatenate([part for _, part in sorted(zip(chunks, parts), key=lambda p: p[0])], axis=1)
+
+
+def after(values, *others):
+    return lax.optimization_barrier((values, *others))[0]
+
+
+def send_round(sends, waits=()):
+    values, _ = lax.optimization_barrier(([v for v, _ in sends], list(waits)))
+    return [lax.ppermute(v, "expert", pairs) for v, (_, pairs) in zip(values, sends)]
+
+
+def on_device_dense(tokens, cotangent, expert_ids, probs, gate_weight, up_weight, down_weight):
+    local_count, hidden, width = down_weight.shape
+    devices = lax.axis_size("expert")
+    layers = devices // 4
+    experts = local_count * devices
+    block = tokens.shape[0]
+    chunks = cut_columns(width, ((6, 8), (0, 3), (3, 6)))
+    back_chunks = cut_columns(width, ((0, 3), (3, 6), (6, 8)))
+    me = lax.axis_index("expert")
+    twin = [(d, d ^ 1) for d in range(devices)]
+    side = [(d, d ^ 2) for d in range(devices)]
+    layer = [[(d, (d + 4 * k) % devices) for d in range(devices)] for k in range(layers)]
+    hops = list(range(1, layers))
+    ends, middle = [hops[0], hops[-1]], hops[1:-1]
+
+    labels = lax.broadcasted_iota(jnp.int32, (1, 1, experts), 2)
+    weight = jnp.sum(jnp.where(expert_ids[:, :, None] == labels, probs[:, :, None], 0.0), axis=1)
+    first = lax.reduce_precision(weight, 8, 7)
+    second = lax.reduce_precision(weight - first, 8, 7)
+    third = weight - first - second
+    spare = jnp.zeros((block, -3 * experts % 128), jnp.bfloat16)
+    terms = [t.astype(jnp.bfloat16) for t in (first, second, third)]
+    rows = jnp.concatenate([tokens] + terms + [spare], axis=1)
+
+    def turn(weights):
+        return weights.transpose(0, 2, 1).reshape(local_count * hidden, width)
+
+    near_rows, far_rows = {0: rows}, {}
+    near_grads, far_grads = {0: cotangent}, {}
+    down = down_weight.reshape(local_count * hidden, width)
+    downs = [down[:, lo:hi] for lo, hi in chunks]
+    got = send_round(
+        [(gate_weight, twin), (rows, side), (cotangent, side)] + [(rows, layer[-k]) for k in ends]
+    )
+    other_gate, far_rows[0], far_grads[0], near_rows[ends[0]], near_rows[ends[1]] = got
+    own_turned = jnp.concatenate([turn(gate_weight), turn(up_weight)], axis=0)
+    got = send_round(
+        [(up_weight, twin)] + [(near_rows[k], side) for k in ends] + [(rows, layer[-k]) for k in middle],
+        got[1:] + [own_turned],
+    )
+    other_up, far_rows[ends[0]], far_rows[ends[1]] = got[:3]
+    near_rows.update(zip(middle, got[3:]))
+    got = send_round(
+        [(downs[0], twin)] + [(cotangent, layer[-k]) for k in ends] + [(near_rows[k], side) for k in middle],
+        got[1:] + [other_gate],
+    )
+    other_down = got[:1]
+    near_grads[ends[0]], near_grads[ends[1]] = got[1:3]
+    far_rows.update(zip(middle, got[3:]))
+    all_rows = jnp.concatenate(
+        [near_rows[k] for k in range(layers)] + [far_rows[k] for k in range(layers)], axis=0
+    )
+    other_turned = turn(other_gate)
+    got = send_round(
+        [(near_grads[k], side) for k in ends] + [(cotangent, layer[-k]) for k in middle], got[1:]
+    )
+    far_grads[ends[0]], far_grads[ends[1]] = got[:2]
+    near_grads.update(zip(middle, got[2:]))
+    terms = [
+        all_rows[:, width + t * experts : width + (t + 1) * experts].astype(jnp.float32) for t in range(3)
+    ]
+    all_weight = terms[0] + terms[1] + terms[2]
+    own_weight, other_weight = (
+        lax.dynamic_slice_in_dim(all_weight, owner * local_count, local_count, axis=1)
+        for owner in (me, me ^ 1)
+    )
+    activ, by = hidden_forward(all_rows, own_weight, gate_weight, up_weight)
+    ready = got + [other_up, activ, other_turned, other_weight]
+    got = send_round([(downs[1], twin)] + [(near_grads[k], side) for k in middle], ready)
+    other_down += got[:1]
+    far_grads.update(zip(middle, got[1:]))
+    other_up = after(other_up, *ready)
+    all_grads = jnp.concatenate(
+        [near_grads[k] for k in range(layers)] + [far_grads[k] for k in range(layers)], axis=0
+    )
+
+    def grad_act(grads, down):
+        return lax.dot_general(grads, down, (((1,), (1,)), ((), ())), preferred_element_type=jnp.float32)
+
+    def spread(grad, by):
+        return (jnp.concatenate([grad, grad], axis=1) * by).astype(jnp.bfloat16)
+
+    def mix(c):
+        lo, hi = chunks[c]
+        return sum_columns(
+            "mix_columns", activ, other_activ, down, other_down[c], lo // (hi - lo), 0, hi - lo
+        )
+
+    def back(c):
+        lo, hi = back_chunks[c]
+        at = lo // (hi - lo)
+        return sum_columns(
+            "back_columns", own_grads, other_grads, own_turned, other_turned, at, at, hi - lo
+        )
+
+    def across(total):
+        return [
+            (total[k * block : (k + 1) * block].astype(jnp.bfloat16), layer[k]) for k in hops
+        ]
+
+    def finish(total, parts):
+        return total[:block] + sum(p.astype(jnp.float32) for p in parts)
+
+    other_activ, other_by = hidden_forward(all_rows, other_weight, other_gate, other_up)
+    other_down[0] = after(other_down[0], other_activ)
+    keep, send = mix(0)
+    got = send_round([(downs[2], twin), (send, side)], [all_grads])
+    other_down += got[:1]
+    own_grads = spread(grad_act(all_grads, down), by)
+    other_turned = jnp.concatenate([other_turned, turn(other_up)], axis=0)
+    totals, parts = [keep + got[1].astype(jnp.float32)], []
+
+    other_down[1] = after(other_down[1], send)
+    keep, send = mix(1)
+    got = send_round([(send, side)] + across(totals[0]), [own_grads, other_turned])
+    totals.append(keep + got[0].astype(jnp.float32))
+    parts.append(got[1:])
+
+    other_down[2] = after(other_down[2], send)
+    keep, send = mix(2)
+    got = send_round([(send, side)] + across(totals[1]), got)
+    totals.append(keep + got[0].astype(jnp.float32))
+    parts.append(got[1:])
+    other_grad = sum(grad_act(all_grads[:, lo:hi], down) for (lo, hi), down in zip(chunks, other_down))
+    other_grads = spread(other_grad, other_by)
+
+    for c in range(len(back_chunks)):
+        keep, send = back(c)
+        got = send_round([(send, side)] + across(totals[-1]), got)
+        totals.append(keep + got[0].astype(jnp.float32))
+        parts.append(got[1:])
+    parts.append(send_round(across(totals[-1]), got))
+    sums = [finish(total, part) for total, part in zip(totals, parts)]
+    count = len(chunks)
+    return (join_columns(chunks, sums[:count]), join_columns(back_chunks, sums[count:]))
 
 
 def route_slots(expert_ids, local_count, device_count, capacity):
@@ -62,7 +303,7 @@
     return jnp.sum(picked.astype(jnp.float32) * probs[:, :, None], axis=1)
 
 
-def on_device(tokens, cotangent, expert_ids, probs, gate_weight, up_weight, down_weight):
+def on_device_routed(tokens, cotangent, expert_ids, probs, gate_weight, up_weight, down_weight):
     local_count = gate_weight.shape[0]
     device_count = lax.axis_size("expert")
     experts = local_count * device_count
@@ -87,6 +328,13 @@
     return (mixed, input_grad)
 
 
+def on_device(tokens, cotangent, expert_ids, probs, gate_weight, up_weight, down_weight):
+    devices = lax.axis_size("expert")
+    dense = devices % 4 == 0 and 16 <= devices <= 2 * expert_ids.shape[1]
+    body = on_device_dense if dense else on_device_routed
+    return body(tokens, cotangent, expert_ids, probs, gate_weight, up_weight, down_weight)
+
+
 def solution(mesh):
     in_specs = (
         P(("dp", "expert"), None),

time: 736 us -> 301 us (0.41)
  the two profiles are of different devices: /device:TPU:14 before, /device:TPU:0 now
where the time goes in v4:
time: 301 us; the launch traced here: 299 us
  waiting for transfers between devices  112 us (37%)
  starting transfers between devices  67.1 us (22%)
  local copies, waits for them, and re-layouts  46.8 us (16%)
  Pallas kernels  43.5 us (14%)
  other arithmetic  18.2 us (6%)
  matrix products  10.3 us (3%)
    ppermute x43, waiting for transfers between devices, send_round(): lax.ppermute(v, 'expert', pairs)  112 us
    ppermute x43, starting transfers between devices, send_round(): lax.ppermute(v, 'expert', pairs)  67.1 us
    pallas_call x6, Pallas kernels, sum_columns(): pl.pallas_call(columns_kernel, grid=(2,), in_specs=[rows, rows, pl.BlockS...  25.8 us
    unnamed x50, local copies, waits for them, and re-layouts  25.1 us
    pallas_call x2, Pallas kernels, hidden_forward(): pl.pallas_call(hidden_kernel, grid=(count // tile,), in_specs=[pl.BlockSp...  17.7 us
    transpose x4, local copies, waits for them, and re-layouts, turn(): return weights.transpose(0, 2, 1).reshape(local_count * hidden, width)  14.4 us
    dot_general x4, matrix products, grad_act(): lax.dot_general(grads, down, (((1,), (1,)), ((), ())), preferred_element_...  10.3 us
  transfers between devices with their start and end apart: 43, of which 19 were waited for; matrix products, arithmetic and copies ran while one was open for 21% of the time, Pallas kernels for 15%

profile of v4, /device:TPU:0, one launch (start us, length us, event | category | flops | bytes accessed | tf_op | source)
XLA Modules:
  0.0 299.2 jit_solution(11330841450471313585)
XLA Ops:
  3.0 3.0 %collective-permute-start.3 = (bf16[128,2048]{1,0:T(8,128)(2,1)}, bf16[128,2048]{1,0:T(8,128)(2,1)}, u32[]{:S(2)}, u32[]{:S(2)}) collective-permute-start(bf16[128,2048]{1,0:T(8,128)(2,1)} %param.8), channel_id=1, source_target_pairs={{0,2},{1,3},{2,0},{3,1},{4,6},{5,7},{6,4},{7,5},{8,10},{9,11},{10,... | collective-permute-start | bytes 1572872 | tf_op jit(solution)/shard_map/ppermute | solution.py:108
  6.0 3.6 %collective-permute-start = (bf16[128,2176]{1,0:T(8,128)(2,1)S(1)}, bf16[128,2176]{1,0:T(8,128)(2,1)}, u32[]{:S(2)}, u32[]{:S(2)}) collective-permute-start(bf16[128,2176]{1,0:T(8,128)(2,1)S(1)} %concatenate.27), channel_id=1, source_target_pairs={{0,12},{1,13},{2,14},{3,15},{4,0},{5,1},{6,2},{7,3},{8,4},{9,5},{1... | collective-permute-start | bytes 1671176 | tf_op jit(solution)/shard_map/ppermute | solution.py:108
  11.6 4.0 %copy.35 = bf16[2,256,2048]{2,1,0:T(8,128)(2,1)} copy(bf16[2,256,2048]{1,2,0:T(8,128)(2,1)} %bitcast.2) | data formatting | bytes 4194304 | tf_op jit(solution)/shard_map/transpose | solution.py:136
  15.6 2.4 copy.34
  18.1 4.8 %pad_maximum_fusion.own_weight_ref = bf16[1024,2048]{1,0:T(8,128)(2,1)} fusion(bf16[512,2048]{1,0:T(8,128)(2,1)} %bitcast.23, bf16[512,2048]{1,0:T(8,128)(2,1)} %bitcast.24), kind=kLoop, calls=%fused_computation | loop fusion | flops 8388608 | bytes 8388608 | tf_op jit(solution)/shard_map/concatenate | solution.py:146
  22.9 1.9 slice.150
  24.7 2.6 fusion.17
  28.2 5.9 %collective-permute-done.1 = bf16[128,2176]{1,0:T(8,128)(2,1)} collective-permute-done((bf16[128,2176]{1,0:T(8,128)(2,1)S(1)}, bf16[128,2176]{1,0:T(8,128)(2,1)}, u32[]{:S(2)}, u32[]{:S(2)}) %collective-permute-start.1) | collective-permute-done | bytes 557088 | tf_op jit(solution)/shard_map/ppermute | solution.py:108
  34.9 1.9 constant_dynamic-update-slice_fusion.15
  37.3 1.5 collective-permute-start.6
  40.3 1.9 constant_dynamic-update-slice_fusion.6
  42.2 18.1 %collective-permute-done.4 = bf16[128,2176]{1,0:T(8,128)(2,1)} collective-permute-done((bf16[128,2176]{1,0:T(8,128)(2,1)S(1)}, bf16[128,2176]{1,0:T(8,128)(2,1)}, u32[]{:S(2)}, u32[]{:S(2)}) %collective-permute-start.4) | collective-permute-done | bytes 557088 | tf_op jit(solution)/shard_map/ppermute | solution.py:108
  60.3 1.9 constant_dynamic-update-slice_fusion.5
  62.2 1.9 constant_dynamic-update-slice_fusion.4
  69.9 4.0 %copy.36 = bf16[2,256,2048]{2,1,0:T(8,128)(2,1)} copy(bf16[2,256,2048]{1,2,0:T(8,128)(2,1)} %bitcast.5) | data formatting | bytes 4194304 | tf_op jit(solution)/shard_map/transpose | solution.py:136
  73.9 4.3 %collective-permute-done.10 = bf16[128,2048]{1,0:T(8,128)(2,1)} collective-permute-done((bf16[128,2048]{1,0:T(8,128)(2,1)}, bf16[128,2048]{1,0:T(8,128)(2,1)}, u32[]{:S(2)}, u32[]{:S(2)}) %collective-permute-start.10) | collective-permute-done | bytes 524320 | tf_op jit(solution)/shard_map/ppermute | solution.py:108
  78.1 1.9 constant_dynamic-update-slice_fusion.14
  80.0 9.1 %collective-permute-done.11 = bf16[128,2048]{1,0:T(8,128)(2,1)} collective-permute-done((bf16[128,2048]{1,0:T(8,128)(2,1)}, bf16[128,2048]{1,0:T(8,128)(2,1)}, u32[]{:S(2)}, u32[]{:S(2)}) %collective-permute-start.11) | collective-permute-done | bytes 524320 | tf_op jit(solution)/shard_map/ppermute | solution.py:108
  89.7 1.5 collective-permute-start.13
  91.2 1.6 collective-permute-start.14
  94.4 1.7 convert_add_fusion.6
  96.4 8.5 %hidden_forward.2 = (bf16[1024,512]{1,0:T(8,128)(2,1)S(1)}, f32[1024,1024]{1,0:T(8,128)}) custom-call(bf16[1024,2176]{1,0:T(8,128)(2,1)} %constant_dynamic-update-slice_fusion.rows_ref, f32[1024,2]{1,0:T(8,128)S(1)} %get-tuple-element.161.weight_ref, bf16[2,2048,256]{2,1,0:T(8,128)(2,1)S(1)} %copy-done.1, bf16[2,2048,256]{2,1,0:T(8,128)(2,1)} %up_ref.1), custom_call_target="tpu_custom_call" | custom-call | flops 1 | bytes 1 | tf_op jit(solution)/shard_map/hidden_forward/pallas_call | solution.py:34
  105.0 8.9 %collective-permute-done.13 = bf16[128,2048]{1,0:T(8,128)(2,1)S(1)} collective-permute-done((bf16[128,2048]{1,0:T(8,128)(2,1)}, bf16[128,2048]{1,0:T(8,128)(2,1)S(1)}, u32[]{:S(2)}, u32[]{:S(2)}) %collective-permute-start.13) | collective-permute-done | bytes 524320 | tf_op jit(solution)/shard_map/ppermute | solution.py:108
  113.9 2.5 collective-permute-done.14
  116.4 9.1 %hidden_forward.3 = (bf16[1024,512]{1,0:T(8,128)(2,1)S(1)}, f32[1024,1024]{1,0:T(8,128)}) custom-call(bf16[1024,2176]{1,0:T(8,128)(2,1)} %constant_dynamic-update-slice_fusion.rows_ref, f32[1024,2]{1,0:T(8,128)S(1)} %get-tuple-element.160.weight_ref, bf16[2,2048,256]{2,1,0:T(8,128)(2,1)} %collective-permute-done.7.gate_ref, ...), custom_call_target="tpu_custom_call" | custom-call | flops 1 | bytes 1 | tf_op jit(solution)/shard_map/hidden_forward/pallas_call | solution.py:34
  127.5 2.8 mix_columns.3
  131.1 4.0 %copy.39 = bf16[2,256,2048]{2,1,0:T(8,128)(2,1)} copy(bf16[2,256,2048]{1,2,0:T(8,128)(2,1)} %bitcast.7) | data formatting | bytes 4194304 | tf_op jit(solution)/shard_map/transpose | solution.py:136
  135.1 2.0 constant_dynamic-update-slice_fusion.13
  137.1 1.9 constant_dynamic-update-slice_fusion.12
  139.0 1.9 constant_dynamic-update-slice_fusion.11
  140.9 1.9 constant_dynamic-update-slice_fusion.10
  142.9 2.7 pad_maximum_fusion.1.other_weight_ref
  147.9 1.6 collective-permute-start.18
  150.1 3.8 %fusion.24 = f32[1024,512]{1,0:T(8,128)} fusion(bf16[1024,2048]{1,0:T(8,128)(2,1)S(1)} %constant_dynamic-update-slice_fusion.8, bf16[512,2048]{1,0:T(8,128)(2,1)S(1)} %bitcast.20), kind=kOutput, calls=%fused_computation.64 | convolution fusion | flops 2147483648 | bytes 8388608 | tf_op jit(solution)/shard_map/dot_general | solution.py:188
  153.8 1.8 fusion.8
  155.6 3.6 %mix_columns.4 = (f32[512,768]{1,0:T(8,128)S(1)}, bf16[512,768]{1,0:T(8,128)(2,1)S(1)}) custom-call(bf16[1024,512]{1,0:T(8,128)(2,1)S(1)} %get-tuple-element.74.own_ref, bf16[1024,512]{1,0:T(8,128)(2,1)S(1)} %get-tuple-element.82.other_ref, bf16[512,2048]{1,0:T(8,128)(2,1)} %bitcast.18, bf16[512,768]{1,0:T(8,128)(2,1)} %collective-permute-done.15.other_weight_ref), custom_call_target="tpu_custom_call" | custom-call | flops 1 | bytes 1 | tf_op jit(solution)/shard_map/mix_columns/pallas_call | solution.py:73
  159.2 2.1 fusion.6
  162.6 4.6 %collective-permute-done.20.other_weight_ref = bf16[512,768]{1,0:T(8,128)(2,1)S(1)} collective-permute-done((bf16[512,768]{1,0:T(8,128)(2,1)S(1)}, bf16[512,768]{1,0:T(8,128)(2,1)S(1)}, u32[]{:S(2)}, u32[]{:S(2)}) %collective-permute-start.20) | collective-permute-done | bytes 786464 | tf_op jit(solution)/shard_map/ppermute | solution.py:108
  167.1 2.6 add_add_fusion
  171.1 2.5 fusion
  174.1 3.3 %mix_columns.5 = (f32[512,768]{1,0:T(8,128)S(1)}, bf16[512,768]{1,0:T(8,128)(2,1)S(1)}) custom-call(bf16[1024,512]{1,0:T(8,128)(2,1)S(1)} %get-tuple-element.74.own_ref, bf16[1024,512]{1,0:T(8,128)(2,1)S(1)} %get-tuple-element.82.other_ref, bf16[512,2048]{1,0:T(8,128)(2,1)} %bitcast.19, bf16[512,768]{1,0:T(8,128)(2,1)S(1)} %collective-permute-done.20.other_weight_ref), custom_call_target="tpu_custom_call" | custom-call | flops 1 | bytes 1 | tf_op jit(solution)/shard_map/mix_columns/pallas_call | solution.py:73
  177.7 3.4 %collective-permute-start.22 = (bf16[128,512]{1,0:T(8,128)(2,1)S(1)}, bf16[128,512]{1,0:T(8,128)(2,1)S(1)}, u32[]{:S(2)}, u32[]{:S(2)}) collective-permute-start(bf16[128,512]{1,0:T(8,128)(2,1)S(1)} %get-tuple-element.99), channel_id=1, source_target_pairs={{0,8},{1,9},{2,10},{3,11},{4,12},{5,13},{6,14},{7,15},{8,0},{9,1},... | collective-permute-start | bytes 393224 | tf_op jit(solution)/shard_map/ppermute | solution.py:108
  181.5 9.0 %collective-permute-done.19 = bf16[512,768]{1,0:T(8,128)(2,1)S(1)} collective-permute-done((bf16[512,768]{1,0:T(8,128)(2,1)S(1)}, bf16[512,768]{1,0:T(8,128)(2,1)S(1)}, u32[]{:S(2)}, u32[]{:S(2)}) %collective-permute-start.19) | collective-permute-done | bytes 786464 | tf_op jit(solution)/shard_map/ppermute | solution.py:108
  191.2 6.0 %back_columns.3 = (f32[512,768]{1,0:T(8,128)S(1)}, bf16[512,768]{1,0:T(8,128)(2,1)S(1)}) custom-call(bf16[1024,1024]{1,0:T(8,128)(2,1)S(1)} %get-tuple-element.165.own_ref, bf16[1024,1024]{1,0:T(8,128)(2,1)} %get-tuple-element.166.other_ref, bf16[1024,2048]{1,0:T(8,128)(2,1)} %pad_maximum_fusion.own_weight_ref, ...), custom_call_target="tpu_custom_call" | custom-call | flops 1 | bytes 1 | tf_op jit(solution)/shard_map/back_columns/pallas_call | solution.py:73
  197.2 1.6 collective-permute-start.24
  198.8 2.8 collective-permute-start.25
  201.6 5.6 %collective-permute-done.27 = bf16[512,768]{1,0:T(8,128)(2,1)S(1)} collective-permute-done((bf16[512,768]{1,0:T(8,128)(2,1)S(1)}, bf16[512,768]{1,0:T(8,128)(2,1)S(1)}, u32[]{:S(2)}, u32[]{:S(2)}) %collective-permute-start.27) | collective-permute-done | bytes 786464 | tf_op jit(solution)/shard_map/ppermute | solution.py:108
  207.4 4.5 %collective-permute-done.25 = bf16[128,768]{1,0:T(8,128)(2,1)S(1)} collective-permute-done((bf16[128,768]{1,0:T(8,128)(2,1)S(1)}, bf16[128,768]{1,0:T(8,128)(2,1)S(1)}, u32[]{:S(2)}, u32[]{:S(2)}) %collective-permute-start.25) | collective-permute-done | bytes 196640 | tf_op jit(solution)/shard_map/ppermute | solution.py:108
  213.2 6.0 %back_columns.4 = (f32[512,768]{1,0:T(8,128)S(1)}, bf16[512,768]{1,0:T(8,128)(2,1)S(1)}) custom-call(bf16[1024,1024]{1,0:T(8,128)(2,1)S(1)} %get-tuple-element.165.own_ref, bf16[1024,1024]{1,0:T(8,128)(2,1)} %get-tuple-element.166.other_ref, bf16[1024,2048]{1,0:T(8,128)(2,1)} %pad_maximum_fusion.own_weight_ref, ...), custom_call_target="tpu_custom_call" | custom-call | flops 1 | bytes 1 | tf_op jit(solution)/shard_map/back_columns/pallas_call | solution.py:73
  219.3 4.7 %collective-permute-start.28 = (bf16[128,768]{1,0:T(8,128)(2,1)S(1)}, bf16[128,768]{1,0:T(8,128)(2,1)S(1)}, u32[]{:S(2)}, u32[]{:S(2)}) collective-permute-start(bf16[128,768]{1,0:T(8,128)(2,1)S(1)} %get-tuple-element.108), channel_id=1, source_target_pairs={{0,4},{1,5},{2,6},{3,7},{4,8},{5,9},{6,10},{7,11},{8,12},{9,13},{1... | collective-permute-start | bytes 589832 | tf_op jit(solution)/shard_map/ppermute | solution.py:108
  226.4 4.8 %collective-permute-done.31 = bf16[512,768]{1,0:T(8,128)(2,1)S(1)} collective-permute-done((bf16[512,768]{1,0:T(8,128)(2,1)S(1)}, bf16[512,768]{1,0:T(8,128)(2,1)S(1)}, u32[]{:S(2)}, u32[]{:S(2)}) %collective-permute-start.31) | collective-permute-done | bytes 786464 | tf_op jit(solution)/shard_map/ppermute | solution.py:108
  231.5 5.4 %collective-permute-done.29 = bf16[128,768]{1,0:T(8,128)(2,1)S(1)} collective-permute-done((bf16[128,768]{1,0:T(8,128)(2,1)S(1)}, bf16[128,768]{1,0:T(8,128)(2,1)S(1)}, u32[]{:S(2)}, u32[]{:S(2)}) %collective-permute-start.29) | collective-permute-done | bytes 196640 | tf_op jit(solution)/shard_map/ppermute | solution.py:108
  238.2 4.2 %back_columns.5 = (f32[512,512]{1,0:T(8,128)S(1)}, bf16[512,512]{1,0:T(8,128)(2,1)S(1)}) custom-call(bf16[1024,1024]{1,0:T(8,128)(2,1)S(1)} %get-tuple-element.165.own_ref, bf16[1024,1024]{1,0:T(8,128)(2,1)S(1)} %copy-done, bf16[1024,2048]{1,0:T(8,128)(2,1)} %pad_maximum_fusion.own_weight_ref, bf16[1024,2048]{1,0:T(8,128)(2,1)} %pad_maximum_fusion.1.other_weight_ref), custom_call_target="tpu_custom_call" | custom-call | flops 1 | bytes 1 | tf_op jit(solution)/shard_map/back_columns/pallas_call | solution.py:73
  243.5 4.7 %collective-permute-start.32 = (bf16[128,768]{1,0:T(8,128)(2,1)S(1)}, bf16[128,768]{1,0:T(8,128)(2,1)S(1)}, u32[]{:S(2)}, u32[]{:S(2)}) collective-permute-start(bf16[128,768]{1,0:T(8,128)(2,1)S(1)} %get-tuple-element.114), channel_id=1, source_target_pairs={{0,4},{1,5},{2,6},{3,7},{4,8},{5,9},{6,10},{7,11},{8,12},{9,13},{1... | collective-permute-start | bytes 589832 | tf_op jit(solution)/shard_map/ppermute | solution.py:108
  248.2 2.1 collective-permute-start.33
  250.7 5.6 %collective-permute-done.35 = bf16[512,768]{1,0:T(8,128)(2,1)S(1)} collective-permute-done((bf16[512,768]{1,0:T(8,128)(2,1)S(1)}, bf16[512,768]{1,0:T(8,128)(2,1)S(1)}, u32[]{:S(2)}, u32[]{:S(2)}) %collective-permute-start.35) | collective-permute-done | bytes 786464 | tf_op jit(solution)/shard_map/ppermute | solution.py:108
  256.5 5.8 %collective-permute-done.33 = bf16[128,768]{1,0:T(8,128)(2,1)S(1)} collective-permute-done((bf16[128,768]{1,0:T(8,128)(2,1)S(1)}, bf16[128,768]{1,0:T(8,128)(2,1)S(1)}, u32[]{:S(2)}, u32[]{:S(2)}) %collective-permute-start.33) | collective-permute-done | bytes 196640 | tf_op jit(solution)/shard_map/ppermute | solution.py:108
  264.9 4.7 %collective-permute-start.36 = (bf16[128,768]{1,0:T(8,128)(2,1)S(1)}, bf16[128,768]{1,0:T(8,128)(2,1)S(1)}, u32[]{:S(2)}, u32[]{:S(2)}) collective-permute-start(bf16[128,768]{1,0:T(8,128)(2,1)S(1)} %get-tuple-element.120), channel_id=1, source_target_pairs={{0,4},{1,5},{2,6},{3,7},{4,8},{5,9},{6,10},{7,11},{8,12},{9,13},{1... | collective-permute-start | bytes 589832 | tf_op jit(solution)/shard_map/ppermute | solution.py:108
  272.1 4.0 %collective-permute-done.39 = bf16[512,512]{1,0:T(8,128)(2,1)S(1)} collective-permute-done((bf16[512,512]{1,0:T(8,128)(2,1)S(1)}, bf16[512,512]{1,0:T(8,128)(2,1)S(1)}, u32[]{:S(2)}, u32[]{:S(2)}) %collective-permute-start.39) | collective-permute-done | bytes 524320 | tf_op jit(solution)/shard_map/ppermute | solution.py:108
  276.3 6.2 %collective-permute-done.37 = bf16[128,768]{1,0:T(8,128)(2,1)S(1)} collective-permute-done((bf16[128,768]{1,0:T(8,128)(2,1)S(1)}, bf16[128,768]{1,0:T(8,128)(2,1)S(1)}, u32[]{:S(2)}, u32[]{:S(2)}) %collective-permute-start.37) | collective-permute-done | bytes 196640 | tf_op jit(solution)/shard_map/ppermute | solution.py:108
  282.5 4.7 %collective-permute-start.40 = (bf16[128,512]{1,0:T(8,128)(2,1)S(1)}, bf16[128,512]{1,0:T(8,128)(2,1)S(1)}, u32[]{:S(2)}, u32[]{:S(2)}) collective-permute-start(bf16[128,512]{1,0:T(8,128)(2,1)S(1)} %get-tuple-element.125), channel_id=1, source_target_pairs={{0,4},{1,5},{2,6},{3,7},{4,8},{5,9},{6,10},{7,11},{8,12},{9,13},{1... | collective-permute-start | bytes 393224 | tf_op jit(solution)/shard_map/ppermute | solution.py:108
  287.2 2.8 collective-permute-start.41
  290.1 3.8 %collective-permute-done.40 = bf16[128,512]{1,0:T(8,128)(2,1)S(1)} collective-permute-done((bf16[128,512]{1,0:T(8,128)(2,1)S(1)}, bf16[128,512]{1,0:T(8,128)(2,1)S(1)}, u32[]{:S(2)}, u32[]{:S(2)}) %collective-permute-start.40) | collective-permute-done | bytes 131104 | tf_op jit(solution)/shard_map/ppermute | solution.py:108
  293.9 4.1 %collective-permute-done.41 = bf16[128,512]{1,0:T(8,128)(2,1)S(1)} collective-permute-done((bf16[128,512]{1,0:T(8,128)(2,1)S(1)}, bf16[128,512]{1,0:T(8,128)(2,1)S(1)}, u32[]{:S(2)}, u32[]{:S(2)}) %collective-permute-start.41) | collective-permute-done | bytes 131104 | tf_op jit(solution)/shard_map/ppermute | solution.py:108
  (124 shorter events, 40.1 us)
Async XLA Ops:
  0.6 15.0 %copy-start.1 = (bf16[2,2048,256]{2,1,0:T(8,128)(2,1)S(1)}, bf16[2,2048,256]{2,1,0:T(8,128)(2,1)}, u32[]{:S(2)}) copy-start(bf16[2,2048,256]{2,1,0:T(8,128)(2,1)} %gate_ref.1) | copy-start | bytes 6291460
  3.0 25.2 %collective-permute-start.3 = (bf16[128,2048]{1,0:T(8,128)(2,1)}, bf16[128,2048]{1,0:T(8,128)(2,1)}, u32[]{:S(2)}, u32[]{:S(2)}) collective-permute-start(bf16[128,2048]{1,0:T(8,128)(2,1)} %param.8), channel_id=1, source_target_pairs={{0,2},{1,3},{2,0},{3,1},{4,6},{5,7},{6,4},{7,5},{8,10},{9,11},{10,... | collective-permute-start | bytes 1572872 | tf_op jit(solution)/shard_map/ppermute | solution.py:108
  6.0 22.2 %collective-permute-start = (bf16[128,2176]{1,0:T(8,128)(2,1)S(1)}, bf16[128,2176]{1,0:T(8,128)(2,1)}, u32[]{:S(2)}, u32[]{:S(2)}) collective-permute-start(bf16[128,2176]{1,0:T(8,128)(2,1)S(1)} %concatenate.27), channel_id=1, source_target_pairs={{0,12},{1,13},{2,14},{3,15},{4,0},{5,1},{6,2},{7,3},{8,4},{9,5},{1... | collective-permute-start | bytes 1671176 | tf_op jit(solution)/shard_map/ppermute | solution.py:108
  9.6 24.6 %collective-permute-start.1 = (bf16[128,2176]{1,0:T(8,128)(2,1)S(1)}, bf16[128,2176]{1,0:T(8,128)(2,1)}, u32[]{:S(2)}, u32[]{:S(2)}) collective-permute-start(bf16[128,2176]{1,0:T(8,128)(2,1)S(1)} %concatenate.27), channel_id=1, source_target_pairs={{0,4},{1,5},{2,6},{3,7},{4,8},{5,9},{6,10},{7,11},{8,12},{9,13},{1... | collective-permute-start | bytes 1671176 | tf_op jit(solution)/shard_map/ppermute | solution.py:108
  9.6 24.6 %collective-permute-start.2 = (bf16[128,2176]{1,0:T(8,128)(2,1)S(1)}, bf16[128,2176]{1,0:T(8,128)(2,1)S(1)}, u32[]{:S(2)}, u32[]{:S(2)}) collective-permute-start(bf16[128,2176]{1,0:T(8,128)(2,1)S(1)} %concatenate.27), channel_id=1, source_target_pairs={{0,2},{1,3},{2,0},{3,1},{4,6},{5,7},{6,4},{7,5},{8,10},{9,11},{10,... | collective-permute-start | bytes 1671176 | tf_op jit(solution)/shard_map/ppermute | solution.py:108
  10.1 54.0 %collective-permute-start.7 = (bf16[2,2048,256]{2,1,0:T(8,128)(2,1)}, bf16[2,2048,256]{2,1,0:T(8,128)(2,1)}, u32[]{:S(2)}, u32[]{:S(2)}) collective-permute-start(bf16[2,2048,256]{2,1,0:T(8,128)(2,1)} %gate_ref.1), channel_id=1, source_target_pairs={{0,1},{1,0},{2,3},{3,2},{4,5},{5,4},{6,7},{7,6},{8,9},{9,8},{10,11... | collective-permute-start | bytes 6291464 | tf_op jit(solution)/shard_map/ppermute | solution.py:108
  34.2 26.1 %collective-permute-start.4 = (bf16[128,2176]{1,0:T(8,128)(2,1)S(1)}, bf16[128,2176]{1,0:T(8,128)(2,1)}, u32[]{:S(2)}, u32[]{:S(2)}) collective-permute-start(bf16[128,2176]{1,0:T(8,128)(2,1)S(1)} %concatenate.27), channel_id=1, source_target_pairs={{0,8},{1,9},{2,10},{3,11},{4,12},{5,13},{6,14},{7,15},{8,0},{9,1},... | collective-permute-start | bytes 1671176 | tf_op jit(solution)/shard_map/ppermute | solution.py:108
  36.8 27.3 %collective-permute-start.5 = (bf16[128,2176]{1,0:T(8,128)(2,1)}, bf16[128,2176]{1,0:T(8,128)(2,1)S(1)}, u32[]{:S(2)}, u32[]{:S(2)}) collective-permute-start(bf16[128,2176]{1,0:T(8,128)(2,1)} %collective-permute-done), channel_id=1, source_target_pairs={{0,2},{1,3},{2,0},{3,1},{4,6},{5,7},{6,4},{7,5},{8,10},{9,11},{10,... | collective-permute-start | bytes 1671176 | tf_op jit(solution)/shard_map/ppermute | solution.py:108
  37.3 26.8 %collective-permute-start.6 = (bf16[128,2176]{1,0:T(8,128)(2,1)}, bf16[128,2176]{1,0:T(8,128)(2,1)S(1)}, u32[]{:S(2)}, u32[]{:S(2)}) collective-permute-start(bf16[128,2176]{1,0:T(8,128)(2,1)} %collective-permute-done.1), channel_id=1, source_target_pairs={{0,2},{1,3},{2,0},{3,1},{4,6},{5,7},{6,4},{7,5},{8,10},{9,11},{10,... | collective-permute-start | bytes 1671176 | tf_op jit(solution)/shard_map/ppermute | solution.py:108
  38.8 66.2 %collective-permute-start.9 = (bf16[2,2048,256]{2,1,0:T(8,128)(2,1)}, bf16[2,2048,256]{2,1,0:T(8,128)(2,1)}, u32[]{:S(2)}, u32[]{:S(2)}) collective-permute-start(bf16[2,2048,256]{2,1,0:T(8,128)(2,1)} %up_ref.1), channel_id=1, source_target_pairs={{0,1},{1,0},{2,3},{3,2},{4,5},{5,4},{6,7},{7,6},{8,9},{9,8},{10,11... | collective-permute-start | bytes 6291464 | tf_op jit(solution)/shard_map/ppermute | solution.py:108
  64.1 2.3 copy-start.13
  64.1 14.1 %collective-permute-start.10 = (bf16[128,2048]{1,0:T(8,128)(2,1)}, bf16[128,2048]{1,0:T(8,128)(2,1)}, u32[]{:S(2)}, u32[]{:S(2)}) collective-permute-start(bf16[128,2048]{1,0:T(8,128)(2,1)} %param.8), channel_id=1, source_target_pairs={{0,12},{1,13},{2,14},{3,15},{4,0},{5,1},{6,2},{7,3},{8,4},{9,5},{1... | collective-permute-start | bytes 1572872 | tf_op jit(solution)/shard_map/ppermute | solution.py:108
  66.3 22.8 %collective-permute-start.11 = (bf16[128,2048]{1,0:T(8,128)(2,1)}, bf16[128,2048]{1,0:T(8,128)(2,1)}, u32[]{:S(2)}, u32[]{:S(2)}) collective-permute-start(bf16[128,2048]{1,0:T(8,128)(2,1)} %param.8), channel_id=1, source_target_pairs={{0,4},{1,5},{2,6},{3,7},{4,8},{5,9},{6,10},{7,11},{8,12},{9,13},{1... | collective-permute-start | bytes 1572872 | tf_op jit(solution)/shard_map/ppermute | solution.py:108
  67.0 26.6 %copy-start.14 = (bf16[128,2176]{1,0:T(8,128)(2,1)S(1)}, bf16[128,2176]{1,0:T(8,128)(2,1)}, u32[]{:S(2)}) copy-start(bf16[128,2176]{1,0:T(8,128)(2,1)} %copy-done.13) | copy-start | bytes 1671172
  67.0 22.1 %collective-permute-start.8 = (bf16[128,2176]{1,0:T(8,128)(2,1)}, bf16[128,2176]{1,0:T(8,128)(2,1)S(1)}, u32[]{:S(2)}, u32[]{:S(2)}) collective-permute-start(bf16[128,2176]{1,0:T(8,128)(2,1)} %collective-permute-done.4), channel_id=1, source_target_pairs={{0,2},{1,3},{2,0},{3,1},{4,6},{5,7},{6,4},{7,5},{8,10},{9,11},{10,... | collective-permute-start | bytes 1671176 | tf_op jit(solution)/shard_map/ppermute | solution.py:108
  68.4 57.1 %collective-permute-start.16 = (bf16[512,512]{1,0:T(8,128)(2,1)}, bf16[512,512]{1,0:T(8,128)(2,1)}, u32[]{:S(2)}, u32[]{:S(2)}) collective-permute-start(bf16[512,512]{1,0:T(8,128)(2,1)} %slice.150), channel_id=1, source_target_pairs={{0,1},{1,0},{2,3},{3,2},{4,5},{5,4},{6,7},{7,6},{8,9},{9,8},{10,11... | collective-permute-start | bytes 1572872 | tf_op jit(solution)/shard_map/ppermute | solution.py:108
  89.1 15.8 %collective-permute-start.12 = (bf16[128,2048]{1,0:T(8,128)(2,1)}, bf16[128,2048]{1,0:T(8,128)(2,1)S(1)}, u32[]{:S(2)}, u32[]{:S(2)}) collective-permute-start(bf16[128,2048]{1,0:T(8,128)(2,1)} %collective-permute-done.10), channel_id=1, source_target_pairs={{0,2},{1,3},{2,0},{3,1},{4,6},{5,7},{6,4},{7,5},{8,10},{9,11},{10,... | collective-permute-start | bytes 1572872 | tf_op jit(solution)/shard_map/ppermute | solution.py:108
  89.7 24.3 %collective-permute-start.13 = (bf16[128,2048]{1,0:T(8,128)(2,1)}, bf16[128,2048]{1,0:T(8,128)(2,1)S(1)}, u32[]{:S(2)}, u32[]{:S(2)}) collective-permute-start(bf16[128,2048]{1,0:T(8,128)(2,1)} %collective-permute-done.11), channel_id=1, source_target_pairs={{0,2},{1,3},{2,0},{3,1},{4,6},{5,7},{6,4},{7,5},{8,10},{9,11},{10,... | collective-permute-start | bytes 1572872 | tf_op jit(solution)/shard_map/ppermute | solution.py:108
  91.2 25.2 %collective-permute-start.14 = (bf16[128,2048]{1,0:T(8,128)(2,1)}, bf16[128,2048]{1,0:T(8,128)(2,1)}, u32[]{:S(2)}, u32[]{:S(2)}) collective-permute-start(bf16[128,2048]{1,0:T(8,128)(2,1)} %param.8), channel_id=1, source_target_pairs={{0,8},{1,9},{2,10},{3,11},{4,12},{5,13},{6,14},{7,15},{8,0},{9,1},... | collective-permute-start | bytes 1572872 | tf_op jit(solution)/shard_map/ppermute | solution.py:108
  105.0 11.4 %copy-start.17 = (bf16[128,2048]{1,0:T(8,128)(2,1)}, bf16[128,2048]{1,0:T(8,128)(2,1)S(1)}, u32[]{:S(2)}) copy-start(bf16[128,2048]{1,0:T(8,128)(2,1)S(1)} %collective-permute-done.12) | copy-start | bytes 1572868
  113.9 2.5 copy-start.15
  125.5 20.1 %collective-permute-start.17 = (bf16[128,2048]{1,0:T(8,128)(2,1)}, bf16[128,2048]{1,0:T(8,128)(2,1)}, u32[]{:S(2)}, u32[]{:S(2)}) collective-permute-start(bf16[128,2048]{1,0:T(8,128)(2,1)} %collective-permute-done.14), channel_id=1, source_target_pairs={{0,2},{1,3},{2,0},{3,1},{4,6},{5,7},{6,4},{7,5},{8,10},{9,11},{10,... | collective-permute-start | bytes 1572872 | tf_op jit(solution)/shard_map/ppermute | solution.py:108
  126.0 29.6 %collective-permute-start.15 = (bf16[512,768]{1,0:T(8,128)(2,1)}, bf16[512,768]{1,0:T(8,128)(2,1)}, u32[]{:S(2)}, u32[]{:S(2)}) collective-permute-start(bf16[512,768]{1,0:T(8,128)(2,1)} %get-tuple-element.83), channel_id=1, source_target_pairs={{0,1},{1,0},{2,3},{3,2},{4,5},{5,4},{6,7},{7,6},{8,9},{9,8},{10,11... | collective-permute-start | bytes 2359304 | tf_op jit(solution)/shard_map/ppermute | solution.py:108
  130.3 0.8 copy-start.2
  135.1 7.8 %copy-start.5 = (bf16[2,256,2048]{2,1,0:T(8,128)(2,1)S(1)}, bf16[2,256,2048]{2,1,0:T(8,128)(2,1)}, u32[]{:S(2)}) copy-start(bf16[2,256,2048]{2,1,0:T(8,128)(2,1)} %copy.36) | copy-start | bytes 6291460
  135.1 7.8 %copy-start.6 = (bf16[2,256,2048]{2,1,0:T(8,128)(2,1)S(1)}, bf16[2,256,2048]{2,1,0:T(8,128)(2,1)}, u32[]{:S(2)}) copy-start(bf16[2,256,2048]{2,1,0:T(8,128)(2,1)} %copy.39) | copy-start | bytes 6291460
  142.8 3.7 %copy-start.9 = (bf16[1024,2048]{1,0:T(8,128)(2,1)S(1)}, bf16[1024,2048]{1,0:T(8,128)(2,1)}, u32[]{:S(2)}) copy-start(bf16[1024,2048]{1,0:T(8,128)(2,1)} %constant_dynamic-update-slice_fusion.10) | copy-start | bytes 12582916
  142.8 5.0 %copy-start.16 = (bf16[128,2048]{1,0:T(8,128)(2,1)S(1)}, bf16[128,2048]{1,0:T(8,128)(2,1)}, u32[]{:S(2)}) copy-start(bf16[128,2048]{1,0:T(8,128)(2,1)} %copy-done.15) | copy-start | bytes 1572868
  142.9 5.1 %copy-start.3 = (bf16[512,512]{1,0:T(8,128)(2,1)S(1)}, bf16[512,512]{1,0:T(8,128)(2,1)}, u32[]{:S(2)}) copy-start(bf16[512,512]{1,0:T(8,128)(2,1)} %copy-done.2) | copy-start | bytes 1572868
  142.9 6.7 %copy-start.12 = (bf16[512,768]{1,0:T(8,128)(2,1)S(1)}, bf16[512,768]{1,0:T(8,128)(2,1)}, u32[]{:S(2)}) copy-start(bf16[512,768]{1,0:T(8,128)(2,1)} %get-tuple-element.95) | copy-start | bytes 2359300
  142.9 7.2 %copy-start.4 = (bf16[2,256,2048]{2,1,0:T(8,128)(2,1)S(1)}, bf16[2,256,2048]{2,1,0:T(8,128)(2,1)}, u32[]{:S(2)}) copy-start(bf16[2,256,2048]{2,1,0:T(8,128)(2,1)} %param.13) | copy-start | bytes 6291460
  147.9 11.3 %copy-start.10 = (bf16[1024,2048]{1,0:T(8,128)(2,1)}, bf16[1024,2048]{1,0:T(8,128)(2,1)S(1)}, u32[]{:S(2)}) copy-start(bf16[1024,2048]{1,0:T(8,128)(2,1)S(1)} %constant_dynamic-update-slice_fusion.8) | copy-start | bytes 12582916
  147.9 13.4 %collective-permute-start.18 = (bf16[512,512]{1,0:T(8,128)(2,1)S(1)}, bf16[512,512]{1,0:T(8,128)(2,1)S(1)}, u32[]{:S(2)}, u32[]{:S(2)}) collective-permute-start(bf16[512,512]{1,0:T(8,128)(2,1)S(1)} %copy-done.3), channel_id=1, source_target_pairs={{0,2},{1,3},{2,0},{3,1},{4,6},{5,7},{6,4},{7,5},{8,10},{9,11},{10,... | collective-permute-start | bytes 1572872 | tf_op jit(solution)/shard_map/ppermute | solution.py:108
  149.5 17.6 %collective-permute-start.20 = (bf16[512,768]{1,0:T(8,128)(2,1)S(1)}, bf16[512,768]{1,0:T(8,128)(2,1)S(1)}, u32[]{:S(2)}, u32[]{:S(2)}) collective-permute-start(bf16[512,768]{1,0:T(8,128)(2,1)S(1)} %copy-done.12), channel_id=1, source_target_pairs={{0,1},{1,0},{2,3},{3,2},{4,5},{5,4},{6,7},{7,6},{8,9},{9,8},{10,11... | collective-permute-start | bytes 2359304 | tf_op jit(solution)/shard_map/ppermute | solution.py:108
  161.4 8.4 %copy-start.11 = (f32[1024,512]{1,0:T(8,128)S(1)}, f32[1024,512]{1,0:T(8,128)}, u32[]{:S(2)}) copy-start(f32[1024,512]{1,0:T(8,128)} %fusion.24) | copy-start | bytes 6291460
  167.1 2.7 copy-start.7
  167.1 3.9 %copy-start.8 = (f32[1024,1024]{1,0:T(8,128)S(1)}, f32[1024,1024]{1,0:T(8,128)}, u32[]{:S(2)}) copy-start(f32[1024,1024]{1,0:T(8,128)} %get-tuple-element.106) | copy-start | bytes 12582916
  173.6 17.0 %collective-permute-start.19 = (bf16[512,768]{1,0:T(8,128)(2,1)S(1)}, bf16[512,768]{1,0:T(8,128)(2,1)S(1)}, u32[]{:S(2)}, u32[]{:S(2)}) collective-permute-start(bf16[512,768]{1,0:T(8,128)(2,1)S(1)} %get-tuple-element.94), channel_id=1, source_target_pairs={{0,2},{1,3},{2,0},{3,1},{4,6},{5,7},{6,4},{7,5},{8,10},{9,11},{10,... | collective-permute-start | bytes 2359304 | tf_op jit(solution)/shard_map/ppermute | solution.py:108
  177.4 13.4 %collective-permute-start.21 = (bf16[128,512]{1,0:T(8,128)(2,1)S(1)}, bf16[128,512]{1,0:T(8,128)(2,1)S(1)}, u32[]{:S(2)}, u32[]{:S(2)}) collective-permute-start(bf16[128,512]{1,0:T(8,128)(2,1)S(1)} %get-tuple-element.98), channel_id=1, source_target_pairs={{0,4},{1,5},{2,6},{3,7},{4,8},{5,9},{6,10},{7,11},{8,12},{9,13},{1... | collective-permute-start | bytes 393224 | tf_op jit(solution)/shard_map/ppermute | solution.py:108
  177.7 13.1 %collective-permute-start.22 = (bf16[128,512]{1,0:T(8,128)(2,1)S(1)}, bf16[128,512]{1,0:T(8,128)(2,1)S(1)}, u32[]{:S(2)}, u32[]{:S(2)}) collective-permute-start(bf16[128,512]{1,0:T(8,128)(2,1)S(1)} %get-tuple-element.99), channel_id=1, source_target_pairs={{0,8},{1,9},{2,10},{3,11},{4,12},{5,13},{6,14},{7,15},{8,0},{9,1},... | collective-permute-start | bytes 393224 | tf_op jit(solution)/shard_map/ppermute | solution.py:108
  181.1 9.7 %collective-permute-start.23 = (bf16[128,512]{1,0:T(8,128)(2,1)S(1)}, bf16[128,512]{1,0:T(8,128)(2,1)S(1)}, u32[]{:S(2)}, u32[]{:S(2)}) collective-permute-start(bf16[128,512]{1,0:T(8,128)(2,1)S(1)} %get-tuple-element.100), channel_id=1, source_target_pairs={{0,12},{1,13},{2,14},{3,15},{4,0},{5,1},{6,2},{7,3},{8,4},{9,5},{1... | collective-permute-start | bytes 393224 | tf_op jit(solution)/shard_map/ppermute | solution.py:108
  190.8 16.3 %collective-permute-start.27 = (bf16[512,768]{1,0:T(8,128)(2,1)S(1)}, bf16[512,768]{1,0:T(8,128)(2,1)S(1)}, u32[]{:S(2)}, u32[]{:S(2)}) collective-permute-start(bf16[512,768]{1,0:T(8,128)(2,1)S(1)} %get-tuple-element.105), channel_id=1, source_target_pairs={{0,2},{1,3},{2,0},{3,1},{4,6},{5,7},{6,4},{7,5},{8,10},{9,11},{10,... | collective-permute-start | bytes 2359304 | tf_op jit(solution)/shard_map/ppermute | solution.py:108
  197.2 10.2 %collective-permute-start.24 = (bf16[128,768]{1,0:T(8,128)(2,1)S(1)}, bf16[128,768]{1,0:T(8,128)(2,1)S(1)}, u32[]{:S(2)}, u32[]{:S(2)}) collective-permute-start(bf16[128,768]{1,0:T(8,128)(2,1)S(1)} %get-tuple-element.101), channel_id=1, source_target_pairs={{0,4},{1,5},{2,6},{3,7},{4,8},{5,9},{6,10},{7,11},{8,12},{9,13},{1... | collective-permute-start | bytes 589832 | tf_op jit(solution)/shard_map/ppermute | solution.py:108
  198.8 13.1 %collective-permute-start.25 = (bf16[128,768]{1,0:T(8,128)(2,1)S(1)}, bf16[128,768]{1,0:T(8,128)(2,1)S(1)}, u32[]{:S(2)}, u32[]{:S(2)}) collective-permute-start(bf16[128,768]{1,0:T(8,128)(2,1)S(1)} %get-tuple-element.102), channel_id=1, source_target_pairs={{0,8},{1,9},{2,10},{3,11},{4,12},{5,13},{6,14},{7,15},{8,0},{9,1},... | collective-permute-start | bytes 589832 | tf_op jit(solution)/shard_map/ppermute | solution.py:108
  201.6 10.3 %collective-permute-start.26 = (bf16[128,768]{1,0:T(8,128)(2,1)S(1)}, bf16[128,768]{1,0:T(8,128)(2,1)S(1)}, u32[]{:S(2)}, u32[]{:S(2)}) collective-permute-start(bf16[128,768]{1,0:T(8,128)(2,1)S(1)} %get-tuple-element.103), channel_id=1, source_target_pairs={{0,12},{1,13},{2,14},{3,15},{4,0},{5,1},{6,2},{7,3},{8,4},{9,5},{1... | collective-permute-start | bytes 589832 | tf_op jit(solution)/shard_map/ppermute | solution.py:108
  211.8 19.4 %collective-permute-start.31 = (bf16[512,768]{1,0:T(8,128)(2,1)S(1)}, bf16[512,768]{1,0:T(8,128)(2,1)S(1)}, u32[]{:S(2)}, u32[]{:S(2)}) collective-permute-start(bf16[512,768]{1,0:T(8,128)(2,1)S(1)} %get-tuple-element.112), channel_id=1, source_target_pairs={{0,2},{1,3},{2,0},{3,1},{4,6},{5,7},{6,4},{7,5},{8,10},{9,11},{10,... | collective-permute-start | bytes 2359304 | tf_op jit(solution)/shard_map/ppermute | solution.py:108
  219.2 19.0 %copy-start = (bf16[1024,1024]{1,0:T(8,128)(2,1)S(1)}, bf16[1024,1024]{1,0:T(8,128)(2,1)}, u32[]{:S(2)}) copy-start(bf16[1024,1024]{1,0:T(8,128)(2,1)} %get-tuple-element.166.other_ref) | copy-start | bytes 6291460
  219.3 12.2 %collective-permute-start.28 = (bf16[128,768]{1,0:T(8,128)(2,1)S(1)}, bf16[128,768]{1,0:T(8,128)(2,1)S(1)}, u32[]{:S(2)}, u32[]{:S(2)}) collective-permute-start(bf16[128,768]{1,0:T(8,128)(2,1)S(1)} %get-tuple-element.108), channel_id=1, source_target_pairs={{0,4},{1,5},{2,6},{3,7},{4,8},{5,9},{6,10},{7,11},{8,12},{9,13},{1... | collective-permute-start | bytes 589832 | tf_op jit(solution)/shard_map/ppermute | solution.py:108
  224.0 12.9 %collective-permute-start.29 = (bf16[128,768]{1,0:T(8,128)(2,1)S(1)}, bf16[128,768]{1,0:T(8,128)(2,1)S(1)}, u32[]{:S(2)}, u32[]{:S(2)}) collective-permute-start(bf16[128,768]{1,0:T(8,128)(2,1)S(1)} %get-tuple-element.109), channel_id=1, source_target_pairs={{0,8},{1,9},{2,10},{3,11},{4,12},{5,13},{6,14},{7,15},{8,0},{9,1},... | collective-permute-start | bytes 589832 | tf_op jit(solution)/shard_map/ppermute | solution.py:108
  225.3 11.6 %collective-permute-start.30 = (bf16[128,768]{1,0:T(8,128)(2,1)S(1)}, bf16[128,768]{1,0:T(8,128)(2,1)S(1)}, u32[]{:S(2)}, u32[]{:S(2)}) collective-permute-start(bf16[128,768]{1,0:T(8,128)(2,1)S(1)} %get-tuple-element.110), channel_id=1, source_target_pairs={{0,12},{1,13},{2,14},{3,15},{4,0},{5,1},{6,2},{7,3},{8,4},{9,5},{1... | collective-permute-start | bytes 589832 | tf_op jit(solution)/shard_map/ppermute | solution.py:108
  236.9 19.4 %collective-permute-start.35 = (bf16[512,768]{1,0:T(8,128)(2,1)S(1)}, bf16[512,768]{1,0:T(8,128)(2,1)S(1)}, u32[]{:S(2)}, u32[]{:S(2)}) collective-permute-start(bf16[512,768]{1,0:T(8,128)(2,1)S(1)} %get-tuple-element.118), channel_id=1, source_target_pairs={{0,2},{1,3},{2,0},{3,1},{4,6},{5,7},{6,4},{7,5},{8,10},{9,11},{10,... | collective-permute-start | bytes 2359304 | tf_op jit(solution)/shard_map/ppermute | solution.py:108
  243.5 13.0 %collective-permute-start.32 = (bf16[128,768]{1,0:T(8,128)(2,1)S(1)}, bf16[128,768]{1,0:T(8,128)(2,1)S(1)}, u32[]{:S(2)}, u32[]{:S(2)}) collective-permute-start(bf16[128,768]{1,0:T(8,128)(2,1)S(1)} %get-tuple-element.114), channel_id=1, source_target_pairs={{0,4},{1,5},{2,6},{3,7},{4,8},{5,9},{6,10},{7,11},{8,12},{9,13},{1... | collective-permute-start | bytes 589832 | tf_op jit(solution)/shard_map/ppermute | solution.py:108
  248.2 14.0 %collective-permute-start.33 = (bf16[128,768]{1,0:T(8,128)(2,1)S(1)}, bf16[128,768]{1,0:T(8,128)(2,1)S(1)}, u32[]{:S(2)}, u32[]{:S(2)}) collective-permute-start(bf16[128,768]{1,0:T(8,128)(2,1)S(1)} %get-tuple-element.115), channel_id=1, source_target_pairs={{0,8},{1,9},{2,10},{3,11},{4,12},{5,13},{6,14},{7,15},{8,0},{9,1},... | collective-permute-start | bytes 589832 | tf_op jit(solution)/shard_map/ppermute | solution.py:108
  250.3 11.9 %collective-permute-start.34 = (bf16[128,768]{1,0:T(8,128)(2,1)S(1)}, bf16[128,768]{1,0:T(8,128)(2,1)S(1)}, u32[]{:S(2)}, u32[]{:S(2)}) collective-permute-start(bf16[128,768]{1,0:T(8,128)(2,1)S(1)} %get-tuple-element.116), channel_id=1, source_target_pairs={{0,12},{1,13},{2,14},{3,15},{4,0},{5,1},{6,2},{7,3},{8,4},{9,5},{1... | collective-permute-start | bytes 589832 | tf_op jit(solution)/shard_map/ppermute | solution.py:108
  262.3 13.8 %collective-permute-start.39 = (bf16[512,512]{1,0:T(8,128)(2,1)S(1)}, bf16[512,512]{1,0:T(8,128)(2,1)S(1)}, u32[]{:S(2)}, u32[]{:S(2)}) collective-permute-start(bf16[512,512]{1,0:T(8,128)(2,1)S(1)} %get-tuple-element.124), channel_id=1, source_target_pairs={{0,2},{1,3},{2,0},{3,1},{4,6},{5,7},{6,4},{7,5},{8,10},{9,11},{10,... | collective-permute-start | bytes 1572872 | tf_op jit(solution)/shard_map/ppermute | solution.py:108
  264.9 11.4 %collective-permute-start.36 = (bf16[128,768]{1,0:T(8,128)(2,1)S(1)}, bf16[128,768]{1,0:T(8,128)(2,1)S(1)}, u32[]{:S(2)}, u32[]{:S(2)}) collective-permute-start(bf16[128,768]{1,0:T(8,128)(2,1)S(1)} %get-tuple-element.120), channel_id=1, source_target_pairs={{0,4},{1,5},{2,6},{3,7},{4,8},{5,9},{6,10},{7,11},{8,12},{9,13},{1... | collective-permute-start | bytes 589832 | tf_op jit(solution)/shard_map/ppermute | solution.py:108
  269.6 12.9 %collective-permute-start.37 = (bf16[128,768]{1,0:T(8,128)(2,1)S(1)}, bf16[128,768]{1,0:T(8,128)(2,1)S(1)}, u32[]{:S(2)}, u32[]{:S(2)}) collective-permute-start(bf16[128,768]{1,0:T(8,128)(2,1)S(1)} %get-tuple-element.121), channel_id=1, source_target_pairs={{0,8},{1,9},{2,10},{3,11},{4,12},{5,13},{6,14},{7,15},{8,0},{9,1},... | collective-permute-start | bytes 589832 | tf_op jit(solution)/shard_map/ppermute | solution.py:108
  270.6 11.9 %collective-permute-start.38 = (bf16[128,768]{1,0:T(8,128)(2,1)S(1)}, bf16[128,768]{1,0:T(8,128)(2,1)S(1)}, u32[]{:S(2)}, u32[]{:S(2)}) collective-permute-start(bf16[128,768]{1,0:T(8,128)(2,1)S(1)} %get-tuple-element.122), channel_id=1, source_target_pairs={{0,12},{1,13},{2,14},{3,15},{4,0},{5,1},{6,2},{7,3},{8,4},{9,5},{1... | collective-permute-start | bytes 589832 | tf_op jit(solution)/shard_map/ppermute | solution.py:108
  282.5 11.4 %collective-permute-start.40 = (bf16[128,512]{1,0:T(8,128)(2,1)S(1)}, bf16[128,512]{1,0:T(8,128)(2,1)S(1)}, u32[]{:S(2)}, u32[]{:S(2)}) collective-permute-start(bf16[128,512]{1,0:T(8,128)(2,1)S(1)} %get-tuple-element.125), channel_id=1, source_target_pairs={{0,4},{1,5},{2,6},{3,7},{4,8},{5,9},{6,10},{7,11},{8,12},{9,13},{1... | collective-permute-start | bytes 393224 | tf_op jit(solution)/shard_map/ppermute | solution.py:108
  287.2 10.8 %collective-permute-start.41 = (bf16[128,512]{1,0:T(8,128)(2,1)S(1)}, bf16[128,512]{1,0:T(8,128)(2,1)S(1)}, u32[]{:S(2)}, u32[]{:S(2)}) collective-permute-start(bf16[128,512]{1,0:T(8,128)(2,1)S(1)} %get-tuple-element.126), channel_id=1, source_target_pairs={{0,8},{1,9},{2,10},{3,11},{4,12},{5,13},{6,14},{7,15},{8,0},{9,1},... | collective-permute-start | bytes 393224 | tf_op jit(solution)/shard_map/ppermute | solution.py:108
  290.0 8.1 %collective-permute-start.42 = (bf16[128,512]{1,0:T(8,128)(2,1)S(1)}, bf16[128,512]{1,0:T(8,128)(2,1)S(1)}, u32[]{:S(2)}, u32[]{:S(2)}) collective-permute-start(bf16[128,512]{1,0:T(8,128)(2,1)S(1)} %get-tuple-element.127), channel_id=1, source_target_pairs={{0,12},{1,13},{2,14},{3,15},{4,0},{5,1},{6,2},{7,3},{8,4},{9,5},{1... | collective-permute-start | bytes 393224 | tf_op jit(solution)/shard_map/ppermute | solution.py:108

commit v5 on v0

--- a/solution.py
+++ b/solution.py
@@ -1,7 +1,351 @@
+import functools
+
 import jax
 import jax.numpy as jnp
 from jax import lax
+from jax.experimental import pallas as pl
+from jax.experimental.pallas import tpu as pltpu
 from jax.sharding import PartitionSpec as P
+
+VMEM_BYTES = 32 * 2**20
+AT_ONCE = pl.CostEstimate(flops=1, bytes_accessed=1, transcendentals=0)
+
+
+def compiler_params():
+    return pltpu.CompilerParams(vmem_limit_bytes=VMEM_BYTES)
+
+
+def fetch_rows(block_refs, buffer, sems):
+    step = pl.program_id(0)
+    count = len(block_refs) // pl.num_programs(0)
+
+    @pl.when(step == 0)
+    def _():
+        for j, ref in enumerate(block_refs):
+            pltpu.make_async_copy(ref, buffer.at[j], sems.at[j]).start()
+
+    for j in range(len(block_refs)):
+
+        @pl.when(step == j // count)
+        def _(j=j):
+            pltpu.make_async_copy(block_refs[j], buffer.at[j], sems.at[j]).wait()
+
+    rows = buffer[pl.ds(step * count, count)]
+    return rows.reshape(count * rows.shape[1], rows.shape[2])
+
+
+def hidden_kernel(blocks, all_experts, owner_ref, gate_ref, up_ref, *refs):
+    activ_ref, by_ref, buffer, sems = refs[blocks:]
+    experts, width, hidden = gate_ref.shape
+    rows = fetch_rows(refs[:blocks], buffer, sems)
+    terms = rows[:, width:].astype(jnp.float32)
+    rows = rows[:, :width]
+    lanes = lax.broadcasted_iota(jnp.int32, terms.shape, 1)
+    for e in range(experts):
+        cut = slice(e * hidden, (e + 1) * hidden)
+        cut_up = slice((experts + e) * hidden, (experts + e + 1) * hidden)
+        label = owner_ref[0] * experts + e
+        named = (lanes == label) | (lanes == label + all_experts) | (lanes == label + 2 * all_experts)
+        weight = jnp.sum(jnp.where(named, terms, 0.0), axis=1, keepdims=True)
+        gate_pre = jnp.dot(rows, gate_ref[e], preferred_element_type=jnp.float32)
+        up_pre = jnp.dot(rows, up_ref[e], preferred_element_type=jnp.float32)
+        sig = jax.nn.sigmoid(gate_pre)
+        factor = sig * weight
+        silu = gate_pre * factor
+        activ_ref[:, cut] = (silu * up_pre).astype(jnp.bfloat16)
+        by_ref[:, cut] = up_pre * factor * (1.0 + gate_pre * (1.0 - sig))
+        by_ref[:, cut_up] = silu
+
+
+def hidden_forward(row_blocks, owner, gate_weight, up_weight, all_experts):
+    blocks = len(row_blocks)
+    block, row_width = row_blocks[0].shape
+    experts, width, hidden = gate_weight.shape
+    count, columns, tile = blocks * block, experts * hidden, 2 * block
+    weights = pl.BlockSpec((experts, width, hidden), lambda i: (0, 0, 0))
+    return pl.pallas_call(
+        functools.partial(hidden_kernel, blocks, all_experts),
+        grid=(blocks // 2,),
+        in_specs=[pl.BlockSpec(memory_space=pltpu.SMEM), weights, weights]
+        + [pl.BlockSpec(memory_space=pl.ANY)] * blocks,
+        out_specs=[
+            pl.BlockSpec((tile, columns), lambda i: (i, 0)),
+            pl.BlockSpec((tile, 2 * columns), lambda i: (i, 0)),
+        ],
+        out_shape=[
+            jax.ShapeDtypeStruct((count, columns), jnp.bfloat16),
+            jax.ShapeDtypeStruct((count, 2 * columns), jnp.float32),
+        ],
+        scratch_shapes=[
+            pltpu.VMEM((blocks, block, row_width), jnp.bfloat16),
+            pltpu.SemaphoreType.DMA((blocks,)),
+        ],
+        compiler_params=compiler_params(),
+        cost_estimate=AT_ONCE,
+        name="hidden_forward",
+    )(owner.reshape(1), gate_weight, up_weight, *row_blocks)
+
+
+NT = (((1,), (1,)), ((), ()))
+
+
+def grads_kernel(blocks, chunks, by_ref, *refs):
+    down_refs, block_refs = refs[: len(chunks)], refs[len(chunks) : len(chunks) + blocks]
+    out_ref, buffer, sems = refs[len(chunks) + blocks :]
+    rows = fetch_rows(block_refs, buffer, sems)
+    total = None
+    for (lo, hi), down_ref in zip(chunks, down_refs):
+        term = lax.dot_general(rows[:, lo:hi], down_ref[...], NT, preferred_element_type=jnp.float32)
+        total = term if total is None else total + term
+    columns = total.shape[1]
+    out_ref[:, :columns] = (total * by_ref[:, :columns]).astype(jnp.bfloat16)
+    out_ref[:, columns:] = (total * by_ref[:, columns:]).astype(jnp.bfloat16)
+
+
+def hidden_grads(grad_blocks, by, downs, chunks):
+    blocks = len(grad_blocks)
+    block, width = grad_blocks[0].shape
+    tile = 2 * block
+    rows = pl.BlockSpec((tile, by.shape[1]), lambda i: (i, 0))
+    return pl.pallas_call(
+        functools.partial(grads_kernel, blocks, tuple(chunks)),
+        grid=(blocks // 2,),
+        in_specs=[rows]
+        + [pl.BlockSpec(d.shape, lambda i: (0, 0)) for d in downs]
+        + [pl.BlockSpec(memory_space=pl.ANY)] * blocks,
+        out_specs=rows,
+        out_shape=jax.ShapeDtypeStruct(by.shape, jnp.bfloat16),
+        scratch_shapes=[
+            pltpu.VMEM((blocks, block, width), jnp.bfloat16),
+            pltpu.SemaphoreType.DMA((blocks,)),
+        ],
+        compiler_params=compiler_params(),
+        cost_estimate=AT_ONCE,
+        name="hidden_grads",
+    )(by, *downs, *grad_blocks)
+
+
+def store_half(total, keep_ref, send_ref):
+    @pl.when(pl.program_id(0) == 0)
+    def _():
+        send_ref[...] = total.astype(send_ref.dtype)
+
+    @pl.when(pl.program_id(0) == 1)
+    def _():
+        keep_ref[...] = total
+
+
+def mix_kernel(own_ref, other_ref, own_down_ref, other_down_ref, keep_ref, send_ref):
+    total = jnp.dot(own_ref[...], own_down_ref[...], preferred_element_type=jnp.float32)
+    total += jnp.dot(other_ref[...], other_down_ref[...], preferred_element_type=jnp.float32)
+    store_half(total, keep_ref, send_ref)
+
+
+def back_kernel(own_ref, other_ref, *refs):
+    weight_refs, (keep_ref, send_ref) = refs[:-2], refs[-2:]
+    experts, _, hidden = weight_refs[0].shape
+    total = None
+    for at, weight_ref in enumerate(weight_refs):
+        grads_ref = (own_ref, other_ref)[at // 2]
+        for e in range(experts):
+            first = (at % 2 * experts + e) * hidden
+            term = lax.dot_general(
+                grads_ref[:, first : first + hidden], weight_ref[e], NT, preferred_element_type=jnp.float32
+            )
+            total = term if total is None else total + term
+    store_half(total, keep_ref, send_ref)
+
+
+def sum_columns(kernel, name, columns, own, other, weights, weight_specs):
+    half, depth = own.shape[0] // 2, own.shape[1]
+    rows = pl.BlockSpec((half, depth), lambda i: (1 - i, 0))
+    return pl.pallas_call(
+        kernel,
+        grid=(2,),
+        in_specs=[rows, rows] + weight_specs,
+        out_specs=[pl.BlockSpec((half, columns), lambda i: (0, 0))] * 2,
+        out_shape=[
+            jax.ShapeDtypeStruct((half, columns), jnp.float32),
+            jax.ShapeDtypeStruct((half, columns), jnp.bfloat16),
+        ],
+        compiler_params=compiler_params(),
+        cost_estimate=AT_ONCE,
+        name=name,
+    )(own, other, *weights)
+
+
+def mix_columns(own, other, own_down, other_down, at):
+    depth, columns = other_down.shape
+    specs = [
+        pl.BlockSpec((depth, columns), lambda i: (0, at)),
+        pl.BlockSpec((depth, columns), lambda i: (0, 0)),
+    ]
+    return sum_columns(mix_kernel, "mix_columns", columns, own, other, [own_down, other_down], specs)
+
+
+def back_columns(own, other, weights, at, columns):
+    experts, _, hidden = weights[0].shape
+    specs = [pl.BlockSpec((experts, columns, hidden), lambda i: (0, at, 0))] * len(weights)
+    return sum_columns(back_kernel, "back_columns", columns, own, other, weights, specs)
+
+
+def add_kernel(keep_ref, come_ref, own_ref, *piece_refs):
+    block = own_ref.shape[0]
+    own_ref[...] = keep_ref[:block, :] + come_ref[:block, :].astype(jnp.float32)
+    for k, piece_ref in enumerate(piece_refs, 1):
+        cut = slice(k * block, (k + 1) * block)
+        total = keep_ref[cut, :] + come_ref[cut, :].astype(jnp.float32)
+        piece_ref[...] = total.astype(piece_ref.dtype)
+
+
+def add_sides(keep, come, layers):
+    block, columns = keep.shape[0] // layers, keep.shape[1]
+    pieces = [jax.ShapeDtypeStruct((block, columns), jnp.bfloat16)] * (layers - 1)
+    return pl.pallas_call(
+        add_kernel,
+        out_shape=[jax.ShapeDtypeStruct((block, columns), jnp.float32)] + pieces,
+        compiler_params=compiler_params(),
+        cost_estimate=AT_ONCE,
+        name="add_sides",
+    )(keep, come)
+
+
+def finish_kernel(chunks, layers, *refs):
+    out_ref = refs[-1]
+    for c, (lo, hi) in enumerate(chunks):
+        own_ref, *piece_refs = refs[c * layers : (c + 1) * layers]
+        total = own_ref[...]
+        for piece_ref in piece_refs:
+            total += piece_ref[...].astype(jnp.float32)
+        out_ref[:, lo:hi] = total
+
+
+def finish(chunks, parts, width):
+    return pl.pallas_call(
+        functools.partial(finish_kernel, tuple(chunks), len(parts[0])),
+        out_shape=jax.ShapeDtypeStruct((parts[0][0].shape[0], width), jnp.float32),
+        compiler_params=compiler_params(),
+        cost_estimate=AT_ONCE,
+        name="finish",
+    )(*[p for part in parts for p in part])
+
+
+def cut_columns(width, eighths):
+    eighth = width // 8
+    return [(lo * eighth, hi * eighth) for lo, hi in eighths]
+
+
+def after(values, *others):
+    return lax.optimization_barrier((values, *others))[0]
+
+
+def send_all(sends, *waits):
+    values, _ = lax.optimization_barrier(([v for v, _ in sends], waits))
+    return [lax.ppermute(v, "expert", pairs) for v, (_, pairs) in zip(values, sends)]
+
+
+def on_device_dense(tokens, cotangent, expert_ids, probs, gate_weight, up_weight, down_weight):
+    local_count, hidden, width = down_weight.shape
+    devices = lax.axis_size("expert")
+    layers = devices // 4
+    experts = local_count * devices
+    block = tokens.shape[0]
+    chunks = cut_columns(width, ((6, 8), (0, 3), (3, 6)))
+    back_chunks = cut_columns(width, ((0, 3), (3, 6), (6, 8)))
+    me = lax.axis_index("expert")
+    twin = [(d, d ^ 1) for d in range(devices)]
+    side = [(d, d ^ 2) for d in range(devices)]
+    layer = [[(d, (d + 4 * k) % devices) for d in range(devices)] for k in range(layers)]
+
+    labels = lax.broadcasted_iota(jnp.int32, (1, 1, experts), 2)
+    weight = jnp.sum(jnp.where(expert_ids[:, :, None] == labels, probs[:, :, None], 0.0), axis=1)
+    first = lax.reduce_precision(weight, 8, 7)
+    second = lax.reduce_precision(weight - first, 8, 7)
+    third = weight - first - second
+    spare = jnp.zeros((block, -3 * experts % 128), jnp.bfloat16)
+    terms = [t.astype(jnp.bfloat16) for t in (first, second, third)]
+    row = jnp.concatenate([tokens] + terms + [spare], axis=1)
+    grad = cotangent
+    down = down_weight.reshape(local_count * hidden, width)
+    downs = [down[:, lo:hi] for lo, hi in chunks]
+
+    one, last, *middle = [1, layers - 1, *range(2, layers - 1)]
+    rows, far_rows, grads, far_grads = {0: row}, {}, {0: grad}, {}
+    other_gate, rows[one], far_rows[0] = send_all([(gate_weight, twin), (row, layer[-one]), (row, side)])
+    rows[last], far_grads[0] = send_all([(row, layer[-last]), (grad, side)])
+    got = send_all([(rows[one], side)] + [(row, layer[-k]) for k in middle], far_rows[0])
+    far_rows[one] = got[0]
+    rows.update(zip(middle, got[1:]))
+    other_up, far_rows[last] = send_all([(up_weight, twin), (rows[last], side)], far_grads[0])
+    got = send_all(
+        [(grad, layer[-one])] + [(rows[k], side) for k in middle], far_rows[one]
+    )
+    grads[one] = got[0]
+    far_rows.update(zip(middle, got[1:]))
+    down_0, grads[last] = send_all([(downs[0], twin), (grad, layer[-last])], far_rows[last], other_gate)
+    got = send_all(
+        [(grads[one], side)] + [(grad, layer[-k]) for k in middle], *far_rows.values()
+    )
+    far_grads[one] = got[0]
+    grads.update(zip(middle, got[1:]))
+    row_blocks = [rows[k] for k in range(layers)] + [far_rows[k] for k in range(layers)]
+    activ, by = hidden_forward(row_blocks, me, gate_weight, up_weight, experts)
+    (far_grads[last],) = send_all([(grads[last], side)], activ)
+    waits = [other_up, far_grads[one]]
+    got = send_all([(downs[1], twin)] + [(grads[k], side) for k in middle], *waits)
+    down_1 = got[0]
+    far_grads.update(zip(middle, got[1:]))
+
+    other_up = after(other_up, *waits)
+    other_activ, other_by = hidden_forward(row_blocks, me ^ 1, other_gate, other_up, experts)
+
+    def mix(c, other_down, *waits):
+        lo, hi = chunks[c]
+        return mix_columns(activ, other_activ, down, after(other_down, *waits), lo // (hi - lo))
+
+    def across(pieces):
+        return [(piece, layer[k]) for k, piece in enumerate(pieces, 1)]
+
+    keep_0, send = mix(0, down_0, other_activ)
+    come_0, down_2 = send_all([(send, side), (downs[2], twin)], far_grads[last])
+    grad_blocks = [grads[k] for k in range(layers)] + [far_grads[k] for k in range(layers)]
+    own_grads = hidden_grads(grad_blocks, by, [down], [(0, width)])
+
+    keep_1, send = mix(1, down_1, send)
+    own_0, *pieces = add_sides(keep_0, come_0, layers)
+    come_1, *parts_0 = send_all([(send, side)] + across(pieces), own_grads)
+
+    keep_2, send = mix(2, down_2, send)
+    own_1, *pieces = add_sides(keep_1, come_1, layers)
+    come_2, *parts_1 = send_all([(send, side)] + across(pieces), *parts_0)
+
+    other_grads = hidden_grads(grad_blocks, other_by, [down_0, down_1, down_2], chunks)
+    weights = [gate_weight, up_weight, other_gate, other_up]
+
+    def back(c):
+        lo, hi = back_chunks[c]
+        return back_columns(own_grads, other_grads, weights, lo // (hi - lo), hi - lo)
+
+    keep_3, send = back(0)
+    (come_3,) = send_all([(send, side)])
+
+    keep_4, send = back(1)
+    own_2, *pieces = add_sides(keep_2, come_2, layers)
+    come_4, *parts_2 = send_all([(send, side)] + across(pieces), *parts_1)
+
+    keep_5, send = back(2)
+    own_3, *pieces = add_sides(keep_3, come_3, layers)
+    come_5, *parts_3 = send_all([(send, side)] + across(pieces), *parts_2)
+
+    own_4, *pieces = add_sides(keep_4, come_4, layers)
+    parts_4 = send_all(across(pieces), *parts_3)
+
+    own_5, *pieces = add_sides(keep_5, after(come_5, own_4), layers)
+    parts_5 = send_all(across(pieces))
+
+    mixed = finish(chunks, [(own_0, *parts_0), (own_1, *parts_1), (own_2, *parts_2)], width)
+    back_sum = finish(back_chunks, [(own_3, *parts_3), (own_4, *parts_4), (own_5, *parts_5)], width)
+    return (mixed, back_sum)
 
 
 def route_slots(expert_ids, local_count, device_count, capacity):
@@ -62,7 +406,7 @@
     return jnp.sum(picked.astype(jnp.float32) * probs[:, :, None], axis=1)
 
 
-def on_device(tokens, cotangent, expert_ids, probs, gate_weight, up_weight, down_weight):
+def on_device_routed(tokens, cotangent, expert_ids, probs, gate_weight, up_weight, down_weight):
     local_count = gate_weight.shape[0]
     device_count = lax.axis_size("expert")
     experts = local_count * device_count
@@ -87,6 +431,13 @@
     return (mixed, input_grad)
 
 
+def on_device(tokens, cotangent, expert_ids, probs, gate_weight, up_weight, down_weight):
+    devices = lax.axis_size("expert")
+    dense = devices % 4 == 0 and 16 <= devices <= 2 * expert_ids.shape[1]
+    body = on_device_dense if dense else on_device_routed
+    return body(tokens, cotangent, expert_ids, probs, gate_weight, up_weight, down_weight)
+
+
 def solution(mesh):
     in_specs = (
         P(("dp", "expert"), None),

time: 736 us -> 270 us (0.37)
  the two profiles are of different devices: /device:TPU:14 before, /device:TPU:0 now
where the time goes in v5:
time: 270 us; the launch traced here: 268 us
  waiting for transfers between devices  93.6 us (35%)
  starting transfers between devices  85.8 us (32%)
  Pallas kernels  51 us (19%)
  local copies, waits for them, and re-layouts  36.1 us (13%)
    ppermute x43, waiting for transfers between devices, send_all(): lax.ppermute(v, 'expert', pairs)  93.6 us
    ppermute x43, starting transfers between devices, send_all(): lax.ppermute(v, 'expert', pairs)  85.8 us
    unnamed x74, local copies, waits for them, and re-layouts  31.6 us
    pallas_call x6, Pallas kernels, sum_columns(): pl.pallas_call(kernel, grid=(2,), in_specs=[rows, rows] + weight_specs, o...  23.5 us
    pallas_call x2, Pallas kernels, hidden_forward(): pl.pallas_call(functools.partial(hidden_kernel, blocks, all_experts), gri...  13.7 us
    pallas_call x2, Pallas kernels, hidden_grads(): pl.pallas_call(functools.partial(grads_kernel, blocks, tuple(chunks)), gr...  10.8 us
  transfers between devices with their start and end apart: 43, of which 14 were waited for; matrix products, arithmetic and copies ran while one was open for 1% of the time, Pallas kernels for 19%

profile of v5, /device:TPU:0, one launch (start us, length us, event | category | flops | bytes accessed | tf_op | source)
XLA Modules:
  0.0 268.4 jit_solution(1900435133992080685)
XLA Ops:
  1.6 1.2 concatenate.3.refs_0_
  2.8 3.0 %collective-permute-start.8 = (bf16[2,2048,256]{2,1,0:T(8,128)(2,1)}, bf16[2,2048,256]{2,1,0:T(8,128)(2,1)S(1)}, u32[]{:S(2)}, u32[]{:S(2)}) collective-permute-start(bf16[2,2048,256]{2,1,0:T(8,128)(2,1)} %refs_0_.5), channel_id=1, source_target_pairs={{0,1},{1,0},{2,3},{3,2},{4,5},{5,4},{6,7},{7,6},{8,9},{9,8},{10,11... | collective-permute-start | bytes 6291464 | tf_op jit(solution)/shard_map/ppermute | solution.py:244
  5.8 1.6 collective-permute-start.3
  7.4 1.5 collective-permute-start.6
  9.4 2.2 collective-permute-start
  11.7 10.8 %collective-permute-done.6.refs_5_.refs_7_ = bf16[128,2048]{1,0:T(8,128)(2,1)S(1)} collective-permute-done((bf16[128,2048]{1,0:T(8,128)(2,1)}, bf16[128,2048]{1,0:T(8,128)(2,1)S(1)}, u32[]{:S(2)}, u32[]{:S(2)}) %collective-permute-start.6) | collective-permute-done | bytes 524320 | tf_op jit(solution)/shard_map/ppermute | solution.py:244
  23.8 8.8 %collective-permute-done.1.refs_4_ = bf16[128,2176]{1,0:T(8,128)(2,1)S(1)} collective-permute-done((bf16[128,2176]{1,0:T(8,128)(2,1)S(1)}, bf16[128,2176]{1,0:T(8,128)(2,1)S(1)}, u32[]{:S(2)}, u32[]{:S(2)}) %collective-permute-start.1) | collective-permute-done | bytes 557088 | tf_op jit(solution)/shard_map/ppermute | solution.py:244
  33.7 1.5 collective-permute-start.4
  36.0 2.3 collective-permute-start.2
  39.7 9.5 %collective-permute-done.4.refs_5_ = bf16[128,2176]{1,0:T(8,128)(2,1)S(1)} collective-permute-done((bf16[128,2176]{1,0:T(8,128)(2,1)S(1)}, bf16[128,2176]{1,0:T(8,128)(2,1)S(1)}, u32[]{:S(2)}, u32[]{:S(2)}) %collective-permute-start.4) | collective-permute-done | bytes 557088 | tf_op jit(solution)/shard_map/ppermute | solution.py:244
  50.1 13.0 %collective-permute-done.2.refs_2_ = bf16[128,2176]{1,0:T(8,128)(2,1)S(1)} collective-permute-done((bf16[128,2176]{1,0:T(8,128)(2,1)S(1)}, bf16[128,2176]{1,0:T(8,128)(2,1)S(1)}, u32[]{:S(2)}, u32[]{:S(2)}) %collective-permute-start.2) | collective-permute-done | bytes 557088 | tf_op jit(solution)/shard_map/ppermute | solution.py:244
  64.9 1.9 slice.12
  67.6 1.4 copy-done.5
  69.0 1.5 collective-permute-start.13
  70.5 18.7 %collective-permute-done.10.refs_2_.refs_4_ = bf16[128,2048]{1,0:T(8,128)(2,1)} collective-permute-done((bf16[128,2048]{1,0:T(8,128)(2,1)}, bf16[128,2048]{1,0:T(8,128)(2,1)}, u32[]{:S(2)}, u32[]{:S(2)}) %collective-permute-start.10) | collective-permute-done | bytes 524320 | tf_op jit(solution)/shard_map/ppermute | solution.py:244
  90.1 1.5 collective-permute-start.11
  91.6 1.6 copy-done.1
  93.2 1.6 copy-done.3
  96.9 1.1 copy-done.17
  97.9 1.1 copy-done.20
  99.0 1.1 copy-done.23
  101.1 1.1 copy-done.29
  102.1 1.1 copy-done.32
  103.2 6.0 %hidden_forward.2 = (bf16[1024,512]{1,0:T(8,128)(2,1)S(1)}, f32[1024,1024]{1,0:T(8,128)S(1)}) custom-call(s32[1]{0:T(128)} %bitcast.owner_ref, bf16[2,2048,256]{2,1,0:T(8,128)(2,1)S(1)} %copy-done.1, bf16[2,2048,256]{2,1,0:T(8,128)(2,1)S(1)} %copy-done.3, bf16[128,2176]{1,0:T(8,128)(2,1)S(1)} %copy-done.9, bf16[128,2176]{1,0:T(8,128)(2,1)S(1)} %copy-done.20, ...), custom_call_target="tpu_custom_call" | custom-call | flops 1 | bytes 1 | tf_op jit(solution)/shard_map/hidden_forward/pallas_call | solution.py:66
  109.2 2.0 copy-done.11
  112.3 1.3 fusion.1
  113.5 1.6 collective-permute-start.17
  115.1 1.5 collective-permute-start.18
  116.6 1.6 copy-done.6
  118.2 1.1 copy-done.10
  119.3 1.1 copy-done.15
  126.6 7.7 %hidden_forward.3 = (bf16[1024,512]{1,0:T(8,128)(2,1)S(1)}, f32[1024,1024]{1,0:T(8,128)S(1)}) custom-call(s32[1]{0:T(128)} %bitcast.1.owner_ref, bf16[2,2048,256]{2,1,0:T(8,128)(2,1)S(1)} %copy-done.6, bf16[2,2048,256]{2,1,0:T(8,128)(2,1)} %collective-permute-done.9.up_ref.refs_3_, bf16[128,2176]{1,0:T(8,128)(2,1)S(1)} %copy-done.10, ...), custom_call_target="tpu_custom_call" | custom-call | flops 1 | bytes 1 | tf_op jit(solution)/shard_map/hidden_forward/pallas_call | solution.py:66
  134.4 2.8 %mix_columns.3 = (f32[512,512]{1,0:T(8,128)S(1)}, bf16[512,512]{1,0:T(8,128)(2,1)S(1)}) custom-call(bf16[1024,512]{1,0:T(8,128)(2,1)S(1)} %get-tuple-element.97.own_ref, bf16[1024,512]{1,0:T(8,128)(2,1)S(1)} %get-tuple-element.103.other_ref, bf16[512,2048]{1,0:T(8,128)(2,1)S(1)} %bitcast.5, bf16[512,512]{1,0:T(8,128)(2,1)} %collective-permute-done.12.other_down_ref.refs_0_), custom_call_target="tpu_custom_call" | custom-call | flops 1 | bytes 1 | tf_op jit(solution)/shard_map/mix_columns/pallas_call | solution.py:162
  138.3 4.3 %hidden_grads.2.own_ref = bf16[1024,1024]{1,0:T(8,128)(2,1)S(1)} custom-call(f32[1024,1024]{1,0:T(8,128)S(1)} %copy-done.12, bf16[512,2048]{1,0:T(8,128)(2,1)S(1)} %bitcast.6, bf16[128,2048]{1,0:T(8,128)(2,1)} %refs_3_.1, bf16[128,2048]{1,0:T(8,128)(2,1)} %collective-permute-done.10.refs_2_.refs_4_, ...), custom_call_target="tpu_custom_call" | custom-call | flops 1 | bytes 1 | tf_op jit(solution)/shard_map/hidden_grads/pallas_call | solution.py:110
  142.7 3.4 %mix_columns.4 = (f32[512,768]{1,0:T(8,128)S(1)}, bf16[512,768]{1,0:T(8,128)(2,1)S(1)}) custom-call(bf16[1024,512]{1,0:T(8,128)(2,1)S(1)} %get-tuple-element.97.own_ref, bf16[1024,512]{1,0:T(8,128)(2,1)S(1)} %get-tuple-element.103.other_ref, bf16[512,2048]{1,0:T(8,128)(2,1)S(1)} %bitcast.7, bf16[512,768]{1,0:T(8,128)(2,1)} %collective-permute-done.17.other_down_ref.refs_1_), custom_call_target="tpu_custom_call" | custom-call | flops 1 | bytes 1 | tf_op jit(solution)/shard_map/mix_columns/pallas_call | solution.py:162
  146.0 2.9 %collective-permute-done.15.come_ref = bf16[512,512]{1,0:T(8,128)(2,1)S(1)} collective-permute-done((bf16[512,512]{1,0:T(8,128)(2,1)S(1)}, bf16[512,512]{1,0:T(8,128)(2,1)S(1)}, u32[]{:S(2)}, u32[]{:S(2)}) %collective-permute-start.15) | collective-permute-done | bytes 524320 | tf_op jit(solution)/shard_map/ppermute | solution.py:244
  149.2 5.4 %collective-permute-start.20 = (bf16[128,512]{1,0:T(8,128)(2,1)S(1)}, bf16[128,512]{1,0:T(8,128)(2,1)S(1)}, u32[]{:S(2)}, u32[]{:S(2)}) collective-permute-start(bf16[128,512]{1,0:T(8,128)(2,1)S(1)} %get-tuple-element.122), channel_id=1, source_target_pairs={{0,8},{1,9},{2,10},{3,11},{4,12},{5,13},{6,14},{7,15},{8,0},{9,1},... | collective-permute-start | bytes 393224 | tf_op jit(solution)/shard_map/ppermute | solution.py:244
  154.6 2.8 %collective-permute-start.21 = (bf16[128,512]{1,0:T(8,128)(2,1)S(1)}, bf16[128,512]{1,0:T(8,128)(2,1)S(1)}, u32[]{:S(2)}, u32[]{:S(2)}) collective-permute-start(bf16[128,512]{1,0:T(8,128)(2,1)S(1)} %get-tuple-element.123), channel_id=1, source_target_pairs={{0,12},{1,13},{2,14},{3,15},{4,0},{5,1},{6,2},{7,3},{8,4},{9,5},{1... | collective-permute-start | bytes 393224 | tf_op jit(solution)/shard_map/ppermute | solution.py:244
  157.4 3.1 %mix_columns.5 = (f32[512,768]{1,0:T(8,128)S(1)}, bf16[512,768]{1,0:T(8,128)(2,1)}) custom-call(bf16[1024,512]{1,0:T(8,128)(2,1)S(1)} %get-tuple-element.97.own_ref, bf16[1024,512]{1,0:T(8,128)(2,1)S(1)} %get-tuple-element.103.other_ref, bf16[512,2048]{1,0:T(8,128)(2,1)S(1)} %bitcast.8, bf16[512,768]{1,0:T(8,128)(2,1)S(1)} %collective-permute-done.23.other_down_ref.refs_2_), custom_call_target="tpu_custom_call" | custom-call | flops 1 | bytes 1 | tf_op jit(solution)/shard_map/mix_columns/pallas_call | solution.py:162
  160.5 5.9 %collective-permute-done.22.come_ref = bf16[512,768]{1,0:T(8,128)(2,1)S(1)} collective-permute-done((bf16[512,768]{1,0:T(8,128)(2,1)S(1)}, bf16[512,768]{1,0:T(8,128)(2,1)S(1)}, u32[]{:S(2)}, u32[]{:S(2)}) %collective-permute-start.22) | collective-permute-done | bytes 786464 | tf_op jit(solution)/shard_map/ppermute | solution.py:244
  166.6 6.5 %hidden_grads.3.other_ref = bf16[1024,1024]{1,0:T(8,128)(2,1)S(1)} custom-call(f32[1024,1024]{1,0:T(8,128)S(1)} %get-tuple-element.139.by_ref, bf16[512,512]{1,0:T(8,128)(2,1)} %collective-permute-done.12.other_down_ref.refs_0_, bf16[512,768]{1,0:T(8,128)(2,1)} %collective-permute-done.17.other_down_ref.refs_1_, ...), custom_call_target="tpu_custom_call" | custom-call | flops 1 | bytes 1 | tf_op jit(solution)/shard_map/hidden_grads/pallas_call | solution.py:110
  173.1 5.2 %back_columns.4 = (f32[512,768]{1,0:T(8,128)S(1)}, bf16[512,768]{1,0:T(8,128)(2,1)S(1)}) custom-call(bf16[1024,1024]{1,0:T(8,128)(2,1)S(1)} %hidden_grads.2.own_ref, bf16[1024,1024]{1,0:T(8,128)(2,1)S(1)} %hidden_grads.3.other_ref, bf16[2,2048,256]{2,1,0:T(8,128)(2,1)S(1)} %copy-done.2, bf16[2,2048,256]{2,1,0:T(8,128)(2,1)S(1)} %copy-done.4, ...), custom_call_target="tpu_custom_call" | custom-call | flops 1 | bytes 1 | tf_op jit(solution)/shard_map/back_columns/pallas_call | solution.py:162
  178.4 2.0 collective-permute-start.31
  180.4 5.7 %collective-permute-start.25 = (bf16[128,768]{1,0:T(8,128)(2,1)S(1)}, bf16[128,768]{1,0:T(8,128)(2,1)S(1)}, u32[]{:S(2)}, u32[]{:S(2)}) collective-permute-start(bf16[128,768]{1,0:T(8,128)(2,1)S(1)} %get-tuple-element.134), channel_id=1, source_target_pairs={{0,8},{1,9},{2,10},{3,11},{4,12},{5,13},{6,14},{7,15},{8,0},{9,1},... | collective-permute-start | bytes 589832 | tf_op jit(solution)/shard_map/ppermute | solution.py:244
  186.1 2.9 %collective-permute-start.26 = (bf16[128,768]{1,0:T(8,128)(2,1)S(1)}, bf16[128,768]{1,0:T(8,128)(2,1)S(1)}, u32[]{:S(2)}, u32[]{:S(2)}) collective-permute-start(bf16[128,768]{1,0:T(8,128)(2,1)S(1)} %get-tuple-element.135), channel_id=1, source_target_pairs={{0,12},{1,13},{2,14},{3,15},{4,0},{5,1},{6,2},{7,3},{8,4},{9,5},{1... | collective-permute-start | bytes 589832 | tf_op jit(solution)/shard_map/ppermute | solution.py:244
  189.0 5.2 %back_columns.3 = (f32[512,768]{1,0:T(8,128)S(1)}, bf16[512,768]{1,0:T(8,128)(2,1)S(1)}) custom-call(bf16[1024,1024]{1,0:T(8,128)(2,1)S(1)} %hidden_grads.2.own_ref, bf16[1024,1024]{1,0:T(8,128)(2,1)S(1)} %hidden_grads.3.other_ref, bf16[2,2048,256]{2,1,0:T(8,128)(2,1)S(1)} %copy-done.2, bf16[2,2048,256]{2,1,0:T(8,128)(2,1)S(1)} %copy-done.4, ...), custom_call_target="tpu_custom_call" | custom-call | flops 1 | bytes 1 | tf_op jit(solution)/shard_map/back_columns/pallas_call | solution.py:162
  194.4 3.9 %collective-permute-done.25.refs_6_ = bf16[128,768]{1,0:T(8,128)(2,1)S(1)} collective-permute-done((bf16[128,768]{1,0:T(8,128)(2,1)S(1)}, bf16[128,768]{1,0:T(8,128)(2,1)S(1)}, u32[]{:S(2)}, u32[]{:S(2)}) %collective-permute-start.25) | collective-permute-done | bytes 196640 | tf_op jit(solution)/shard_map/ppermute | solution.py:244
  198.3 6.2 %collective-permute-start.28 = (bf16[128,768]{1,0:T(8,128)(2,1)S(1)}, bf16[128,768]{1,0:T(8,128)(2,1)S(1)}, u32[]{:S(2)}, u32[]{:S(2)}) collective-permute-start(bf16[128,768]{1,0:T(8,128)(2,1)S(1)} %get-tuple-element.144), channel_id=1, source_target_pairs={{0,4},{1,5},{2,6},{3,7},{4,8},{5,9},{6,10},{7,11},{8,12},{9,13},{1... | collective-permute-start | bytes 589832 | tf_op jit(solution)/shard_map/ppermute | solution.py:244
  204.5 3.4 %collective-permute-start.29 = (bf16[128,768]{1,0:T(8,128)(2,1)S(1)}, bf16[128,768]{1,0:T(8,128)(2,1)S(1)}, u32[]{:S(2)}, u32[]{:S(2)}) collective-permute-start(bf16[128,768]{1,0:T(8,128)(2,1)S(1)} %get-tuple-element.145), channel_id=1, source_target_pairs={{0,8},{1,9},{2,10},{3,11},{4,12},{5,13},{6,14},{7,15},{8,0},{9,1},... | collective-permute-start | bytes 589832 | tf_op jit(solution)/shard_map/ppermute | solution.py:244
  207.9 3.9 %back_columns.5 = (f32[512,512]{1,0:T(8,128)S(1)}, bf16[512,512]{1,0:T(8,128)(2,1)S(1)}) custom-call(bf16[1024,1024]{1,0:T(8,128)(2,1)S(1)} %hidden_grads.2.own_ref, bf16[1024,1024]{1,0:T(8,128)(2,1)S(1)} %hidden_grads.3.other_ref, bf16[2,2048,256]{2,1,0:T(8,128)(2,1)S(1)} %copy-done.2, bf16[2,2048,256]{2,1,0:T(8,128)(2,1)S(1)} %copy-done.4, ...), custom_call_target="tpu_custom_call" | custom-call | flops 1 | bytes 1 | tf_op jit(solution)/shard_map/back_columns/pallas_call | solution.py:162
  211.9 1.3 collective-permute-done.28.refs_9_
  213.2 7.4 %collective-permute-done.29.refs_10_ = bf16[128,768]{1,0:T(8,128)(2,1)S(1)} collective-permute-done((bf16[128,768]{1,0:T(8,128)(2,1)S(1)}, bf16[128,768]{1,0:T(8,128)(2,1)S(1)}, u32[]{:S(2)}, u32[]{:S(2)}) %collective-permute-start.29) | collective-permute-done | bytes 196640 | tf_op jit(solution)/shard_map/ppermute | solution.py:244
  220.8 10.0 %collective-permute-start.32 = (bf16[128,768]{1,0:T(8,128)(2,1)S(1)}, bf16[128,768]{1,0:T(8,128)(2,1)S(1)}, u32[]{:S(2)}, u32[]{:S(2)}) collective-permute-start(bf16[128,768]{1,0:T(8,128)(2,1)S(1)} %get-tuple-element.154), channel_id=1, source_target_pairs={{0,4},{1,5},{2,6},{3,7},{4,8},{5,9},{6,10},{7,11},{8,12},{9,13},{1... | collective-permute-start | bytes 589832 | tf_op jit(solution)/shard_map/ppermute | solution.py:244
  230.8 2.4 collective-permute-start.34
  233.4 6.7 %collective-permute-start.40 = (bf16[128,512]{1,0:T(8,128)(2,1)S(1)}, bf16[128,512]{1,0:T(8,128)(2,1)S(1)}, u32[]{:S(2)}, u32[]{:S(2)}) collective-permute-start(bf16[128,512]{1,0:T(8,128)(2,1)S(1)} %get-tuple-element.173), channel_id=1, source_target_pairs={{0,4},{1,5},{2,6},{3,7},{4,8},{5,9},{6,10},{7,11},{8,12},{9,13},{1... | collective-permute-start | bytes 393224 | tf_op jit(solution)/shard_map/ppermute | solution.py:244
  240.1 3.1 %collective-permute-done.33.refs_2_ = bf16[128,768]{1,0:T(8,128)(2,1)S(1)} collective-permute-done((bf16[128,768]{1,0:T(8,128)(2,1)S(1)}, bf16[128,768]{1,0:T(8,128)(2,1)S(1)}, u32[]{:S(2)}, u32[]{:S(2)}) %collective-permute-start.33) | collective-permute-done | bytes 196640 | tf_op jit(solution)/shard_map/ppermute | solution.py:244
  243.3 1.3 collective-permute-done.34.refs_3_
  244.6 6.9 %collective-permute-start.36 = (bf16[128,768]{1,0:T(8,128)(2,1)S(1)}, bf16[128,768]{1,0:T(8,128)(2,1)S(1)}, u32[]{:S(2)}, u32[]{:S(2)}) collective-permute-start(bf16[128,768]{1,0:T(8,128)(2,1)S(1)} %get-tuple-element.163), channel_id=1, source_target_pairs={{0,4},{1,5},{2,6},{3,7},{4,8},{5,9},{6,10},{7,11},{8,12},{9,13},{1... | collective-permute-start | bytes 589832 | tf_op jit(solution)/shard_map/ppermute | solution.py:244
  251.5 3.4 %collective-permute-start.37 = (bf16[128,768]{1,0:T(8,128)(2,1)S(1)}, bf16[128,768]{1,0:T(8,128)(2,1)S(1)}, u32[]{:S(2)}, u32[]{:S(2)}) collective-permute-start(bf16[128,768]{1,0:T(8,128)(2,1)S(1)} %get-tuple-element.164), channel_id=1, source_target_pairs={{0,8},{1,9},{2,10},{3,11},{4,12},{5,13},{6,14},{7,15},{8,0},{9,1},... | collective-permute-start | bytes 589832 | tf_op jit(solution)/shard_map/ppermute | solution.py:244
  254.9 1.5 collective-permute-start.41
  256.4 2.9 %collective-permute-start.42 = (bf16[128,512]{1,0:T(8,128)(2,1)S(1)}, bf16[128,512]{1,0:T(8,128)(2,1)S(1)}, u32[]{:S(2)}, u32[]{:S(2)}) collective-permute-start(bf16[128,512]{1,0:T(8,128)(2,1)S(1)} %get-tuple-element.175), channel_id=1, source_target_pairs={{0,12},{1,13},{2,14},{3,15},{4,0},{5,1},{6,2},{7,3},{8,4},{9,5},{1... | collective-permute-start | bytes 393224 | tf_op jit(solution)/shard_map/ppermute | solution.py:244
  259.3 1.2 finish.2
  260.5 6.7 %collective-permute-done.41.refs_10_ = bf16[128,512]{1,0:T(8,128)(2,1)S(1)} collective-permute-done((bf16[128,512]{1,0:T(8,128)(2,1)S(1)}, bf16[128,512]{1,0:T(8,128)(2,1)S(1)}, u32[]{:S(2)}, u32[]{:S(2)}) %collective-permute-start.41) | collective-permute-done | bytes 131104 | tf_op jit(solution)/shard_map/ppermute | solution.py:244
  267.2 1.2 finish.3
  (123 shorter events, 23.3 us)
Async XLA Ops:
  2.8 88.8 %copy-start.8 = (bf16[128,2176]{1,0:T(8,128)(2,1)}, bf16[128,2176]{1,0:T(8,128)(2,1)S(1)}, u32[]{:S(2)}) copy-start(bf16[128,2176]{1,0:T(8,128)(2,1)S(1)} %concatenate.3.refs_0_) | copy-start | bytes 1671172
  2.8 64.8 %collective-permute-start.8 = (bf16[2,2048,256]{2,1,0:T(8,128)(2,1)}, bf16[2,2048,256]{2,1,0:T(8,128)(2,1)S(1)}, u32[]{:S(2)}, u32[]{:S(2)}) collective-permute-start(bf16[2,2048,256]{2,1,0:T(8,128)(2,1)} %refs_0_.5), channel_id=1, source_target_pairs={{0,1},{1,0},{2,3},{3,2},{4,5},{5,4},{6,7},{7,6},{8,9},{9,8},{10,11... | collective-permute-start | bytes 6291464 | tf_op jit(solution)/shard_map/ppermute | solution.py:244
  5.8 17.5 %collective-permute-start.3 = (bf16[128,2176]{1,0:T(8,128)(2,1)S(1)}, bf16[128,2176]{1,0:T(8,128)(2,1)S(1)}, u32[]{:S(2)}, u32[]{:S(2)}) collective-permute-start(bf16[128,2176]{1,0:T(8,128)(2,1)S(1)} %concatenate.3.refs_0_), channel_id=1, source_target_pairs={{0,4},{1,5},{2,6},{3,7},{4,8},{5,9},{6,10},{7,11},{8,12},{9,13},{1... | collective-permute-start | bytes 1671176 | tf_op jit(solution)/shard_map/ppermute | solution.py:244
  7.4 15.1 %collective-permute-start.6 = (bf16[128,2048]{1,0:T(8,128)(2,1)}, bf16[128,2048]{1,0:T(8,128)(2,1)S(1)}, u32[]{:S(2)}, u32[]{:S(2)}) collective-permute-start(bf16[128,2048]{1,0:T(8,128)(2,1)} %refs_3_.1), channel_id=1, source_target_pairs={{0,2},{1,3},{2,0},{3,1},{4,6},{5,7},{6,4},{7,5},{8,10},{9,11},{10,... | collective-permute-start | bytes 1572872 | tf_op jit(solution)/shard_map/ppermute | solution.py:244
  8.9 23.7 %collective-permute-start.1 = (bf16[128,2176]{1,0:T(8,128)(2,1)S(1)}, bf16[128,2176]{1,0:T(8,128)(2,1)S(1)}, u32[]{:S(2)}, u32[]{:S(2)}) collective-permute-start(bf16[128,2176]{1,0:T(8,128)(2,1)S(1)} %concatenate.3.refs_0_), channel_id=1, source_target_pairs={{0,2},{1,3},{2,0},{3,1},{4,6},{5,7},{6,4},{7,5},{8,10},{9,11},{10,... | collective-permute-start | bytes 1671176 | tf_op jit(solution)/shard_map/ppermute | solution.py:244
  9.4 24.3 %collective-permute-start = (bf16[128,2176]{1,0:T(8,128)(2,1)S(1)}, bf16[128,2176]{1,0:T(8,128)(2,1)S(1)}, u32[]{:S(2)}, u32[]{:S(2)}) collective-permute-start(bf16[128,2176]{1,0:T(8,128)(2,1)S(1)} %concatenate.3.refs_0_), channel_id=1, source_target_pairs={{0,12},{1,13},{2,14},{3,15},{4,0},{5,1},{6,2},{7,3},{8,4},{9,5},{1... | collective-permute-start | bytes 1671176 | tf_op jit(solution)/shard_map/ppermute | solution.py:244
  23.3 90.3 %collective-permute-start.9 = (bf16[2,2048,256]{2,1,0:T(8,128)(2,1)}, bf16[2,2048,256]{2,1,0:T(8,128)(2,1)}, u32[]{:S(2)}, u32[]{:S(2)}) collective-permute-start(bf16[2,2048,256]{2,1,0:T(8,128)(2,1)} %refs_1_.7), channel_id=1, source_target_pairs={{0,1},{1,0},{2,3},{3,2},{4,5},{5,4},{6,7},{7,6},{8,9},{9,8},{10,11... | collective-permute-start | bytes 6291464 | tf_op jit(solution)/shard_map/ppermute | solution.py:244
  33.7 15.5 %collective-permute-start.4 = (bf16[128,2176]{1,0:T(8,128)(2,1)S(1)}, bf16[128,2176]{1,0:T(8,128)(2,1)S(1)}, u32[]{:S(2)}, u32[]{:S(2)}) collective-permute-start(bf16[128,2176]{1,0:T(8,128)(2,1)S(1)} %collective-permute-done.refs_1_), channel_id=1, source_target_pairs={{0,2},{1,3},{2,0},{3,1},{4,6},{5,7},{6,4},{7,5},{8,10},{9,11},{10,... | collective-permute-start | bytes 1671176 | tf_op jit(solution)/shard_map/ppermute | solution.py:244
  36.0 27.0 %collective-permute-start.2 = (bf16[128,2176]{1,0:T(8,128)(2,1)S(1)}, bf16[128,2176]{1,0:T(8,128)(2,1)S(1)}, u32[]{:S(2)}, u32[]{:S(2)}) collective-permute-start(bf16[128,2176]{1,0:T(8,128)(2,1)S(1)} %concatenate.3.refs_0_), channel_id=1, source_target_pairs={{0,8},{1,9},{2,10},{3,11},{4,12},{5,13},{6,14},{7,15},{8,0},{9,1},... | collective-permute-start | bytes 1671176 | tf_op jit(solution)/shard_map/ppermute | solution.py:244
  38.4 28.4 %collective-permute-start.7 = (bf16[128,2176]{1,0:T(8,128)(2,1)S(1)}, bf16[128,2176]{1,0:T(8,128)(2,1)S(1)}, u32[]{:S(2)}, u32[]{:S(2)}) collective-permute-start(bf16[128,2176]{1,0:T(8,128)(2,1)S(1)} %collective-permute-done.3.refs_3_), channel_id=1, source_target_pairs={{0,2},{1,3},{2,0},{3,1},{4,6},{5,7},{6,4},{7,5},{8,10},{9,11},{10,... | collective-permute-start | bytes 1671176 | tf_op jit(solution)/shard_map/ppermute | solution.py:244
  63.1 26.1 %collective-permute-start.5 = (bf16[128,2176]{1,0:T(8,128)(2,1)S(1)}, bf16[128,2176]{1,0:T(8,128)(2,1)S(1)}, u32[]{:S(2)}, u32[]{:S(2)}) collective-permute-start(bf16[128,2176]{1,0:T(8,128)(2,1)S(1)} %collective-permute-done.2.refs_2_), channel_id=1, source_target_pairs={{0,2},{1,3},{2,0},{3,1},{4,6},{5,7},{6,4},{7,5},{8,10},{9,11},{10,... | collective-permute-start | bytes 1671176 | tf_op jit(solution)/shard_map/ppermute | solution.py:244
  64.4 24.8 %collective-permute-start.10 = (bf16[128,2048]{1,0:T(8,128)(2,1)}, bf16[128,2048]{1,0:T(8,128)(2,1)}, u32[]{:S(2)}, u32[]{:S(2)}) collective-permute-start(bf16[128,2048]{1,0:T(8,128)(2,1)} %refs_3_.1), channel_id=1, source_target_pairs={{0,12},{1,13},{2,14},{3,15},{4,0},{5,1},{6,2},{7,3},{8,4},{9,5},{1... | collective-permute-start | bytes 1572872 | tf_op jit(solution)/shard_map/ppermute | solution.py:244
  67.6 1.4 copy-start.5
  69.0 42.7 %collective-permute-start.13 = (bf16[128,2048]{1,0:T(8,128)(2,1)}, bf16[128,2048]{1,0:T(8,128)(2,1)}, u32[]{:S(2)}, u32[]{:S(2)}) collective-permute-start(bf16[128,2048]{1,0:T(8,128)(2,1)} %refs_3_.1), channel_id=1, source_target_pairs={{0,4},{1,5},{2,6},{3,7},{4,8},{5,9},{6,10},{7,11},{8,12},{9,13},{1... | collective-permute-start | bytes 1572872 | tf_op jit(solution)/shard_map/ppermute | solution.py:244
  90.1 23.5 %collective-permute-start.11 = (bf16[128,2048]{1,0:T(8,128)(2,1)}, bf16[128,2048]{1,0:T(8,128)(2,1)}, u32[]{:S(2)}, u32[]{:S(2)}) collective-permute-start(bf16[128,2048]{1,0:T(8,128)(2,1)} %collective-permute-done.10.refs_2_.refs_4_), channel_id=1, source_target_pairs={{0,2},{1,3},{2,0},{3,1},{4,6},{5,7},{6,4},{7,5},{8,10},{9,11},{10,... | collective-permute-start | bytes 1572872 | tf_op jit(solution)/shard_map/ppermute | solution.py:244
  91.6 22.0 %collective-permute-start.16 = (bf16[128,2048]{1,0:T(8,128)(2,1)}, bf16[128,2048]{1,0:T(8,128)(2,1)}, u32[]{:S(2)}, u32[]{:S(2)}) collective-permute-start(bf16[128,2048]{1,0:T(8,128)(2,1)} %refs_3_.1), channel_id=1, source_target_pairs={{0,8},{1,9},{2,10},{3,11},{4,12},{5,13},{6,14},{7,15},{8,0},{9,1},... | collective-permute-start | bytes 1572872 | tf_op jit(solution)/shard_map/ppermute | solution.py:244
  91.6 1.6 copy-start.1
  93.2 1.6 copy-start.3
  94.8 1.1 copy-start.9
  96.9 1.1 copy-start.17
  97.9 1.1 copy-start.20
  99.0 1.1 copy-start.23
  100.0 1.1 copy-start.26
  101.1 1.1 copy-start.29
  102.1 1.1 copy-start.32
  103.2 9.1 %copy-start = (bf16[2,256,2048]{2,1,0:T(8,128)(2,1)S(1)}, bf16[2,256,2048]{2,1,0:T(8,128)(2,1)}, u32[]{:S(2)}) copy-start(bf16[2,256,2048]{2,1,0:T(8,128)(2,1)} %param.13) | copy-start | bytes 6291460
  109.2 2.0 copy-start.11
  111.2 23.1 %collective-permute-start.12 = (bf16[512,512]{1,0:T(8,128)(2,1)}, bf16[512,512]{1,0:T(8,128)(2,1)}, u32[]{:S(2)}, u32[]{:S(2)}) collective-permute-start(bf16[512,512]{1,0:T(8,128)(2,1)} %slice.12), channel_id=1, source_target_pairs={{0,1},{1,0},{2,3},{3,2},{4,5},{5,4},{6,7},{7,6},{8,9},{9,8},{10,11... | collective-permute-start | bytes 1572872 | tf_op jit(solution)/shard_map/ppermute | solution.py:244
  111.8 25.4 %collective-permute-start.14 = (bf16[128,2048]{1,0:T(8,128)(2,1)}, bf16[128,2048]{1,0:T(8,128)(2,1)}, u32[]{:S(2)}, u32[]{:S(2)}) collective-permute-start(bf16[128,2048]{1,0:T(8,128)(2,1)} %collective-permute-done.13.refs_4_.refs_6_), channel_id=1, source_target_pairs={{0,2},{1,3},{2,0},{3,1},{4,6},{5,7},{6,4},{7,5},{8,10},{9,11},{10,... | collective-permute-start | bytes 1572872 | tf_op jit(solution)/shard_map/ppermute | solution.py:244
  113.5 29.1 %collective-permute-start.17 = (bf16[512,768]{1,0:T(8,128)(2,1)}, bf16[512,768]{1,0:T(8,128)(2,1)}, u32[]{:S(2)}, u32[]{:S(2)}) collective-permute-start(bf16[512,768]{1,0:T(8,128)(2,1)} %get-tuple-element.113), channel_id=1, source_target_pairs={{0,1},{1,0},{2,3},{3,2},{4,5},{5,4},{6,7},{7,6},{8,9},{9,8},{10,11... | collective-permute-start | bytes 2359304 | tf_op jit(solution)/shard_map/ppermute | solution.py:244
  115.1 23.2 %collective-permute-start.18 = (bf16[128,2048]{1,0:T(8,128)(2,1)}, bf16[128,2048]{1,0:T(8,128)(2,1)S(1)}, u32[]{:S(2)}, u32[]{:S(2)}) collective-permute-start(bf16[128,2048]{1,0:T(8,128)(2,1)} %collective-permute-done.16.refs_3_.refs_5_), channel_id=1, source_target_pairs={{0,2},{1,3},{2,0},{3,1},{4,6},{5,7},{6,4},{7,5},{8,10},{9,11},{10,... | collective-permute-start | bytes 1572872 | tf_op jit(solution)/shard_map/ppermute | solution.py:244
  116.6 1.6 copy-start.6
  118.2 1.1 copy-start.10
  126.6 11.1 %copy-start.36 = (bf16[512,768]{1,0:T(8,128)(2,1)S(1)}, bf16[512,768]{1,0:T(8,128)(2,1)}, u32[]{:S(2)}) copy-start(bf16[512,768]{1,0:T(8,128)(2,1)} %get-tuple-element.127) | copy-start | bytes 2359300
  134.4 4.0 %copy-start.12 = (f32[1024,1024]{1,0:T(8,128)S(1)}, f32[1024,1024]{1,0:T(8,128)}, u32[]{:S(2)}) copy-start(f32[1024,1024]{1,0:T(8,128)} %copy-done.11) | copy-start | bytes 12582916
  134.4 4.0 %copy-start.35 = (bf16[128,2048]{1,0:T(8,128)(2,1)S(1)}, bf16[128,2048]{1,0:T(8,128)(2,1)}, u32[]{:S(2)}) copy-start(bf16[128,2048]{1,0:T(8,128)(2,1)} %copy-done.34) | copy-start | bytes 1572868
  137.2 11.7 %collective-permute-start.15 = (bf16[512,512]{1,0:T(8,128)(2,1)S(1)}, bf16[512,512]{1,0:T(8,128)(2,1)S(1)}, u32[]{:S(2)}, u32[]{:S(2)}) collective-permute-start(bf16[512,512]{1,0:T(8,128)(2,1)S(1)} %get-tuple-element.110), channel_id=1, source_target_pairs={{0,2},{1,3},{2,0},{3,1},{4,6},{5,7},{6,4},{7,5},{8,10},{9,11},{10,... | collective-permute-start | bytes 1572872 | tf_op jit(solution)/shard_map/ppermute | solution.py:244
  137.8 19.6 %collective-permute-start.23 = (bf16[512,768]{1,0:T(8,128)(2,1)S(1)}, bf16[512,768]{1,0:T(8,128)(2,1)S(1)}, u32[]{:S(2)}, u32[]{:S(2)}) collective-permute-start(bf16[512,768]{1,0:T(8,128)(2,1)S(1)} %copy-done.36), channel_id=1, source_target_pairs={{0,1},{1,0},{2,3},{3,2},{4,5},{5,4},{6,7},{7,6},{8,9},{9,8},{10,11... | collective-permute-start | bytes 2359304 | tf_op jit(solution)/shard_map/ppermute | solution.py:244
  149.0 17.3 %collective-permute-start.22 = (bf16[512,768]{1,0:T(8,128)(2,1)S(1)}, bf16[512,768]{1,0:T(8,128)(2,1)S(1)}, u32[]{:S(2)}, u32[]{:S(2)}) collective-permute-start(bf16[512,768]{1,0:T(8,128)(2,1)S(1)} %get-tuple-element.125), channel_id=1, source_target_pairs={{0,2},{1,3},{2,0},{3,1},{4,6},{5,7},{6,4},{7,5},{8,10},{9,11},{10,... | collective-permute-start | bytes 2359304 | tf_op jit(solution)/shard_map/ppermute | solution.py:244
  149.1 17.4 %collective-permute-start.19 = (bf16[128,512]{1,0:T(8,128)(2,1)S(1)}, bf16[128,512]{1,0:T(8,128)(2,1)S(1)}, u32[]{:S(2)}, u32[]{:S(2)}) collective-permute-start(bf16[128,512]{1,0:T(8,128)(2,1)S(1)} %get-tuple-element.121), channel_id=1, source_target_pairs={{0,4},{1,5},{2,6},{3,7},{4,8},{5,9},{6,10},{7,11},{8,12},{9,13},{1... | collective-permute-start | bytes 393224 | tf_op jit(solution)/shard_map/ppermute | solution.py:244
  149.2 17.3 %collective-permute-start.20 = (bf16[128,512]{1,0:T(8,128)(2,1)S(1)}, bf16[128,512]{1,0:T(8,128)(2,1)S(1)}, u32[]{:S(2)}, u32[]{:S(2)}) collective-permute-start(bf16[128,512]{1,0:T(8,128)(2,1)S(1)} %get-tuple-element.122), channel_id=1, source_target_pairs={{0,8},{1,9},{2,10},{3,11},{4,12},{5,13},{6,14},{7,15},{8,0},{9,1},... | collective-permute-start | bytes 393224 | tf_op jit(solution)/shard_map/ppermute | solution.py:244
  154.6 12.0 %collective-permute-start.21 = (bf16[128,512]{1,0:T(8,128)(2,1)S(1)}, bf16[128,512]{1,0:T(8,128)(2,1)S(1)}, u32[]{:S(2)}, u32[]{:S(2)}) collective-permute-start(bf16[128,512]{1,0:T(8,128)(2,1)S(1)} %get-tuple-element.123), channel_id=1, source_target_pairs={{0,12},{1,13},{2,14},{3,15},{4,0},{5,1},{6,2},{7,3},{8,4},{9,5},{1... | collective-permute-start | bytes 393224 | tf_op jit(solution)/shard_map/ppermute | solution.py:244
  166.5 27.7 %collective-permute-start.27 = (bf16[512,768]{1,0:T(8,128)(2,1)}, bf16[512,768]{1,0:T(8,128)(2,1)S(1)}, u32[]{:S(2)}, u32[]{:S(2)}) collective-permute-start(bf16[512,768]{1,0:T(8,128)(2,1)} %get-tuple-element.137), channel_id=1, source_target_pairs={{0,2},{1,3},{2,0},{3,1},{4,6},{5,7},{6,4},{7,5},{8,10},{9,11},{10,... | collective-permute-start | bytes 2359304 | tf_op jit(solution)/shard_map/ppermute | solution.py:244
  166.6 6.5 %copy-start.2 = (bf16[2,2048,256]{2,1,0:T(8,128)(2,1)S(1)}, bf16[2,2048,256]{2,1,0:T(8,128)(2,1)}, u32[]{:S(2)}) copy-start(bf16[2,2048,256]{2,1,0:T(8,128)(2,1)} %refs_0_.5) | copy-start | bytes 6291460
  166.6 6.5 %copy-start.4 = (bf16[2,2048,256]{2,1,0:T(8,128)(2,1)S(1)}, bf16[2,2048,256]{2,1,0:T(8,128)(2,1)}, u32[]{:S(2)}) copy-start(bf16[2,2048,256]{2,1,0:T(8,128)(2,1)} %refs_1_.7) | copy-start | bytes 6291460
  166.6 6.5 %copy-start.7 = (bf16[2,2048,256]{2,1,0:T(8,128)(2,1)S(1)}, bf16[2,2048,256]{2,1,0:T(8,128)(2,1)}, u32[]{:S(2)}) copy-start(bf16[2,2048,256]{2,1,0:T(8,128)(2,1)} %copy-done.5) | copy-start | bytes 6291460
  178.4 33.4 %collective-permute-start.31 = (bf16[512,768]{1,0:T(8,128)(2,1)S(1)}, bf16[512,768]{1,0:T(8,128)(2,1)S(1)}, u32[]{:S(2)}, u32[]{:S(2)}) collective-permute-start(bf16[512,768]{1,0:T(8,128)(2,1)S(1)} %get-tuple-element.148), channel_id=1, source_target_pairs={{0,2},{1,3},{2,0},{3,1},{4,6},{5,7},{6,4},{7,5},{8,10},{9,11},{10,... | collective-permute-start | bytes 2359304 | tf_op jit(solution)/shard_map/ppermute | solution.py:244
  180.4 14.0 %collective-permute-start.24 = (bf16[128,768]{1,0:T(8,128)(2,1)S(1)}, bf16[128,768]{1,0:T(8,128)(2,1)S(1)}, u32[]{:S(2)}, u32[]{:S(2)}) collective-permute-start(bf16[128,768]{1,0:T(8,128)(2,1)S(1)} %get-tuple-element.133), channel_id=1, source_target_pairs={{0,4},{1,5},{2,6},{3,7},{4,8},{5,9},{6,10},{7,11},{8,12},{9,13},{1... | collective-permute-start | bytes 589832 | tf_op jit(solution)/shard_map/ppermute | solution.py:244
  180.4 17.9 %collective-permute-start.25 = (bf16[128,768]{1,0:T(8,128)(2,1)S(1)}, bf16[128,768]{1,0:T(8,128)(2,1)S(1)}, u32[]{:S(2)}, u32[]{:S(2)}) collective-permute-start(bf16[128,768]{1,0:T(8,128)(2,1)S(1)} %get-tuple-element.134), channel_id=1, source_target_pairs={{0,8},{1,9},{2,10},{3,11},{4,12},{5,13},{6,14},{7,15},{8,0},{9,1},... | collective-permute-start | bytes 589832 | tf_op jit(solution)/shard_map/ppermute | solution.py:244
  186.1 12.2 %collective-permute-start.26 = (bf16[128,768]{1,0:T(8,128)(2,1)S(1)}, bf16[128,768]{1,0:T(8,128)(2,1)S(1)}, u32[]{:S(2)}, u32[]{:S(2)}) collective-permute-start(bf16[128,768]{1,0:T(8,128)(2,1)S(1)} %get-tuple-element.135), channel_id=1, source_target_pairs={{0,12},{1,13},{2,14},{3,15},{4,0},{5,1},{6,2},{7,3},{8,4},{9,5},{1... | collective-permute-start | bytes 589832 | tf_op jit(solution)/shard_map/ppermute | solution.py:244
  198.3 34.9 %collective-permute-start.35 = (bf16[512,768]{1,0:T(8,128)(2,1)S(1)}, bf16[512,768]{1,0:T(8,128)(2,1)S(1)}, u32[]{:S(2)}, u32[]{:S(2)}) collective-permute-start(bf16[512,768]{1,0:T(8,128)(2,1)S(1)} %get-tuple-element.158), channel_id=1, source_target_pairs={{0,2},{1,3},{2,0},{3,1},{4,6},{5,7},{6,4},{7,5},{8,10},{9,11},{10,... | collective-permute-start | bytes 2359304 | tf_op jit(solution)/shard_map/ppermute | solution.py:244
  198.3 14.9 %collective-permute-start.28 = (bf16[128,768]{1,0:T(8,128)(2,1)S(1)}, bf16[128,768]{1,0:T(8,128)(2,1)S(1)}, u32[]{:S(2)}, u32[]{:S(2)}) collective-permute-start(bf16[128,768]{1,0:T(8,128)(2,1)S(1)} %get-tuple-element.144), channel_id=1, source_target_pairs={{0,4},{1,5},{2,6},{3,7},{4,8},{5,9},{6,10},{7,11},{8,12},{9,13},{1... | collective-permute-start | bytes 589832 | tf_op jit(solution)/shard_map/ppermute | solution.py:244
  204.5 16.0 %collective-permute-start.29 = (bf16[128,768]{1,0:T(8,128)(2,1)S(1)}, bf16[128,768]{1,0:T(8,128)(2,1)S(1)}, u32[]{:S(2)}, u32[]{:S(2)}) collective-permute-start(bf16[128,768]{1,0:T(8,128)(2,1)S(1)} %get-tuple-element.145), channel_id=1, source_target_pairs={{0,8},{1,9},{2,10},{3,11},{4,12},{5,13},{6,14},{7,15},{8,0},{9,1},... | collective-permute-start | bytes 589832 | tf_op jit(solution)/shard_map/ppermute | solution.py:244
  207.9 12.6 %collective-permute-start.30 = (bf16[128,768]{1,0:T(8,128)(2,1)S(1)}, bf16[128,768]{1,0:T(8,128)(2,1)S(1)}, u32[]{:S(2)}, u32[]{:S(2)}) collective-permute-start(bf16[128,768]{1,0:T(8,128)(2,1)S(1)} %get-tuple-element.146), channel_id=1, source_target_pairs={{0,12},{1,13},{2,14},{3,15},{4,0},{5,1},{6,2},{7,3},{8,4},{9,5},{1... | collective-permute-start | bytes 589832 | tf_op jit(solution)/shard_map/ppermute | solution.py:244
  220.5 12.8 %collective-permute-start.39 = (bf16[512,512]{1,0:T(8,128)(2,1)S(1)}, bf16[512,512]{1,0:T(8,128)(2,1)S(1)}, u32[]{:S(2)}, u32[]{:S(2)}) collective-permute-start(bf16[512,512]{1,0:T(8,128)(2,1)S(1)} %get-tuple-element.167), channel_id=1, source_target_pairs={{0,2},{1,3},{2,0},{3,1},{4,6},{5,7},{6,4},{7,5},{8,10},{9,11},{10,... | collective-permute-start | bytes 1572872 | tf_op jit(solution)/shard_map/ppermute | solution.py:244
  220.8 19.3 %collective-permute-start.32 = (bf16[128,768]{1,0:T(8,128)(2,1)S(1)}, bf16[128,768]{1,0:T(8,128)(2,1)S(1)}, u32[]{:S(2)}, u32[]{:S(2)}) collective-permute-start(bf16[128,768]{1,0:T(8,128)(2,1)S(1)} %get-tuple-element.154), channel_id=1, source_target_pairs={{0,4},{1,5},{2,6},{3,7},{4,8},{5,9},{6,10},{7,11},{8,12},{9,13},{1... | collective-permute-start | bytes 589832 | tf_op jit(solution)/shard_map/ppermute | solution.py:244
  230.8 12.5 %collective-permute-start.33 = (bf16[128,768]{1,0:T(8,128)(2,1)S(1)}, bf16[128,768]{1,0:T(8,128)(2,1)S(1)}, u32[]{:S(2)}, u32[]{:S(2)}) collective-permute-start(bf16[128,768]{1,0:T(8,128)(2,1)S(1)} %get-tuple-element.155), channel_id=1, source_target_pairs={{0,8},{1,9},{2,10},{3,11},{4,12},{5,13},{6,14},{7,15},{8,0},{9,1},... | collective-permute-start | bytes 589832 | tf_op jit(solution)/shard_map/ppermute | solution.py:244
  230.8 13.7 %collective-permute-start.34 = (bf16[128,768]{1,0:T(8,128)(2,1)S(1)}, bf16[128,768]{1,0:T(8,128)(2,1)S(1)}, u32[]{:S(2)}, u32[]{:S(2)}) collective-permute-start(bf16[128,768]{1,0:T(8,128)(2,1)S(1)} %get-tuple-element.156), channel_id=1, source_target_pairs={{0,12},{1,13},{2,14},{3,15},{4,0},{5,1},{6,2},{7,3},{8,4},{9,5},{1... | collective-permute-start | bytes 589832 | tf_op jit(solution)/shard_map/ppermute | solution.py:244
  233.4 22.9 %collective-permute-start.40 = (bf16[128,512]{1,0:T(8,128)(2,1)S(1)}, bf16[128,512]{1,0:T(8,128)(2,1)S(1)}, u32[]{:S(2)}, u32[]{:S(2)}) collective-permute-start(bf16[128,512]{1,0:T(8,128)(2,1)S(1)} %get-tuple-element.173), channel_id=1, source_target_pairs={{0,4},{1,5},{2,6},{3,7},{4,8},{5,9},{6,10},{7,11},{8,12},{9,13},{1... | collective-permute-start | bytes 393224 | tf_op jit(solution)/shard_map/ppermute | solution.py:244
  244.6 22.6 %collective-permute-start.36 = (bf16[128,768]{1,0:T(8,128)(2,1)S(1)}, bf16[128,768]{1,0:T(8,128)(2,1)S(1)}, u32[]{:S(2)}, u32[]{:S(2)}) collective-permute-start(bf16[128,768]{1,0:T(8,128)(2,1)S(1)} %get-tuple-element.163), channel_id=1, source_target_pairs={{0,4},{1,5},{2,6},{3,7},{4,8},{5,9},{6,10},{7,11},{8,12},{9,13},{1... | collective-permute-start | bytes 589832 | tf_op jit(solution)/shard_map/ppermute | solution.py:244
  251.5 15.6 %collective-permute-start.37 = (bf16[128,768]{1,0:T(8,128)(2,1)S(1)}, bf16[128,768]{1,0:T(8,128)(2,1)S(1)}, u32[]{:S(2)}, u32[]{:S(2)}) collective-permute-start(bf16[128,768]{1,0:T(8,128)(2,1)S(1)} %get-tuple-element.164), channel_id=1, source_target_pairs={{0,8},{1,9},{2,10},{3,11},{4,12},{5,13},{6,14},{7,15},{8,0},{9,1},... | collective-permute-start | bytes 589832 | tf_op jit(solution)/shard_map/ppermute | solution.py:244
  254.9 12.3 %collective-permute-start.38 = (bf16[128,768]{1,0:T(8,128)(2,1)S(1)}, bf16[128,768]{1,0:T(8,128)(2,1)S(1)}, u32[]{:S(2)}, u32[]{:S(2)}) collective-permute-start(bf16[128,768]{1,0:T(8,128)(2,1)S(1)} %get-tuple-element.165), channel_id=1, source_target_pairs={{0,12},{1,13},{2,14},{3,15},{4,0},{5,1},{6,2},{7,3},{8,4},{9,5},{1... | collective-permute-start | bytes 589832 | tf_op jit(solution)/shard_map/ppermute | solution.py:244
  254.9 12.3 %collective-permute-start.41 = (bf16[128,512]{1,0:T(8,128)(2,1)S(1)}, bf16[128,512]{1,0:T(8,128)(2,1)S(1)}, u32[]{:S(2)}, u32[]{:S(2)}) collective-permute-start(bf16[128,512]{1,0:T(8,128)(2,1)S(1)} %get-tuple-element.174), channel_id=1, source_target_pairs={{0,8},{1,9},{2,10},{3,11},{4,12},{5,13},{6,14},{7,15},{8,0},{9,1},... | collective-permute-start | bytes 393224 | tf_op jit(solution)/shard_map/ppermute | solution.py:244
  256.4 10.8 %collective-permute-start.42 = (bf16[128,512]{1,0:T(8,128)(2,1)S(1)}, bf16[128,512]{1,0:T(8,128)(2,1)S(1)}, u32[]{:S(2)}, u32[]{:S(2)}) collective-permute-start(bf16[128,512]{1,0:T(8,128)(2,1)S(1)} %get-tuple-element.175), channel_id=1, source_target_pairs={{0,12},{1,13},{2,14},{3,15},{4,0},{5,1},{6,2},{7,3},{8,4},{9,5},{1... | collective-permute-start | bytes 393224 | tf_op jit(solution)/shard_map/ppermute | solution.py:244
  (16 other events, 15.0 us)

commit v6 on v5

--- a/solution.py
+++ b/solution.py
@@ -7,8 +7,12 @@
 from jax.experimental.pallas import tpu as pltpu
 from jax.sharding import PartitionSpec as P
 
-VMEM_BYTES = 32 * 2**20
+VMEM_BYTES = 18 * 2**20
 AT_ONCE = pl.CostEstimate(flops=1, bytes_accessed=1, transcendentals=0)
+
+
+def resident(shape, index):
+    return pl.BlockSpec(shape, index, pipeline_mode=pl.Buffered(1))
 
 
 def compiler_params():
@@ -62,7 +66,7 @@
     block, row_width = row_blocks[0].shape
     experts, width, hidden = gate_weight.shape
     count, columns, tile = blocks * block, experts * hidden, 2 * block
-    weights = pl.BlockSpec((experts, width, hidden), lambda i: (0, 0, 0))
+    weights = resident((experts, width, hidden), lambda i: (0, 0, 0))
     return pl.pallas_call(
         functools.partial(hidden_kernel, blocks, all_experts),
         grid=(blocks // 2,),
@@ -89,32 +93,44 @@
 NT = (((1,), (1,)), ((), ()))
 
 
-def grads_kernel(blocks, chunks, by_ref, *refs):
-    down_refs, block_refs = refs[: len(chunks)], refs[len(chunks) : len(chunks) + blocks]
-    out_ref, buffer, sems = refs[len(chunks) + blocks :]
+def grads_kernel(blocks, cuts, has_by, has_before, *refs):
+    refs = list(refs)
+    by_ref = refs.pop(0) if has_by else None
+    before_ref = refs.pop(0) if has_before else None
+    down_refs, block_refs = refs[: len(cuts)], refs[len(cuts) : len(cuts) + blocks]
+    out_ref, buffer, sems = refs[len(cuts) + blocks :]
     rows = fetch_rows(block_refs, buffer, sems)
-    total = None
-    for (lo, hi), down_ref in zip(chunks, down_refs):
+    total = before_ref[...] if has_before else None
+    for (lo, hi), down_ref in zip(cuts, down_refs):
         term = lax.dot_general(rows[:, lo:hi], down_ref[...], NT, preferred_element_type=jnp.float32)
         total = term if total is None else total + term
-    columns = total.shape[1]
-    out_ref[:, :columns] = (total * by_ref[:, :columns]).astype(jnp.bfloat16)
-    out_ref[:, columns:] = (total * by_ref[:, columns:]).astype(jnp.bfloat16)
-
-
-def hidden_grads(grad_blocks, by, downs, chunks):
+    if has_by:
+        columns = total.shape[1]
+        out_ref[:, :columns] = (total * by_ref[:, :columns]).astype(jnp.bfloat16)
+        out_ref[:, columns:] = (total * by_ref[:, columns:]).astype(jnp.bfloat16)
+    else:
+        out_ref[...] = total
+
+
+def hidden_grads(grad_blocks, downs, cuts, by=None, before=None):
     blocks = len(grad_blocks)
     block, width = grad_blocks[0].shape
+    columns = downs[0].shape[0]
     tile = 2 * block
-    rows = pl.BlockSpec((tile, by.shape[1]), lambda i: (i, 0))
-    return pl.pallas_call(
-        functools.partial(grads_kernel, blocks, tuple(chunks)),
+
+    def rows(count):
+        return pl.BlockSpec((tile, count), lambda i: (i, 0))
+
+    given = [x for x in (by, before) if x is not None]
+    out_columns, out_type = (columns, jnp.float32) if by is None else (2 * columns, jnp.bfloat16)
+    return pl.pallas_call(
+        functools.partial(grads_kernel, blocks, tuple(cuts), by is not None, before is not None),
         grid=(blocks // 2,),
-        in_specs=[rows]
-        + [pl.BlockSpec(d.shape, lambda i: (0, 0)) for d in downs]
+        in_specs=[rows(x.shape[1]) for x in given]
+        + [resident(d.shape, lambda i: (0, 0)) for d in downs]
         + [pl.BlockSpec(memory_space=pl.ANY)] * blocks,
-        out_specs=rows,
-        out_shape=jax.ShapeDtypeStruct(by.shape, jnp.bfloat16),
+        out_specs=rows(out_columns),
+        out_shape=jax.ShapeDtypeStruct((blocks * block, out_columns), out_type),
         scratch_shapes=[
             pltpu.VMEM((blocks, block, width), jnp.bfloat16),
             pltpu.SemaphoreType.DMA((blocks,)),
@@ -122,7 +138,7 @@
         compiler_params=compiler_params(),
         cost_estimate=AT_ONCE,
         name="hidden_grads",
-    )(by, *downs, *grad_blocks)
+    )(*given, *downs, *grad_blocks)
 
 
 def store_half(total, keep_ref, send_ref):
@@ -177,37 +193,45 @@
 def mix_columns(own, other, own_down, other_down, at):
     depth, columns = other_down.shape
     specs = [
-        pl.BlockSpec((depth, columns), lambda i: (0, at)),
-        pl.BlockSpec((depth, columns), lambda i: (0, 0)),
+        resident((depth, columns), lambda i: (0, at)),
+        resident((depth, columns), lambda i: (0, 0)),
     ]
     return sum_columns(mix_kernel, "mix_columns", columns, own, other, [own_down, other_down], specs)
 
 
 def back_columns(own, other, weights, at, columns):
     experts, _, hidden = weights[0].shape
-    specs = [pl.BlockSpec((experts, columns, hidden), lambda i: (0, at, 0))] * len(weights)
+    specs = [resident((experts, columns, hidden), lambda i: (0, at, 0))] * len(weights)
     return sum_columns(back_kernel, "back_columns", columns, own, other, weights, specs)
 
 
-def add_kernel(keep_ref, come_ref, own_ref, *piece_refs):
-    block = own_ref.shape[0]
-    own_ref[...] = keep_ref[:block, :] + come_ref[:block, :].astype(jnp.float32)
-    for k, piece_ref in enumerate(piece_refs, 1):
+def add_kernel(keep_ref, come_ref, *out_refs):
+    block = out_refs[0].shape[0]
+    for k, out_ref in enumerate(out_refs):
         cut = slice(k * block, (k + 1) * block)
         total = keep_ref[cut, :] + come_ref[cut, :].astype(jnp.float32)
-        piece_ref[...] = total.astype(piece_ref.dtype)
-
-
-def add_sides(keep, come, layers):
-    block, columns = keep.shape[0] // layers, keep.shape[1]
-    pieces = [jax.ShapeDtypeStruct((block, columns), jnp.bfloat16)] * (layers - 1)
+        out_ref[...] = total.astype(out_ref.dtype)
+
+
+def add_sides(keep, come, types):
+    block, columns = keep.shape[0] // len(types), keep.shape[1]
     return pl.pallas_call(
         add_kernel,
-        out_shape=[jax.ShapeDtypeStruct((block, columns), jnp.float32)] + pieces,
+        out_shape=[jax.ShapeDtypeStruct((block, columns), t) for t in types],
         compiler_params=compiler_params(),
         cost_estimate=AT_ONCE,
         name="add_sides",
     )(keep, come)
+
+
+def add_piece(piece, come):
+    return pl.pallas_call(
+        add_kernel,
+        out_shape=jax.ShapeDtypeStruct(piece.shape, jnp.bfloat16),
+        compiler_params=compiler_params(),
+        cost_estimate=AT_ONCE,
+        name="add_piece",
+    )(piece, come)
 
 
 def finish_kernel(chunks, layers, *refs):
@@ -273,79 +297,97 @@
     rows, far_rows, grads, far_grads = {0: row}, {}, {0: grad}, {}
     other_gate, rows[one], far_rows[0] = send_all([(gate_weight, twin), (row, layer[-one]), (row, side)])
     rows[last], far_grads[0] = send_all([(row, layer[-last]), (grad, side)])
-    got = send_all([(rows[one], side)] + [(row, layer[-k]) for k in middle], far_rows[0])
-    far_rows[one] = got[0]
-    rows.update(zip(middle, got[1:]))
+    (far_rows[one],) = send_all([(rows[one], side)], far_rows[0])
+    for k in middle:
+        (rows[k],) = send_all([(rows[k - 1], layer[-one])], far_rows[0])
     other_up, far_rows[last] = send_all([(up_weight, twin), (rows[last], side)], far_grads[0])
-    got = send_all(
-        [(grad, layer[-one])] + [(rows[k], side) for k in middle], far_rows[one]
-    )
+    got = send_all([(grad, layer[-one])] + [(rows[k], side) for k in middle], far_rows[one])
     grads[one] = got[0]
     far_rows.update(zip(middle, got[1:]))
     down_0, grads[last] = send_all([(downs[0], twin), (grad, layer[-last])], far_rows[last], other_gate)
-    got = send_all(
-        [(grads[one], side)] + [(grad, layer[-k]) for k in middle], *far_rows.values()
-    )
-    far_grads[one] = got[0]
-    grads.update(zip(middle, got[1:]))
+    (far_grads[one],) = send_all([(grads[one], side)], *far_rows.values())
+    for k in middle:
+        (grads[k],) = send_all([(grads[k - 1], layer[-one])], *far_rows.values())
+    (far_grads[last],) = send_all([(grads[last], side)], *far_rows.values())
+    for k in middle:
+        (far_grads[k],) = send_all([(grads[k], side)], far_grads[one])
     row_blocks = [rows[k] for k in range(layers)] + [far_rows[k] for k in range(layers)]
-    activ, by = hidden_forward(row_blocks, me, gate_weight, up_weight, experts)
-    (far_grads[last],) = send_all([(grads[last], side)], activ)
-    waits = [other_up, far_grads[one]]
-    got = send_all([(downs[1], twin)] + [(grads[k], side) for k in middle], *waits)
-    down_1 = got[0]
-    far_grads.update(zip(middle, got[1:]))
-
-    other_up = after(other_up, *waits)
+    own = after(me, far_grads[one])
+    activ, by = hidden_forward(row_blocks, own, gate_weight, up_weight, experts)
+    other_up = after(other_up, activ)
     other_activ, other_by = hidden_forward(row_blocks, me ^ 1, other_gate, other_up, experts)
+
+    (down_1,) = send_all([(downs[1], twin)], down_0, activ, other_activ, *far_grads.values())
 
     def mix(c, other_down, *waits):
         lo, hi = chunks[c]
         return mix_columns(activ, other_activ, down, after(other_down, *waits), lo // (hi - lo))
 
-    def across(pieces):
-        return [(piece, layer[k]) for k, piece in enumerate(pieces, 1)]
+    types = [jnp.float32, jnp.float32] + [jnp.bfloat16] * (layers - 2)
+
+    def send_on(pieces, *waits):
+        (far,) = send_all([(pieces[-1], layer[last])], *waits)
+        come = None
+        for k in reversed(middle):
+            piece = pieces[k - 1] if come is None else add_piece(pieces[k - 1], come)
+            (come,) = send_all([(piece, layer[one])], *waits)
+        return far, come
+
+    def send_last(pieces, come, far):
+        piece = pieces[0].astype(jnp.bfloat16) if come is None else add_piece(pieces[0], come)
+        return send_all([(piece, layer[one])], far)[0]
 
     keep_0, send = mix(0, down_0, other_activ)
     come_0, down_2 = send_all([(send, side), (downs[2], twin)], far_grads[last])
     grad_blocks = [grads[k] for k in range(layers)] + [far_grads[k] for k in range(layers)]
-    own_grads = hidden_grads(grad_blocks, by, [down], [(0, width)])
+    own_grads = hidden_grads(grad_blocks, [down], [(0, width)], by=by)
 
     keep_1, send = mix(1, down_1, send)
-    own_0, *pieces = add_sides(keep_0, come_0, layers)
-    come_1, *parts_0 = send_all([(send, side)] + across(pieces), own_grads)
-
-    keep_2, send = mix(2, down_2, send)
-    own_1, *pieces = add_sides(keep_1, come_1, layers)
-    come_2, *parts_1 = send_all([(send, side)] + across(pieces), *parts_0)
-
-    other_grads = hidden_grads(grad_blocks, other_by, [down_0, down_1, down_2], chunks)
+    own_0, *pieces = add_sides(keep_0, come_0, types)
+    (come_1,) = send_all([(send, side)], own_0, own_grads)
+    far_0, next_0 = send_on(pieces)
+    near_0 = send_last(pieces, next_0, far_0)
+    other_grad = hidden_grads(grad_blocks, [down_0, down_1], chunks[:2])
+
+    keep_2, send = mix(2, down_2, send, other_grad, near_0)
+    own_1, *pieces = add_sides(keep_1, come_1, types)
+    (come_2,) = send_all([(send, side)], own_1)
+    far_1, next_1 = send_on(pieces, near_0)
+
+    other_by = after(other_by, next_1)
+    other_grads = hidden_grads(grad_blocks, [down_2], chunks[2:], by=other_by, before=other_grad)
     weights = [gate_weight, up_weight, other_gate, other_up]
 
     def back(c):
         lo, hi = back_chunks[c]
         return back_columns(own_grads, other_grads, weights, lo // (hi - lo), hi - lo)
 
+    near_1 = send_last(pieces, next_1, far_1)
     keep_3, send = back(0)
     (come_3,) = send_all([(send, side)])
 
     keep_4, send = back(1)
-    own_2, *pieces = add_sides(keep_2, come_2, layers)
-    come_4, *parts_2 = send_all([(send, side)] + across(pieces), *parts_1)
+    own_2, *pieces = add_sides(keep_2, come_2, types)
+    (come_4,) = send_all([(send, side)], own_2)
+    far_2, next_2 = send_on(pieces, near_1)
+    near_2 = send_last(pieces, next_2, far_2)
 
     keep_5, send = back(2)
-    own_3, *pieces = add_sides(keep_3, come_3, layers)
-    come_5, *parts_3 = send_all([(send, side)] + across(pieces), *parts_2)
-
-    own_4, *pieces = add_sides(keep_4, come_4, layers)
-    parts_4 = send_all(across(pieces), *parts_3)
-
-    own_5, *pieces = add_sides(keep_5, after(come_5, own_4), layers)
-    parts_5 = send_all(across(pieces))
-
-    mixed = finish(chunks, [(own_0, *parts_0), (own_1, *parts_1), (own_2, *parts_2)], width)
-    back_sum = finish(back_chunks, [(own_3, *parts_3), (own_4, *parts_4), (own_5, *parts_5)], width)
-    return (mixed, back_sum)
+    own_3, *pieces = add_sides(keep_3, come_3, types)
+    (come_5,) = send_all([(send, side)], own_3)
+    far_3, next_3 = send_on(pieces, near_2)
+    near_3 = send_last(pieces, next_3, far_3)
+
+    mixed = finish(chunks, [(own_0, far_0, near_0), (own_1, far_1, near_1), (own_2, far_2, near_2)], width)
+    own_4, *pieces = add_sides(keep_4, after(come_4, mixed), types)
+    far_4, next_4 = send_on(pieces, near_3)
+    near_4 = send_last(pieces, next_4, far_4)
+
+    own_5, *pieces = add_sides(keep_5, after(come_5, own_4), types)
+    far_5, next_5 = send_on(pieces, near_4)
+    near_5 = send_last(pieces, next_5, far_5)
+    back_parts = [(own_3, far_3, near_3), (own_4, far_4, near_4), (own_5, far_5, near_5)]
+    return (mixed, finish(back_chunks, back_parts, width))
 
 
 def route_slots(expert_ids, local_count, device_count, capacity):
@@ -433,7 +475,7 @@
 
 def on_device(tokens, cotangent, expert_ids, probs, gate_weight, up_weight, down_weight):
     devices = lax.axis_size("expert")
-    dense = devices % 4 == 0 and 16 <= devices <= 2 * expert_ids.shape[1]
+    dense = devices % 4 == 0 and 12 <= devices <= 2 * expert_ids.shape[1]
     body = on_device_dense if dense else on_device_routed
     return body(tokens, cotangent, expert_ids, probs, gate_weight, up_weight, down_weight)
 

time: 270 us -> 259 us (0.959)
  waiting for transfers between devices: 93.6 us -> 126 us
  starting transfers between devices: 85.8 us -> 59.5 us
  local copies, waits for them, and re-layouts: 36.1 us -> 21.6 us
  Pallas kernels: 51 us -> 48.3 us
    ppermute x43, waiting for transfers between devices: 93.6 us -> 126 us  [send_all(): lax.ppermute(v, 'expert', pairs)]
    ppermute x43, starting transfers between devices: 85.8 us -> 59.5 us  [send_all(): lax.ppermute(v, 'expert', pairs)]
    unnamed x74 -> x56, local copies, waits for them, and re-layouts: 31.6 us -> 18.2 us
    pallas_call x2 -> x9, Pallas kernels: 10.8 us -> 10.6 us  [the longest x3 10.4 us: hidden_grads(): pl.pallas_call(functools.partial(grads_kernel, blocks, tuple(cuts), by is...]
  transfers between devices with their start and end apart: 43 -> 43, of which waited for: 14 -> 29; matrix products, arithmetic and copies ran while one was open for 1% -> 1% of each run, Pallas kernels for 19% -> 18%
where the time goes in v6:
time: 259 us; the launch traced here: 258 us
  waiting for transfers between devices  126 us (49%)
  starting transfers between devices  59.5 us (23%)
  Pallas kernels  48.3 us (19%)
  local copies, waits for them, and re-layouts  21.6 us (8%)
    ppermute x43, waiting for transfers between devices, send_all(): lax.ppermute(v, 'expert', pairs)  126 us
    ppermute x43, starting transfers between devices, send_all(): lax.ppermute(v, 'expert', pairs)  59.5 us
    pallas_call x6, Pallas kernels, sum_columns(): pl.pallas_call(kernel, grid=(2,), in_specs=[rows, rows] + weight_specs, o...  21.3 us
    unnamed x56, local copies, waits for them, and re-layouts  18.2 us
    pallas_call x2, Pallas kernels, hidden_forward(): pl.pallas_call(functools.partial(hidden_kernel, blocks, all_experts), gri...  13.4 us
    pallas_call x3, Pallas kernels, hidden_grads(): pl.pallas_call(functools.partial(grads_kernel, blocks, tuple(cuts), by is...  10.4 us
  transfers between devices with their start and end apart: 43, of which 29 were waited for; matrix products, arithmetic and copies ran while one was open for 1% of the time, Pallas kernels for 18%

profile of v6, /device:TPU:0, one launch (start us, length us, event | category | flops | bytes accessed | tf_op | source)
XLA Modules:
  0.0 257.7 jit_solution(1376678106779022083)
XLA Ops:
  1.8 1.2 concatenate.3.refs_0_
  3.0 3.0 %collective-permute-start.10 = (bf16[2,2048,256]{2,1,0:T(8,128)(2,1)}, bf16[2,2048,256]{2,1,0:T(8,128)(2,1)S(1)}, u32[]{:S(2)}, u32[]{:S(2)}) collective-permute-start(bf16[2,2048,256]{2,1,0:T(8,128)(2,1)} %refs_0_.5), channel_id=1, source_target_pairs={{0,1},{1,0},{2,3},{3,2},{4,5},{5,4},{6,7},{7,6},{8,9},{9,8},{10,11... | collective-permute-start | bytes 6291464 | tf_op jit(solution)/shard_map/ppermute | solution.py:268
  6.0 1.5 collective-permute-start.1
  7.5 3.6 %collective-permute-start = (bf16[128,2176]{1,0:T(8,128)(2,1)S(1)}, bf16[128,2176]{1,0:T(8,128)(2,1)S(1)}, u32[]{:S(2)}, u32[]{:S(2)}) collective-permute-start(bf16[128,2176]{1,0:T(8,128)(2,1)S(1)} %concatenate.3.refs_0_), channel_id=1, source_target_pairs={{0,12},{1,13},{2,14},{3,15},{4,0},{5,1},{6,2},{7,3},{8,4},{9,5},{1... | collective-permute-start | bytes 1671176 | tf_op jit(solution)/shard_map/ppermute | solution.py:268
  11.6 9.9 %collective-permute-done.1.refs_4_ = bf16[128,2176]{1,0:T(8,128)(2,1)S(1)} collective-permute-done((bf16[128,2176]{1,0:T(8,128)(2,1)S(1)}, bf16[128,2176]{1,0:T(8,128)(2,1)S(1)}, u32[]{:S(2)}, u32[]{:S(2)}) %collective-permute-start.1) | collective-permute-done | bytes 557088 | tf_op jit(solution)/shard_map/ppermute | solution.py:268
  22.4 1.8 collective-permute-done.refs_1_
  24.7 4.3 %collective-permute-start.2 = (bf16[128,2176]{1,0:T(8,128)(2,1)S(1)}, bf16[128,2176]{1,0:T(8,128)(2,1)S(1)}, u32[]{:S(2)}, u32[]{:S(2)}) collective-permute-start(bf16[128,2176]{1,0:T(8,128)(2,1)S(1)} %collective-permute-done.refs_1_), channel_id=1, source_target_pairs={{0,12},{1,13},{2,14},{3,15},{4,0},{5,1},{6,2},{7,3},{8,4},{9,5},{1... | collective-permute-start | bytes 1671176 | tf_op jit(solution)/shard_map/ppermute | solution.py:268
  29.8 3.0 %collective-permute-done.6.refs_6_.refs_7_ = bf16[128,2048]{1,0:T(8,128)(2,1)S(1)} collective-permute-done((bf16[128,2048]{1,0:T(8,128)(2,1)}, bf16[128,2048]{1,0:T(8,128)(2,1)S(1)}, u32[]{:S(2)}, u32[]{:S(2)}) %collective-permute-start.6) | collective-permute-done | bytes 524320 | tf_op jit(solution)/shard_map/ppermute | solution.py:268
  33.6 3.5 %collective-permute-done.5.refs_3_ = bf16[128,2176]{1,0:T(8,128)(2,1)S(1)} collective-permute-done((bf16[128,2176]{1,0:T(8,128)(2,1)S(1)}, bf16[128,2176]{1,0:T(8,128)(2,1)S(1)}, u32[]{:S(2)}, u32[]{:S(2)}) %collective-permute-start.5) | collective-permute-done | bytes 557088 | tf_op jit(solution)/shard_map/ppermute | solution.py:268
  38.1 6.6 %collective-permute-done.3.refs_5_ = bf16[128,2176]{1,0:T(8,128)(2,1)S(1)} collective-permute-done((bf16[128,2176]{1,0:T(8,128)(2,1)S(1)}, bf16[128,2176]{1,0:T(8,128)(2,1)S(1)}, u32[]{:S(2)}, u32[]{:S(2)}) %collective-permute-start.3) | collective-permute-done | bytes 557088 | tf_op jit(solution)/shard_map/ppermute | solution.py:268
  48.3 3.6 %collective-permute-start.4 = (bf16[128,2048]{1,0:T(8,128)(2,1)}, bf16[128,2048]{1,0:T(8,128)(2,1)S(1)}, u32[]{:S(2)}, u32[]{:S(2)}) collective-permute-start(bf16[128,2048]{1,0:T(8,128)(2,1)} %refs_3_.1), channel_id=1, source_target_pairs={{0,12},{1,13},{2,14},{3,15},{4,0},{5,1},{6,2},{7,3},{8,4},{9,5},{1... | collective-permute-start | bytes 1572872 | tf_op jit(solution)/shard_map/ppermute | solution.py:268
  51.9 1.9 slice.12
  53.8 2.8 %collective-permute-done.7.refs_7_ = bf16[128,2176]{1,0:T(8,128)(2,1)S(1)} collective-permute-done((bf16[128,2176]{1,0:T(8,128)(2,1)S(1)}, bf16[128,2176]{1,0:T(8,128)(2,1)S(1)}, u32[]{:S(2)}, u32[]{:S(2)}) %collective-permute-start.7) | collective-permute-done | bytes 557088 | tf_op jit(solution)/shard_map/ppermute | solution.py:268
  57.5 4.4 %collective-permute-done.4.refs_3_.refs_4_ = bf16[128,2048]{1,0:T(8,128)(2,1)S(1)} collective-permute-done((bf16[128,2048]{1,0:T(8,128)(2,1)}, bf16[128,2048]{1,0:T(8,128)(2,1)S(1)}, u32[]{:S(2)}, u32[]{:S(2)}) %collective-permute-start.4) | collective-permute-done | bytes 524320 | tf_op jit(solution)/shard_map/ppermute | solution.py:268
  61.9 5.3 %collective-permute-done.8.refs_6_ = bf16[128,2176]{1,0:T(8,128)(2,1)S(1)} collective-permute-done((bf16[128,2176]{1,0:T(8,128)(2,1)S(1)}, bf16[128,2176]{1,0:T(8,128)(2,1)S(1)}, u32[]{:S(2)}, u32[]{:S(2)}) %collective-permute-start.8) | collective-permute-done | bytes 557088 | tf_op jit(solution)/shard_map/ppermute | solution.py:268
  67.9 1.5 collective-permute-start.9
  69.5 3.6 %collective-permute-start.19 = (bf16[128,2048]{1,0:T(8,128)(2,1)S(1)}, bf16[128,2048]{1,0:T(8,128)(2,1)}, u32[]{:S(2)}, u32[]{:S(2)}) collective-permute-start(bf16[128,2048]{1,0:T(8,128)(2,1)S(1)} %collective-permute-done.4.refs_3_.refs_4_), channel_id=1, source_target_pairs={{0,12},{1,13},{2,14},{3,15},{4,0},{5,1},{6,2},{7,3},{8,4},{9,5},{1... | collective-permute-start | bytes 1572872 | tf_op jit(solution)/shard_map/ppermute | solution.py:268
  73.9 1.4 copy-done.4
  75.8 4.7 %collective-permute-done.9.refs_7_.refs_8_ = bf16[128,2048]{1,0:T(8,128)(2,1)S(1)} collective-permute-done((bf16[128,2048]{1,0:T(8,128)(2,1)S(1)}, bf16[128,2048]{1,0:T(8,128)(2,1)S(1)}, u32[]{:S(2)}, u32[]{:S(2)}) %collective-permute-start.9) | collective-permute-done | bytes 524320 | tf_op jit(solution)/shard_map/ppermute | solution.py:268
  81.3 4.1 %collective-permute-done.19.refs_4_.refs_5_ = bf16[128,2048]{1,0:T(8,128)(2,1)} collective-permute-done((bf16[128,2048]{1,0:T(8,128)(2,1)S(1)}, bf16[128,2048]{1,0:T(8,128)(2,1)}, u32[]{:S(2)}, u32[]{:S(2)}) %collective-permute-start.19) | collective-permute-done | bytes 524320 | tf_op jit(solution)/shard_map/ppermute | solution.py:268
  85.9 9.2 %collective-permute-done.13.refs_5_.refs_6_ = bf16[128,2048]{1,0:T(8,128)(2,1)} collective-permute-done((bf16[128,2048]{1,0:T(8,128)(2,1)S(1)}, bf16[128,2048]{1,0:T(8,128)(2,1)}, u32[]{:S(2)}, u32[]{:S(2)}) %collective-permute-start.13) | collective-permute-done | bytes 524320 | tf_op jit(solution)/shard_map/ppermute | solution.py:268
  95.8 1.5 copy-done.1
  97.3 1.6 copy-done.2
  98.9 1.1 copy-done.16
  100.0 1.1 copy-done.18
  102.1 1.1 copy-done.22
  105.2 5.9 %hidden_forward.2 = (bf16[1024,512]{1,0:T(8,128)(2,1)S(1)}, f32[1024,1024]{1,0:T(8,128)S(1)}) custom-call(s32[1]{0:T(128)} %bitcast.owner_ref, bf16[2,2048,256]{2,1,0:T(8,128)(2,1)S(1)} %copy-done.1, bf16[2,2048,256]{2,1,0:T(8,128)(2,1)S(1)} %copy-done.2, bf16[128,2176]{1,0:T(8,128)(2,1)S(1)} %concatenate.3.refs_0_, bf16[128,2176]{1,0:T(8,128)(2,1)S(1)} %copy-done.16, ...), custom_call_target="tpu_custom_call" | custom-call | flops 1 | bytes 1 | tf_op jit(solution)/shard_map/hidden_forward/pallas_call | solution.py:70
  111.2 7.5 %hidden_forward.3 = (bf16[1024,512]{1,0:T(8,128)(2,1)S(1)}, f32[1024,1024]{1,0:T(8,128)S(1)}) custom-call(s32[1]{0:T(128)} %bitcast.1.owner_ref, bf16[2,2048,256]{2,1,0:T(8,128)(2,1)S(1)} %copy-done.5, bf16[2,2048,256]{2,1,0:T(8,128)(2,1)} %collective-permute-done.11.up_ref.refs_3_, bf16[128,2176]{1,0:T(8,128)(2,1)S(1)} %concatenate.3.refs_0_, ...), custom_call_target="tpu_custom_call" | custom-call | flops 1 | bytes 1 | tf_op jit(solution)/shard_map/hidden_forward/pallas_call | solution.py:70
  119.4 2.6 %mix_columns.3 = (f32[512,512]{1,0:T(8,128)S(1)}, bf16[512,512]{1,0:T(8,128)(2,1)S(1)}) custom-call(bf16[1024,512]{1,0:T(8,128)(2,1)S(1)} %get-tuple-element.98.own_ref, bf16[1024,512]{1,0:T(8,128)(2,1)S(1)} %get-tuple-element.102.other_ref, bf16[512,2048]{1,0:T(8,128)(2,1)S(1)} %bitcast.5, bf16[512,512]{1,0:T(8,128)(2,1)} %collective-permute-done.12.other_down_ref.refs_0_), custom_call_target="tpu_custom_call" | custom-call | flops 1 | bytes 1 | tf_op jit(solution)/shard_map/mix_columns/pallas_call | solution.py:178
  122.0 1.6 collective-permute-start.15
  123.6 1.5 collective-permute-start.26
  125.1 3.6 %hidden_grads.3.own_ref = bf16[1024,1024]{1,0:T(8,128)(2,1)S(1)} custom-call(f32[1024,1024]{1,0:T(8,128)S(1)} %get-tuple-element.120.refs_0_, bf16[512,2048]{1,0:T(8,128)(2,1)S(1)} %bitcast.6, bf16[128,2048]{1,0:T(8,128)(2,1)S(1)} %copy-done.6, bf16[128,2048]{1,0:T(8,128)(2,1)S(1)} %copy-done.10, bf16[128,2048]{1,0:T(8,128)(2,1)} %collective-permute-done.19.refs_4_.refs_5_, ...), custom_call_target="tpu_custom_call" | custom-call | flops 1 | bytes 1 | tf_op jit(solution)/shard_map/hidden_grads/pallas_call | solution.py:126
  128.8 4.2 %collective-permute-done.15.come_ref = bf16[512,512]{1,0:T(8,128)(2,1)S(1)} collective-permute-done((bf16[512,512]{1,0:T(8,128)(2,1)S(1)}, bf16[512,512]{1,0:T(8,128)(2,1)S(1)}, u32[]{:S(2)}, u32[]{:S(2)}) %collective-permute-start.15) | collective-permute-done | bytes 524320 | tf_op jit(solution)/shard_map/ppermute | solution.py:268
  133.1 6.2 %collective-permute-done.21.other_down_ref.refs_1_ = bf16[512,768]{1,0:T(8,128)(2,1)S(1)} collective-permute-done((bf16[512,768]{1,0:T(8,128)(2,1)S(1)}, bf16[512,768]{1,0:T(8,128)(2,1)S(1)}, u32[]{:S(2)}, u32[]{:S(2)}) %collective-permute-start.21) | collective-permute-done | bytes 786464 | tf_op jit(solution)/shard_map/ppermute | solution.py:268
  139.3 2.2 mix_columns.4
  141.6 1.6 collective-permute-start.22
  143.1 1.6 collective-permute-start.17
  144.8 2.2 collective-permute-start.16
  147.0 3.1 %collective-permute-done.17.come_ref = bf16[128,512]{1,0:T(8,128)(2,1)S(1)} collective-permute-done((bf16[128,512]{1,0:T(8,128)(2,1)S(1)}, bf16[128,512]{1,0:T(8,128)(2,1)S(1)}, u32[]{:S(2)}, u32[]{:S(2)}) %collective-permute-start.17) | collective-permute-done | bytes 131104 | tf_op jit(solution)/shard_map/ppermute | solution.py:268
  151.9 4.0 %hidden_grads.4.refs_1_ = f32[1024,512]{1,0:T(8,128)S(1)} custom-call(bf16[512,512]{1,0:T(8,128)(2,1)} %collective-permute-done.12.other_down_ref.refs_0_, bf16[512,768]{1,0:T(8,128)(2,1)S(1)} %collective-permute-done.21.other_down_ref.refs_1_, bf16[128,2048]{1,0:T(8,128)(2,1)S(1)} %copy-done.6, bf16[128,2048]{1,0:T(8,128)(2,1)S(1)} %copy-done.10, ...), custom_call_target="tpu_custom_call" | custom-call | flops 1 | bytes 1 | tf_op jit(solution)/shard_map/hidden_grads/pallas_call | solution.py:126
  155.9 2.1 collective-permute-done.18.refs_2_
  158.0 2.2 mix_columns.5
  161.0 3.8 %collective-permute-start.23 = (bf16[128,768]{1,0:T(8,128)(2,1)S(1)}, bf16[128,768]{1,0:T(8,128)(2,1)S(1)}, u32[]{:S(2)}, u32[]{:S(2)}) collective-permute-start(bf16[128,768]{1,0:T(8,128)(2,1)S(1)} %get-tuple-element.124), channel_id=1, source_target_pairs={{0,12},{1,13},{2,14},{3,15},{4,0},{5,1},{6,2},{7,3},{8,4},{9,5},{1... | collective-permute-start | bytes 589832 | tf_op jit(solution)/shard_map/ppermute | solution.py:268
  164.8 3.8 %collective-permute-done.24.come_ref = bf16[128,768]{1,0:T(8,128)(2,1)S(1)} collective-permute-done((bf16[128,768]{1,0:T(8,128)(2,1)S(1)}, bf16[128,768]{1,0:T(8,128)(2,1)S(1)}, u32[]{:S(2)}, u32[]{:S(2)}) %collective-permute-start.24) | collective-permute-done | bytes 196640 | tf_op jit(solution)/shard_map/ppermute | solution.py:268
  168.6 2.8 %hidden_grads.5.other_ref = bf16[1024,1024]{1,0:T(8,128)(2,1)S(1)} custom-call(f32[1024,1024]{1,0:T(8,128)S(1)} %get-tuple-element.142.refs_0_, f32[1024,512]{1,0:T(8,128)S(1)} %hidden_grads.4.refs_1_, bf16[512,768]{1,0:T(8,128)(2,1)S(1)} %collective-permute-done.26.other_down_ref.refs_2_, bf16[128,2048]{1,0:T(8,128)(2,1)S(1)} %copy-done.6, ...), custom_call_target="tpu_custom_call" | custom-call | flops 1 | bytes 1 | tf_op jit(solution)/shard_map/hidden_grads/pallas_call | solution.py:126
  171.3 5.2 %back_columns.3 = (f32[512,768]{1,0:T(8,128)S(1)}, bf16[512,768]{1,0:T(8,128)(2,1)S(1)}) custom-call(bf16[1024,1024]{1,0:T(8,128)(2,1)S(1)} %hidden_grads.3.own_ref, bf16[1024,1024]{1,0:T(8,128)(2,1)S(1)} %hidden_grads.5.other_ref, bf16[2,2048,256]{2,1,0:T(8,128)(2,1)S(1)} %copy-done.1, bf16[2,2048,256]{2,1,0:T(8,128)(2,1)S(1)} %copy-done.3, ...), custom_call_target="tpu_custom_call" | custom-call | flops 1 | bytes 1 | tf_op jit(solution)/shard_map/back_columns/pallas_call | solution.py:178
  176.5 1.6 collective-permute-start.31
  178.4 9.4 %collective-permute-done.25.refs_5_ = bf16[128,768]{1,0:T(8,128)(2,1)S(1)} collective-permute-done((bf16[128,768]{1,0:T(8,128)(2,1)S(1)}, bf16[128,768]{1,0:T(8,128)(2,1)S(1)}, u32[]{:S(2)}, u32[]{:S(2)}) %collective-permute-start.25) | collective-permute-done | bytes 196640 | tf_op jit(solution)/shard_map/ppermute | solution.py:268
  187.8 3.8 %collective-permute-start.28 = (bf16[128,768]{1,0:T(8,128)(2,1)S(1)}, bf16[128,768]{1,0:T(8,128)(2,1)S(1)}, u32[]{:S(2)}, u32[]{:S(2)}) collective-permute-start(bf16[128,768]{1,0:T(8,128)(2,1)S(1)} %get-tuple-element.136), channel_id=1, source_target_pairs={{0,12},{1,13},{2,14},{3,15},{4,0},{5,1},{6,2},{7,3},{8,4},{9,5},{1... | collective-permute-start | bytes 589832 | tf_op jit(solution)/shard_map/ppermute | solution.py:268
  191.6 5.2 %back_columns.4 = (f32[512,768]{1,0:T(8,128)S(1)}, bf16[512,768]{1,0:T(8,128)(2,1)S(1)}) custom-call(bf16[1024,1024]{1,0:T(8,128)(2,1)S(1)} %hidden_grads.3.own_ref, bf16[1024,1024]{1,0:T(8,128)(2,1)S(1)} %hidden_grads.5.other_ref, bf16[2,2048,256]{2,1,0:T(8,128)(2,1)S(1)} %copy-done.1, bf16[2,2048,256]{2,1,0:T(8,128)(2,1)S(1)} %copy-done.3, ...), custom_call_target="tpu_custom_call" | custom-call | flops 1 | bytes 1 | tf_op jit(solution)/shard_map/back_columns/pallas_call | solution.py:178
  197.8 9.4 %collective-permute-done.30.refs_8_ = bf16[128,768]{1,0:T(8,128)(2,1)S(1)} collective-permute-done((bf16[128,768]{1,0:T(8,128)(2,1)S(1)}, bf16[128,768]{1,0:T(8,128)(2,1)S(1)}, u32[]{:S(2)}, u32[]{:S(2)}) %collective-permute-start.30) | collective-permute-done | bytes 196640 | tf_op jit(solution)/shard_map/ppermute | solution.py:268
  207.2 3.8 %collective-permute-start.32 = (bf16[128,768]{1,0:T(8,128)(2,1)S(1)}, bf16[128,768]{1,0:T(8,128)(2,1)S(1)}, u32[]{:S(2)}, u32[]{:S(2)}) collective-permute-start(bf16[128,768]{1,0:T(8,128)(2,1)S(1)} %get-tuple-element.147), channel_id=1, source_target_pairs={{0,12},{1,13},{2,14},{3,15},{4,0},{5,1},{6,2},{7,3},{8,4},{9,5},{1... | collective-permute-start | bytes 589832 | tf_op jit(solution)/shard_map/ppermute | solution.py:268
  211.0 3.8 %collective-permute-done.33.come_ref = bf16[128,768]{1,0:T(8,128)(2,1)S(1)} collective-permute-done((bf16[128,768]{1,0:T(8,128)(2,1)S(1)}, bf16[128,768]{1,0:T(8,128)(2,1)S(1)}, u32[]{:S(2)}, u32[]{:S(2)}) %collective-permute-start.33) | collective-permute-done | bytes 196640 | tf_op jit(solution)/shard_map/ppermute | solution.py:268
  215.6 3.9 %back_columns.5 = (f32[512,512]{1,0:T(8,128)S(1)}, bf16[512,512]{1,0:T(8,128)(2,1)S(1)}) custom-call(bf16[1024,1024]{1,0:T(8,128)(2,1)S(1)} %hidden_grads.3.own_ref, bf16[1024,1024]{1,0:T(8,128)(2,1)S(1)} %hidden_grads.5.other_ref, bf16[2,2048,256]{2,1,0:T(8,128)(2,1)S(1)} %copy-done.1, bf16[2,2048,256]{2,1,0:T(8,128)(2,1)S(1)} %copy-done.3, ...), custom_call_target="tpu_custom_call" | custom-call | flops 1 | bytes 1 | tf_op jit(solution)/shard_map/back_columns/pallas_call | solution.py:178
  220.2 1.1 finish.2
  221.4 1.7 collective-permute-done.34.refs_2_
  223.1 3.2 %collective-permute-start.37 = (bf16[128,768]{1,0:T(8,128)(2,1)S(1)}, bf16[128,768]{1,0:T(8,128)(2,1)S(1)}, u32[]{:S(2)}, u32[]{:S(2)}) collective-permute-start(bf16[128,768]{1,0:T(8,128)(2,1)S(1)} %get-tuple-element.161), channel_id=1, source_target_pairs={{0,4},{1,5},{2,6},{3,7},{4,8},{5,9},{6,10},{7,11},{8,12},{9,13},{1... | collective-permute-start | bytes 589832 | tf_op jit(solution)/shard_map/ppermute | solution.py:268
  226.9 3.9 %collective-permute-done.37.come_ref = bf16[128,768]{1,0:T(8,128)(2,1)S(1)} collective-permute-done((bf16[128,768]{1,0:T(8,128)(2,1)S(1)}, bf16[128,768]{1,0:T(8,128)(2,1)S(1)}, u32[]{:S(2)}, u32[]{:S(2)}) %collective-permute-start.37) | collective-permute-done | bytes 196640 | tf_op jit(solution)/shard_map/ppermute | solution.py:268
  230.9 4.6 %collective-permute-done.36.refs_4_ = bf16[128,768]{1,0:T(8,128)(2,1)S(1)} collective-permute-done((bf16[128,768]{1,0:T(8,128)(2,1)S(1)}, bf16[128,768]{1,0:T(8,128)(2,1)S(1)}, u32[]{:S(2)}, u32[]{:S(2)}) %collective-permute-start.36) | collective-permute-done | bytes 196640 | tf_op jit(solution)/shard_map/ppermute | solution.py:268
  236.1 6.8 %collective-permute-done.38.refs_5_ = bf16[128,768]{1,0:T(8,128)(2,1)S(1)} collective-permute-done((bf16[128,768]{1,0:T(8,128)(2,1)S(1)}, bf16[128,768]{1,0:T(8,128)(2,1)S(1)}, u32[]{:S(2)}, u32[]{:S(2)}) %collective-permute-start.38) | collective-permute-done | bytes 196640 | tf_op jit(solution)/shard_map/ppermute | solution.py:268
  243.0 3.8 %collective-permute-start.40 = (bf16[128,512]{1,0:T(8,128)(2,1)S(1)}, bf16[128,512]{1,0:T(8,128)(2,1)S(1)}, u32[]{:S(2)}, u32[]{:S(2)}) collective-permute-start(bf16[128,512]{1,0:T(8,128)(2,1)S(1)} %get-tuple-element.169), channel_id=1, source_target_pairs={{0,12},{1,13},{2,14},{3,15},{4,0},{5,1},{6,2},{7,3},{8,4},{9,5},{1... | collective-permute-start | bytes 393224 | tf_op jit(solution)/shard_map/ppermute | solution.py:268
  246.8 2.9 %collective-permute-done.41.come_ref = bf16[128,512]{1,0:T(8,128)(2,1)S(1)} collective-permute-done((bf16[128,512]{1,0:T(8,128)(2,1)S(1)}, bf16[128,512]{1,0:T(8,128)(2,1)S(1)}, u32[]{:S(2)}, u32[]{:S(2)}) %collective-permute-start.41) | collective-permute-done | bytes 131104 | tf_op jit(solution)/shard_map/ppermute | solution.py:268
  249.9 6.8 %collective-permute-done.42.refs_8_ = bf16[128,512]{1,0:T(8,128)(2,1)S(1)} collective-permute-done((bf16[128,512]{1,0:T(8,128)(2,1)S(1)}, bf16[128,512]{1,0:T(8,128)(2,1)S(1)}, u32[]{:S(2)}, u32[]{:S(2)}) %collective-permute-start.42) | collective-permute-done | bytes 131104 | tf_op jit(solution)/shard_map/ppermute | solution.py:268
  256.6 1.1 finish.3
  (112 shorter events, 25.1 us)
Async XLA Ops:
  0.6 74.6 %copy-start.6 = (bf16[128,2048]{1,0:T(8,128)(2,1)S(1)}, bf16[128,2048]{1,0:T(8,128)(2,1)}, u32[]{:S(2)}) copy-start(bf16[128,2048]{1,0:T(8,128)(2,1)} %refs_3_.1) | copy-start | bytes 1572868
  0.6 95.0 %copy-start = (bf16[2,256,2048]{2,1,0:T(8,128)(2,1)S(1)}, bf16[2,256,2048]{2,1,0:T(8,128)(2,1)}, u32[]{:S(2)}) copy-start(bf16[2,256,2048]{2,1,0:T(8,128)(2,1)} %param.13) | copy-start | bytes 6291460
  3.0 70.9 %collective-permute-start.10 = (bf16[2,2048,256]{2,1,0:T(8,128)(2,1)}, bf16[2,2048,256]{2,1,0:T(8,128)(2,1)S(1)}, u32[]{:S(2)}, u32[]{:S(2)}) collective-permute-start(bf16[2,2048,256]{2,1,0:T(8,128)(2,1)} %refs_0_.5), channel_id=1, source_target_pairs={{0,1},{1,0},{2,3},{3,2},{4,5},{5,4},{6,7},{7,6},{8,9},{9,8},{10,11... | collective-permute-start | bytes 6291464 | tf_op jit(solution)/shard_map/ppermute | solution.py:268
  6.0 15.6 %collective-permute-start.1 = (bf16[128,2176]{1,0:T(8,128)(2,1)S(1)}, bf16[128,2176]{1,0:T(8,128)(2,1)S(1)}, u32[]{:S(2)}, u32[]{:S(2)}) collective-permute-start(bf16[128,2176]{1,0:T(8,128)(2,1)S(1)} %concatenate.3.refs_0_), channel_id=1, source_target_pairs={{0,2},{1,3},{2,0},{3,1},{4,6},{5,7},{6,4},{7,5},{8,10},{9,11},{10,... | collective-permute-start | bytes 1671176 | tf_op jit(solution)/shard_map/ppermute | solution.py:268
  7.5 16.7 %collective-permute-start = (bf16[128,2176]{1,0:T(8,128)(2,1)S(1)}, bf16[128,2176]{1,0:T(8,128)(2,1)S(1)}, u32[]{:S(2)}, u32[]{:S(2)}) collective-permute-start(bf16[128,2176]{1,0:T(8,128)(2,1)S(1)} %concatenate.3.refs_0_), channel_id=1, source_target_pairs={{0,12},{1,13},{2,14},{3,15},{4,0},{5,1},{6,2},{7,3},{8,4},{9,5},{1... | collective-permute-start | bytes 1671176 | tf_op jit(solution)/shard_map/ppermute | solution.py:268
  11.1 26.0 %collective-permute-start.5 = (bf16[128,2176]{1,0:T(8,128)(2,1)S(1)}, bf16[128,2176]{1,0:T(8,128)(2,1)S(1)}, u32[]{:S(2)}, u32[]{:S(2)}) collective-permute-start(bf16[128,2176]{1,0:T(8,128)(2,1)S(1)} %concatenate.3.refs_0_), channel_id=1, source_target_pairs={{0,4},{1,5},{2,6},{3,7},{4,8},{5,9},{6,10},{7,11},{8,12},{9,13},{1... | collective-permute-start | bytes 1671176 | tf_op jit(solution)/shard_map/ppermute | solution.py:268
  11.1 21.7 %collective-permute-start.6 = (bf16[128,2048]{1,0:T(8,128)(2,1)}, bf16[128,2048]{1,0:T(8,128)(2,1)S(1)}, u32[]{:S(2)}, u32[]{:S(2)}) collective-permute-start(bf16[128,2048]{1,0:T(8,128)(2,1)} %refs_3_.1), channel_id=1, source_target_pairs={{0,2},{1,3},{2,0},{3,1},{4,6},{5,7},{6,4},{7,5},{8,10},{9,11},{10,... | collective-permute-start | bytes 1572872 | tf_op jit(solution)/shard_map/ppermute | solution.py:268
  24.2 20.5 %collective-permute-start.3 = (bf16[128,2176]{1,0:T(8,128)(2,1)S(1)}, bf16[128,2176]{1,0:T(8,128)(2,1)S(1)}, u32[]{:S(2)}, u32[]{:S(2)}) collective-permute-start(bf16[128,2176]{1,0:T(8,128)(2,1)S(1)} %collective-permute-done.refs_1_), channel_id=1, source_target_pairs={{0,2},{1,3},{2,0},{3,1},{4,6},{5,7},{6,4},{7,5},{8,10},{9,11},{10,... | collective-permute-start | bytes 1671176 | tf_op jit(solution)/shard_map/ppermute | solution.py:268
  24.7 21.8 %collective-permute-start.2 = (bf16[128,2176]{1,0:T(8,128)(2,1)S(1)}, bf16[128,2176]{1,0:T(8,128)(2,1)S(1)}, u32[]{:S(2)}, u32[]{:S(2)}) collective-permute-start(bf16[128,2176]{1,0:T(8,128)(2,1)S(1)} %collective-permute-done.refs_1_), channel_id=1, source_target_pairs={{0,12},{1,13},{2,14},{3,15},{4,0},{5,1},{6,2},{7,3},{8,4},{9,5},{1... | collective-permute-start | bytes 1671176 | tf_op jit(solution)/shard_map/ppermute | solution.py:268
  32.8 0.9 copy-start.7
  37.1 58.0 %copy-start.17 = (bf16[128,2176]{1,0:T(8,128)(2,1)}, bf16[128,2176]{1,0:T(8,128)(2,1)S(1)}, u32[]{:S(2)}) copy-start(bf16[128,2176]{1,0:T(8,128)(2,1)S(1)} %collective-permute-done.5.refs_3_) | copy-start | bytes 1671172
  37.1 74.1 %collective-permute-start.11 = (bf16[2,2048,256]{2,1,0:T(8,128)(2,1)}, bf16[2,2048,256]{2,1,0:T(8,128)(2,1)}, u32[]{:S(2)}, u32[]{:S(2)}) collective-permute-start(bf16[2,2048,256]{2,1,0:T(8,128)(2,1)} %refs_1_.5), channel_id=1, source_target_pairs={{0,1},{1,0},{2,3},{3,2},{4,5},{5,4},{6,7},{7,6},{8,9},{9,8},{10,11... | collective-permute-start | bytes 6291464 | tf_op jit(solution)/shard_map/ppermute | solution.py:268
  37.6 19.0 %collective-permute-start.7 = (bf16[128,2176]{1,0:T(8,128)(2,1)S(1)}, bf16[128,2176]{1,0:T(8,128)(2,1)S(1)}, u32[]{:S(2)}, u32[]{:S(2)}) collective-permute-start(bf16[128,2176]{1,0:T(8,128)(2,1)S(1)} %collective-permute-done.5.refs_3_), channel_id=1, source_target_pairs={{0,2},{1,3},{2,0},{3,1},{4,6},{5,7},{6,4},{7,5},{8,10},{9,11},{10,... | collective-permute-start | bytes 1671176 | tf_op jit(solution)/shard_map/ppermute | solution.py:268
  46.5 20.6 %collective-permute-start.8 = (bf16[128,2176]{1,0:T(8,128)(2,1)S(1)}, bf16[128,2176]{1,0:T(8,128)(2,1)S(1)}, u32[]{:S(2)}, u32[]{:S(2)}) collective-permute-start(bf16[128,2176]{1,0:T(8,128)(2,1)S(1)} %collective-permute-done.2.refs_2_), channel_id=1, source_target_pairs={{0,2},{1,3},{2,0},{3,1},{4,6},{5,7},{6,4},{7,5},{8,10},{9,11},{10,... | collective-permute-start | bytes 1671176 | tf_op jit(solution)/shard_map/ppermute | solution.py:268
  48.3 13.5 %collective-permute-start.4 = (bf16[128,2048]{1,0:T(8,128)(2,1)}, bf16[128,2048]{1,0:T(8,128)(2,1)S(1)}, u32[]{:S(2)}, u32[]{:S(2)}) collective-permute-start(bf16[128,2048]{1,0:T(8,128)(2,1)} %refs_3_.1), channel_id=1, source_target_pairs={{0,12},{1,13},{2,14},{3,15},{4,0},{5,1},{6,2},{7,3},{8,4},{9,5},{1... | collective-permute-start | bytes 1572872 | tf_op jit(solution)/shard_map/ppermute | solution.py:268
  67.9 12.6 %collective-permute-start.9 = (bf16[128,2048]{1,0:T(8,128)(2,1)S(1)}, bf16[128,2048]{1,0:T(8,128)(2,1)S(1)}, u32[]{:S(2)}, u32[]{:S(2)}) collective-permute-start(bf16[128,2048]{1,0:T(8,128)(2,1)S(1)} %collective-permute-done.4.refs_3_.refs_4_), channel_id=1, source_target_pairs={{0,2},{1,3},{2,0},{3,1},{4,6},{5,7},{6,4},{7,5},{8,10},{9,11},{10,... | collective-permute-start | bytes 1572872 | tf_op jit(solution)/shard_map/ppermute | solution.py:268
  69.5 16.0 %collective-permute-start.19 = (bf16[128,2048]{1,0:T(8,128)(2,1)S(1)}, bf16[128,2048]{1,0:T(8,128)(2,1)}, u32[]{:S(2)}, u32[]{:S(2)}) collective-permute-start(bf16[128,2048]{1,0:T(8,128)(2,1)S(1)} %collective-permute-done.4.refs_3_.refs_4_), channel_id=1, source_target_pairs={{0,12},{1,13},{2,14},{3,15},{4,0},{5,1},{6,2},{7,3},{8,4},{9,5},{1... | collective-permute-start | bytes 1572872 | tf_op jit(solution)/shard_map/ppermute | solution.py:268
  73.9 1.4 copy-start.4
  75.2 19.9 %collective-permute-start.13 = (bf16[128,2048]{1,0:T(8,128)(2,1)S(1)}, bf16[128,2048]{1,0:T(8,128)(2,1)}, u32[]{:S(2)}, u32[]{:S(2)}) collective-permute-start(bf16[128,2048]{1,0:T(8,128)(2,1)S(1)} %copy-done.6), channel_id=1, source_target_pairs={{0,4},{1,5},{2,6},{3,7},{4,8},{5,9},{6,10},{7,11},{8,12},{9,13},{1... | collective-permute-start | bytes 1572872 | tf_op jit(solution)/shard_map/ppermute | solution.py:268
  75.2 43.5 %collective-permute-start.12 = (bf16[512,512]{1,0:T(8,128)(2,1)}, bf16[512,512]{1,0:T(8,128)(2,1)}, u32[]{:S(2)}, u32[]{:S(2)}) collective-permute-start(bf16[512,512]{1,0:T(8,128)(2,1)} %slice.12), channel_id=1, source_target_pairs={{0,1},{1,0},{2,3},{3,2},{4,5},{5,4},{6,7},{7,6},{8,9},{9,8},{10,11... | collective-permute-start | bytes 1572872 | tf_op jit(solution)/shard_map/ppermute | solution.py:268
  80.5 0.8 copy-start.11
  85.4 33.3 %collective-permute-start.20 = (bf16[128,2048]{1,0:T(8,128)(2,1)}, bf16[128,2048]{1,0:T(8,128)(2,1)}, u32[]{:S(2)}, u32[]{:S(2)}) collective-permute-start(bf16[128,2048]{1,0:T(8,128)(2,1)} %collective-permute-done.19.refs_4_.refs_5_), channel_id=1, source_target_pairs={{0,2},{1,3},{2,0},{3,1},{4,6},{5,7},{6,4},{7,5},{8,10},{9,11},{10,... | collective-permute-start | bytes 1572872 | tf_op jit(solution)/shard_map/ppermute | solution.py:268
  95.1 23.6 %collective-permute-start.14 = (bf16[128,2048]{1,0:T(8,128)(2,1)}, bf16[128,2048]{1,0:T(8,128)(2,1)}, u32[]{:S(2)}, u32[]{:S(2)}) collective-permute-start(bf16[128,2048]{1,0:T(8,128)(2,1)} %collective-permute-done.13.refs_5_.refs_6_), channel_id=1, source_target_pairs={{0,2},{1,3},{2,0},{3,1},{4,6},{5,7},{6,4},{7,5},{8,10},{9,11},{10,... | collective-permute-start | bytes 1572872 | tf_op jit(solution)/shard_map/ppermute | solution.py:268
  95.6 1.6 copy-start.1
  95.6 1.7 copy-start.14
  97.3 1.6 copy-start.2
  98.9 1.1 copy-start.16
  100.0 1.1 copy-start.18
  101.0 1.1 copy-start.20
  102.1 1.1 copy-start.22
  103.1 1.1 copy-start.25
  104.2 1.1 copy-start.27
  105.2 5.9 %copy-start.5 = (bf16[2,2048,256]{2,1,0:T(8,128)(2,1)S(1)}, bf16[2,2048,256]{2,1,0:T(8,128)(2,1)}, u32[]{:S(2)}) copy-start(bf16[2,2048,256]{2,1,0:T(8,128)(2,1)} %copy-done.4) | copy-start | bytes 6291460
  105.2 5.9 %copy-start.23 = (bf16[128,2176]{1,0:T(8,128)(2,1)S(1)}, bf16[128,2176]{1,0:T(8,128)(2,1)}, u32[]{:S(2)}) copy-start(bf16[128,2176]{1,0:T(8,128)(2,1)} %copy-done.21) | copy-start | bytes 1671172
  118.8 6.4 %copy-start.8 = (bf16[128,2048]{1,0:T(8,128)(2,1)S(1)}, bf16[128,2048]{1,0:T(8,128)(2,1)}, u32[]{:S(2)}) copy-start(bf16[128,2048]{1,0:T(8,128)(2,1)} %copy-done.7) | copy-start | bytes 1572868
  118.8 6.4 %copy-start.10 = (bf16[128,2048]{1,0:T(8,128)(2,1)S(1)}, bf16[128,2048]{1,0:T(8,128)(2,1)}, u32[]{:S(2)}) copy-start(bf16[128,2048]{1,0:T(8,128)(2,1)} %copy-done.9) | copy-start | bytes 1572868
  118.8 6.3 %copy-start.12 = (bf16[128,2048]{1,0:T(8,128)(2,1)S(1)}, bf16[128,2048]{1,0:T(8,128)(2,1)}, u32[]{:S(2)}) copy-start(bf16[128,2048]{1,0:T(8,128)(2,1)} %copy-done.11) | copy-start | bytes 1572868
  118.8 20.5 %collective-permute-start.21 = (bf16[512,768]{1,0:T(8,128)(2,1)S(1)}, bf16[512,768]{1,0:T(8,128)(2,1)S(1)}, u32[]{:S(2)}, u32[]{:S(2)}) collective-permute-start(bf16[512,768]{1,0:T(8,128)(2,1)S(1)} %get-tuple-element.116), channel_id=1, source_target_pairs={{0,1},{1,0},{2,3},{3,2},{4,5},{5,4},{6,7},{7,6},{8,9},{9,8},{10,11... | collective-permute-start | bytes 2359304 | tf_op jit(solution)/shard_map/ppermute | solution.py:268
  122.0 11.0 %collective-permute-start.15 = (bf16[512,512]{1,0:T(8,128)(2,1)S(1)}, bf16[512,512]{1,0:T(8,128)(2,1)S(1)}, u32[]{:S(2)}, u32[]{:S(2)}) collective-permute-start(bf16[512,512]{1,0:T(8,128)(2,1)S(1)} %get-tuple-element.109), channel_id=1, source_target_pairs={{0,2},{1,3},{2,0},{3,1},{4,6},{5,7},{6,4},{7,5},{8,10},{9,11},{10,... | collective-permute-start | bytes 1572872 | tf_op jit(solution)/shard_map/ppermute | solution.py:268
  123.6 34.4 %collective-permute-start.26 = (bf16[512,768]{1,0:T(8,128)(2,1)S(1)}, bf16[512,768]{1,0:T(8,128)(2,1)S(1)}, u32[]{:S(2)}, u32[]{:S(2)}) collective-permute-start(bf16[512,768]{1,0:T(8,128)(2,1)S(1)} %get-tuple-element.129), channel_id=1, source_target_pairs={{0,1},{1,0},{2,3},{3,2},{4,5},{5,4},{6,7},{7,6},{8,9},{9,8},{10,11... | collective-permute-start | bytes 2359304 | tf_op jit(solution)/shard_map/ppermute | solution.py:268
  141.6 18.7 %collective-permute-start.22 = (bf16[512,768]{1,0:T(8,128)(2,1)S(1)}, bf16[512,768]{1,0:T(8,128)(2,1)S(1)}, u32[]{:S(2)}, u32[]{:S(2)}) collective-permute-start(bf16[512,768]{1,0:T(8,128)(2,1)S(1)} %get-tuple-element.121), channel_id=1, source_target_pairs={{0,2},{1,3},{2,0},{3,1},{4,6},{5,7},{6,4},{7,5},{8,10},{9,11},{10,... | collective-permute-start | bytes 2359304 | tf_op jit(solution)/shard_map/ppermute | solution.py:268
  143.1 6.9 %collective-permute-start.17 = (bf16[128,512]{1,0:T(8,128)(2,1)S(1)}, bf16[128,512]{1,0:T(8,128)(2,1)S(1)}, u32[]{:S(2)}, u32[]{:S(2)}) collective-permute-start(bf16[128,512]{1,0:T(8,128)(2,1)S(1)} %get-tuple-element.113), channel_id=1, source_target_pairs={{0,4},{1,5},{2,6},{3,7},{4,8},{5,9},{6,10},{7,11},{8,12},{9,13},{1... | collective-permute-start | bytes 393224 | tf_op jit(solution)/shard_map/ppermute | solution.py:268
  144.8 6.4 %collective-permute-start.16 = (bf16[128,512]{1,0:T(8,128)(2,1)S(1)}, bf16[128,512]{1,0:T(8,128)(2,1)S(1)}, u32[]{:S(2)}, u32[]{:S(2)}) collective-permute-start(bf16[128,512]{1,0:T(8,128)(2,1)S(1)} %get-tuple-element.111), channel_id=1, source_target_pairs={{0,12},{1,13},{2,14},{3,15},{4,0},{5,1},{6,2},{7,3},{8,4},{9,5},{1... | collective-permute-start | bytes 393224 | tf_op jit(solution)/shard_map/ppermute | solution.py:268
  151.1 6.8 %collective-permute-start.18 = (bf16[128,512]{1,0:T(8,128)(2,1)S(1)}, bf16[128,512]{1,0:T(8,128)(2,1)S(1)}, u32[]{:S(2)}, u32[]{:S(2)}) collective-permute-start(bf16[128,512]{1,0:T(8,128)(2,1)S(1)} %add_piece.6), channel_id=1, source_target_pairs={{0,4},{1,5},{2,6},{3,7},{4,8},{5,9},{6,10},{7,11},{8,12},{9,13},{1... | collective-permute-start | bytes 393224 | tf_op jit(solution)/shard_map/ppermute | solution.py:268
  160.4 17.9 %collective-permute-start.27 = (bf16[512,768]{1,0:T(8,128)(2,1)S(1)}, bf16[512,768]{1,0:T(8,128)(2,1)S(1)}, u32[]{:S(2)}, u32[]{:S(2)}) collective-permute-start(bf16[512,768]{1,0:T(8,128)(2,1)S(1)} %get-tuple-element.133), channel_id=1, source_target_pairs={{0,2},{1,3},{2,0},{3,1},{4,6},{5,7},{6,4},{7,5},{8,10},{9,11},{10,... | collective-permute-start | bytes 2359304 | tf_op jit(solution)/shard_map/ppermute | solution.py:268
  160.9 7.6 %collective-permute-start.24 = (bf16[128,768]{1,0:T(8,128)(2,1)S(1)}, bf16[128,768]{1,0:T(8,128)(2,1)S(1)}, u32[]{:S(2)}, u32[]{:S(2)}) collective-permute-start(bf16[128,768]{1,0:T(8,128)(2,1)S(1)} %get-tuple-element.127), channel_id=1, source_target_pairs={{0,4},{1,5},{2,6},{3,7},{4,8},{5,9},{6,10},{7,11},{8,12},{9,13},{1... | collective-permute-start | bytes 589832 | tf_op jit(solution)/shard_map/ppermute | solution.py:268
  161.0 17.2 %collective-permute-start.23 = (bf16[128,768]{1,0:T(8,128)(2,1)S(1)}, bf16[128,768]{1,0:T(8,128)(2,1)S(1)}, u32[]{:S(2)}, u32[]{:S(2)}) collective-permute-start(bf16[128,768]{1,0:T(8,128)(2,1)S(1)} %get-tuple-element.124), channel_id=1, source_target_pairs={{0,12},{1,13},{2,14},{3,15},{4,0},{5,1},{6,2},{7,3},{8,4},{9,5},{1... | collective-permute-start | bytes 589832 | tf_op jit(solution)/shard_map/ppermute | solution.py:268
  168.6 2.8 %copy-start.3 = (bf16[2,2048,256]{2,1,0:T(8,128)(2,1)S(1)}, bf16[2,2048,256]{2,1,0:T(8,128)(2,1)}, u32[]{:S(2)}) copy-start(bf16[2,2048,256]{2,1,0:T(8,128)(2,1)} %refs_1_.5) | copy-start | bytes 6291460
  176.5 21.1 %collective-permute-start.31 = (bf16[512,768]{1,0:T(8,128)(2,1)S(1)}, bf16[512,768]{1,0:T(8,128)(2,1)S(1)}, u32[]{:S(2)}, u32[]{:S(2)}) collective-permute-start(bf16[512,768]{1,0:T(8,128)(2,1)S(1)} %get-tuple-element.144), channel_id=1, source_target_pairs={{0,2},{1,3},{2,0},{3,1},{4,6},{5,7},{6,4},{7,5},{8,10},{9,11},{10,... | collective-permute-start | bytes 2359304 | tf_op jit(solution)/shard_map/ppermute | solution.py:268
  178.2 9.6 %collective-permute-start.25 = (bf16[128,768]{1,0:T(8,128)(2,1)S(1)}, bf16[128,768]{1,0:T(8,128)(2,1)S(1)}, u32[]{:S(2)}, u32[]{:S(2)}) collective-permute-start(bf16[128,768]{1,0:T(8,128)(2,1)S(1)} %add_piece.7), channel_id=1, source_target_pairs={{0,4},{1,5},{2,6},{3,7},{4,8},{5,9},{6,10},{7,11},{8,12},{9,13},{1... | collective-permute-start | bytes 589832 | tf_op jit(solution)/shard_map/ppermute | solution.py:268
  187.8 9.6 %collective-permute-start.29 = (bf16[128,768]{1,0:T(8,128)(2,1)S(1)}, bf16[128,768]{1,0:T(8,128)(2,1)S(1)}, u32[]{:S(2)}, u32[]{:S(2)}) collective-permute-start(bf16[128,768]{1,0:T(8,128)(2,1)S(1)} %get-tuple-element.139), channel_id=1, source_target_pairs={{0,4},{1,5},{2,6},{3,7},{4,8},{5,9},{6,10},{7,11},{8,12},{9,13},{1... | collective-permute-start | bytes 589832 | tf_op jit(solution)/shard_map/ppermute | solution.py:268
  187.8 9.9 %collective-permute-start.28 = (bf16[128,768]{1,0:T(8,128)(2,1)S(1)}, bf16[128,768]{1,0:T(8,128)(2,1)S(1)}, u32[]{:S(2)}, u32[]{:S(2)}) collective-permute-start(bf16[128,768]{1,0:T(8,128)(2,1)S(1)} %get-tuple-element.136), channel_id=1, source_target_pairs={{0,12},{1,13},{2,14},{3,15},{4,0},{5,1},{6,2},{7,3},{8,4},{9,5},{1... | collective-permute-start | bytes 589832 | tf_op jit(solution)/shard_map/ppermute | solution.py:268
  196.8 24.5 %collective-permute-start.35 = (bf16[512,768]{1,0:T(8,128)(2,1)S(1)}, bf16[512,768]{1,0:T(8,128)(2,1)S(1)}, u32[]{:S(2)}, u32[]{:S(2)}) collective-permute-start(bf16[512,768]{1,0:T(8,128)(2,1)S(1)} %get-tuple-element.154), channel_id=1, source_target_pairs={{0,2},{1,3},{2,0},{3,1},{4,6},{5,7},{6,4},{7,5},{8,10},{9,11},{10,... | collective-permute-start | bytes 2359304 | tf_op jit(solution)/shard_map/ppermute | solution.py:268
  197.7 9.5 %collective-permute-start.30 = (bf16[128,768]{1,0:T(8,128)(2,1)S(1)}, bf16[128,768]{1,0:T(8,128)(2,1)S(1)}, u32[]{:S(2)}, u32[]{:S(2)}) collective-permute-start(bf16[128,768]{1,0:T(8,128)(2,1)S(1)} %add_piece.8), channel_id=1, source_target_pairs={{0,4},{1,5},{2,6},{3,7},{4,8},{5,9},{6,10},{7,11},{8,12},{9,13},{1... | collective-permute-start | bytes 589832 | tf_op jit(solution)/shard_map/ppermute | solution.py:268
  207.2 7.6 %collective-permute-start.33 = (bf16[128,768]{1,0:T(8,128)(2,1)S(1)}, bf16[128,768]{1,0:T(8,128)(2,1)S(1)}, u32[]{:S(2)}, u32[]{:S(2)}) collective-permute-start(bf16[128,768]{1,0:T(8,128)(2,1)S(1)} %get-tuple-element.150), channel_id=1, source_target_pairs={{0,4},{1,5},{2,6},{3,7},{4,8},{5,9},{6,10},{7,11},{8,12},{9,13},{1... | collective-permute-start | bytes 589832 | tf_op jit(solution)/shard_map/ppermute | solution.py:268
  207.2 7.8 %collective-permute-start.32 = (bf16[128,768]{1,0:T(8,128)(2,1)S(1)}, bf16[128,768]{1,0:T(8,128)(2,1)S(1)}, u32[]{:S(2)}, u32[]{:S(2)}) collective-permute-start(bf16[128,768]{1,0:T(8,128)(2,1)S(1)} %get-tuple-element.147), channel_id=1, source_target_pairs={{0,12},{1,13},{2,14},{3,15},{4,0},{5,1},{6,2},{7,3},{8,4},{9,5},{1... | collective-permute-start | bytes 589832 | tf_op jit(solution)/shard_map/ppermute | solution.py:268
  214.9 8.2 %collective-permute-start.34 = (bf16[128,768]{1,0:T(8,128)(2,1)S(1)}, bf16[128,768]{1,0:T(8,128)(2,1)S(1)}, u32[]{:S(2)}, u32[]{:S(2)}) collective-permute-start(bf16[128,768]{1,0:T(8,128)(2,1)S(1)} %add_piece.9), channel_id=1, source_target_pairs={{0,4},{1,5},{2,6},{3,7},{4,8},{5,9},{6,10},{7,11},{8,12},{9,13},{1... | collective-permute-start | bytes 589832 | tf_op jit(solution)/shard_map/ppermute | solution.py:268
  219.5 16.6 %collective-permute-start.39 = (bf16[512,512]{1,0:T(8,128)(2,1)S(1)}, bf16[512,512]{1,0:T(8,128)(2,1)S(1)}, u32[]{:S(2)}, u32[]{:S(2)}) collective-permute-start(bf16[512,512]{1,0:T(8,128)(2,1)S(1)} %get-tuple-element.165), channel_id=1, source_target_pairs={{0,2},{1,3},{2,0},{3,1},{4,6},{5,7},{6,4},{7,5},{8,10},{9,11},{10,... | collective-permute-start | bytes 1572872 | tf_op jit(solution)/shard_map/ppermute | solution.py:268
  223.1 7.8 %collective-permute-start.37 = (bf16[128,768]{1,0:T(8,128)(2,1)S(1)}, bf16[128,768]{1,0:T(8,128)(2,1)S(1)}, u32[]{:S(2)}, u32[]{:S(2)}) collective-permute-start(bf16[128,768]{1,0:T(8,128)(2,1)S(1)} %get-tuple-element.161), channel_id=1, source_target_pairs={{0,4},{1,5},{2,6},{3,7},{4,8},{5,9},{6,10},{7,11},{8,12},{9,13},{1... | collective-permute-start | bytes 589832 | tf_op jit(solution)/shard_map/ppermute | solution.py:268
  226.3 9.3 %collective-permute-start.36 = (bf16[128,768]{1,0:T(8,128)(2,1)S(1)}, bf16[128,768]{1,0:T(8,128)(2,1)S(1)}, u32[]{:S(2)}, u32[]{:S(2)}) collective-permute-start(bf16[128,768]{1,0:T(8,128)(2,1)S(1)} %get-tuple-element.158), channel_id=1, source_target_pairs={{0,12},{1,13},{2,14},{3,15},{4,0},{5,1},{6,2},{7,3},{8,4},{9,5},{1... | collective-permute-start | bytes 589832 | tf_op jit(solution)/shard_map/ppermute | solution.py:268
  235.5 7.5 %collective-permute-start.38 = (bf16[128,768]{1,0:T(8,128)(2,1)S(1)}, bf16[128,768]{1,0:T(8,128)(2,1)S(1)}, u32[]{:S(2)}, u32[]{:S(2)}) collective-permute-start(bf16[128,768]{1,0:T(8,128)(2,1)S(1)} %add_piece.10), channel_id=1, source_target_pairs={{0,4},{1,5},{2,6},{3,7},{4,8},{5,9},{6,10},{7,11},{8,12},{9,13},{1... | collective-permute-start | bytes 589832 | tf_op jit(solution)/shard_map/ppermute | solution.py:268
  243.0 6.8 %collective-permute-start.41 = (bf16[128,512]{1,0:T(8,128)(2,1)S(1)}, bf16[128,512]{1,0:T(8,128)(2,1)S(1)}, u32[]{:S(2)}, u32[]{:S(2)}) collective-permute-start(bf16[128,512]{1,0:T(8,128)(2,1)S(1)} %get-tuple-element.172), channel_id=1, source_target_pairs={{0,4},{1,5},{2,6},{3,7},{4,8},{5,9},{6,10},{7,11},{8,12},{9,13},{1... | collective-permute-start | bytes 393224 | tf_op jit(solution)/shard_map/ppermute | solution.py:268
  243.0 6.8 %collective-permute-start.40 = (bf16[128,512]{1,0:T(8,128)(2,1)S(1)}, bf16[128,512]{1,0:T(8,128)(2,1)S(1)}, u32[]{:S(2)}, u32[]{:S(2)}) collective-permute-start(bf16[128,512]{1,0:T(8,128)(2,1)S(1)} %get-tuple-element.169), channel_id=1, source_target_pairs={{0,12},{1,13},{2,14},{3,15},{4,0},{5,1},{6,2},{7,3},{8,4},{9,5},{1... | collective-permute-start | bytes 393224 | tf_op jit(solution)/shard_map/ppermute | solution.py:268
  249.8 6.8 %collective-permute-start.42 = (bf16[128,512]{1,0:T(8,128)(2,1)S(1)}, bf16[128,512]{1,0:T(8,128)(2,1)S(1)}, u32[]{:S(2)}, u32[]{:S(2)}) collective-permute-start(bf16[128,512]{1,0:T(8,128)(2,1)S(1)} %add_piece.11), channel_id=1, source_target_pairs={{0,4},{1,5},{2,6},{3,7},{4,8},{5,9},{6,10},{7,11},{8,12},{9,13},{1... | collective-permute-start | bytes 393224 | tf_op jit(solution)/shard_map/ppermute | solution.py:268
  (7 other events, 5.7 us)

commit v7 on v6

--- a/solution.py
+++ b/solution.py
@@ -8,6 +8,7 @@
 from jax.sharding import PartitionSpec as P
 
 VMEM_BYTES = 18 * 2**20
+VMEM_BYTES_FETCH = 56 * 2**20
 AT_ONCE = pl.CostEstimate(flops=1, bytes_accessed=1, transcendentals=0)
 
 
@@ -15,8 +16,8 @@
     return pl.BlockSpec(shape, index, pipeline_mode=pl.Buffered(1))
 
 
-def compiler_params():
-    return pltpu.CompilerParams(vmem_limit_bytes=VMEM_BYTES)
+def compiler_params(vmem_bytes=VMEM_BYTES):
+    return pltpu.CompilerParams(vmem_limit_bytes=vmem_bytes)
 
 
 def fetch_rows(block_refs, buffer, sems):
@@ -84,7 +85,7 @@
             pltpu.VMEM((blocks, block, row_width), jnp.bfloat16),
             pltpu.SemaphoreType.DMA((blocks,)),
         ],
-        compiler_params=compiler_params(),
+        compiler_params=compiler_params(VMEM_BYTES_FETCH),
         cost_estimate=AT_ONCE,
         name="hidden_forward",
     )(owner.reshape(1), gate_weight, up_weight, *row_blocks)
@@ -234,10 +235,12 @@
     )(piece, come)
 
 
-def finish_kernel(chunks, layers, *refs):
+def finish_kernel(chunks, counts, *refs):
     out_ref = refs[-1]
-    for c, (lo, hi) in enumerate(chunks):
-        own_ref, *piece_refs = refs[c * layers : (c + 1) * layers]
+    refs = list(refs[:-1])
+    for (lo, hi), count in zip(chunks, counts):
+        own_ref, *piece_refs = refs[:count]
+        del refs[:count]
         total = own_ref[...]
         for piece_ref in piece_refs:
             total += piece_ref[...].astype(jnp.float32)
@@ -246,7 +249,7 @@
 
 def finish(chunks, parts, width):
     return pl.pallas_call(
-        functools.partial(finish_kernel, tuple(chunks), len(parts[0])),
+        functools.partial(finish_kernel, tuple(chunks), tuple(map(len, parts))),
         out_shape=jax.ShapeDtypeStruct((parts[0][0].shape[0], width), jnp.float32),
         compiler_params=compiler_params(),
         cost_estimate=AT_ONCE,
@@ -274,8 +277,8 @@
     layers = devices // 4
     experts = local_count * devices
     block = tokens.shape[0]
-    chunks = cut_columns(width, ((6, 8), (0, 3), (3, 6)))
-    back_chunks = cut_columns(width, ((0, 3), (3, 6), (6, 8)))
+    chunks = cut_columns(width, ((0, 3), (3, 6), (6, 8)))
+    back_chunks = cut_columns(width, ((4, 8), (0, 3), (3, 4)))
     me = lax.axis_index("expert")
     twin = [(d, d ^ 1) for d in range(devices)]
     side = [(d, d ^ 2) for d in range(devices)]
@@ -309,15 +312,14 @@
     for k in middle:
         (grads[k],) = send_all([(grads[k - 1], layer[-one])], *far_rows.values())
     (far_grads[last],) = send_all([(grads[last], side)], *far_rows.values())
+    row_blocks = [rows[k] for k in range(layers)] + [far_rows[k] for k in range(layers)]
+    activ, by = hidden_forward(row_blocks, me, gate_weight, up_weight, experts)
     for k in middle:
-        (far_grads[k],) = send_all([(grads[k], side)], far_grads[one])
-    row_blocks = [rows[k] for k in range(layers)] + [far_rows[k] for k in range(layers)]
-    own = after(me, far_grads[one])
-    activ, by = hidden_forward(row_blocks, own, gate_weight, up_weight, experts)
+        (far_grads[k],) = send_all([(grads[k], side)], far_grads[one], activ)
     other_up = after(other_up, activ)
     other_activ, other_by = hidden_forward(row_blocks, me ^ 1, other_gate, other_up, experts)
 
-    (down_1,) = send_all([(downs[1], twin)], down_0, activ, other_activ, *far_grads.values())
+    (down_1,) = send_all([(downs[1], twin)], down_0, activ, other_activ)
 
     def mix(c, other_down, *waits):
         lo, hi = chunks[c]
@@ -337,7 +339,7 @@
         piece = pieces[0].astype(jnp.bfloat16) if come is None else add_piece(pieces[0], come)
         return send_all([(piece, layer[one])], far)[0]
 
-    keep_0, send = mix(0, down_0, other_activ)
+    keep_0, send = mix(0, down_0, other_activ, *far_grads.values())
     come_0, down_2 = send_all([(send, side), (downs[2], twin)], far_grads[last])
     grad_blocks = [grads[k] for k in range(layers)] + [far_grads[k] for k in range(layers)]
     own_grads = hidden_grads(grad_blocks, [down], [(0, width)], by=by)
@@ -352,41 +354,41 @@
     keep_2, send = mix(2, down_2, send, other_grad, near_0)
     own_1, *pieces = add_sides(keep_1, come_1, types)
     (come_2,) = send_all([(send, side)], own_1)
-    far_1, next_1 = send_on(pieces, near_0)
-
-    other_by = after(other_by, next_1)
+    far_1, next_1 = send_on(pieces)
+
+    other_by = after(other_by, next_1, far_1)
     other_grads = hidden_grads(grad_blocks, [down_2], chunks[2:], by=other_by, before=other_grad)
     weights = [gate_weight, up_weight, other_gate, other_up]
 
-    def back(c):
+    def back(c, *waits):
         lo, hi = back_chunks[c]
-        return back_columns(own_grads, other_grads, weights, lo // (hi - lo), hi - lo)
+        return back_columns(own_grads, after(other_grads, *waits), weights, lo // (hi - lo), hi - lo)
 
     near_1 = send_last(pieces, next_1, far_1)
     keep_3, send = back(0)
     (come_3,) = send_all([(send, side)])
 
-    keep_4, send = back(1)
+    keep_4, send = back(1, near_1)
     own_2, *pieces = add_sides(keep_2, come_2, types)
     (come_4,) = send_all([(send, side)], own_2)
-    far_2, next_2 = send_on(pieces, near_1)
+    far_2, next_2 = send_on(pieces, far_1)
     near_2 = send_last(pieces, next_2, far_2)
 
-    keep_5, send = back(2)
+    keep_5, send = back(2, near_2)
     own_3, *pieces = add_sides(keep_3, come_3, types)
     (come_5,) = send_all([(send, side)], own_3)
-    far_3, next_3 = send_on(pieces, near_2)
+    far_3, next_3 = send_on(pieces, near_1)
     near_3 = send_last(pieces, next_3, far_3)
 
     mixed = finish(chunks, [(own_0, far_0, near_0), (own_1, far_1, near_1), (own_2, far_2, near_2)], width)
     own_4, *pieces = add_sides(keep_4, after(come_4, mixed), types)
-    far_4, next_4 = send_on(pieces, near_3)
+    far_4, next_4 = send_on(pieces, near_2)
     near_4 = send_last(pieces, next_4, far_4)
 
+    types = [jnp.float32] + [jnp.bfloat16] * (layers - 1)
     own_5, *pieces = add_sides(keep_5, after(come_5, own_4), types)
-    far_5, next_5 = send_on(pieces, near_4)
-    near_5 = send_last(pieces, next_5, far_5)
-    back_parts = [(own_3, far_3, near_3), (own_4, far_4, near_4), (own_5, far_5, near_5)]
+    parts_5 = send_all([(piece, layer[k]) for k, piece in enumerate(pieces, 1)], near_3)
+    back_parts = [(own_3, far_3, near_3), (own_4, far_4, near_4), (own_5, *parts_5)]
     return (mixed, finish(back_chunks, back_parts, width))
 
 

time: 259 us -> 246 us (0.950)
  local copies, waits for them, and re-layouts: 21.6 us -> 7.36 us
  Pallas kernels: 48.3 us -> 56.9 us
  waiting for transfers between devices: 126 us -> 120 us
    unnamed x56 -> x36, local copies, waits for them, and re-layouts: 18.2 us -> 2.45 us
    pallas_call x2, Pallas kernels: 13.4 us -> 20.1 us  [hidden_forward(): pl.pallas_call(functools.partial(hidden_kernel, blocks, all_experts), gri...]
    ppermute x43, waiting for transfers between devices: 126 us -> 120 us  [send_all(): lax.ppermute(v, 'expert', pairs)]
  transfers between devices with their start and end apart: 43 -> 43, of which waited for: 29 -> 24; matrix products, arithmetic and copies ran while one was open for 1% -> 1% of each run, Pallas kernels for 18% -> 23%
where the time goes in v7:
time: 246 us; the launch traced here: 245 us
  waiting for transfers between devices  120 us (49%)
  starting transfers between devices  58.9 us (24%)
  Pallas kernels  56.9 us (23%)
  local copies, waits for them, and re-layouts  7.36 us (3%)
    ppermute x43, waiting for transfers between devices, send_all(): lax.ppermute(v, 'expert', pairs)  120 us
    ppermute x43, starting transfers between devices, send_all(): lax.ppermute(v, 'expert', pairs)  58.9 us
    pallas_call x6, Pallas kernels, sum_columns(): pl.pallas_call(kernel, grid=(2,), in_specs=[rows, rows] + weight_specs, o...  22 us
    pallas_call x2, Pallas kernels, hidden_forward(): pl.pallas_call(functools.partial(hidden_kernel, blocks, all_experts), gri...  20.1 us
    pallas_call x3, Pallas kernels, hidden_grads(): pl.pallas_call(functools.partial(grads_kernel, blocks, tuple(cuts), by is...  11.7 us
  transfers between devices with their start and end apart: 43, of which 24 were waited for; matrix products, arithmetic and copies ran while one was open for 1% of the time, Pallas kernels for 23%

profile of v7, /device:TPU:0, one launch (start us, length us, event | category | flops | bytes accessed | tf_op | source)
XLA Modules:
  0.0 245.2 jit_solution(2770079962307666218)
XLA Ops:
  1.6 1.2 concatenate.3.refs_0_
  2.9 3.0 %collective-permute-start.8 = (bf16[2,2048,256]{2,1,0:T(8,128)(2,1)}, bf16[2,2048,256]{2,1,0:T(8,128)(2,1)}, u32[]{:S(2)}, u32[]{:S(2)}) collective-permute-start(bf16[2,2048,256]{2,1,0:T(8,128)(2,1)} %refs_0_.5), channel_id=1, source_target_pairs={{0,1},{1,0},{2,3},{3,2},{4,5},{5,4},{6,7},{7,6},{8,9},{9,8},{10,11... | collective-permute-start | bytes 6291464 | tf_op jit(solution)/shard_map/ppermute | solution.py:271
  5.9 3.6 %collective-permute-start = (bf16[128,2176]{1,0:T(8,128)(2,1)S(1)}, bf16[128,2176]{1,0:T(8,128)(2,1)S(1)}, u32[]{:S(2)}, u32[]{:S(2)}) collective-permute-start(bf16[128,2176]{1,0:T(8,128)(2,1)S(1)} %concatenate.3.refs_0_), channel_id=1, source_target_pairs={{0,12},{1,13},{2,14},{3,15},{4,0},{5,1},{6,2},{7,3},{8,4},{9,5},{1... | collective-permute-start | bytes 1671176 | tf_op jit(solution)/shard_map/ppermute | solution.py:271
  9.5 1.5 collective-permute-start.1
  11.5 11.0 %collective-permute-done.refs_1_ = bf16[128,2176]{1,0:T(8,128)(2,1)S(1)} collective-permute-done((bf16[128,2176]{1,0:T(8,128)(2,1)S(1)}, bf16[128,2176]{1,0:T(8,128)(2,1)S(1)}, u32[]{:S(2)}, u32[]{:S(2)}) %collective-permute-start) | collective-permute-done | bytes 557088 | tf_op jit(solution)/shard_map/ppermute | solution.py:271
  22.6 2.5 %collective-permute-done.1.refs_4_ = bf16[128,2176]{1,0:T(8,128)(2,1)S(1)} collective-permute-done((bf16[128,2176]{1,0:T(8,128)(2,1)S(1)}, bf16[128,2176]{1,0:T(8,128)(2,1)S(1)}, u32[]{:S(2)}, u32[]{:S(2)}) %collective-permute-start.1) | collective-permute-done | bytes 557088 | tf_op jit(solution)/shard_map/ppermute | solution.py:271
  25.1 1.5 collective-permute-start.4
  26.6 1.9 collective-permute-start.2
  28.4 7.9 %collective-permute-done.6.refs_6_.refs_7_ = bf16[128,2048]{1,0:T(8,128)(2,1)S(1)} collective-permute-done((bf16[128,2048]{1,0:T(8,128)(2,1)}, bf16[128,2048]{1,0:T(8,128)(2,1)S(1)}, u32[]{:S(2)}, u32[]{:S(2)}) %collective-permute-start.6) | collective-permute-done | bytes 524320 | tf_op jit(solution)/shard_map/ppermute | solution.py:271
  36.8 1.5 collective-permute-start.7
  38.4 9.9 %collective-permute-done.4.refs_5_ = bf16[128,2176]{1,0:T(8,128)(2,1)S(1)} collective-permute-done((bf16[128,2176]{1,0:T(8,128)(2,1)S(1)}, bf16[128,2176]{1,0:T(8,128)(2,1)S(1)}, u32[]{:S(2)}, u32[]{:S(2)}) %collective-permute-start.4) | collective-permute-done | bytes 557088 | tf_op jit(solution)/shard_map/ppermute | solution.py:271
  48.2 0.8 copy-done.12
  49.0 1.5 collective-permute-start.5
  51.0 2.6 %fusion.1 = (bf16[512,768]{1,0:T(8,128)(2,1)}, bf16[512,768]{1,0:T(8,128)(2,1)}) fusion(bf16[512,2048]{1,0:T(8,128)(2,1)} %bitcast.3), kind=kLoop, calls=%fused_computation.5 | loop fusion | bytes 3145728 | tf_op jit(solution)/shard_map/slice | solution.py:297
  53.6 6.5 %collective-permute-done.7.refs_7_ = bf16[128,2176]{1,0:T(8,128)(2,1)S(1)} collective-permute-done((bf16[128,2176]{1,0:T(8,128)(2,1)S(1)}, bf16[128,2176]{1,0:T(8,128)(2,1)S(1)}, u32[]{:S(2)}, u32[]{:S(2)}) %collective-permute-start.7) | collective-permute-done | bytes 557088 | tf_op jit(solution)/shard_map/ppermute | solution.py:271
  60.2 1.3 collective-permute-done.11.refs_3_.refs_4_
  61.5 8.9 %collective-permute-done.5.refs_6_ = bf16[128,2176]{1,0:T(8,128)(2,1)S(1)} collective-permute-done((bf16[128,2176]{1,0:T(8,128)(2,1)S(1)}, bf16[128,2176]{1,0:T(8,128)(2,1)S(1)}, u32[]{:S(2)}, u32[]{:S(2)}) %collective-permute-start.5) | collective-permute-done | bytes 557088 | tf_op jit(solution)/shard_map/ppermute | solution.py:271
  70.8 1.5 collective-permute-start.12
  72.3 1.6 collective-permute-start.13
  74.5 10.0 %hidden_forward.2 = (bf16[1024,512]{1,0:T(8,128)(2,1)}, f32[1024,1024]{1,0:T(8,128)}) custom-call(s32[1]{0:T(128)} %bitcast.owner_ref, bf16[2,2048,256]{2,1,0:T(8,128)(2,1)} %refs_0_.5, bf16[2,2048,256]{2,1,0:T(8,128)(2,1)} %refs_1_.5, bf16[128,2176]{1,0:T(8,128)(2,1)} %copy-done.8, bf16[128,2176]{1,0:T(8,128)(2,1)} %copy-done.9, ...), custom_call_target="tpu_custom_call" | custom-call | flops 1 | bytes 1 | tf_op jit(solution)/shard_map/hidden_forward/pallas_call | solution.py:71
  84.5 9.6 %collective-permute-done.15.refs_4_.refs_5_ = bf16[128,2048]{1,0:T(8,128)(2,1)} collective-permute-done((bf16[128,2048]{1,0:T(8,128)(2,1)}, bf16[128,2048]{1,0:T(8,128)(2,1)}, u32[]{:S(2)}, u32[]{:S(2)}) %collective-permute-start.15) | collective-permute-done | bytes 524320 | tf_op jit(solution)/shard_map/ppermute | solution.py:271
  94.2 1.5 collective-permute-start.16
  96.2 0.8 slice.13
  97.6 10.1 %hidden_forward.3 = (bf16[1024,512]{1,0:T(8,128)(2,1)}, f32[1024,1024]{1,0:T(8,128)}) custom-call(s32[1]{0:T(128)} %bitcast.1.owner_ref, bf16[2,2048,256]{2,1,0:T(8,128)(2,1)} %collective-permute-done.8.gate_ref.refs_2_, bf16[2,2048,256]{2,1,0:T(8,128)(2,1)} %collective-permute-done.9.up_ref.refs_3_, bf16[128,2176]{1,0:T(8,128)(2,1)} %copy-done.8, ...), custom_call_target="tpu_custom_call" | custom-call | flops 1 | bytes 1 | tf_op jit(solution)/shard_map/hidden_forward/pallas_call | solution.py:71
  107.7 5.9 %collective-permute-done.10.other_down_ref.refs_0_ = bf16[512,768]{1,0:T(8,128)(2,1)} collective-permute-done((bf16[512,768]{1,0:T(8,128)(2,1)}, bf16[512,768]{1,0:T(8,128)(2,1)}, u32[]{:S(2)}, u32[]{:S(2)}) %collective-permute-start.10) | collective-permute-done | bytes 786464 | tf_op jit(solution)/shard_map/ppermute | solution.py:271
  113.6 1.7 collective-permute-start.21
  115.4 1.2 copy-done.4
  116.6 3.5 %mix_columns.3 = (f32[512,768]{1,0:T(8,128)S(1)}, bf16[512,768]{1,0:T(8,128)(2,1)S(1)}) custom-call(bf16[1024,512]{1,0:T(8,128)(2,1)S(1)} %copy-done.3, bf16[1024,512]{1,0:T(8,128)(2,1)S(1)} %copy-done.4, bf16[512,2048]{1,0:T(8,128)(2,1)S(1)} %bitcast.5, bf16[512,768]{1,0:T(8,128)(2,1)} %collective-permute-done.10.other_down_ref.refs_0_), custom_call_target="tpu_custom_call" | custom-call | flops 1 | bytes 1 | tf_op jit(solution)/shard_map/mix_columns/pallas_call | solution.py:179
  120.1 1.6 collective-permute-start.17
  121.7 4.2 %hidden_grads.3.own_ref = bf16[1024,1024]{1,0:T(8,128)(2,1)S(1)} custom-call(f32[1024,1024]{1,0:T(8,128)S(1)} %copy-done.7, bf16[512,2048]{1,0:T(8,128)(2,1)S(1)} %bitcast.6, bf16[128,2048]{1,0:T(8,128)(2,1)S(1)} %copy-done.5, bf16[128,2048]{1,0:T(8,128)(2,1)} %collective-permute-done.11.refs_3_.refs_4_, ...), custom_call_target="tpu_custom_call" | custom-call | flops 1 | bytes 1 | tf_op jit(solution)/shard_map/hidden_grads/pallas_call | solution.py:127
  125.9 6.5 %collective-permute-done.21.other_down_ref.refs_1_ = bf16[512,768]{1,0:T(8,128)(2,1)S(1)} collective-permute-done((bf16[512,768]{1,0:T(8,128)(2,1)S(1)}, bf16[512,768]{1,0:T(8,128)(2,1)S(1)}, u32[]{:S(2)}, u32[]{:S(2)}) %collective-permute-start.21) | collective-permute-done | bytes 786464 | tf_op jit(solution)/shard_map/ppermute | solution.py:271
  132.4 2.2 mix_columns.4
  134.6 3.7 %collective-permute-done.17.come_ref = bf16[512,768]{1,0:T(8,128)(2,1)S(1)} collective-permute-done((bf16[512,768]{1,0:T(8,128)(2,1)S(1)}, bf16[512,768]{1,0:T(8,128)(2,1)S(1)}, u32[]{:S(2)}, u32[]{:S(2)}) %collective-permute-start.17) | collective-permute-done | bytes 786464 | tf_op jit(solution)/shard_map/ppermute | solution.py:271
  138.5 1.6 collective-permute-start.22
  140.6 1.6 collective-permute-start.19
  142.2 2.2 collective-permute-start.18
  144.4 4.3 %collective-permute-done.19.come_ref = bf16[128,768]{1,0:T(8,128)(2,1)S(1)} collective-permute-done((bf16[128,768]{1,0:T(8,128)(2,1)S(1)}, bf16[128,768]{1,0:T(8,128)(2,1)S(1)}, u32[]{:S(2)}, u32[]{:S(2)}) %collective-permute-start.19) | collective-permute-done | bytes 196640 | tf_op jit(solution)/shard_map/ppermute | solution.py:271
  148.8 1.3 collective-permute-done.18.refs_1_
  150.1 1.2 collective-permute-start.20
  151.3 4.4 %collective-permute-done.22.come_ref = bf16[512,768]{1,0:T(8,128)(2,1)S(1)} collective-permute-done((bf16[512,768]{1,0:T(8,128)(2,1)S(1)}, bf16[512,768]{1,0:T(8,128)(2,1)S(1)}, u32[]{:S(2)}, u32[]{:S(2)}) %collective-permute-start.22) | collective-permute-done | bytes 786464 | tf_op jit(solution)/shard_map/ppermute | solution.py:271
  155.9 3.7 %collective-permute-start.23 = (bf16[128,768]{1,0:T(8,128)(2,1)S(1)}, bf16[128,768]{1,0:T(8,128)(2,1)S(1)}, u32[]{:S(2)}, u32[]{:S(2)}) collective-permute-start(bf16[128,768]{1,0:T(8,128)(2,1)S(1)} %get-tuple-element.121), channel_id=1, source_target_pairs={{0,12},{1,13},{2,14},{3,15},{4,0},{5,1},{6,2},{7,3},{8,4},{9,5},{1... | collective-permute-start | bytes 589832 | tf_op jit(solution)/shard_map/ppermute | solution.py:271
  159.5 4.7 %hidden_grads.4.refs_1_ = f32[1024,512]{1,0:T(8,128)S(1)} custom-call(bf16[512,768]{1,0:T(8,128)(2,1)} %collective-permute-done.10.other_down_ref.refs_0_, bf16[512,768]{1,0:T(8,128)(2,1)S(1)} %collective-permute-done.21.other_down_ref.refs_1_, bf16[128,2048]{1,0:T(8,128)(2,1)S(1)} %copy-done.5, bf16[128,2048]{1,0:T(8,128)(2,1)} %collective-permute-done.11.refs_3_.refs_4_, ...), custom_call_target="tpu_custom_call" | custom-call | flops 1 | bytes 1 | tf_op jit(solution)/shard_map/hidden_grads/pallas_call | solution.py:127
  164.3 1.6 mix_columns.5
  165.9 1.6 collective-permute-start.27
  167.6 2.8 %hidden_grads.5.other_ref = bf16[1024,1024]{1,0:T(8,128)(2,1)S(1)} custom-call(f32[1024,1024]{1,0:T(8,128)S(1)} %copy-done.6, f32[1024,512]{1,0:T(8,128)S(1)} %hidden_grads.4.refs_1_, bf16[512,512]{1,0:T(8,128)(2,1)S(1)} %collective-permute-done.26.other_down_ref.refs_2_, bf16[128,2048]{1,0:T(8,128)(2,1)S(1)} %copy-done.5, ...), custom_call_target="tpu_custom_call" | custom-call | flops 1 | bytes 1 | tf_op jit(solution)/shard_map/hidden_grads/pallas_call | solution.py:127
  170.7 6.7 %back_columns.3 = (f32[512,1024]{1,0:T(8,128)S(1)}, bf16[512,1024]{1,0:T(8,128)(2,1)S(1)}) custom-call(bf16[1024,1024]{1,0:T(8,128)(2,1)S(1)} %hidden_grads.3.own_ref, bf16[1024,1024]{1,0:T(8,128)(2,1)S(1)} %hidden_grads.5.other_ref, bf16[2,2048,256]{2,1,0:T(8,128)(2,1)S(1)} %copy-done.1, bf16[2,2048,256]{2,1,0:T(8,128)(2,1)S(1)} %copy-done.2, ...), custom_call_target="tpu_custom_call" | custom-call | flops 1 | bytes 1 | tf_op jit(solution)/shard_map/back_columns/pallas_call | solution.py:179
  177.4 1.1 collective-permute-start.31
  179.2 7.0 %collective-permute-done.25.refs_5_ = bf16[128,768]{1,0:T(8,128)(2,1)S(1)} collective-permute-done((bf16[128,768]{1,0:T(8,128)(2,1)S(1)}, bf16[128,768]{1,0:T(8,128)(2,1)S(1)}, u32[]{:S(2)}, u32[]{:S(2)}) %collective-permute-start.25) | collective-permute-done | bytes 196640 | tf_op jit(solution)/shard_map/ppermute | solution.py:271
  186.2 5.4 %back_columns.4 = (f32[512,768]{1,0:T(8,128)S(1)}, bf16[512,768]{1,0:T(8,128)(2,1)S(1)}) custom-call(bf16[1024,1024]{1,0:T(8,128)(2,1)S(1)} %hidden_grads.3.own_ref, bf16[1024,1024]{1,0:T(8,128)(2,1)S(1)} %hidden_grads.5.other_ref, bf16[2,2048,256]{2,1,0:T(8,128)(2,1)S(1)} %copy-done.1, bf16[2,2048,256]{2,1,0:T(8,128)(2,1)S(1)} %copy-done.2, ...), custom_call_target="tpu_custom_call" | custom-call | flops 1 | bytes 1 | tf_op jit(solution)/shard_map/back_columns/pallas_call | solution.py:179
  191.6 1.1 collective-permute-start.35
  192.8 3.8 %collective-permute-start.28 = (bf16[128,512]{1,0:T(8,128)(2,1)S(1)}, bf16[128,512]{1,0:T(8,128)(2,1)S(1)}, u32[]{:S(2)}, u32[]{:S(2)}) collective-permute-start(bf16[128,512]{1,0:T(8,128)(2,1)S(1)} %get-tuple-element.132), channel_id=1, source_target_pairs={{0,12},{1,13},{2,14},{3,15},{4,0},{5,1},{6,2},{7,3},{8,4},{9,5},{1... | collective-permute-start | bytes 393224 | tf_op jit(solution)/shard_map/ppermute | solution.py:271
  196.6 7.0 %collective-permute-done.31.come_ref = bf16[512,1024]{1,0:T(8,128)(2,1)S(1)} collective-permute-done((bf16[512,1024]{1,0:T(8,128)(2,1)S(1)}, bf16[512,1024]{1,0:T(8,128)(2,1)S(1)}, u32[]{:S(2)}, u32[]{:S(2)}) %collective-permute-start.31) | collective-permute-done | bytes 1048608 | tf_op jit(solution)/shard_map/ppermute | solution.py:271
  203.8 3.9 %collective-permute-start.32 = (bf16[128,1024]{1,0:T(8,128)(2,1)S(1)}, bf16[128,1024]{1,0:T(8,128)(2,1)S(1)}, u32[]{:S(2)}, u32[]{:S(2)}) collective-permute-start(bf16[128,1024]{1,0:T(8,128)(2,1)S(1)} %get-tuple-element.143), channel_id=1, source_target_pairs={{0,12},{1,13},{2,14},{3,15},{4,0},{5,1},{6,2},{7,3},{8,4},{9,5},{1... | collective-permute-start | bytes 786440 | tf_op jit(solution)/shard_map/ppermute | solution.py:271
  207.8 9.1 %collective-permute-done.30.refs_8_ = bf16[128,512]{1,0:T(8,128)(2,1)S(1)} collective-permute-done((bf16[128,512]{1,0:T(8,128)(2,1)S(1)}, bf16[128,512]{1,0:T(8,128)(2,1)S(1)}, u32[]{:S(2)}, u32[]{:S(2)}) %collective-permute-start.30) | collective-permute-done | bytes 131104 | tf_op jit(solution)/shard_map/ppermute | solution.py:271
  216.8 1.1 finish.2
  218.1 3.8 %collective-permute-start.36 = (bf16[128,768]{1,0:T(8,128)(2,1)S(1)}, bf16[128,768]{1,0:T(8,128)(2,1)S(1)}, u32[]{:S(2)}, u32[]{:S(2)}) collective-permute-start(bf16[128,768]{1,0:T(8,128)(2,1)S(1)} %get-tuple-element.155), channel_id=1, source_target_pairs={{0,12},{1,13},{2,14},{3,15},{4,0},{5,1},{6,2},{7,3},{8,4},{9,5},{1... | collective-permute-start | bytes 589832 | tf_op jit(solution)/shard_map/ppermute | solution.py:271
  221.9 2.6 %back_columns.5 = (f32[512,256]{1,0:T(8,128)S(1)}, bf16[512,256]{1,0:T(8,128)(2,1)S(1)}) custom-call(bf16[1024,1024]{1,0:T(8,128)(2,1)S(1)} %hidden_grads.3.own_ref, bf16[1024,1024]{1,0:T(8,128)(2,1)S(1)} %hidden_grads.5.other_ref, bf16[2,2048,256]{2,1,0:T(8,128)(2,1)S(1)} %copy-done.1, bf16[2,2048,256]{2,1,0:T(8,128)(2,1)S(1)} %copy-done.2, ...), custom_call_target="tpu_custom_call" | custom-call | flops 1 | bytes 1 | tf_op jit(solution)/shard_map/back_columns/pallas_call | solution.py:179
  225.3 2.3 collective-permute-done.37.come_ref
  228.1 2.0 collective-permute-start.38
  230.2 0.9 collective-permute-done.39.come_ref
  231.1 6.2 %collective-permute-done.34.refs_2_ = bf16[128,1024]{1,0:T(8,128)(2,1)S(1)} collective-permute-done((bf16[128,1024]{1,0:T(8,128)(2,1)S(1)}, bf16[128,1024]{1,0:T(8,128)(2,1)S(1)}, u32[]{:S(2)}, u32[]{:S(2)}) %collective-permute-start.34) | collective-permute-done | bytes 262176 | tf_op jit(solution)/shard_map/ppermute | solution.py:271
  237.4 3.7 %collective-permute-start.42 = (bf16[128,256]{1,0:T(8,128)(2,1)S(1)}, bf16[128,256]{1,0:T(8,128)(2,1)S(1)}, u32[]{:S(2)}, u32[]{:S(2)}) collective-permute-start(bf16[128,256]{1,0:T(8,128)(2,1)S(1)} %get-tuple-element.171), channel_id=1, source_target_pairs={{0,12},{1,13},{2,14},{3,15},{4,0},{5,1},{6,2},{7,3},{8,4},{9,5},{1... | collective-permute-start | bytes 196616 | tf_op jit(solution)/shard_map/ppermute | solution.py:271
  241.1 2.2 collective-permute-done.40.refs_7_
  244.1 1.1 finish.3
  (91 shorter events, 9.2 us)
Async XLA Ops:
  1.6 70.7 %copy-start.5 = (bf16[128,2048]{1,0:T(8,128)(2,1)S(1)}, bf16[128,2048]{1,0:T(8,128)(2,1)}, u32[]{:S(2)}) copy-start(bf16[128,2048]{1,0:T(8,128)(2,1)} %refs_3_.1) | copy-start | bytes 1572868
  2.9 71.6 %copy-start.8 = (bf16[128,2176]{1,0:T(8,128)(2,1)}, bf16[128,2176]{1,0:T(8,128)(2,1)S(1)}, u32[]{:S(2)}) copy-start(bf16[128,2176]{1,0:T(8,128)(2,1)S(1)} %concatenate.3.refs_0_) | copy-start | bytes 1671172
  2.9 69.4 %collective-permute-start.8 = (bf16[2,2048,256]{2,1,0:T(8,128)(2,1)}, bf16[2,2048,256]{2,1,0:T(8,128)(2,1)}, u32[]{:S(2)}, u32[]{:S(2)}) collective-permute-start(bf16[2,2048,256]{2,1,0:T(8,128)(2,1)} %refs_0_.5), channel_id=1, source_target_pairs={{0,1},{1,0},{2,3},{3,2},{4,5},{5,4},{6,7},{7,6},{8,9},{9,8},{10,11... | collective-permute-start | bytes 6291464 | tf_op jit(solution)/shard_map/ppermute | solution.py:271
  5.9 16.7 %collective-permute-start = (bf16[128,2176]{1,0:T(8,128)(2,1)S(1)}, bf16[128,2176]{1,0:T(8,128)(2,1)S(1)}, u32[]{:S(2)}, u32[]{:S(2)}) collective-permute-start(bf16[128,2176]{1,0:T(8,128)(2,1)S(1)} %concatenate.3.refs_0_), channel_id=1, source_target_pairs={{0,12},{1,13},{2,14},{3,15},{4,0},{5,1},{6,2},{7,3},{8,4},{9,5},{1... | collective-permute-start | bytes 1671176 | tf_op jit(solution)/shard_map/ppermute | solution.py:271
  9.5 15.6 %collective-permute-start.1 = (bf16[128,2176]{1,0:T(8,128)(2,1)S(1)}, bf16[128,2176]{1,0:T(8,128)(2,1)S(1)}, u32[]{:S(2)}, u32[]{:S(2)}) collective-permute-start(bf16[128,2176]{1,0:T(8,128)(2,1)S(1)} %concatenate.3.refs_0_), channel_id=1, source_target_pairs={{0,2},{1,3},{2,0},{3,1},{4,6},{5,7},{6,4},{7,5},{8,10},{9,11},{10,... | collective-permute-start | bytes 1671176 | tf_op jit(solution)/shard_map/ppermute | solution.py:271
  11.0 25.3 %collective-permute-start.3 = (bf16[128,2176]{1,0:T(8,128)(2,1)S(1)}, bf16[128,2176]{1,0:T(8,128)(2,1)S(1)}, u32[]{:S(2)}, u32[]{:S(2)}) collective-permute-start(bf16[128,2176]{1,0:T(8,128)(2,1)S(1)} %concatenate.3.refs_0_), channel_id=1, source_target_pairs={{0,4},{1,5},{2,6},{3,7},{4,8},{5,9},{6,10},{7,11},{8,12},{9,13},{1... | collective-permute-start | bytes 1671176 | tf_op jit(solution)/shard_map/ppermute | solution.py:271
  11.0 25.3 %collective-permute-start.6 = (bf16[128,2048]{1,0:T(8,128)(2,1)}, bf16[128,2048]{1,0:T(8,128)(2,1)S(1)}, u32[]{:S(2)}, u32[]{:S(2)}) collective-permute-start(bf16[128,2048]{1,0:T(8,128)(2,1)} %refs_3_.1), channel_id=1, source_target_pairs={{0,2},{1,3},{2,0},{3,1},{4,6},{5,7},{6,4},{7,5},{8,10},{9,11},{10,... | collective-permute-start | bytes 1572872 | tf_op jit(solution)/shard_map/ppermute | solution.py:271
  22.6 52.0 %copy-start.9 = (bf16[128,2176]{1,0:T(8,128)(2,1)}, bf16[128,2176]{1,0:T(8,128)(2,1)S(1)}, u32[]{:S(2)}) copy-start(bf16[128,2176]{1,0:T(8,128)(2,1)S(1)} %collective-permute-done.refs_1_) | copy-start | bytes 1671172
  25.1 49.5 %copy-start.10 = (bf16[128,2176]{1,0:T(8,128)(2,1)}, bf16[128,2176]{1,0:T(8,128)(2,1)S(1)}, u32[]{:S(2)}) copy-start(bf16[128,2176]{1,0:T(8,128)(2,1)S(1)} %collective-permute-done.1.refs_4_) | copy-start | bytes 1671172
  25.1 23.2 %collective-permute-start.4 = (bf16[128,2176]{1,0:T(8,128)(2,1)S(1)}, bf16[128,2176]{1,0:T(8,128)(2,1)S(1)}, u32[]{:S(2)}, u32[]{:S(2)}) collective-permute-start(bf16[128,2176]{1,0:T(8,128)(2,1)S(1)} %collective-permute-done.refs_1_), channel_id=1, source_target_pairs={{0,2},{1,3},{2,0},{3,1},{4,6},{5,7},{6,4},{7,5},{8,10},{9,11},{10,... | collective-permute-start | bytes 1671176 | tf_op jit(solution)/shard_map/ppermute | solution.py:271
  26.6 21.7 %collective-permute-start.2 = (bf16[128,2176]{1,0:T(8,128)(2,1)S(1)}, bf16[128,2176]{1,0:T(8,128)(2,1)S(1)}, u32[]{:S(2)}, u32[]{:S(2)}) collective-permute-start(bf16[128,2176]{1,0:T(8,128)(2,1)S(1)} %collective-permute-done.refs_1_), channel_id=1, source_target_pairs={{0,12},{1,13},{2,14},{3,15},{4,0},{5,1},{6,2},{7,3},{8,4},{9,5},{1... | collective-permute-start | bytes 1671176 | tf_op jit(solution)/shard_map/ppermute | solution.py:271
  36.3 36.0 %copy-start.11 = (bf16[128,2176]{1,0:T(8,128)(2,1)}, bf16[128,2176]{1,0:T(8,128)(2,1)S(1)}, u32[]{:S(2)}) copy-start(bf16[128,2176]{1,0:T(8,128)(2,1)S(1)} %collective-permute-done.3.refs_3_) | copy-start | bytes 1671172
  36.3 61.3 %collective-permute-start.9 = (bf16[2,2048,256]{2,1,0:T(8,128)(2,1)}, bf16[2,2048,256]{2,1,0:T(8,128)(2,1)}, u32[]{:S(2)}, u32[]{:S(2)}) collective-permute-start(bf16[2,2048,256]{2,1,0:T(8,128)(2,1)} %refs_1_.5), channel_id=1, source_target_pairs={{0,1},{1,0},{2,3},{3,2},{4,5},{5,4},{6,7},{7,6},{8,9},{9,8},{10,11... | collective-permute-start | bytes 6291464 | tf_op jit(solution)/shard_map/ppermute | solution.py:271
  36.8 23.3 %collective-permute-start.7 = (bf16[128,2176]{1,0:T(8,128)(2,1)S(1)}, bf16[128,2176]{1,0:T(8,128)(2,1)S(1)}, u32[]{:S(2)}, u32[]{:S(2)}) collective-permute-start(bf16[128,2176]{1,0:T(8,128)(2,1)S(1)} %collective-permute-done.3.refs_3_), channel_id=1, source_target_pairs={{0,2},{1,3},{2,0},{3,1},{4,6},{5,7},{6,4},{7,5},{8,10},{9,11},{10,... | collective-permute-start | bytes 1671176 | tf_op jit(solution)/shard_map/ppermute | solution.py:271
  48.2 0.8 copy-start.12
  49.0 23.3 %copy-start.13 = (bf16[128,2176]{1,0:T(8,128)(2,1)}, bf16[128,2176]{1,0:T(8,128)(2,1)S(1)}, u32[]{:S(2)}) copy-start(bf16[128,2176]{1,0:T(8,128)(2,1)S(1)} %collective-permute-done.2.refs_2_) | copy-start | bytes 1671172
  49.0 21.3 %collective-permute-start.5 = (bf16[128,2176]{1,0:T(8,128)(2,1)S(1)}, bf16[128,2176]{1,0:T(8,128)(2,1)S(1)}, u32[]{:S(2)}, u32[]{:S(2)}) collective-permute-start(bf16[128,2176]{1,0:T(8,128)(2,1)S(1)} %collective-permute-done.2.refs_2_), channel_id=1, source_target_pairs={{0,2},{1,3},{2,0},{3,1},{4,6},{5,7},{6,4},{7,5},{8,10},{9,11},{10,... | collective-permute-start | bytes 1671176 | tf_op jit(solution)/shard_map/ppermute | solution.py:271
  50.6 10.9 %collective-permute-start.11 = (bf16[128,2048]{1,0:T(8,128)(2,1)}, bf16[128,2048]{1,0:T(8,128)(2,1)}, u32[]{:S(2)}, u32[]{:S(2)}) collective-permute-start(bf16[128,2048]{1,0:T(8,128)(2,1)} %refs_3_.1), channel_id=1, source_target_pairs={{0,12},{1,13},{2,14},{3,15},{4,0},{5,1},{6,2},{7,3},{8,4},{9,5},{1... | collective-permute-start | bytes 1572872 | tf_op jit(solution)/shard_map/ppermute | solution.py:271
  60.2 13.8 %copy-start.14 = (bf16[128,2176]{1,0:T(8,128)(2,1)}, bf16[128,2176]{1,0:T(8,128)(2,1)S(1)}, u32[]{:S(2)}) copy-start(bf16[128,2176]{1,0:T(8,128)(2,1)S(1)} %collective-permute-done.7.refs_7_) | copy-start | bytes 1671172
  70.3 4.2 %copy-start.15 = (bf16[128,2176]{1,0:T(8,128)(2,1)}, bf16[128,2176]{1,0:T(8,128)(2,1)S(1)}, u32[]{:S(2)}) copy-start(bf16[128,2176]{1,0:T(8,128)(2,1)S(1)} %collective-permute-done.5.refs_6_) | copy-start | bytes 1671172
  70.4 23.8 %collective-permute-start.15 = (bf16[128,2048]{1,0:T(8,128)(2,1)}, bf16[128,2048]{1,0:T(8,128)(2,1)}, u32[]{:S(2)}, u32[]{:S(2)}) collective-permute-start(bf16[128,2048]{1,0:T(8,128)(2,1)} %collective-permute-done.11.refs_3_.refs_4_), channel_id=1, source_target_pairs={{0,12},{1,13},{2,14},{3,15},{4,0},{5,1},{6,2},{7,3},{8,4},{9,5},{1... | collective-permute-start | bytes 1572872 | tf_op jit(solution)/shard_map/ppermute | solution.py:271
  70.8 23.4 %collective-permute-start.12 = (bf16[128,2048]{1,0:T(8,128)(2,1)}, bf16[128,2048]{1,0:T(8,128)(2,1)}, u32[]{:S(2)}, u32[]{:S(2)}) collective-permute-start(bf16[128,2048]{1,0:T(8,128)(2,1)} %collective-permute-done.11.refs_3_.refs_4_), channel_id=1, source_target_pairs={{0,2},{1,3},{2,0},{3,1},{4,6},{5,7},{6,4},{7,5},{8,10},{9,11},{10,... | collective-permute-start | bytes 1572872 | tf_op jit(solution)/shard_map/ppermute | solution.py:271
  72.3 23.4 %collective-permute-start.13 = (bf16[128,2048]{1,0:T(8,128)(2,1)S(1)}, bf16[128,2048]{1,0:T(8,128)(2,1)}, u32[]{:S(2)}, u32[]{:S(2)}) collective-permute-start(bf16[128,2048]{1,0:T(8,128)(2,1)S(1)} %copy-done.5), channel_id=1, source_target_pairs={{0,4},{1,5},{2,6},{3,7},{4,8},{5,9},{6,10},{7,11},{8,12},{9,13},{1... | collective-permute-start | bytes 1572872 | tf_op jit(solution)/shard_map/ppermute | solution.py:271
  74.0 39.7 %collective-permute-start.10 = (bf16[512,768]{1,0:T(8,128)(2,1)}, bf16[512,768]{1,0:T(8,128)(2,1)}, u32[]{:S(2)}, u32[]{:S(2)}) collective-permute-start(bf16[512,768]{1,0:T(8,128)(2,1)} %get-tuple-element.99), channel_id=1, source_target_pairs={{0,1},{1,0},{2,3},{3,2},{4,5},{5,4},{6,7},{7,6},{8,9},{9,8},{10,11... | collective-permute-start | bytes 2359304 | tf_op jit(solution)/shard_map/ppermute | solution.py:271
  74.5 21.7 %copy-start = (bf16[2,256,2048]{2,1,0:T(8,128)(2,1)S(1)}, bf16[2,256,2048]{2,1,0:T(8,128)(2,1)}, u32[]{:S(2)}) copy-start(bf16[2,256,2048]{2,1,0:T(8,128)(2,1)} %param.13) | copy-start | bytes 6291460
  94.2 21.2 %collective-permute-start.16 = (bf16[128,2048]{1,0:T(8,128)(2,1)}, bf16[128,2048]{1,0:T(8,128)(2,1)}, u32[]{:S(2)}, u32[]{:S(2)}) collective-permute-start(bf16[128,2048]{1,0:T(8,128)(2,1)} %collective-permute-done.15.refs_4_.refs_5_), channel_id=1, source_target_pairs={{0,2},{1,3},{2,0},{3,1},{4,6},{5,7},{6,4},{7,5},{8,10},{9,11},{10,... | collective-permute-start | bytes 1572872 | tf_op jit(solution)/shard_map/ppermute | solution.py:271
  95.7 19.7 %collective-permute-start.14 = (bf16[128,2048]{1,0:T(8,128)(2,1)}, bf16[128,2048]{1,0:T(8,128)(2,1)}, u32[]{:S(2)}, u32[]{:S(2)}) collective-permute-start(bf16[128,2048]{1,0:T(8,128)(2,1)} %collective-permute-done.13.refs_5_.refs_6_), channel_id=1, source_target_pairs={{0,2},{1,3},{2,0},{3,1},{4,6},{5,7},{6,4},{7,5},{8,10},{9,11},{10,... | collective-permute-start | bytes 1572872 | tf_op jit(solution)/shard_map/ppermute | solution.py:271
  97.6 16.0 %copy-start.16 = (bf16[512,768]{1,0:T(8,128)(2,1)S(1)}, bf16[512,768]{1,0:T(8,128)(2,1)}, u32[]{:S(2)}) copy-start(bf16[512,768]{1,0:T(8,128)(2,1)} %get-tuple-element.114) | copy-start | bytes 2359300
  97.6 17.8 %copy-start.3 = (bf16[1024,512]{1,0:T(8,128)(2,1)S(1)}, bf16[1024,512]{1,0:T(8,128)(2,1)}, u32[]{:S(2)}) copy-start(bf16[1024,512]{1,0:T(8,128)(2,1)} %get-tuple-element.94.own_ref) | copy-start | bytes 3145732
  113.6 18.7 %collective-permute-start.21 = (bf16[512,768]{1,0:T(8,128)(2,1)S(1)}, bf16[512,768]{1,0:T(8,128)(2,1)S(1)}, u32[]{:S(2)}, u32[]{:S(2)}) collective-permute-start(bf16[512,768]{1,0:T(8,128)(2,1)S(1)} %copy-done.16), channel_id=1, source_target_pairs={{0,1},{1,0},{2,3},{3,2},{4,5},{5,4},{6,7},{7,6},{8,9},{9,8},{10,11... | collective-permute-start | bytes 2359304 | tf_op jit(solution)/shard_map/ppermute | solution.py:271
  115.4 1.2 copy-start.4
  116.6 5.1 %copy-start.7 = (f32[1024,1024]{1,0:T(8,128)S(1)}, f32[1024,1024]{1,0:T(8,128)}, u32[]{:S(2)}) copy-start(f32[1024,1024]{1,0:T(8,128)} %get-tuple-element.118.refs_0_) | copy-start | bytes 12582916
  120.1 18.2 %collective-permute-start.17 = (bf16[512,768]{1,0:T(8,128)(2,1)S(1)}, bf16[512,768]{1,0:T(8,128)(2,1)S(1)}, u32[]{:S(2)}, u32[]{:S(2)}) collective-permute-start(bf16[512,768]{1,0:T(8,128)(2,1)S(1)} %get-tuple-element.108), channel_id=1, source_target_pairs={{0,2},{1,3},{2,0},{3,1},{4,6},{5,7},{6,4},{7,5},{8,10},{9,11},{10,... | collective-permute-start | bytes 2359304 | tf_op jit(solution)/shard_map/ppermute | solution.py:271
  134.6 5.5 %copy-start.17 = (bf16[512,512]{1,0:T(8,128)(2,1)S(1)}, bf16[512,512]{1,0:T(8,128)(2,1)}, u32[]{:S(2)}) copy-start(bf16[512,512]{1,0:T(8,128)(2,1)} %slice.13) | copy-start | bytes 1572868
  138.5 17.3 %collective-permute-start.22 = (bf16[512,768]{1,0:T(8,128)(2,1)S(1)}, bf16[512,768]{1,0:T(8,128)(2,1)S(1)}, u32[]{:S(2)}, u32[]{:S(2)}) collective-permute-start(bf16[512,768]{1,0:T(8,128)(2,1)S(1)} %get-tuple-element.119), channel_id=1, source_target_pairs={{0,2},{1,3},{2,0},{3,1},{4,6},{5,7},{6,4},{7,5},{8,10},{9,11},{10,... | collective-permute-start | bytes 2359304 | tf_op jit(solution)/shard_map/ppermute | solution.py:271
  140.0 24.2 %collective-permute-start.26 = (bf16[512,512]{1,0:T(8,128)(2,1)S(1)}, bf16[512,512]{1,0:T(8,128)(2,1)S(1)}, u32[]{:S(2)}, u32[]{:S(2)}) collective-permute-start(bf16[512,512]{1,0:T(8,128)(2,1)S(1)} %copy-done.17), channel_id=1, source_target_pairs={{0,1},{1,0},{2,3},{3,2},{4,5},{5,4},{6,7},{7,6},{8,9},{9,8},{10,11... | collective-permute-start | bytes 1572872 | tf_op jit(solution)/shard_map/ppermute | solution.py:271
  140.6 8.1 %collective-permute-start.19 = (bf16[128,768]{1,0:T(8,128)(2,1)S(1)}, bf16[128,768]{1,0:T(8,128)(2,1)S(1)}, u32[]{:S(2)}, u32[]{:S(2)}) collective-permute-start(bf16[128,768]{1,0:T(8,128)(2,1)S(1)} %get-tuple-element.112), channel_id=1, source_target_pairs={{0,4},{1,5},{2,6},{3,7},{4,8},{5,9},{6,10},{7,11},{8,12},{9,13},{1... | collective-permute-start | bytes 589832 | tf_op jit(solution)/shard_map/ppermute | solution.py:271
  142.2 7.9 %collective-permute-start.18 = (bf16[128,768]{1,0:T(8,128)(2,1)S(1)}, bf16[128,768]{1,0:T(8,128)(2,1)S(1)}, u32[]{:S(2)}, u32[]{:S(2)}) collective-permute-start(bf16[128,768]{1,0:T(8,128)(2,1)S(1)} %get-tuple-element.110), channel_id=1, source_target_pairs={{0,12},{1,13},{2,14},{3,15},{4,0},{5,1},{6,2},{7,3},{8,4},{9,5},{1... | collective-permute-start | bytes 589832 | tf_op jit(solution)/shard_map/ppermute | solution.py:271
  150.1 14.2 %collective-permute-start.20 = (bf16[128,768]{1,0:T(8,128)(2,1)S(1)}, bf16[128,768]{1,0:T(8,128)(2,1)S(1)}, u32[]{:S(2)}, u32[]{:S(2)}) collective-permute-start(bf16[128,768]{1,0:T(8,128)(2,1)S(1)} %add_piece.5), channel_id=1, source_target_pairs={{0,4},{1,5},{2,6},{3,7},{4,8},{5,9},{6,10},{7,11},{8,12},{9,13},{1... | collective-permute-start | bytes 589832 | tf_op jit(solution)/shard_map/ppermute | solution.py:271
  155.9 11.6 %collective-permute-start.23 = (bf16[128,768]{1,0:T(8,128)(2,1)S(1)}, bf16[128,768]{1,0:T(8,128)(2,1)S(1)}, u32[]{:S(2)}, u32[]{:S(2)}) collective-permute-start(bf16[128,768]{1,0:T(8,128)(2,1)S(1)} %get-tuple-element.121), channel_id=1, source_target_pairs={{0,12},{1,13},{2,14},{3,15},{4,0},{5,1},{6,2},{7,3},{8,4},{9,5},{1... | collective-permute-start | bytes 589832 | tf_op jit(solution)/shard_map/ppermute | solution.py:271
  159.5 8.0 %collective-permute-start.24 = (bf16[128,768]{1,0:T(8,128)(2,1)S(1)}, bf16[128,768]{1,0:T(8,128)(2,1)S(1)}, u32[]{:S(2)}, u32[]{:S(2)}) collective-permute-start(bf16[128,768]{1,0:T(8,128)(2,1)S(1)} %get-tuple-element.123), channel_id=1, source_target_pairs={{0,4},{1,5},{2,6},{3,7},{4,8},{5,9},{6,10},{7,11},{8,12},{9,13},{1... | collective-permute-start | bytes 589832 | tf_op jit(solution)/shard_map/ppermute | solution.py:271
  164.3 3.3 %copy-start.6 = (f32[1024,1024]{1,0:T(8,128)S(1)}, f32[1024,1024]{1,0:T(8,128)}, u32[]{:S(2)}) copy-start(f32[1024,1024]{1,0:T(8,128)} %get-tuple-element.138.refs_0_) | copy-start | bytes 12582916
  165.9 25.6 %collective-permute-start.27 = (bf16[512,512]{1,0:T(8,128)(2,1)S(1)}, bf16[512,512]{1,0:T(8,128)(2,1)S(1)}, u32[]{:S(2)}, u32[]{:S(2)}) collective-permute-start(bf16[512,512]{1,0:T(8,128)(2,1)S(1)} %get-tuple-element.129), channel_id=1, source_target_pairs={{0,2},{1,3},{2,0},{3,1},{4,6},{5,7},{6,4},{7,5},{8,10},{9,11},{10,... | collective-permute-start | bytes 1572872 | tf_op jit(solution)/shard_map/ppermute | solution.py:271
  167.5 2.8 %copy-start.1 = (bf16[2,2048,256]{2,1,0:T(8,128)(2,1)S(1)}, bf16[2,2048,256]{2,1,0:T(8,128)(2,1)}, u32[]{:S(2)}) copy-start(bf16[2,2048,256]{2,1,0:T(8,128)(2,1)} %refs_0_.5) | copy-start | bytes 6291460
  167.5 3.2 %copy-start.2 = (bf16[2,2048,256]{2,1,0:T(8,128)(2,1)S(1)}, bf16[2,2048,256]{2,1,0:T(8,128)(2,1)}, u32[]{:S(2)}) copy-start(bf16[2,2048,256]{2,1,0:T(8,128)(2,1)} %refs_1_.5) | copy-start | bytes 6291460
  177.4 26.2 %collective-permute-start.31 = (bf16[512,1024]{1,0:T(8,128)(2,1)S(1)}, bf16[512,1024]{1,0:T(8,128)(2,1)S(1)}, u32[]{:S(2)}, u32[]{:S(2)}) collective-permute-start(bf16[512,1024]{1,0:T(8,128)(2,1)S(1)} %get-tuple-element.140), channel_id=1, source_target_pairs={{0,2},{1,3},{2,0},{3,1},{4,6},{5,7},{6,4},{7,5},{8,10},{9,11},{10,... | collective-permute-start | bytes 3145736 | tf_op jit(solution)/shard_map/ppermute | solution.py:271
  178.5 7.7 %collective-permute-start.25 = (bf16[128,768]{1,0:T(8,128)(2,1)S(1)}, bf16[128,768]{1,0:T(8,128)(2,1)S(1)}, u32[]{:S(2)}, u32[]{:S(2)}) collective-permute-start(bf16[128,768]{1,0:T(8,128)(2,1)S(1)} %add_piece.6), channel_id=1, source_target_pairs={{0,4},{1,5},{2,6},{3,7},{4,8},{5,9},{6,10},{7,11},{8,12},{9,13},{1... | collective-permute-start | bytes 589832 | tf_op jit(solution)/shard_map/ppermute | solution.py:271
  191.6 26.3 %collective-permute-start.35 = (bf16[512,768]{1,0:T(8,128)(2,1)S(1)}, bf16[512,768]{1,0:T(8,128)(2,1)S(1)}, u32[]{:S(2)}, u32[]{:S(2)}) collective-permute-start(bf16[512,768]{1,0:T(8,128)(2,1)S(1)} %get-tuple-element.151), channel_id=1, source_target_pairs={{0,2},{1,3},{2,0},{3,1},{4,6},{5,7},{6,4},{7,5},{8,10},{9,11},{10,... | collective-permute-start | bytes 2359304 | tf_op jit(solution)/shard_map/ppermute | solution.py:271
  192.8 14.9 %collective-permute-start.29 = (bf16[128,512]{1,0:T(8,128)(2,1)S(1)}, bf16[128,512]{1,0:T(8,128)(2,1)S(1)}, u32[]{:S(2)}, u32[]{:S(2)}) collective-permute-start(bf16[128,512]{1,0:T(8,128)(2,1)S(1)} %get-tuple-element.135), channel_id=1, source_target_pairs={{0,4},{1,5},{2,6},{3,7},{4,8},{5,9},{6,10},{7,11},{8,12},{9,13},{1... | collective-permute-start | bytes 393224 | tf_op jit(solution)/shard_map/ppermute | solution.py:271
  192.8 14.9 %collective-permute-start.28 = (bf16[128,512]{1,0:T(8,128)(2,1)S(1)}, bf16[128,512]{1,0:T(8,128)(2,1)S(1)}, u32[]{:S(2)}, u32[]{:S(2)}) collective-permute-start(bf16[128,512]{1,0:T(8,128)(2,1)S(1)} %get-tuple-element.132), channel_id=1, source_target_pairs={{0,12},{1,13},{2,14},{3,15},{4,0},{5,1},{6,2},{7,3},{8,4},{9,5},{1... | collective-permute-start | bytes 393224 | tf_op jit(solution)/shard_map/ppermute | solution.py:271
  203.7 21.4 %collective-permute-start.33 = (bf16[128,1024]{1,0:T(8,128)(2,1)S(1)}, bf16[128,1024]{1,0:T(8,128)(2,1)S(1)}, u32[]{:S(2)}, u32[]{:S(2)}) collective-permute-start(bf16[128,1024]{1,0:T(8,128)(2,1)S(1)} %get-tuple-element.146), channel_id=1, source_target_pairs={{0,4},{1,5},{2,6},{3,7},{4,8},{5,9},{6,10},{7,11},{8,12},{9,13},{1... | collective-permute-start | bytes 786440 | tf_op jit(solution)/shard_map/ppermute | solution.py:271
  203.8 21.4 %collective-permute-start.32 = (bf16[128,1024]{1,0:T(8,128)(2,1)S(1)}, bf16[128,1024]{1,0:T(8,128)(2,1)S(1)}, u32[]{:S(2)}, u32[]{:S(2)}) collective-permute-start(bf16[128,1024]{1,0:T(8,128)(2,1)S(1)} %get-tuple-element.143), channel_id=1, source_target_pairs={{0,12},{1,13},{2,14},{3,15},{4,0},{5,1},{6,2},{7,3},{8,4},{9,5},{1... | collective-permute-start | bytes 786440 | tf_op jit(solution)/shard_map/ppermute | solution.py:271
  207.7 9.1 %collective-permute-start.30 = (bf16[128,512]{1,0:T(8,128)(2,1)S(1)}, bf16[128,512]{1,0:T(8,128)(2,1)S(1)}, u32[]{:S(2)}, u32[]{:S(2)}) collective-permute-start(bf16[128,512]{1,0:T(8,128)(2,1)S(1)} %add_piece.7), channel_id=1, source_target_pairs={{0,4},{1,5},{2,6},{3,7},{4,8},{5,9},{6,10},{7,11},{8,12},{9,13},{1... | collective-permute-start | bytes 393224 | tf_op jit(solution)/shard_map/ppermute | solution.py:271
  218.1 9.5 %collective-permute-start.37 = (bf16[128,768]{1,0:T(8,128)(2,1)S(1)}, bf16[128,768]{1,0:T(8,128)(2,1)S(1)}, u32[]{:S(2)}, u32[]{:S(2)}) collective-permute-start(bf16[128,768]{1,0:T(8,128)(2,1)S(1)} %get-tuple-element.158), channel_id=1, source_target_pairs={{0,4},{1,5},{2,6},{3,7},{4,8},{5,9},{6,10},{7,11},{8,12},{9,13},{1... | collective-permute-start | bytes 589832 | tf_op jit(solution)/shard_map/ppermute | solution.py:271
  218.1 10.0 %collective-permute-start.36 = (bf16[128,768]{1,0:T(8,128)(2,1)S(1)}, bf16[128,768]{1,0:T(8,128)(2,1)S(1)}, u32[]{:S(2)}, u32[]{:S(2)}) collective-permute-start(bf16[128,768]{1,0:T(8,128)(2,1)S(1)} %get-tuple-element.155), channel_id=1, source_target_pairs={{0,12},{1,13},{2,14},{3,15},{4,0},{5,1},{6,2},{7,3},{8,4},{9,5},{1... | collective-permute-start | bytes 589832 | tf_op jit(solution)/shard_map/ppermute | solution.py:271
  224.6 6.4 %collective-permute-start.39 = (bf16[512,256]{1,0:T(8,128)(2,1)S(1)}, bf16[512,256]{1,0:T(8,128)(2,1)S(1)}, u32[]{:S(2)}, u32[]{:S(2)}) collective-permute-start(bf16[512,256]{1,0:T(8,128)(2,1)S(1)} %get-tuple-element.163), channel_id=1, source_target_pairs={{0,2},{1,3},{2,0},{3,1},{4,6},{5,7},{6,4},{7,5},{8,10},{9,11},{10,... | collective-permute-start | bytes 786440 | tf_op jit(solution)/shard_map/ppermute | solution.py:271
  225.2 12.1 %collective-permute-start.34 = (bf16[128,1024]{1,0:T(8,128)(2,1)S(1)}, bf16[128,1024]{1,0:T(8,128)(2,1)S(1)}, u32[]{:S(2)}, u32[]{:S(2)}) collective-permute-start(bf16[128,1024]{1,0:T(8,128)(2,1)S(1)} %add_piece.8), channel_id=1, source_target_pairs={{0,4},{1,5},{2,6},{3,7},{4,8},{5,9},{6,10},{7,11},{8,12},{9,13},{1... | collective-permute-start | bytes 786440 | tf_op jit(solution)/shard_map/ppermute | solution.py:271
  228.1 13.0 %collective-permute-start.38 = (bf16[128,768]{1,0:T(8,128)(2,1)S(1)}, bf16[128,768]{1,0:T(8,128)(2,1)S(1)}, u32[]{:S(2)}, u32[]{:S(2)}) collective-permute-start(bf16[128,768]{1,0:T(8,128)(2,1)S(1)} %add_piece.9), channel_id=1, source_target_pairs={{0,4},{1,5},{2,6},{3,7},{4,8},{5,9},{6,10},{7,11},{8,12},{9,13},{1... | collective-permute-start | bytes 589832 | tf_op jit(solution)/shard_map/ppermute | solution.py:271
  237.3 6.1 %collective-permute-start.40 = (bf16[128,256]{1,0:T(8,128)(2,1)S(1)}, bf16[128,256]{1,0:T(8,128)(2,1)S(1)}, u32[]{:S(2)}, u32[]{:S(2)}) collective-permute-start(bf16[128,256]{1,0:T(8,128)(2,1)S(1)} %get-tuple-element.169), channel_id=1, source_target_pairs={{0,4},{1,5},{2,6},{3,7},{4,8},{5,9},{6,10},{7,11},{8,12},{9,13},{1... | collective-permute-start | bytes 196616 | tf_op jit(solution)/shard_map/ppermute | solution.py:271
  237.3 6.1 %collective-permute-start.41 = (bf16[128,256]{1,0:T(8,128)(2,1)S(1)}, bf16[128,256]{1,0:T(8,128)(2,1)S(1)}, u32[]{:S(2)}, u32[]{:S(2)}) collective-permute-start(bf16[128,256]{1,0:T(8,128)(2,1)S(1)} %get-tuple-element.170), channel_id=1, source_target_pairs={{0,8},{1,9},{2,10},{3,11},{4,12},{5,13},{6,14},{7,15},{8,0},{9,1},... | collective-permute-start | bytes 196616 | tf_op jit(solution)/shard_map/ppermute | solution.py:271
  237.4 6.7 %collective-permute-start.42 = (bf16[128,256]{1,0:T(8,128)(2,1)S(1)}, bf16[128,256]{1,0:T(8,128)(2,1)S(1)}, u32[]{:S(2)}, u32[]{:S(2)}) collective-permute-start(bf16[128,256]{1,0:T(8,128)(2,1)S(1)} %get-tuple-element.171), channel_id=1, source_target_pairs={{0,12},{1,13},{2,14},{3,15},{4,0},{5,1},{6,2},{7,3},{8,4},{9,5},{1... | collective-permute-start | bytes 196616 | tf_op jit(solution)/shard_map/ppermute | solution.py:271

commit v8 on v7

--- a/solution.py
+++ b/solution.py
@@ -235,6 +235,46 @@
     )(piece, come)
 
 
+def pair_kernel(keep_ref, send_ref, own_ref, side_ref, *piece_refs):
+    block = own_ref.shape[0]
+    own_ref[...] = keep_ref[:block, :]
+    side_ref[...] = send_ref[:block, :].astype(side_ref.dtype)
+    for k, piece_ref in enumerate(piece_refs, 1):
+        cut = slice(k * block, (k + 1) * block)
+        piece_ref[:block, :] = keep_ref[cut, :].astype(piece_ref.dtype)
+        piece_ref[block:, :] = send_ref[cut, :].astype(piece_ref.dtype)
+
+
+def pair_sides(keep, send, types):
+    block, columns = keep.shape[0] // len(types), keep.shape[1]
+    pieces = [jax.ShapeDtypeStruct((2 * block, columns), t) for t in types[1:]]
+    return pl.pallas_call(
+        pair_kernel,
+        out_shape=[jax.ShapeDtypeStruct((block, columns), jnp.float32)] * 2 + pieces,
+        compiler_params=compiler_params(),
+        cost_estimate=AT_ONCE,
+        name="pair_sides",
+    )(keep, send)
+
+
+def parts_kernel(side_ref, *refs):
+    block = side_ref.shape[0]
+    total = side_ref[...]
+    for part_ref in refs[:-1]:
+        total += part_ref[block:, :].astype(jnp.float32)
+    refs[-1][...] = total.astype(refs[-1].dtype)
+
+
+def add_parts(side, *parts):
+    return pl.pallas_call(
+        parts_kernel,
+        out_shape=jax.ShapeDtypeStruct(side.shape, jnp.bfloat16),
+        compiler_params=compiler_params(),
+        cost_estimate=AT_ONCE,
+        name="add_parts",
+    )(side, *parts)
+
+
 def finish_kernel(chunks, counts, *refs):
     out_ref = refs[-1]
     refs = list(refs[:-1])
@@ -243,7 +283,7 @@
         del refs[:count]
         total = own_ref[...]
         for piece_ref in piece_refs:
-            total += piece_ref[...].astype(jnp.float32)
+            total += piece_ref[: total.shape[0], :].astype(jnp.float32)
         out_ref[:, lo:hi] = total
 
 
@@ -277,8 +317,8 @@
     layers = devices // 4
     experts = local_count * devices
     block = tokens.shape[0]
-    chunks = cut_columns(width, ((0, 3), (3, 6), (6, 8)))
-    back_chunks = cut_columns(width, ((4, 8), (0, 3), (3, 4)))
+    chunks = cut_columns(width, ((0, 4), (4, 8)))
+    back_chunks = cut_columns(width, ((6, 8), (0, 4), (4, 6)))
     me = lax.axis_index("expert")
     twin = [(d, d ^ 1) for d in range(devices)]
     side = [(d, d ^ 2) for d in range(devices)]
@@ -335,60 +375,52 @@
             (come,) = send_all([(piece, layer[one])], *waits)
         return far, come
 
-    def send_last(pieces, come, far):
+    def send_last(pieces, come, *waits):
         piece = pieces[0].astype(jnp.bfloat16) if come is None else add_piece(pieces[0], come)
-        return send_all([(piece, layer[one])], far)[0]
+        return send_all([(piece, layer[one])], *waits)[0]
 
     keep_0, send = mix(0, down_0, other_activ, *far_grads.values())
-    come_0, down_2 = send_all([(send, side), (downs[2], twin)], far_grads[last])
+    (come_0,) = send_all([(send, side)])
     grad_blocks = [grads[k] for k in range(layers)] + [far_grads[k] for k in range(layers)]
     own_grads = hidden_grads(grad_blocks, [down], [(0, width)], by=by)
 
     keep_1, send = mix(1, down_1, send)
-    own_0, *pieces = add_sides(keep_0, come_0, types)
-    (come_1,) = send_all([(send, side)], own_0, own_grads)
-    far_0, next_0 = send_on(pieces)
-    near_0 = send_last(pieces, next_0, far_0)
-    other_grad = hidden_grads(grad_blocks, [down_0, down_1], chunks[:2])
-
-    keep_2, send = mix(2, down_2, send, other_grad, near_0)
-    own_1, *pieces = add_sides(keep_1, come_1, types)
-    (come_2,) = send_all([(send, side)], own_1)
-    far_1, next_1 = send_on(pieces)
-
-    other_by = after(other_by, next_1, far_1)
-    other_grads = hidden_grads(grad_blocks, [down_2], chunks[2:], by=other_by, before=other_grad)
+    (come_1,) = send_all([(send, side)], own_grads)
+    own_0, *pieces_0 = add_sides(after(keep_0, send), come_0, types)
+    far_0, next_0 = send_on(pieces_0)
+
+    other_by = after(other_by, next_0, far_0)
+    other_grads = hidden_grads(grad_blocks, [down_0, down_1], chunks, by=other_by)
     weights = [gate_weight, up_weight, other_gate, other_up]
 
     def back(c, *waits):
         lo, hi = back_chunks[c]
         return back_columns(own_grads, after(other_grads, *waits), weights, lo // (hi - lo), hi - lo)
 
-    near_1 = send_last(pieces, next_1, far_1)
-    keep_3, send = back(0)
-    (come_3,) = send_all([(send, side)])
-
-    keep_4, send = back(1, near_1)
-    own_2, *pieces = add_sides(keep_2, come_2, types)
-    (come_4,) = send_all([(send, side)], own_2)
-    far_2, next_2 = send_on(pieces, far_1)
-    near_2 = send_last(pieces, next_2, far_2)
-
-    keep_5, send = back(2, near_2)
-    own_3, *pieces = add_sides(keep_3, come_3, types)
-    (come_5,) = send_all([(send, side)], own_3)
-    far_3, next_3 = send_on(pieces, near_1)
-    near_3 = send_last(pieces, next_3, far_3)
-
-    mixed = finish(chunks, [(own_0, far_0, near_0), (own_1, far_1, near_1), (own_2, far_2, near_2)], width)
-    own_4, *pieces = add_sides(keep_4, after(come_4, mixed), types)
-    far_4, next_4 = send_on(pieces, near_2)
-    near_4 = send_last(pieces, next_4, far_4)
-
+    own_2, side_2, *pieces_2 = pair_sides(*back(0), types)
+    far_2, next_2 = send_on(pieces_2)
+    near_0 = send_last(pieces_0, next_0)
+
+    keep_3, send = back(1, own_2)
+    (come_3,) = send_all([(send, side)], own_0)
+
+    own_1, *pieces_1 = add_sides(after(keep_1, send), come_1, types)
+    near_2 = send_last(pieces_2, next_2, far_2)
+    far_1, next_1 = send_on(pieces_1, near_0)
+    keep_4, send = back(2, next_1)
+    (come_4,) = send_all([(send, side)], own_1)
+    near_1 = send_last(pieces_1, next_1, far_1, near_2)
+    (come_2,) = send_all([(add_parts(side_2, far_2, near_2), side)], own_1)
+
+    own_3, *pieces_3 = add_sides(after(keep_3, send), come_3, types)
+    far_3, next_3 = send_on(pieces_3, near_1)
+    near_3 = send_last(pieces_3, next_3, far_3)
+
+    mixed = finish(chunks, [(own_0, far_0, near_0), (own_1, far_1, near_1)], width)
     types = [jnp.float32] + [jnp.bfloat16] * (layers - 1)
-    own_5, *pieces = add_sides(keep_5, after(come_5, own_4), types)
-    parts_5 = send_all([(piece, layer[k]) for k, piece in enumerate(pieces, 1)], near_3)
-    back_parts = [(own_3, far_3, near_3), (own_4, far_4, near_4), (own_5, *parts_5)]
+    own_4, *pieces_4 = add_sides(keep_4, after(come_4, own_3), types)
+    parts_4 = send_all([(piece, layer[k]) for k, piece in enumerate(pieces_4, 1)], mixed)
+    back_parts = [(own_2, far_2, near_2, come_2), (own_3, far_3, near_3), (own_4, *parts_4)]
     return (mixed, finish(back_chunks, back_parts, width))
 
 

time: 246 us -> 257 us (1.045)
  waiting for transfers between devices: 120 us -> 138 us
  Pallas kernels: 56.9 us -> 51.8 us
    ppermute x43 -> x38, waiting for transfers between devices: 120 us -> 138 us  [send_all(): lax.ppermute(v, 'expert', pairs)]
    pallas_call x3 -> x2, Pallas kernels: 11.7 us -> 8.86 us  [hidden_grads(): pl.pallas_call(functools.partial(grads_kernel, blocks, tuple(cuts), by is...]
    pallas_call x6 -> x5, Pallas kernels: 22 us -> 19.9 us  [sum_columns(): pl.pallas_call(kernel, grid=(2,), in_specs=[rows, rows] + weight_specs, o...]
    ppermute x43 -> x38, starting transfers between devices: 58.9 us -> 58 us  [send_all(): lax.ppermute(v, 'expert', pairs)]
  transfers between devices with their start and end apart: 43 -> 38, of which waited for: 24 -> 21; matrix products, arithmetic and copies ran while one was open for 1% -> 1% of each run, Pallas kernels for 23% -> 20%
where the time goes in v8:
time: 257 us
  waiting for transfers between devices  138 us (54%)
  starting transfers between devices  58 us (23%)
  Pallas kernels  51.8 us (20%)
  local copies, waits for them, and re-layouts  7.04 us (3%)
    ppermute x38, waiting for transfers between devices, send_all(): lax.ppermute(v, 'expert', pairs)  138 us
    ppermute x38, starting transfers between devices, send_all(): lax.ppermute(v, 'expert', pairs)  58 us
    pallas_call x2, Pallas kernels, hidden_forward(): pl.pallas_call(functools.partial(hidden_kernel, blocks, all_experts), gri...  19.9 us
    pallas_call x5, Pallas kernels, sum_columns(): pl.pallas_call(kernel, grid=(2,), in_specs=[rows, rows] + weight_specs, o...  19.9 us
    pallas_call x2, Pallas kernels, hidden_grads(): pl.pallas_call(functools.partial(grads_kernel, blocks, tuple(cuts), by is...  8.86 us
  transfers between devices with their start and end apart: 38, of which 21 were waited for; matrix products, arithmetic and copies ran while one was open for 1% of the time, Pallas kernels for 20%

profile of v8, /device:TPU:0, one launch (start us, length us, event | category | flops | bytes accessed | tf_op | source)
XLA Modules:
  0.0 256.9 jit_solution(924906893142170173)
XLA Ops:
  0.6 0.7 select_reduce_fusion
  1.6 1.2 concatenate.3.refs_0_
  2.8 3.0 %collective-permute-start.8 = (bf16[2,2048,256]{2,1,0:T(8,128)(2,1)}, bf16[2,2048,256]{2,1,0:T(8,128)(2,1)S(1)}, u32[]{:S(2)}, u32[]{:S(2)}) collective-permute-start(bf16[2,2048,256]{2,1,0:T(8,128)(2,1)} %refs_0_.5), channel_id=1, source_target_pairs={{0,1},{1,0},{2,3},{3,2},{4,5},{5,4},{6,7},{7,6},{8,9},{9,8},{10,11... | collective-permute-start | bytes 6291464 | tf_op jit(solution)/shard_map/ppermute | solution.py:311
  5.8 1.6 collective-permute-start.3
  7.4 1.5 collective-permute-start.6
  8.9 2.2 collective-permute-start
  11.7 10.8 %collective-permute-done.6.refs_6_.refs_7_ = bf16[128,2048]{1,0:T(8,128)(2,1)S(1)} collective-permute-done((bf16[128,2048]{1,0:T(8,128)(2,1)}, bf16[128,2048]{1,0:T(8,128)(2,1)S(1)}, u32[]{:S(2)}, u32[]{:S(2)}) %collective-permute-start.6) | collective-permute-done | bytes 524320 | tf_op jit(solution)/shard_map/ppermute | solution.py:311
  22.5 0.8 copy-done.10
  23.8 9.9 %collective-permute-done.refs_1_ = bf16[128,2176]{1,0:T(8,128)(2,1)S(1)} collective-permute-done((bf16[128,2176]{1,0:T(8,128)(2,1)S(1)}, bf16[128,2176]{1,0:T(8,128)(2,1)S(1)}, u32[]{:S(2)}, u32[]{:S(2)}) %collective-permute-start) | collective-permute-done | bytes 557088 | tf_op jit(solution)/shard_map/ppermute | solution.py:311
  33.7 1.2 collective-permute-start.4
  35.0 2.6 %collective-permute-start.2 = (bf16[128,2176]{1,0:T(8,128)(2,1)S(1)}, bf16[128,2176]{1,0:T(8,128)(2,1)S(1)}, u32[]{:S(2)}, u32[]{:S(2)}) collective-permute-start(bf16[128,2176]{1,0:T(8,128)(2,1)S(1)} %collective-permute-done.refs_1_), channel_id=1, source_target_pairs={{0,12},{1,13},{2,14},{3,15},{4,0},{5,1},{6,2},{7,3},{8,4},{9,5},{1... | collective-permute-start | bytes 1671176 | tf_op jit(solution)/shard_map/ppermute | solution.py:311
  37.6 0.7 collective-permute-start.7
  38.3 11.0 %collective-permute-done.4.refs_5_ = bf16[128,2176]{1,0:T(8,128)(2,1)S(1)} collective-permute-done((bf16[128,2176]{1,0:T(8,128)(2,1)S(1)}, bf16[128,2176]{1,0:T(8,128)(2,1)S(1)}, u32[]{:S(2)}, u32[]{:S(2)}) %collective-permute-start.4) | collective-permute-done | bytes 557088 | tf_op jit(solution)/shard_map/ppermute | solution.py:311
  49.3 2.4 collective-permute-start.11
  51.7 1.5 collective-permute-start.5
  53.2 3.0 %fusion.1 = (bf16[512,1024]{1,0:T(8,128)(2,1)}, bf16[512,1024]{1,0:T(8,128)(2,1)}) fusion(bf16[512,2048]{1,0:T(8,128)(2,1)} %bitcast.3), kind=kLoop, calls=%fused_computation.5 | loop fusion | bytes 4194304 | tf_op jit(solution)/shard_map/slice | solution.py:337
  56.3 4.9 %collective-permute-done.7.refs_7_ = bf16[128,2176]{1,0:T(8,128)(2,1)S(1)} collective-permute-done((bf16[128,2176]{1,0:T(8,128)(2,1)S(1)}, bf16[128,2176]{1,0:T(8,128)(2,1)S(1)}, u32[]{:S(2)}, u32[]{:S(2)}) %collective-permute-start.7) | collective-permute-done | bytes 557088 | tf_op jit(solution)/shard_map/ppermute | solution.py:311
  61.2 0.6 collective-permute-start.10
  61.8 10.3 %collective-permute-done.5.refs_6_ = bf16[128,2176]{1,0:T(8,128)(2,1)S(1)} collective-permute-done((bf16[128,2176]{1,0:T(8,128)(2,1)S(1)}, bf16[128,2176]{1,0:T(8,128)(2,1)S(1)}, u32[]{:S(2)}, u32[]{:S(2)}) %collective-permute-start.5) | collective-permute-done | bytes 557088 | tf_op jit(solution)/shard_map/ppermute | solution.py:311
  73.0 1.0 collective-permute-start.12
  73.9 1.2 collective-permute-start.13
  75.1 9.9 %hidden_forward.2 = (bf16[1024,512]{1,0:T(8,128)(2,1)}, f32[1024,1024]{1,0:T(8,128)}) custom-call(s32[1]{0:T(128)} %bitcast.owner_ref, bf16[2,2048,256]{2,1,0:T(8,128)(2,1)} %refs_0_.5, bf16[2,2048,256]{2,1,0:T(8,128)(2,1)} %refs_1_.5, bf16[128,2176]{1,0:T(8,128)(2,1)} %copy-done.12, bf16[128,2176]{1,0:T(8,128)(2,1)} %copy-done.14, ...), custom_call_target="tpu_custom_call" | custom-call | flops 1 | bytes 1 | tf_op jit(solution)/shard_map/hidden_forward/pallas_call | solution.py:71
  85.0 11.8 %collective-permute-done.15.refs_4_.refs_5_ = bf16[128,2048]{1,0:T(8,128)(2,1)} collective-permute-done((bf16[128,2048]{1,0:T(8,128)(2,1)}, bf16[128,2048]{1,0:T(8,128)(2,1)}, u32[]{:S(2)}, u32[]{:S(2)}) %collective-permute-start.15) | collective-permute-done | bytes 524320 | tf_op jit(solution)/shard_map/ppermute | solution.py:311
  97.2 1.6 collective-permute-start.14
  98.8 10.0 %hidden_forward.3 = (bf16[1024,512]{1,0:T(8,128)(2,1)}, f32[1024,1024]{1,0:T(8,128)}) custom-call(s32[1]{0:T(128)} %bitcast.1.owner_ref, bf16[2,2048,256]{2,1,0:T(8,128)(2,1)} %copy-done.3, bf16[2,2048,256]{2,1,0:T(8,128)(2,1)} %collective-permute-done.9.up_ref.refs_3_, bf16[128,2176]{1,0:T(8,128)(2,1)} %copy-done.12, bf16[128,2176]{1,0:T(8,128)(2,1)} %copy-done.14, ...), custom_call_target="tpu_custom_call" | custom-call | flops 1 | bytes 1 | tf_op jit(solution)/shard_map/hidden_forward/pallas_call | solution.py:71
  108.8 10.2 %collective-permute-done.10.other_down_ref.refs_1_ = bf16[512,1024]{1,0:T(8,128)(2,1)S(1)} collective-permute-done((bf16[512,1024]{1,0:T(8,128)(2,1)}, bf16[512,1024]{1,0:T(8,128)(2,1)S(1)}, u32[]{:S(2)}, u32[]{:S(2)}) %collective-permute-start.10) | collective-permute-done | bytes 1048608 | tf_op jit(solution)/shard_map/ppermute | solution.py:311
  119.1 1.7 collective-permute-start.17
  120.9 1.2 copy-done.8
  122.1 2.8 %mix_columns.2 = (f32[512,1024]{1,0:T(8,128)S(1)}, bf16[512,1024]{1,0:T(8,128)(2,1)S(1)}) custom-call(bf16[1024,512]{1,0:T(8,128)(2,1)S(1)} %copy-done.7, bf16[1024,512]{1,0:T(8,128)(2,1)S(1)} %copy-done.8, bf16[512,2048]{1,0:T(8,128)(2,1)S(1)} %bitcast.4, bf16[512,1024]{1,0:T(8,128)(2,1)S(1)} %collective-permute-done.10.other_down_ref.refs_1_), custom_call_target="tpu_custom_call" | custom-call | flops 1 | bytes 1 | tf_op jit(solution)/shard_map/mix_columns/pallas_call | solution.py:179
  124.9 1.6 collective-permute-start.18
  126.5 4.4 %hidden_grads.2.own_ref = bf16[1024,1024]{1,0:T(8,128)(2,1)S(1)} custom-call(f32[1024,1024]{1,0:T(8,128)S(1)} %copy-done.6, bf16[512,2048]{1,0:T(8,128)(2,1)S(1)} %bitcast.5, bf16[128,2048]{1,0:T(8,128)(2,1)} %refs_3_.1, bf16[128,2048]{1,0:T(8,128)(2,1)} %collective-permute-done.11.refs_3_.refs_4_, ...), custom_call_target="tpu_custom_call" | custom-call | flops 1 | bytes 1 | tf_op jit(solution)/shard_map/hidden_grads/pallas_call | solution.py:127
  130.9 12.7 %collective-permute-done.17.other_down_ref.refs_2_ = bf16[512,1024]{1,0:T(8,128)(2,1)S(1)} collective-permute-done((bf16[512,1024]{1,0:T(8,128)(2,1)}, bf16[512,1024]{1,0:T(8,128)(2,1)S(1)}, u32[]{:S(2)}, u32[]{:S(2)}) %collective-permute-start.17) | collective-permute-done | bytes 1048608 | tf_op jit(solution)/shard_map/ppermute | solution.py:311
  143.6 2.8 %mix_columns.3 = (f32[512,1024]{1,0:T(8,128)S(1)}, bf16[512,1024]{1,0:T(8,128)(2,1)S(1)}) custom-call(bf16[1024,512]{1,0:T(8,128)(2,1)S(1)} %copy-done.7, bf16[1024,512]{1,0:T(8,128)(2,1)S(1)} %copy-done.9, bf16[512,2048]{1,0:T(8,128)(2,1)S(1)} %bitcast.6, bf16[512,1024]{1,0:T(8,128)(2,1)S(1)} %collective-permute-done.17.other_down_ref.refs_2_), custom_call_target="tpu_custom_call" | custom-call | flops 1 | bytes 1 | tf_op jit(solution)/shard_map/mix_columns/pallas_call | solution.py:179
  146.5 1.5 collective-permute-start.22
  148.0 2.1 collective-permute-done.18.come_ref
  150.2 3.9 %collective-permute-start.19 = (bf16[128,1024]{1,0:T(8,128)(2,1)S(1)}, bf16[128,1024]{1,0:T(8,128)(2,1)S(1)}, u32[]{:S(2)}, u32[]{:S(2)}) collective-permute-start(bf16[128,1024]{1,0:T(8,128)(2,1)S(1)} %get-tuple-element.103), channel_id=1, source_target_pairs={{0,12},{1,13},{2,14},{3,15},{4,0},{5,1},{6,2},{7,3},{8,4},{9,5},{1... | collective-permute-start | bytes 786440 | tf_op jit(solution)/shard_map/ppermute | solution.py:311
  154.2 5.3 %collective-permute-done.19.refs_1_ = bf16[128,1024]{1,0:T(8,128)(2,1)S(1)} collective-permute-done((bf16[128,1024]{1,0:T(8,128)(2,1)S(1)}, bf16[128,1024]{1,0:T(8,128)(2,1)S(1)}, u32[]{:S(2)}, u32[]{:S(2)}) %collective-permute-start.19) | collective-permute-done | bytes 262176 | tf_op jit(solution)/shard_map/ppermute | solution.py:311
  159.5 3.4 %collective-permute-done.20.come_ref = bf16[128,1024]{1,0:T(8,128)(2,1)S(1)} collective-permute-done((bf16[128,1024]{1,0:T(8,128)(2,1)S(1)}, bf16[128,1024]{1,0:T(8,128)(2,1)S(1)}, u32[]{:S(2)}, u32[]{:S(2)}) %collective-permute-start.20) | collective-permute-done | bytes 262176 | tf_op jit(solution)/shard_map/ppermute | solution.py:311
  162.9 4.5 %hidden_grads.3.other_ref = bf16[1024,1024]{1,0:T(8,128)(2,1)S(1)} custom-call(f32[1024,1024]{1,0:T(8,128)S(1)} %copy-done.5, bf16[512,1024]{1,0:T(8,128)(2,1)S(1)} %collective-permute-done.10.other_down_ref.refs_1_, bf16[512,1024]{1,0:T(8,128)(2,1)S(1)} %collective-permute-done.17.other_down_ref.refs_2_, bf16[128,2048]{1,0:T(8,128)(2,1)} %refs_3_.1, ...), custom_call_target="tpu_custom_call" | custom-call | flops 1 | bytes 1 | tf_op jit(solution)/shard_map/hidden_grads/pallas_call | solution.py:127
  167.4 3.9 %back_columns.3 = (f32[512,512]{1,0:T(8,128)S(1)}, bf16[512,512]{1,0:T(8,128)(2,1)S(1)}) custom-call(bf16[1024,1024]{1,0:T(8,128)(2,1)S(1)} %hidden_grads.2.own_ref, bf16[1024,1024]{1,0:T(8,128)(2,1)S(1)} %hidden_grads.3.other_ref, bf16[2,2048,256]{2,1,0:T(8,128)(2,1)S(1)} %copy-done.1, bf16[2,2048,256]{2,1,0:T(8,128)(2,1)S(1)} %copy-done.2, ...), custom_call_target="tpu_custom_call" | custom-call | flops 1 | bytes 1 | tf_op jit(solution)/shard_map/back_columns/pallas_call | solution.py:179
  171.5 6.4 %back_columns.4 = (f32[512,1024]{1,0:T(8,128)S(1)}, bf16[512,1024]{1,0:T(8,128)(2,1)S(1)}) custom-call(bf16[1024,1024]{1,0:T(8,128)(2,1)S(1)} %hidden_grads.2.own_ref, bf16[1024,1024]{1,0:T(8,128)(2,1)S(1)} %hidden_grads.3.other_ref, bf16[2,2048,256]{2,1,0:T(8,128)(2,1)S(1)} %copy-done.1, bf16[2,2048,256]{2,1,0:T(8,128)(2,1)S(1)} %copy-done.2, ...), custom_call_target="tpu_custom_call" | custom-call | flops 1 | bytes 1 | tf_op jit(solution)/shard_map/back_columns/pallas_call | solution.py:179
  177.9 1.6 collective-permute-start.30
  179.5 1.4 collective-permute-start.25
  180.9 2.4 collective-permute-start.26
  183.4 7.3 %collective-permute-done.25.come_ref = bf16[256,512]{1,0:T(8,128)(2,1)S(1)} collective-permute-done((bf16[256,512]{1,0:T(8,128)(2,1)S(1)}, bf16[256,512]{1,0:T(8,128)(2,1)S(1)}, u32[]{:S(2)}, u32[]{:S(2)}) %collective-permute-start.25) | collective-permute-done | bytes 262176 | tf_op jit(solution)/shard_map/ppermute | solution.py:311
  190.7 12.1 %collective-permute-done.26.refs_0_.refs_1_ = bf16[256,512]{1,0:T(8,128)(2,1)S(1)} collective-permute-done((bf16[256,512]{1,0:T(8,128)(2,1)S(1)}, bf16[256,512]{1,0:T(8,128)(2,1)S(1)}, u32[]{:S(2)}, u32[]{:S(2)}) %collective-permute-start.26) | collective-permute-done | bytes 262176 | tf_op jit(solution)/shard_map/ppermute | solution.py:311
  203.1 3.9 %collective-permute-start.23 = (bf16[128,1024]{1,0:T(8,128)(2,1)S(1)}, bf16[128,1024]{1,0:T(8,128)(2,1)S(1)}, u32[]{:S(2)}, u32[]{:S(2)}) collective-permute-start(bf16[128,1024]{1,0:T(8,128)(2,1)S(1)} %get-tuple-element.119), channel_id=1, source_target_pairs={{0,12},{1,13},{2,14},{3,15},{4,0},{5,1},{6,2},{7,3},{8,4},{9,5},{1... | collective-permute-start | bytes 786440 | tf_op jit(solution)/shard_map/ppermute | solution.py:311
  207.0 9.8 %collective-permute-done.24.come_ref = bf16[128,1024]{1,0:T(8,128)(2,1)S(1)} collective-permute-done((bf16[128,1024]{1,0:T(8,128)(2,1)S(1)}, bf16[128,1024]{1,0:T(8,128)(2,1)S(1)}, u32[]{:S(2)}, u32[]{:S(2)}) %collective-permute-start.24) | collective-permute-done | bytes 262176 | tf_op jit(solution)/shard_map/ppermute | solution.py:311
  216.9 2.8 %collective-permute-done.23.refs_4_ = bf16[128,1024]{1,0:T(8,128)(2,1)S(1)} collective-permute-done((bf16[128,1024]{1,0:T(8,128)(2,1)S(1)}, bf16[128,1024]{1,0:T(8,128)(2,1)S(1)}, u32[]{:S(2)}, u32[]{:S(2)}) %collective-permute-start.23) | collective-permute-done | bytes 262176 | tf_op jit(solution)/shard_map/ppermute | solution.py:311
  219.6 5.9 %collective-permute-start.28 = (bf16[128,1024]{1,0:T(8,128)(2,1)S(1)}, bf16[128,1024]{1,0:T(8,128)(2,1)S(1)}, u32[]{:S(2)}, u32[]{:S(2)}) collective-permute-start(bf16[128,1024]{1,0:T(8,128)(2,1)S(1)} %add_piece.5), channel_id=1, source_target_pairs={{0,4},{1,5},{2,6},{3,7},{4,8},{5,9},{6,10},{7,11},{8,12},{9,13},{1... | collective-permute-start | bytes 786440 | tf_op jit(solution)/shard_map/ppermute | solution.py:311
  225.5 3.9 %back_columns.5 = (f32[512,512]{1,0:T(8,128)S(1)}, bf16[512,512]{1,0:T(8,128)(2,1)S(1)}) custom-call(bf16[1024,1024]{1,0:T(8,128)(2,1)S(1)} %hidden_grads.2.own_ref, bf16[1024,1024]{1,0:T(8,128)(2,1)S(1)} %hidden_grads.3.other_ref, bf16[2,2048,256]{2,1,0:T(8,128)(2,1)S(1)} %copy-done.1, bf16[2,2048,256]{2,1,0:T(8,128)(2,1)S(1)} %copy-done.2, ...), custom_call_target="tpu_custom_call" | custom-call | flops 1 | bytes 1 | tf_op jit(solution)/shard_map/back_columns/pallas_call | solution.py:179
  229.4 0.6 collective-permute-start.34
  230.2 2.0 collective-permute-done.28.refs_5_
  232.2 2.5 collective-permute-start.32
  234.7 1.3 collective-permute-start.31
  236.0 4.5 %collective-permute-done.32.come_ref = bf16[128,1024]{1,0:T(8,128)(2,1)S(1)} collective-permute-done((bf16[128,1024]{1,0:T(8,128)(2,1)S(1)}, bf16[128,1024]{1,0:T(8,128)(2,1)S(1)}, u32[]{:S(2)}, u32[]{:S(2)}) %collective-permute-start.32) | collective-permute-done | bytes 262176 | tf_op jit(solution)/shard_map/ppermute | solution.py:311
  240.6 2.6 %collective-permute-done.31.refs_5_ = bf16[128,1024]{1,0:T(8,128)(2,1)S(1)} collective-permute-done((bf16[128,1024]{1,0:T(8,128)(2,1)S(1)}, bf16[128,1024]{1,0:T(8,128)(2,1)S(1)}, u32[]{:S(2)}, u32[]{:S(2)}) %collective-permute-start.31) | collective-permute-done | bytes 262176 | tf_op jit(solution)/shard_map/ppermute | solution.py:311
  244.4 1.1 finish.2
  245.6 2.1 collective-permute-start.35
  247.7 1.8 collective-permute-start.36
  249.5 1.6 collective-permute-start.37
  251.2 1.7 collective-permute-done.35.refs_8_
  252.9 2.8 %collective-permute-done.36.refs_9_ = bf16[128,512]{1,0:T(8,128)(2,1)S(1)} collective-permute-done((bf16[128,512]{1,0:T(8,128)(2,1)S(1)}, bf16[128,512]{1,0:T(8,128)(2,1)S(1)}, u32[]{:S(2)}, u32[]{:S(2)}) %collective-permute-start.36) | collective-permute-done | bytes 131104 | tf_op jit(solution)/shard_map/ppermute | solution.py:311
  255.8 1.1 finish.3
  (81 shorter events, 4.8 us)
Async XLA Ops:
  2.8 58.4 %copy-start.12 = (bf16[128,2176]{1,0:T(8,128)(2,1)}, bf16[128,2176]{1,0:T(8,128)(2,1)S(1)}, u32[]{:S(2)}) copy-start(bf16[128,2176]{1,0:T(8,128)(2,1)S(1)} %concatenate.3.refs_0_) | copy-start | bytes 1671172
  2.8 58.4 %collective-permute-start.8 = (bf16[2,2048,256]{2,1,0:T(8,128)(2,1)}, bf16[2,2048,256]{2,1,0:T(8,128)(2,1)S(1)}, u32[]{:S(2)}, u32[]{:S(2)}) collective-permute-start(bf16[2,2048,256]{2,1,0:T(8,128)(2,1)} %refs_0_.5), channel_id=1, source_target_pairs={{0,1},{1,0},{2,3},{3,2},{4,5},{5,4},{6,7},{7,6},{8,9},{9,8},{10,11... | collective-permute-start | bytes 6291464 | tf_op jit(solution)/shard_map/ppermute | solution.py:311
  5.8 17.4 %collective-permute-start.3 = (bf16[128,2176]{1,0:T(8,128)(2,1)S(1)}, bf16[128,2176]{1,0:T(8,128)(2,1)S(1)}, u32[]{:S(2)}, u32[]{:S(2)}) collective-permute-start(bf16[128,2176]{1,0:T(8,128)(2,1)S(1)} %concatenate.3.refs_0_), channel_id=1, source_target_pairs={{0,4},{1,5},{2,6},{3,7},{4,8},{5,9},{6,10},{7,11},{8,12},{9,13},{1... | collective-permute-start | bytes 1671176 | tf_op jit(solution)/shard_map/ppermute | solution.py:311
  7.4 15.1 %collective-permute-start.6 = (bf16[128,2048]{1,0:T(8,128)(2,1)}, bf16[128,2048]{1,0:T(8,128)(2,1)S(1)}, u32[]{:S(2)}, u32[]{:S(2)}) collective-permute-start(bf16[128,2048]{1,0:T(8,128)(2,1)} %refs_3_.1), channel_id=1, source_target_pairs={{0,2},{1,3},{2,0},{3,1},{4,6},{5,7},{6,4},{7,5},{8,10},{9,11},{10,... | collective-permute-start | bytes 1572872 | tf_op jit(solution)/shard_map/ppermute | solution.py:311
  8.9 24.8 %collective-permute-start = (bf16[128,2176]{1,0:T(8,128)(2,1)S(1)}, bf16[128,2176]{1,0:T(8,128)(2,1)S(1)}, u32[]{:S(2)}, u32[]{:S(2)}) collective-permute-start(bf16[128,2176]{1,0:T(8,128)(2,1)S(1)} %concatenate.3.refs_0_), channel_id=1, source_target_pairs={{0,12},{1,13},{2,14},{3,15},{4,0},{5,1},{6,2},{7,3},{8,4},{9,5},{1... | collective-permute-start | bytes 1671176 | tf_op jit(solution)/shard_map/ppermute | solution.py:311
  11.2 22.5 %collective-permute-start.1 = (bf16[128,2176]{1,0:T(8,128)(2,1)S(1)}, bf16[128,2176]{1,0:T(8,128)(2,1)S(1)}, u32[]{:S(2)}, u32[]{:S(2)}) collective-permute-start(bf16[128,2176]{1,0:T(8,128)(2,1)S(1)} %concatenate.3.refs_0_), channel_id=1, source_target_pairs={{0,2},{1,3},{2,0},{3,1},{4,6},{5,7},{6,4},{7,5},{8,10},{9,11},{10,... | collective-permute-start | bytes 1671176 | tf_op jit(solution)/shard_map/ppermute | solution.py:311
  22.5 0.8 copy-start.10
  23.3 33.0 %copy-start.13 = (bf16[128,2176]{1,0:T(8,128)(2,1)}, bf16[128,2176]{1,0:T(8,128)(2,1)S(1)}, u32[]{:S(2)}) copy-start(bf16[128,2176]{1,0:T(8,128)(2,1)S(1)} %collective-permute-done.3.refs_3_) | copy-start | bytes 1671172
  23.3 75.5 %collective-permute-start.9 = (bf16[2,2048,256]{2,1,0:T(8,128)(2,1)}, bf16[2,2048,256]{2,1,0:T(8,128)(2,1)}, u32[]{:S(2)}, u32[]{:S(2)}) collective-permute-start(bf16[2,2048,256]{2,1,0:T(8,128)(2,1)} %refs_1_.5), channel_id=1, source_target_pairs={{0,1},{1,0},{2,3},{3,2},{4,5},{5,4},{6,7},{7,6},{8,9},{9,8},{10,11... | collective-permute-start | bytes 6291464 | tf_op jit(solution)/shard_map/ppermute | solution.py:311
  33.7 1.3 copy-start.14
  33.7 15.6 %copy-start.15 = (bf16[128,2176]{1,0:T(8,128)(2,1)}, bf16[128,2176]{1,0:T(8,128)(2,1)S(1)}, u32[]{:S(2)}) copy-start(bf16[128,2176]{1,0:T(8,128)(2,1)S(1)} %collective-permute-done.1.refs_4_) | copy-start | bytes 1671172
  33.7 15.6 %collective-permute-start.4 = (bf16[128,2176]{1,0:T(8,128)(2,1)S(1)}, bf16[128,2176]{1,0:T(8,128)(2,1)S(1)}, u32[]{:S(2)}, u32[]{:S(2)}) collective-permute-start(bf16[128,2176]{1,0:T(8,128)(2,1)S(1)} %collective-permute-done.refs_1_), channel_id=1, source_target_pairs={{0,2},{1,3},{2,0},{3,1},{4,6},{5,7},{6,4},{7,5},{8,10},{9,11},{10,... | collective-permute-start | bytes 1671176 | tf_op jit(solution)/shard_map/ppermute | solution.py:311
  35.0 14.3 %collective-permute-start.2 = (bf16[128,2176]{1,0:T(8,128)(2,1)S(1)}, bf16[128,2176]{1,0:T(8,128)(2,1)S(1)}, u32[]{:S(2)}, u32[]{:S(2)}) collective-permute-start(bf16[128,2176]{1,0:T(8,128)(2,1)S(1)} %collective-permute-done.refs_1_), channel_id=1, source_target_pairs={{0,12},{1,13},{2,14},{3,15},{4,0},{5,1},{6,2},{7,3},{8,4},{9,5},{1... | collective-permute-start | bytes 1671176 | tf_op jit(solution)/shard_map/ppermute | solution.py:311
  37.6 23.6 %collective-permute-start.7 = (bf16[128,2176]{1,0:T(8,128)(2,1)S(1)}, bf16[128,2176]{1,0:T(8,128)(2,1)S(1)}, u32[]{:S(2)}, u32[]{:S(2)}) collective-permute-start(bf16[128,2176]{1,0:T(8,128)(2,1)S(1)} %collective-permute-done.3.refs_3_), channel_id=1, source_target_pairs={{0,2},{1,3},{2,0},{3,1},{4,6},{5,7},{6,4},{7,5},{8,10},{9,11},{10,... | collective-permute-start | bytes 1671176 | tf_op jit(solution)/shard_map/ppermute | solution.py:311
  49.3 2.4 copy-start.16
  49.3 7.0 %copy-start.17 = (bf16[128,2176]{1,0:T(8,128)(2,1)}, bf16[128,2176]{1,0:T(8,128)(2,1)S(1)}, u32[]{:S(2)}) copy-start(bf16[128,2176]{1,0:T(8,128)(2,1)S(1)} %collective-permute-done.2.refs_2_) | copy-start | bytes 1671172
  49.3 12.5 %collective-permute-start.11 = (bf16[128,2048]{1,0:T(8,128)(2,1)}, bf16[128,2048]{1,0:T(8,128)(2,1)}, u32[]{:S(2)}, u32[]{:S(2)}) collective-permute-start(bf16[128,2048]{1,0:T(8,128)(2,1)} %refs_3_.1), channel_id=1, source_target_pairs={{0,12},{1,13},{2,14},{3,15},{4,0},{5,1},{6,2},{7,3},{8,4},{9,5},{1... | collective-permute-start | bytes 1572872 | tf_op jit(solution)/shard_map/ppermute | solution.py:311
  51.7 20.4 %collective-permute-start.5 = (bf16[128,2176]{1,0:T(8,128)(2,1)S(1)}, bf16[128,2176]{1,0:T(8,128)(2,1)S(1)}, u32[]{:S(2)}, u32[]{:S(2)}) collective-permute-start(bf16[128,2176]{1,0:T(8,128)(2,1)S(1)} %collective-permute-done.2.refs_2_), channel_id=1, source_target_pairs={{0,2},{1,3},{2,0},{3,1},{4,6},{5,7},{6,4},{7,5},{8,10},{9,11},{10,... | collective-permute-start | bytes 1671176 | tf_op jit(solution)/shard_map/ppermute | solution.py:311
  61.2 10.9 %copy-start.18 = (bf16[128,2176]{1,0:T(8,128)(2,1)}, bf16[128,2176]{1,0:T(8,128)(2,1)S(1)}, u32[]{:S(2)}) copy-start(bf16[128,2176]{1,0:T(8,128)(2,1)S(1)} %collective-permute-done.7.refs_7_) | copy-start | bytes 1671172
  61.2 23.8 %copy-start.3 = (bf16[2,2048,256]{2,1,0:T(8,128)(2,1)}, bf16[2,2048,256]{2,1,0:T(8,128)(2,1)S(1)}, u32[]{:S(2)}) copy-start(bf16[2,2048,256]{2,1,0:T(8,128)(2,1)S(1)} %collective-permute-done.8.gate_ref.refs_2_) | copy-start | bytes 6291460
  61.2 57.8 %collective-permute-start.10 = (bf16[512,1024]{1,0:T(8,128)(2,1)}, bf16[512,1024]{1,0:T(8,128)(2,1)S(1)}, u32[]{:S(2)}, u32[]{:S(2)}) collective-permute-start(bf16[512,1024]{1,0:T(8,128)(2,1)} %get-tuple-element.89), channel_id=1, source_target_pairs={{0,1},{1,0},{2,3},{3,2},{4,5},{5,4},{6,7},{7,6},{8,9},{9,8},{10,11... | collective-permute-start | bytes 3145736 | tf_op jit(solution)/shard_map/ppermute | solution.py:311
  72.2 0.8 copy-start.19
  72.2 24.6 %collective-permute-start.15 = (bf16[128,2048]{1,0:T(8,128)(2,1)}, bf16[128,2048]{1,0:T(8,128)(2,1)}, u32[]{:S(2)}, u32[]{:S(2)}) collective-permute-start(bf16[128,2048]{1,0:T(8,128)(2,1)} %collective-permute-done.11.refs_3_.refs_4_), channel_id=1, source_target_pairs={{0,12},{1,13},{2,14},{3,15},{4,0},{5,1},{6,2},{7,3},{8,4},{9,5},{1... | collective-permute-start | bytes 1572872 | tf_op jit(solution)/shard_map/ppermute | solution.py:311
  73.0 23.8 %collective-permute-start.12 = (bf16[128,2048]{1,0:T(8,128)(2,1)}, bf16[128,2048]{1,0:T(8,128)(2,1)}, u32[]{:S(2)}, u32[]{:S(2)}) collective-permute-start(bf16[128,2048]{1,0:T(8,128)(2,1)} %collective-permute-done.11.refs_3_.refs_4_), channel_id=1, source_target_pairs={{0,2},{1,3},{2,0},{3,1},{4,6},{5,7},{6,4},{7,5},{8,10},{9,11},{10,... | collective-permute-start | bytes 1572872 | tf_op jit(solution)/shard_map/ppermute | solution.py:311
  73.9 23.3 %collective-permute-start.13 = (bf16[128,2048]{1,0:T(8,128)(2,1)}, bf16[128,2048]{1,0:T(8,128)(2,1)}, u32[]{:S(2)}, u32[]{:S(2)}) collective-permute-start(bf16[128,2048]{1,0:T(8,128)(2,1)} %refs_3_.1), channel_id=1, source_target_pairs={{0,4},{1,5},{2,6},{3,7},{4,8},{5,9},{6,10},{7,11},{8,12},{9,13},{1... | collective-permute-start | bytes 1572872 | tf_op jit(solution)/shard_map/ppermute | solution.py:311
  96.8 24.1 %collective-permute-start.16 = (bf16[128,2048]{1,0:T(8,128)(2,1)}, bf16[128,2048]{1,0:T(8,128)(2,1)S(1)}, u32[]{:S(2)}, u32[]{:S(2)}) collective-permute-start(bf16[128,2048]{1,0:T(8,128)(2,1)} %collective-permute-done.15.refs_4_.refs_5_), channel_id=1, source_target_pairs={{0,2},{1,3},{2,0},{3,1},{4,6},{5,7},{6,4},{7,5},{8,10},{9,11},{10,... | collective-permute-start | bytes 1572872 | tf_op jit(solution)/shard_map/ppermute | solution.py:311
  97.2 23.6 %collective-permute-start.14 = (bf16[128,2048]{1,0:T(8,128)(2,1)}, bf16[128,2048]{1,0:T(8,128)(2,1)S(1)}, u32[]{:S(2)}, u32[]{:S(2)}) collective-permute-start(bf16[128,2048]{1,0:T(8,128)(2,1)} %collective-permute-done.13.refs_5_.refs_6_), channel_id=1, source_target_pairs={{0,2},{1,3},{2,0},{3,1},{4,6},{5,7},{6,4},{7,5},{8,10},{9,11},{10,... | collective-permute-start | bytes 1572872 | tf_op jit(solution)/shard_map/ppermute | solution.py:311
  98.8 22.0 %copy-start = (bf16[2,256,2048]{2,1,0:T(8,128)(2,1)S(1)}, bf16[2,256,2048]{2,1,0:T(8,128)(2,1)}, u32[]{:S(2)}) copy-start(bf16[2,256,2048]{2,1,0:T(8,128)(2,1)} %param.13) | copy-start | bytes 6291460
  98.8 22.0 %copy-start.7 = (bf16[1024,512]{1,0:T(8,128)(2,1)S(1)}, bf16[1024,512]{1,0:T(8,128)(2,1)}, u32[]{:S(2)}) copy-start(bf16[1024,512]{1,0:T(8,128)(2,1)} %get-tuple-element.84.own_ref) | copy-start | bytes 3145732
  119.1 7.4 %copy-start.6 = (f32[1024,1024]{1,0:T(8,128)S(1)}, f32[1024,1024]{1,0:T(8,128)}, u32[]{:S(2)}) copy-start(f32[1024,1024]{1,0:T(8,128)} %get-tuple-element.107.refs_0_) | copy-start | bytes 12582916
  119.1 24.6 %collective-permute-start.17 = (bf16[512,1024]{1,0:T(8,128)(2,1)}, bf16[512,1024]{1,0:T(8,128)(2,1)S(1)}, u32[]{:S(2)}, u32[]{:S(2)}) collective-permute-start(bf16[512,1024]{1,0:T(8,128)(2,1)} %get-tuple-element.97), channel_id=1, source_target_pairs={{0,1},{1,0},{2,3},{3,2},{4,5},{5,4},{6,7},{7,6},{8,9},{9,8},{10,11... | collective-permute-start | bytes 3145736 | tf_op jit(solution)/shard_map/ppermute | solution.py:311
  120.8 1.2 copy-start.8
  122.1 4.4 %copy-start.11 = (bf16[128,2048]{1,0:T(8,128)(2,1)S(1)}, bf16[128,2048]{1,0:T(8,128)(2,1)}, u32[]{:S(2)}) copy-start(bf16[128,2048]{1,0:T(8,128)(2,1)} %copy-done.10) | copy-start | bytes 1572868
  124.9 25.2 %collective-permute-start.18 = (bf16[512,1024]{1,0:T(8,128)(2,1)S(1)}, bf16[512,1024]{1,0:T(8,128)(2,1)S(1)}, u32[]{:S(2)}, u32[]{:S(2)}) collective-permute-start(bf16[512,1024]{1,0:T(8,128)(2,1)S(1)} %get-tuple-element.98), channel_id=1, source_target_pairs={{0,2},{1,3},{2,0},{3,1},{4,6},{5,7},{6,4},{7,5},{8,10},{9,11},{10,... | collective-permute-start | bytes 3145736 | tf_op jit(solution)/shard_map/ppermute | solution.py:311
  126.5 17.1 %copy-start.9 = (bf16[1024,512]{1,0:T(8,128)(2,1)S(1)}, bf16[1024,512]{1,0:T(8,128)(2,1)}, u32[]{:S(2)}) copy-start(bf16[1024,512]{1,0:T(8,128)(2,1)} %get-tuple-element.88.other_ref) | copy-start | bytes 3145732
  143.6 19.3 %copy-start.5 = (f32[1024,1024]{1,0:T(8,128)S(1)}, f32[1024,1024]{1,0:T(8,128)}, u32[]{:S(2)}) copy-start(f32[1024,1024]{1,0:T(8,128)} %get-tuple-element.109.refs_0_) | copy-start | bytes 12582916
  146.5 56.4 %collective-permute-start.22 = (bf16[512,1024]{1,0:T(8,128)(2,1)S(1)}, bf16[512,1024]{1,0:T(8,128)(2,1)S(1)}, u32[]{:S(2)}, u32[]{:S(2)}) collective-permute-start(bf16[512,1024]{1,0:T(8,128)(2,1)S(1)} %get-tuple-element.116), channel_id=1, source_target_pairs={{0,2},{1,3},{2,0},{3,1},{4,6},{5,7},{6,4},{7,5},{8,10},{9,11},{10,... | collective-permute-start | bytes 3145736 | tf_op jit(solution)/shard_map/ppermute | solution.py:311
  150.2 9.2 %collective-permute-start.19 = (bf16[128,1024]{1,0:T(8,128)(2,1)S(1)}, bf16[128,1024]{1,0:T(8,128)(2,1)S(1)}, u32[]{:S(2)}, u32[]{:S(2)}) collective-permute-start(bf16[128,1024]{1,0:T(8,128)(2,1)S(1)} %get-tuple-element.103), channel_id=1, source_target_pairs={{0,12},{1,13},{2,14},{3,15},{4,0},{5,1},{6,2},{7,3},{8,4},{9,5},{1... | collective-permute-start | bytes 786440 | tf_op jit(solution)/shard_map/ppermute | solution.py:311
  154.2 8.8 %collective-permute-start.20 = (bf16[128,1024]{1,0:T(8,128)(2,1)S(1)}, bf16[128,1024]{1,0:T(8,128)(2,1)S(1)}, u32[]{:S(2)}, u32[]{:S(2)}) collective-permute-start(bf16[128,1024]{1,0:T(8,128)(2,1)S(1)} %get-tuple-element.105), channel_id=1, source_target_pairs={{0,4},{1,5},{2,6},{3,7},{4,8},{5,9},{6,10},{7,11},{8,12},{9,13},{1... | collective-permute-start | bytes 786440 | tf_op jit(solution)/shard_map/ppermute | solution.py:311
  162.9 4.5 %copy-start.1 = (bf16[2,2048,256]{2,1,0:T(8,128)(2,1)S(1)}, bf16[2,2048,256]{2,1,0:T(8,128)(2,1)}, u32[]{:S(2)}) copy-start(bf16[2,2048,256]{2,1,0:T(8,128)(2,1)} %refs_0_.5) | copy-start | bytes 6291460
  162.9 4.5 %copy-start.2 = (bf16[2,2048,256]{2,1,0:T(8,128)(2,1)S(1)}, bf16[2,2048,256]{2,1,0:T(8,128)(2,1)}, u32[]{:S(2)}) copy-start(bf16[2,2048,256]{2,1,0:T(8,128)(2,1)} %refs_1_.5) | copy-start | bytes 6291460
  162.9 4.5 %copy-start.4 = (bf16[2,2048,256]{2,1,0:T(8,128)(2,1)S(1)}, bf16[2,2048,256]{2,1,0:T(8,128)(2,1)}, u32[]{:S(2)}) copy-start(bf16[2,2048,256]{2,1,0:T(8,128)(2,1)} %copy-done.3) | copy-start | bytes 6291460
  177.9 52.1 %collective-permute-start.30 = (bf16[512,1024]{1,0:T(8,128)(2,1)S(1)}, bf16[512,1024]{1,0:T(8,128)(2,1)S(1)}, u32[]{:S(2)}, u32[]{:S(2)}) collective-permute-start(bf16[512,1024]{1,0:T(8,128)(2,1)S(1)} %get-tuple-element.134), channel_id=1, source_target_pairs={{0,2},{1,3},{2,0},{3,1},{4,6},{5,7},{6,4},{7,5},{8,10},{9,11},{10,... | collective-permute-start | bytes 3145736 | tf_op jit(solution)/shard_map/ppermute | solution.py:311
  179.5 11.2 %collective-permute-start.25 = (bf16[256,512]{1,0:T(8,128)(2,1)S(1)}, bf16[256,512]{1,0:T(8,128)(2,1)S(1)}, u32[]{:S(2)}, u32[]{:S(2)}) collective-permute-start(bf16[256,512]{1,0:T(8,128)(2,1)S(1)} %get-tuple-element.124), channel_id=1, source_target_pairs={{0,4},{1,5},{2,6},{3,7},{4,8},{5,9},{6,10},{7,11},{8,12},{9,13},{1... | collective-permute-start | bytes 786440 | tf_op jit(solution)/shard_map/ppermute | solution.py:311
  180.9 22.0 %collective-permute-start.26 = (bf16[256,512]{1,0:T(8,128)(2,1)S(1)}, bf16[256,512]{1,0:T(8,128)(2,1)S(1)}, u32[]{:S(2)}, u32[]{:S(2)}) collective-permute-start(bf16[256,512]{1,0:T(8,128)(2,1)S(1)} %get-tuple-element.125), channel_id=1, source_target_pairs={{0,12},{1,13},{2,14},{3,15},{4,0},{5,1},{6,2},{7,3},{8,4},{9,5},{1... | collective-permute-start | bytes 786440 | tf_op jit(solution)/shard_map/ppermute | solution.py:311
  183.4 19.7 %collective-permute-start.21 = (bf16[128,1024]{1,0:T(8,128)(2,1)S(1)}, bf16[128,1024]{1,0:T(8,128)(2,1)S(1)}, u32[]{:S(2)}, u32[]{:S(2)}) collective-permute-start(bf16[128,1024]{1,0:T(8,128)(2,1)S(1)} %add_piece.4), channel_id=1, source_target_pairs={{0,4},{1,5},{2,6},{3,7},{4,8},{5,9},{6,10},{7,11},{8,12},{9,13},{1... | collective-permute-start | bytes 786440 | tf_op jit(solution)/shard_map/ppermute | solution.py:311
  202.9 14.0 %collective-permute-start.27 = (bf16[256,512]{1,0:T(8,128)(2,1)S(1)}, bf16[256,512]{1,0:T(8,128)(2,1)S(1)}, u32[]{:S(2)}, u32[]{:S(2)}) collective-permute-start(bf16[256,512]{1,0:T(8,128)(2,1)S(1)} %add_piece.6), channel_id=1, source_target_pairs={{0,4},{1,5},{2,6},{3,7},{4,8},{5,9},{6,10},{7,11},{8,12},{9,13},{1... | collective-permute-start | bytes 786440 | tf_op jit(solution)/shard_map/ppermute | solution.py:311
  203.1 13.7 %collective-permute-start.24 = (bf16[128,1024]{1,0:T(8,128)(2,1)S(1)}, bf16[128,1024]{1,0:T(8,128)(2,1)S(1)}, u32[]{:S(2)}, u32[]{:S(2)}) collective-permute-start(bf16[128,1024]{1,0:T(8,128)(2,1)S(1)} %get-tuple-element.122), channel_id=1, source_target_pairs={{0,4},{1,5},{2,6},{3,7},{4,8},{5,9},{6,10},{7,11},{8,12},{9,13},{1... | collective-permute-start | bytes 786440 | tf_op jit(solution)/shard_map/ppermute | solution.py:311
  203.1 16.5 %collective-permute-start.23 = (bf16[128,1024]{1,0:T(8,128)(2,1)S(1)}, bf16[128,1024]{1,0:T(8,128)(2,1)S(1)}, u32[]{:S(2)}, u32[]{:S(2)}) collective-permute-start(bf16[128,1024]{1,0:T(8,128)(2,1)S(1)} %get-tuple-element.119), channel_id=1, source_target_pairs={{0,12},{1,13},{2,14},{3,15},{4,0},{5,1},{6,2},{7,3},{8,4},{9,5},{1... | collective-permute-start | bytes 786440 | tf_op jit(solution)/shard_map/ppermute | solution.py:311
  219.6 12.6 %collective-permute-start.28 = (bf16[128,1024]{1,0:T(8,128)(2,1)S(1)}, bf16[128,1024]{1,0:T(8,128)(2,1)S(1)}, u32[]{:S(2)}, u32[]{:S(2)}) collective-permute-start(bf16[128,1024]{1,0:T(8,128)(2,1)S(1)} %add_piece.5), channel_id=1, source_target_pairs={{0,4},{1,5},{2,6},{3,7},{4,8},{5,9},{6,10},{7,11},{8,12},{9,13},{1... | collective-permute-start | bytes 786440 | tf_op jit(solution)/shard_map/ppermute | solution.py:311
  229.4 16.1 %collective-permute-start.34 = (bf16[512,512]{1,0:T(8,128)(2,1)S(1)}, bf16[512,512]{1,0:T(8,128)(2,1)S(1)}, u32[]{:S(2)}, u32[]{:S(2)}) collective-permute-start(bf16[512,512]{1,0:T(8,128)(2,1)S(1)} %get-tuple-element.143), channel_id=1, source_target_pairs={{0,2},{1,3},{2,0},{3,1},{4,6},{5,7},{6,4},{7,5},{8,10},{9,11},{10,... | collective-permute-start | bytes 1572872 | tf_op jit(solution)/shard_map/ppermute | solution.py:311
  232.2 8.3 %collective-permute-start.32 = (bf16[128,1024]{1,0:T(8,128)(2,1)S(1)}, bf16[128,1024]{1,0:T(8,128)(2,1)S(1)}, u32[]{:S(2)}, u32[]{:S(2)}) collective-permute-start(bf16[128,1024]{1,0:T(8,128)(2,1)S(1)} %get-tuple-element.140), channel_id=1, source_target_pairs={{0,4},{1,5},{2,6},{3,7},{4,8},{5,9},{6,10},{7,11},{8,12},{9,13},{1... | collective-permute-start | bytes 786440 | tf_op jit(solution)/shard_map/ppermute | solution.py:311
  234.7 8.5 %collective-permute-start.31 = (bf16[128,1024]{1,0:T(8,128)(2,1)S(1)}, bf16[128,1024]{1,0:T(8,128)(2,1)S(1)}, u32[]{:S(2)}, u32[]{:S(2)}) collective-permute-start(bf16[128,1024]{1,0:T(8,128)(2,1)S(1)} %get-tuple-element.137), channel_id=1, source_target_pairs={{0,12},{1,13},{2,14},{3,15},{4,0},{5,1},{6,2},{7,3},{8,4},{9,5},{1... | collective-permute-start | bytes 786440 | tf_op jit(solution)/shard_map/ppermute | solution.py:311
  243.2 12.6 %collective-permute-start.33 = (bf16[128,1024]{1,0:T(8,128)(2,1)S(1)}, bf16[128,1024]{1,0:T(8,128)(2,1)S(1)}, u32[]{:S(2)}, u32[]{:S(2)}) collective-permute-start(bf16[128,1024]{1,0:T(8,128)(2,1)S(1)} %add_piece.7), channel_id=1, source_target_pairs={{0,4},{1,5},{2,6},{3,7},{4,8},{5,9},{6,10},{7,11},{8,12},{9,13},{1... | collective-permute-start | bytes 786440 | tf_op jit(solution)/shard_map/ppermute | solution.py:311
  243.8 7.3 %collective-permute-start.29 = (bf16[128,512]{1,0:T(8,128)(2,1)S(1)}, bf16[128,512]{1,0:T(8,128)(2,1)S(1)}, u32[]{:S(2)}, u32[]{:S(2)}) collective-permute-start(bf16[128,512]{1,0:T(8,128)(2,1)S(1)} %add_parts.1), channel_id=1, source_target_pairs={{0,2},{1,3},{2,0},{3,1},{4,6},{5,7},{6,4},{7,5},{8,10},{9,11},{10,... | collective-permute-start | bytes 393224 | tf_op jit(solution)/shard_map/ppermute | solution.py:311
  245.6 7.3 %collective-permute-start.35 = (bf16[128,512]{1,0:T(8,128)(2,1)S(1)}, bf16[128,512]{1,0:T(8,128)(2,1)S(1)}, u32[]{:S(2)}, u32[]{:S(2)}) collective-permute-start(bf16[128,512]{1,0:T(8,128)(2,1)S(1)} %get-tuple-element.149), channel_id=1, source_target_pairs={{0,4},{1,5},{2,6},{3,7},{4,8},{5,9},{6,10},{7,11},{8,12},{9,13},{1... | collective-permute-start | bytes 393224 | tf_op jit(solution)/shard_map/ppermute | solution.py:311
  247.7 8.0 %collective-permute-start.36 = (bf16[128,512]{1,0:T(8,128)(2,1)S(1)}, bf16[128,512]{1,0:T(8,128)(2,1)S(1)}, u32[]{:S(2)}, u32[]{:S(2)}) collective-permute-start(bf16[128,512]{1,0:T(8,128)(2,1)S(1)} %get-tuple-element.150), channel_id=1, source_target_pairs={{0,8},{1,9},{2,10},{3,11},{4,12},{5,13},{6,14},{7,15},{8,0},{9,1},... | collective-permute-start | bytes 393224 | tf_op jit(solution)/shard_map/ppermute | solution.py:311
  249.5 6.3 %collective-permute-start.37 = (bf16[128,512]{1,0:T(8,128)(2,1)S(1)}, bf16[128,512]{1,0:T(8,128)(2,1)S(1)}, u32[]{:S(2)}, u32[]{:S(2)}) collective-permute-start(bf16[128,512]{1,0:T(8,128)(2,1)S(1)} %get-tuple-element.151), channel_id=1, source_target_pairs={{0,12},{1,13},{2,14},{3,15},{4,0},{5,1},{6,2},{7,3},{8,4},{9,5},{1... | collective-permute-start | bytes 393224 | tf_op jit(solution)/shard_map/ppermute | solution.py:311

commit v9 on v7

--- a/solution.py
+++ b/solution.py
@@ -277,8 +277,8 @@
     layers = devices // 4
     experts = local_count * devices
     block = tokens.shape[0]
-    chunks = cut_columns(width, ((0, 3), (3, 6), (6, 8)))
-    back_chunks = cut_columns(width, ((4, 8), (0, 3), (3, 4)))
+    chunks = cut_columns(width, ((0, 4), (4, 8)))
+    back_chunks = cut_columns(width, ((0, 5), (6, 8), (5, 6)))
     me = lax.axis_index("expert")
     twin = [(d, d ^ 1) for d in range(devices)]
     side = [(d, d ^ 2) for d in range(devices)]
@@ -335,60 +335,53 @@
             (come,) = send_all([(piece, layer[one])], *waits)
         return far, come
 
-    def send_last(pieces, come, far):
+    def send_last(pieces, come, *waits):
         piece = pieces[0].astype(jnp.bfloat16) if come is None else add_piece(pieces[0], come)
-        return send_all([(piece, layer[one])], far)[0]
+        return send_all([(piece, layer[one])], *waits)[0]
 
     keep_0, send = mix(0, down_0, other_activ, *far_grads.values())
-    come_0, down_2 = send_all([(send, side), (downs[2], twin)], far_grads[last])
+    (come_0,) = send_all([(send, side)])
     grad_blocks = [grads[k] for k in range(layers)] + [far_grads[k] for k in range(layers)]
     own_grads = hidden_grads(grad_blocks, [down], [(0, width)], by=by)
 
     keep_1, send = mix(1, down_1, send)
-    own_0, *pieces = add_sides(keep_0, come_0, types)
-    (come_1,) = send_all([(send, side)], own_0, own_grads)
-    far_0, next_0 = send_on(pieces)
-    near_0 = send_last(pieces, next_0, far_0)
-    other_grad = hidden_grads(grad_blocks, [down_0, down_1], chunks[:2])
-
-    keep_2, send = mix(2, down_2, send, other_grad, near_0)
-    own_1, *pieces = add_sides(keep_1, come_1, types)
-    (come_2,) = send_all([(send, side)], own_1)
-    far_1, next_1 = send_on(pieces)
-
-    other_by = after(other_by, next_1, far_1)
-    other_grads = hidden_grads(grad_blocks, [down_2], chunks[2:], by=other_by, before=other_grad)
+    (come_1,) = send_all([(send, side)], own_grads)
+
+    other_by = after(other_by, send)
+    other_grads = hidden_grads(grad_blocks, [down_0, down_1], chunks, by=other_by)
     weights = [gate_weight, up_weight, other_gate, other_up]
 
     def back(c, *waits):
         lo, hi = back_chunks[c]
         return back_columns(own_grads, after(other_grads, *waits), weights, lo // (hi - lo), hi - lo)
 
+    own_0, *pieces = add_sides(after(keep_0, other_grads), come_0, types)
+    far_0, next_0 = send_on(pieces)
+    keep_2, send = back(0, next_0, far_0)
+    near_0 = send_last(pieces, next_0)
+    (come_2,) = send_all([(send, side)], own_0)
+
+    own_1, *pieces = add_sides(after(keep_1, send), come_1, types)
+    far_1, next_1 = send_on(pieces, near_0)
+    keep_3, send = back(1, next_1)
+    (come_3,) = send_all([(send, side)], own_1)
     near_1 = send_last(pieces, next_1, far_1)
-    keep_3, send = back(0)
-    (come_3,) = send_all([(send, side)])
-
-    keep_4, send = back(1, near_1)
-    own_2, *pieces = add_sides(keep_2, come_2, types)
+
+    keep_4, send = back(2, near_1)
+    own_2, *pieces = add_sides(after(keep_2, send), come_2, types)
     (come_4,) = send_all([(send, side)], own_2)
-    far_2, next_2 = send_on(pieces, far_1)
+    far_2, next_2 = send_on(pieces)
     near_2 = send_last(pieces, next_2, far_2)
 
-    keep_5, send = back(2, near_2)
-    own_3, *pieces = add_sides(keep_3, come_3, types)
-    (come_5,) = send_all([(send, side)], own_3)
-    far_3, next_3 = send_on(pieces, near_1)
+    own_3, *pieces = add_sides(keep_3, after(come_3, next_2), types)
+    far_3, next_3 = send_on(pieces)
     near_3 = send_last(pieces, next_3, far_3)
 
-    mixed = finish(chunks, [(own_0, far_0, near_0), (own_1, far_1, near_1), (own_2, far_2, near_2)], width)
-    own_4, *pieces = add_sides(keep_4, after(come_4, mixed), types)
-    far_4, next_4 = send_on(pieces, near_2)
-    near_4 = send_last(pieces, next_4, far_4)
-
+    mixed = finish(chunks, [(own_0, far_0, near_0), (own_1, far_1, near_1)], width)
     types = [jnp.float32] + [jnp.bfloat16] * (layers - 1)
-    own_5, *pieces = add_sides(keep_5, after(come_5, own_4), types)
-    parts_5 = send_all([(piece, layer[k]) for k, piece in enumerate(pieces, 1)], near_3)
-    back_parts = [(own_3, far_3, near_3), (own_4, far_4, near_4), (own_5, *parts_5)]
+    own_4, *pieces = add_sides(keep_4, after(come_4, own_3), types)
+    parts_4 = send_all([(piece, layer[k]) for k, piece in enumerate(pieces, 1)], mixed)
+    back_parts = [(own_2, far_2, near_2), (own_3, far_3, near_3), (own_4, *parts_4)]
     return (mixed, finish(back_chunks, back_parts, width))
 
 

time: 246 us -> 248 us (level)
  waiting for transfers between devices: 120 us -> 134 us
  starting transfers between devices: 58.9 us -> 53 us
  Pallas kernels: 56.9 us -> 51.8 us
    ppermute x43 -> x38, waiting for transfers between devices: 120 us -> 134 us  [send_all(): lax.ppermute(v, 'expert', pairs)]
    ppermute x43 -> x38, starting transfers between devices: 58.9 us -> 53 us  [send_all(): lax.ppermute(v, 'expert', pairs)]
    pallas_call x3 -> x2, Pallas kernels: 11.7 us -> 8.83 us  [hidden_grads(): pl.pallas_call(functools.partial(grads_kernel, blocks, tuple(cuts), by is...]
    pallas_call x6 -> x5, Pallas kernels: 22 us -> 19.9 us  [sum_columns(): pl.pallas_call(kernel, grid=(2,), in_specs=[rows, rows] + weight_specs, o...]
  transfers between devices with their start and end apart: 43 -> 38, of which waited for: 24 -> 23; matrix products, arithmetic and copies ran while one was open for 1% -> 1% of each run, Pallas kernels for 23% -> 20%
where the time goes in v9:
time: 248 us
  waiting for transfers between devices  134 us (54%)
  starting transfers between devices  53 us (21%)
  Pallas kernels  51.8 us (21%)
  local copies, waits for them, and re-layouts  6.83 us (3%)
    ppermute x38, waiting for transfers between devices, send_all(): lax.ppermute(v, 'expert', pairs)  134 us
    ppermute x38, starting transfers between devices, send_all(): lax.ppermute(v, 'expert', pairs)  53 us
    pallas_call x2, Pallas kernels, hidden_forward(): pl.pallas_call(functools.partial(hidden_kernel, blocks, all_experts), gri...  19.9 us
    pallas_call x5, Pallas kernels, sum_columns(): pl.pallas_call(kernel, grid=(2,), in_specs=[rows, rows] + weight_specs, o...  19.9 us
    pallas_call x2, Pallas kernels, hidden_grads(): pl.pallas_call(functools.partial(grads_kernel, blocks, tuple(cuts), by is...  8.83 us
  transfers between devices with their start and end apart: 38, of which 23 were waited for; matrix products, arithmetic and copies ran while one was open for 1% of the time, Pallas kernels for 20%

profile of v9, /device:TPU:0, one launch (start us, length us, event | category | flops | bytes accessed | tf_op | source)
XLA Modules:
  0.0 247.7 jit_solution(3535283620155603430)
XLA Ops:
  0.6 0.7 select_reduce_fusion
  1.6 1.2 concatenate.3.refs_0_
  2.8 3.0 %collective-permute-start.8 = (bf16[2,2048,256]{2,1,0:T(8,128)(2,1)}, bf16[2,2048,256]{2,1,0:T(8,128)(2,1)S(1)}, u32[]{:S(2)}, u32[]{:S(2)}) collective-permute-start(bf16[2,2048,256]{2,1,0:T(8,128)(2,1)} %refs_0_.5), channel_id=1, source_target_pairs={{0,1},{1,0},{2,3},{3,2},{4,5},{5,4},{6,7},{7,6},{8,9},{9,8},{10,11... | collective-permute-start | bytes 6291464 | tf_op jit(solution)/shard_map/ppermute | solution.py:271
  5.8 3.6 %collective-permute-start = (bf16[128,2176]{1,0:T(8,128)(2,1)S(1)}, bf16[128,2176]{1,0:T(8,128)(2,1)S(1)}, u32[]{:S(2)}, u32[]{:S(2)}) collective-permute-start(bf16[128,2176]{1,0:T(8,128)(2,1)S(1)} %concatenate.3.refs_0_), channel_id=1, source_target_pairs={{0,12},{1,13},{2,14},{3,15},{4,0},{5,1},{6,2},{7,3},{8,4},{9,5},{1... | collective-permute-start | bytes 1671176 | tf_op jit(solution)/shard_map/ppermute | solution.py:271
  9.4 1.5 collective-permute-start.1
  11.5 11.0 %collective-permute-done.refs_1_ = bf16[128,2176]{1,0:T(8,128)(2,1)S(1)} collective-permute-done((bf16[128,2176]{1,0:T(8,128)(2,1)S(1)}, bf16[128,2176]{1,0:T(8,128)(2,1)S(1)}, u32[]{:S(2)}, u32[]{:S(2)}) %collective-permute-start) | collective-permute-done | bytes 557088 | tf_op jit(solution)/shard_map/ppermute | solution.py:271
  22.5 2.5 %collective-permute-done.1.refs_4_ = bf16[128,2176]{1,0:T(8,128)(2,1)S(1)} collective-permute-done((bf16[128,2176]{1,0:T(8,128)(2,1)S(1)}, bf16[128,2176]{1,0:T(8,128)(2,1)S(1)}, u32[]{:S(2)}, u32[]{:S(2)}) %collective-permute-start.1) | collective-permute-done | bytes 557088 | tf_op jit(solution)/shard_map/ppermute | solution.py:271
  25.0 1.5 collective-permute-start.4
  26.5 1.9 collective-permute-start.2
  28.4 7.9 %collective-permute-done.6.refs_7_.refs_6_ = bf16[128,2048]{1,0:T(8,128)(2,1)S(1)} collective-permute-done((bf16[128,2048]{1,0:T(8,128)(2,1)}, bf16[128,2048]{1,0:T(8,128)(2,1)S(1)}, u32[]{:S(2)}, u32[]{:S(2)}) %collective-permute-start.6) | collective-permute-done | bytes 524320 | tf_op jit(solution)/shard_map/ppermute | solution.py:271
  36.2 0.8 copy-done.10
  37.6 1.5 collective-permute-start.7
  39.1 9.0 %collective-permute-done.4.refs_5_ = bf16[128,2176]{1,0:T(8,128)(2,1)S(1)} collective-permute-done((bf16[128,2176]{1,0:T(8,128)(2,1)S(1)}, bf16[128,2176]{1,0:T(8,128)(2,1)S(1)}, u32[]{:S(2)}, u32[]{:S(2)}) %collective-permute-start.4) | collective-permute-done | bytes 557088 | tf_op jit(solution)/shard_map/ppermute | solution.py:271
  48.2 1.6 collective-permute-start.5
  49.8 1.0 collective-permute-start.11
  50.8 3.0 %fusion.1 = (bf16[512,1024]{1,0:T(8,128)(2,1)}, bf16[512,1024]{1,0:T(8,128)(2,1)}) fusion(bf16[512,2048]{1,0:T(8,128)(2,1)} %bitcast.3), kind=kLoop, calls=%fused_computation.5 | loop fusion | bytes 4194304 | tf_op jit(solution)/shard_map/slice | solution.py:297
  53.8 6.3 %collective-permute-done.7.refs_7_ = bf16[128,2176]{1,0:T(8,128)(2,1)S(1)} collective-permute-done((bf16[128,2176]{1,0:T(8,128)(2,1)S(1)}, bf16[128,2176]{1,0:T(8,128)(2,1)S(1)}, u32[]{:S(2)}, u32[]{:S(2)}) %collective-permute-start.7) | collective-permute-done | bytes 557088 | tf_op jit(solution)/shard_map/ppermute | solution.py:271
  60.1 0.6 collective-permute-start.10
  61.3 9.0 %collective-permute-done.5.refs_6_ = bf16[128,2176]{1,0:T(8,128)(2,1)S(1)} collective-permute-done((bf16[128,2176]{1,0:T(8,128)(2,1)S(1)}, bf16[128,2176]{1,0:T(8,128)(2,1)S(1)}, u32[]{:S(2)}, u32[]{:S(2)}) %collective-permute-start.5) | collective-permute-done | bytes 557088 | tf_op jit(solution)/shard_map/ppermute | solution.py:271
  71.1 1.5 collective-permute-start.12
  72.6 1.2 collective-permute-start.13
  73.8 9.9 %hidden_forward.2 = (bf16[1024,512]{1,0:T(8,128)(2,1)}, f32[1024,1024]{1,0:T(8,128)}) custom-call(s32[1]{0:T(128)} %bitcast.owner_ref, bf16[2,2048,256]{2,1,0:T(8,128)(2,1)} %refs_0_.5, bf16[2,2048,256]{2,1,0:T(8,128)(2,1)} %refs_1_.5, bf16[128,2176]{1,0:T(8,128)(2,1)} %copy-done.12, bf16[128,2176]{1,0:T(8,128)(2,1)} %copy-done.13, ...), custom_call_target="tpu_custom_call" | custom-call | flops 1 | bytes 1 | tf_op jit(solution)/shard_map/hidden_forward/pallas_call | solution.py:71
  83.8 10.4 %collective-permute-done.15.refs_5_.refs_4_ = bf16[128,2048]{1,0:T(8,128)(2,1)} collective-permute-done((bf16[128,2048]{1,0:T(8,128)(2,1)}, bf16[128,2048]{1,0:T(8,128)(2,1)}, u32[]{:S(2)}, u32[]{:S(2)}) %collective-permute-start.15) | collective-permute-done | bytes 524320 | tf_op jit(solution)/shard_map/ppermute | solution.py:271
  94.1 1.5 collective-permute-start.16
  96.2 1.4 collective-permute-done.9.up_ref.refs_3_
  97.5 10.0 %hidden_forward.3 = (bf16[1024,512]{1,0:T(8,128)(2,1)}, f32[1024,1024]{1,0:T(8,128)}) custom-call(s32[1]{0:T(128)} %bitcast.1.owner_ref, bf16[2,2048,256]{2,1,0:T(8,128)(2,1)} %copy-done.3, bf16[2,2048,256]{2,1,0:T(8,128)(2,1)} %collective-permute-done.9.up_ref.refs_3_, bf16[128,2176]{1,0:T(8,128)(2,1)} %copy-done.12, bf16[128,2176]{1,0:T(8,128)(2,1)} %copy-done.13, ...), custom_call_target="tpu_custom_call" | custom-call | flops 1 | bytes 1 | tf_op jit(solution)/shard_map/hidden_forward/pallas_call | solution.py:71
  107.6 11.5 %collective-permute-done.10.other_down_ref.refs_1_ = bf16[512,1024]{1,0:T(8,128)(2,1)S(1)} collective-permute-done((bf16[512,1024]{1,0:T(8,128)(2,1)}, bf16[512,1024]{1,0:T(8,128)(2,1)S(1)}, u32[]{:S(2)}, u32[]{:S(2)}) %collective-permute-start.10) | collective-permute-done | bytes 1048608 | tf_op jit(solution)/shard_map/ppermute | solution.py:271
  119.1 1.7 collective-permute-start.17
  120.9 1.2 copy-done.8
  122.1 2.8 %mix_columns.2 = (f32[512,1024]{1,0:T(8,128)S(1)}, bf16[512,1024]{1,0:T(8,128)(2,1)S(1)}) custom-call(bf16[1024,512]{1,0:T(8,128)(2,1)S(1)} %copy-done.7, bf16[1024,512]{1,0:T(8,128)(2,1)S(1)} %copy-done.8, bf16[512,2048]{1,0:T(8,128)(2,1)S(1)} %bitcast.4, bf16[512,1024]{1,0:T(8,128)(2,1)S(1)} %collective-permute-done.10.other_down_ref.refs_1_), custom_call_target="tpu_custom_call" | custom-call | flops 1 | bytes 1 | tf_op jit(solution)/shard_map/mix_columns/pallas_call | solution.py:179
  124.9 1.6 collective-permute-start.18
  126.5 4.4 %hidden_grads.3.own_ref = bf16[1024,1024]{1,0:T(8,128)(2,1)S(1)} custom-call(f32[1024,1024]{1,0:T(8,128)S(1)} %copy-done.5, bf16[512,2048]{1,0:T(8,128)(2,1)S(1)} %bitcast.5, bf16[128,2048]{1,0:T(8,128)(2,1)} %refs_2_.1, bf16[128,2048]{1,0:T(8,128)(2,1)} %collective-permute-done.11.refs_4_.refs_3_, ...), custom_call_target="tpu_custom_call" | custom-call | flops 1 | bytes 1 | tf_op jit(solution)/shard_map/hidden_grads/pallas_call | solution.py:127
  130.9 12.7 %collective-permute-done.17.other_down_ref.refs_2_ = bf16[512,1024]{1,0:T(8,128)(2,1)S(1)} collective-permute-done((bf16[512,1024]{1,0:T(8,128)(2,1)}, bf16[512,1024]{1,0:T(8,128)(2,1)S(1)}, u32[]{:S(2)}, u32[]{:S(2)}) %collective-permute-start.17) | collective-permute-done | bytes 1048608 | tf_op jit(solution)/shard_map/ppermute | solution.py:271
  143.6 2.8 %mix_columns.3 = (f32[512,1024]{1,0:T(8,128)S(1)}, bf16[512,1024]{1,0:T(8,128)(2,1)S(1)}) custom-call(bf16[1024,512]{1,0:T(8,128)(2,1)S(1)} %copy-done.7, bf16[1024,512]{1,0:T(8,128)(2,1)S(1)} %copy-done.9, bf16[512,2048]{1,0:T(8,128)(2,1)S(1)} %bitcast.6, bf16[512,1024]{1,0:T(8,128)(2,1)S(1)} %collective-permute-done.17.other_down_ref.refs_2_), custom_call_target="tpu_custom_call" | custom-call | flops 1 | bytes 1 | tf_op jit(solution)/shard_map/mix_columns/pallas_call | solution.py:179
  146.5 1.5 collective-permute-start.22
  148.0 4.4 %hidden_grads.2.other_ref = bf16[1024,1024]{1,0:T(8,128)(2,1)S(1)} custom-call(f32[1024,1024]{1,0:T(8,128)S(1)} %copy-done.6, bf16[512,1024]{1,0:T(8,128)(2,1)S(1)} %collective-permute-done.10.other_down_ref.refs_1_, bf16[512,1024]{1,0:T(8,128)(2,1)S(1)} %collective-permute-done.17.other_down_ref.refs_2_, bf16[128,2048]{1,0:T(8,128)(2,1)} %refs_2_.1, ...), custom_call_target="tpu_custom_call" | custom-call | flops 1 | bytes 1 | tf_op jit(solution)/shard_map/hidden_grads/pallas_call | solution.py:127
  152.7 3.6 %collective-permute-start.19 = (bf16[128,1024]{1,0:T(8,128)(2,1)S(1)}, bf16[128,1024]{1,0:T(8,128)(2,1)S(1)}, u32[]{:S(2)}, u32[]{:S(2)}) collective-permute-start(bf16[128,1024]{1,0:T(8,128)(2,1)S(1)} %get-tuple-element.104), channel_id=1, source_target_pairs={{0,12},{1,13},{2,14},{3,15},{4,0},{5,1},{6,2},{7,3},{8,4},{9,5},{1... | collective-permute-start | bytes 786440 | tf_op jit(solution)/shard_map/ppermute | solution.py:271
  156.3 6.3 %collective-permute-done.19.refs_1_ = bf16[128,1024]{1,0:T(8,128)(2,1)S(1)} collective-permute-done((bf16[128,1024]{1,0:T(8,128)(2,1)S(1)}, bf16[128,1024]{1,0:T(8,128)(2,1)S(1)}, u32[]{:S(2)}, u32[]{:S(2)}) %collective-permute-start.19) | collective-permute-done | bytes 262176 | tf_op jit(solution)/shard_map/ppermute | solution.py:271
  162.7 4.0 %collective-permute-done.20.come_ref = bf16[128,1024]{1,0:T(8,128)(2,1)S(1)} collective-permute-done((bf16[128,1024]{1,0:T(8,128)(2,1)S(1)}, bf16[128,1024]{1,0:T(8,128)(2,1)S(1)}, u32[]{:S(2)}, u32[]{:S(2)}) %collective-permute-start.20) | collective-permute-done | bytes 262176 | tf_op jit(solution)/shard_map/ppermute | solution.py:271
  166.6 7.8 %back_columns.3 = (f32[512,1280]{1,0:T(8,128)S(1)}, bf16[512,1280]{1,0:T(8,128)(2,1)S(1)}) custom-call(bf16[1024,1024]{1,0:T(8,128)(2,1)S(1)} %hidden_grads.3.own_ref, bf16[1024,1024]{1,0:T(8,128)(2,1)S(1)} %hidden_grads.2.other_ref, bf16[2,2048,256]{2,1,0:T(8,128)(2,1)S(1)} %copy-done.1, bf16[2,2048,256]{2,1,0:T(8,128)(2,1)S(1)} %copy-done.2, ...), custom_call_target="tpu_custom_call" | custom-call | flops 1 | bytes 1 | tf_op jit(solution)/shard_map/back_columns/pallas_call | solution.py:179
  175.1 1.4 collective-permute-start.21
  176.6 7.0 %collective-permute-done.21.refs_2_ = bf16[128,1024]{1,0:T(8,128)(2,1)S(1)} collective-permute-done((bf16[128,1024]{1,0:T(8,128)(2,1)S(1)}, bf16[128,1024]{1,0:T(8,128)(2,1)S(1)}, u32[]{:S(2)}, u32[]{:S(2)}) %collective-permute-start.21) | collective-permute-done | bytes 262176 | tf_op jit(solution)/shard_map/ppermute | solution.py:271
  183.9 3.5 %collective-permute-start.23 = (bf16[128,1024]{1,0:T(8,128)(2,1)S(1)}, bf16[128,1024]{1,0:T(8,128)(2,1)S(1)}, u32[]{:S(2)}, u32[]{:S(2)}) collective-permute-start(bf16[128,1024]{1,0:T(8,128)(2,1)S(1)} %get-tuple-element.115), channel_id=1, source_target_pairs={{0,12},{1,13},{2,14},{3,15},{4,0},{5,1},{6,2},{7,3},{8,4},{9,5},{1... | collective-permute-start | bytes 786440 | tf_op jit(solution)/shard_map/ppermute | solution.py:271
  187.4 4.5 %collective-permute-done.24.come_ref = bf16[128,1024]{1,0:T(8,128)(2,1)S(1)} collective-permute-done((bf16[128,1024]{1,0:T(8,128)(2,1)S(1)}, bf16[128,1024]{1,0:T(8,128)(2,1)S(1)}, u32[]{:S(2)}, u32[]{:S(2)}) %collective-permute-start.24) | collective-permute-done | bytes 262176 | tf_op jit(solution)/shard_map/ppermute | solution.py:271
  192.0 2.6 %collective-permute-done.23.refs_4_ = bf16[128,1024]{1,0:T(8,128)(2,1)S(1)} collective-permute-done((bf16[128,1024]{1,0:T(8,128)(2,1)S(1)}, bf16[128,1024]{1,0:T(8,128)(2,1)S(1)}, u32[]{:S(2)}, u32[]{:S(2)}) %collective-permute-start.23) | collective-permute-done | bytes 262176 | tf_op jit(solution)/shard_map/ppermute | solution.py:271
  194.9 3.9 %back_columns.5 = (f32[512,512]{1,0:T(8,128)S(1)}, bf16[512,512]{1,0:T(8,128)(2,1)S(1)}) custom-call(bf16[1024,1024]{1,0:T(8,128)(2,1)S(1)} %hidden_grads.3.own_ref, bf16[1024,1024]{1,0:T(8,128)(2,1)S(1)} %hidden_grads.2.other_ref, bf16[2,2048,256]{2,1,0:T(8,128)(2,1)S(1)} %copy-done.1, bf16[2,2048,256]{2,1,0:T(8,128)(2,1)S(1)} %copy-done.2, ...), custom_call_target="tpu_custom_call" | custom-call | flops 1 | bytes 1 | tf_op jit(solution)/shard_map/back_columns/pallas_call | solution.py:179
  198.8 1.7 collective-permute-start.30
  200.5 2.9 %collective-permute-done.25.refs_5_ = bf16[128,1024]{1,0:T(8,128)(2,1)S(1)} collective-permute-done((bf16[128,1024]{1,0:T(8,128)(2,1)S(1)}, bf16[128,1024]{1,0:T(8,128)(2,1)S(1)}, u32[]{:S(2)}, u32[]{:S(2)}) %collective-permute-start.25) | collective-permute-done | bytes 262176 | tf_op jit(solution)/shard_map/ppermute | solution.py:271
  203.4 2.6 %back_columns.4 = (f32[512,256]{1,0:T(8,128)S(1)}, bf16[512,256]{1,0:T(8,128)(2,1)S(1)}) custom-call(bf16[1024,1024]{1,0:T(8,128)(2,1)S(1)} %hidden_grads.3.own_ref, bf16[1024,1024]{1,0:T(8,128)(2,1)S(1)} %hidden_grads.2.other_ref, bf16[2,2048,256]{2,1,0:T(8,128)(2,1)S(1)} %copy-done.1, bf16[2,2048,256]{2,1,0:T(8,128)(2,1)S(1)} %copy-done.2, ...), custom_call_target="tpu_custom_call" | custom-call | flops 1 | bytes 1 | tf_op jit(solution)/shard_map/back_columns/pallas_call | solution.py:179
  206.6 3.4 %collective-permute-start.27 = (bf16[128,1280]{1,0:T(8,128)(2,1)S(1)}, bf16[128,1280]{1,0:T(8,128)(2,1)S(1)}, u32[]{:S(2)}, u32[]{:S(2)}) collective-permute-start(bf16[128,1280]{1,0:T(8,128)(2,1)S(1)} %get-tuple-element.126), channel_id=1, source_target_pairs={{0,12},{1,13},{2,14},{3,15},{4,0},{5,1},{6,2},{7,3},{8,4},{9,5},{1... | collective-permute-start | bytes 983048 | tf_op jit(solution)/shard_map/ppermute | solution.py:271
  210.1 1.4 collective-permute-start.34
  211.5 7.2 %collective-permute-done.28.come_ref = bf16[128,1280]{1,0:T(8,128)(2,1)S(1)} collective-permute-done((bf16[128,1280]{1,0:T(8,128)(2,1)S(1)}, bf16[128,1280]{1,0:T(8,128)(2,1)S(1)}, u32[]{:S(2)}, u32[]{:S(2)}) %collective-permute-start.28) | collective-permute-done | bytes 327712 | tf_op jit(solution)/shard_map/ppermute | solution.py:271
  218.8 2.0 collective-permute-done.27.refs_1_
  220.9 3.0 %collective-permute-start.32 = (bf16[128,512]{1,0:T(8,128)(2,1)S(1)}, bf16[128,512]{1,0:T(8,128)(2,1)S(1)}, u32[]{:S(2)}, u32[]{:S(2)}) collective-permute-start(bf16[128,512]{1,0:T(8,128)(2,1)S(1)} %get-tuple-element.138), channel_id=1, source_target_pairs={{0,4},{1,5},{2,6},{3,7},{4,8},{5,9},{6,10},{7,11},{8,12},{9,13},{1... | collective-permute-start | bytes 393224 | tf_op jit(solution)/shard_map/ppermute | solution.py:271
  223.8 1.0 collective-permute-start.31
  224.8 9.9 %collective-permute-done.32.come_ref = bf16[128,512]{1,0:T(8,128)(2,1)S(1)} collective-permute-done((bf16[128,512]{1,0:T(8,128)(2,1)S(1)}, bf16[128,512]{1,0:T(8,128)(2,1)S(1)}, u32[]{:S(2)}, u32[]{:S(2)}) %collective-permute-start.32) | collective-permute-done | bytes 131104 | tf_op jit(solution)/shard_map/ppermute | solution.py:271
  234.8 0.7 collective-permute-done.31.refs_4_
  235.5 1.1 collective-permute-start.33
  236.5 1.1 finish.2
  237.7 0.7 collective-permute-start.35
  238.4 2.7 %collective-permute-start.36 = (bf16[128,256]{1,0:T(8,128)(2,1)S(1)}, bf16[128,256]{1,0:T(8,128)(2,1)S(1)}, u32[]{:S(2)}, u32[]{:S(2)}) collective-permute-start(bf16[128,256]{1,0:T(8,128)(2,1)S(1)} %get-tuple-element.148), channel_id=1, source_target_pairs={{0,8},{1,9},{2,10},{3,11},{4,12},{5,13},{6,14},{7,15},{8,0},{9,1},... | collective-permute-start | bytes 196616 | tf_op jit(solution)/shard_map/ppermute | solution.py:271
  241.6 3.0 %collective-permute-done.35.refs_7_ = bf16[128,256]{1,0:T(8,128)(2,1)S(1)} collective-permute-done((bf16[128,256]{1,0:T(8,128)(2,1)S(1)}, bf16[128,256]{1,0:T(8,128)(2,1)S(1)}, u32[]{:S(2)}, u32[]{:S(2)}) %collective-permute-start.35) | collective-permute-done | bytes 65568 | tf_op jit(solution)/shard_map/ppermute | solution.py:271
  244.5 2.0 collective-permute-done.36.refs_8_
  246.5 1.1 finish.3
  (80 shorter events, 6.4 us)
Async XLA Ops:
  2.8 57.3 %copy-start.12 = (bf16[128,2176]{1,0:T(8,128)(2,1)}, bf16[128,2176]{1,0:T(8,128)(2,1)S(1)}, u32[]{:S(2)}) copy-start(bf16[128,2176]{1,0:T(8,128)(2,1)S(1)} %concatenate.3.refs_0_) | copy-start | bytes 1671172
  2.8 57.3 %collective-permute-start.8 = (bf16[2,2048,256]{2,1,0:T(8,128)(2,1)}, bf16[2,2048,256]{2,1,0:T(8,128)(2,1)S(1)}, u32[]{:S(2)}, u32[]{:S(2)}) collective-permute-start(bf16[2,2048,256]{2,1,0:T(8,128)(2,1)} %refs_0_.5), channel_id=1, source_target_pairs={{0,1},{1,0},{2,3},{3,2},{4,5},{5,4},{6,7},{7,6},{8,9},{9,8},{10,11... | collective-permute-start | bytes 6291464 | tf_op jit(solution)/shard_map/ppermute | solution.py:271
  5.8 16.7 %collective-permute-start = (bf16[128,2176]{1,0:T(8,128)(2,1)S(1)}, bf16[128,2176]{1,0:T(8,128)(2,1)S(1)}, u32[]{:S(2)}, u32[]{:S(2)}) collective-permute-start(bf16[128,2176]{1,0:T(8,128)(2,1)S(1)} %concatenate.3.refs_0_), channel_id=1, source_target_pairs={{0,12},{1,13},{2,14},{3,15},{4,0},{5,1},{6,2},{7,3},{8,4},{9,5},{1... | collective-permute-start | bytes 1671176 | tf_op jit(solution)/shard_map/ppermute | solution.py:271
  9.4 15.6 %collective-permute-start.1 = (bf16[128,2176]{1,0:T(8,128)(2,1)S(1)}, bf16[128,2176]{1,0:T(8,128)(2,1)S(1)}, u32[]{:S(2)}, u32[]{:S(2)}) collective-permute-start(bf16[128,2176]{1,0:T(8,128)(2,1)S(1)} %concatenate.3.refs_0_), channel_id=1, source_target_pairs={{0,2},{1,3},{2,0},{3,1},{4,6},{5,7},{6,4},{7,5},{8,10},{9,11},{10,... | collective-permute-start | bytes 1671176 | tf_op jit(solution)/shard_map/ppermute | solution.py:271
  10.9 26.1 %collective-permute-start.3 = (bf16[128,2176]{1,0:T(8,128)(2,1)S(1)}, bf16[128,2176]{1,0:T(8,128)(2,1)S(1)}, u32[]{:S(2)}, u32[]{:S(2)}) collective-permute-start(bf16[128,2176]{1,0:T(8,128)(2,1)S(1)} %concatenate.3.refs_0_), channel_id=1, source_target_pairs={{0,4},{1,5},{2,6},{3,7},{4,8},{5,9},{6,10},{7,11},{8,12},{9,13},{1... | collective-permute-start | bytes 1671176 | tf_op jit(solution)/shard_map/ppermute | solution.py:271
  10.9 25.3 %collective-permute-start.6 = (bf16[128,2048]{1,0:T(8,128)(2,1)}, bf16[128,2048]{1,0:T(8,128)(2,1)S(1)}, u32[]{:S(2)}, u32[]{:S(2)}) collective-permute-start(bf16[128,2048]{1,0:T(8,128)(2,1)} %refs_2_.1), channel_id=1, source_target_pairs={{0,2},{1,3},{2,0},{3,1},{4,6},{5,7},{6,4},{7,5},{8,10},{9,11},{10,... | collective-permute-start | bytes 1572872 | tf_op jit(solution)/shard_map/ppermute | solution.py:271
  22.5 14.5 %copy-start.13 = (bf16[128,2176]{1,0:T(8,128)(2,1)}, bf16[128,2176]{1,0:T(8,128)(2,1)S(1)}, u32[]{:S(2)}) copy-start(bf16[128,2176]{1,0:T(8,128)(2,1)S(1)} %collective-permute-done.refs_1_) | copy-start | bytes 1671172
  25.0 23.2 %copy-start.14 = (bf16[128,2176]{1,0:T(8,128)(2,1)}, bf16[128,2176]{1,0:T(8,128)(2,1)S(1)}, u32[]{:S(2)}) copy-start(bf16[128,2176]{1,0:T(8,128)(2,1)S(1)} %collective-permute-done.1.refs_4_) | copy-start | bytes 1671172
  25.0 23.2 %collective-permute-start.4 = (bf16[128,2176]{1,0:T(8,128)(2,1)S(1)}, bf16[128,2176]{1,0:T(8,128)(2,1)S(1)}, u32[]{:S(2)}, u32[]{:S(2)}) collective-permute-start(bf16[128,2176]{1,0:T(8,128)(2,1)S(1)} %collective-permute-done.refs_1_), channel_id=1, source_target_pairs={{0,2},{1,3},{2,0},{3,1},{4,6},{5,7},{6,4},{7,5},{8,10},{9,11},{10,... | collective-permute-start | bytes 1671176 | tf_op jit(solution)/shard_map/ppermute | solution.py:271
  26.5 21.7 %collective-permute-start.2 = (bf16[128,2176]{1,0:T(8,128)(2,1)S(1)}, bf16[128,2176]{1,0:T(8,128)(2,1)S(1)}, u32[]{:S(2)}, u32[]{:S(2)}) collective-permute-start(bf16[128,2176]{1,0:T(8,128)(2,1)S(1)} %collective-permute-done.refs_1_), channel_id=1, source_target_pairs={{0,12},{1,13},{2,14},{3,15},{4,0},{5,1},{6,2},{7,3},{8,4},{9,5},{1... | collective-permute-start | bytes 1671176 | tf_op jit(solution)/shard_map/ppermute | solution.py:271
  36.2 0.8 copy-start.10
  37.0 16.8 %copy-start.15 = (bf16[128,2176]{1,0:T(8,128)(2,1)}, bf16[128,2176]{1,0:T(8,128)(2,1)S(1)}, u32[]{:S(2)}) copy-start(bf16[128,2176]{1,0:T(8,128)(2,1)S(1)} %collective-permute-done.3.refs_3_) | copy-start | bytes 1671172
  37.0 60.5 %collective-permute-start.9 = (bf16[2,2048,256]{2,1,0:T(8,128)(2,1)}, bf16[2,2048,256]{2,1,0:T(8,128)(2,1)}, u32[]{:S(2)}, u32[]{:S(2)}) collective-permute-start(bf16[2,2048,256]{2,1,0:T(8,128)(2,1)} %refs_1_.5), channel_id=1, source_target_pairs={{0,1},{1,0},{2,3},{3,2},{4,5},{5,4},{6,7},{7,6},{8,9},{9,8},{10,11... | collective-permute-start | bytes 6291464 | tf_op jit(solution)/shard_map/ppermute | solution.py:271
  37.6 22.5 %collective-permute-start.7 = (bf16[128,2176]{1,0:T(8,128)(2,1)S(1)}, bf16[128,2176]{1,0:T(8,128)(2,1)S(1)}, u32[]{:S(2)}, u32[]{:S(2)}) collective-permute-start(bf16[128,2176]{1,0:T(8,128)(2,1)S(1)} %collective-permute-done.3.refs_3_), channel_id=1, source_target_pairs={{0,2},{1,3},{2,0},{3,1},{4,6},{5,7},{6,4},{7,5},{8,10},{9,11},{10,... | collective-permute-start | bytes 1671176 | tf_op jit(solution)/shard_map/ppermute | solution.py:271
  48.2 1.6 copy-start.16
  48.2 5.6 %copy-start.17 = (bf16[128,2176]{1,0:T(8,128)(2,1)}, bf16[128,2176]{1,0:T(8,128)(2,1)S(1)}, u32[]{:S(2)}) copy-start(bf16[128,2176]{1,0:T(8,128)(2,1)S(1)} %collective-permute-done.2.refs_2_) | copy-start | bytes 1671172
  48.2 22.1 %collective-permute-start.5 = (bf16[128,2176]{1,0:T(8,128)(2,1)S(1)}, bf16[128,2176]{1,0:T(8,128)(2,1)S(1)}, u32[]{:S(2)}, u32[]{:S(2)}) collective-permute-start(bf16[128,2176]{1,0:T(8,128)(2,1)S(1)} %collective-permute-done.2.refs_2_), channel_id=1, source_target_pairs={{0,2},{1,3},{2,0},{3,1},{4,6},{5,7},{6,4},{7,5},{8,10},{9,11},{10,... | collective-permute-start | bytes 1671176 | tf_op jit(solution)/shard_map/ppermute | solution.py:271
  49.8 11.5 %collective-permute-start.11 = (bf16[128,2048]{1,0:T(8,128)(2,1)}, bf16[128,2048]{1,0:T(8,128)(2,1)}, u32[]{:S(2)}, u32[]{:S(2)}) collective-permute-start(bf16[128,2048]{1,0:T(8,128)(2,1)} %refs_2_.1), channel_id=1, source_target_pairs={{0,12},{1,13},{2,14},{3,15},{4,0},{5,1},{6,2},{7,3},{8,4},{9,5},{1... | collective-permute-start | bytes 1572872 | tf_op jit(solution)/shard_map/ppermute | solution.py:271
  60.1 10.2 %copy-start.18 = (bf16[128,2176]{1,0:T(8,128)(2,1)}, bf16[128,2176]{1,0:T(8,128)(2,1)S(1)}, u32[]{:S(2)}) copy-start(bf16[128,2176]{1,0:T(8,128)(2,1)S(1)} %collective-permute-done.7.refs_7_) | copy-start | bytes 1671172
  60.1 23.6 %copy-start.3 = (bf16[2,2048,256]{2,1,0:T(8,128)(2,1)}, bf16[2,2048,256]{2,1,0:T(8,128)(2,1)S(1)}, u32[]{:S(2)}) copy-start(bf16[2,2048,256]{2,1,0:T(8,128)(2,1)S(1)} %collective-permute-done.8.gate_ref.refs_2_) | copy-start | bytes 6291460
  60.1 59.0 %collective-permute-start.10 = (bf16[512,1024]{1,0:T(8,128)(2,1)}, bf16[512,1024]{1,0:T(8,128)(2,1)S(1)}, u32[]{:S(2)}, u32[]{:S(2)}) collective-permute-start(bf16[512,1024]{1,0:T(8,128)(2,1)} %get-tuple-element.88), channel_id=1, source_target_pairs={{0,1},{1,0},{2,3},{3,2},{4,5},{5,4},{6,7},{7,6},{8,9},{9,8},{10,11... | collective-permute-start | bytes 3145736 | tf_op jit(solution)/shard_map/ppermute | solution.py:271
  70.3 0.8 copy-start.19
  70.3 23.8 %collective-permute-start.15 = (bf16[128,2048]{1,0:T(8,128)(2,1)}, bf16[128,2048]{1,0:T(8,128)(2,1)}, u32[]{:S(2)}, u32[]{:S(2)}) collective-permute-start(bf16[128,2048]{1,0:T(8,128)(2,1)} %collective-permute-done.11.refs_4_.refs_3_), channel_id=1, source_target_pairs={{0,12},{1,13},{2,14},{3,15},{4,0},{5,1},{6,2},{7,3},{8,4},{9,5},{1... | collective-permute-start | bytes 1572872 | tf_op jit(solution)/shard_map/ppermute | solution.py:271
  71.1 23.0 %collective-permute-start.12 = (bf16[128,2048]{1,0:T(8,128)(2,1)}, bf16[128,2048]{1,0:T(8,128)(2,1)}, u32[]{:S(2)}, u32[]{:S(2)}) collective-permute-start(bf16[128,2048]{1,0:T(8,128)(2,1)} %collective-permute-done.11.refs_4_.refs_3_), channel_id=1, source_target_pairs={{0,2},{1,3},{2,0},{3,1},{4,6},{5,7},{6,4},{7,5},{8,10},{9,11},{10,... | collective-permute-start | bytes 1572872 | tf_op jit(solution)/shard_map/ppermute | solution.py:271
  72.6 23.0 %collective-permute-start.13 = (bf16[128,2048]{1,0:T(8,128)(2,1)}, bf16[128,2048]{1,0:T(8,128)(2,1)}, u32[]{:S(2)}, u32[]{:S(2)}) collective-permute-start(bf16[128,2048]{1,0:T(8,128)(2,1)} %refs_2_.1), channel_id=1, source_target_pairs={{0,4},{1,5},{2,6},{3,7},{4,8},{5,9},{6,10},{7,11},{8,12},{9,13},{1... | collective-permute-start | bytes 1572872 | tf_op jit(solution)/shard_map/ppermute | solution.py:271
  94.1 26.7 %collective-permute-start.16 = (bf16[128,2048]{1,0:T(8,128)(2,1)}, bf16[128,2048]{1,0:T(8,128)(2,1)S(1)}, u32[]{:S(2)}, u32[]{:S(2)}) collective-permute-start(bf16[128,2048]{1,0:T(8,128)(2,1)} %collective-permute-done.15.refs_5_.refs_4_), channel_id=1, source_target_pairs={{0,2},{1,3},{2,0},{3,1},{4,6},{5,7},{6,4},{7,5},{8,10},{9,11},{10,... | collective-permute-start | bytes 1572872 | tf_op jit(solution)/shard_map/ppermute | solution.py:271
  95.6 25.2 %collective-permute-start.14 = (bf16[128,2048]{1,0:T(8,128)(2,1)}, bf16[128,2048]{1,0:T(8,128)(2,1)S(1)}, u32[]{:S(2)}, u32[]{:S(2)}) collective-permute-start(bf16[128,2048]{1,0:T(8,128)(2,1)} %collective-permute-done.13.refs_6_.refs_5_), channel_id=1, source_target_pairs={{0,2},{1,3},{2,0},{3,1},{4,6},{5,7},{6,4},{7,5},{8,10},{9,11},{10,... | collective-permute-start | bytes 1572872 | tf_op jit(solution)/shard_map/ppermute | solution.py:271
  97.5 23.3 %copy-start = (bf16[2,256,2048]{2,1,0:T(8,128)(2,1)S(1)}, bf16[2,256,2048]{2,1,0:T(8,128)(2,1)}, u32[]{:S(2)}) copy-start(bf16[2,256,2048]{2,1,0:T(8,128)(2,1)} %param.13) | copy-start | bytes 6291460
  97.5 23.3 %copy-start.7 = (bf16[1024,512]{1,0:T(8,128)(2,1)S(1)}, bf16[1024,512]{1,0:T(8,128)(2,1)}, u32[]{:S(2)}) copy-start(bf16[1024,512]{1,0:T(8,128)(2,1)} %get-tuple-element.83.own_ref) | copy-start | bytes 3145732
  119.1 7.4 %copy-start.5 = (f32[1024,1024]{1,0:T(8,128)S(1)}, f32[1024,1024]{1,0:T(8,128)}, u32[]{:S(2)}) copy-start(f32[1024,1024]{1,0:T(8,128)} %get-tuple-element.108.refs_0_) | copy-start | bytes 12582916
  119.1 24.6 %collective-permute-start.17 = (bf16[512,1024]{1,0:T(8,128)(2,1)}, bf16[512,1024]{1,0:T(8,128)(2,1)S(1)}, u32[]{:S(2)}, u32[]{:S(2)}) collective-permute-start(bf16[512,1024]{1,0:T(8,128)(2,1)} %get-tuple-element.97), channel_id=1, source_target_pairs={{0,1},{1,0},{2,3},{3,2},{4,5},{5,4},{6,7},{7,6},{8,9},{9,8},{10,11... | collective-permute-start | bytes 3145736 | tf_op jit(solution)/shard_map/ppermute | solution.py:271
  120.8 1.2 copy-start.8
  122.1 4.4 %copy-start.11 = (bf16[128,2048]{1,0:T(8,128)(2,1)S(1)}, bf16[128,2048]{1,0:T(8,128)(2,1)}, u32[]{:S(2)}) copy-start(bf16[128,2048]{1,0:T(8,128)(2,1)} %copy-done.10) | copy-start | bytes 1572868
  124.9 27.6 %collective-permute-start.18 = (bf16[512,1024]{1,0:T(8,128)(2,1)S(1)}, bf16[512,1024]{1,0:T(8,128)(2,1)S(1)}, u32[]{:S(2)}, u32[]{:S(2)}) collective-permute-start(bf16[512,1024]{1,0:T(8,128)(2,1)S(1)} %get-tuple-element.98), channel_id=1, source_target_pairs={{0,2},{1,3},{2,0},{3,1},{4,6},{5,7},{6,4},{7,5},{8,10},{9,11},{10,... | collective-permute-start | bytes 3145736 | tf_op jit(solution)/shard_map/ppermute | solution.py:271
  126.5 17.1 %copy-start.9 = (bf16[1024,512]{1,0:T(8,128)(2,1)S(1)}, bf16[1024,512]{1,0:T(8,128)(2,1)}, u32[]{:S(2)}) copy-start(bf16[1024,512]{1,0:T(8,128)(2,1)} %get-tuple-element.87.other_ref) | copy-start | bytes 3145732
  130.9 17.1 %copy-start.6 = (f32[1024,1024]{1,0:T(8,128)S(1)}, f32[1024,1024]{1,0:T(8,128)}, u32[]{:S(2)}) copy-start(f32[1024,1024]{1,0:T(8,128)} %get-tuple-element.101.refs_0_) | copy-start | bytes 12582916
  146.5 30.0 %collective-permute-start.22 = (bf16[512,1024]{1,0:T(8,128)(2,1)S(1)}, bf16[512,1024]{1,0:T(8,128)(2,1)S(1)}, u32[]{:S(2)}, u32[]{:S(2)}) collective-permute-start(bf16[512,1024]{1,0:T(8,128)(2,1)S(1)} %get-tuple-element.112), channel_id=1, source_target_pairs={{0,2},{1,3},{2,0},{3,1},{4,6},{5,7},{6,4},{7,5},{8,10},{9,11},{10,... | collective-permute-start | bytes 3145736 | tf_op jit(solution)/shard_map/ppermute | solution.py:271
  148.0 18.6 %copy-start.2 = (bf16[2,2048,256]{2,1,0:T(8,128)(2,1)S(1)}, bf16[2,2048,256]{2,1,0:T(8,128)(2,1)}, u32[]{:S(2)}) copy-start(bf16[2,2048,256]{2,1,0:T(8,128)(2,1)} %refs_1_.5) | copy-start | bytes 6291460
  148.0 18.6 %copy-start.4 = (bf16[2,2048,256]{2,1,0:T(8,128)(2,1)S(1)}, bf16[2,2048,256]{2,1,0:T(8,128)(2,1)}, u32[]{:S(2)}) copy-start(bf16[2,2048,256]{2,1,0:T(8,128)(2,1)} %copy-done.3) | copy-start | bytes 6291460
  152.5 14.2 %copy-start.1 = (bf16[2,2048,256]{2,1,0:T(8,128)(2,1)S(1)}, bf16[2,2048,256]{2,1,0:T(8,128)(2,1)}, u32[]{:S(2)}) copy-start(bf16[2,2048,256]{2,1,0:T(8,128)(2,1)} %refs_0_.5) | copy-start | bytes 6291460
  152.7 10.0 %collective-permute-start.19 = (bf16[128,1024]{1,0:T(8,128)(2,1)S(1)}, bf16[128,1024]{1,0:T(8,128)(2,1)S(1)}, u32[]{:S(2)}, u32[]{:S(2)}) collective-permute-start(bf16[128,1024]{1,0:T(8,128)(2,1)S(1)} %get-tuple-element.104), channel_id=1, source_target_pairs={{0,12},{1,13},{2,14},{3,15},{4,0},{5,1},{6,2},{7,3},{8,4},{9,5},{1... | collective-permute-start | bytes 786440 | tf_op jit(solution)/shard_map/ppermute | solution.py:271
  156.3 10.3 %collective-permute-start.20 = (bf16[128,1024]{1,0:T(8,128)(2,1)S(1)}, bf16[128,1024]{1,0:T(8,128)(2,1)S(1)}, u32[]{:S(2)}, u32[]{:S(2)}) collective-permute-start(bf16[128,1024]{1,0:T(8,128)(2,1)S(1)} %get-tuple-element.106), channel_id=1, source_target_pairs={{0,4},{1,5},{2,6},{3,7},{4,8},{5,9},{6,10},{7,11},{8,12},{9,13},{1... | collective-permute-start | bytes 786440 | tf_op jit(solution)/shard_map/ppermute | solution.py:271
  174.4 31.5 %collective-permute-start.26 = (bf16[512,1280]{1,0:T(8,128)(2,1)S(1)}, bf16[512,1280]{1,0:T(8,128)(2,1)S(1)}, u32[]{:S(2)}, u32[]{:S(2)}) collective-permute-start(bf16[512,1280]{1,0:T(8,128)(2,1)S(1)} %get-tuple-element.124), channel_id=1, source_target_pairs={{0,2},{1,3},{2,0},{3,1},{4,6},{5,7},{6,4},{7,5},{8,10},{9,11},{10,... | collective-permute-start | bytes 3932168 | tf_op jit(solution)/shard_map/ppermute | solution.py:271
  175.1 8.6 %collective-permute-start.21 = (bf16[128,1024]{1,0:T(8,128)(2,1)S(1)}, bf16[128,1024]{1,0:T(8,128)(2,1)S(1)}, u32[]{:S(2)}, u32[]{:S(2)}) collective-permute-start(bf16[128,1024]{1,0:T(8,128)(2,1)S(1)} %add_piece.4), channel_id=1, source_target_pairs={{0,4},{1,5},{2,6},{3,7},{4,8},{5,9},{6,10},{7,11},{8,12},{9,13},{1... | collective-permute-start | bytes 786440 | tf_op jit(solution)/shard_map/ppermute | solution.py:271
  183.6 8.3 %collective-permute-start.24 = (bf16[128,1024]{1,0:T(8,128)(2,1)S(1)}, bf16[128,1024]{1,0:T(8,128)(2,1)S(1)}, u32[]{:S(2)}, u32[]{:S(2)}) collective-permute-start(bf16[128,1024]{1,0:T(8,128)(2,1)S(1)} %get-tuple-element.118), channel_id=1, source_target_pairs={{0,4},{1,5},{2,6},{3,7},{4,8},{5,9},{6,10},{7,11},{8,12},{9,13},{1... | collective-permute-start | bytes 786440 | tf_op jit(solution)/shard_map/ppermute | solution.py:271
  183.9 10.7 %collective-permute-start.23 = (bf16[128,1024]{1,0:T(8,128)(2,1)S(1)}, bf16[128,1024]{1,0:T(8,128)(2,1)S(1)}, u32[]{:S(2)}, u32[]{:S(2)}) collective-permute-start(bf16[128,1024]{1,0:T(8,128)(2,1)S(1)} %get-tuple-element.115), channel_id=1, source_target_pairs={{0,12},{1,13},{2,14},{3,15},{4,0},{5,1},{6,2},{7,3},{8,4},{9,5},{1... | collective-permute-start | bytes 786440 | tf_op jit(solution)/shard_map/ppermute | solution.py:271
  194.6 8.8 %collective-permute-start.25 = (bf16[128,1024]{1,0:T(8,128)(2,1)S(1)}, bf16[128,1024]{1,0:T(8,128)(2,1)S(1)}, u32[]{:S(2)}, u32[]{:S(2)}) collective-permute-start(bf16[128,1024]{1,0:T(8,128)(2,1)S(1)} %add_piece.5), channel_id=1, source_target_pairs={{0,4},{1,5},{2,6},{3,7},{4,8},{5,9},{6,10},{7,11},{8,12},{9,13},{1... | collective-permute-start | bytes 786440 | tf_op jit(solution)/shard_map/ppermute | solution.py:271
  198.8 22.0 %collective-permute-start.30 = (bf16[512,512]{1,0:T(8,128)(2,1)S(1)}, bf16[512,512]{1,0:T(8,128)(2,1)S(1)}, u32[]{:S(2)}, u32[]{:S(2)}) collective-permute-start(bf16[512,512]{1,0:T(8,128)(2,1)S(1)} %get-tuple-element.133), channel_id=1, source_target_pairs={{0,2},{1,3},{2,0},{3,1},{4,6},{5,7},{6,4},{7,5},{8,10},{9,11},{10,... | collective-permute-start | bytes 1572872 | tf_op jit(solution)/shard_map/ppermute | solution.py:271
  206.2 12.5 %collective-permute-start.28 = (bf16[128,1280]{1,0:T(8,128)(2,1)S(1)}, bf16[128,1280]{1,0:T(8,128)(2,1)S(1)}, u32[]{:S(2)}, u32[]{:S(2)}) collective-permute-start(bf16[128,1280]{1,0:T(8,128)(2,1)S(1)} %get-tuple-element.128), channel_id=1, source_target_pairs={{0,4},{1,5},{2,6},{3,7},{4,8},{5,9},{6,10},{7,11},{8,12},{9,13},{1... | collective-permute-start | bytes 983048 | tf_op jit(solution)/shard_map/ppermute | solution.py:271
  206.6 14.1 %collective-permute-start.27 = (bf16[128,1280]{1,0:T(8,128)(2,1)S(1)}, bf16[128,1280]{1,0:T(8,128)(2,1)S(1)}, u32[]{:S(2)}, u32[]{:S(2)}) collective-permute-start(bf16[128,1280]{1,0:T(8,128)(2,1)S(1)} %get-tuple-element.126), channel_id=1, source_target_pairs={{0,12},{1,13},{2,14},{3,15},{4,0},{5,1},{6,2},{7,3},{8,4},{9,5},{1... | collective-permute-start | bytes 983048 | tf_op jit(solution)/shard_map/ppermute | solution.py:271
  210.1 27.6 %collective-permute-start.34 = (bf16[512,256]{1,0:T(8,128)(2,1)S(1)}, bf16[512,256]{1,0:T(8,128)(2,1)S(1)}, u32[]{:S(2)}, u32[]{:S(2)}) collective-permute-start(bf16[512,256]{1,0:T(8,128)(2,1)S(1)} %get-tuple-element.141), channel_id=1, source_target_pairs={{0,2},{1,3},{2,0},{3,1},{4,6},{5,7},{6,4},{7,5},{8,10},{9,11},{10,... | collective-permute-start | bytes 786440 | tf_op jit(solution)/shard_map/ppermute | solution.py:271
  220.8 25.8 %collective-permute-start.29 = (bf16[128,1280]{1,0:T(8,128)(2,1)S(1)}, bf16[128,1280]{1,0:T(8,128)(2,1)S(1)}, u32[]{:S(2)}, u32[]{:S(2)}) collective-permute-start(bf16[128,1280]{1,0:T(8,128)(2,1)S(1)} %add_piece.6), channel_id=1, source_target_pairs={{0,4},{1,5},{2,6},{3,7},{4,8},{5,9},{6,10},{7,11},{8,12},{9,13},{1... | collective-permute-start | bytes 983048 | tf_op jit(solution)/shard_map/ppermute | solution.py:271
  220.9 13.8 %collective-permute-start.32 = (bf16[128,512]{1,0:T(8,128)(2,1)S(1)}, bf16[128,512]{1,0:T(8,128)(2,1)S(1)}, u32[]{:S(2)}, u32[]{:S(2)}) collective-permute-start(bf16[128,512]{1,0:T(8,128)(2,1)S(1)} %get-tuple-element.138), channel_id=1, source_target_pairs={{0,4},{1,5},{2,6},{3,7},{4,8},{5,9},{6,10},{7,11},{8,12},{9,13},{1... | collective-permute-start | bytes 393224 | tf_op jit(solution)/shard_map/ppermute | solution.py:271
  223.8 11.6 %collective-permute-start.31 = (bf16[128,512]{1,0:T(8,128)(2,1)S(1)}, bf16[128,512]{1,0:T(8,128)(2,1)S(1)}, u32[]{:S(2)}, u32[]{:S(2)}) collective-permute-start(bf16[128,512]{1,0:T(8,128)(2,1)S(1)} %get-tuple-element.136), channel_id=1, source_target_pairs={{0,12},{1,13},{2,14},{3,15},{4,0},{5,1},{6,2},{7,3},{8,4},{9,5},{1... | collective-permute-start | bytes 393224 | tf_op jit(solution)/shard_map/ppermute | solution.py:271
  235.5 11.1 %collective-permute-start.33 = (bf16[128,512]{1,0:T(8,128)(2,1)S(1)}, bf16[128,512]{1,0:T(8,128)(2,1)S(1)}, u32[]{:S(2)}, u32[]{:S(2)}) collective-permute-start(bf16[128,512]{1,0:T(8,128)(2,1)S(1)} %add_piece.7), channel_id=1, source_target_pairs={{0,4},{1,5},{2,6},{3,7},{4,8},{5,9},{6,10},{7,11},{8,12},{9,13},{1... | collective-permute-start | bytes 393224 | tf_op jit(solution)/shard_map/ppermute | solution.py:271
  237.7 6.8 %collective-permute-start.35 = (bf16[128,256]{1,0:T(8,128)(2,1)S(1)}, bf16[128,256]{1,0:T(8,128)(2,1)S(1)}, u32[]{:S(2)}, u32[]{:S(2)}) collective-permute-start(bf16[128,256]{1,0:T(8,128)(2,1)S(1)} %get-tuple-element.147), channel_id=1, source_target_pairs={{0,4},{1,5},{2,6},{3,7},{4,8},{5,9},{6,10},{7,11},{8,12},{9,13},{1... | collective-permute-start | bytes 196616 | tf_op jit(solution)/shard_map/ppermute | solution.py:271
  238.4 8.2 %collective-permute-start.36 = (bf16[128,256]{1,0:T(8,128)(2,1)S(1)}, bf16[128,256]{1,0:T(8,128)(2,1)S(1)}, u32[]{:S(2)}, u32[]{:S(2)}) collective-permute-start(bf16[128,256]{1,0:T(8,128)(2,1)S(1)} %get-tuple-element.148), channel_id=1, source_target_pairs={{0,8},{1,9},{2,10},{3,11},{4,12},{5,13},{6,14},{7,15},{8,0},{9,1},... | collective-permute-start | bytes 196616 | tf_op jit(solution)/shard_map/ppermute | solution.py:271
  241.1 5.5 %collective-permute-start.37 = (bf16[128,256]{1,0:T(8,128)(2,1)S(1)}, bf16[128,256]{1,0:T(8,128)(2,1)S(1)}, u32[]{:S(2)}, u32[]{:S(2)}) collective-permute-start(bf16[128,256]{1,0:T(8,128)(2,1)S(1)} %get-tuple-element.149), channel_id=1, source_target_pairs={{0,12},{1,13},{2,14},{3,15},{4,0},{5,1},{6,2},{7,3},{8,4},{9,5},{1... | collective-permute-start | bytes 196616 | tf_op jit(solution)/shard_map/ppermute | solution.py:271

commit v10 on v9

--- a/solution.py
+++ b/solution.py
@@ -278,7 +278,7 @@
     experts = local_count * devices
     block = tokens.shape[0]
     chunks = cut_columns(width, ((0, 4), (4, 8)))
-    back_chunks = cut_columns(width, ((0, 5), (6, 8), (5, 6)))
+    back_chunks = cut_columns(width, ((0, 4), (4, 6), (6, 8)))
     me = lax.axis_index("expert")
     twin = [(d, d ^ 1) for d in range(devices)]
     side = [(d, d ^ 2) for d in range(devices)]
@@ -355,32 +355,32 @@
         lo, hi = back_chunks[c]
         return back_columns(own_grads, after(other_grads, *waits), weights, lo // (hi - lo), hi - lo)
 
-    own_0, *pieces = add_sides(after(keep_0, other_grads), come_0, types)
+    keep_2, send = back(0)
+    own_0, *pieces = add_sides(after(keep_0, send), come_0, types)
+    (come_2,) = send_all([(send, side)], own_0)
     far_0, next_0 = send_on(pieces)
-    keep_2, send = back(0, next_0, far_0)
     near_0 = send_last(pieces, next_0)
-    (come_2,) = send_all([(send, side)], own_0)
-
+
+    keep_3, send = back(1, next_0, far_0)
     own_1, *pieces = add_sides(after(keep_1, send), come_1, types)
-    far_1, next_1 = send_on(pieces, near_0)
-    keep_3, send = back(1, next_1)
     (come_3,) = send_all([(send, side)], own_1)
-    near_1 = send_last(pieces, next_1, far_1)
-
-    keep_4, send = back(2, near_1)
+    far_1, next_1 = send_on(pieces)
+    near_1 = send_last(pieces, next_1, far_1, near_0)
+
+    keep_4, send = back(2, next_1)
     own_2, *pieces = add_sides(after(keep_2, send), come_2, types)
     (come_4,) = send_all([(send, side)], own_2)
     far_2, next_2 = send_on(pieces)
-    near_2 = send_last(pieces, next_2, far_2)
-
-    own_3, *pieces = add_sides(keep_3, after(come_3, next_2), types)
+    near_2 = send_last(pieces, next_2, far_2, near_1)
+    mixed = finish(chunks, [(own_0, far_0, near_0), (own_1, far_1, near_1)], width)
+
+    own_3, *pieces = add_sides(after(keep_3, mixed), come_3, types)
     far_3, next_3 = send_on(pieces)
     near_3 = send_last(pieces, next_3, far_3)
 
-    mixed = finish(chunks, [(own_0, far_0, near_0), (own_1, far_1, near_1)], width)
     types = [jnp.float32] + [jnp.bfloat16] * (layers - 1)
     own_4, *pieces = add_sides(keep_4, after(come_4, own_3), types)
-    parts_4 = send_all([(piece, layer[k]) for k, piece in enumerate(pieces, 1)], mixed)
+    parts_4 = send_all([(piece, layer[k]) for k, piece in enumerate(pieces, 1)], near_2)
     back_parts = [(own_2, far_2, near_2), (own_3, far_3, near_3), (own_4, *parts_4)]
     return (mixed, finish(back_chunks, back_parts, width))
 

time: 248 us -> 246 us (level)
  waiting for transfers between devices: 134 us -> 131 us
    ppermute x38, waiting for transfers between devices: 134 us -> 131 us  [send_all(): lax.ppermute(v, 'expert', pairs)]
  transfers between devices with their start and end apart: 38 -> 38, of which waited for: 23 -> 20; matrix products, arithmetic and copies ran while one was open for 1% -> 1% of each run, Pallas kernels for 20% -> 21%
where the time goes in v10:
time: 246 us; the launch traced here: 245 us
  waiting for transfers between devices  131 us (53%)
  starting transfers between devices  53.3 us (22%)
  Pallas kernels  51.9 us (21%)
  local copies, waits for them, and re-layouts  7.07 us (3%)
    ppermute x38, waiting for transfers between devices, send_all(): lax.ppermute(v, 'expert', pairs)  131 us
    ppermute x38, starting transfers between devices, send_all(): lax.ppermute(v, 'expert', pairs)  53.3 us
    pallas_call x2, Pallas kernels, hidden_forward(): pl.pallas_call(functools.partial(hidden_kernel, blocks, all_experts), gri...  20 us
    pallas_call x5, Pallas kernels, sum_columns(): pl.pallas_call(kernel, grid=(2,), in_specs=[rows, rows] + weight_specs, o...  19.9 us
    pallas_call x2, Pallas kernels, hidden_grads(): pl.pallas_call(functools.partial(grads_kernel, blocks, tuple(cuts), by is...  8.85 us
  transfers between devices with their start and end apart: 38, of which 20 were waited for; matrix products, arithmetic and copies ran while one was open for 1% of the time, Pallas kernels for 21%

profile of v10, /device:TPU:0, one launch (start us, length us, event | category | flops | bytes accessed | tf_op | source)
XLA Modules:
  0.0 244.6 jit_solution(15045744324498181359)
XLA Ops:
  0.6 0.7 select_reduce_fusion
  1.6 1.2 concatenate.3.refs_0_
  2.8 3.0 %collective-permute-start.8 = (bf16[2,2048,256]{2,1,0:T(8,128)(2,1)}, bf16[2,2048,256]{2,1,0:T(8,128)(2,1)S(1)}, u32[]{:S(2)}, u32[]{:S(2)}) collective-permute-start(bf16[2,2048,256]{2,1,0:T(8,128)(2,1)} %refs_0_.5), channel_id=1, source_target_pairs={{0,1},{1,0},{2,3},{3,2},{4,5},{5,4},{6,7},{7,6},{8,9},{9,8},{10,11... | collective-permute-start | bytes 6291464 | tf_op jit(solution)/shard_map/ppermute | solution.py:271
  5.8 1.6 collective-permute-start.3
  7.4 1.5 collective-permute-start.6
  8.9 2.2 collective-permute-start
  11.7 10.8 %collective-permute-done.6.refs_6_.refs_7_ = bf16[128,2048]{1,0:T(8,128)(2,1)S(1)} collective-permute-done((bf16[128,2048]{1,0:T(8,128)(2,1)}, bf16[128,2048]{1,0:T(8,128)(2,1)S(1)}, u32[]{:S(2)}, u32[]{:S(2)}) %collective-permute-start.6) | collective-permute-done | bytes 524320 | tf_op jit(solution)/shard_map/ppermute | solution.py:271
  22.5 0.8 copy-done.10
  23.8 9.9 %collective-permute-done.refs_1_ = bf16[128,2176]{1,0:T(8,128)(2,1)S(1)} collective-permute-done((bf16[128,2176]{1,0:T(8,128)(2,1)S(1)}, bf16[128,2176]{1,0:T(8,128)(2,1)S(1)}, u32[]{:S(2)}, u32[]{:S(2)}) %collective-permute-start) | collective-permute-done | bytes 557088 | tf_op jit(solution)/shard_map/ppermute | solution.py:271
  33.7 1.2 collective-permute-start.4
  35.0 2.6 %collective-permute-start.2 = (bf16[128,2176]{1,0:T(8,128)(2,1)S(1)}, bf16[128,2176]{1,0:T(8,128)(2,1)S(1)}, u32[]{:S(2)}, u32[]{:S(2)}) collective-permute-start(bf16[128,2176]{1,0:T(8,128)(2,1)S(1)} %collective-permute-done.refs_1_), channel_id=1, source_target_pairs={{0,12},{1,13},{2,14},{3,15},{4,0},{5,1},{6,2},{7,3},{8,4},{9,5},{1... | collective-permute-start | bytes 1671176 | tf_op jit(solution)/shard_map/ppermute | solution.py:271
  37.6 0.7 collective-permute-start.7
  38.3 10.9 %collective-permute-done.4.refs_5_ = bf16[128,2176]{1,0:T(8,128)(2,1)S(1)} collective-permute-done((bf16[128,2176]{1,0:T(8,128)(2,1)S(1)}, bf16[128,2176]{1,0:T(8,128)(2,1)S(1)}, u32[]{:S(2)}, u32[]{:S(2)}) %collective-permute-start.4) | collective-permute-done | bytes 557088 | tf_op jit(solution)/shard_map/ppermute | solution.py:271
  49.3 2.4 collective-permute-start.11
  51.7 1.5 collective-permute-start.5
  53.2 3.0 %fusion.1 = (bf16[512,1024]{1,0:T(8,128)(2,1)}, bf16[512,1024]{1,0:T(8,128)(2,1)}) fusion(bf16[512,2048]{1,0:T(8,128)(2,1)} %bitcast.3), kind=kLoop, calls=%fused_computation.5 | loop fusion | bytes 4194304 | tf_op jit(solution)/shard_map/slice | solution.py:297
  56.3 4.9 %collective-permute-done.7.refs_7_ = bf16[128,2176]{1,0:T(8,128)(2,1)S(1)} collective-permute-done((bf16[128,2176]{1,0:T(8,128)(2,1)S(1)}, bf16[128,2176]{1,0:T(8,128)(2,1)S(1)}, u32[]{:S(2)}, u32[]{:S(2)}) %collective-permute-start.7) | collective-permute-done | bytes 557088 | tf_op jit(solution)/shard_map/ppermute | solution.py:271
  61.2 0.6 collective-permute-start.10
  61.8 10.3 %collective-permute-done.5.refs_6_ = bf16[128,2176]{1,0:T(8,128)(2,1)S(1)} collective-permute-done((bf16[128,2176]{1,0:T(8,128)(2,1)S(1)}, bf16[128,2176]{1,0:T(8,128)(2,1)S(1)}, u32[]{:S(2)}, u32[]{:S(2)}) %collective-permute-start.5) | collective-permute-done | bytes 557088 | tf_op jit(solution)/shard_map/ppermute | solution.py:271
  73.0 0.9 collective-permute-start.12
  73.9 1.2 collective-permute-start.13
  75.1 9.8 %hidden_forward.2 = (bf16[1024,512]{1,0:T(8,128)(2,1)}, f32[1024,1024]{1,0:T(8,128)}) custom-call(s32[1]{0:T(128)} %bitcast.owner_ref, bf16[2,2048,256]{2,1,0:T(8,128)(2,1)} %refs_0_.5, bf16[2,2048,256]{2,1,0:T(8,128)(2,1)} %refs_1_.5, bf16[128,2176]{1,0:T(8,128)(2,1)} %copy-done.12, bf16[128,2176]{1,0:T(8,128)(2,1)} %copy-done.14, ...), custom_call_target="tpu_custom_call" | custom-call | flops 1 | bytes 1 | tf_op jit(solution)/shard_map/hidden_forward/pallas_call | solution.py:71
  85.0 11.8 %collective-permute-done.15.refs_4_.refs_5_ = bf16[128,2048]{1,0:T(8,128)(2,1)} collective-permute-done((bf16[128,2048]{1,0:T(8,128)(2,1)}, bf16[128,2048]{1,0:T(8,128)(2,1)}, u32[]{:S(2)}, u32[]{:S(2)}) %collective-permute-start.15) | collective-permute-done | bytes 524320 | tf_op jit(solution)/shard_map/ppermute | solution.py:271
  97.2 1.6 collective-permute-start.14
  98.8 10.2 %hidden_forward.3 = (bf16[1024,512]{1,0:T(8,128)(2,1)}, f32[1024,1024]{1,0:T(8,128)}) custom-call(s32[1]{0:T(128)} %bitcast.1.owner_ref, bf16[2,2048,256]{2,1,0:T(8,128)(2,1)} %copy-done.3, bf16[2,2048,256]{2,1,0:T(8,128)(2,1)} %collective-permute-done.9.up_ref.refs_3_, bf16[128,2176]{1,0:T(8,128)(2,1)} %copy-done.12, bf16[128,2176]{1,0:T(8,128)(2,1)} %copy-done.14, ...), custom_call_target="tpu_custom_call" | custom-call | flops 1 | bytes 1 | tf_op jit(solution)/shard_map/hidden_forward/pallas_call | solution.py:71
  109.0 10.1 %collective-permute-done.10.other_down_ref.refs_1_ = bf16[512,1024]{1,0:T(8,128)(2,1)S(1)} collective-permute-done((bf16[512,1024]{1,0:T(8,128)(2,1)}, bf16[512,1024]{1,0:T(8,128)(2,1)S(1)}, u32[]{:S(2)}, u32[]{:S(2)}) %collective-permute-start.10) | collective-permute-done | bytes 1048608 | tf_op jit(solution)/shard_map/ppermute | solution.py:271
  119.1 1.7 collective-permute-start.17
  120.9 1.2 copy-done.8
  122.1 2.8 %mix_columns.2 = (f32[512,1024]{1,0:T(8,128)S(1)}, bf16[512,1024]{1,0:T(8,128)(2,1)S(1)}) custom-call(bf16[1024,512]{1,0:T(8,128)(2,1)S(1)} %copy-done.7, bf16[1024,512]{1,0:T(8,128)(2,1)S(1)} %copy-done.8, bf16[512,2048]{1,0:T(8,128)(2,1)S(1)} %bitcast.4, bf16[512,1024]{1,0:T(8,128)(2,1)S(1)} %collective-permute-done.10.other_down_ref.refs_1_), custom_call_target="tpu_custom_call" | custom-call | flops 1 | bytes 1 | tf_op jit(solution)/shard_map/mix_columns/pallas_call | solution.py:179
  124.9 1.6 collective-permute-start.18
  126.5 4.4 %hidden_grads.2.own_ref = bf16[1024,1024]{1,0:T(8,128)(2,1)S(1)} custom-call(f32[1024,1024]{1,0:T(8,128)S(1)} %copy-done.5, bf16[512,2048]{1,0:T(8,128)(2,1)S(1)} %bitcast.5, bf16[128,2048]{1,0:T(8,128)(2,1)} %refs_3_.1, bf16[128,2048]{1,0:T(8,128)(2,1)} %collective-permute-done.11.refs_3_.refs_4_, ...), custom_call_target="tpu_custom_call" | custom-call | flops 1 | bytes 1 | tf_op jit(solution)/shard_map/hidden_grads/pallas_call | solution.py:127
  130.9 12.5 %collective-permute-done.17.other_down_ref.refs_2_ = bf16[512,1024]{1,0:T(8,128)(2,1)S(1)} collective-permute-done((bf16[512,1024]{1,0:T(8,128)(2,1)S(1)}, bf16[512,1024]{1,0:T(8,128)(2,1)S(1)}, u32[]{:S(2)}, u32[]{:S(2)}) %collective-permute-start.17) | collective-permute-done | bytes 1048608 | tf_op jit(solution)/shard_map/ppermute | solution.py:271
  143.4 2.8 %mix_columns.3 = (f32[512,1024]{1,0:T(8,128)S(1)}, bf16[512,1024]{1,0:T(8,128)(2,1)S(1)}) custom-call(bf16[1024,512]{1,0:T(8,128)(2,1)S(1)} %copy-done.7, bf16[1024,512]{1,0:T(8,128)(2,1)S(1)} %copy-done.9, bf16[512,2048]{1,0:T(8,128)(2,1)S(1)} %bitcast.6, bf16[512,1024]{1,0:T(8,128)(2,1)S(1)} %collective-permute-done.17.other_down_ref.refs_2_), custom_call_target="tpu_custom_call" | custom-call | flops 1 | bytes 1 | tf_op jit(solution)/shard_map/mix_columns/pallas_call | solution.py:179
  146.3 1.5 collective-permute-start.22
  147.8 4.5 %hidden_grads.3.other_ref = bf16[1024,1024]{1,0:T(8,128)(2,1)S(1)} custom-call(f32[1024,1024]{1,0:T(8,128)S(1)} %copy-done.6, bf16[512,1024]{1,0:T(8,128)(2,1)S(1)} %collective-permute-done.10.other_down_ref.refs_1_, bf16[512,1024]{1,0:T(8,128)(2,1)S(1)} %collective-permute-done.17.other_down_ref.refs_2_, bf16[128,2048]{1,0:T(8,128)(2,1)} %refs_3_.1, ...), custom_call_target="tpu_custom_call" | custom-call | flops 1 | bytes 1 | tf_op jit(solution)/shard_map/hidden_grads/pallas_call | solution.py:127
  152.3 6.5 %back_columns.3 = (f32[512,1024]{1,0:T(8,128)S(1)}, bf16[512,1024]{1,0:T(8,128)(2,1)S(1)}) custom-call(bf16[1024,1024]{1,0:T(8,128)(2,1)S(1)} %hidden_grads.2.own_ref, bf16[1024,1024]{1,0:T(8,128)(2,1)S(1)} %hidden_grads.3.other_ref, bf16[2,2048,256]{2,1,0:T(8,128)(2,1)S(1)} %copy-done.1, bf16[2,2048,256]{2,1,0:T(8,128)(2,1)S(1)} %copy-done.2, ...), custom_call_target="tpu_custom_call" | custom-call | flops 1 | bytes 1 | tf_op jit(solution)/shard_map/back_columns/pallas_call | solution.py:179
  159.0 0.6 collective-permute-start.26
  159.6 3.5 %collective-permute-start.19 = (bf16[128,1024]{1,0:T(8,128)(2,1)S(1)}, bf16[128,1024]{1,0:T(8,128)(2,1)S(1)}, u32[]{:S(2)}, u32[]{:S(2)}) collective-permute-start(bf16[128,1024]{1,0:T(8,128)(2,1)S(1)} %get-tuple-element.103), channel_id=1, source_target_pairs={{0,12},{1,13},{2,14},{3,15},{4,0},{5,1},{6,2},{7,3},{8,4},{9,5},{1... | collective-permute-start | bytes 786440 | tf_op jit(solution)/shard_map/ppermute | solution.py:271
  163.1 6.1 %collective-permute-done.19.refs_1_ = bf16[128,1024]{1,0:T(8,128)(2,1)S(1)} collective-permute-done((bf16[128,1024]{1,0:T(8,128)(2,1)S(1)}, bf16[128,1024]{1,0:T(8,128)(2,1)S(1)}, u32[]{:S(2)}, u32[]{:S(2)}) %collective-permute-start.19) | collective-permute-done | bytes 262176 | tf_op jit(solution)/shard_map/ppermute | solution.py:271
  169.2 4.0 %collective-permute-done.20.come_ref = bf16[128,1024]{1,0:T(8,128)(2,1)S(1)} collective-permute-done((bf16[128,1024]{1,0:T(8,128)(2,1)S(1)}, bf16[128,1024]{1,0:T(8,128)(2,1)S(1)}, u32[]{:S(2)}, u32[]{:S(2)}) %collective-permute-start.20) | collective-permute-done | bytes 262176 | tf_op jit(solution)/shard_map/ppermute | solution.py:271
  173.1 3.9 %back_columns.4 = (f32[512,512]{1,0:T(8,128)S(1)}, bf16[512,512]{1,0:T(8,128)(2,1)S(1)}) custom-call(bf16[1024,1024]{1,0:T(8,128)(2,1)S(1)} %hidden_grads.2.own_ref, bf16[1024,1024]{1,0:T(8,128)(2,1)S(1)} %hidden_grads.3.other_ref, bf16[2,2048,256]{2,1,0:T(8,128)(2,1)S(1)} %copy-done.1, bf16[2,2048,256]{2,1,0:T(8,128)(2,1)S(1)} %copy-done.2, ...), custom_call_target="tpu_custom_call" | custom-call | flops 1 | bytes 1 | tf_op jit(solution)/shard_map/back_columns/pallas_call | solution.py:179
  177.2 1.4 collective-permute-start.24
  178.7 3.8 %collective-permute-start.23 = (bf16[128,1024]{1,0:T(8,128)(2,1)S(1)}, bf16[128,1024]{1,0:T(8,128)(2,1)S(1)}, u32[]{:S(2)}, u32[]{:S(2)}) collective-permute-start(bf16[128,1024]{1,0:T(8,128)(2,1)S(1)} %get-tuple-element.112), channel_id=1, source_target_pairs={{0,12},{1,13},{2,14},{3,15},{4,0},{5,1},{6,2},{7,3},{8,4},{9,5},{1... | collective-permute-start | bytes 786440 | tf_op jit(solution)/shard_map/ppermute | solution.py:271
  182.5 1.5 collective-permute-start.30
  184.1 4.3 %collective-permute-done.24.come_ref = bf16[128,1024]{1,0:T(8,128)(2,1)S(1)} collective-permute-done((bf16[128,1024]{1,0:T(8,128)(2,1)S(1)}, bf16[128,1024]{1,0:T(8,128)(2,1)S(1)}, u32[]{:S(2)}, u32[]{:S(2)}) %collective-permute-start.24) | collective-permute-done | bytes 262176 | tf_op jit(solution)/shard_map/ppermute | solution.py:271
  188.4 3.9 %back_columns.5 = (f32[512,512]{1,0:T(8,128)S(1)}, bf16[512,512]{1,0:T(8,128)(2,1)S(1)}) custom-call(bf16[1024,1024]{1,0:T(8,128)(2,1)S(1)} %hidden_grads.2.own_ref, bf16[1024,1024]{1,0:T(8,128)(2,1)S(1)} %hidden_grads.3.other_ref, bf16[2,2048,256]{2,1,0:T(8,128)(2,1)S(1)} %copy-done.1, bf16[2,2048,256]{2,1,0:T(8,128)(2,1)S(1)} %copy-done.2, ...), custom_call_target="tpu_custom_call" | custom-call | flops 1 | bytes 1 | tf_op jit(solution)/shard_map/back_columns/pallas_call | solution.py:179
  192.3 3.0 %collective-permute-done.26.come_ref = bf16[512,1024]{1,0:T(8,128)(2,1)S(1)} collective-permute-done((bf16[512,1024]{1,0:T(8,128)(2,1)S(1)}, bf16[512,1024]{1,0:T(8,128)(2,1)S(1)}, u32[]{:S(2)}, u32[]{:S(2)}) %collective-permute-start.26) | collective-permute-done | bytes 1048608 | tf_op jit(solution)/shard_map/ppermute | solution.py:271
  195.4 1.9 collective-permute-start.28
  197.3 1.5 collective-permute-start.34
  198.8 2.2 collective-permute-start.27
  201.1 5.5 %collective-permute-done.28.come_ref = bf16[128,1024]{1,0:T(8,128)(2,1)S(1)} collective-permute-done((bf16[128,1024]{1,0:T(8,128)(2,1)S(1)}, bf16[128,1024]{1,0:T(8,128)(2,1)S(1)}, u32[]{:S(2)}, u32[]{:S(2)}) %collective-permute-start.28) | collective-permute-done | bytes 262176 | tf_op jit(solution)/shard_map/ppermute | solution.py:271
  206.6 5.5 %collective-permute-done.27.refs_1_ = bf16[128,1024]{1,0:T(8,128)(2,1)S(1)} collective-permute-done((bf16[128,1024]{1,0:T(8,128)(2,1)S(1)}, bf16[128,1024]{1,0:T(8,128)(2,1)S(1)}, u32[]{:S(2)}, u32[]{:S(2)}) %collective-permute-start.27) | collective-permute-done | bytes 262176 | tf_op jit(solution)/shard_map/ppermute | solution.py:271
  212.2 3.2 %collective-permute-done.25.refs_5_ = bf16[128,1024]{1,0:T(8,128)(2,1)S(1)} collective-permute-done((bf16[128,1024]{1,0:T(8,128)(2,1)S(1)}, bf16[128,1024]{1,0:T(8,128)(2,1)S(1)}, u32[]{:S(2)}, u32[]{:S(2)}) %collective-permute-start.25) | collective-permute-done | bytes 262176 | tf_op jit(solution)/shard_map/ppermute | solution.py:271
  215.4 1.1 finish.2
  216.8 3.8 %collective-permute-start.31 = (bf16[128,512]{1,0:T(8,128)(2,1)S(1)}, bf16[128,512]{1,0:T(8,128)(2,1)S(1)}, u32[]{:S(2)}, u32[]{:S(2)}) collective-permute-start(bf16[128,512]{1,0:T(8,128)(2,1)S(1)} %get-tuple-element.130), channel_id=1, source_target_pairs={{0,12},{1,13},{2,14},{3,15},{4,0},{5,1},{6,2},{7,3},{8,4},{9,5},{1... | collective-permute-start | bytes 393224 | tf_op jit(solution)/shard_map/ppermute | solution.py:271
  220.5 7.0 %collective-permute-done.32.come_ref = bf16[128,512]{1,0:T(8,128)(2,1)S(1)} collective-permute-done((bf16[128,512]{1,0:T(8,128)(2,1)S(1)}, bf16[128,512]{1,0:T(8,128)(2,1)S(1)}, u32[]{:S(2)}, u32[]{:S(2)}) %collective-permute-start.32) | collective-permute-done | bytes 131104 | tf_op jit(solution)/shard_map/ppermute | solution.py:271
  227.5 0.7 collective-permute-done.31.refs_4_
  228.3 1.1 collective-permute-start.33
  229.4 0.7 collective-permute-start.35
  230.1 2.7 %collective-permute-start.36 = (bf16[128,512]{1,0:T(8,128)(2,1)S(1)}, bf16[128,512]{1,0:T(8,128)(2,1)S(1)}, u32[]{:S(2)}, u32[]{:S(2)}) collective-permute-start(bf16[128,512]{1,0:T(8,128)(2,1)S(1)} %get-tuple-element.142), channel_id=1, source_target_pairs={{0,8},{1,9},{2,10},{3,11},{4,12},{5,13},{6,14},{7,15},{8,0},{9,1},... | collective-permute-start | bytes 393224 | tf_op jit(solution)/shard_map/ppermute | solution.py:271
  233.3 3.2 %collective-permute-done.33.refs_5_ = bf16[128,512]{1,0:T(8,128)(2,1)S(1)} collective-permute-done((bf16[128,512]{1,0:T(8,128)(2,1)S(1)}, bf16[128,512]{1,0:T(8,128)(2,1)S(1)}, u32[]{:S(2)}, u32[]{:S(2)}) %collective-permute-start.33) | collective-permute-done | bytes 131104 | tf_op jit(solution)/shard_map/ppermute | solution.py:271
  236.5 2.8 %collective-permute-done.35.refs_7_ = bf16[128,512]{1,0:T(8,128)(2,1)S(1)} collective-permute-done((bf16[128,512]{1,0:T(8,128)(2,1)S(1)}, bf16[128,512]{1,0:T(8,128)(2,1)S(1)}, u32[]{:S(2)}, u32[]{:S(2)}) %collective-permute-start.35) | collective-permute-done | bytes 131104 | tf_op jit(solution)/shard_map/ppermute | solution.py:271
  239.3 4.2 %collective-permute-done.36.refs_8_ = bf16[128,512]{1,0:T(8,128)(2,1)S(1)} collective-permute-done((bf16[128,512]{1,0:T(8,128)(2,1)S(1)}, bf16[128,512]{1,0:T(8,128)(2,1)S(1)}, u32[]{:S(2)}, u32[]{:S(2)}) %collective-permute-start.36) | collective-permute-done | bytes 131104 | tf_op jit(solution)/shard_map/ppermute | solution.py:271
  243.5 1.1 finish.3
  (82 shorter events, 4.3 us)
Async XLA Ops:
  2.8 58.4 %copy-start.12 = (bf16[128,2176]{1,0:T(8,128)(2,1)}, bf16[128,2176]{1,0:T(8,128)(2,1)S(1)}, u32[]{:S(2)}) copy-start(bf16[128,2176]{1,0:T(8,128)(2,1)S(1)} %concatenate.3.refs_0_) | copy-start | bytes 1671172
  2.8 58.4 %collective-permute-start.8 = (bf16[2,2048,256]{2,1,0:T(8,128)(2,1)}, bf16[2,2048,256]{2,1,0:T(8,128)(2,1)S(1)}, u32[]{:S(2)}, u32[]{:S(2)}) collective-permute-start(bf16[2,2048,256]{2,1,0:T(8,128)(2,1)} %refs_0_.5), channel_id=1, source_target_pairs={{0,1},{1,0},{2,3},{3,2},{4,5},{5,4},{6,7},{7,6},{8,9},{9,8},{10,11... | collective-permute-start | bytes 6291464 | tf_op jit(solution)/shard_map/ppermute | solution.py:271
  5.8 17.5 %collective-permute-start.3 = (bf16[128,2176]{1,0:T(8,128)(2,1)S(1)}, bf16[128,2176]{1,0:T(8,128)(2,1)S(1)}, u32[]{:S(2)}, u32[]{:S(2)}) collective-permute-start(bf16[128,2176]{1,0:T(8,128)(2,1)S(1)} %concatenate.3.refs_0_), channel_id=1, source_target_pairs={{0,4},{1,5},{2,6},{3,7},{4,8},{5,9},{6,10},{7,11},{8,12},{9,13},{1... | collective-permute-start | bytes 1671176 | tf_op jit(solution)/shard_map/ppermute | solution.py:271
  7.4 15.1 %collective-permute-start.6 = (bf16[128,2048]{1,0:T(8,128)(2,1)}, bf16[128,2048]{1,0:T(8,128)(2,1)S(1)}, u32[]{:S(2)}, u32[]{:S(2)}) collective-permute-start(bf16[128,2048]{1,0:T(8,128)(2,1)} %refs_3_.1), channel_id=1, source_target_pairs={{0,2},{1,3},{2,0},{3,1},{4,6},{5,7},{6,4},{7,5},{8,10},{9,11},{10,... | collective-permute-start | bytes 1572872 | tf_op jit(solution)/shard_map/ppermute | solution.py:271
  8.9 24.8 %collective-permute-start = (bf16[128,2176]{1,0:T(8,128)(2,1)S(1)}, bf16[128,2176]{1,0:T(8,128)(2,1)S(1)}, u32[]{:S(2)}, u32[]{:S(2)}) collective-permute-start(bf16[128,2176]{1,0:T(8,128)(2,1)S(1)} %concatenate.3.refs_0_), channel_id=1, source_target_pairs={{0,12},{1,13},{2,14},{3,15},{4,0},{5,1},{6,2},{7,3},{8,4},{9,5},{1... | collective-permute-start | bytes 1671176 | tf_op jit(solution)/shard_map/ppermute | solution.py:271
  11.2 22.5 %collective-permute-start.1 = (bf16[128,2176]{1,0:T(8,128)(2,1)S(1)}, bf16[128,2176]{1,0:T(8,128)(2,1)S(1)}, u32[]{:S(2)}, u32[]{:S(2)}) collective-permute-start(bf16[128,2176]{1,0:T(8,128)(2,1)S(1)} %concatenate.3.refs_0_), channel_id=1, source_target_pairs={{0,2},{1,3},{2,0},{3,1},{4,6},{5,7},{6,4},{7,5},{8,10},{9,11},{10,... | collective-permute-start | bytes 1671176 | tf_op jit(solution)/shard_map/ppermute | solution.py:271
  22.5 0.8 copy-start.10
  23.3 33.0 %copy-start.13 = (bf16[128,2176]{1,0:T(8,128)(2,1)}, bf16[128,2176]{1,0:T(8,128)(2,1)S(1)}, u32[]{:S(2)}) copy-start(bf16[128,2176]{1,0:T(8,128)(2,1)S(1)} %collective-permute-done.3.refs_3_) | copy-start | bytes 1671172
  23.3 75.5 %collective-permute-start.9 = (bf16[2,2048,256]{2,1,0:T(8,128)(2,1)}, bf16[2,2048,256]{2,1,0:T(8,128)(2,1)}, u32[]{:S(2)}, u32[]{:S(2)}) collective-permute-start(bf16[2,2048,256]{2,1,0:T(8,128)(2,1)} %refs_1_.5), channel_id=1, source_target_pairs={{0,1},{1,0},{2,3},{3,2},{4,5},{5,4},{6,7},{7,6},{8,9},{9,8},{10,11... | collective-permute-start | bytes 6291464 | tf_op jit(solution)/shard_map/ppermute | solution.py:271
  33.7 1.3 copy-start.14
  33.7 15.6 %copy-start.15 = (bf16[128,2176]{1,0:T(8,128)(2,1)}, bf16[128,2176]{1,0:T(8,128)(2,1)S(1)}, u32[]{:S(2)}) copy-start(bf16[128,2176]{1,0:T(8,128)(2,1)S(1)} %collective-permute-done.1.refs_4_) | copy-start | bytes 1671172
  33.7 15.6 %collective-permute-start.4 = (bf16[128,2176]{1,0:T(8,128)(2,1)S(1)}, bf16[128,2176]{1,0:T(8,128)(2,1)S(1)}, u32[]{:S(2)}, u32[]{:S(2)}) collective-permute-start(bf16[128,2176]{1,0:T(8,128)(2,1)S(1)} %collective-permute-done.refs_1_), channel_id=1, source_target_pairs={{0,2},{1,3},{2,0},{3,1},{4,6},{5,7},{6,4},{7,5},{8,10},{9,11},{10,... | collective-permute-start | bytes 1671176 | tf_op jit(solution)/shard_map/ppermute | solution.py:271
  35.0 14.3 %collective-permute-start.2 = (bf16[128,2176]{1,0:T(8,128)(2,1)S(1)}, bf16[128,2176]{1,0:T(8,128)(2,1)S(1)}, u32[]{:S(2)}, u32[]{:S(2)}) collective-permute-start(bf16[128,2176]{1,0:T(8,128)(2,1)S(1)} %collective-permute-done.refs_1_), channel_id=1, source_target_pairs={{0,12},{1,13},{2,14},{3,15},{4,0},{5,1},{6,2},{7,3},{8,4},{9,5},{1... | collective-permute-start | bytes 1671176 | tf_op jit(solution)/shard_map/ppermute | solution.py:271
  37.6 23.6 %collective-permute-start.7 = (bf16[128,2176]{1,0:T(8,128)(2,1)S(1)}, bf16[128,2176]{1,0:T(8,128)(2,1)S(1)}, u32[]{:S(2)}, u32[]{:S(2)}) collective-permute-start(bf16[128,2176]{1,0:T(8,128)(2,1)S(1)} %collective-permute-done.3.refs_3_), channel_id=1, source_target_pairs={{0,2},{1,3},{2,0},{3,1},{4,6},{5,7},{6,4},{7,5},{8,10},{9,11},{10,... | collective-permute-start | bytes 1671176 | tf_op jit(solution)/shard_map/ppermute | solution.py:271
  49.3 2.4 copy-start.16
  49.3 7.0 %copy-start.17 = (bf16[128,2176]{1,0:T(8,128)(2,1)}, bf16[128,2176]{1,0:T(8,128)(2,1)S(1)}, u32[]{:S(2)}) copy-start(bf16[128,2176]{1,0:T(8,128)(2,1)S(1)} %collective-permute-done.2.refs_2_) | copy-start | bytes 1671172
  49.3 12.5 %collective-permute-start.11 = (bf16[128,2048]{1,0:T(8,128)(2,1)}, bf16[128,2048]{1,0:T(8,128)(2,1)}, u32[]{:S(2)}, u32[]{:S(2)}) collective-permute-start(bf16[128,2048]{1,0:T(8,128)(2,1)} %refs_3_.1), channel_id=1, source_target_pairs={{0,12},{1,13},{2,14},{3,15},{4,0},{5,1},{6,2},{7,3},{8,4},{9,5},{1... | collective-permute-start | bytes 1572872 | tf_op jit(solution)/shard_map/ppermute | solution.py:271
  51.7 20.4 %collective-permute-start.5 = (bf16[128,2176]{1,0:T(8,128)(2,1)S(1)}, bf16[128,2176]{1,0:T(8,128)(2,1)S(1)}, u32[]{:S(2)}, u32[]{:S(2)}) collective-permute-start(bf16[128,2176]{1,0:T(8,128)(2,1)S(1)} %collective-permute-done.2.refs_2_), channel_id=1, source_target_pairs={{0,2},{1,3},{2,0},{3,1},{4,6},{5,7},{6,4},{7,5},{8,10},{9,11},{10,... | collective-permute-start | bytes 1671176 | tf_op jit(solution)/shard_map/ppermute | solution.py:271
  61.2 10.9 %copy-start.18 = (bf16[128,2176]{1,0:T(8,128)(2,1)}, bf16[128,2176]{1,0:T(8,128)(2,1)S(1)}, u32[]{:S(2)}) copy-start(bf16[128,2176]{1,0:T(8,128)(2,1)S(1)} %collective-permute-done.7.refs_7_) | copy-start | bytes 1671172
  61.2 23.7 %copy-start.3 = (bf16[2,2048,256]{2,1,0:T(8,128)(2,1)}, bf16[2,2048,256]{2,1,0:T(8,128)(2,1)S(1)}, u32[]{:S(2)}) copy-start(bf16[2,2048,256]{2,1,0:T(8,128)(2,1)S(1)} %collective-permute-done.8.gate_ref.refs_2_) | copy-start | bytes 6291460
  61.2 57.8 %collective-permute-start.10 = (bf16[512,1024]{1,0:T(8,128)(2,1)}, bf16[512,1024]{1,0:T(8,128)(2,1)S(1)}, u32[]{:S(2)}, u32[]{:S(2)}) collective-permute-start(bf16[512,1024]{1,0:T(8,128)(2,1)} %get-tuple-element.85), channel_id=1, source_target_pairs={{0,1},{1,0},{2,3},{3,2},{4,5},{5,4},{6,7},{7,6},{8,9},{9,8},{10,11... | collective-permute-start | bytes 3145736 | tf_op jit(solution)/shard_map/ppermute | solution.py:271
  72.2 0.8 copy-start.19
  72.2 24.6 %collective-permute-start.15 = (bf16[128,2048]{1,0:T(8,128)(2,1)}, bf16[128,2048]{1,0:T(8,128)(2,1)}, u32[]{:S(2)}, u32[]{:S(2)}) collective-permute-start(bf16[128,2048]{1,0:T(8,128)(2,1)} %collective-permute-done.11.refs_3_.refs_4_), channel_id=1, source_target_pairs={{0,12},{1,13},{2,14},{3,15},{4,0},{5,1},{6,2},{7,3},{8,4},{9,5},{1... | collective-permute-start | bytes 1572872 | tf_op jit(solution)/shard_map/ppermute | solution.py:271
  73.0 23.8 %collective-permute-start.12 = (bf16[128,2048]{1,0:T(8,128)(2,1)}, bf16[128,2048]{1,0:T(8,128)(2,1)}, u32[]{:S(2)}, u32[]{:S(2)}) collective-permute-start(bf16[128,2048]{1,0:T(8,128)(2,1)} %collective-permute-done.11.refs_3_.refs_4_), channel_id=1, source_target_pairs={{0,2},{1,3},{2,0},{3,1},{4,6},{5,7},{6,4},{7,5},{8,10},{9,11},{10,... | collective-permute-start | bytes 1572872 | tf_op jit(solution)/shard_map/ppermute | solution.py:271
  73.9 23.3 %collective-permute-start.13 = (bf16[128,2048]{1,0:T(8,128)(2,1)}, bf16[128,2048]{1,0:T(8,128)(2,1)}, u32[]{:S(2)}, u32[]{:S(2)}) collective-permute-start(bf16[128,2048]{1,0:T(8,128)(2,1)} %refs_3_.1), channel_id=1, source_target_pairs={{0,4},{1,5},{2,6},{3,7},{4,8},{5,9},{6,10},{7,11},{8,12},{9,13},{1... | collective-permute-start | bytes 1572872 | tf_op jit(solution)/shard_map/ppermute | solution.py:271
  96.8 24.1 %collective-permute-start.16 = (bf16[128,2048]{1,0:T(8,128)(2,1)}, bf16[128,2048]{1,0:T(8,128)(2,1)S(1)}, u32[]{:S(2)}, u32[]{:S(2)}) collective-permute-start(bf16[128,2048]{1,0:T(8,128)(2,1)} %collective-permute-done.15.refs_4_.refs_5_), channel_id=1, source_target_pairs={{0,2},{1,3},{2,0},{3,1},{4,6},{5,7},{6,4},{7,5},{8,10},{9,11},{10,... | collective-permute-start | bytes 1572872 | tf_op jit(solution)/shard_map/ppermute | solution.py:271
  97.2 23.6 %collective-permute-start.14 = (bf16[128,2048]{1,0:T(8,128)(2,1)}, bf16[128,2048]{1,0:T(8,128)(2,1)S(1)}, u32[]{:S(2)}, u32[]{:S(2)}) collective-permute-start(bf16[128,2048]{1,0:T(8,128)(2,1)} %collective-permute-done.13.refs_5_.refs_6_), channel_id=1, source_target_pairs={{0,2},{1,3},{2,0},{3,1},{4,6},{5,7},{6,4},{7,5},{8,10},{9,11},{10,... | collective-permute-start | bytes 1572872 | tf_op jit(solution)/shard_map/ppermute | solution.py:271
  98.8 20.3 %copy-start.20 = (bf16[512,1024]{1,0:T(8,128)(2,1)S(1)}, bf16[512,1024]{1,0:T(8,128)(2,1)}, u32[]{:S(2)}) copy-start(bf16[512,1024]{1,0:T(8,128)(2,1)} %get-tuple-element.95) | copy-start | bytes 3145732
  98.8 22.0 %copy-start = (bf16[2,256,2048]{2,1,0:T(8,128)(2,1)S(1)}, bf16[2,256,2048]{2,1,0:T(8,128)(2,1)}, u32[]{:S(2)}) copy-start(bf16[2,256,2048]{2,1,0:T(8,128)(2,1)} %param.13) | copy-start | bytes 6291460
  98.8 22.0 %copy-start.7 = (bf16[1024,512]{1,0:T(8,128)(2,1)S(1)}, bf16[1024,512]{1,0:T(8,128)(2,1)}, u32[]{:S(2)}) copy-start(bf16[1024,512]{1,0:T(8,128)(2,1)} %get-tuple-element.80.own_ref) | copy-start | bytes 3145732
  119.1 7.4 %copy-start.5 = (f32[1024,1024]{1,0:T(8,128)S(1)}, f32[1024,1024]{1,0:T(8,128)}, u32[]{:S(2)}) copy-start(f32[1024,1024]{1,0:T(8,128)} %get-tuple-element.93.refs_0_) | copy-start | bytes 12582916
  119.1 24.3 %collective-permute-start.17 = (bf16[512,1024]{1,0:T(8,128)(2,1)S(1)}, bf16[512,1024]{1,0:T(8,128)(2,1)S(1)}, u32[]{:S(2)}, u32[]{:S(2)}) collective-permute-start(bf16[512,1024]{1,0:T(8,128)(2,1)S(1)} %copy-done.20), channel_id=1, source_target_pairs={{0,1},{1,0},{2,3},{3,2},{4,5},{5,4},{6,7},{7,6},{8,9},{9,8},{10,11... | collective-permute-start | bytes 3145736 | tf_op jit(solution)/shard_map/ppermute | solution.py:271
  120.8 1.2 copy-start.8
  122.1 4.4 %copy-start.11 = (bf16[128,2048]{1,0:T(8,128)(2,1)S(1)}, bf16[128,2048]{1,0:T(8,128)(2,1)}, u32[]{:S(2)}) copy-start(bf16[128,2048]{1,0:T(8,128)(2,1)} %copy-done.10) | copy-start | bytes 1572868
  124.9 33.8 %collective-permute-start.18 = (bf16[512,1024]{1,0:T(8,128)(2,1)S(1)}, bf16[512,1024]{1,0:T(8,128)(2,1)S(1)}, u32[]{:S(2)}, u32[]{:S(2)}) collective-permute-start(bf16[512,1024]{1,0:T(8,128)(2,1)S(1)} %get-tuple-element.96), channel_id=1, source_target_pairs={{0,2},{1,3},{2,0},{3,1},{4,6},{5,7},{6,4},{7,5},{8,10},{9,11},{10,... | collective-permute-start | bytes 3145736 | tf_op jit(solution)/shard_map/ppermute | solution.py:271
  126.5 16.9 %copy-start.9 = (bf16[1024,512]{1,0:T(8,128)(2,1)S(1)}, bf16[1024,512]{1,0:T(8,128)(2,1)}, u32[]{:S(2)}) copy-start(bf16[1024,512]{1,0:T(8,128)(2,1)} %get-tuple-element.84.other_ref) | copy-start | bytes 3145732
  130.9 16.9 %copy-start.6 = (f32[1024,1024]{1,0:T(8,128)S(1)}, f32[1024,1024]{1,0:T(8,128)}, u32[]{:S(2)}) copy-start(f32[1024,1024]{1,0:T(8,128)} %get-tuple-element.99.refs_0_) | copy-start | bytes 12582916
  146.3 30.8 %collective-permute-start.22 = (bf16[512,1024]{1,0:T(8,128)(2,1)S(1)}, bf16[512,1024]{1,0:T(8,128)(2,1)S(1)}, u32[]{:S(2)}, u32[]{:S(2)}) collective-permute-start(bf16[512,1024]{1,0:T(8,128)(2,1)S(1)} %get-tuple-element.110), channel_id=1, source_target_pairs={{0,2},{1,3},{2,0},{3,1},{4,6},{5,7},{6,4},{7,5},{8,10},{9,11},{10,... | collective-permute-start | bytes 3145736 | tf_op jit(solution)/shard_map/ppermute | solution.py:271
  147.8 4.5 %copy-start.1 = (bf16[2,2048,256]{2,1,0:T(8,128)(2,1)S(1)}, bf16[2,2048,256]{2,1,0:T(8,128)(2,1)}, u32[]{:S(2)}) copy-start(bf16[2,2048,256]{2,1,0:T(8,128)(2,1)} %refs_0_.5) | copy-start | bytes 6291460
  147.8 4.5 %copy-start.2 = (bf16[2,2048,256]{2,1,0:T(8,128)(2,1)S(1)}, bf16[2,2048,256]{2,1,0:T(8,128)(2,1)}, u32[]{:S(2)}) copy-start(bf16[2,2048,256]{2,1,0:T(8,128)(2,1)} %refs_1_.5) | copy-start | bytes 6291460
  147.8 4.5 %copy-start.4 = (bf16[2,2048,256]{2,1,0:T(8,128)(2,1)S(1)}, bf16[2,2048,256]{2,1,0:T(8,128)(2,1)}, u32[]{:S(2)}) copy-start(bf16[2,2048,256]{2,1,0:T(8,128)(2,1)} %copy-done.3) | copy-start | bytes 6291460
  159.0 36.3 %collective-permute-start.26 = (bf16[512,1024]{1,0:T(8,128)(2,1)S(1)}, bf16[512,1024]{1,0:T(8,128)(2,1)S(1)}, u32[]{:S(2)}, u32[]{:S(2)}) collective-permute-start(bf16[512,1024]{1,0:T(8,128)(2,1)S(1)} %get-tuple-element.120), channel_id=1, source_target_pairs={{0,2},{1,3},{2,0},{3,1},{4,6},{5,7},{6,4},{7,5},{8,10},{9,11},{10,... | collective-permute-start | bytes 3145736 | tf_op jit(solution)/shard_map/ppermute | solution.py:271
  159.6 9.6 %collective-permute-start.19 = (bf16[128,1024]{1,0:T(8,128)(2,1)S(1)}, bf16[128,1024]{1,0:T(8,128)(2,1)S(1)}, u32[]{:S(2)}, u32[]{:S(2)}) collective-permute-start(bf16[128,1024]{1,0:T(8,128)(2,1)S(1)} %get-tuple-element.103), channel_id=1, source_target_pairs={{0,12},{1,13},{2,14},{3,15},{4,0},{5,1},{6,2},{7,3},{8,4},{9,5},{1... | collective-permute-start | bytes 786440 | tf_op jit(solution)/shard_map/ppermute | solution.py:271
  163.1 10.0 %collective-permute-start.20 = (bf16[128,1024]{1,0:T(8,128)(2,1)S(1)}, bf16[128,1024]{1,0:T(8,128)(2,1)S(1)}, u32[]{:S(2)}, u32[]{:S(2)}) collective-permute-start(bf16[128,1024]{1,0:T(8,128)(2,1)S(1)} %get-tuple-element.105), channel_id=1, source_target_pairs={{0,4},{1,5},{2,6},{3,7},{4,8},{5,9},{6,10},{7,11},{8,12},{9,13},{1... | collective-permute-start | bytes 786440 | tf_op jit(solution)/shard_map/ppermute | solution.py:271
  177.2 11.1 %collective-permute-start.24 = (bf16[128,1024]{1,0:T(8,128)(2,1)S(1)}, bf16[128,1024]{1,0:T(8,128)(2,1)S(1)}, u32[]{:S(2)}, u32[]{:S(2)}) collective-permute-start(bf16[128,1024]{1,0:T(8,128)(2,1)S(1)} %get-tuple-element.114), channel_id=1, source_target_pairs={{0,4},{1,5},{2,6},{3,7},{4,8},{5,9},{6,10},{7,11},{8,12},{9,13},{1... | collective-permute-start | bytes 786440 | tf_op jit(solution)/shard_map/ppermute | solution.py:271
  178.7 16.8 %collective-permute-start.21 = (bf16[128,1024]{1,0:T(8,128)(2,1)S(1)}, bf16[128,1024]{1,0:T(8,128)(2,1)S(1)}, u32[]{:S(2)}, u32[]{:S(2)}) collective-permute-start(bf16[128,1024]{1,0:T(8,128)(2,1)S(1)} %add_piece.4), channel_id=1, source_target_pairs={{0,4},{1,5},{2,6},{3,7},{4,8},{5,9},{6,10},{7,11},{8,12},{9,13},{1... | collective-permute-start | bytes 786440 | tf_op jit(solution)/shard_map/ppermute | solution.py:271
  178.7 16.7 %collective-permute-start.23 = (bf16[128,1024]{1,0:T(8,128)(2,1)S(1)}, bf16[128,1024]{1,0:T(8,128)(2,1)S(1)}, u32[]{:S(2)}, u32[]{:S(2)}) collective-permute-start(bf16[128,1024]{1,0:T(8,128)(2,1)S(1)} %get-tuple-element.112), channel_id=1, source_target_pairs={{0,12},{1,13},{2,14},{3,15},{4,0},{5,1},{6,2},{7,3},{8,4},{9,5},{1... | collective-permute-start | bytes 786440 | tf_op jit(solution)/shard_map/ppermute | solution.py:271
  182.5 34.0 %collective-permute-start.30 = (bf16[512,512]{1,0:T(8,128)(2,1)S(1)}, bf16[512,512]{1,0:T(8,128)(2,1)S(1)}, u32[]{:S(2)}, u32[]{:S(2)}) collective-permute-start(bf16[512,512]{1,0:T(8,128)(2,1)S(1)} %get-tuple-element.128), channel_id=1, source_target_pairs={{0,2},{1,3},{2,0},{3,1},{4,6},{5,7},{6,4},{7,5},{8,10},{9,11},{10,... | collective-permute-start | bytes 1572872 | tf_op jit(solution)/shard_map/ppermute | solution.py:271
  195.4 11.2 %collective-permute-start.28 = (bf16[128,1024]{1,0:T(8,128)(2,1)S(1)}, bf16[128,1024]{1,0:T(8,128)(2,1)S(1)}, u32[]{:S(2)}, u32[]{:S(2)}) collective-permute-start(bf16[128,1024]{1,0:T(8,128)(2,1)S(1)} %get-tuple-element.124), channel_id=1, source_target_pairs={{0,4},{1,5},{2,6},{3,7},{4,8},{5,9},{6,10},{7,11},{8,12},{9,13},{1... | collective-permute-start | bytes 786440 | tf_op jit(solution)/shard_map/ppermute | solution.py:271
  197.3 32.0 %collective-permute-start.34 = (bf16[512,512]{1,0:T(8,128)(2,1)S(1)}, bf16[512,512]{1,0:T(8,128)(2,1)S(1)}, u32[]{:S(2)}, u32[]{:S(2)}) collective-permute-start(bf16[512,512]{1,0:T(8,128)(2,1)S(1)} %get-tuple-element.135), channel_id=1, source_target_pairs={{0,2},{1,3},{2,0},{3,1},{4,6},{5,7},{6,4},{7,5},{8,10},{9,11},{10,... | collective-permute-start | bytes 1572872 | tf_op jit(solution)/shard_map/ppermute | solution.py:271
  198.8 13.3 %collective-permute-start.27 = (bf16[128,1024]{1,0:T(8,128)(2,1)S(1)}, bf16[128,1024]{1,0:T(8,128)(2,1)S(1)}, u32[]{:S(2)}, u32[]{:S(2)}) collective-permute-start(bf16[128,1024]{1,0:T(8,128)(2,1)S(1)} %get-tuple-element.122), channel_id=1, source_target_pairs={{0,12},{1,13},{2,14},{3,15},{4,0},{5,1},{6,2},{7,3},{8,4},{9,5},{1... | collective-permute-start | bytes 786440 | tf_op jit(solution)/shard_map/ppermute | solution.py:271
  201.1 14.3 %collective-permute-start.25 = (bf16[128,1024]{1,0:T(8,128)(2,1)S(1)}, bf16[128,1024]{1,0:T(8,128)(2,1)S(1)}, u32[]{:S(2)}, u32[]{:S(2)}) collective-permute-start(bf16[128,1024]{1,0:T(8,128)(2,1)S(1)} %add_piece.5), channel_id=1, source_target_pairs={{0,4},{1,5},{2,6},{3,7},{4,8},{5,9},{6,10},{7,11},{8,12},{9,13},{1... | collective-permute-start | bytes 786440 | tf_op jit(solution)/shard_map/ppermute | solution.py:271
  215.4 14.0 %collective-permute-start.29 = (bf16[128,1024]{1,0:T(8,128)(2,1)S(1)}, bf16[128,1024]{1,0:T(8,128)(2,1)S(1)}, u32[]{:S(2)}, u32[]{:S(2)}) collective-permute-start(bf16[128,1024]{1,0:T(8,128)(2,1)S(1)} %add_piece.6), channel_id=1, source_target_pairs={{0,4},{1,5},{2,6},{3,7},{4,8},{5,9},{6,10},{7,11},{8,12},{9,13},{1... | collective-permute-start | bytes 786440 | tf_op jit(solution)/shard_map/ppermute | solution.py:271
  216.6 10.9 %collective-permute-start.32 = (bf16[128,512]{1,0:T(8,128)(2,1)S(1)}, bf16[128,512]{1,0:T(8,128)(2,1)S(1)}, u32[]{:S(2)}, u32[]{:S(2)}) collective-permute-start(bf16[128,512]{1,0:T(8,128)(2,1)S(1)} %get-tuple-element.132), channel_id=1, source_target_pairs={{0,4},{1,5},{2,6},{3,7},{4,8},{5,9},{6,10},{7,11},{8,12},{9,13},{1... | collective-permute-start | bytes 393224 | tf_op jit(solution)/shard_map/ppermute | solution.py:271
  216.8 11.5 %collective-permute-start.31 = (bf16[128,512]{1,0:T(8,128)(2,1)S(1)}, bf16[128,512]{1,0:T(8,128)(2,1)S(1)}, u32[]{:S(2)}, u32[]{:S(2)}) collective-permute-start(bf16[128,512]{1,0:T(8,128)(2,1)S(1)} %get-tuple-element.130), channel_id=1, source_target_pairs={{0,12},{1,13},{2,14},{3,15},{4,0},{5,1},{6,2},{7,3},{8,4},{9,5},{1... | collective-permute-start | bytes 393224 | tf_op jit(solution)/shard_map/ppermute | solution.py:271
  228.3 8.3 %collective-permute-start.33 = (bf16[128,512]{1,0:T(8,128)(2,1)S(1)}, bf16[128,512]{1,0:T(8,128)(2,1)S(1)}, u32[]{:S(2)}, u32[]{:S(2)}) collective-permute-start(bf16[128,512]{1,0:T(8,128)(2,1)S(1)} %add_piece.7), channel_id=1, source_target_pairs={{0,4},{1,5},{2,6},{3,7},{4,8},{5,9},{6,10},{7,11},{8,12},{9,13},{1... | collective-permute-start | bytes 393224 | tf_op jit(solution)/shard_map/ppermute | solution.py:271
  229.4 9.8 %collective-permute-start.35 = (bf16[128,512]{1,0:T(8,128)(2,1)S(1)}, bf16[128,512]{1,0:T(8,128)(2,1)S(1)}, u32[]{:S(2)}, u32[]{:S(2)}) collective-permute-start(bf16[128,512]{1,0:T(8,128)(2,1)S(1)} %get-tuple-element.141), channel_id=1, source_target_pairs={{0,4},{1,5},{2,6},{3,7},{4,8},{5,9},{6,10},{7,11},{8,12},{9,13},{1... | collective-permute-start | bytes 393224 | tf_op jit(solution)/shard_map/ppermute | solution.py:271
  230.1 13.4 %collective-permute-start.36 = (bf16[128,512]{1,0:T(8,128)(2,1)S(1)}, bf16[128,512]{1,0:T(8,128)(2,1)S(1)}, u32[]{:S(2)}, u32[]{:S(2)}) collective-permute-start(bf16[128,512]{1,0:T(8,128)(2,1)S(1)} %get-tuple-element.142), channel_id=1, source_target_pairs={{0,8},{1,9},{2,10},{3,11},{4,12},{5,13},{6,14},{7,15},{8,0},{9,1},... | collective-permute-start | bytes 393224 | tf_op jit(solution)/shard_map/ppermute | solution.py:271
  232.8 10.7 %collective-permute-start.37 = (bf16[128,512]{1,0:T(8,128)(2,1)S(1)}, bf16[128,512]{1,0:T(8,128)(2,1)S(1)}, u32[]{:S(2)}, u32[]{:S(2)}) collective-permute-start(bf16[128,512]{1,0:T(8,128)(2,1)S(1)} %get-tuple-element.143), channel_id=1, source_target_pairs={{0,12},{1,13},{2,14},{3,15},{4,0},{5,1},{6,2},{7,3},{8,4},{9,5},{1... | collective-permute-start | bytes 393224 | tf_op jit(solution)/shard_map/ppermute | solution.py:271

commit v11 on v10

--- a/solution.py
+++ b/solution.py
@@ -277,8 +277,8 @@
     layers = devices // 4
     experts = local_count * devices
     block = tokens.shape[0]
-    chunks = cut_columns(width, ((0, 4), (4, 8)))
-    back_chunks = cut_columns(width, ((0, 4), (4, 6), (6, 8)))
+    chunks = cut_columns(width, ((6, 8), (0, 3), (3, 6)))
+    back_chunks = cut_columns(width, ((0, 3), (3, 6), (6, 8)))
     me = lax.axis_index("expert")
     twin = [(d, d ^ 1) for d in range(devices)]
     side = [(d, d ^ 2) for d in range(devices)]
@@ -340,48 +340,56 @@
         return send_all([(piece, layer[one])], *waits)[0]
 
     keep_0, send = mix(0, down_0, other_activ, *far_grads.values())
-    (come_0,) = send_all([(send, side)])
+    come_0, down_2 = send_all([(send, side), (downs[2], twin)])
     grad_blocks = [grads[k] for k in range(layers)] + [far_grads[k] for k in range(layers)]
     own_grads = hidden_grads(grad_blocks, [down], [(0, width)], by=by)
 
-    keep_1, send = mix(1, down_1, send)
-    (come_1,) = send_all([(send, side)], own_grads)
+    keep_1, send = mix(1, down_1, send, own_grads)
+    own_0, *pieces = add_sides(keep_0, come_0, types)
+    (come_1,) = send_all([(send, side)])
+    far_0, next_0 = send_on(pieces)
+    near_0 = send_last(pieces, next_0, far_0)
+    grad_blocks = [after(grad_blocks[0], next_0), *grad_blocks[1:]]
+    other_grad = hidden_grads(grad_blocks, [down_0, down_1], chunks[:2])
+
+    keep_2, send = mix(2, down_2, other_grad, near_0)
+    (come_2,) = send_all([(send, side)], own_0)
 
     other_by = after(other_by, send)
-    other_grads = hidden_grads(grad_blocks, [down_0, down_1], chunks, by=other_by)
+    other_grads = hidden_grads(grad_blocks, [down_2], chunks[2:], by=other_by, before=other_grad)
     weights = [gate_weight, up_weight, other_gate, other_up]
 
     def back(c, *waits):
         lo, hi = back_chunks[c]
         return back_columns(own_grads, after(other_grads, *waits), weights, lo // (hi - lo), hi - lo)
 
-    keep_2, send = back(0)
-    own_0, *pieces = add_sides(after(keep_0, send), come_0, types)
-    (come_2,) = send_all([(send, side)], own_0)
-    far_0, next_0 = send_on(pieces)
-    near_0 = send_last(pieces, next_0)
-
-    keep_3, send = back(1, next_0, far_0)
+    keep_3, send = back(0)
     own_1, *pieces = add_sides(after(keep_1, send), come_1, types)
     (come_3,) = send_all([(send, side)], own_1)
     far_1, next_1 = send_on(pieces)
-    near_1 = send_last(pieces, next_1, far_1, near_0)
-
-    keep_4, send = back(2, next_1)
+    near_1 = send_last(pieces, next_1, far_1)
+
+    keep_4, send = back(1, next_1, far_1)
     own_2, *pieces = add_sides(after(keep_2, send), come_2, types)
     (come_4,) = send_all([(send, side)], own_2)
     far_2, next_2 = send_on(pieces)
     near_2 = send_last(pieces, next_2, far_2, near_1)
-    mixed = finish(chunks, [(own_0, far_0, near_0), (own_1, far_1, near_1)], width)
-
-    own_3, *pieces = add_sides(after(keep_3, mixed), come_3, types)
+
+    keep_5, send = back(2, next_2)
+    own_3, *pieces = add_sides(after(keep_3, send), come_3, types)
+    (come_5,) = send_all([(send, side)], own_3)
     far_3, next_3 = send_on(pieces)
-    near_3 = send_last(pieces, next_3, far_3)
+    near_3 = send_last(pieces, next_3, far_3, near_2)
+    mixed = finish(chunks, [(own_0, far_0, near_0), (own_1, far_1, near_1), (own_2, far_2, near_2)], width)
+
+    own_4, *pieces = add_sides(after(keep_4, mixed), after(come_4, next_3), types)
+    far_4, next_4 = send_on(pieces)
+    near_4 = send_last(pieces, next_4, far_4)
 
     types = [jnp.float32] + [jnp.bfloat16] * (layers - 1)
-    own_4, *pieces = add_sides(keep_4, after(come_4, own_3), types)
-    parts_4 = send_all([(piece, layer[k]) for k, piece in enumerate(pieces, 1)], near_2)
-    back_parts = [(own_2, far_2, near_2), (own_3, far_3, near_3), (own_4, *parts_4)]
+    own_5, *pieces = add_sides(keep_5, after(come_5, own_4), types)
+    parts_5 = send_all([(piece, layer[k]) for k, piece in enumerate(pieces, 1)], near_3)
+    back_parts = [(own_3, far_3, near_3), (own_4, far_4, near_4), (own_5, *parts_5)]
     return (mixed, finish(back_chunks, back_parts, width))
 
 

time: 246 us -> 236 us (0.959)
  waiting for transfers between devices: 131 us -> 119 us
  Pallas kernels: 51.9 us -> 56.2 us
    ppermute x38 -> x43, waiting for transfers between devices: 131 us -> 119 us  [send_all(): lax.ppermute(v, 'expert', pairs)]
    pallas_call x2 -> x3, Pallas kernels: 8.85 us -> 11.6 us  [hidden_grads(): pl.pallas_call(functools.partial(grads_kernel, blocks, tuple(cuts), by is...]
    pallas_call x5 -> x6, Pallas kernels: 19.9 us -> 21.4 us  [sum_columns(): pl.pallas_call(kernel, grid=(2,), in_specs=[rows, rows] + weight_specs, o...]
    ppermute x38 -> x43, starting transfers between devices: 53.3 us -> 52.3 us  [send_all(): lax.ppermute(v, 'expert', pairs)]
  transfers between devices with their start and end apart: 38 -> 43, of which waited for: 20 -> 24; matrix products, arithmetic and copies ran while one was open for 1% -> 1% of each run, Pallas kernels for 21% -> 23%
where the time goes in v11:
time: 236 us
  waiting for transfers between devices  119 us (50%)
  Pallas kernels  56.2 us (24%)
  starting transfers between devices  52.3 us (22%)
  local copies, waits for them, and re-layouts  6.68 us (3%)
    ppermute x43, waiting for transfers between devices, send_all(): lax.ppermute(v, 'expert', pairs)  119 us
    ppermute x43, starting transfers between devices, send_all(): lax.ppermute(v, 'expert', pairs)  52.3 us
    pallas_call x6, Pallas kernels, sum_columns(): pl.pallas_call(kernel, grid=(2,), in_specs=[rows, rows] + weight_specs, o...  21.4 us
    pallas_call x2, Pallas kernels, hidden_forward(): pl.pallas_call(functools.partial(hidden_kernel, blocks, all_experts), gri...  20 us
    pallas_call x3, Pallas kernels, hidden_grads(): pl.pallas_call(functools.partial(grads_kernel, blocks, tuple(cuts), by is...  11.6 us
  transfers between devices with their start and end apart: 43, of which 24 were waited for; matrix products, arithmetic and copies ran while one was open for 1% of the time, Pallas kernels for 23%

profile of v11, /device:TPU:0, one launch (start us, length us, event | category | flops | bytes accessed | tf_op | source)
XLA Modules:
  0.0 235.6 jit_solution(1802372637493621901)
XLA Ops:
  0.6 0.8 select_reduce_fusion
  1.7 1.9 concatenate.3.refs_0_
  3.6 2.9 %collective-permute-start.8 = (bf16[2,2048,256]{2,1,0:T(8,128)(2,1)}, bf16[2,2048,256]{2,1,0:T(8,128)(2,1)S(1)}, u32[]{:S(2)}, u32[]{:S(2)}) collective-permute-start(bf16[2,2048,256]{2,1,0:T(8,128)(2,1)} %refs_0_.5), channel_id=1, source_target_pairs={{0,1},{1,0},{2,3},{3,2},{4,5},{5,4},{6,7},{7,6},{8,9},{9,8},{10,11... | collective-permute-start | bytes 6291464 | tf_op jit(solution)/shard_map/ppermute | solution.py:271
  6.5 1.6 collective-permute-start.3
  8.1 1.5 collective-permute-start.6
  9.6 2.2 collective-permute-start
  12.4 10.8 %collective-permute-done.6.refs_6_.refs_7_ = bf16[128,2048]{1,0:T(8,128)(2,1)S(1)} collective-permute-done((bf16[128,2048]{1,0:T(8,128)(2,1)}, bf16[128,2048]{1,0:T(8,128)(2,1)S(1)}, u32[]{:S(2)}, u32[]{:S(2)}) %collective-permute-start.6) | collective-permute-done | bytes 524320 | tf_op jit(solution)/shard_map/ppermute | solution.py:271
  23.2 0.9 collective-permute-done.3.refs_3_
  24.4 10.2 %collective-permute-done.refs_1_ = bf16[128,2176]{1,0:T(8,128)(2,1)S(1)} collective-permute-done((bf16[128,2176]{1,0:T(8,128)(2,1)}, bf16[128,2176]{1,0:T(8,128)(2,1)S(1)}, u32[]{:S(2)}, u32[]{:S(2)}) %collective-permute-start) | collective-permute-done | bytes 557088 | tf_op jit(solution)/shard_map/ppermute | solution.py:271
  34.6 2.3 collective-permute-start.2
  37.0 1.5 collective-permute-start.4
  39.0 10.2 %collective-permute-done.2.refs_2_ = bf16[128,2176]{1,0:T(8,128)(2,1)S(1)} collective-permute-done((bf16[128,2176]{1,0:T(8,128)(2,1)S(1)}, bf16[128,2176]{1,0:T(8,128)(2,1)S(1)}, u32[]{:S(2)}, u32[]{:S(2)}) %collective-permute-start.2) | collective-permute-done | bytes 557088 | tf_op jit(solution)/shard_map/ppermute | solution.py:271
  49.2 3.4 %collective-permute-done.4.refs_5_ = bf16[128,2176]{1,0:T(8,128)(2,1)S(1)} collective-permute-done((bf16[128,2176]{1,0:T(8,128)(2,1)S(1)}, bf16[128,2176]{1,0:T(8,128)(2,1)S(1)}, u32[]{:S(2)}, u32[]{:S(2)}) %collective-permute-start.4) | collective-permute-done | bytes 557088 | tf_op jit(solution)/shard_map/ppermute | solution.py:271
  52.5 1.5 collective-permute-start.5
  54.5 10.0 %collective-permute-done.7.refs_7_ = bf16[128,2176]{1,0:T(8,128)(2,1)S(1)} collective-permute-done((bf16[128,2176]{1,0:T(8,128)(2,1)S(1)}, bf16[128,2176]{1,0:T(8,128)(2,1)S(1)}, u32[]{:S(2)}, u32[]{:S(2)}) %collective-permute-start.7) | collective-permute-done | bytes 557088 | tf_op jit(solution)/shard_map/ppermute | solution.py:271
  64.5 8.8 %collective-permute-done.5.refs_6_ = bf16[128,2176]{1,0:T(8,128)(2,1)S(1)} collective-permute-done((bf16[128,2176]{1,0:T(8,128)(2,1)S(1)}, bf16[128,2176]{1,0:T(8,128)(2,1)S(1)}, u32[]{:S(2)}, u32[]{:S(2)}) %collective-permute-start.5) | collective-permute-done | bytes 557088 | tf_op jit(solution)/shard_map/ppermute | solution.py:271
  73.3 1.5 collective-permute-start.12
  75.4 1.9 slice.12
  77.3 1.5 collective-permute-start.13
  78.8 1.5 collective-permute-start.10
  80.3 10.1 %hidden_forward.2 = (bf16[1024,512]{1,0:T(8,128)(2,1)}, f32[1024,1024]{1,0:T(8,128)}) custom-call(s32[1]{0:T(128)} %bitcast.owner_ref, bf16[2,2048,256]{2,1,0:T(8,128)(2,1)} %refs_0_.5, bf16[2,2048,256]{2,1,0:T(8,128)(2,1)} %refs_1_.5, bf16[128,2176]{1,0:T(8,128)(2,1)} %concatenate.3.refs_0_, bf16[128,2176]{1,0:T(8,128)(2,1)} %copy-done.12, ...), custom_call_target="tpu_custom_call" | custom-call | flops 1 | bytes 1 | tf_op jit(solution)/shard_map/hidden_forward/pallas_call | solution.py:71
  90.4 0.6 collective-permute-start.16
  91.0 8.9 %collective-permute-done.13.refs_5_.refs_6_ = bf16[128,2048]{1,0:T(8,128)(2,1)} collective-permute-done((bf16[128,2048]{1,0:T(8,128)(2,1)S(1)}, bf16[128,2048]{1,0:T(8,128)(2,1)}, u32[]{:S(2)}, u32[]{:S(2)}) %collective-permute-start.13) | collective-permute-done | bytes 524320 | tf_op jit(solution)/shard_map/ppermute | solution.py:271
  100.3 1.0 fusion.1
  101.4 9.9 %hidden_forward.3 = (bf16[1024,512]{1,0:T(8,128)(2,1)}, f32[1024,1024]{1,0:T(8,128)}) custom-call(s32[1]{0:T(128)} %bitcast.1.owner_ref, bf16[2,2048,256]{2,1,0:T(8,128)(2,1)} %copy-done.3, bf16[2,2048,256]{2,1,0:T(8,128)(2,1)} %collective-permute-done.9.up_ref.refs_3_, bf16[128,2176]{1,0:T(8,128)(2,1)} %concatenate.3.refs_0_, bf16[128,2176]{1,0:T(8,128)(2,1)} %copy-done.12, ...), custom_call_target="tpu_custom_call" | custom-call | flops 1 | bytes 1 | tf_op jit(solution)/shard_map/hidden_forward/pallas_call | solution.py:71
  111.9 1.2 copy-done.6
  113.1 2.8 %mix_columns.3 = (f32[512,512]{1,0:T(8,128)S(1)}, bf16[512,512]{1,0:T(8,128)(2,1)S(1)}) custom-call(bf16[1024,512]{1,0:T(8,128)(2,1)S(1)} %copy-done.5, bf16[1024,512]{1,0:T(8,128)(2,1)S(1)} %copy-done.6, bf16[512,2048]{1,0:T(8,128)(2,1)S(1)} %bitcast.5, bf16[512,512]{1,0:T(8,128)(2,1)} %collective-permute-done.10.other_down_ref.refs_0_), custom_call_target="tpu_custom_call" | custom-call | flops 1 | bytes 1 | tf_op jit(solution)/shard_map/mix_columns/pallas_call | solution.py:179
  115.9 1.3 collective-permute-start.17
  117.2 1.8 collective-permute-start.22
  119.0 4.2 %hidden_grads.3.own_ref = bf16[1024,1024]{1,0:T(8,128)(2,1)S(1)} custom-call(f32[1024,1024]{1,0:T(8,128)S(1)} %copy-done.10, bf16[512,2048]{1,0:T(8,128)(2,1)S(1)} %bitcast.6, bf16[128,2048]{1,0:T(8,128)(2,1)S(1)} %copy-done.8, bf16[128,2048]{1,0:T(8,128)(2,1)} %collective-permute-done.11.refs_3_.refs_4_, ...), custom_call_target="tpu_custom_call" | custom-call | flops 1 | bytes 1 | tf_op jit(solution)/shard_map/hidden_grads/pallas_call | solution.py:127
  123.2 8.6 %collective-permute-done.21.other_down_ref.refs_1_ = bf16[512,768]{1,0:T(8,128)(2,1)S(1)} collective-permute-done((bf16[512,768]{1,0:T(8,128)(2,1)S(1)}, bf16[512,768]{1,0:T(8,128)(2,1)S(1)}, u32[]{:S(2)}, u32[]{:S(2)}) %collective-permute-start.21) | collective-permute-done | bytes 786464 | tf_op jit(solution)/shard_map/ppermute | solution.py:271
  132.0 3.8 %collective-permute-start.18 = (bf16[128,512]{1,0:T(8,128)(2,1)S(1)}, bf16[128,512]{1,0:T(8,128)(2,1)S(1)}, u32[]{:S(2)}, u32[]{:S(2)}) collective-permute-start(bf16[128,512]{1,0:T(8,128)(2,1)S(1)} %get-tuple-element.109), channel_id=1, source_target_pairs={{0,12},{1,13},{2,14},{3,15},{4,0},{5,1},{6,2},{7,3},{8,4},{9,5},{1... | collective-permute-start | bytes 393224 | tf_op jit(solution)/shard_map/ppermute | solution.py:271
  135.8 2.2 mix_columns.4
  138.1 1.6 collective-permute-start.23
  140.3 4.4 %hidden_grads.4.refs_1_ = f32[1024,512]{1,0:T(8,128)S(1)} custom-call(bf16[512,512]{1,0:T(8,128)(2,1)} %collective-permute-done.10.other_down_ref.refs_0_, bf16[512,768]{1,0:T(8,128)(2,1)S(1)} %collective-permute-done.21.other_down_ref.refs_1_, bf16[128,2048]{1,0:T(8,128)(2,1)S(1)} %copy-done.8, bf16[128,2048]{1,0:T(8,128)(2,1)} %collective-permute-done.11.refs_3_.refs_4_, ...), custom_call_target="tpu_custom_call" | custom-call | flops 1 | bytes 1 | tf_op jit(solution)/shard_map/hidden_grads/pallas_call | solution.py:127
  144.7 2.3 collective-permute-done.20.refs_2_
  147.0 2.2 mix_columns.5
  149.3 1.4 collective-permute-start.27
  150.7 3.0 %hidden_grads.5.other_ref = bf16[1024,1024]{1,0:T(8,128)(2,1)S(1)} custom-call(f32[1024,1024]{1,0:T(8,128)S(1)} %copy-done.9, f32[1024,512]{1,0:T(8,128)S(1)} %hidden_grads.4.refs_1_, bf16[512,768]{1,0:T(8,128)(2,1)S(1)} %collective-permute-done.22.other_down_ref.refs_2_, bf16[128,2048]{1,0:T(8,128)(2,1)S(1)} %copy-done.8, ...), custom_call_target="tpu_custom_call" | custom-call | flops 1 | bytes 1 | tf_op jit(solution)/shard_map/hidden_grads/pallas_call | solution.py:127
  154.2 5.2 %back_columns.3 = (f32[512,768]{1,0:T(8,128)S(1)}, bf16[512,768]{1,0:T(8,128)(2,1)S(1)}) custom-call(bf16[1024,1024]{1,0:T(8,128)(2,1)S(1)} %hidden_grads.3.own_ref, bf16[1024,1024]{1,0:T(8,128)(2,1)S(1)} %hidden_grads.5.other_ref, bf16[2,2048,256]{2,1,0:T(8,128)(2,1)S(1)} %copy-done.1, bf16[2,2048,256]{2,1,0:T(8,128)(2,1)S(1)} %copy-done.2, ...), custom_call_target="tpu_custom_call" | custom-call | flops 1 | bytes 1 | tf_op jit(solution)/shard_map/back_columns/pallas_call | solution.py:179
  159.5 0.7 collective-permute-start.31
  160.2 1.5 collective-permute-start.24
  162.3 4.5 %collective-permute-done.24.refs_4_ = bf16[128,768]{1,0:T(8,128)(2,1)S(1)} collective-permute-done((bf16[128,768]{1,0:T(8,128)(2,1)S(1)}, bf16[128,768]{1,0:T(8,128)(2,1)S(1)}, u32[]{:S(2)}, u32[]{:S(2)}) %collective-permute-start.24) | collective-permute-done | bytes 196640 | tf_op jit(solution)/shard_map/ppermute | solution.py:271
  166.8 2.4 %collective-permute-done.25.come_ref = bf16[128,768]{1,0:T(8,128)(2,1)S(1)} collective-permute-done((bf16[128,768]{1,0:T(8,128)(2,1)S(1)}, bf16[128,768]{1,0:T(8,128)(2,1)S(1)}, u32[]{:S(2)}, u32[]{:S(2)}) %collective-permute-start.25) | collective-permute-done | bytes 196640 | tf_op jit(solution)/shard_map/ppermute | solution.py:271
  169.2 5.2 %back_columns.4 = (f32[512,768]{1,0:T(8,128)S(1)}, bf16[512,768]{1,0:T(8,128)(2,1)S(1)}) custom-call(bf16[1024,1024]{1,0:T(8,128)(2,1)S(1)} %hidden_grads.3.own_ref, bf16[1024,1024]{1,0:T(8,128)(2,1)S(1)} %hidden_grads.5.other_ref, bf16[2,2048,256]{2,1,0:T(8,128)(2,1)S(1)} %copy-done.1, bf16[2,2048,256]{2,1,0:T(8,128)(2,1)S(1)} %copy-done.2, ...), custom_call_target="tpu_custom_call" | custom-call | flops 1 | bytes 1 | tf_op jit(solution)/shard_map/back_columns/pallas_call | solution.py:179
  174.5 1.4 collective-permute-start.35
  177.0 3.4 %collective-permute-start.28 = (bf16[128,768]{1,0:T(8,128)(2,1)S(1)}, bf16[128,768]{1,0:T(8,128)(2,1)S(1)}, u32[]{:S(2)}, u32[]{:S(2)}) collective-permute-start(bf16[128,768]{1,0:T(8,128)(2,1)S(1)} %get-tuple-element.137), channel_id=1, source_target_pairs={{0,12},{1,13},{2,14},{3,15},{4,0},{5,1},{6,2},{7,3},{8,4},{9,5},{1... | collective-permute-start | bytes 589832 | tf_op jit(solution)/shard_map/ppermute | solution.py:271
  180.4 4.6 %collective-permute-done.29.come_ref = bf16[128,768]{1,0:T(8,128)(2,1)S(1)} collective-permute-done((bf16[128,768]{1,0:T(8,128)(2,1)S(1)}, bf16[128,768]{1,0:T(8,128)(2,1)S(1)}, u32[]{:S(2)}, u32[]{:S(2)}) %collective-permute-start.29) | collective-permute-done | bytes 196640 | tf_op jit(solution)/shard_map/ppermute | solution.py:271
  184.9 3.9 %back_columns.5 = (f32[512,512]{1,0:T(8,128)S(1)}, bf16[512,512]{1,0:T(8,128)(2,1)S(1)}) custom-call(bf16[1024,1024]{1,0:T(8,128)(2,1)S(1)} %hidden_grads.3.own_ref, bf16[1024,1024]{1,0:T(8,128)(2,1)S(1)} %hidden_grads.5.other_ref, bf16[2,2048,256]{2,1,0:T(8,128)(2,1)S(1)} %copy-done.1, bf16[2,2048,256]{2,1,0:T(8,128)(2,1)S(1)} %copy-done.2, ...), custom_call_target="tpu_custom_call" | custom-call | flops 1 | bytes 1 | tf_op jit(solution)/shard_map/back_columns/pallas_call | solution.py:179
  188.8 2.1 collective-permute-done.31.come_ref
  191.2 0.7 collective-permute-start.33
  191.9 3.2 %collective-permute-start.32 = (bf16[128,768]{1,0:T(8,128)(2,1)S(1)}, bf16[128,768]{1,0:T(8,128)(2,1)S(1)}, u32[]{:S(2)}, u32[]{:S(2)}) collective-permute-start(bf16[128,768]{1,0:T(8,128)(2,1)S(1)} %get-tuple-element.147), channel_id=1, source_target_pairs={{0,12},{1,13},{2,14},{3,15},{4,0},{5,1},{6,2},{7,3},{8,4},{9,5},{1... | collective-permute-start | bytes 589832 | tf_op jit(solution)/shard_map/ppermute | solution.py:271
  195.1 4.4 %collective-permute-done.30.refs_8_ = bf16[128,768]{1,0:T(8,128)(2,1)S(1)} collective-permute-done((bf16[128,768]{1,0:T(8,128)(2,1)S(1)}, bf16[128,768]{1,0:T(8,128)(2,1)S(1)}, u32[]{:S(2)}, u32[]{:S(2)}) %collective-permute-start.30) | collective-permute-done | bytes 196640 | tf_op jit(solution)/shard_map/ppermute | solution.py:271
  199.5 1.1 finish.2
  200.6 1.0 collective-permute-done.33.come_ref
  201.6 6.2 %collective-permute-done.35.come_ref = bf16[512,768]{1,0:T(8,128)(2,1)S(1)} collective-permute-done((bf16[512,768]{1,0:T(8,128)(2,1)S(1)}, bf16[512,768]{1,0:T(8,128)(2,1)S(1)}, u32[]{:S(2)}, u32[]{:S(2)}) %collective-permute-start.35) | collective-permute-done | bytes 786464 | tf_op jit(solution)/shard_map/ppermute | solution.py:271
  207.9 3.8 %collective-permute-start.36 = (bf16[128,768]{1,0:T(8,128)(2,1)S(1)}, bf16[128,768]{1,0:T(8,128)(2,1)S(1)}, u32[]{:S(2)}, u32[]{:S(2)}) collective-permute-start(bf16[128,768]{1,0:T(8,128)(2,1)S(1)} %get-tuple-element.156), channel_id=1, source_target_pairs={{0,12},{1,13},{2,14},{3,15},{4,0},{5,1},{6,2},{7,3},{8,4},{9,5},{1... | collective-permute-start | bytes 589832 | tf_op jit(solution)/shard_map/ppermute | solution.py:271
  211.9 4.3 %collective-permute-done.37.come_ref = bf16[128,768]{1,0:T(8,128)(2,1)S(1)} collective-permute-done((bf16[128,768]{1,0:T(8,128)(2,1)S(1)}, bf16[128,768]{1,0:T(8,128)(2,1)S(1)}, u32[]{:S(2)}, u32[]{:S(2)}) %collective-permute-start.37) | collective-permute-done | bytes 196640 | tf_op jit(solution)/shard_map/ppermute | solution.py:271
  216.2 6.6 %collective-permute-done.36.refs_4_ = bf16[128,768]{1,0:T(8,128)(2,1)S(1)} collective-permute-done((bf16[128,768]{1,0:T(8,128)(2,1)S(1)}, bf16[128,768]{1,0:T(8,128)(2,1)S(1)}, u32[]{:S(2)}, u32[]{:S(2)}) %collective-permute-start.36) | collective-permute-done | bytes 196640 | tf_op jit(solution)/shard_map/ppermute | solution.py:271
  222.9 0.9 collective-permute-done.34.refs_2_
  223.9 3.5 %collective-permute-start.41 = (bf16[128,512]{1,0:T(8,128)(2,1)S(1)}, bf16[128,512]{1,0:T(8,128)(2,1)S(1)}, u32[]{:S(2)}, u32[]{:S(2)}) collective-permute-start(bf16[128,512]{1,0:T(8,128)(2,1)S(1)} %get-tuple-element.168), channel_id=1, source_target_pairs={{0,8},{1,9},{2,10},{3,11},{4,12},{5,13},{6,14},{7,15},{8,0},{9,1},... | collective-permute-start | bytes 393224 | tf_op jit(solution)/shard_map/ppermute | solution.py:271
  227.7 4.2 %collective-permute-done.40.refs_7_ = bf16[128,512]{1,0:T(8,128)(2,1)S(1)} collective-permute-done((bf16[128,512]{1,0:T(8,128)(2,1)S(1)}, bf16[128,512]{1,0:T(8,128)(2,1)S(1)}, u32[]{:S(2)}, u32[]{:S(2)}) %collective-permute-start.40) | collective-permute-done | bytes 131104 | tf_op jit(solution)/shard_map/ppermute | solution.py:271
  231.9 2.6 %collective-permute-done.41.refs_8_ = bf16[128,512]{1,0:T(8,128)(2,1)S(1)} collective-permute-done((bf16[128,512]{1,0:T(8,128)(2,1)S(1)}, bf16[128,512]{1,0:T(8,128)(2,1)S(1)}, u32[]{:S(2)}, u32[]{:S(2)}) %collective-permute-start.41) | collective-permute-done | bytes 131104 | tf_op jit(solution)/shard_map/ppermute | solution.py:271
  234.5 1.1 finish.3
  (91 shorter events, 7.7 us)
Async XLA Ops:
  0.6 76.7 %copy-start.8 = (bf16[128,2048]{1,0:T(8,128)(2,1)S(1)}, bf16[128,2048]{1,0:T(8,128)(2,1)}, u32[]{:S(2)}) copy-start(bf16[128,2048]{1,0:T(8,128)(2,1)} %refs_3_) | copy-start | bytes 1572868
  3.6 73.7 %collective-permute-start.8 = (bf16[2,2048,256]{2,1,0:T(8,128)(2,1)}, bf16[2,2048,256]{2,1,0:T(8,128)(2,1)S(1)}, u32[]{:S(2)}, u32[]{:S(2)}) collective-permute-start(bf16[2,2048,256]{2,1,0:T(8,128)(2,1)} %refs_0_.5), channel_id=1, source_target_pairs={{0,1},{1,0},{2,3},{3,2},{4,5},{5,4},{6,7},{7,6},{8,9},{9,8},{10,11... | collective-permute-start | bytes 6291464 | tf_op jit(solution)/shard_map/ppermute | solution.py:271
  6.5 17.6 %collective-permute-start.3 = (bf16[128,2176]{1,0:T(8,128)(2,1)}, bf16[128,2176]{1,0:T(8,128)(2,1)S(1)}, u32[]{:S(2)}, u32[]{:S(2)}) collective-permute-start(bf16[128,2176]{1,0:T(8,128)(2,1)} %concatenate.3.refs_0_), channel_id=1, source_target_pairs={{0,4},{1,5},{2,6},{3,7},{4,8},{5,9},{6,10},{7,11},{8,12},{9,13},{1... | collective-permute-start | bytes 1671176 | tf_op jit(solution)/shard_map/ppermute | solution.py:271
  8.1 15.1 %collective-permute-start.6 = (bf16[128,2048]{1,0:T(8,128)(2,1)}, bf16[128,2048]{1,0:T(8,128)(2,1)S(1)}, u32[]{:S(2)}, u32[]{:S(2)}) collective-permute-start(bf16[128,2048]{1,0:T(8,128)(2,1)} %refs_3_), channel_id=1, source_target_pairs={{0,2},{1,3},{2,0},{3,1},{4,6},{5,7},{6,4},{7,5},{8,10},{9,11},{10,... | collective-permute-start | bytes 1572872 | tf_op jit(solution)/shard_map/ppermute | solution.py:271
  9.6 25.0 %collective-permute-start = (bf16[128,2176]{1,0:T(8,128)(2,1)}, bf16[128,2176]{1,0:T(8,128)(2,1)S(1)}, u32[]{:S(2)}, u32[]{:S(2)}) collective-permute-start(bf16[128,2176]{1,0:T(8,128)(2,1)} %concatenate.3.refs_0_), channel_id=1, source_target_pairs={{0,12},{1,13},{2,14},{3,15},{4,0},{5,1},{6,2},{7,3},{8,4},{9,5},{1... | collective-permute-start | bytes 1671176 | tf_op jit(solution)/shard_map/ppermute | solution.py:271
  11.8 22.8 %collective-permute-start.1 = (bf16[128,2176]{1,0:T(8,128)(2,1)}, bf16[128,2176]{1,0:T(8,128)(2,1)S(1)}, u32[]{:S(2)}, u32[]{:S(2)}) collective-permute-start(bf16[128,2176]{1,0:T(8,128)(2,1)} %concatenate.3.refs_0_), channel_id=1, source_target_pairs={{0,2},{1,3},{2,0},{3,1},{4,6},{5,7},{6,4},{7,5},{8,10},{9,11},{10,... | collective-permute-start | bytes 1671176 | tf_op jit(solution)/shard_map/ppermute | solution.py:271
  24.1 14.4 %copy-start.11 = (bf16[128,2176]{1,0:T(8,128)(2,1)}, bf16[128,2176]{1,0:T(8,128)(2,1)S(1)}, u32[]{:S(2)}) copy-start(bf16[128,2176]{1,0:T(8,128)(2,1)S(1)} %collective-permute-done.3.refs_3_) | copy-start | bytes 1671172
  24.1 77.3 %collective-permute-start.9 = (bf16[2,2048,256]{2,1,0:T(8,128)(2,1)}, bf16[2,2048,256]{2,1,0:T(8,128)(2,1)}, u32[]{:S(2)}, u32[]{:S(2)}) collective-permute-start(bf16[2,2048,256]{2,1,0:T(8,128)(2,1)} %refs_1_.5), channel_id=1, source_target_pairs={{0,1},{1,0},{2,3},{3,2},{4,5},{5,4},{6,7},{7,6},{8,9},{9,8},{10,11... | collective-permute-start | bytes 6291464 | tf_op jit(solution)/shard_map/ppermute | solution.py:271
  34.6 29.9 %copy-start.12 = (bf16[128,2176]{1,0:T(8,128)(2,1)}, bf16[128,2176]{1,0:T(8,128)(2,1)S(1)}, u32[]{:S(2)}) copy-start(bf16[128,2176]{1,0:T(8,128)(2,1)S(1)} %collective-permute-done.refs_1_) | copy-start | bytes 1671172
  34.6 29.9 %copy-start.13 = (bf16[128,2176]{1,0:T(8,128)(2,1)}, bf16[128,2176]{1,0:T(8,128)(2,1)S(1)}, u32[]{:S(2)}) copy-start(bf16[128,2176]{1,0:T(8,128)(2,1)S(1)} %collective-permute-done.1.refs_4_) | copy-start | bytes 1671172
  34.6 14.6 %collective-permute-start.2 = (bf16[128,2176]{1,0:T(8,128)(2,1)S(1)}, bf16[128,2176]{1,0:T(8,128)(2,1)S(1)}, u32[]{:S(2)}, u32[]{:S(2)}) collective-permute-start(bf16[128,2176]{1,0:T(8,128)(2,1)S(1)} %collective-permute-done.refs_1_), channel_id=1, source_target_pairs={{0,12},{1,13},{2,14},{3,15},{4,0},{5,1},{6,2},{7,3},{8,4},{9,5},{1... | collective-permute-start | bytes 1671176 | tf_op jit(solution)/shard_map/ppermute | solution.py:271
  37.0 15.6 %collective-permute-start.4 = (bf16[128,2176]{1,0:T(8,128)(2,1)S(1)}, bf16[128,2176]{1,0:T(8,128)(2,1)S(1)}, u32[]{:S(2)}, u32[]{:S(2)}) collective-permute-start(bf16[128,2176]{1,0:T(8,128)(2,1)S(1)} %collective-permute-done.refs_1_), channel_id=1, source_target_pairs={{0,2},{1,3},{2,0},{3,1},{4,6},{5,7},{6,4},{7,5},{8,10},{9,11},{10,... | collective-permute-start | bytes 1671176 | tf_op jit(solution)/shard_map/ppermute | solution.py:271
  38.5 26.0 %collective-permute-start.7 = (bf16[128,2176]{1,0:T(8,128)(2,1)S(1)}, bf16[128,2176]{1,0:T(8,128)(2,1)S(1)}, u32[]{:S(2)}, u32[]{:S(2)}) collective-permute-start(bf16[128,2176]{1,0:T(8,128)(2,1)S(1)} %collective-permute-done.3.refs_3_), channel_id=1, source_target_pairs={{0,2},{1,3},{2,0},{3,1},{4,6},{5,7},{6,4},{7,5},{8,10},{9,11},{10,... | collective-permute-start | bytes 1671176 | tf_op jit(solution)/shard_map/ppermute | solution.py:271
  49.2 24.1 %copy-start.14 = (bf16[128,2176]{1,0:T(8,128)(2,1)}, bf16[128,2176]{1,0:T(8,128)(2,1)S(1)}, u32[]{:S(2)}) copy-start(bf16[128,2176]{1,0:T(8,128)(2,1)S(1)} %collective-permute-done.2.refs_2_) | copy-start | bytes 1671172
  52.5 22.3 %copy-start.15 = (bf16[128,2176]{1,0:T(8,128)(2,1)}, bf16[128,2176]{1,0:T(8,128)(2,1)S(1)}, u32[]{:S(2)}) copy-start(bf16[128,2176]{1,0:T(8,128)(2,1)S(1)} %collective-permute-done.4.refs_5_) | copy-start | bytes 1671172
  52.5 20.8 %collective-permute-start.5 = (bf16[128,2176]{1,0:T(8,128)(2,1)S(1)}, bf16[128,2176]{1,0:T(8,128)(2,1)S(1)}, u32[]{:S(2)}, u32[]{:S(2)}) collective-permute-start(bf16[128,2176]{1,0:T(8,128)(2,1)S(1)} %collective-permute-done.2.refs_2_), channel_id=1, source_target_pairs={{0,2},{1,3},{2,0},{3,1},{4,6},{5,7},{6,4},{7,5},{8,10},{9,11},{10,... | collective-permute-start | bytes 1671176 | tf_op jit(solution)/shard_map/ppermute | solution.py:271
  54.0 10.4 %collective-permute-start.11 = (bf16[128,2048]{1,0:T(8,128)(2,1)}, bf16[128,2048]{1,0:T(8,128)(2,1)}, u32[]{:S(2)}, u32[]{:S(2)}) collective-permute-start(bf16[128,2048]{1,0:T(8,128)(2,1)} %refs_3_), channel_id=1, source_target_pairs={{0,12},{1,13},{2,14},{3,15},{4,0},{5,1},{6,2},{7,3},{8,4},{9,5},{1... | collective-permute-start | bytes 1572872 | tf_op jit(solution)/shard_map/ppermute | solution.py:271
  64.5 10.9 %copy-start.16 = (bf16[128,2176]{1,0:T(8,128)(2,1)}, bf16[128,2176]{1,0:T(8,128)(2,1)S(1)}, u32[]{:S(2)}) copy-start(bf16[128,2176]{1,0:T(8,128)(2,1)S(1)} %collective-permute-done.7.refs_7_) | copy-start | bytes 1671172
  73.3 2.1 copy-start.17
  73.3 17.1 %collective-permute-start.12 = (bf16[128,2048]{1,0:T(8,128)(2,1)}, bf16[128,2048]{1,0:T(8,128)(2,1)}, u32[]{:S(2)}, u32[]{:S(2)}) collective-permute-start(bf16[128,2048]{1,0:T(8,128)(2,1)} %collective-permute-done.11.refs_3_.refs_4_), channel_id=1, source_target_pairs={{0,2},{1,3},{2,0},{3,1},{4,6},{5,7},{6,4},{7,5},{8,10},{9,11},{10,... | collective-permute-start | bytes 1572872 | tf_op jit(solution)/shard_map/ppermute | solution.py:271
  74.8 15.6 %collective-permute-start.15 = (bf16[128,2048]{1,0:T(8,128)(2,1)}, bf16[128,2048]{1,0:T(8,128)(2,1)}, u32[]{:S(2)}, u32[]{:S(2)}) collective-permute-start(bf16[128,2048]{1,0:T(8,128)(2,1)} %collective-permute-done.11.refs_3_.refs_4_), channel_id=1, source_target_pairs={{0,12},{1,13},{2,14},{3,15},{4,0},{5,1},{6,2},{7,3},{8,4},{9,5},{1... | collective-permute-start | bytes 1572872 | tf_op jit(solution)/shard_map/ppermute | solution.py:271
  77.3 13.1 %copy-start.3 = (bf16[2,2048,256]{2,1,0:T(8,128)(2,1)}, bf16[2,2048,256]{2,1,0:T(8,128)(2,1)S(1)}, u32[]{:S(2)}) copy-start(bf16[2,2048,256]{2,1,0:T(8,128)(2,1)S(1)} %collective-permute-done.8.gate_ref.refs_2_) | copy-start | bytes 6291460
  77.3 22.6 %collective-permute-start.13 = (bf16[128,2048]{1,0:T(8,128)(2,1)S(1)}, bf16[128,2048]{1,0:T(8,128)(2,1)}, u32[]{:S(2)}, u32[]{:S(2)}) collective-permute-start(bf16[128,2048]{1,0:T(8,128)(2,1)S(1)} %copy-done.8), channel_id=1, source_target_pairs={{0,4},{1,5},{2,6},{3,7},{4,8},{5,9},{6,10},{7,11},{8,12},{9,13},{1... | collective-permute-start | bytes 1572872 | tf_op jit(solution)/shard_map/ppermute | solution.py:271
  78.8 32.5 %collective-permute-start.10 = (bf16[512,512]{1,0:T(8,128)(2,1)}, bf16[512,512]{1,0:T(8,128)(2,1)}, u32[]{:S(2)}, u32[]{:S(2)}) collective-permute-start(bf16[512,512]{1,0:T(8,128)(2,1)} %slice.12), channel_id=1, source_target_pairs={{0,1},{1,0},{2,3},{3,2},{4,5},{5,4},{6,7},{7,6},{8,9},{9,8},{10,11... | collective-permute-start | bytes 1572872 | tf_op jit(solution)/shard_map/ppermute | solution.py:271
  80.3 20.1 %copy-start = (bf16[2,256,2048]{2,1,0:T(8,128)(2,1)S(1)}, bf16[2,256,2048]{2,1,0:T(8,128)(2,1)}, u32[]{:S(2)}) copy-start(bf16[2,256,2048]{2,1,0:T(8,128)(2,1)} %param.13) | copy-start | bytes 6291460
  90.4 21.3 %collective-permute-start.16 = (bf16[128,2048]{1,0:T(8,128)(2,1)}, bf16[128,2048]{1,0:T(8,128)(2,1)S(1)}, u32[]{:S(2)}, u32[]{:S(2)}) collective-permute-start(bf16[128,2048]{1,0:T(8,128)(2,1)} %collective-permute-done.15.refs_4_.refs_5_), channel_id=1, source_target_pairs={{0,2},{1,3},{2,0},{3,1},{4,6},{5,7},{6,4},{7,5},{8,10},{9,11},{10,... | collective-permute-start | bytes 1572872 | tf_op jit(solution)/shard_map/ppermute | solution.py:271
  99.8 12.0 %collective-permute-start.14 = (bf16[128,2048]{1,0:T(8,128)(2,1)}, bf16[128,2048]{1,0:T(8,128)(2,1)S(1)}, u32[]{:S(2)}, u32[]{:S(2)}) collective-permute-start(bf16[128,2048]{1,0:T(8,128)(2,1)} %collective-permute-done.13.refs_5_.refs_6_), channel_id=1, source_target_pairs={{0,2},{1,3},{2,0},{3,1},{4,6},{5,7},{6,4},{7,5},{8,10},{9,11},{10,... | collective-permute-start | bytes 1572872 | tf_op jit(solution)/shard_map/ppermute | solution.py:271
  101.4 10.5 %copy-start.5 = (bf16[1024,512]{1,0:T(8,128)(2,1)S(1)}, bf16[1024,512]{1,0:T(8,128)(2,1)}, u32[]{:S(2)}) copy-start(bf16[1024,512]{1,0:T(8,128)(2,1)} %get-tuple-element.93.own_ref) | copy-start | bytes 3145732
  111.3 20.5 %collective-permute-start.21 = (bf16[512,768]{1,0:T(8,128)(2,1)S(1)}, bf16[512,768]{1,0:T(8,128)(2,1)S(1)}, u32[]{:S(2)}, u32[]{:S(2)}) collective-permute-start(bf16[512,768]{1,0:T(8,128)(2,1)S(1)} %get-tuple-element.113), channel_id=1, source_target_pairs={{0,1},{1,0},{2,3},{3,2},{4,5},{5,4},{6,7},{7,6},{8,9},{9,8},{10,11... | collective-permute-start | bytes 2359304 | tf_op jit(solution)/shard_map/ppermute | solution.py:271
  111.9 1.2 copy-start.6
  113.1 5.9 %copy-start.10 = (f32[1024,1024]{1,0:T(8,128)S(1)}, f32[1024,1024]{1,0:T(8,128)}, u32[]{:S(2)}) copy-start(f32[1024,1024]{1,0:T(8,128)} %get-tuple-element.114.refs_0_) | copy-start | bytes 12582916
  115.9 15.9 %collective-permute-start.17 = (bf16[512,512]{1,0:T(8,128)(2,1)S(1)}, bf16[512,512]{1,0:T(8,128)(2,1)S(1)}, u32[]{:S(2)}, u32[]{:S(2)}) collective-permute-start(bf16[512,512]{1,0:T(8,128)(2,1)S(1)} %get-tuple-element.107), channel_id=1, source_target_pairs={{0,2},{1,3},{2,0},{3,1},{4,6},{5,7},{6,4},{7,5},{8,10},{9,11},{10,... | collective-permute-start | bytes 1572872 | tf_op jit(solution)/shard_map/ppermute | solution.py:271
  117.2 29.8 %collective-permute-start.22 = (bf16[512,768]{1,0:T(8,128)(2,1)}, bf16[512,768]{1,0:T(8,128)(2,1)S(1)}, u32[]{:S(2)}, u32[]{:S(2)}) collective-permute-start(bf16[512,768]{1,0:T(8,128)(2,1)} %get-tuple-element.118), channel_id=1, source_target_pairs={{0,1},{1,0},{2,3},{3,2},{4,5},{5,4},{6,7},{7,6},{8,9},{9,8},{10,11... | collective-permute-start | bytes 2359304 | tf_op jit(solution)/shard_map/ppermute | solution.py:271
  123.2 12.6 %copy-start.7 = (bf16[1024,512]{1,0:T(8,128)(2,1)S(1)}, bf16[1024,512]{1,0:T(8,128)(2,1)}, u32[]{:S(2)}) copy-start(bf16[1024,512]{1,0:T(8,128)(2,1)} %get-tuple-element.97.other_ref) | copy-start | bytes 3145732
  132.0 8.2 %collective-permute-start.19 = (bf16[128,512]{1,0:T(8,128)(2,1)S(1)}, bf16[128,512]{1,0:T(8,128)(2,1)S(1)}, u32[]{:S(2)}, u32[]{:S(2)}) collective-permute-start(bf16[128,512]{1,0:T(8,128)(2,1)S(1)} %get-tuple-element.111), channel_id=1, source_target_pairs={{0,4},{1,5},{2,6},{3,7},{4,8},{5,9},{6,10},{7,11},{8,12},{9,13},{1... | collective-permute-start | bytes 393224 | tf_op jit(solution)/shard_map/ppermute | solution.py:271
  132.0 8.2 %collective-permute-start.18 = (bf16[128,512]{1,0:T(8,128)(2,1)S(1)}, bf16[128,512]{1,0:T(8,128)(2,1)S(1)}, u32[]{:S(2)}, u32[]{:S(2)}) collective-permute-start(bf16[128,512]{1,0:T(8,128)(2,1)S(1)} %get-tuple-element.109), channel_id=1, source_target_pairs={{0,12},{1,13},{2,14},{3,15},{4,0},{5,1},{6,2},{7,3},{8,4},{9,5},{1... | collective-permute-start | bytes 393224 | tf_op jit(solution)/shard_map/ppermute | solution.py:271
  138.1 21.3 %collective-permute-start.23 = (bf16[512,768]{1,0:T(8,128)(2,1)S(1)}, bf16[512,768]{1,0:T(8,128)(2,1)S(1)}, u32[]{:S(2)}, u32[]{:S(2)}) collective-permute-start(bf16[512,768]{1,0:T(8,128)(2,1)S(1)} %get-tuple-element.125), channel_id=1, source_target_pairs={{0,2},{1,3},{2,0},{3,1},{4,6},{5,7},{6,4},{7,5},{8,10},{9,11},{10,... | collective-permute-start | bytes 2359304 | tf_op jit(solution)/shard_map/ppermute | solution.py:271
  140.2 6.8 %collective-permute-start.20 = (bf16[128,512]{1,0:T(8,128)(2,1)S(1)}, bf16[128,512]{1,0:T(8,128)(2,1)S(1)}, u32[]{:S(2)}, u32[]{:S(2)}) collective-permute-start(bf16[128,512]{1,0:T(8,128)(2,1)S(1)} %add_piece.5), channel_id=1, source_target_pairs={{0,4},{1,5},{2,6},{3,7},{4,8},{5,9},{6,10},{7,11},{8,12},{9,13},{1... | collective-permute-start | bytes 393224 | tf_op jit(solution)/shard_map/ppermute | solution.py:271
  144.7 6.0 %copy-start.9 = (f32[1024,1024]{1,0:T(8,128)S(1)}, f32[1024,1024]{1,0:T(8,128)}, u32[]{:S(2)}) copy-start(f32[1024,1024]{1,0:T(8,128)} %get-tuple-element.122.refs_0_) | copy-start | bytes 12582916
  149.3 25.1 %collective-permute-start.27 = (bf16[512,768]{1,0:T(8,128)(2,1)S(1)}, bf16[512,768]{1,0:T(8,128)(2,1)S(1)}, u32[]{:S(2)}, u32[]{:S(2)}) collective-permute-start(bf16[512,768]{1,0:T(8,128)(2,1)S(1)} %get-tuple-element.135), channel_id=1, source_target_pairs={{0,2},{1,3},{2,0},{3,1},{4,6},{5,7},{6,4},{7,5},{8,10},{9,11},{10,... | collective-permute-start | bytes 2359304 | tf_op jit(solution)/shard_map/ppermute | solution.py:271
  150.7 3.0 %copy-start.1 = (bf16[2,2048,256]{2,1,0:T(8,128)(2,1)S(1)}, bf16[2,2048,256]{2,1,0:T(8,128)(2,1)}, u32[]{:S(2)}) copy-start(bf16[2,2048,256]{2,1,0:T(8,128)(2,1)} %refs_0_.5) | copy-start | bytes 6291460
  150.7 3.1 %copy-start.2 = (bf16[2,2048,256]{2,1,0:T(8,128)(2,1)S(1)}, bf16[2,2048,256]{2,1,0:T(8,128)(2,1)}, u32[]{:S(2)}) copy-start(bf16[2,2048,256]{2,1,0:T(8,128)(2,1)} %refs_1_.5) | copy-start | bytes 6291460
  150.7 3.5 %copy-start.4 = (bf16[2,2048,256]{2,1,0:T(8,128)(2,1)S(1)}, bf16[2,2048,256]{2,1,0:T(8,128)(2,1)}, u32[]{:S(2)}) copy-start(bf16[2,2048,256]{2,1,0:T(8,128)(2,1)} %copy-done.3) | copy-start | bytes 6291460
  159.5 31.4 %collective-permute-start.31 = (bf16[512,768]{1,0:T(8,128)(2,1)S(1)}, bf16[512,768]{1,0:T(8,128)(2,1)S(1)}, u32[]{:S(2)}, u32[]{:S(2)}) collective-permute-start(bf16[512,768]{1,0:T(8,128)(2,1)S(1)} %get-tuple-element.145), channel_id=1, source_target_pairs={{0,2},{1,3},{2,0},{3,1},{4,6},{5,7},{6,4},{7,5},{8,10},{9,11},{10,... | collective-permute-start | bytes 2359304 | tf_op jit(solution)/shard_map/ppermute | solution.py:271
  160.2 6.6 %collective-permute-start.24 = (bf16[128,768]{1,0:T(8,128)(2,1)S(1)}, bf16[128,768]{1,0:T(8,128)(2,1)S(1)}, u32[]{:S(2)}, u32[]{:S(2)}) collective-permute-start(bf16[128,768]{1,0:T(8,128)(2,1)S(1)} %get-tuple-element.127), channel_id=1, source_target_pairs={{0,12},{1,13},{2,14},{3,15},{4,0},{5,1},{6,2},{7,3},{8,4},{9,5},{1... | collective-permute-start | bytes 589832 | tf_op jit(solution)/shard_map/ppermute | solution.py:271
  161.7 7.5 %collective-permute-start.25 = (bf16[128,768]{1,0:T(8,128)(2,1)S(1)}, bf16[128,768]{1,0:T(8,128)(2,1)S(1)}, u32[]{:S(2)}, u32[]{:S(2)}) collective-permute-start(bf16[128,768]{1,0:T(8,128)(2,1)S(1)} %get-tuple-element.129), channel_id=1, source_target_pairs={{0,4},{1,5},{2,6},{3,7},{4,8},{5,9},{6,10},{7,11},{8,12},{9,13},{1... | collective-permute-start | bytes 589832 | tf_op jit(solution)/shard_map/ppermute | solution.py:271
  174.5 33.2 %collective-permute-start.35 = (bf16[512,768]{1,0:T(8,128)(2,1)S(1)}, bf16[512,768]{1,0:T(8,128)(2,1)S(1)}, u32[]{:S(2)}, u32[]{:S(2)}) collective-permute-start(bf16[512,768]{1,0:T(8,128)(2,1)S(1)} %get-tuple-element.153), channel_id=1, source_target_pairs={{0,2},{1,3},{2,0},{3,1},{4,6},{5,7},{6,4},{7,5},{8,10},{9,11},{10,... | collective-permute-start | bytes 2359304 | tf_op jit(solution)/shard_map/ppermute | solution.py:271
  175.9 9.0 %collective-permute-start.29 = (bf16[128,768]{1,0:T(8,128)(2,1)S(1)}, bf16[128,768]{1,0:T(8,128)(2,1)S(1)}, u32[]{:S(2)}, u32[]{:S(2)}) collective-permute-start(bf16[128,768]{1,0:T(8,128)(2,1)S(1)} %get-tuple-element.139), channel_id=1, source_target_pairs={{0,4},{1,5},{2,6},{3,7},{4,8},{5,9},{6,10},{7,11},{8,12},{9,13},{1... | collective-permute-start | bytes 589832 | tf_op jit(solution)/shard_map/ppermute | solution.py:271
  176.5 14.7 %collective-permute-start.26 = (bf16[128,768]{1,0:T(8,128)(2,1)S(1)}, bf16[128,768]{1,0:T(8,128)(2,1)S(1)}, u32[]{:S(2)}, u32[]{:S(2)}) collective-permute-start(bf16[128,768]{1,0:T(8,128)(2,1)S(1)} %add_piece.6), channel_id=1, source_target_pairs={{0,4},{1,5},{2,6},{3,7},{4,8},{5,9},{6,10},{7,11},{8,12},{9,13},{1... | collective-permute-start | bytes 589832 | tf_op jit(solution)/shard_map/ppermute | solution.py:271
  177.0 14.2 %collective-permute-start.28 = (bf16[128,768]{1,0:T(8,128)(2,1)S(1)}, bf16[128,768]{1,0:T(8,128)(2,1)S(1)}, u32[]{:S(2)}, u32[]{:S(2)}) collective-permute-start(bf16[128,768]{1,0:T(8,128)(2,1)S(1)} %get-tuple-element.137), channel_id=1, source_target_pairs={{0,12},{1,13},{2,14},{3,15},{4,0},{5,1},{6,2},{7,3},{8,4},{9,5},{1... | collective-permute-start | bytes 589832 | tf_op jit(solution)/shard_map/ppermute | solution.py:271
  191.0 31.8 %collective-permute-start.39 = (bf16[512,512]{1,0:T(8,128)(2,1)S(1)}, bf16[512,512]{1,0:T(8,128)(2,1)S(1)}, u32[]{:S(2)}, u32[]{:S(2)}) collective-permute-start(bf16[512,512]{1,0:T(8,128)(2,1)S(1)} %get-tuple-element.161), channel_id=1, source_target_pairs={{0,2},{1,3},{2,0},{3,1},{4,6},{5,7},{6,4},{7,5},{8,10},{9,11},{10,... | collective-permute-start | bytes 1572872 | tf_op jit(solution)/shard_map/ppermute | solution.py:271
  191.2 8.3 %collective-permute-start.30 = (bf16[128,768]{1,0:T(8,128)(2,1)S(1)}, bf16[128,768]{1,0:T(8,128)(2,1)S(1)}, u32[]{:S(2)}, u32[]{:S(2)}) collective-permute-start(bf16[128,768]{1,0:T(8,128)(2,1)S(1)} %add_piece.7), channel_id=1, source_target_pairs={{0,4},{1,5},{2,6},{3,7},{4,8},{5,9},{6,10},{7,11},{8,12},{9,13},{1... | collective-permute-start | bytes 589832 | tf_op jit(solution)/shard_map/ppermute | solution.py:271
  191.2 10.3 %collective-permute-start.33 = (bf16[128,768]{1,0:T(8,128)(2,1)S(1)}, bf16[128,768]{1,0:T(8,128)(2,1)S(1)}, u32[]{:S(2)}, u32[]{:S(2)}) collective-permute-start(bf16[128,768]{1,0:T(8,128)(2,1)S(1)} %get-tuple-element.149), channel_id=1, source_target_pairs={{0,4},{1,5},{2,6},{3,7},{4,8},{5,9},{6,10},{7,11},{8,12},{9,13},{1... | collective-permute-start | bytes 589832 | tf_op jit(solution)/shard_map/ppermute | solution.py:271
  191.9 19.9 %collective-permute-start.32 = (bf16[128,768]{1,0:T(8,128)(2,1)S(1)}, bf16[128,768]{1,0:T(8,128)(2,1)S(1)}, u32[]{:S(2)}, u32[]{:S(2)}) collective-permute-start(bf16[128,768]{1,0:T(8,128)(2,1)S(1)} %get-tuple-element.147), channel_id=1, source_target_pairs={{0,12},{1,13},{2,14},{3,15},{4,0},{5,1},{6,2},{7,3},{8,4},{9,5},{1... | collective-permute-start | bytes 589832 | tf_op jit(solution)/shard_map/ppermute | solution.py:271
  207.9 8.3 %collective-permute-start.37 = (bf16[128,768]{1,0:T(8,128)(2,1)S(1)}, bf16[128,768]{1,0:T(8,128)(2,1)S(1)}, u32[]{:S(2)}, u32[]{:S(2)}) collective-permute-start(bf16[128,768]{1,0:T(8,128)(2,1)S(1)} %get-tuple-element.158), channel_id=1, source_target_pairs={{0,4},{1,5},{2,6},{3,7},{4,8},{5,9},{6,10},{7,11},{8,12},{9,13},{1... | collective-permute-start | bytes 589832 | tf_op jit(solution)/shard_map/ppermute | solution.py:271
  207.9 14.9 %collective-permute-start.36 = (bf16[128,768]{1,0:T(8,128)(2,1)S(1)}, bf16[128,768]{1,0:T(8,128)(2,1)S(1)}, u32[]{:S(2)}, u32[]{:S(2)}) collective-permute-start(bf16[128,768]{1,0:T(8,128)(2,1)S(1)} %get-tuple-element.156), channel_id=1, source_target_pairs={{0,12},{1,13},{2,14},{3,15},{4,0},{5,1},{6,2},{7,3},{8,4},{9,5},{1... | collective-permute-start | bytes 589832 | tf_op jit(solution)/shard_map/ppermute | solution.py:271
  211.8 12.1 %collective-permute-start.34 = (bf16[128,768]{1,0:T(8,128)(2,1)S(1)}, bf16[128,768]{1,0:T(8,128)(2,1)S(1)}, u32[]{:S(2)}, u32[]{:S(2)}) collective-permute-start(bf16[128,768]{1,0:T(8,128)(2,1)S(1)} %add_piece.8), channel_id=1, source_target_pairs={{0,4},{1,5},{2,6},{3,7},{4,8},{5,9},{6,10},{7,11},{8,12},{9,13},{1... | collective-permute-start | bytes 589832 | tf_op jit(solution)/shard_map/ppermute | solution.py:271
  222.8 11.7 %collective-permute-start.38 = (bf16[128,768]{1,0:T(8,128)(2,1)S(1)}, bf16[128,768]{1,0:T(8,128)(2,1)S(1)}, u32[]{:S(2)}, u32[]{:S(2)}) collective-permute-start(bf16[128,768]{1,0:T(8,128)(2,1)S(1)} %add_piece.9), channel_id=1, source_target_pairs={{0,4},{1,5},{2,6},{3,7},{4,8},{5,9},{6,10},{7,11},{8,12},{9,13},{1... | collective-permute-start | bytes 589832 | tf_op jit(solution)/shard_map/ppermute | solution.py:271
  223.9 8.0 %collective-permute-start.40 = (bf16[128,512]{1,0:T(8,128)(2,1)S(1)}, bf16[128,512]{1,0:T(8,128)(2,1)S(1)}, u32[]{:S(2)}, u32[]{:S(2)}) collective-permute-start(bf16[128,512]{1,0:T(8,128)(2,1)S(1)} %get-tuple-element.167), channel_id=1, source_target_pairs={{0,4},{1,5},{2,6},{3,7},{4,8},{5,9},{6,10},{7,11},{8,12},{9,13},{1... | collective-permute-start | bytes 393224 | tf_op jit(solution)/shard_map/ppermute | solution.py:271
  223.9 10.6 %collective-permute-start.41 = (bf16[128,512]{1,0:T(8,128)(2,1)S(1)}, bf16[128,512]{1,0:T(8,128)(2,1)S(1)}, u32[]{:S(2)}, u32[]{:S(2)}) collective-permute-start(bf16[128,512]{1,0:T(8,128)(2,1)S(1)} %get-tuple-element.168), channel_id=1, source_target_pairs={{0,8},{1,9},{2,10},{3,11},{4,12},{5,13},{6,14},{7,15},{8,0},{9,1},... | collective-permute-start | bytes 393224 | tf_op jit(solution)/shard_map/ppermute | solution.py:271
  227.4 7.1 %collective-permute-start.42 = (bf16[128,512]{1,0:T(8,128)(2,1)S(1)}, bf16[128,512]{1,0:T(8,128)(2,1)S(1)}, u32[]{:S(2)}, u32[]{:S(2)}) collective-permute-start(bf16[128,512]{1,0:T(8,128)(2,1)S(1)} %get-tuple-element.169), channel_id=1, source_target_pairs={{0,12},{1,13},{2,14},{3,15},{4,0},{5,1},{6,2},{7,3},{8,4},{9,5},{1... | collective-permute-start | bytes 393224 | tf_op jit(solution)/shard_map/ppermute | solution.py:271

commit v12 on v11

--- a/solution.py
+++ b/solution.py
@@ -66,11 +66,11 @@
     blocks = len(row_blocks)
     block, row_width = row_blocks[0].shape
     experts, width, hidden = gate_weight.shape
-    count, columns, tile = blocks * block, experts * hidden, 2 * block
+    count, columns, tile = blocks * block, experts * hidden, blocks // 2 * block
     weights = resident((experts, width, hidden), lambda i: (0, 0, 0))
     return pl.pallas_call(
         functools.partial(hidden_kernel, blocks, all_experts),
-        grid=(blocks // 2,),
+        grid=(2,),
         in_specs=[pl.BlockSpec(memory_space=pltpu.SMEM), weights, weights]
         + [pl.BlockSpec(memory_space=pl.ANY)] * blocks,
         out_specs=[
@@ -117,7 +117,7 @@
     blocks = len(grad_blocks)
     block, width = grad_blocks[0].shape
     columns = downs[0].shape[0]
-    tile = 2 * block
+    tile = blocks // 2 * block
 
     def rows(count):
         return pl.BlockSpec((tile, count), lambda i: (i, 0))
@@ -126,7 +126,7 @@
     out_columns, out_type = (columns, jnp.float32) if by is None else (2 * columns, jnp.bfloat16)
     return pl.pallas_call(
         functools.partial(grads_kernel, blocks, tuple(cuts), by is not None, before is not None),
-        grid=(blocks // 2,),
+        grid=(2,),
         in_specs=[rows(x.shape[1]) for x in given]
         + [resident(d.shape, lambda i: (0, 0)) for d in downs]
         + [pl.BlockSpec(memory_space=pl.ANY)] * blocks,
@@ -322,8 +322,7 @@
     (down_1,) = send_all([(downs[1], twin)], down_0, activ, other_activ)
 
     def mix(c, other_down, *waits):
-        lo, hi = chunks[c]
-        return mix_columns(activ, other_activ, down, after(other_down, *waits), lo // (hi - lo))
+        return mix_columns(activ, other_activ, downs[c], after(other_down, *waits), 0)
 
     types = [jnp.float32, jnp.float32] + [jnp.bfloat16] * (layers - 2)
 
@@ -345,7 +344,7 @@
     own_grads = hidden_grads(grad_blocks, [down], [(0, width)], by=by)
 
     keep_1, send = mix(1, down_1, send, own_grads)
-    own_0, *pieces = add_sides(keep_0, come_0, types)
+    own_0, *pieces = add_sides(after(keep_0, send), come_0, types)
     (come_1,) = send_all([(send, side)])
     far_0, next_0 = send_on(pieces)
     near_0 = send_last(pieces, next_0, far_0)
@@ -382,7 +381,7 @@
     near_3 = send_last(pieces, next_3, far_3, near_2)
     mixed = finish(chunks, [(own_0, far_0, near_0), (own_1, far_1, near_1), (own_2, far_2, near_2)], width)
 
-    own_4, *pieces = add_sides(after(keep_4, mixed), after(come_4, next_3), types)
+    own_4, *pieces = add_sides(after(keep_4, mixed), after(come_4, near_3), types)
     far_4, next_4 = send_on(pieces)
     near_4 = send_last(pieces, next_4, far_4)
 

time: 236 us -> 246 us (1.042)
  starting transfers between devices: 52.3 us -> 58.2 us
  local copies, waits for them, and re-layouts: 6.68 us -> 9.27 us
    ppermute x43, starting transfers between devices: 52.3 us -> 58.2 us  [send_all(): lax.ppermute(v, 'expert', pairs)]
  transfers between devices with their start and end apart: 43 -> 43, of which waited for: 24 -> 25; matrix products, arithmetic and copies ran while one was open for 1% -> 1% of each run, Pallas kernels for 23% -> 23%
where the time goes in v12:
time: 246 us; the launch traced here: 245 us
  waiting for transfers between devices  118 us (48%)
  starting transfers between devices  58.2 us (24%)
  Pallas kernels  58 us (24%)
  local copies, waits for them, and re-layouts  9.27 us (4%)
    ppermute x43, waiting for transfers between devices, send_all(): lax.ppermute(v, 'expert', pairs)  118 us
    ppermute x43, starting transfers between devices, send_all(): lax.ppermute(v, 'expert', pairs)  58.2 us
    pallas_call x6, Pallas kernels, sum_columns(): pl.pallas_call(kernel, grid=(2,), in_specs=[rows, rows] + weight_specs, o...  22.4 us
    pallas_call x2, Pallas kernels, hidden_forward(): pl.pallas_call(functools.partial(hidden_kernel, blocks, all_experts), gri...  20.8 us
    pallas_call x3, Pallas kernels, hidden_grads(): pl.pallas_call(functools.partial(grads_kernel, blocks, tuple(cuts), by is...  11.6 us
  transfers between devices with their start and end apart: 43, of which 25 were waited for; matrix products, arithmetic and copies ran while one was open for 1% of the time, Pallas kernels for 23%

profile of v12, /device:TPU:0, one launch (start us, length us, event | category | flops | bytes accessed | tf_op | source)
XLA Modules:
  0.0 245.4 jit_solution(1572472474027445601)
XLA Ops:
  1.7 1.9 concatenate.3.refs_0_
  3.6 2.9 %collective-permute-start.8 = (bf16[2,2048,256]{2,1,0:T(8,128)(2,1)}, bf16[2,2048,256]{2,1,0:T(8,128)(2,1)S(1)}, u32[]{:S(2)}, u32[]{:S(2)}) collective-permute-start(bf16[2,2048,256]{2,1,0:T(8,128)(2,1)} %refs_0_.5), channel_id=1, source_target_pairs={{0,1},{1,0},{2,3},{3,2},{4,5},{5,4},{6,7},{7,6},{8,9},{9,8},{10,11... | collective-permute-start | bytes 6291464 | tf_op jit(solution)/shard_map/ppermute | solution.py:271
  6.5 1.6 collective-permute-start.3
  8.1 1.5 collective-permute-start.6
  9.6 2.2 collective-permute-start
  12.4 10.8 %collective-permute-done.6.refs_6_.refs_7_ = bf16[128,2048]{1,0:T(8,128)(2,1)S(1)} collective-permute-done((bf16[128,2048]{1,0:T(8,128)(2,1)}, bf16[128,2048]{1,0:T(8,128)(2,1)S(1)}, u32[]{:S(2)}, u32[]{:S(2)}) %collective-permute-start.6) | collective-permute-done | bytes 524320 | tf_op jit(solution)/shard_map/ppermute | solution.py:271
  24.4 10.2 %collective-permute-done.refs_1_ = bf16[128,2176]{1,0:T(8,128)(2,1)S(1)} collective-permute-done((bf16[128,2176]{1,0:T(8,128)(2,1)}, bf16[128,2176]{1,0:T(8,128)(2,1)S(1)}, u32[]{:S(2)}, u32[]{:S(2)}) %collective-permute-start) | collective-permute-done | bytes 557088 | tf_op jit(solution)/shard_map/ppermute | solution.py:271
  34.6 1.2 collective-permute-start.4
  35.8 2.6 %collective-permute-start.2 = (bf16[128,2176]{1,0:T(8,128)(2,1)S(1)}, bf16[128,2176]{1,0:T(8,128)(2,1)S(1)}, u32[]{:S(2)}, u32[]{:S(2)}) collective-permute-start(bf16[128,2176]{1,0:T(8,128)(2,1)S(1)} %collective-permute-done.refs_1_), channel_id=1, source_target_pairs={{0,12},{1,13},{2,14},{3,15},{4,0},{5,1},{6,2},{7,3},{8,4},{9,5},{1... | collective-permute-start | bytes 1671176 | tf_op jit(solution)/shard_map/ppermute | solution.py:271
  39.0 11.2 %collective-permute-done.4.refs_5_ = bf16[128,2176]{1,0:T(8,128)(2,1)S(1)} collective-permute-done((bf16[128,2176]{1,0:T(8,128)(2,1)S(1)}, bf16[128,2176]{1,0:T(8,128)(2,1)S(1)}, u32[]{:S(2)}, u32[]{:S(2)}) %collective-permute-start.4) | collective-permute-done | bytes 557088 | tf_op jit(solution)/shard_map/ppermute | solution.py:271
  50.2 1.3 collective-permute-start.5
  51.5 2.6 %collective-permute-start.11 = (bf16[128,2048]{1,0:T(8,128)(2,1)}, bf16[128,2048]{1,0:T(8,128)(2,1)}, u32[]{:S(2)}, u32[]{:S(2)}) collective-permute-start(bf16[128,2048]{1,0:T(8,128)(2,1)} %refs_3_), channel_id=1, source_target_pairs={{0,12},{1,13},{2,14},{3,15},{4,0},{5,1},{6,2},{7,3},{8,4},{9,5},{1... | collective-permute-start | bytes 1572872 | tf_op jit(solution)/shard_map/ppermute | solution.py:271
  54.1 8.0 %collective-permute-done.7.refs_7_ = bf16[128,2176]{1,0:T(8,128)(2,1)S(1)} collective-permute-done((bf16[128,2176]{1,0:T(8,128)(2,1)S(1)}, bf16[128,2176]{1,0:T(8,128)(2,1)S(1)}, u32[]{:S(2)}, u32[]{:S(2)}) %collective-permute-start.7) | collective-permute-done | bytes 557088 | tf_op jit(solution)/shard_map/ppermute | solution.py:271
  62.1 1.5 collective-permute-done.11.refs_3_.refs_4_
  63.6 9.5 %collective-permute-done.5.refs_6_ = bf16[128,2176]{1,0:T(8,128)(2,1)S(1)} collective-permute-done((bf16[128,2176]{1,0:T(8,128)(2,1)S(1)}, bf16[128,2176]{1,0:T(8,128)(2,1)S(1)}, u32[]{:S(2)}, u32[]{:S(2)}) %collective-permute-start.5) | collective-permute-done | bytes 557088 | tf_op jit(solution)/shard_map/ppermute | solution.py:271
  73.3 1.5 collective-permute-start.12
  74.8 1.9 slice.12.own_down_ref
  76.7 1.1 collective-permute-start.13
  78.3 10.4 %hidden_forward.2 = (bf16[1024,512]{1,0:T(8,128)(2,1)}, f32[1024,1024]{1,0:T(8,128)}) custom-call(s32[1]{0:T(128)} %bitcast.owner_ref, bf16[2,2048,256]{2,1,0:T(8,128)(2,1)} %refs_0_.5, bf16[2,2048,256]{2,1,0:T(8,128)(2,1)} %refs_1_.5, bf16[128,2176]{1,0:T(8,128)(2,1)} %concatenate.3.refs_0_, bf16[128,2176]{1,0:T(8,128)(2,1)} %copy-done.14, ...), custom_call_target="tpu_custom_call" | custom-call | flops 1 | bytes 1 | tf_op jit(solution)/shard_map/hidden_forward/pallas_call | solution.py:71
  88.7 8.9 %collective-permute-done.15.refs_4_.refs_5_ = bf16[128,2048]{1,0:T(8,128)(2,1)} collective-permute-done((bf16[128,2048]{1,0:T(8,128)(2,1)}, bf16[128,2048]{1,0:T(8,128)(2,1)}, u32[]{:S(2)}, u32[]{:S(2)}) %collective-permute-start.15) | collective-permute-done | bytes 524320 | tf_op jit(solution)/shard_map/ppermute | solution.py:271
  98.1 1.6 collective-permute-start.14
  99.7 1.3 fusion.1
  101.0 10.5 %hidden_forward.3 = (bf16[1024,512]{1,0:T(8,128)(2,1)}, f32[1024,1024]{1,0:T(8,128)}) custom-call(s32[1]{0:T(128)} %bitcast.1.owner_ref, bf16[2,2048,256]{2,1,0:T(8,128)(2,1)} %copy-done.2, bf16[2,2048,256]{2,1,0:T(8,128)(2,1)} %collective-permute-done.9.up_ref.refs_3_, bf16[128,2176]{1,0:T(8,128)(2,1)} %concatenate.3.refs_0_, bf16[128,2176]{1,0:T(8,128)(2,1)} %copy-done.14, ...), custom_call_target="tpu_custom_call" | custom-call | flops 1 | bytes 1 | tf_op jit(solution)/shard_map/hidden_forward/pallas_call | solution.py:71
  112.7 8.5 %collective-permute-done.14.refs_9_.refs_10_ = bf16[128,2048]{1,0:T(8,128)(2,1)S(1)} collective-permute-done((bf16[128,2048]{1,0:T(8,128)(2,1)}, bf16[128,2048]{1,0:T(8,128)(2,1)S(1)}, u32[]{:S(2)}, u32[]{:S(2)}) %collective-permute-start.14) | collective-permute-done | bytes 524320 | tf_op jit(solution)/shard_map/ppermute | solution.py:271
  121.2 1.2 copy-done.5
  122.5 2.8 %mix_columns.3 = (f32[512,512]{1,0:T(8,128)S(1)}, bf16[512,512]{1,0:T(8,128)(2,1)S(1)}) custom-call(bf16[1024,512]{1,0:T(8,128)(2,1)S(1)} %copy-done.4, bf16[1024,512]{1,0:T(8,128)(2,1)S(1)} %copy-done.5, bf16[512,512]{1,0:T(8,128)(2,1)} %slice.12.own_down_ref, bf16[512,512]{1,0:T(8,128)(2,1)} %collective-permute-done.10.other_down_ref.refs_0_), custom_call_target="tpu_custom_call" | custom-call | flops 1 | bytes 1 | tf_op jit(solution)/shard_map/mix_columns/pallas_call | solution.py:179
  126.1 2.2 copy-done.11
  128.3 4.1 %hidden_grads.3.own_ref = bf16[1024,1024]{1,0:T(8,128)(2,1)S(1)} custom-call(f32[1024,1024]{1,0:T(8,128)S(1)} %copy-done.11, bf16[512,2048]{1,0:T(8,128)(2,1)S(1)} %bitcast.5, bf16[128,2048]{1,0:T(8,128)(2,1)S(1)} %copy-done.9, bf16[128,2048]{1,0:T(8,128)(2,1)} %collective-permute-done.11.refs_3_.refs_4_, ...), custom_call_target="tpu_custom_call" | custom-call | flops 1 | bytes 1 | tf_op jit(solution)/shard_map/hidden_grads/pallas_call | solution.py:127
  132.5 3.3 %mix_columns.4 = (f32[512,768]{1,0:T(8,128)S(1)}, bf16[512,768]{1,0:T(8,128)(2,1)S(1)}) custom-call(bf16[1024,512]{1,0:T(8,128)(2,1)S(1)} %copy-done.4, bf16[1024,512]{1,0:T(8,128)(2,1)S(1)} %copy-done.6, bf16[512,768]{1,0:T(8,128)(2,1)} %get-tuple-element.107.own_down_ref, bf16[512,768]{1,0:T(8,128)(2,1)S(1)} %collective-permute-done.17.other_down_ref.refs_1_), custom_call_target="tpu_custom_call" | custom-call | flops 1 | bytes 1 | tf_op jit(solution)/shard_map/mix_columns/pallas_call | solution.py:179
  135.8 1.8 collective-permute-start.23
  138.5 3.1 %collective-permute-start.19 = (bf16[128,512]{1,0:T(8,128)(2,1)S(1)}, bf16[128,512]{1,0:T(8,128)(2,1)S(1)}, u32[]{:S(2)}, u32[]{:S(2)}) collective-permute-start(bf16[128,512]{1,0:T(8,128)(2,1)S(1)} %get-tuple-element.115), channel_id=1, source_target_pairs={{0,12},{1,13},{2,14},{3,15},{4,0},{5,1},{6,2},{7,3},{8,4},{9,5},{1... | collective-permute-start | bytes 393224 | tf_op jit(solution)/shard_map/ppermute | solution.py:271
  141.6 3.0 %collective-permute-done.20.come_ref = bf16[128,512]{1,0:T(8,128)(2,1)S(1)} collective-permute-done((bf16[128,512]{1,0:T(8,128)(2,1)S(1)}, bf16[128,512]{1,0:T(8,128)(2,1)S(1)}, u32[]{:S(2)}, u32[]{:S(2)}) %collective-permute-start.20) | collective-permute-done | bytes 131104 | tf_op jit(solution)/shard_map/ppermute | solution.py:271
  144.9 4.6 %hidden_grads.4.refs_1_ = f32[1024,512]{1,0:T(8,128)S(1)} custom-call(bf16[512,512]{1,0:T(8,128)(2,1)} %collective-permute-done.10.other_down_ref.refs_0_, bf16[512,768]{1,0:T(8,128)(2,1)S(1)} %collective-permute-done.17.other_down_ref.refs_1_, bf16[128,2048]{1,0:T(8,128)(2,1)S(1)} %copy-done.9, bf16[128,2048]{1,0:T(8,128)(2,1)} %collective-permute-done.11.refs_3_.refs_4_, ...), custom_call_target="tpu_custom_call" | custom-call | flops 1 | bytes 1 | tf_op jit(solution)/shard_map/hidden_grads/pallas_call | solution.py:127
  149.6 2.1 collective-permute-done.21.refs_2_
  151.7 2.2 mix_columns.5
  153.9 1.4 collective-permute-start.27
  155.3 2.9 %hidden_grads.5.other_ref = bf16[1024,1024]{1,0:T(8,128)(2,1)S(1)} custom-call(f32[1024,1024]{1,0:T(8,128)S(1)} %copy-done.10, f32[1024,512]{1,0:T(8,128)S(1)} %hidden_grads.4.refs_1_, bf16[512,768]{1,0:T(8,128)(2,1)S(1)} %collective-permute-done.22.other_down_ref.refs_2_, bf16[128,2048]{1,0:T(8,128)(2,1)S(1)} %copy-done.9, ...), custom_call_target="tpu_custom_call" | custom-call | flops 1 | bytes 1 | tf_op jit(solution)/shard_map/hidden_grads/pallas_call | solution.py:127
  158.8 5.2 %back_columns.3 = (f32[512,768]{1,0:T(8,128)S(1)}, bf16[512,768]{1,0:T(8,128)(2,1)S(1)}) custom-call(bf16[1024,1024]{1,0:T(8,128)(2,1)S(1)} %hidden_grads.3.own_ref, bf16[1024,1024]{1,0:T(8,128)(2,1)S(1)} %hidden_grads.5.other_ref, bf16[2,2048,256]{2,1,0:T(8,128)(2,1)S(1)} %copy-done, bf16[2,2048,256]{2,1,0:T(8,128)(2,1)S(1)} %copy-done.1, ...), custom_call_target="tpu_custom_call" | custom-call | flops 1 | bytes 1 | tf_op jit(solution)/shard_map/back_columns/pallas_call | solution.py:179
  164.8 1.8 collective-permute-start.24
  166.9 3.6 %collective-permute-done.24.refs_4_ = bf16[128,768]{1,0:T(8,128)(2,1)S(1)} collective-permute-done((bf16[128,768]{1,0:T(8,128)(2,1)S(1)}, bf16[128,768]{1,0:T(8,128)(2,1)S(1)}, u32[]{:S(2)}, u32[]{:S(2)}) %collective-permute-start.24) | collective-permute-done | bytes 196640 | tf_op jit(solution)/shard_map/ppermute | solution.py:271
  170.5 3.6 %collective-permute-done.25.come_ref = bf16[128,768]{1,0:T(8,128)(2,1)S(1)} collective-permute-done((bf16[128,768]{1,0:T(8,128)(2,1)S(1)}, bf16[128,768]{1,0:T(8,128)(2,1)S(1)}, u32[]{:S(2)}, u32[]{:S(2)}) %collective-permute-start.25) | collective-permute-done | bytes 196640 | tf_op jit(solution)/shard_map/ppermute | solution.py:271
  174.1 5.2 %back_columns.4 = (f32[512,768]{1,0:T(8,128)S(1)}, bf16[512,768]{1,0:T(8,128)(2,1)S(1)}) custom-call(bf16[1024,1024]{1,0:T(8,128)(2,1)S(1)} %hidden_grads.3.own_ref, bf16[1024,1024]{1,0:T(8,128)(2,1)S(1)} %hidden_grads.5.other_ref, bf16[2,2048,256]{2,1,0:T(8,128)(2,1)S(1)} %copy-done, bf16[2,2048,256]{2,1,0:T(8,128)(2,1)S(1)} %copy-done.1, ...), custom_call_target="tpu_custom_call" | custom-call | flops 1 | bytes 1 | tf_op jit(solution)/shard_map/back_columns/pallas_call | solution.py:179
  179.4 1.4 collective-permute-start.35
  181.7 3.3 %collective-permute-start.28 = (bf16[128,768]{1,0:T(8,128)(2,1)S(1)}, bf16[128,768]{1,0:T(8,128)(2,1)S(1)}, u32[]{:S(2)}, u32[]{:S(2)}) collective-permute-start(bf16[128,768]{1,0:T(8,128)(2,1)S(1)} %get-tuple-element.139), channel_id=1, source_target_pairs={{0,12},{1,13},{2,14},{3,15},{4,0},{5,1},{6,2},{7,3},{8,4},{9,5},{1... | collective-permute-start | bytes 589832 | tf_op jit(solution)/shard_map/ppermute | solution.py:271
  185.1 3.3 %collective-permute-done.29.come_ref = bf16[128,768]{1,0:T(8,128)(2,1)S(1)} collective-permute-done((bf16[128,768]{1,0:T(8,128)(2,1)S(1)}, bf16[128,768]{1,0:T(8,128)(2,1)S(1)}, u32[]{:S(2)}, u32[]{:S(2)}) %collective-permute-start.29) | collective-permute-done | bytes 196640 | tf_op jit(solution)/shard_map/ppermute | solution.py:271
  188.5 3.9 %back_columns.5 = (f32[512,512]{1,0:T(8,128)S(1)}, bf16[512,512]{1,0:T(8,128)(2,1)S(1)}) custom-call(bf16[1024,1024]{1,0:T(8,128)(2,1)S(1)} %hidden_grads.3.own_ref, bf16[1024,1024]{1,0:T(8,128)(2,1)S(1)} %hidden_grads.5.other_ref, bf16[2,2048,256]{2,1,0:T(8,128)(2,1)S(1)} %copy-done, bf16[2,2048,256]{2,1,0:T(8,128)(2,1)S(1)} %copy-done.1, ...), custom_call_target="tpu_custom_call" | custom-call | flops 1 | bytes 1 | tf_op jit(solution)/shard_map/back_columns/pallas_call | solution.py:179
  192.4 4.5 %collective-permute-done.28.refs_7_ = bf16[128,768]{1,0:T(8,128)(2,1)S(1)} collective-permute-done((bf16[128,768]{1,0:T(8,128)(2,1)S(1)}, bf16[128,768]{1,0:T(8,128)(2,1)S(1)}, u32[]{:S(2)}, u32[]{:S(2)}) %collective-permute-start.28) | collective-permute-done | bytes 196640 | tf_op jit(solution)/shard_map/ppermute | solution.py:271
  197.0 2.4 collective-permute-start.33
  199.5 3.8 %collective-permute-start.32 = (bf16[128,768]{1,0:T(8,128)(2,1)S(1)}, bf16[128,768]{1,0:T(8,128)(2,1)S(1)}, u32[]{:S(2)}, u32[]{:S(2)}) collective-permute-start(bf16[128,768]{1,0:T(8,128)(2,1)S(1)} %get-tuple-element.149), channel_id=1, source_target_pairs={{0,12},{1,13},{2,14},{3,15},{4,0},{5,1},{6,2},{7,3},{8,4},{9,5},{1... | collective-permute-start | bytes 589832 | tf_op jit(solution)/shard_map/ppermute | solution.py:271
  204.0 2.8 %collective-permute-done.33.come_ref = bf16[128,768]{1,0:T(8,128)(2,1)S(1)} collective-permute-done((bf16[128,768]{1,0:T(8,128)(2,1)S(1)}, bf16[128,768]{1,0:T(8,128)(2,1)S(1)}, u32[]{:S(2)}, u32[]{:S(2)}) %collective-permute-start.33) | collective-permute-done | bytes 196640 | tf_op jit(solution)/shard_map/ppermute | solution.py:271
  206.8 2.1 collective-permute-done.30.refs_8_
  208.9 5.2 %collective-permute-done.32.refs_1_ = bf16[128,768]{1,0:T(8,128)(2,1)S(1)} collective-permute-done((bf16[128,768]{1,0:T(8,128)(2,1)S(1)}, bf16[128,768]{1,0:T(8,128)(2,1)S(1)}, u32[]{:S(2)}, u32[]{:S(2)}) %collective-permute-start.32) | collective-permute-done | bytes 196640 | tf_op jit(solution)/shard_map/ppermute | solution.py:271
  214.1 1.4 collective-permute-start.34
  215.5 1.1 finish.2
  216.6 7.1 %collective-permute-done.34.refs_2_ = bf16[128,768]{1,0:T(8,128)(2,1)S(1)} collective-permute-done((bf16[128,768]{1,0:T(8,128)(2,1)S(1)}, bf16[128,768]{1,0:T(8,128)(2,1)S(1)}, u32[]{:S(2)}, u32[]{:S(2)}) %collective-permute-start.34) | collective-permute-done | bytes 196640 | tf_op jit(solution)/shard_map/ppermute | solution.py:271
  223.9 3.8 %collective-permute-start.36 = (bf16[128,768]{1,0:T(8,128)(2,1)S(1)}, bf16[128,768]{1,0:T(8,128)(2,1)S(1)}, u32[]{:S(2)}, u32[]{:S(2)}) collective-permute-start(bf16[128,768]{1,0:T(8,128)(2,1)S(1)} %get-tuple-element.158), channel_id=1, source_target_pairs={{0,12},{1,13},{2,14},{3,15},{4,0},{5,1},{6,2},{7,3},{8,4},{9,5},{1... | collective-permute-start | bytes 589832 | tf_op jit(solution)/shard_map/ppermute | solution.py:271
  227.7 3.8 %collective-permute-done.37.come_ref = bf16[128,768]{1,0:T(8,128)(2,1)S(1)} collective-permute-done((bf16[128,768]{1,0:T(8,128)(2,1)S(1)}, bf16[128,768]{1,0:T(8,128)(2,1)S(1)}, u32[]{:S(2)}, u32[]{:S(2)}) %collective-permute-start.37) | collective-permute-done | bytes 196640 | tf_op jit(solution)/shard_map/ppermute | solution.py:271
  231.6 1.0 collective-permute-done.36.refs_4_
  233.6 1.2 collective-permute-start.40
  234.8 2.3 collective-permute-start.41
  237.1 1.7 collective-permute-start.42
  238.8 2.8 %collective-permute-done.40.refs_7_ = bf16[128,512]{1,0:T(8,128)(2,1)S(1)} collective-permute-done((bf16[128,512]{1,0:T(8,128)(2,1)S(1)}, bf16[128,512]{1,0:T(8,128)(2,1)S(1)}, u32[]{:S(2)}, u32[]{:S(2)}) %collective-permute-start.40) | collective-permute-done | bytes 131104 | tf_op jit(solution)/shard_map/ppermute | solution.py:271
  241.7 2.6 %collective-permute-done.41.refs_8_ = bf16[128,512]{1,0:T(8,128)(2,1)S(1)} collective-permute-done((bf16[128,512]{1,0:T(8,128)(2,1)S(1)}, bf16[128,512]{1,0:T(8,128)(2,1)S(1)}, u32[]{:S(2)}, u32[]{:S(2)}) %collective-permute-start.41) | collective-permute-done | bytes 131104 | tf_op jit(solution)/shard_map/ppermute | solution.py:271
  244.3 1.1 finish.3
  (95 shorter events, 12.8 us)
Async XLA Ops:
  0.6 76.1 %copy-start.9 = (bf16[128,2048]{1,0:T(8,128)(2,1)S(1)}, bf16[128,2048]{1,0:T(8,128)(2,1)}, u32[]{:S(2)}) copy-start(bf16[128,2048]{1,0:T(8,128)(2,1)} %refs_3_) | copy-start | bytes 1572868
  3.6 73.1 %collective-permute-start.8 = (bf16[2,2048,256]{2,1,0:T(8,128)(2,1)}, bf16[2,2048,256]{2,1,0:T(8,128)(2,1)S(1)}, u32[]{:S(2)}, u32[]{:S(2)}) collective-permute-start(bf16[2,2048,256]{2,1,0:T(8,128)(2,1)} %refs_0_.5), channel_id=1, source_target_pairs={{0,1},{1,0},{2,3},{3,2},{4,5},{5,4},{6,7},{7,6},{8,9},{9,8},{10,11... | collective-permute-start | bytes 6291464 | tf_op jit(solution)/shard_map/ppermute | solution.py:271
  6.5 17.6 %collective-permute-start.3 = (bf16[128,2176]{1,0:T(8,128)(2,1)}, bf16[128,2176]{1,0:T(8,128)(2,1)S(1)}, u32[]{:S(2)}, u32[]{:S(2)}) collective-permute-start(bf16[128,2176]{1,0:T(8,128)(2,1)} %concatenate.3.refs_0_), channel_id=1, source_target_pairs={{0,4},{1,5},{2,6},{3,7},{4,8},{5,9},{6,10},{7,11},{8,12},{9,13},{1... | collective-permute-start | bytes 1671176 | tf_op jit(solution)/shard_map/ppermute | solution.py:271
  8.1 15.1 %collective-permute-start.6 = (bf16[128,2048]{1,0:T(8,128)(2,1)}, bf16[128,2048]{1,0:T(8,128)(2,1)S(1)}, u32[]{:S(2)}, u32[]{:S(2)}) collective-permute-start(bf16[128,2048]{1,0:T(8,128)(2,1)} %refs_3_), channel_id=1, source_target_pairs={{0,2},{1,3},{2,0},{3,1},{4,6},{5,7},{6,4},{7,5},{8,10},{9,11},{10,... | collective-permute-start | bytes 1572872 | tf_op jit(solution)/shard_map/ppermute | solution.py:271
  9.6 25.0 %collective-permute-start = (bf16[128,2176]{1,0:T(8,128)(2,1)}, bf16[128,2176]{1,0:T(8,128)(2,1)S(1)}, u32[]{:S(2)}, u32[]{:S(2)}) collective-permute-start(bf16[128,2176]{1,0:T(8,128)(2,1)} %concatenate.3.refs_0_), channel_id=1, source_target_pairs={{0,12},{1,13},{2,14},{3,15},{4,0},{5,1},{6,2},{7,3},{8,4},{9,5},{1... | collective-permute-start | bytes 1671176 | tf_op jit(solution)/shard_map/ppermute | solution.py:271
  11.8 22.8 %collective-permute-start.1 = (bf16[128,2176]{1,0:T(8,128)(2,1)}, bf16[128,2176]{1,0:T(8,128)(2,1)S(1)}, u32[]{:S(2)}, u32[]{:S(2)}) collective-permute-start(bf16[128,2176]{1,0:T(8,128)(2,1)} %concatenate.3.refs_0_), channel_id=1, source_target_pairs={{0,2},{1,3},{2,0},{3,1},{4,6},{5,7},{6,4},{7,5},{8,10},{9,11},{10,... | collective-permute-start | bytes 1671176 | tf_op jit(solution)/shard_map/ppermute | solution.py:271
  24.1 14.4 %copy-start.13 = (bf16[128,2176]{1,0:T(8,128)(2,1)}, bf16[128,2176]{1,0:T(8,128)(2,1)S(1)}, u32[]{:S(2)}) copy-start(bf16[128,2176]{1,0:T(8,128)(2,1)S(1)} %collective-permute-done.3.refs_3_) | copy-start | bytes 1671172
  24.1 76.9 %collective-permute-start.9 = (bf16[2,2048,256]{2,1,0:T(8,128)(2,1)}, bf16[2,2048,256]{2,1,0:T(8,128)(2,1)}, u32[]{:S(2)}, u32[]{:S(2)}) collective-permute-start(bf16[2,2048,256]{2,1,0:T(8,128)(2,1)} %refs_1_.5), channel_id=1, source_target_pairs={{0,1},{1,0},{2,3},{3,2},{4,5},{5,4},{6,7},{7,6},{8,9},{9,8},{10,11... | collective-permute-start | bytes 6291464 | tf_op jit(solution)/shard_map/ppermute | solution.py:271
  34.6 27.5 %copy-start.14 = (bf16[128,2176]{1,0:T(8,128)(2,1)}, bf16[128,2176]{1,0:T(8,128)(2,1)S(1)}, u32[]{:S(2)}) copy-start(bf16[128,2176]{1,0:T(8,128)(2,1)S(1)} %collective-permute-done.refs_1_) | copy-start | bytes 1671172
  34.6 29.0 %copy-start.15 = (bf16[128,2176]{1,0:T(8,128)(2,1)}, bf16[128,2176]{1,0:T(8,128)(2,1)S(1)}, u32[]{:S(2)}) copy-start(bf16[128,2176]{1,0:T(8,128)(2,1)S(1)} %collective-permute-done.1.refs_4_) | copy-start | bytes 1671172
  34.6 15.6 %collective-permute-start.4 = (bf16[128,2176]{1,0:T(8,128)(2,1)S(1)}, bf16[128,2176]{1,0:T(8,128)(2,1)S(1)}, u32[]{:S(2)}, u32[]{:S(2)}) collective-permute-start(bf16[128,2176]{1,0:T(8,128)(2,1)S(1)} %collective-permute-done.refs_1_), channel_id=1, source_target_pairs={{0,2},{1,3},{2,0},{3,1},{4,6},{5,7},{6,4},{7,5},{8,10},{9,11},{10,... | collective-permute-start | bytes 1671176 | tf_op jit(solution)/shard_map/ppermute | solution.py:271
  35.8 14.3 %collective-permute-start.2 = (bf16[128,2176]{1,0:T(8,128)(2,1)S(1)}, bf16[128,2176]{1,0:T(8,128)(2,1)S(1)}, u32[]{:S(2)}, u32[]{:S(2)}) collective-permute-start(bf16[128,2176]{1,0:T(8,128)(2,1)S(1)} %collective-permute-done.refs_1_), channel_id=1, source_target_pairs={{0,12},{1,13},{2,14},{3,15},{4,0},{5,1},{6,2},{7,3},{8,4},{9,5},{1... | collective-permute-start | bytes 1671176 | tf_op jit(solution)/shard_map/ppermute | solution.py:271
  38.5 23.6 %collective-permute-start.7 = (bf16[128,2176]{1,0:T(8,128)(2,1)S(1)}, bf16[128,2176]{1,0:T(8,128)(2,1)S(1)}, u32[]{:S(2)}, u32[]{:S(2)}) collective-permute-start(bf16[128,2176]{1,0:T(8,128)(2,1)S(1)} %collective-permute-done.3.refs_3_), channel_id=1, source_target_pairs={{0,2},{1,3},{2,0},{3,1},{4,6},{5,7},{6,4},{7,5},{8,10},{9,11},{10,... | collective-permute-start | bytes 1671176 | tf_op jit(solution)/shard_map/ppermute | solution.py:271
  50.2 22.9 %copy-start.16 = (bf16[128,2176]{1,0:T(8,128)(2,1)}, bf16[128,2176]{1,0:T(8,128)(2,1)S(1)}, u32[]{:S(2)}) copy-start(bf16[128,2176]{1,0:T(8,128)(2,1)S(1)} %collective-permute-done.4.refs_5_) | copy-start | bytes 1671172
  50.2 23.1 %copy-start.17 = (bf16[128,2176]{1,0:T(8,128)(2,1)}, bf16[128,2176]{1,0:T(8,128)(2,1)S(1)}, u32[]{:S(2)}) copy-start(bf16[128,2176]{1,0:T(8,128)(2,1)S(1)} %collective-permute-done.2.refs_2_) | copy-start | bytes 1671172
  50.2 22.9 %collective-permute-start.5 = (bf16[128,2176]{1,0:T(8,128)(2,1)S(1)}, bf16[128,2176]{1,0:T(8,128)(2,1)S(1)}, u32[]{:S(2)}, u32[]{:S(2)}) collective-permute-start(bf16[128,2176]{1,0:T(8,128)(2,1)S(1)} %collective-permute-done.2.refs_2_), channel_id=1, source_target_pairs={{0,2},{1,3},{2,0},{3,1},{4,6},{5,7},{6,4},{7,5},{8,10},{9,11},{10,... | collective-permute-start | bytes 1671176 | tf_op jit(solution)/shard_map/ppermute | solution.py:271
  51.5 12.1 %collective-permute-start.11 = (bf16[128,2048]{1,0:T(8,128)(2,1)}, bf16[128,2048]{1,0:T(8,128)(2,1)}, u32[]{:S(2)}, u32[]{:S(2)}) collective-permute-start(bf16[128,2048]{1,0:T(8,128)(2,1)} %refs_3_), channel_id=1, source_target_pairs={{0,12},{1,13},{2,14},{3,15},{4,0},{5,1},{6,2},{7,3},{8,4},{9,5},{1... | collective-permute-start | bytes 1572872 | tf_op jit(solution)/shard_map/ppermute | solution.py:271
  62.1 12.7 %copy-start.18 = (bf16[128,2176]{1,0:T(8,128)(2,1)}, bf16[128,2176]{1,0:T(8,128)(2,1)S(1)}, u32[]{:S(2)}) copy-start(bf16[128,2176]{1,0:T(8,128)(2,1)S(1)} %collective-permute-done.7.refs_7_) | copy-start | bytes 1671172
  73.0 1.8 copy-start.19
  73.0 24.6 %collective-permute-start.15 = (bf16[128,2048]{1,0:T(8,128)(2,1)}, bf16[128,2048]{1,0:T(8,128)(2,1)}, u32[]{:S(2)}, u32[]{:S(2)}) collective-permute-start(bf16[128,2048]{1,0:T(8,128)(2,1)} %collective-permute-done.11.refs_3_.refs_4_), channel_id=1, source_target_pairs={{0,12},{1,13},{2,14},{3,15},{4,0},{5,1},{6,2},{7,3},{8,4},{9,5},{1... | collective-permute-start | bytes 1572872 | tf_op jit(solution)/shard_map/ppermute | solution.py:271
  73.3 24.4 %collective-permute-start.12 = (bf16[128,2048]{1,0:T(8,128)(2,1)}, bf16[128,2048]{1,0:T(8,128)(2,1)}, u32[]{:S(2)}, u32[]{:S(2)}) collective-permute-start(bf16[128,2048]{1,0:T(8,128)(2,1)} %collective-permute-done.11.refs_3_.refs_4_), channel_id=1, source_target_pairs={{0,2},{1,3},{2,0},{3,1},{4,6},{5,7},{6,4},{7,5},{8,10},{9,11},{10,... | collective-permute-start | bytes 1572872 | tf_op jit(solution)/shard_map/ppermute | solution.py:271
  76.7 12.0 %copy-start.2 = (bf16[2,2048,256]{2,1,0:T(8,128)(2,1)}, bf16[2,2048,256]{2,1,0:T(8,128)(2,1)S(1)}, u32[]{:S(2)}) copy-start(bf16[2,2048,256]{2,1,0:T(8,128)(2,1)S(1)} %collective-permute-done.8.gate_ref.refs_2_) | copy-start | bytes 6291460
  76.7 21.4 %collective-permute-start.13 = (bf16[128,2048]{1,0:T(8,128)(2,1)S(1)}, bf16[128,2048]{1,0:T(8,128)(2,1)}, u32[]{:S(2)}, u32[]{:S(2)}) collective-permute-start(bf16[128,2048]{1,0:T(8,128)(2,1)S(1)} %copy-done.9), channel_id=1, source_target_pairs={{0,4},{1,5},{2,6},{3,7},{4,8},{5,9},{6,10},{7,11},{8,12},{9,13},{1... | collective-permute-start | bytes 1572872 | tf_op jit(solution)/shard_map/ppermute | solution.py:271
  77.8 33.6 %collective-permute-start.10 = (bf16[512,512]{1,0:T(8,128)(2,1)}, bf16[512,512]{1,0:T(8,128)(2,1)}, u32[]{:S(2)}, u32[]{:S(2)}) collective-permute-start(bf16[512,512]{1,0:T(8,128)(2,1)} %slice.12.own_down_ref), channel_id=1, source_target_pairs={{0,1},{1,0},{2,3},{3,2},{4,5},{5,4},{6,7},{7,6},{8,9},{9,8},{10,11... | collective-permute-start | bytes 1572872 | tf_op jit(solution)/shard_map/ppermute | solution.py:271
  78.3 21.3 %copy-start.7 = (bf16[2,256,2048]{2,1,0:T(8,128)(2,1)S(1)}, bf16[2,256,2048]{2,1,0:T(8,128)(2,1)}, u32[]{:S(2)}) copy-start(bf16[2,256,2048]{2,1,0:T(8,128)(2,1)} %param.13) | copy-start | bytes 6291460
  97.7 15.1 %collective-permute-start.16 = (bf16[128,2048]{1,0:T(8,128)(2,1)}, bf16[128,2048]{1,0:T(8,128)(2,1)S(1)}, u32[]{:S(2)}, u32[]{:S(2)}) collective-permute-start(bf16[128,2048]{1,0:T(8,128)(2,1)} %collective-permute-done.15.refs_4_.refs_5_), channel_id=1, source_target_pairs={{0,2},{1,3},{2,0},{3,1},{4,6},{5,7},{6,4},{7,5},{8,10},{9,11},{10,... | collective-permute-start | bytes 1572872 | tf_op jit(solution)/shard_map/ppermute | solution.py:271
  98.1 23.1 %collective-permute-start.14 = (bf16[128,2048]{1,0:T(8,128)(2,1)}, bf16[128,2048]{1,0:T(8,128)(2,1)S(1)}, u32[]{:S(2)}, u32[]{:S(2)}) collective-permute-start(bf16[128,2048]{1,0:T(8,128)(2,1)} %collective-permute-done.13.refs_5_.refs_6_), channel_id=1, source_target_pairs={{0,2},{1,3},{2,0},{3,1},{4,6},{5,7},{6,4},{7,5},{8,10},{9,11},{10,... | collective-permute-start | bytes 1572872 | tf_op jit(solution)/shard_map/ppermute | solution.py:271
  101.0 20.3 %copy-start.4 = (bf16[1024,512]{1,0:T(8,128)(2,1)S(1)}, bf16[1024,512]{1,0:T(8,128)(2,1)}, u32[]{:S(2)}) copy-start(bf16[1024,512]{1,0:T(8,128)(2,1)} %get-tuple-element.94.own_ref) | copy-start | bytes 3145732
  101.0 24.6 %copy-start.12 = (bf16[512,768]{1,0:T(8,128)(2,1)S(1)}, bf16[512,768]{1,0:T(8,128)(2,1)}, u32[]{:S(2)}) copy-start(bf16[512,768]{1,0:T(8,128)(2,1)} %get-tuple-element.121.own_down_ref) | copy-start | bytes 2359300
  101.0 25.1 %copy-start.8 = (bf16[2,256,2048]{2,1,0:T(8,128)(2,1)S(1)}, bf16[2,256,2048]{2,1,0:T(8,128)(2,1)}, u32[]{:S(2)}) copy-start(bf16[2,256,2048]{2,1,0:T(8,128)(2,1)} %param.13) | copy-start | bytes 6291460
  111.5 21.0 %collective-permute-start.17 = (bf16[512,768]{1,0:T(8,128)(2,1)}, bf16[512,768]{1,0:T(8,128)(2,1)S(1)}, u32[]{:S(2)}, u32[]{:S(2)}) collective-permute-start(bf16[512,768]{1,0:T(8,128)(2,1)} %get-tuple-element.107.own_down_ref), channel_id=1, source_target_pairs={{0,1},{1,0},{2,3},{3,2},{4,5},{5,4},{6,7},{7,6},{8,9},{9,8},{10,11... | collective-permute-start | bytes 2359304 | tf_op jit(solution)/shard_map/ppermute | solution.py:271
  121.2 1.2 copy-start.5
  125.2 12.4 %collective-permute-start.18 = (bf16[512,512]{1,0:T(8,128)(2,1)S(1)}, bf16[512,512]{1,0:T(8,128)(2,1)S(1)}, u32[]{:S(2)}, u32[]{:S(2)}) collective-permute-start(bf16[512,512]{1,0:T(8,128)(2,1)S(1)} %get-tuple-element.113), channel_id=1, source_target_pairs={{0,2},{1,3},{2,0},{3,1},{4,6},{5,7},{6,4},{7,5},{8,10},{9,11},{10,... | collective-permute-start | bytes 1572872 | tf_op jit(solution)/shard_map/ppermute | solution.py:271
  125.6 24.0 %collective-permute-start.22 = (bf16[512,768]{1,0:T(8,128)(2,1)S(1)}, bf16[512,768]{1,0:T(8,128)(2,1)S(1)}, u32[]{:S(2)}, u32[]{:S(2)}) collective-permute-start(bf16[512,768]{1,0:T(8,128)(2,1)S(1)} %copy-done.12), channel_id=1, source_target_pairs={{0,1},{1,0},{2,3},{3,2},{4,5},{5,4},{6,7},{7,6},{8,9},{9,8},{10,11... | collective-permute-start | bytes 2359304 | tf_op jit(solution)/shard_map/ppermute | solution.py:271
  126.1 2.2 copy-start.11
  128.3 4.2 %copy-start.6 = (bf16[1024,512]{1,0:T(8,128)(2,1)S(1)}, bf16[1024,512]{1,0:T(8,128)(2,1)}, u32[]{:S(2)}) copy-start(bf16[1024,512]{1,0:T(8,128)(2,1)} %get-tuple-element.98.other_ref) | copy-start | bytes 3145732
  135.8 28.2 %collective-permute-start.23 = (bf16[512,768]{1,0:T(8,128)(2,1)S(1)}, bf16[512,768]{1,0:T(8,128)(2,1)S(1)}, u32[]{:S(2)}, u32[]{:S(2)}) collective-permute-start(bf16[512,768]{1,0:T(8,128)(2,1)S(1)} %get-tuple-element.111), channel_id=1, source_target_pairs={{0,2},{1,3},{2,0},{3,1},{4,6},{5,7},{6,4},{7,5},{8,10},{9,11},{10,... | collective-permute-start | bytes 2359304 | tf_op jit(solution)/shard_map/ppermute | solution.py:271
  137.7 6.9 %collective-permute-start.20 = (bf16[128,512]{1,0:T(8,128)(2,1)S(1)}, bf16[128,512]{1,0:T(8,128)(2,1)S(1)}, u32[]{:S(2)}, u32[]{:S(2)}) collective-permute-start(bf16[128,512]{1,0:T(8,128)(2,1)S(1)} %get-tuple-element.117), channel_id=1, source_target_pairs={{0,4},{1,5},{2,6},{3,7},{4,8},{5,9},{6,10},{7,11},{8,12},{9,13},{1... | collective-permute-start | bytes 393224 | tf_op jit(solution)/shard_map/ppermute | solution.py:271
  138.5 6.5 %collective-permute-start.19 = (bf16[128,512]{1,0:T(8,128)(2,1)S(1)}, bf16[128,512]{1,0:T(8,128)(2,1)S(1)}, u32[]{:S(2)}, u32[]{:S(2)}) collective-permute-start(bf16[128,512]{1,0:T(8,128)(2,1)S(1)} %get-tuple-element.115), channel_id=1, source_target_pairs={{0,12},{1,13},{2,14},{3,15},{4,0},{5,1},{6,2},{7,3},{8,4},{9,5},{1... | collective-permute-start | bytes 393224 | tf_op jit(solution)/shard_map/ppermute | solution.py:271
  144.9 6.8 %collective-permute-start.21 = (bf16[128,512]{1,0:T(8,128)(2,1)S(1)}, bf16[128,512]{1,0:T(8,128)(2,1)S(1)}, u32[]{:S(2)}, u32[]{:S(2)}) collective-permute-start(bf16[128,512]{1,0:T(8,128)(2,1)S(1)} %add_piece.5), channel_id=1, source_target_pairs={{0,4},{1,5},{2,6},{3,7},{4,8},{5,9},{6,10},{7,11},{8,12},{9,13},{1... | collective-permute-start | bytes 393224 | tf_op jit(solution)/shard_map/ppermute | solution.py:271
  144.9 10.4 %copy-start.10 = (f32[1024,1024]{1,0:T(8,128)S(1)}, f32[1024,1024]{1,0:T(8,128)}, u32[]{:S(2)}) copy-start(f32[1024,1024]{1,0:T(8,128)} %get-tuple-element.125.refs_0_) | copy-start | bytes 12582916
  153.9 25.4 %collective-permute-start.27 = (bf16[512,768]{1,0:T(8,128)(2,1)S(1)}, bf16[512,768]{1,0:T(8,128)(2,1)S(1)}, u32[]{:S(2)}, u32[]{:S(2)}) collective-permute-start(bf16[512,768]{1,0:T(8,128)(2,1)S(1)} %get-tuple-element.137), channel_id=1, source_target_pairs={{0,2},{1,3},{2,0},{3,1},{4,6},{5,7},{6,4},{7,5},{8,10},{9,11},{10,... | collective-permute-start | bytes 2359304 | tf_op jit(solution)/shard_map/ppermute | solution.py:271
  155.3 2.9 %copy-start = (bf16[2,2048,256]{2,1,0:T(8,128)(2,1)S(1)}, bf16[2,2048,256]{2,1,0:T(8,128)(2,1)}, u32[]{:S(2)}) copy-start(bf16[2,2048,256]{2,1,0:T(8,128)(2,1)} %refs_0_.5) | copy-start | bytes 6291460
  155.3 2.9 %copy-start.1 = (bf16[2,2048,256]{2,1,0:T(8,128)(2,1)S(1)}, bf16[2,2048,256]{2,1,0:T(8,128)(2,1)}, u32[]{:S(2)}) copy-start(bf16[2,2048,256]{2,1,0:T(8,128)(2,1)} %refs_1_.5) | copy-start | bytes 6291460
  155.3 3.5 %copy-start.3 = (bf16[2,2048,256]{2,1,0:T(8,128)(2,1)S(1)}, bf16[2,2048,256]{2,1,0:T(8,128)(2,1)}, u32[]{:S(2)}) copy-start(bf16[2,2048,256]{2,1,0:T(8,128)(2,1)} %copy-done.2) | copy-start | bytes 6291460
  164.1 32.8 %collective-permute-start.31 = (bf16[512,768]{1,0:T(8,128)(2,1)S(1)}, bf16[512,768]{1,0:T(8,128)(2,1)S(1)}, u32[]{:S(2)}, u32[]{:S(2)}) collective-permute-start(bf16[512,768]{1,0:T(8,128)(2,1)S(1)} %get-tuple-element.147), channel_id=1, source_target_pairs={{0,2},{1,3},{2,0},{3,1},{4,6},{5,7},{6,4},{7,5},{8,10},{9,11},{10,... | collective-permute-start | bytes 2359304 | tf_op jit(solution)/shard_map/ppermute | solution.py:271
  164.8 5.7 %collective-permute-start.24 = (bf16[128,768]{1,0:T(8,128)(2,1)S(1)}, bf16[128,768]{1,0:T(8,128)(2,1)S(1)}, u32[]{:S(2)}, u32[]{:S(2)}) collective-permute-start(bf16[128,768]{1,0:T(8,128)(2,1)S(1)} %get-tuple-element.129), channel_id=1, source_target_pairs={{0,12},{1,13},{2,14},{3,15},{4,0},{5,1},{6,2},{7,3},{8,4},{9,5},{1... | collective-permute-start | bytes 589832 | tf_op jit(solution)/shard_map/ppermute | solution.py:271
  166.6 7.5 %collective-permute-start.25 = (bf16[128,768]{1,0:T(8,128)(2,1)S(1)}, bf16[128,768]{1,0:T(8,128)(2,1)S(1)}, u32[]{:S(2)}, u32[]{:S(2)}) collective-permute-start(bf16[128,768]{1,0:T(8,128)(2,1)S(1)} %get-tuple-element.131), channel_id=1, source_target_pairs={{0,4},{1,5},{2,6},{3,7},{4,8},{5,9},{6,10},{7,11},{8,12},{9,13},{1... | collective-permute-start | bytes 589832 | tf_op jit(solution)/shard_map/ppermute | solution.py:271
  179.4 44.3 %collective-permute-start.35 = (bf16[512,768]{1,0:T(8,128)(2,1)S(1)}, bf16[512,768]{1,0:T(8,128)(2,1)S(1)}, u32[]{:S(2)}, u32[]{:S(2)}) collective-permute-start(bf16[512,768]{1,0:T(8,128)(2,1)S(1)} %get-tuple-element.155), channel_id=1, source_target_pairs={{0,2},{1,3},{2,0},{3,1},{4,6},{5,7},{6,4},{7,5},{8,10},{9,11},{10,... | collective-permute-start | bytes 2359304 | tf_op jit(solution)/shard_map/ppermute | solution.py:271
  180.8 7.6 %collective-permute-start.29 = (bf16[128,768]{1,0:T(8,128)(2,1)S(1)}, bf16[128,768]{1,0:T(8,128)(2,1)S(1)}, u32[]{:S(2)}, u32[]{:S(2)}) collective-permute-start(bf16[128,768]{1,0:T(8,128)(2,1)S(1)} %get-tuple-element.141), channel_id=1, source_target_pairs={{0,4},{1,5},{2,6},{3,7},{4,8},{5,9},{6,10},{7,11},{8,12},{9,13},{1... | collective-permute-start | bytes 589832 | tf_op jit(solution)/shard_map/ppermute | solution.py:271
  181.2 11.2 %collective-permute-start.26 = (bf16[128,768]{1,0:T(8,128)(2,1)S(1)}, bf16[128,768]{1,0:T(8,128)(2,1)S(1)}, u32[]{:S(2)}, u32[]{:S(2)}) collective-permute-start(bf16[128,768]{1,0:T(8,128)(2,1)S(1)} %add_piece.6), channel_id=1, source_target_pairs={{0,4},{1,5},{2,6},{3,7},{4,8},{5,9},{6,10},{7,11},{8,12},{9,13},{1... | collective-permute-start | bytes 589832 | tf_op jit(solution)/shard_map/ppermute | solution.py:271
  181.7 15.1 %collective-permute-start.28 = (bf16[128,768]{1,0:T(8,128)(2,1)S(1)}, bf16[128,768]{1,0:T(8,128)(2,1)S(1)}, u32[]{:S(2)}, u32[]{:S(2)}) collective-permute-start(bf16[128,768]{1,0:T(8,128)(2,1)S(1)} %get-tuple-element.139), channel_id=1, source_target_pairs={{0,12},{1,13},{2,14},{3,15},{4,0},{5,1},{6,2},{7,3},{8,4},{9,5},{1... | collective-permute-start | bytes 589832 | tf_op jit(solution)/shard_map/ppermute | solution.py:271
  197.0 9.8 %collective-permute-start.33 = (bf16[128,768]{1,0:T(8,128)(2,1)S(1)}, bf16[128,768]{1,0:T(8,128)(2,1)S(1)}, u32[]{:S(2)}, u32[]{:S(2)}) collective-permute-start(bf16[128,768]{1,0:T(8,128)(2,1)S(1)} %get-tuple-element.151), channel_id=1, source_target_pairs={{0,4},{1,5},{2,6},{3,7},{4,8},{5,9},{6,10},{7,11},{8,12},{9,13},{1... | collective-permute-start | bytes 589832 | tf_op jit(solution)/shard_map/ppermute | solution.py:271
  199.5 9.4 %collective-permute-start.30 = (bf16[128,768]{1,0:T(8,128)(2,1)S(1)}, bf16[128,768]{1,0:T(8,128)(2,1)S(1)}, u32[]{:S(2)}, u32[]{:S(2)}) collective-permute-start(bf16[128,768]{1,0:T(8,128)(2,1)S(1)} %add_piece.7), channel_id=1, source_target_pairs={{0,4},{1,5},{2,6},{3,7},{4,8},{5,9},{6,10},{7,11},{8,12},{9,13},{1... | collective-permute-start | bytes 589832 | tf_op jit(solution)/shard_map/ppermute | solution.py:271
  199.5 14.6 %collective-permute-start.32 = (bf16[128,768]{1,0:T(8,128)(2,1)S(1)}, bf16[128,768]{1,0:T(8,128)(2,1)S(1)}, u32[]{:S(2)}, u32[]{:S(2)}) collective-permute-start(bf16[128,768]{1,0:T(8,128)(2,1)S(1)} %get-tuple-element.149), channel_id=1, source_target_pairs={{0,12},{1,13},{2,14},{3,15},{4,0},{5,1},{6,2},{7,3},{8,4},{9,5},{1... | collective-permute-start | bytes 589832 | tf_op jit(solution)/shard_map/ppermute | solution.py:271
  203.3 30.2 %collective-permute-start.39 = (bf16[512,512]{1,0:T(8,128)(2,1)S(1)}, bf16[512,512]{1,0:T(8,128)(2,1)S(1)}, u32[]{:S(2)}, u32[]{:S(2)}) collective-permute-start(bf16[512,512]{1,0:T(8,128)(2,1)S(1)} %get-tuple-element.163), channel_id=1, source_target_pairs={{0,2},{1,3},{2,0},{3,1},{4,6},{5,7},{6,4},{7,5},{8,10},{9,11},{10,... | collective-permute-start | bytes 1572872 | tf_op jit(solution)/shard_map/ppermute | solution.py:271
  214.1 9.6 %collective-permute-start.34 = (bf16[128,768]{1,0:T(8,128)(2,1)S(1)}, bf16[128,768]{1,0:T(8,128)(2,1)S(1)}, u32[]{:S(2)}, u32[]{:S(2)}) collective-permute-start(bf16[128,768]{1,0:T(8,128)(2,1)S(1)} %add_piece.8), channel_id=1, source_target_pairs={{0,4},{1,5},{2,6},{3,7},{4,8},{5,9},{6,10},{7,11},{8,12},{9,13},{1... | collective-permute-start | bytes 589832 | tf_op jit(solution)/shard_map/ppermute | solution.py:271
  223.9 7.7 %collective-permute-start.37 = (bf16[128,768]{1,0:T(8,128)(2,1)S(1)}, bf16[128,768]{1,0:T(8,128)(2,1)S(1)}, u32[]{:S(2)}, u32[]{:S(2)}) collective-permute-start(bf16[128,768]{1,0:T(8,128)(2,1)S(1)} %get-tuple-element.160), channel_id=1, source_target_pairs={{0,4},{1,5},{2,6},{3,7},{4,8},{5,9},{6,10},{7,11},{8,12},{9,13},{1... | collective-permute-start | bytes 589832 | tf_op jit(solution)/shard_map/ppermute | solution.py:271
  223.9 8.7 %collective-permute-start.36 = (bf16[128,768]{1,0:T(8,128)(2,1)S(1)}, bf16[128,768]{1,0:T(8,128)(2,1)S(1)}, u32[]{:S(2)}, u32[]{:S(2)}) collective-permute-start(bf16[128,768]{1,0:T(8,128)(2,1)S(1)} %get-tuple-element.158), channel_id=1, source_target_pairs={{0,12},{1,13},{2,14},{3,15},{4,0},{5,1},{6,2},{7,3},{8,4},{9,5},{1... | collective-permute-start | bytes 589832 | tf_op jit(solution)/shard_map/ppermute | solution.py:271
  232.6 11.7 %collective-permute-start.38 = (bf16[128,768]{1,0:T(8,128)(2,1)S(1)}, bf16[128,768]{1,0:T(8,128)(2,1)S(1)}, u32[]{:S(2)}, u32[]{:S(2)}) collective-permute-start(bf16[128,768]{1,0:T(8,128)(2,1)S(1)} %add_piece.9), channel_id=1, source_target_pairs={{0,4},{1,5},{2,6},{3,7},{4,8},{5,9},{6,10},{7,11},{8,12},{9,13},{1... | collective-permute-start | bytes 589832 | tf_op jit(solution)/shard_map/ppermute | solution.py:271
  233.6 8.1 %collective-permute-start.40 = (bf16[128,512]{1,0:T(8,128)(2,1)S(1)}, bf16[128,512]{1,0:T(8,128)(2,1)S(1)}, u32[]{:S(2)}, u32[]{:S(2)}) collective-permute-start(bf16[128,512]{1,0:T(8,128)(2,1)S(1)} %get-tuple-element.169), channel_id=1, source_target_pairs={{0,4},{1,5},{2,6},{3,7},{4,8},{5,9},{6,10},{7,11},{8,12},{9,13},{1... | collective-permute-start | bytes 393224 | tf_op jit(solution)/shard_map/ppermute | solution.py:271
  234.8 9.5 %collective-permute-start.41 = (bf16[128,512]{1,0:T(8,128)(2,1)S(1)}, bf16[128,512]{1,0:T(8,128)(2,1)S(1)}, u32[]{:S(2)}, u32[]{:S(2)}) collective-permute-start(bf16[128,512]{1,0:T(8,128)(2,1)S(1)} %get-tuple-element.170), channel_id=1, source_target_pairs={{0,8},{1,9},{2,10},{3,11},{4,12},{5,13},{6,14},{7,15},{8,0},{9,1},... | collective-permute-start | bytes 393224 | tf_op jit(solution)/shard_map/ppermute | solution.py:271
  237.1 7.1 %collective-permute-start.42 = (bf16[128,512]{1,0:T(8,128)(2,1)S(1)}, bf16[128,512]{1,0:T(8,128)(2,1)S(1)}, u32[]{:S(2)}, u32[]{:S(2)}) collective-permute-start(bf16[128,512]{1,0:T(8,128)(2,1)S(1)} %get-tuple-element.171), channel_id=1, source_target_pairs={{0,12},{1,13},{2,14},{3,15},{4,0},{5,1},{6,2},{7,3},{8,4},{9,5},{1... | collective-permute-start | bytes 393224 | tf_op jit(solution)/shard_map/ppermute | solution.py:271

commit v13 on v11

--- a/solution.py
+++ b/solution.py
@@ -307,7 +307,8 @@
     got = send_all([(grad, layer[-one])] + [(rows[k], side) for k in middle], far_rows[one])
     grads[one] = got[0]
     far_rows.update(zip(middle, got[1:]))
-    down_0, grads[last] = send_all([(downs[0], twin), (grad, layer[-last])], far_rows[last], other_gate)
+    (grads[last],) = send_all([(grad, layer[-last])], far_rows[last])
+    (down_0,) = send_all([(downs[0], twin)], far_rows[last], other_gate)
     (far_grads[one],) = send_all([(grads[one], side)], *far_rows.values())
     for k in middle:
         (grads[k],) = send_all([(grads[k - 1], layer[-one])], *far_rows.values())
@@ -345,7 +346,7 @@
     own_grads = hidden_grads(grad_blocks, [down], [(0, width)], by=by)
 
     keep_1, send = mix(1, down_1, send, own_grads)
-    own_0, *pieces = add_sides(keep_0, come_0, types)
+    own_0, *pieces = add_sides(after(keep_0, send), come_0, types)
     (come_1,) = send_all([(send, side)])
     far_0, next_0 = send_on(pieces)
     near_0 = send_last(pieces, next_0, far_0)

time: 236 us -> 237 us (level)
  starting transfers between devices: 52.3 us -> 59.6 us
  waiting for transfers between devices: 119 us -> 114 us
    ppermute x43, starting transfers between devices: 52.3 us -> 59.6 us  [send_all(): lax.ppermute(v, 'expert', pairs)]
    ppermute x43, waiting for transfers between devices: 119 us -> 114 us  [send_all(): lax.ppermute(v, 'expert', pairs)]
  transfers between devices with their start and end apart: 43 -> 43, of which waited for: 24 -> 25; matrix products, arithmetic and copies ran while one was open for 1% -> 1% of each run, Pallas kernels for 23% -> 23%
where the time goes in v13:
time: 237 us
  waiting for transfers between devices  114 us (48%)
  starting transfers between devices  59.6 us (25%)
  Pallas kernels  55 us (23%)
  local copies, waits for them, and re-layouts  6.06 us (3%)
    ppermute x43, waiting for transfers between devices, send_all(): lax.ppermute(v, 'expert', pairs)  114 us
    ppermute x43, starting transfers between devices, send_all(): lax.ppermute(v, 'expert', pairs)  59.6 us
    pallas_call x6, Pallas kernels, sum_columns(): pl.pallas_call(kernel, grid=(2,), in_specs=[rows, rows] + weight_specs, o...  21.4 us
    pallas_call x2, Pallas kernels, hidden_forward(): pl.pallas_call(functools.partial(hidden_kernel, blocks, all_experts), gri...  20 us
    pallas_call x3, Pallas kernels, hidden_grads(): pl.pallas_call(functools.partial(grads_kernel, blocks, tuple(cuts), by is...  10.5 us
  transfers between devices with their start and end apart: 43, of which 25 were waited for; matrix products, arithmetic and copies ran while one was open for 1% of the time, Pallas kernels for 23%

profile of v13, /device:TPU:0, one launch (start us, length us, event | category | flops | bytes accessed | tf_op | source)
XLA Modules:
  0.0 236.7 jit_solution(2251917151772666373)
XLA Ops:
  1.6 1.2 concatenate.3.refs_0_
  2.8 3.1 %collective-permute-start.3 = (bf16[128,2176]{1,0:T(8,128)(2,1)S(1)}, bf16[128,2176]{1,0:T(8,128)(2,1)S(1)}, u32[]{:S(2)}, u32[]{:S(2)}) collective-permute-start(bf16[128,2176]{1,0:T(8,128)(2,1)S(1)} %concatenate.3.refs_0_), channel_id=1, source_target_pairs={{0,4},{1,5},{2,6},{3,7},{4,8},{5,9},{6,10},{7,11},{8,12},{9,13},{1... | collective-permute-start | bytes 1671176 | tf_op jit(solution)/shard_map/ppermute | solution.py:271
  5.9 1.5 collective-permute-start.6
  7.4 1.5 collective-permute-start.8
  8.9 2.2 collective-permute-start
  11.7 9.3 %collective-permute-done.6.refs_6_.refs_7_ = bf16[128,2048]{1,0:T(8,128)(2,1)S(1)} collective-permute-done((bf16[128,2048]{1,0:T(8,128)(2,1)}, bf16[128,2048]{1,0:T(8,128)(2,1)S(1)}, u32[]{:S(2)}, u32[]{:S(2)}) %collective-permute-start.6) | collective-permute-done | bytes 524320 | tf_op jit(solution)/shard_map/ppermute | solution.py:271
  21.4 1.7 collective-permute-start.9
  23.2 9.3 %collective-permute-done.refs_1_ = bf16[128,2176]{1,0:T(8,128)(2,1)S(1)} collective-permute-done((bf16[128,2176]{1,0:T(8,128)(2,1)S(1)}, bf16[128,2176]{1,0:T(8,128)(2,1)S(1)}, u32[]{:S(2)}, u32[]{:S(2)}) %collective-permute-start) | collective-permute-done | bytes 557088 | tf_op jit(solution)/shard_map/ppermute | solution.py:271
  32.5 1.6 collective-permute-start.4
  34.1 3.3 %collective-permute-start.2 = (bf16[128,2176]{1,0:T(8,128)(2,1)S(1)}, bf16[128,2176]{1,0:T(8,128)(2,1)S(1)}, u32[]{:S(2)}, u32[]{:S(2)}) collective-permute-start(bf16[128,2176]{1,0:T(8,128)(2,1)S(1)} %collective-permute-done.refs_1_), channel_id=1, source_target_pairs={{0,12},{1,13},{2,14},{3,15},{4,0},{5,1},{6,2},{7,3},{8,4},{9,5},{1... | collective-permute-start | bytes 1671176 | tf_op jit(solution)/shard_map/ppermute | solution.py:271
  37.8 10.2 %collective-permute-done.4.refs_5_ = bf16[128,2176]{1,0:T(8,128)(2,1)S(1)} collective-permute-done((bf16[128,2176]{1,0:T(8,128)(2,1)S(1)}, bf16[128,2176]{1,0:T(8,128)(2,1)S(1)}, u32[]{:S(2)}, u32[]{:S(2)}) %collective-permute-start.4) | collective-permute-done | bytes 557088 | tf_op jit(solution)/shard_map/ppermute | solution.py:271
  48.3 1.4 collective-permute-start.5
  49.7 3.3 %collective-permute-start.11 = (bf16[128,2048]{1,0:T(8,128)(2,1)}, bf16[128,2048]{1,0:T(8,128)(2,1)S(1)}, u32[]{:S(2)}, u32[]{:S(2)}) collective-permute-start(bf16[128,2048]{1,0:T(8,128)(2,1)} %refs_3_), channel_id=1, source_target_pairs={{0,12},{1,13},{2,14},{3,15},{4,0},{5,1},{6,2},{7,3},{8,4},{9,5},{1... | collective-permute-start | bytes 1572872 | tf_op jit(solution)/shard_map/ppermute | solution.py:271
  53.0 7.0 %collective-permute-done.7.refs_7_ = bf16[128,2176]{1,0:T(8,128)(2,1)S(1)} collective-permute-done((bf16[128,2176]{1,0:T(8,128)(2,1)S(1)}, bf16[128,2176]{1,0:T(8,128)(2,1)S(1)}, u32[]{:S(2)}, u32[]{:S(2)}) %collective-permute-start.7) | collective-permute-done | bytes 557088 | tf_op jit(solution)/shard_map/ppermute | solution.py:271
  60.5 1.0 collective-permute-done.11.refs_3_.refs_4_
  61.5 9.4 %collective-permute-done.5.refs_6_ = bf16[128,2176]{1,0:T(8,128)(2,1)S(1)} collective-permute-done((bf16[128,2176]{1,0:T(8,128)(2,1)S(1)}, bf16[128,2176]{1,0:T(8,128)(2,1)S(1)}, u32[]{:S(2)}, u32[]{:S(2)}) %collective-permute-start.5) | collective-permute-done | bytes 557088 | tf_op jit(solution)/shard_map/ppermute | solution.py:271
  71.5 1.5 collective-permute-start.12
  73.0 1.9 slice.12
  74.9 1.5 collective-permute-start.10
  77.0 1.5 collective-permute-start.14
  78.5 10.1 %hidden_forward.2 = (bf16[1024,512]{1,0:T(8,128)(2,1)}, f32[1024,1024]{1,0:T(8,128)}) custom-call(s32[1]{0:T(128)} %bitcast.owner_ref, bf16[2,2048,256]{2,1,0:T(8,128)(2,1)} %refs_0_.5, bf16[2,2048,256]{2,1,0:T(8,128)(2,1)} %refs_1_.5, bf16[128,2176]{1,0:T(8,128)(2,1)} %copy-done.11, bf16[128,2176]{1,0:T(8,128)(2,1)} %copy-done.13, ...), custom_call_target="tpu_custom_call" | custom-call | flops 1 | bytes 1 | tf_op jit(solution)/shard_map/hidden_forward/pallas_call | solution.py:71
  89.2 1.0 fusion.1
  90.2 11.0 %collective-permute-done.9.up_ref.refs_3_ = bf16[2,2048,256]{2,1,0:T(8,128)(2,1)} collective-permute-done((bf16[2,2048,256]{2,1,0:T(8,128)(2,1)}, bf16[2,2048,256]{2,1,0:T(8,128)(2,1)}, u32[]{:S(2)}, u32[]{:S(2)}) %collective-permute-start.9) | collective-permute-done | bytes 2097184 | tf_op jit(solution)/shard_map/ppermute | solution.py:271
  101.2 9.9 %hidden_forward.3 = (bf16[1024,512]{1,0:T(8,128)(2,1)}, f32[1024,1024]{1,0:T(8,128)}) custom-call(s32[1]{0:T(128)} %bitcast.1.owner_ref, bf16[2,2048,256]{2,1,0:T(8,128)(2,1)} %copy-done.3, bf16[2,2048,256]{2,1,0:T(8,128)(2,1)} %collective-permute-done.9.up_ref.refs_3_, bf16[128,2176]{1,0:T(8,128)(2,1)} %copy-done.11, bf16[128,2176]{1,0:T(8,128)(2,1)} %copy-done.13, ...), custom_call_target="tpu_custom_call" | custom-call | flops 1 | bytes 1 | tf_op jit(solution)/shard_map/hidden_forward/pallas_call | solution.py:71
  111.2 1.6 collective-permute-start.17
  112.8 1.2 copy-done.6
  114.0 2.8 %mix_columns.3 = (f32[512,512]{1,0:T(8,128)S(1)}, bf16[512,512]{1,0:T(8,128)(2,1)S(1)}) custom-call(bf16[1024,512]{1,0:T(8,128)(2,1)S(1)} %copy-done.5, bf16[1024,512]{1,0:T(8,128)(2,1)S(1)} %copy-done.6, bf16[512,2048]{1,0:T(8,128)(2,1)S(1)} %bitcast.5, bf16[512,512]{1,0:T(8,128)(2,1)} %collective-permute-done.10.other_down_ref.refs_0_), custom_call_target="tpu_custom_call" | custom-call | flops 1 | bytes 1 | tf_op jit(solution)/shard_map/mix_columns/pallas_call | solution.py:179
  117.9 3.7 %hidden_grads.3.own_ref = bf16[1024,1024]{1,0:T(8,128)(2,1)S(1)} custom-call(f32[1024,1024]{1,0:T(8,128)S(1)} %copy-done.10, bf16[512,2048]{1,0:T(8,128)(2,1)S(1)} %bitcast.6, bf16[128,2048]{1,0:T(8,128)(2,1)S(1)} %copy-done.8, bf16[128,2048]{1,0:T(8,128)(2,1)S(1)} %collective-permute-done.11.refs_3_.refs_4_, ...), custom_call_target="tpu_custom_call" | custom-call | flops 1 | bytes 1 | tf_op jit(solution)/shard_map/hidden_grads/pallas_call | solution.py:127
  121.6 10.1 %collective-permute-done.17.other_down_ref.refs_1_ = bf16[512,768]{1,0:T(8,128)(2,1)S(1)} collective-permute-done((bf16[512,768]{1,0:T(8,128)(2,1)S(1)}, bf16[512,768]{1,0:T(8,128)(2,1)S(1)}, u32[]{:S(2)}, u32[]{:S(2)}) %collective-permute-start.17) | collective-permute-done | bytes 786464 | tf_op jit(solution)/shard_map/ppermute | solution.py:271
  131.7 2.2 mix_columns.4
  134.1 1.6 collective-permute-start.20
  135.7 2.2 collective-permute-start.19
  138.5 3.5 %collective-permute-done.20.come_ref = bf16[128,512]{1,0:T(8,128)(2,1)S(1)} collective-permute-done((bf16[128,512]{1,0:T(8,128)(2,1)S(1)}, bf16[128,512]{1,0:T(8,128)(2,1)S(1)}, u32[]{:S(2)}, u32[]{:S(2)}) %collective-permute-start.20) | collective-permute-done | bytes 131104 | tf_op jit(solution)/shard_map/ppermute | solution.py:271
  142.0 1.2 collective-permute-done.19.refs_1_
  143.8 4.0 %hidden_grads.4.refs_1_ = f32[1024,512]{1,0:T(8,128)S(1)} custom-call(bf16[512,512]{1,0:T(8,128)(2,1)} %collective-permute-done.10.other_down_ref.refs_0_, bf16[512,768]{1,0:T(8,128)(2,1)S(1)} %collective-permute-done.17.other_down_ref.refs_1_, bf16[128,2048]{1,0:T(8,128)(2,1)S(1)} %copy-done.8, ...), custom_call_target="tpu_custom_call" | custom-call | flops 1 | bytes 1 | tf_op jit(solution)/shard_map/hidden_grads/pallas_call | solution.py:127
  147.8 2.2 collective-permute-done.21.refs_2_
  150.0 2.2 mix_columns.5
  152.8 2.8 %hidden_grads.5.other_ref = bf16[1024,1024]{1,0:T(8,128)(2,1)S(1)} custom-call(f32[1024,1024]{1,0:T(8,128)S(1)} %copy-done.9, f32[1024,512]{1,0:T(8,128)S(1)} %hidden_grads.4.refs_1_, bf16[512,768]{1,0:T(8,128)(2,1)S(1)} %collective-permute-done.22.other_down_ref.refs_2_, bf16[128,2048]{1,0:T(8,128)(2,1)S(1)} %copy-done.8, ...), custom_call_target="tpu_custom_call" | custom-call | flops 1 | bytes 1 | tf_op jit(solution)/shard_map/hidden_grads/pallas_call | solution.py:127
  156.1 5.2 %back_columns.3 = (f32[512,768]{1,0:T(8,128)S(1)}, bf16[512,768]{1,0:T(8,128)(2,1)S(1)}) custom-call(bf16[1024,1024]{1,0:T(8,128)(2,1)S(1)} %hidden_grads.3.own_ref, bf16[1024,1024]{1,0:T(8,128)(2,1)S(1)} %hidden_grads.5.other_ref, bf16[2,2048,256]{2,1,0:T(8,128)(2,1)S(1)} %copy-done.1, bf16[2,2048,256]{2,1,0:T(8,128)(2,1)S(1)} %copy-done.2, ...), custom_call_target="tpu_custom_call" | custom-call | flops 1 | bytes 1 | tf_op jit(solution)/shard_map/back_columns/pallas_call | solution.py:179
  161.4 1.6 collective-permute-start.31
  163.0 1.1 collective-permute-start.24
  164.2 0.9 collective-permute-start.25
  165.1 3.6 %collective-permute-done.24.refs_4_ = bf16[128,768]{1,0:T(8,128)(2,1)S(1)} collective-permute-done((bf16[128,768]{1,0:T(8,128)(2,1)S(1)}, bf16[128,768]{1,0:T(8,128)(2,1)S(1)}, u32[]{:S(2)}, u32[]{:S(2)}) %collective-permute-start.24) | collective-permute-done | bytes 196640 | tf_op jit(solution)/shard_map/ppermute | solution.py:271
  168.7 2.9 %collective-permute-done.25.come_ref = bf16[128,768]{1,0:T(8,128)(2,1)S(1)} collective-permute-done((bf16[128,768]{1,0:T(8,128)(2,1)S(1)}, bf16[128,768]{1,0:T(8,128)(2,1)S(1)}, u32[]{:S(2)}, u32[]{:S(2)}) %collective-permute-start.25) | collective-permute-done | bytes 196640 | tf_op jit(solution)/shard_map/ppermute | solution.py:271
  171.6 5.2 %back_columns.4 = (f32[512,768]{1,0:T(8,128)S(1)}, bf16[512,768]{1,0:T(8,128)(2,1)S(1)}) custom-call(bf16[1024,1024]{1,0:T(8,128)(2,1)S(1)} %hidden_grads.3.own_ref, bf16[1024,1024]{1,0:T(8,128)(2,1)S(1)} %hidden_grads.5.other_ref, bf16[2,2048,256]{2,1,0:T(8,128)(2,1)S(1)} %copy-done.1, bf16[2,2048,256]{2,1,0:T(8,128)(2,1)S(1)} %copy-done.2, ...), custom_call_target="tpu_custom_call" | custom-call | flops 1 | bytes 1 | tf_op jit(solution)/shard_map/back_columns/pallas_call | solution.py:179
  177.9 0.9 collective-permute-start.26
  178.8 3.0 %collective-permute-start.28 = (bf16[128,768]{1,0:T(8,128)(2,1)S(1)}, bf16[128,768]{1,0:T(8,128)(2,1)S(1)}, u32[]{:S(2)}, u32[]{:S(2)}) collective-permute-start(bf16[128,768]{1,0:T(8,128)(2,1)S(1)} %get-tuple-element.139), channel_id=1, source_target_pairs={{0,12},{1,13},{2,14},{3,15},{4,0},{5,1},{6,2},{7,3},{8,4},{9,5},{1... | collective-permute-start | bytes 589832 | tf_op jit(solution)/shard_map/ppermute | solution.py:271
  181.8 3.3 %collective-permute-done.29.come_ref = bf16[128,768]{1,0:T(8,128)(2,1)S(1)} collective-permute-done((bf16[128,768]{1,0:T(8,128)(2,1)S(1)}, bf16[128,768]{1,0:T(8,128)(2,1)S(1)}, u32[]{:S(2)}, u32[]{:S(2)}) %collective-permute-start.29) | collective-permute-done | bytes 196640 | tf_op jit(solution)/shard_map/ppermute | solution.py:271
  185.2 3.9 %back_columns.5 = (f32[512,512]{1,0:T(8,128)S(1)}, bf16[512,512]{1,0:T(8,128)(2,1)S(1)}) custom-call(bf16[1024,1024]{1,0:T(8,128)(2,1)S(1)} %hidden_grads.3.own_ref, bf16[1024,1024]{1,0:T(8,128)(2,1)S(1)} %hidden_grads.5.other_ref, bf16[2,2048,256]{2,1,0:T(8,128)(2,1)S(1)} %copy-done.1, bf16[2,2048,256]{2,1,0:T(8,128)(2,1)S(1)} %copy-done.2, ...), custom_call_target="tpu_custom_call" | custom-call | flops 1 | bytes 1 | tf_op jit(solution)/shard_map/back_columns/pallas_call | solution.py:179
  189.7 1.0 collective-permute-start.39
  190.8 3.5 %collective-permute-done.28.refs_7_ = bf16[128,768]{1,0:T(8,128)(2,1)S(1)} collective-permute-done((bf16[128,768]{1,0:T(8,128)(2,1)S(1)}, bf16[128,768]{1,0:T(8,128)(2,1)S(1)}, u32[]{:S(2)}, u32[]{:S(2)}) %collective-permute-start.28) | collective-permute-done | bytes 196640 | tf_op jit(solution)/shard_map/ppermute | solution.py:271
  194.3 1.7 collective-permute-start.30
  196.0 3.8 %collective-permute-start.32 = (bf16[128,768]{1,0:T(8,128)(2,1)S(1)}, bf16[128,768]{1,0:T(8,128)(2,1)S(1)}, u32[]{:S(2)}, u32[]{:S(2)}) collective-permute-start(bf16[128,768]{1,0:T(8,128)(2,1)S(1)} %get-tuple-element.149), channel_id=1, source_target_pairs={{0,12},{1,13},{2,14},{3,15},{4,0},{5,1},{6,2},{7,3},{8,4},{9,5},{1... | collective-permute-start | bytes 589832 | tf_op jit(solution)/shard_map/ppermute | solution.py:271
  199.8 3.6 %collective-permute-done.30.refs_8_ = bf16[128,768]{1,0:T(8,128)(2,1)S(1)} collective-permute-done((bf16[128,768]{1,0:T(8,128)(2,1)S(1)}, bf16[128,768]{1,0:T(8,128)(2,1)S(1)}, u32[]{:S(2)}, u32[]{:S(2)}) %collective-permute-start.30) | collective-permute-done | bytes 196640 | tf_op jit(solution)/shard_map/ppermute | solution.py:271
  203.4 1.1 finish.2
  204.5 3.0 %collective-permute-done.33.come_ref = bf16[128,768]{1,0:T(8,128)(2,1)S(1)} collective-permute-done((bf16[128,768]{1,0:T(8,128)(2,1)S(1)}, bf16[128,768]{1,0:T(8,128)(2,1)S(1)}, u32[]{:S(2)}, u32[]{:S(2)}) %collective-permute-start.33) | collective-permute-done | bytes 196640 | tf_op jit(solution)/shard_map/ppermute | solution.py:271
  208.2 3.4 %collective-permute-start.36 = (bf16[128,768]{1,0:T(8,128)(2,1)S(1)}, bf16[128,768]{1,0:T(8,128)(2,1)S(1)}, u32[]{:S(2)}, u32[]{:S(2)}) collective-permute-start(bf16[128,768]{1,0:T(8,128)(2,1)S(1)} %get-tuple-element.158), channel_id=1, source_target_pairs={{0,12},{1,13},{2,14},{3,15},{4,0},{5,1},{6,2},{7,3},{8,4},{9,5},{1... | collective-permute-start | bytes 589832 | tf_op jit(solution)/shard_map/ppermute | solution.py:271
  212.2 3.6 %collective-permute-done.37.come_ref = bf16[128,768]{1,0:T(8,128)(2,1)S(1)} collective-permute-done((bf16[128,768]{1,0:T(8,128)(2,1)S(1)}, bf16[128,768]{1,0:T(8,128)(2,1)S(1)}, u32[]{:S(2)}, u32[]{:S(2)}) %collective-permute-start.37) | collective-permute-done | bytes 196640 | tf_op jit(solution)/shard_map/ppermute | solution.py:271
  215.8 8.2 %collective-permute-done.36.refs_4_ = bf16[128,768]{1,0:T(8,128)(2,1)S(1)} collective-permute-done((bf16[128,768]{1,0:T(8,128)(2,1)S(1)}, bf16[128,768]{1,0:T(8,128)(2,1)S(1)}, u32[]{:S(2)}, u32[]{:S(2)}) %collective-permute-start.36) | collective-permute-done | bytes 196640 | tf_op jit(solution)/shard_map/ppermute | solution.py:271
  223.9 1.3 collective-permute-start.38
  225.4 3.1 %collective-permute-start.41 = (bf16[128,512]{1,0:T(8,128)(2,1)S(1)}, bf16[128,512]{1,0:T(8,128)(2,1)S(1)}, u32[]{:S(2)}, u32[]{:S(2)}) collective-permute-start(bf16[128,512]{1,0:T(8,128)(2,1)S(1)} %get-tuple-element.170), channel_id=1, source_target_pairs={{0,8},{1,9},{2,10},{3,11},{4,12},{5,13},{6,14},{7,15},{8,0},{9,1},... | collective-permute-start | bytes 393224 | tf_op jit(solution)/shard_map/ppermute | solution.py:271
  229.2 3.8 %collective-permute-done.40.refs_7_ = bf16[128,512]{1,0:T(8,128)(2,1)S(1)} collective-permute-done((bf16[128,512]{1,0:T(8,128)(2,1)S(1)}, bf16[128,512]{1,0:T(8,128)(2,1)S(1)}, u32[]{:S(2)}, u32[]{:S(2)}) %collective-permute-start.40) | collective-permute-done | bytes 131104 | tf_op jit(solution)/shard_map/ppermute | solution.py:271
  233.0 2.6 %collective-permute-done.41.refs_8_ = bf16[128,512]{1,0:T(8,128)(2,1)S(1)} collective-permute-done((bf16[128,512]{1,0:T(8,128)(2,1)S(1)}, bf16[128,512]{1,0:T(8,128)(2,1)S(1)}, u32[]{:S(2)}, u32[]{:S(2)}) %collective-permute-start.41) | collective-permute-done | bytes 131104 | tf_op jit(solution)/shard_map/ppermute | solution.py:271
  235.6 1.1 finish.3
  (93 shorter events, 12.6 us)
Async XLA Ops:
  2.8 45.5 %copy-start.11 = (bf16[128,2176]{1,0:T(8,128)(2,1)}, bf16[128,2176]{1,0:T(8,128)(2,1)S(1)}, u32[]{:S(2)}) copy-start(bf16[128,2176]{1,0:T(8,128)(2,1)S(1)} %concatenate.3.refs_0_) | copy-start | bytes 1671172
  2.8 18.6 %collective-permute-start.3 = (bf16[128,2176]{1,0:T(8,128)(2,1)S(1)}, bf16[128,2176]{1,0:T(8,128)(2,1)S(1)}, u32[]{:S(2)}, u32[]{:S(2)}) collective-permute-start(bf16[128,2176]{1,0:T(8,128)(2,1)S(1)} %concatenate.3.refs_0_), channel_id=1, source_target_pairs={{0,4},{1,5},{2,6},{3,7},{4,8},{5,9},{6,10},{7,11},{8,12},{9,13},{1... | collective-permute-start | bytes 1671176 | tf_op jit(solution)/shard_map/ppermute | solution.py:271
  5.9 15.1 %collective-permute-start.6 = (bf16[128,2048]{1,0:T(8,128)(2,1)}, bf16[128,2048]{1,0:T(8,128)(2,1)S(1)}, u32[]{:S(2)}, u32[]{:S(2)}) collective-permute-start(bf16[128,2048]{1,0:T(8,128)(2,1)} %refs_3_), channel_id=1, source_target_pairs={{0,2},{1,3},{2,0},{3,1},{4,6},{5,7},{6,4},{7,5},{8,10},{9,11},{10,... | collective-permute-start | bytes 1572872 | tf_op jit(solution)/shard_map/ppermute | solution.py:271
  7.4 67.5 %collective-permute-start.8 = (bf16[2,2048,256]{2,1,0:T(8,128)(2,1)}, bf16[2,2048,256]{2,1,0:T(8,128)(2,1)S(1)}, u32[]{:S(2)}, u32[]{:S(2)}) collective-permute-start(bf16[2,2048,256]{2,1,0:T(8,128)(2,1)} %refs_0_.5), channel_id=1, source_target_pairs={{0,1},{1,0},{2,3},{3,2},{4,5},{5,4},{6,7},{7,6},{8,9},{9,8},{10,11... | collective-permute-start | bytes 6291464 | tf_op jit(solution)/shard_map/ppermute | solution.py:271
  8.9 23.6 %collective-permute-start = (bf16[128,2176]{1,0:T(8,128)(2,1)S(1)}, bf16[128,2176]{1,0:T(8,128)(2,1)S(1)}, u32[]{:S(2)}, u32[]{:S(2)}) collective-permute-start(bf16[128,2176]{1,0:T(8,128)(2,1)S(1)} %concatenate.3.refs_0_), channel_id=1, source_target_pairs={{0,12},{1,13},{2,14},{3,15},{4,0},{5,1},{6,2},{7,3},{8,4},{9,5},{1... | collective-permute-start | bytes 1671176 | tf_op jit(solution)/shard_map/ppermute | solution.py:271
  11.2 21.3 %collective-permute-start.1 = (bf16[128,2176]{1,0:T(8,128)(2,1)S(1)}, bf16[128,2176]{1,0:T(8,128)(2,1)S(1)}, u32[]{:S(2)}, u32[]{:S(2)}) collective-permute-start(bf16[128,2176]{1,0:T(8,128)(2,1)S(1)} %concatenate.3.refs_0_), channel_id=1, source_target_pairs={{0,2},{1,3},{2,0},{3,1},{4,6},{5,7},{6,4},{7,5},{8,10},{9,11},{10,... | collective-permute-start | bytes 1671176 | tf_op jit(solution)/shard_map/ppermute | solution.py:271
  21.4 49.5 %copy-start.12 = (bf16[128,2176]{1,0:T(8,128)(2,1)}, bf16[128,2176]{1,0:T(8,128)(2,1)S(1)}, u32[]{:S(2)}) copy-start(bf16[128,2176]{1,0:T(8,128)(2,1)S(1)} %collective-permute-done.3.refs_3_) | copy-start | bytes 1671172
  21.4 79.8 %collective-permute-start.9 = (bf16[2,2048,256]{2,1,0:T(8,128)(2,1)}, bf16[2,2048,256]{2,1,0:T(8,128)(2,1)}, u32[]{:S(2)}, u32[]{:S(2)}) collective-permute-start(bf16[2,2048,256]{2,1,0:T(8,128)(2,1)} %refs_1_.5), channel_id=1, source_target_pairs={{0,1},{1,0},{2,3},{3,2},{4,5},{5,4},{6,7},{7,6},{8,9},{9,8},{10,11... | collective-permute-start | bytes 6291464 | tf_op jit(solution)/shard_map/ppermute | solution.py:271
  32.5 39.0 %copy-start.13 = (bf16[128,2176]{1,0:T(8,128)(2,1)}, bf16[128,2176]{1,0:T(8,128)(2,1)S(1)}, u32[]{:S(2)}) copy-start(bf16[128,2176]{1,0:T(8,128)(2,1)S(1)} %collective-permute-done.refs_1_) | copy-start | bytes 1671172
  32.5 40.5 %copy-start.14 = (bf16[128,2176]{1,0:T(8,128)(2,1)}, bf16[128,2176]{1,0:T(8,128)(2,1)S(1)}, u32[]{:S(2)}) copy-start(bf16[128,2176]{1,0:T(8,128)(2,1)S(1)} %collective-permute-done.1.refs_4_) | copy-start | bytes 1671172
  32.5 15.6 %collective-permute-start.4 = (bf16[128,2176]{1,0:T(8,128)(2,1)S(1)}, bf16[128,2176]{1,0:T(8,128)(2,1)S(1)}, u32[]{:S(2)}, u32[]{:S(2)}) collective-permute-start(bf16[128,2176]{1,0:T(8,128)(2,1)S(1)} %collective-permute-done.refs_1_), channel_id=1, source_target_pairs={{0,2},{1,3},{2,0},{3,1},{4,6},{5,7},{6,4},{7,5},{8,10},{9,11},{10,... | collective-permute-start | bytes 1671176 | tf_op jit(solution)/shard_map/ppermute | solution.py:271
  34.1 14.2 %collective-permute-start.2 = (bf16[128,2176]{1,0:T(8,128)(2,1)S(1)}, bf16[128,2176]{1,0:T(8,128)(2,1)S(1)}, u32[]{:S(2)}, u32[]{:S(2)}) collective-permute-start(bf16[128,2176]{1,0:T(8,128)(2,1)S(1)} %collective-permute-done.refs_1_), channel_id=1, source_target_pairs={{0,12},{1,13},{2,14},{3,15},{4,0},{5,1},{6,2},{7,3},{8,4},{9,5},{1... | collective-permute-start | bytes 1671176 | tf_op jit(solution)/shard_map/ppermute | solution.py:271
  37.3 22.7 %collective-permute-start.7 = (bf16[128,2176]{1,0:T(8,128)(2,1)S(1)}, bf16[128,2176]{1,0:T(8,128)(2,1)S(1)}, u32[]{:S(2)}, u32[]{:S(2)}) collective-permute-start(bf16[128,2176]{1,0:T(8,128)(2,1)S(1)} %collective-permute-done.3.refs_3_), channel_id=1, source_target_pairs={{0,2},{1,3},{2,0},{3,1},{4,6},{5,7},{6,4},{7,5},{8,10},{9,11},{10,... | collective-permute-start | bytes 1671176 | tf_op jit(solution)/shard_map/ppermute | solution.py:271
  48.1 25.0 %copy-start.15 = (bf16[128,2176]{1,0:T(8,128)(2,1)}, bf16[128,2176]{1,0:T(8,128)(2,1)S(1)}, u32[]{:S(2)}) copy-start(bf16[128,2176]{1,0:T(8,128)(2,1)S(1)} %collective-permute-done.4.refs_5_) | copy-start | bytes 1671172
  48.3 24.7 %copy-start.16 = (bf16[128,2176]{1,0:T(8,128)(2,1)}, bf16[128,2176]{1,0:T(8,128)(2,1)S(1)}, u32[]{:S(2)}) copy-start(bf16[128,2176]{1,0:T(8,128)(2,1)S(1)} %collective-permute-done.2.refs_2_) | copy-start | bytes 1671172
  48.3 22.6 %collective-permute-start.5 = (bf16[128,2176]{1,0:T(8,128)(2,1)S(1)}, bf16[128,2176]{1,0:T(8,128)(2,1)S(1)}, u32[]{:S(2)}, u32[]{:S(2)}) collective-permute-start(bf16[128,2176]{1,0:T(8,128)(2,1)S(1)} %collective-permute-done.2.refs_2_), channel_id=1, source_target_pairs={{0,2},{1,3},{2,0},{3,1},{4,6},{5,7},{6,4},{7,5},{8,10},{9,11},{10,... | collective-permute-start | bytes 1671176 | tf_op jit(solution)/shard_map/ppermute | solution.py:271
  49.7 11.9 %collective-permute-start.11 = (bf16[128,2048]{1,0:T(8,128)(2,1)}, bf16[128,2048]{1,0:T(8,128)(2,1)S(1)}, u32[]{:S(2)}, u32[]{:S(2)}) collective-permute-start(bf16[128,2048]{1,0:T(8,128)(2,1)} %refs_3_), channel_id=1, source_target_pairs={{0,12},{1,13},{2,14},{3,15},{4,0},{5,1},{6,2},{7,3},{8,4},{9,5},{1... | collective-permute-start | bytes 1572872 | tf_op jit(solution)/shard_map/ppermute | solution.py:271
  60.0 13.0 %copy-start.17 = (bf16[128,2176]{1,0:T(8,128)(2,1)}, bf16[128,2176]{1,0:T(8,128)(2,1)S(1)}, u32[]{:S(2)}) copy-start(bf16[128,2176]{1,0:T(8,128)(2,1)S(1)} %collective-permute-done.7.refs_7_) | copy-start | bytes 1671172
  60.0 17.0 %collective-permute-start.13 = (bf16[128,2048]{1,0:T(8,128)(2,1)}, bf16[128,2048]{1,0:T(8,128)(2,1)}, u32[]{:S(2)}, u32[]{:S(2)}) collective-permute-start(bf16[128,2048]{1,0:T(8,128)(2,1)} %refs_3_), channel_id=1, source_target_pairs={{0,4},{1,5},{2,6},{3,7},{4,8},{5,9},{6,10},{7,11},{8,12},{9,13},{1... | collective-permute-start | bytes 1572872 | tf_op jit(solution)/shard_map/ppermute | solution.py:271
  70.9 2.1 copy-start.18
  70.9 17.6 %collective-permute-start.15 = (bf16[128,2048]{1,0:T(8,128)(2,1)S(1)}, bf16[128,2048]{1,0:T(8,128)(2,1)}, u32[]{:S(2)}, u32[]{:S(2)}) collective-permute-start(bf16[128,2048]{1,0:T(8,128)(2,1)S(1)} %collective-permute-done.11.refs_3_.refs_4_), channel_id=1, source_target_pairs={{0,12},{1,13},{2,14},{3,15},{4,0},{5,1},{6,2},{7,3},{8,4},{9,5},{1... | collective-permute-start | bytes 1572872 | tf_op jit(solution)/shard_map/ppermute | solution.py:271
  71.5 17.1 %collective-permute-start.12 = (bf16[128,2048]{1,0:T(8,128)(2,1)S(1)}, bf16[128,2048]{1,0:T(8,128)(2,1)}, u32[]{:S(2)}, u32[]{:S(2)}) collective-permute-start(bf16[128,2048]{1,0:T(8,128)(2,1)S(1)} %collective-permute-done.11.refs_3_.refs_4_), channel_id=1, source_target_pairs={{0,2},{1,3},{2,0},{3,1},{4,6},{5,7},{6,4},{7,5},{8,10},{9,11},{10,... | collective-permute-start | bytes 1572872 | tf_op jit(solution)/shard_map/ppermute | solution.py:271
  74.9 13.7 %copy-start.3 = (bf16[2,2048,256]{2,1,0:T(8,128)(2,1)}, bf16[2,2048,256]{2,1,0:T(8,128)(2,1)S(1)}, u32[]{:S(2)}) copy-start(bf16[2,2048,256]{2,1,0:T(8,128)(2,1)S(1)} %collective-permute-done.8.gate_ref.refs_2_) | copy-start | bytes 6291460
  74.9 36.3 %collective-permute-start.10 = (bf16[512,512]{1,0:T(8,128)(2,1)}, bf16[512,512]{1,0:T(8,128)(2,1)}, u32[]{:S(2)}, u32[]{:S(2)}) collective-permute-start(bf16[512,512]{1,0:T(8,128)(2,1)} %slice.12), channel_id=1, source_target_pairs={{0,1},{1,0},{2,3},{3,2},{4,5},{5,4},{6,7},{7,6},{8,9},{9,8},{10,11... | collective-permute-start | bytes 1572872 | tf_op jit(solution)/shard_map/ppermute | solution.py:271
  77.0 35.8 %collective-permute-start.14 = (bf16[128,2048]{1,0:T(8,128)(2,1)}, bf16[128,2048]{1,0:T(8,128)(2,1)S(1)}, u32[]{:S(2)}, u32[]{:S(2)}) collective-permute-start(bf16[128,2048]{1,0:T(8,128)(2,1)} %collective-permute-done.13.refs_5_.refs_6_), channel_id=1, source_target_pairs={{0,2},{1,3},{2,0},{3,1},{4,6},{5,7},{6,4},{7,5},{8,10},{9,11},{10,... | collective-permute-start | bytes 1572872 | tf_op jit(solution)/shard_map/ppermute | solution.py:271
  78.5 10.7 %copy-start = (bf16[2,256,2048]{2,1,0:T(8,128)(2,1)S(1)}, bf16[2,256,2048]{2,1,0:T(8,128)(2,1)}, u32[]{:S(2)}) copy-start(bf16[2,256,2048]{2,1,0:T(8,128)(2,1)} %param.13) | copy-start | bytes 6291460
  88.6 24.1 %collective-permute-start.16 = (bf16[128,2048]{1,0:T(8,128)(2,1)}, bf16[128,2048]{1,0:T(8,128)(2,1)S(1)}, u32[]{:S(2)}, u32[]{:S(2)}) collective-permute-start(bf16[128,2048]{1,0:T(8,128)(2,1)} %collective-permute-done.15.refs_4_.refs_5_), channel_id=1, source_target_pairs={{0,2},{1,3},{2,0},{3,1},{4,6},{5,7},{6,4},{7,5},{8,10},{9,11},{10,... | collective-permute-start | bytes 1572872 | tf_op jit(solution)/shard_map/ppermute | solution.py:271
  101.2 11.5 %copy-start.5 = (bf16[1024,512]{1,0:T(8,128)(2,1)S(1)}, bf16[1024,512]{1,0:T(8,128)(2,1)}, u32[]{:S(2)}) copy-start(bf16[1024,512]{1,0:T(8,128)(2,1)} %get-tuple-element.94.own_ref) | copy-start | bytes 3145732
  111.2 20.5 %collective-permute-start.17 = (bf16[512,768]{1,0:T(8,128)(2,1)S(1)}, bf16[512,768]{1,0:T(8,128)(2,1)S(1)}, u32[]{:S(2)}, u32[]{:S(2)}) collective-permute-start(bf16[512,768]{1,0:T(8,128)(2,1)S(1)} %get-tuple-element.107), channel_id=1, source_target_pairs={{0,1},{1,0},{2,3},{3,2},{4,5},{5,4},{6,7},{7,6},{8,9},{9,8},{10,11... | collective-permute-start | bytes 2359304 | tf_op jit(solution)/shard_map/ppermute | solution.py:271
  112.8 1.2 copy-start.6
  114.0 3.9 %copy-start.8 = (bf16[128,2048]{1,0:T(8,128)(2,1)S(1)}, bf16[128,2048]{1,0:T(8,128)(2,1)}, u32[]{:S(2)}) copy-start(bf16[128,2048]{1,0:T(8,128)(2,1)} %refs_3_) | copy-start | bytes 1572868
  114.0 3.9 %copy-start.10 = (f32[1024,1024]{1,0:T(8,128)S(1)}, f32[1024,1024]{1,0:T(8,128)}, u32[]{:S(2)}) copy-start(f32[1024,1024]{1,0:T(8,128)} %get-tuple-element.109.refs_0_) | copy-start | bytes 12582916
  116.8 17.2 %collective-permute-start.18 = (bf16[512,512]{1,0:T(8,128)(2,1)S(1)}, bf16[512,512]{1,0:T(8,128)(2,1)S(1)}, u32[]{:S(2)}, u32[]{:S(2)}) collective-permute-start(bf16[512,512]{1,0:T(8,128)(2,1)S(1)} %get-tuple-element.113), channel_id=1, source_target_pairs={{0,2},{1,3},{2,0},{3,1},{4,6},{5,7},{6,4},{7,5},{8,10},{9,11},{10,... | collective-permute-start | bytes 1572872 | tf_op jit(solution)/shard_map/ppermute | solution.py:271
  117.4 30.5 %collective-permute-start.22 = (bf16[512,768]{1,0:T(8,128)(2,1)}, bf16[512,768]{1,0:T(8,128)(2,1)S(1)}, u32[]{:S(2)}, u32[]{:S(2)}) collective-permute-start(bf16[512,768]{1,0:T(8,128)(2,1)} %get-tuple-element.121), channel_id=1, source_target_pairs={{0,1},{1,0},{2,3},{3,2},{4,5},{5,4},{6,7},{7,6},{8,9},{9,8},{10,11... | collective-permute-start | bytes 2359304 | tf_op jit(solution)/shard_map/ppermute | solution.py:271
  117.9 13.8 %copy-start.7 = (bf16[1024,512]{1,0:T(8,128)(2,1)S(1)}, bf16[1024,512]{1,0:T(8,128)(2,1)}, u32[]{:S(2)}) copy-start(bf16[1024,512]{1,0:T(8,128)(2,1)} %get-tuple-element.98.other_ref) | copy-start | bytes 3145732
  134.1 7.9 %collective-permute-start.20 = (bf16[128,512]{1,0:T(8,128)(2,1)S(1)}, bf16[128,512]{1,0:T(8,128)(2,1)S(1)}, u32[]{:S(2)}, u32[]{:S(2)}) collective-permute-start(bf16[128,512]{1,0:T(8,128)(2,1)S(1)} %get-tuple-element.117), channel_id=1, source_target_pairs={{0,4},{1,5},{2,6},{3,7},{4,8},{5,9},{6,10},{7,11},{8,12},{9,13},{1... | collective-permute-start | bytes 393224 | tf_op jit(solution)/shard_map/ppermute | solution.py:271
  135.7 7.5 %collective-permute-start.19 = (bf16[128,512]{1,0:T(8,128)(2,1)S(1)}, bf16[128,512]{1,0:T(8,128)(2,1)S(1)}, u32[]{:S(2)}, u32[]{:S(2)}) collective-permute-start(bf16[128,512]{1,0:T(8,128)(2,1)S(1)} %get-tuple-element.115), channel_id=1, source_target_pairs={{0,12},{1,13},{2,14},{3,15},{4,0},{5,1},{6,2},{7,3},{8,4},{9,5},{1... | collective-permute-start | bytes 393224 | tf_op jit(solution)/shard_map/ppermute | solution.py:271
  138.0 23.3 %collective-permute-start.23 = (bf16[512,768]{1,0:T(8,128)(2,1)S(1)}, bf16[512,768]{1,0:T(8,128)(2,1)S(1)}, u32[]{:S(2)}, u32[]{:S(2)}) collective-permute-start(bf16[512,768]{1,0:T(8,128)(2,1)S(1)} %get-tuple-element.111), channel_id=1, source_target_pairs={{0,2},{1,3},{2,0},{3,1},{4,6},{5,7},{6,4},{7,5},{8,10},{9,11},{10,... | collective-permute-start | bytes 2359304 | tf_op jit(solution)/shard_map/ppermute | solution.py:271
  143.2 6.8 %collective-permute-start.21 = (bf16[128,512]{1,0:T(8,128)(2,1)S(1)}, bf16[128,512]{1,0:T(8,128)(2,1)S(1)}, u32[]{:S(2)}, u32[]{:S(2)}) collective-permute-start(bf16[128,512]{1,0:T(8,128)(2,1)S(1)} %add_piece.5), channel_id=1, source_target_pairs={{0,4},{1,5},{2,6},{3,7},{4,8},{5,9},{6,10},{7,11},{8,12},{9,13},{1... | collective-permute-start | bytes 393224 | tf_op jit(solution)/shard_map/ppermute | solution.py:271
  147.8 5.0 %copy-start.9 = (f32[1024,1024]{1,0:T(8,128)S(1)}, f32[1024,1024]{1,0:T(8,128)}, u32[]{:S(2)}) copy-start(f32[1024,1024]{1,0:T(8,128)} %get-tuple-element.125.refs_0_) | copy-start | bytes 12582916
  152.2 24.6 %collective-permute-start.27 = (bf16[512,768]{1,0:T(8,128)(2,1)S(1)}, bf16[512,768]{1,0:T(8,128)(2,1)S(1)}, u32[]{:S(2)}, u32[]{:S(2)}) collective-permute-start(bf16[512,768]{1,0:T(8,128)(2,1)S(1)} %get-tuple-element.137), channel_id=1, source_target_pairs={{0,2},{1,3},{2,0},{3,1},{4,6},{5,7},{6,4},{7,5},{8,10},{9,11},{10,... | collective-permute-start | bytes 2359304 | tf_op jit(solution)/shard_map/ppermute | solution.py:271
  152.8 2.8 %copy-start.1 = (bf16[2,2048,256]{2,1,0:T(8,128)(2,1)S(1)}, bf16[2,2048,256]{2,1,0:T(8,128)(2,1)}, u32[]{:S(2)}) copy-start(bf16[2,2048,256]{2,1,0:T(8,128)(2,1)} %refs_0_.5) | copy-start | bytes 6291460
  152.8 2.8 %copy-start.2 = (bf16[2,2048,256]{2,1,0:T(8,128)(2,1)S(1)}, bf16[2,2048,256]{2,1,0:T(8,128)(2,1)}, u32[]{:S(2)}) copy-start(bf16[2,2048,256]{2,1,0:T(8,128)(2,1)} %refs_1_.5) | copy-start | bytes 6291460
  152.8 3.3 %copy-start.4 = (bf16[2,2048,256]{2,1,0:T(8,128)(2,1)S(1)}, bf16[2,2048,256]{2,1,0:T(8,128)(2,1)}, u32[]{:S(2)}) copy-start(bf16[2,2048,256]{2,1,0:T(8,128)(2,1)} %copy-done.3) | copy-start | bytes 6291460
  161.4 28.2 %collective-permute-start.31 = (bf16[512,768]{1,0:T(8,128)(2,1)S(1)}, bf16[512,768]{1,0:T(8,128)(2,1)S(1)}, u32[]{:S(2)}, u32[]{:S(2)}) collective-permute-start(bf16[512,768]{1,0:T(8,128)(2,1)S(1)} %get-tuple-element.147), channel_id=1, source_target_pairs={{0,2},{1,3},{2,0},{3,1},{4,6},{5,7},{6,4},{7,5},{8,10},{9,11},{10,... | collective-permute-start | bytes 2359304 | tf_op jit(solution)/shard_map/ppermute | solution.py:271
  163.0 5.7 %collective-permute-start.24 = (bf16[128,768]{1,0:T(8,128)(2,1)S(1)}, bf16[128,768]{1,0:T(8,128)(2,1)S(1)}, u32[]{:S(2)}, u32[]{:S(2)}) collective-permute-start(bf16[128,768]{1,0:T(8,128)(2,1)S(1)} %get-tuple-element.129), channel_id=1, source_target_pairs={{0,12},{1,13},{2,14},{3,15},{4,0},{5,1},{6,2},{7,3},{8,4},{9,5},{1... | collective-permute-start | bytes 589832 | tf_op jit(solution)/shard_map/ppermute | solution.py:271
  164.2 7.5 %collective-permute-start.25 = (bf16[128,768]{1,0:T(8,128)(2,1)S(1)}, bf16[128,768]{1,0:T(8,128)(2,1)S(1)}, u32[]{:S(2)}, u32[]{:S(2)}) collective-permute-start(bf16[128,768]{1,0:T(8,128)(2,1)S(1)} %get-tuple-element.131), channel_id=1, source_target_pairs={{0,4},{1,5},{2,6},{3,7},{4,8},{5,9},{6,10},{7,11},{8,12},{9,13},{1... | collective-permute-start | bytes 589832 | tf_op jit(solution)/shard_map/ppermute | solution.py:271
  177.0 30.6 %collective-permute-start.35 = (bf16[512,768]{1,0:T(8,128)(2,1)S(1)}, bf16[512,768]{1,0:T(8,128)(2,1)S(1)}, u32[]{:S(2)}, u32[]{:S(2)}) collective-permute-start(bf16[512,768]{1,0:T(8,128)(2,1)S(1)} %get-tuple-element.155), channel_id=1, source_target_pairs={{0,2},{1,3},{2,0},{3,1},{4,6},{5,7},{6,4},{7,5},{8,10},{9,11},{10,... | collective-permute-start | bytes 2359304 | tf_op jit(solution)/shard_map/ppermute | solution.py:271
  177.5 7.6 %collective-permute-start.29 = (bf16[128,768]{1,0:T(8,128)(2,1)S(1)}, bf16[128,768]{1,0:T(8,128)(2,1)S(1)}, u32[]{:S(2)}, u32[]{:S(2)}) collective-permute-start(bf16[128,768]{1,0:T(8,128)(2,1)S(1)} %get-tuple-element.141), channel_id=1, source_target_pairs={{0,4},{1,5},{2,6},{3,7},{4,8},{5,9},{6,10},{7,11},{8,12},{9,13},{1... | collective-permute-start | bytes 589832 | tf_op jit(solution)/shard_map/ppermute | solution.py:271
  177.9 12.9 %collective-permute-start.26 = (bf16[128,768]{1,0:T(8,128)(2,1)S(1)}, bf16[128,768]{1,0:T(8,128)(2,1)S(1)}, u32[]{:S(2)}, u32[]{:S(2)}) collective-permute-start(bf16[128,768]{1,0:T(8,128)(2,1)S(1)} %add_piece.6), channel_id=1, source_target_pairs={{0,4},{1,5},{2,6},{3,7},{4,8},{5,9},{6,10},{7,11},{8,12},{9,13},{1... | collective-permute-start | bytes 589832 | tf_op jit(solution)/shard_map/ppermute | solution.py:271
  178.8 15.5 %collective-permute-start.28 = (bf16[128,768]{1,0:T(8,128)(2,1)S(1)}, bf16[128,768]{1,0:T(8,128)(2,1)S(1)}, u32[]{:S(2)}, u32[]{:S(2)}) collective-permute-start(bf16[128,768]{1,0:T(8,128)(2,1)S(1)} %get-tuple-element.139), channel_id=1, source_target_pairs={{0,12},{1,13},{2,14},{3,15},{4,0},{5,1},{6,2},{7,3},{8,4},{9,5},{1... | collective-permute-start | bytes 589832 | tf_op jit(solution)/shard_map/ppermute | solution.py:271
  189.7 35.5 %collective-permute-start.39 = (bf16[512,512]{1,0:T(8,128)(2,1)S(1)}, bf16[512,512]{1,0:T(8,128)(2,1)S(1)}, u32[]{:S(2)}, u32[]{:S(2)}) collective-permute-start(bf16[512,512]{1,0:T(8,128)(2,1)S(1)} %get-tuple-element.163), channel_id=1, source_target_pairs={{0,2},{1,3},{2,0},{3,1},{4,6},{5,7},{6,4},{7,5},{8,10},{9,11},{10,... | collective-permute-start | bytes 1572872 | tf_op jit(solution)/shard_map/ppermute | solution.py:271
  194.3 9.1 %collective-permute-start.30 = (bf16[128,768]{1,0:T(8,128)(2,1)S(1)}, bf16[128,768]{1,0:T(8,128)(2,1)S(1)}, u32[]{:S(2)}, u32[]{:S(2)}) collective-permute-start(bf16[128,768]{1,0:T(8,128)(2,1)S(1)} %add_piece.7), channel_id=1, source_target_pairs={{0,4},{1,5},{2,6},{3,7},{4,8},{5,9},{6,10},{7,11},{8,12},{9,13},{1... | collective-permute-start | bytes 589832 | tf_op jit(solution)/shard_map/ppermute | solution.py:271
  196.0 11.5 %collective-permute-start.33 = (bf16[128,768]{1,0:T(8,128)(2,1)S(1)}, bf16[128,768]{1,0:T(8,128)(2,1)S(1)}, u32[]{:S(2)}, u32[]{:S(2)}) collective-permute-start(bf16[128,768]{1,0:T(8,128)(2,1)S(1)} %get-tuple-element.151), channel_id=1, source_target_pairs={{0,4},{1,5},{2,6},{3,7},{4,8},{5,9},{6,10},{7,11},{8,12},{9,13},{1... | collective-permute-start | bytes 589832 | tf_op jit(solution)/shard_map/ppermute | solution.py:271
  196.0 15.6 %collective-permute-start.32 = (bf16[128,768]{1,0:T(8,128)(2,1)S(1)}, bf16[128,768]{1,0:T(8,128)(2,1)S(1)}, u32[]{:S(2)}, u32[]{:S(2)}) collective-permute-start(bf16[128,768]{1,0:T(8,128)(2,1)S(1)} %get-tuple-element.149), channel_id=1, source_target_pairs={{0,12},{1,13},{2,14},{3,15},{4,0},{5,1},{6,2},{7,3},{8,4},{9,5},{1... | collective-permute-start | bytes 589832 | tf_op jit(solution)/shard_map/ppermute | solution.py:271
  207.7 8.1 %collective-permute-start.37 = (bf16[128,768]{1,0:T(8,128)(2,1)S(1)}, bf16[128,768]{1,0:T(8,128)(2,1)S(1)}, u32[]{:S(2)}, u32[]{:S(2)}) collective-permute-start(bf16[128,768]{1,0:T(8,128)(2,1)S(1)} %get-tuple-element.160), channel_id=1, source_target_pairs={{0,4},{1,5},{2,6},{3,7},{4,8},{5,9},{6,10},{7,11},{8,12},{9,13},{1... | collective-permute-start | bytes 589832 | tf_op jit(solution)/shard_map/ppermute | solution.py:271
  208.2 15.7 %collective-permute-start.36 = (bf16[128,768]{1,0:T(8,128)(2,1)S(1)}, bf16[128,768]{1,0:T(8,128)(2,1)S(1)}, u32[]{:S(2)}, u32[]{:S(2)}) collective-permute-start(bf16[128,768]{1,0:T(8,128)(2,1)S(1)} %get-tuple-element.158), channel_id=1, source_target_pairs={{0,12},{1,13},{2,14},{3,15},{4,0},{5,1},{6,2},{7,3},{8,4},{9,5},{1... | collective-permute-start | bytes 589832 | tf_op jit(solution)/shard_map/ppermute | solution.py:271
  211.6 13.7 %collective-permute-start.34 = (bf16[128,768]{1,0:T(8,128)(2,1)S(1)}, bf16[128,768]{1,0:T(8,128)(2,1)S(1)}, u32[]{:S(2)}, u32[]{:S(2)}) collective-permute-start(bf16[128,768]{1,0:T(8,128)(2,1)S(1)} %add_piece.8), channel_id=1, source_target_pairs={{0,4},{1,5},{2,6},{3,7},{4,8},{5,9},{6,10},{7,11},{8,12},{9,13},{1... | collective-permute-start | bytes 589832 | tf_op jit(solution)/shard_map/ppermute | solution.py:271
  223.9 11.7 %collective-permute-start.38 = (bf16[128,768]{1,0:T(8,128)(2,1)S(1)}, bf16[128,768]{1,0:T(8,128)(2,1)S(1)}, u32[]{:S(2)}, u32[]{:S(2)}) collective-permute-start(bf16[128,768]{1,0:T(8,128)(2,1)S(1)} %add_piece.9), channel_id=1, source_target_pairs={{0,4},{1,5},{2,6},{3,7},{4,8},{5,9},{6,10},{7,11},{8,12},{9,13},{1... | collective-permute-start | bytes 589832 | tf_op jit(solution)/shard_map/ppermute | solution.py:271
  225.4 7.6 %collective-permute-start.40 = (bf16[128,512]{1,0:T(8,128)(2,1)S(1)}, bf16[128,512]{1,0:T(8,128)(2,1)S(1)}, u32[]{:S(2)}, u32[]{:S(2)}) collective-permute-start(bf16[128,512]{1,0:T(8,128)(2,1)S(1)} %get-tuple-element.169), channel_id=1, source_target_pairs={{0,4},{1,5},{2,6},{3,7},{4,8},{5,9},{6,10},{7,11},{8,12},{9,13},{1... | collective-permute-start | bytes 393224 | tf_op jit(solution)/shard_map/ppermute | solution.py:271
  225.4 10.2 %collective-permute-start.41 = (bf16[128,512]{1,0:T(8,128)(2,1)S(1)}, bf16[128,512]{1,0:T(8,128)(2,1)S(1)}, u32[]{:S(2)}, u32[]{:S(2)}) collective-permute-start(bf16[128,512]{1,0:T(8,128)(2,1)S(1)} %get-tuple-element.170), channel_id=1, source_target_pairs={{0,8},{1,9},{2,10},{3,11},{4,12},{5,13},{6,14},{7,15},{8,0},{9,1},... | collective-permute-start | bytes 393224 | tf_op jit(solution)/shard_map/ppermute | solution.py:271
  228.5 7.1 %collective-permute-start.42 = (bf16[128,512]{1,0:T(8,128)(2,1)S(1)}, bf16[128,512]{1,0:T(8,128)(2,1)S(1)}, u32[]{:S(2)}, u32[]{:S(2)}) collective-permute-start(bf16[128,512]{1,0:T(8,128)(2,1)S(1)} %get-tuple-element.171), channel_id=1, source_target_pairs={{0,12},{1,13},{2,14},{3,15},{4,0},{5,1},{6,2},{7,3},{8,4},{9,5},{1... | collective-permute-start | bytes 393224 | tf_op jit(solution)/shard_map/ppermute | solution.py:271

commit v14 on v13

--- a/solution.py
+++ b/solution.py
@@ -348,10 +348,10 @@
     keep_1, send = mix(1, down_1, send, own_grads)
     own_0, *pieces = add_sides(after(keep_0, send), come_0, types)
     (come_1,) = send_all([(send, side)])
-    far_0, next_0 = send_on(pieces)
+    grad_blocks = [after(grad_blocks[0], send), *grad_blocks[1:]]
+    other_grad = hidden_grads(grad_blocks, [down_0, down_1], chunks[:2])
+    far_0, next_0 = send_on(pieces, other_grad)
     near_0 = send_last(pieces, next_0, far_0)
-    grad_blocks = [after(grad_blocks[0], next_0), *grad_blocks[1:]]
-    other_grad = hidden_grads(grad_blocks, [down_0, down_1], chunks[:2])
 
     keep_2, send = mix(2, down_2, other_grad, near_0)
     (come_2,) = send_all([(send, side)], own_0)
@@ -364,14 +364,14 @@
         lo, hi = back_chunks[c]
         return back_columns(own_grads, after(other_grads, *waits), weights, lo // (hi - lo), hi - lo)
 
-    keep_3, send = back(0)
-    own_1, *pieces = add_sides(after(keep_1, send), come_1, types)
-    (come_3,) = send_all([(send, side)], own_1)
+    own_1, *pieces = add_sides(after(keep_1, other_grads), come_1, types)
     far_1, next_1 = send_on(pieces)
     near_1 = send_last(pieces, next_1, far_1)
-
-    keep_4, send = back(1, next_1, far_1)
-    own_2, *pieces = add_sides(after(keep_2, send), come_2, types)
+    keep_3, send = back(0, next_1, far_1)
+    (come_3,) = send_all([(send, side)], own_1)
+
+    keep_4, send = back(1, send)
+    own_2, *pieces = add_sides(keep_2, come_2, types)
     (come_4,) = send_all([(send, side)], own_2)
     far_2, next_2 = send_on(pieces)
     near_2 = send_last(pieces, next_2, far_2, near_1)

time: 237 us -> 238 us (level)
  starting transfers between devices: 59.6 us -> 63 us
    ppermute x43, starting transfers between devices: 59.6 us -> 63 us  [send_all(): lax.ppermute(v, 'expert', pairs)]
    ppermute x43, waiting for transfers between devices: 114 us -> 112 us  [send_all(): lax.ppermute(v, 'expert', pairs)]
where the time goes in v14:
time: 238 us
  waiting for transfers between devices  112 us (47%)
  starting transfers between devices  63 us (26%)
  Pallas kernels  55.5 us (23%)
  local copies, waits for them, and re-layouts  5.83 us (2%)
    ppermute x43, waiting for transfers between devices, send_all(): lax.ppermute(v, 'expert', pairs)  112 us
    ppermute x43, starting transfers between devices, send_all(): lax.ppermute(v, 'expert', pairs)  63 us
    pallas_call x6, Pallas kernels, sum_columns(): pl.pallas_call(kernel, grid=(2,), in_specs=[rows, rows] + weight_specs, o...  22 us
    pallas_call x2, Pallas kernels, hidden_forward(): pl.pallas_call(functools.partial(hidden_kernel, blocks, all_experts), gri...  20.1 us
    pallas_call x3, Pallas kernels, hidden_grads(): pl.pallas_call(functools.partial(grads_kernel, blocks, tuple(cuts), by is...  10.4 us
  transfers between devices with their start and end apart: 43, of which 25 were waited for; matrix products, arithmetic and copies ran while one was open for 1% of the time, Pallas kernels for 23%

profile of v14, /device:TPU:0, one launch (start us, length us, event | category | flops | bytes accessed | tf_op | source)
XLA Modules:
  0.0 237.7 jit_solution(10706565127859153382)
XLA Ops:
  1.6 1.2 concatenate.3.refs_0_
  2.8 3.1 %collective-permute-start.3 = (bf16[128,2176]{1,0:T(8,128)(2,1)S(1)}, bf16[128,2176]{1,0:T(8,128)(2,1)S(1)}, u32[]{:S(2)}, u32[]{:S(2)}) collective-permute-start(bf16[128,2176]{1,0:T(8,128)(2,1)S(1)} %concatenate.3.refs_0_), channel_id=1, source_target_pairs={{0,4},{1,5},{2,6},{3,7},{4,8},{5,9},{6,10},{7,11},{8,12},{9,13},{1... | collective-permute-start | bytes 1671176 | tf_op jit(solution)/shard_map/ppermute | solution.py:271
  5.9 1.5 collective-permute-start.6
  7.4 1.5 collective-permute-start.8
  8.9 2.2 collective-permute-start
  11.7 9.3 %collective-permute-done.6.refs_6_.refs_7_ = bf16[128,2048]{1,0:T(8,128)(2,1)S(1)} collective-permute-done((bf16[128,2048]{1,0:T(8,128)(2,1)}, bf16[128,2048]{1,0:T(8,128)(2,1)S(1)}, u32[]{:S(2)}, u32[]{:S(2)}) %collective-permute-start.6) | collective-permute-done | bytes 524320 | tf_op jit(solution)/shard_map/ppermute | solution.py:271
  21.4 1.7 collective-permute-start.9
  23.2 9.3 %collective-permute-done.refs_1_ = bf16[128,2176]{1,0:T(8,128)(2,1)S(1)} collective-permute-done((bf16[128,2176]{1,0:T(8,128)(2,1)S(1)}, bf16[128,2176]{1,0:T(8,128)(2,1)S(1)}, u32[]{:S(2)}, u32[]{:S(2)}) %collective-permute-start) | collective-permute-done | bytes 557088 | tf_op jit(solution)/shard_map/ppermute | solution.py:271
  32.5 1.6 collective-permute-start.4
  34.1 3.3 %collective-permute-start.2 = (bf16[128,2176]{1,0:T(8,128)(2,1)S(1)}, bf16[128,2176]{1,0:T(8,128)(2,1)S(1)}, u32[]{:S(2)}, u32[]{:S(2)}) collective-permute-start(bf16[128,2176]{1,0:T(8,128)(2,1)S(1)} %collective-permute-done.refs_1_), channel_id=1, source_target_pairs={{0,12},{1,13},{2,14},{3,15},{4,0},{5,1},{6,2},{7,3},{8,4},{9,5},{1... | collective-permute-start | bytes 1671176 | tf_op jit(solution)/shard_map/ppermute | solution.py:271
  37.8 10.2 %collective-permute-done.4.refs_5_ = bf16[128,2176]{1,0:T(8,128)(2,1)S(1)} collective-permute-done((bf16[128,2176]{1,0:T(8,128)(2,1)S(1)}, bf16[128,2176]{1,0:T(8,128)(2,1)S(1)}, u32[]{:S(2)}, u32[]{:S(2)}) %collective-permute-start.4) | collective-permute-done | bytes 557088 | tf_op jit(solution)/shard_map/ppermute | solution.py:271
  48.4 1.2 collective-permute-start.5
  49.6 3.3 %collective-permute-start.11 = (bf16[128,2048]{1,0:T(8,128)(2,1)}, bf16[128,2048]{1,0:T(8,128)(2,1)S(1)}, u32[]{:S(2)}, u32[]{:S(2)}) collective-permute-start(bf16[128,2048]{1,0:T(8,128)(2,1)} %refs_3_), channel_id=1, source_target_pairs={{0,12},{1,13},{2,14},{3,15},{4,0},{5,1},{6,2},{7,3},{8,4},{9,5},{1... | collective-permute-start | bytes 1572872 | tf_op jit(solution)/shard_map/ppermute | solution.py:271
  53.0 7.0 %collective-permute-done.7.refs_7_ = bf16[128,2176]{1,0:T(8,128)(2,1)S(1)} collective-permute-done((bf16[128,2176]{1,0:T(8,128)(2,1)S(1)}, bf16[128,2176]{1,0:T(8,128)(2,1)S(1)}, u32[]{:S(2)}, u32[]{:S(2)}) %collective-permute-start.7) | collective-permute-done | bytes 557088 | tf_op jit(solution)/shard_map/ppermute | solution.py:271
  60.5 1.3 collective-permute-done.11.refs_3_.refs_4_
  61.9 9.2 %collective-permute-done.5.refs_6_ = bf16[128,2176]{1,0:T(8,128)(2,1)S(1)} collective-permute-done((bf16[128,2176]{1,0:T(8,128)(2,1)S(1)}, bf16[128,2176]{1,0:T(8,128)(2,1)S(1)}, u32[]{:S(2)}, u32[]{:S(2)}) %collective-permute-start.5) | collective-permute-done | bytes 557088 | tf_op jit(solution)/shard_map/ppermute | solution.py:271
  71.5 1.5 collective-permute-start.12
  73.0 1.9 slice.12
  74.9 1.5 collective-permute-start.10
  77.0 1.5 collective-permute-start.14
  78.5 10.0 %hidden_forward.2 = (bf16[1024,512]{1,0:T(8,128)(2,1)}, f32[1024,1024]{1,0:T(8,128)}) custom-call(s32[1]{0:T(128)} %bitcast.owner_ref, bf16[2,2048,256]{2,1,0:T(8,128)(2,1)} %refs_0_.5, bf16[2,2048,256]{2,1,0:T(8,128)(2,1)} %refs_1_.5, bf16[128,2176]{1,0:T(8,128)(2,1)} %copy-done.8, bf16[128,2176]{1,0:T(8,128)(2,1)} %copy-done.10, ...), custom_call_target="tpu_custom_call" | custom-call | flops 1 | bytes 1 | tf_op jit(solution)/shard_map/hidden_forward/pallas_call | solution.py:71
  89.1 1.3 fusion.1
  90.4 10.9 %collective-permute-done.9.up_ref.refs_3_ = bf16[2,2048,256]{2,1,0:T(8,128)(2,1)} collective-permute-done((bf16[2,2048,256]{2,1,0:T(8,128)(2,1)}, bf16[2,2048,256]{2,1,0:T(8,128)(2,1)}, u32[]{:S(2)}, u32[]{:S(2)}) %collective-permute-start.9) | collective-permute-done | bytes 2097184 | tf_op jit(solution)/shard_map/ppermute | solution.py:271
  101.2 10.1 %hidden_forward.3 = (bf16[1024,512]{1,0:T(8,128)(2,1)}, f32[1024,1024]{1,0:T(8,128)}) custom-call(s32[1]{0:T(128)} %bitcast.1.owner_ref, bf16[2,2048,256]{2,1,0:T(8,128)(2,1)} %collective-permute-done.8.gate_ref.refs_2_, bf16[2,2048,256]{2,1,0:T(8,128)(2,1)} %collective-permute-done.9.up_ref.refs_3_, bf16[128,2176]{1,0:T(8,128)(2,1)} %copy-done.8, ...), custom_call_target="tpu_custom_call" | custom-call | flops 1 | bytes 1 | tf_op jit(solution)/shard_map/hidden_forward/pallas_call | solution.py:71
  111.4 1.6 collective-permute-start.17
  112.9 1.2 copy-done.4
  114.2 2.8 %mix_columns.3 = (f32[512,512]{1,0:T(8,128)S(1)}, bf16[512,512]{1,0:T(8,128)(2,1)S(1)}) custom-call(bf16[1024,512]{1,0:T(8,128)(2,1)S(1)} %copy-done.3, bf16[1024,512]{1,0:T(8,128)(2,1)S(1)} %copy-done.4, bf16[512,2048]{1,0:T(8,128)(2,1)S(1)} %bitcast.5, bf16[512,512]{1,0:T(8,128)(2,1)} %collective-permute-done.10.other_down_ref.refs_0_), custom_call_target="tpu_custom_call" | custom-call | flops 1 | bytes 1 | tf_op jit(solution)/shard_map/mix_columns/pallas_call | solution.py:179
  118.1 3.6 %hidden_grads.3.own_ref = bf16[1024,1024]{1,0:T(8,128)(2,1)S(1)} custom-call(f32[1024,1024]{1,0:T(8,128)S(1)} %copy-done.7, bf16[512,2048]{1,0:T(8,128)(2,1)S(1)} %bitcast.6, bf16[128,2048]{1,0:T(8,128)(2,1)S(1)} %copy-done.5, bf16[128,2048]{1,0:T(8,128)(2,1)S(1)} %collective-permute-done.11.refs_3_.refs_4_, ...), custom_call_target="tpu_custom_call" | custom-call | flops 1 | bytes 1 | tf_op jit(solution)/shard_map/hidden_grads/pallas_call | solution.py:127
  121.7 10.2 %collective-permute-done.17.other_down_ref.refs_1_ = bf16[512,768]{1,0:T(8,128)(2,1)S(1)} collective-permute-done((bf16[512,768]{1,0:T(8,128)(2,1)S(1)}, bf16[512,768]{1,0:T(8,128)(2,1)S(1)}, u32[]{:S(2)}, u32[]{:S(2)}) %collective-permute-start.17) | collective-permute-done | bytes 786464 | tf_op jit(solution)/shard_map/ppermute | solution.py:271
  131.9 2.2 mix_columns.4
  134.7 4.0 %hidden_grads.4.refs_1_ = f32[1024,512]{1,0:T(8,128)S(1)} custom-call(bf16[512,512]{1,0:T(8,128)(2,1)} %collective-permute-done.10.other_down_ref.refs_0_, bf16[512,768]{1,0:T(8,128)(2,1)S(1)} %collective-permute-done.17.other_down_ref.refs_1_, bf16[128,2048]{1,0:T(8,128)(2,1)S(1)} %copy-done.5, ...), custom_call_target="tpu_custom_call" | custom-call | flops 1 | bytes 1 | tf_op jit(solution)/shard_map/hidden_grads/pallas_call | solution.py:127
  138.8 1.6 collective-permute-start.20
  140.5 2.2 collective-permute-start.19
  142.7 3.4 %collective-permute-done.20.come_ref = bf16[128,512]{1,0:T(8,128)(2,1)S(1)} collective-permute-done((bf16[128,512]{1,0:T(8,128)(2,1)S(1)}, bf16[128,512]{1,0:T(8,128)(2,1)S(1)}, u32[]{:S(2)}, u32[]{:S(2)}) %collective-permute-start.20) | collective-permute-done | bytes 131104 | tf_op jit(solution)/shard_map/ppermute | solution.py:271
  146.2 1.2 collective-permute-done.19.refs_1_
  147.9 7.3 %collective-permute-done.21.refs_2_ = bf16[128,512]{1,0:T(8,128)(2,1)S(1)} collective-permute-done((bf16[128,512]{1,0:T(8,128)(2,1)S(1)}, bf16[128,512]{1,0:T(8,128)(2,1)S(1)}, u32[]{:S(2)}, u32[]{:S(2)}) %collective-permute-start.21) | collective-permute-done | bytes 131104 | tf_op jit(solution)/shard_map/ppermute | solution.py:271
  155.3 2.2 mix_columns.5
  157.5 1.8 collective-permute-start.27
  159.3 2.8 %hidden_grads.5.other_ref = bf16[1024,1024]{1,0:T(8,128)(2,1)S(1)} custom-call(f32[1024,1024]{1,0:T(8,128)S(1)} %copy-done.6, f32[1024,512]{1,0:T(8,128)S(1)} %hidden_grads.4.refs_1_, bf16[512,768]{1,0:T(8,128)(2,1)S(1)} %collective-permute-done.22.other_down_ref.refs_2_, bf16[128,2048]{1,0:T(8,128)(2,1)S(1)} %copy-done.5, ...), custom_call_target="tpu_custom_call" | custom-call | flops 1 | bytes 1 | tf_op jit(solution)/shard_map/hidden_grads/pallas_call | solution.py:127
  162.3 2.0 collective-permute-start.25
  164.3 3.7 %collective-permute-done.24.refs_4_ = bf16[128,768]{1,0:T(8,128)(2,1)S(1)} collective-permute-done((bf16[128,768]{1,0:T(8,128)(2,1)S(1)}, bf16[128,768]{1,0:T(8,128)(2,1)S(1)}, u32[]{:S(2)}, u32[]{:S(2)}) %collective-permute-start.24) | collective-permute-done | bytes 196640 | tf_op jit(solution)/shard_map/ppermute | solution.py:271
  168.0 2.1 collective-permute-done.25.come_ref
  170.1 5.4 %back_columns.3 = (f32[512,768]{1,0:T(8,128)S(1)}, bf16[512,768]{1,0:T(8,128)(2,1)S(1)}) custom-call(bf16[1024,1024]{1,0:T(8,128)(2,1)S(1)} %hidden_grads.3.own_ref, bf16[1024,1024]{1,0:T(8,128)(2,1)S(1)} %hidden_grads.5.other_ref, bf16[2,2048,256]{2,1,0:T(8,128)(2,1)S(1)} %copy-done.1, bf16[2,2048,256]{2,1,0:T(8,128)(2,1)S(1)} %copy-done.2, ...), custom_call_target="tpu_custom_call" | custom-call | flops 1 | bytes 1 | tf_op jit(solution)/shard_map/back_columns/pallas_call | solution.py:179
  175.8 5.4 %back_columns.5 = (f32[512,768]{1,0:T(8,128)S(1)}, bf16[512,768]{1,0:T(8,128)(2,1)S(1)}) custom-call(bf16[1024,1024]{1,0:T(8,128)(2,1)S(1)} %hidden_grads.3.own_ref, bf16[1024,1024]{1,0:T(8,128)(2,1)S(1)} %hidden_grads.5.other_ref, bf16[2,2048,256]{2,1,0:T(8,128)(2,1)S(1)} %copy-done.1, bf16[2,2048,256]{2,1,0:T(8,128)(2,1)S(1)} %copy-done.2, ...), custom_call_target="tpu_custom_call" | custom-call | flops 1 | bytes 1 | tf_op jit(solution)/shard_map/back_columns/pallas_call | solution.py:179
  181.3 1.8 collective-permute-start.35
  183.2 1.5 collective-permute-start.26
  184.7 2.4 %collective-permute-start.28 = (bf16[128,768]{1,0:T(8,128)(2,1)S(1)}, bf16[128,768]{1,0:T(8,128)(2,1)S(1)}, u32[]{:S(2)}, u32[]{:S(2)}) collective-permute-start(bf16[128,768]{1,0:T(8,128)(2,1)S(1)} %get-tuple-element.139), channel_id=1, source_target_pairs={{0,12},{1,13},{2,14},{3,15},{4,0},{5,1},{6,2},{7,3},{8,4},{9,5},{1... | collective-permute-start | bytes 589832 | tf_op jit(solution)/shard_map/ppermute | solution.py:271
  187.1 5.8 %collective-permute-done.29.come_ref = bf16[128,768]{1,0:T(8,128)(2,1)S(1)} collective-permute-done((bf16[128,768]{1,0:T(8,128)(2,1)S(1)}, bf16[128,768]{1,0:T(8,128)(2,1)S(1)}, u32[]{:S(2)}, u32[]{:S(2)}) %collective-permute-start.29) | collective-permute-done | bytes 196640 | tf_op jit(solution)/shard_map/ppermute | solution.py:271
  192.8 4.0 %back_columns.4 = (f32[512,512]{1,0:T(8,128)S(1)}, bf16[512,512]{1,0:T(8,128)(2,1)S(1)}) custom-call(bf16[1024,1024]{1,0:T(8,128)(2,1)S(1)} %hidden_grads.3.own_ref, bf16[1024,1024]{1,0:T(8,128)(2,1)S(1)} %hidden_grads.5.other_ref, bf16[2,2048,256]{2,1,0:T(8,128)(2,1)S(1)} %copy-done.1, bf16[2,2048,256]{2,1,0:T(8,128)(2,1)S(1)} %copy-done.2, ...), custom_call_target="tpu_custom_call" | custom-call | flops 1 | bytes 1 | tf_op jit(solution)/shard_map/back_columns/pallas_call | solution.py:179
  197.4 1.6 collective-permute-done.28.refs_7_
  198.9 2.3 collective-permute-start.30
  201.7 3.3 %collective-permute-start.32 = (bf16[128,768]{1,0:T(8,128)(2,1)S(1)}, bf16[128,768]{1,0:T(8,128)(2,1)S(1)}, u32[]{:S(2)}, u32[]{:S(2)}) collective-permute-start(bf16[128,768]{1,0:T(8,128)(2,1)S(1)} %get-tuple-element.151), channel_id=1, source_target_pairs={{0,12},{1,13},{2,14},{3,15},{4,0},{5,1},{6,2},{7,3},{8,4},{9,5},{1... | collective-permute-start | bytes 589832 | tf_op jit(solution)/shard_map/ppermute | solution.py:271
  205.1 3.7 %collective-permute-done.30.refs_8_ = bf16[128,768]{1,0:T(8,128)(2,1)S(1)} collective-permute-done((bf16[128,768]{1,0:T(8,128)(2,1)S(1)}, bf16[128,768]{1,0:T(8,128)(2,1)S(1)}, u32[]{:S(2)}, u32[]{:S(2)}) %collective-permute-start.30) | collective-permute-done | bytes 196640 | tf_op jit(solution)/shard_map/ppermute | solution.py:271
  208.7 1.1 finish.2
  209.8 3.0 %collective-permute-done.33.come_ref = bf16[128,768]{1,0:T(8,128)(2,1)S(1)} collective-permute-done((bf16[128,768]{1,0:T(8,128)(2,1)S(1)}, bf16[128,768]{1,0:T(8,128)(2,1)S(1)}, u32[]{:S(2)}, u32[]{:S(2)}) %collective-permute-start.33) | collective-permute-done | bytes 196640 | tf_op jit(solution)/shard_map/ppermute | solution.py:271
  213.0 3.8 %collective-permute-start.36 = (bf16[128,768]{1,0:T(8,128)(2,1)S(1)}, bf16[128,768]{1,0:T(8,128)(2,1)S(1)}, u32[]{:S(2)}, u32[]{:S(2)}) collective-permute-start(bf16[128,768]{1,0:T(8,128)(2,1)S(1)} %get-tuple-element.162), channel_id=1, source_target_pairs={{0,12},{1,13},{2,14},{3,15},{4,0},{5,1},{6,2},{7,3},{8,4},{9,5},{1... | collective-permute-start | bytes 589832 | tf_op jit(solution)/shard_map/ppermute | solution.py:271
  216.8 2.7 %collective-permute-done.32.refs_1_ = bf16[128,768]{1,0:T(8,128)(2,1)S(1)} collective-permute-done((bf16[128,768]{1,0:T(8,128)(2,1)S(1)}, bf16[128,768]{1,0:T(8,128)(2,1)S(1)}, u32[]{:S(2)}, u32[]{:S(2)}) %collective-permute-start.32) | collective-permute-done | bytes 196640 | tf_op jit(solution)/shard_map/ppermute | solution.py:271
  219.5 2.7 %collective-permute-start.34 = (bf16[128,768]{1,0:T(8,128)(2,1)S(1)}, bf16[128,768]{1,0:T(8,128)(2,1)S(1)}, u32[]{:S(2)}, u32[]{:S(2)}) collective-permute-start(bf16[128,768]{1,0:T(8,128)(2,1)S(1)} %add_piece.8), channel_id=1, source_target_pairs={{0,4},{1,5},{2,6},{3,7},{4,8},{5,9},{6,10},{7,11},{8,12},{9,13},{1... | collective-permute-start | bytes 589832 | tf_op jit(solution)/shard_map/ppermute | solution.py:271
  223.2 2.0 collective-permute-start.38
  225.2 1.8 collective-permute-done.34.refs_2_
  227.9 2.9 %collective-permute-start.42 = (bf16[128,512]{1,0:T(8,128)(2,1)S(1)}, bf16[128,512]{1,0:T(8,128)(2,1)S(1)}, u32[]{:S(2)}, u32[]{:S(2)}) collective-permute-start(bf16[128,512]{1,0:T(8,128)(2,1)S(1)} %get-tuple-element.175), channel_id=1, source_target_pairs={{0,12},{1,13},{2,14},{3,15},{4,0},{5,1},{6,2},{7,3},{8,4},{9,5},{1... | collective-permute-start | bytes 393224 | tf_op jit(solution)/shard_map/ppermute | solution.py:271
  230.8 3.1 %collective-permute-done.40.refs_7_ = bf16[128,512]{1,0:T(8,128)(2,1)S(1)} collective-permute-done((bf16[128,512]{1,0:T(8,128)(2,1)S(1)}, bf16[128,512]{1,0:T(8,128)(2,1)S(1)}, u32[]{:S(2)}, u32[]{:S(2)}) %collective-permute-start.40) | collective-permute-done | bytes 131104 | tf_op jit(solution)/shard_map/ppermute | solution.py:271
  234.0 2.6 %collective-permute-done.41.refs_8_ = bf16[128,512]{1,0:T(8,128)(2,1)S(1)} collective-permute-done((bf16[128,512]{1,0:T(8,128)(2,1)S(1)}, bf16[128,512]{1,0:T(8,128)(2,1)S(1)}, u32[]{:S(2)}, u32[]{:S(2)}) %collective-permute-start.41) | collective-permute-done | bytes 131104 | tf_op jit(solution)/shard_map/ppermute | solution.py:271
  236.6 1.1 finish.3
  (89 shorter events, 11.3 us)
Async XLA Ops:
  2.8 75.7 %copy-start.8 = (bf16[128,2176]{1,0:T(8,128)(2,1)}, bf16[128,2176]{1,0:T(8,128)(2,1)S(1)}, u32[]{:S(2)}) copy-start(bf16[128,2176]{1,0:T(8,128)(2,1)S(1)} %concatenate.3.refs_0_) | copy-start | bytes 1671172
  2.8 18.6 %collective-permute-start.3 = (bf16[128,2176]{1,0:T(8,128)(2,1)S(1)}, bf16[128,2176]{1,0:T(8,128)(2,1)S(1)}, u32[]{:S(2)}, u32[]{:S(2)}) collective-permute-start(bf16[128,2176]{1,0:T(8,128)(2,1)S(1)} %concatenate.3.refs_0_), channel_id=1, source_target_pairs={{0,4},{1,5},{2,6},{3,7},{4,8},{5,9},{6,10},{7,11},{8,12},{9,13},{1... | collective-permute-start | bytes 1671176 | tf_op jit(solution)/shard_map/ppermute | solution.py:271
  5.9 15.1 %collective-permute-start.6 = (bf16[128,2048]{1,0:T(8,128)(2,1)}, bf16[128,2048]{1,0:T(8,128)(2,1)S(1)}, u32[]{:S(2)}, u32[]{:S(2)}) collective-permute-start(bf16[128,2048]{1,0:T(8,128)(2,1)} %refs_3_), channel_id=1, source_target_pairs={{0,2},{1,3},{2,0},{3,1},{4,6},{5,7},{6,4},{7,5},{8,10},{9,11},{10,... | collective-permute-start | bytes 1572872 | tf_op jit(solution)/shard_map/ppermute | solution.py:271
  7.4 67.5 %collective-permute-start.8 = (bf16[2,2048,256]{2,1,0:T(8,128)(2,1)}, bf16[2,2048,256]{2,1,0:T(8,128)(2,1)}, u32[]{:S(2)}, u32[]{:S(2)}) collective-permute-start(bf16[2,2048,256]{2,1,0:T(8,128)(2,1)} %refs_0_.5), channel_id=1, source_target_pairs={{0,1},{1,0},{2,3},{3,2},{4,5},{5,4},{6,7},{7,6},{8,9},{9,8},{10,11... | collective-permute-start | bytes 6291464 | tf_op jit(solution)/shard_map/ppermute | solution.py:271
  8.9 23.6 %collective-permute-start = (bf16[128,2176]{1,0:T(8,128)(2,1)S(1)}, bf16[128,2176]{1,0:T(8,128)(2,1)S(1)}, u32[]{:S(2)}, u32[]{:S(2)}) collective-permute-start(bf16[128,2176]{1,0:T(8,128)(2,1)S(1)} %concatenate.3.refs_0_), channel_id=1, source_target_pairs={{0,12},{1,13},{2,14},{3,15},{4,0},{5,1},{6,2},{7,3},{8,4},{9,5},{1... | collective-permute-start | bytes 1671176 | tf_op jit(solution)/shard_map/ppermute | solution.py:271
  11.2 21.3 %collective-permute-start.1 = (bf16[128,2176]{1,0:T(8,128)(2,1)S(1)}, bf16[128,2176]{1,0:T(8,128)(2,1)S(1)}, u32[]{:S(2)}, u32[]{:S(2)}) collective-permute-start(bf16[128,2176]{1,0:T(8,128)(2,1)S(1)} %concatenate.3.refs_0_), channel_id=1, source_target_pairs={{0,2},{1,3},{2,0},{3,1},{4,6},{5,7},{6,4},{7,5},{8,10},{9,11},{10,... | collective-permute-start | bytes 1671176 | tf_op jit(solution)/shard_map/ppermute | solution.py:271
  21.4 57.1 %copy-start.9 = (bf16[128,2176]{1,0:T(8,128)(2,1)}, bf16[128,2176]{1,0:T(8,128)(2,1)S(1)}, u32[]{:S(2)}) copy-start(bf16[128,2176]{1,0:T(8,128)(2,1)S(1)} %collective-permute-done.3.refs_3_) | copy-start | bytes 1671172
  21.4 79.8 %collective-permute-start.9 = (bf16[2,2048,256]{2,1,0:T(8,128)(2,1)}, bf16[2,2048,256]{2,1,0:T(8,128)(2,1)}, u32[]{:S(2)}, u32[]{:S(2)}) collective-permute-start(bf16[2,2048,256]{2,1,0:T(8,128)(2,1)} %refs_1_.5), channel_id=1, source_target_pairs={{0,1},{1,0},{2,3},{3,2},{4,5},{5,4},{6,7},{7,6},{8,9},{9,8},{10,11... | collective-permute-start | bytes 6291464 | tf_op jit(solution)/shard_map/ppermute | solution.py:271
  32.5 46.0 %copy-start.10 = (bf16[128,2176]{1,0:T(8,128)(2,1)}, bf16[128,2176]{1,0:T(8,128)(2,1)S(1)}, u32[]{:S(2)}) copy-start(bf16[128,2176]{1,0:T(8,128)(2,1)S(1)} %collective-permute-done.refs_1_) | copy-start | bytes 1671172
  32.5 38.5 %copy-start.11 = (bf16[128,2176]{1,0:T(8,128)(2,1)}, bf16[128,2176]{1,0:T(8,128)(2,1)S(1)}, u32[]{:S(2)}) copy-start(bf16[128,2176]{1,0:T(8,128)(2,1)S(1)} %collective-permute-done.1.refs_4_) | copy-start | bytes 1671172
  32.5 15.5 %collective-permute-start.4 = (bf16[128,2176]{1,0:T(8,128)(2,1)S(1)}, bf16[128,2176]{1,0:T(8,128)(2,1)S(1)}, u32[]{:S(2)}, u32[]{:S(2)}) collective-permute-start(bf16[128,2176]{1,0:T(8,128)(2,1)S(1)} %collective-permute-done.refs_1_), channel_id=1, source_target_pairs={{0,2},{1,3},{2,0},{3,1},{4,6},{5,7},{6,4},{7,5},{8,10},{9,11},{10,... | collective-permute-start | bytes 1671176 | tf_op jit(solution)/shard_map/ppermute | solution.py:271
  34.1 14.3 %collective-permute-start.2 = (bf16[128,2176]{1,0:T(8,128)(2,1)S(1)}, bf16[128,2176]{1,0:T(8,128)(2,1)S(1)}, u32[]{:S(2)}, u32[]{:S(2)}) collective-permute-start(bf16[128,2176]{1,0:T(8,128)(2,1)S(1)} %collective-permute-done.refs_1_), channel_id=1, source_target_pairs={{0,12},{1,13},{2,14},{3,15},{4,0},{5,1},{6,2},{7,3},{8,4},{9,5},{1... | collective-permute-start | bytes 1671176 | tf_op jit(solution)/shard_map/ppermute | solution.py:271
  37.3 22.6 %collective-permute-start.7 = (bf16[128,2176]{1,0:T(8,128)(2,1)S(1)}, bf16[128,2176]{1,0:T(8,128)(2,1)S(1)}, u32[]{:S(2)}, u32[]{:S(2)}) collective-permute-start(bf16[128,2176]{1,0:T(8,128)(2,1)S(1)} %collective-permute-done.3.refs_3_), channel_id=1, source_target_pairs={{0,2},{1,3},{2,0},{3,1},{4,6},{5,7},{6,4},{7,5},{8,10},{9,11},{10,... | collective-permute-start | bytes 1671176 | tf_op jit(solution)/shard_map/ppermute | solution.py:271
  48.0 23.5 %copy-start.12 = (bf16[128,2176]{1,0:T(8,128)(2,1)}, bf16[128,2176]{1,0:T(8,128)(2,1)S(1)}, u32[]{:S(2)}) copy-start(bf16[128,2176]{1,0:T(8,128)(2,1)S(1)} %collective-permute-done.4.refs_5_) | copy-start | bytes 1671172
  48.4 24.6 %copy-start.13 = (bf16[128,2176]{1,0:T(8,128)(2,1)}, bf16[128,2176]{1,0:T(8,128)(2,1)S(1)}, u32[]{:S(2)}) copy-start(bf16[128,2176]{1,0:T(8,128)(2,1)S(1)} %collective-permute-done.2.refs_2_) | copy-start | bytes 1671172
  48.4 22.6 %collective-permute-start.5 = (bf16[128,2176]{1,0:T(8,128)(2,1)S(1)}, bf16[128,2176]{1,0:T(8,128)(2,1)S(1)}, u32[]{:S(2)}, u32[]{:S(2)}) collective-permute-start(bf16[128,2176]{1,0:T(8,128)(2,1)S(1)} %collective-permute-done.2.refs_2_), channel_id=1, source_target_pairs={{0,2},{1,3},{2,0},{3,1},{4,6},{5,7},{6,4},{7,5},{8,10},{9,11},{10,... | collective-permute-start | bytes 1671176 | tf_op jit(solution)/shard_map/ppermute | solution.py:271
  49.6 12.2 %collective-permute-start.11 = (bf16[128,2048]{1,0:T(8,128)(2,1)}, bf16[128,2048]{1,0:T(8,128)(2,1)S(1)}, u32[]{:S(2)}, u32[]{:S(2)}) collective-permute-start(bf16[128,2048]{1,0:T(8,128)(2,1)} %refs_3_), channel_id=1, source_target_pairs={{0,12},{1,13},{2,14},{3,15},{4,0},{5,1},{6,2},{7,3},{8,4},{9,5},{1... | collective-permute-start | bytes 1572872 | tf_op jit(solution)/shard_map/ppermute | solution.py:271
  60.0 13.0 %copy-start.14 = (bf16[128,2176]{1,0:T(8,128)(2,1)}, bf16[128,2176]{1,0:T(8,128)(2,1)S(1)}, u32[]{:S(2)}) copy-start(bf16[128,2176]{1,0:T(8,128)(2,1)S(1)} %collective-permute-done.7.refs_7_) | copy-start | bytes 1671172
  60.0 17.0 %collective-permute-start.13 = (bf16[128,2048]{1,0:T(8,128)(2,1)}, bf16[128,2048]{1,0:T(8,128)(2,1)}, u32[]{:S(2)}, u32[]{:S(2)}) collective-permute-start(bf16[128,2048]{1,0:T(8,128)(2,1)} %refs_3_), channel_id=1, source_target_pairs={{0,4},{1,5},{2,6},{3,7},{4,8},{5,9},{6,10},{7,11},{8,12},{9,13},{1... | collective-permute-start | bytes 1572872 | tf_op jit(solution)/shard_map/ppermute | solution.py:271
  71.0 2.0 copy-start.15
  71.0 17.5 %collective-permute-start.15 = (bf16[128,2048]{1,0:T(8,128)(2,1)S(1)}, bf16[128,2048]{1,0:T(8,128)(2,1)}, u32[]{:S(2)}, u32[]{:S(2)}) collective-permute-start(bf16[128,2048]{1,0:T(8,128)(2,1)S(1)} %collective-permute-done.11.refs_3_.refs_4_), channel_id=1, source_target_pairs={{0,12},{1,13},{2,14},{3,15},{4,0},{5,1},{6,2},{7,3},{8,4},{9,5},{1... | collective-permute-start | bytes 1572872 | tf_op jit(solution)/shard_map/ppermute | solution.py:271
  71.5 17.0 %collective-permute-start.12 = (bf16[128,2048]{1,0:T(8,128)(2,1)S(1)}, bf16[128,2048]{1,0:T(8,128)(2,1)}, u32[]{:S(2)}, u32[]{:S(2)}) collective-permute-start(bf16[128,2048]{1,0:T(8,128)(2,1)S(1)} %collective-permute-done.11.refs_3_.refs_4_), channel_id=1, source_target_pairs={{0,2},{1,3},{2,0},{3,1},{4,6},{5,7},{6,4},{7,5},{8,10},{9,11},{10,... | collective-permute-start | bytes 1572872 | tf_op jit(solution)/shard_map/ppermute | solution.py:271
  74.9 36.4 %collective-permute-start.10 = (bf16[512,512]{1,0:T(8,128)(2,1)}, bf16[512,512]{1,0:T(8,128)(2,1)}, u32[]{:S(2)}, u32[]{:S(2)}) collective-permute-start(bf16[512,512]{1,0:T(8,128)(2,1)} %slice.12), channel_id=1, source_target_pairs={{0,1},{1,0},{2,3},{3,2},{4,5},{5,4},{6,7},{7,6},{8,9},{9,8},{10,11... | collective-permute-start | bytes 1572872 | tf_op jit(solution)/shard_map/ppermute | solution.py:271
  77.0 36.0 %collective-permute-start.14 = (bf16[128,2048]{1,0:T(8,128)(2,1)}, bf16[128,2048]{1,0:T(8,128)(2,1)}, u32[]{:S(2)}, u32[]{:S(2)}) collective-permute-start(bf16[128,2048]{1,0:T(8,128)(2,1)} %collective-permute-done.13.refs_5_.refs_6_), channel_id=1, source_target_pairs={{0,2},{1,3},{2,0},{3,1},{4,6},{5,7},{6,4},{7,5},{8,10},{9,11},{10,... | collective-permute-start | bytes 1572872 | tf_op jit(solution)/shard_map/ppermute | solution.py:271
  78.5 10.6 %copy-start = (bf16[2,256,2048]{2,1,0:T(8,128)(2,1)S(1)}, bf16[2,256,2048]{2,1,0:T(8,128)(2,1)}, u32[]{:S(2)}) copy-start(bf16[2,256,2048]{2,1,0:T(8,128)(2,1)} %param.13) | copy-start | bytes 6291460
  88.5 24.4 %collective-permute-start.16 = (bf16[128,2048]{1,0:T(8,128)(2,1)}, bf16[128,2048]{1,0:T(8,128)(2,1)}, u32[]{:S(2)}, u32[]{:S(2)}) collective-permute-start(bf16[128,2048]{1,0:T(8,128)(2,1)} %collective-permute-done.15.refs_4_.refs_5_), channel_id=1, source_target_pairs={{0,2},{1,3},{2,0},{3,1},{4,6},{5,7},{6,4},{7,5},{8,10},{9,11},{10,... | collective-permute-start | bytes 1572872 | tf_op jit(solution)/shard_map/ppermute | solution.py:271
  101.2 10.1 %copy-start.16 = (bf16[512,768]{1,0:T(8,128)(2,1)S(1)}, bf16[512,768]{1,0:T(8,128)(2,1)}, u32[]{:S(2)}) copy-start(bf16[512,768]{1,0:T(8,128)(2,1)} %get-tuple-element.109) | copy-start | bytes 2359300
  101.2 11.7 %copy-start.3 = (bf16[1024,512]{1,0:T(8,128)(2,1)S(1)}, bf16[1024,512]{1,0:T(8,128)(2,1)}, u32[]{:S(2)}) copy-start(bf16[1024,512]{1,0:T(8,128)(2,1)} %get-tuple-element.96.own_ref) | copy-start | bytes 3145732
  111.4 20.5 %collective-permute-start.17 = (bf16[512,768]{1,0:T(8,128)(2,1)S(1)}, bf16[512,768]{1,0:T(8,128)(2,1)S(1)}, u32[]{:S(2)}, u32[]{:S(2)}) collective-permute-start(bf16[512,768]{1,0:T(8,128)(2,1)S(1)} %copy-done.16), channel_id=1, source_target_pairs={{0,1},{1,0},{2,3},{3,2},{4,5},{5,4},{6,7},{7,6},{8,9},{9,8},{10,11... | collective-permute-start | bytes 2359304 | tf_op jit(solution)/shard_map/ppermute | solution.py:271
  112.9 1.2 copy-start.4
  114.1 3.9 %copy-start.5 = (bf16[128,2048]{1,0:T(8,128)(2,1)S(1)}, bf16[128,2048]{1,0:T(8,128)(2,1)}, u32[]{:S(2)}) copy-start(bf16[128,2048]{1,0:T(8,128)(2,1)} %refs_3_) | copy-start | bytes 1572868
  114.2 3.9 %copy-start.7 = (f32[1024,1024]{1,0:T(8,128)S(1)}, f32[1024,1024]{1,0:T(8,128)}, u32[]{:S(2)}) copy-start(f32[1024,1024]{1,0:T(8,128)} %get-tuple-element.111.refs_0_) | copy-start | bytes 12582916
  117.0 21.8 %collective-permute-start.18 = (bf16[512,512]{1,0:T(8,128)(2,1)S(1)}, bf16[512,512]{1,0:T(8,128)(2,1)S(1)}, u32[]{:S(2)}, u32[]{:S(2)}) collective-permute-start(bf16[512,512]{1,0:T(8,128)(2,1)S(1)} %get-tuple-element.115), channel_id=1, source_target_pairs={{0,2},{1,3},{2,0},{3,1},{4,6},{5,7},{6,4},{7,5},{8,10},{9,11},{10,... | collective-permute-start | bytes 1572872 | tf_op jit(solution)/shard_map/ppermute | solution.py:271
  117.5 30.4 %collective-permute-start.22 = (bf16[512,768]{1,0:T(8,128)(2,1)}, bf16[512,768]{1,0:T(8,128)(2,1)S(1)}, u32[]{:S(2)}, u32[]{:S(2)}) collective-permute-start(bf16[512,768]{1,0:T(8,128)(2,1)} %get-tuple-element.126), channel_id=1, source_target_pairs={{0,1},{1,0},{2,3},{3,2},{4,5},{5,4},{6,7},{7,6},{8,9},{9,8},{10,11... | collective-permute-start | bytes 2359304 | tf_op jit(solution)/shard_map/ppermute | solution.py:271
  134.1 27.9 %collective-permute-start.23 = (bf16[512,768]{1,0:T(8,128)(2,1)S(1)}, bf16[512,768]{1,0:T(8,128)(2,1)S(1)}, u32[]{:S(2)}, u32[]{:S(2)}) collective-permute-start(bf16[512,768]{1,0:T(8,128)(2,1)S(1)} %get-tuple-element.113), channel_id=1, source_target_pairs={{0,2},{1,3},{2,0},{3,1},{4,6},{5,7},{6,4},{7,5},{8,10},{9,11},{10,... | collective-permute-start | bytes 2359304 | tf_op jit(solution)/shard_map/ppermute | solution.py:271
  138.8 7.3 %collective-permute-start.20 = (bf16[128,512]{1,0:T(8,128)(2,1)S(1)}, bf16[128,512]{1,0:T(8,128)(2,1)S(1)}, u32[]{:S(2)}, u32[]{:S(2)}) collective-permute-start(bf16[128,512]{1,0:T(8,128)(2,1)S(1)} %get-tuple-element.122), channel_id=1, source_target_pairs={{0,4},{1,5},{2,6},{3,7},{4,8},{5,9},{6,10},{7,11},{8,12},{9,13},{1... | collective-permute-start | bytes 393224 | tf_op jit(solution)/shard_map/ppermute | solution.py:271
  140.5 6.9 %collective-permute-start.19 = (bf16[128,512]{1,0:T(8,128)(2,1)S(1)}, bf16[128,512]{1,0:T(8,128)(2,1)S(1)}, u32[]{:S(2)}, u32[]{:S(2)}) collective-permute-start(bf16[128,512]{1,0:T(8,128)(2,1)S(1)} %get-tuple-element.119), channel_id=1, source_target_pairs={{0,12},{1,13},{2,14},{3,15},{4,0},{5,1},{6,2},{7,3},{8,4},{9,5},{1... | collective-permute-start | bytes 393224 | tf_op jit(solution)/shard_map/ppermute | solution.py:271
  146.2 13.1 %copy-start.6 = (f32[1024,1024]{1,0:T(8,128)S(1)}, f32[1024,1024]{1,0:T(8,128)}, u32[]{:S(2)}) copy-start(f32[1024,1024]{1,0:T(8,128)} %get-tuple-element.129.refs_0_) | copy-start | bytes 12582916
  147.4 7.9 %collective-permute-start.21 = (bf16[128,512]{1,0:T(8,128)(2,1)S(1)}, bf16[128,512]{1,0:T(8,128)(2,1)S(1)}, u32[]{:S(2)}, u32[]{:S(2)}) collective-permute-start(bf16[128,512]{1,0:T(8,128)(2,1)S(1)} %add_piece.5), channel_id=1, source_target_pairs={{0,4},{1,5},{2,6},{3,7},{4,8},{5,9},{6,10},{7,11},{8,12},{9,13},{1... | collective-permute-start | bytes 393224 | tf_op jit(solution)/shard_map/ppermute | solution.py:271
  157.5 23.7 %collective-permute-start.27 = (bf16[512,768]{1,0:T(8,128)(2,1)S(1)}, bf16[512,768]{1,0:T(8,128)(2,1)S(1)}, u32[]{:S(2)}, u32[]{:S(2)}) collective-permute-start(bf16[512,768]{1,0:T(8,128)(2,1)S(1)} %get-tuple-element.137), channel_id=1, source_target_pairs={{0,2},{1,3},{2,0},{3,1},{4,6},{5,7},{6,4},{7,5},{8,10},{9,11},{10,... | collective-permute-start | bytes 2359304 | tf_op jit(solution)/shard_map/ppermute | solution.py:271
  159.3 10.8 %copy-start.2 = (bf16[2,2048,256]{2,1,0:T(8,128)(2,1)S(1)}, bf16[2,2048,256]{2,1,0:T(8,128)(2,1)}, u32[]{:S(2)}) copy-start(bf16[2,2048,256]{2,1,0:T(8,128)(2,1)} %refs_1_.5) | copy-start | bytes 6291460
  162.1 8.0 %copy-start.1 = (bf16[2,2048,256]{2,1,0:T(8,128)(2,1)S(1)}, bf16[2,2048,256]{2,1,0:T(8,128)(2,1)}, u32[]{:S(2)}) copy-start(bf16[2,2048,256]{2,1,0:T(8,128)(2,1)} %refs_0_.5) | copy-start | bytes 6291460
  162.2 5.7 %collective-permute-start.24 = (bf16[128,768]{1,0:T(8,128)(2,1)S(1)}, bf16[128,768]{1,0:T(8,128)(2,1)S(1)}, u32[]{:S(2)}, u32[]{:S(2)}) collective-permute-start(bf16[128,768]{1,0:T(8,128)(2,1)S(1)} %get-tuple-element.132), channel_id=1, source_target_pairs={{0,12},{1,13},{2,14},{3,15},{4,0},{5,1},{6,2},{7,3},{8,4},{9,5},{1... | collective-permute-start | bytes 589832 | tf_op jit(solution)/shard_map/ppermute | solution.py:271
  162.3 7.8 %collective-permute-start.25 = (bf16[128,768]{1,0:T(8,128)(2,1)S(1)}, bf16[128,768]{1,0:T(8,128)(2,1)S(1)}, u32[]{:S(2)}, u32[]{:S(2)}) collective-permute-start(bf16[128,768]{1,0:T(8,128)(2,1)S(1)} %get-tuple-element.134), channel_id=1, source_target_pairs={{0,4},{1,5},{2,6},{3,7},{4,8},{5,9},{6,10},{7,11},{8,12},{9,13},{1... | collective-permute-start | bytes 589832 | tf_op jit(solution)/shard_map/ppermute | solution.py:271
  175.4 21.4 %collective-permute-start.31 = (bf16[512,768]{1,0:T(8,128)(2,1)S(1)}, bf16[512,768]{1,0:T(8,128)(2,1)S(1)}, u32[]{:S(2)}, u32[]{:S(2)}) collective-permute-start(bf16[512,768]{1,0:T(8,128)(2,1)S(1)} %get-tuple-element.149), channel_id=1, source_target_pairs={{0,2},{1,3},{2,0},{3,1},{4,6},{5,7},{6,4},{7,5},{8,10},{9,11},{10,... | collective-permute-start | bytes 2359304 | tf_op jit(solution)/shard_map/ppermute | solution.py:271
  181.3 28.5 %collective-permute-start.35 = (bf16[512,768]{1,0:T(8,128)(2,1)S(1)}, bf16[512,768]{1,0:T(8,128)(2,1)S(1)}, u32[]{:S(2)}, u32[]{:S(2)}) collective-permute-start(bf16[512,768]{1,0:T(8,128)(2,1)S(1)} %get-tuple-element.159), channel_id=1, source_target_pairs={{0,2},{1,3},{2,0},{3,1},{4,6},{5,7},{6,4},{7,5},{8,10},{9,11},{10,... | collective-permute-start | bytes 2359304 | tf_op jit(solution)/shard_map/ppermute | solution.py:271
  183.1 9.7 %collective-permute-start.29 = (bf16[128,768]{1,0:T(8,128)(2,1)S(1)}, bf16[128,768]{1,0:T(8,128)(2,1)S(1)}, u32[]{:S(2)}, u32[]{:S(2)}) collective-permute-start(bf16[128,768]{1,0:T(8,128)(2,1)S(1)} %get-tuple-element.141), channel_id=1, source_target_pairs={{0,4},{1,5},{2,6},{3,7},{4,8},{5,9},{6,10},{7,11},{8,12},{9,13},{1... | collective-permute-start | bytes 589832 | tf_op jit(solution)/shard_map/ppermute | solution.py:271
  183.2 14.2 %collective-permute-start.26 = (bf16[128,768]{1,0:T(8,128)(2,1)S(1)}, bf16[128,768]{1,0:T(8,128)(2,1)S(1)}, u32[]{:S(2)}, u32[]{:S(2)}) collective-permute-start(bf16[128,768]{1,0:T(8,128)(2,1)S(1)} %add_piece.6), channel_id=1, source_target_pairs={{0,4},{1,5},{2,6},{3,7},{4,8},{5,9},{6,10},{7,11},{8,12},{9,13},{1... | collective-permute-start | bytes 589832 | tf_op jit(solution)/shard_map/ppermute | solution.py:271
  184.7 14.3 %collective-permute-start.28 = (bf16[128,768]{1,0:T(8,128)(2,1)S(1)}, bf16[128,768]{1,0:T(8,128)(2,1)S(1)}, u32[]{:S(2)}, u32[]{:S(2)}) collective-permute-start(bf16[128,768]{1,0:T(8,128)(2,1)S(1)} %get-tuple-element.139), channel_id=1, source_target_pairs={{0,12},{1,13},{2,14},{3,15},{4,0},{5,1},{6,2},{7,3},{8,4},{9,5},{1... | collective-permute-start | bytes 589832 | tf_op jit(solution)/shard_map/ppermute | solution.py:271
  197.0 28.1 %collective-permute-start.39 = (bf16[512,512]{1,0:T(8,128)(2,1)S(1)}, bf16[512,512]{1,0:T(8,128)(2,1)S(1)}, u32[]{:S(2)}, u32[]{:S(2)}) collective-permute-start(bf16[512,512]{1,0:T(8,128)(2,1)S(1)} %get-tuple-element.167), channel_id=1, source_target_pairs={{0,2},{1,3},{2,0},{3,1},{4,6},{5,7},{6,4},{7,5},{8,10},{9,11},{10,... | collective-permute-start | bytes 1572872 | tf_op jit(solution)/shard_map/ppermute | solution.py:271
  198.9 9.8 %collective-permute-start.30 = (bf16[128,768]{1,0:T(8,128)(2,1)S(1)}, bf16[128,768]{1,0:T(8,128)(2,1)S(1)}, u32[]{:S(2)}, u32[]{:S(2)}) collective-permute-start(bf16[128,768]{1,0:T(8,128)(2,1)S(1)} %add_piece.7), channel_id=1, source_target_pairs={{0,4},{1,5},{2,6},{3,7},{4,8},{5,9},{6,10},{7,11},{8,12},{9,13},{1... | collective-permute-start | bytes 589832 | tf_op jit(solution)/shard_map/ppermute | solution.py:271
  201.2 11.5 %collective-permute-start.33 = (bf16[128,768]{1,0:T(8,128)(2,1)S(1)}, bf16[128,768]{1,0:T(8,128)(2,1)S(1)}, u32[]{:S(2)}, u32[]{:S(2)}) collective-permute-start(bf16[128,768]{1,0:T(8,128)(2,1)S(1)} %get-tuple-element.153), channel_id=1, source_target_pairs={{0,4},{1,5},{2,6},{3,7},{4,8},{5,9},{6,10},{7,11},{8,12},{9,13},{1... | collective-permute-start | bytes 589832 | tf_op jit(solution)/shard_map/ppermute | solution.py:271
  201.7 17.8 %collective-permute-start.32 = (bf16[128,768]{1,0:T(8,128)(2,1)S(1)}, bf16[128,768]{1,0:T(8,128)(2,1)S(1)}, u32[]{:S(2)}, u32[]{:S(2)}) collective-permute-start(bf16[128,768]{1,0:T(8,128)(2,1)S(1)} %get-tuple-element.151), channel_id=1, source_target_pairs={{0,12},{1,13},{2,14},{3,15},{4,0},{5,1},{6,2},{7,3},{8,4},{9,5},{1... | collective-permute-start | bytes 589832 | tf_op jit(solution)/shard_map/ppermute | solution.py:271
  212.9 9.3 %collective-permute-start.37 = (bf16[128,768]{1,0:T(8,128)(2,1)S(1)}, bf16[128,768]{1,0:T(8,128)(2,1)S(1)}, u32[]{:S(2)}, u32[]{:S(2)}) collective-permute-start(bf16[128,768]{1,0:T(8,128)(2,1)S(1)} %get-tuple-element.164), channel_id=1, source_target_pairs={{0,4},{1,5},{2,6},{3,7},{4,8},{5,9},{6,10},{7,11},{8,12},{9,13},{1... | collective-permute-start | bytes 589832 | tf_op jit(solution)/shard_map/ppermute | solution.py:271
  213.0 10.2 %collective-permute-start.36 = (bf16[128,768]{1,0:T(8,128)(2,1)S(1)}, bf16[128,768]{1,0:T(8,128)(2,1)S(1)}, u32[]{:S(2)}, u32[]{:S(2)}) collective-permute-start(bf16[128,768]{1,0:T(8,128)(2,1)S(1)} %get-tuple-element.162), channel_id=1, source_target_pairs={{0,12},{1,13},{2,14},{3,15},{4,0},{5,1},{6,2},{7,3},{8,4},{9,5},{1... | collective-permute-start | bytes 589832 | tf_op jit(solution)/shard_map/ppermute | solution.py:271
  219.5 7.5 %collective-permute-start.34 = (bf16[128,768]{1,0:T(8,128)(2,1)S(1)}, bf16[128,768]{1,0:T(8,128)(2,1)S(1)}, u32[]{:S(2)}, u32[]{:S(2)}) collective-permute-start(bf16[128,768]{1,0:T(8,128)(2,1)S(1)} %add_piece.8), channel_id=1, source_target_pairs={{0,4},{1,5},{2,6},{3,7},{4,8},{5,9},{6,10},{7,11},{8,12},{9,13},{1... | collective-permute-start | bytes 589832 | tf_op jit(solution)/shard_map/ppermute | solution.py:271
  223.2 7.7 %collective-permute-start.38 = (bf16[128,768]{1,0:T(8,128)(2,1)S(1)}, bf16[128,768]{1,0:T(8,128)(2,1)S(1)}, u32[]{:S(2)}, u32[]{:S(2)}) collective-permute-start(bf16[128,768]{1,0:T(8,128)(2,1)S(1)} %add_piece.9), channel_id=1, source_target_pairs={{0,4},{1,5},{2,6},{3,7},{4,8},{5,9},{6,10},{7,11},{8,12},{9,13},{1... | collective-permute-start | bytes 589832 | tf_op jit(solution)/shard_map/ppermute | solution.py:271
  227.0 7.0 %collective-permute-start.40 = (bf16[128,512]{1,0:T(8,128)(2,1)S(1)}, bf16[128,512]{1,0:T(8,128)(2,1)S(1)}, u32[]{:S(2)}, u32[]{:S(2)}) collective-permute-start(bf16[128,512]{1,0:T(8,128)(2,1)S(1)} %get-tuple-element.173), channel_id=1, source_target_pairs={{0,4},{1,5},{2,6},{3,7},{4,8},{5,9},{6,10},{7,11},{8,12},{9,13},{1... | collective-permute-start | bytes 393224 | tf_op jit(solution)/shard_map/ppermute | solution.py:271
  227.9 8.7 %collective-permute-start.41 = (bf16[128,512]{1,0:T(8,128)(2,1)S(1)}, bf16[128,512]{1,0:T(8,128)(2,1)S(1)}, u32[]{:S(2)}, u32[]{:S(2)}) collective-permute-start(bf16[128,512]{1,0:T(8,128)(2,1)S(1)} %get-tuple-element.174), channel_id=1, source_target_pairs={{0,8},{1,9},{2,10},{3,11},{4,12},{5,13},{6,14},{7,15},{8,0},{9,1},... | collective-permute-start | bytes 393224 | tf_op jit(solution)/shard_map/ppermute | solution.py:271
  227.9 8.7 %collective-permute-start.42 = (bf16[128,512]{1,0:T(8,128)(2,1)S(1)}, bf16[128,512]{1,0:T(8,128)(2,1)S(1)}, u32[]{:S(2)}, u32[]{:S(2)}) collective-permute-start(bf16[128,512]{1,0:T(8,128)(2,1)S(1)} %get-tuple-element.175), channel_id=1, source_target_pairs={{0,12},{1,13},{2,14},{3,15},{4,0},{5,1},{6,2},{7,3},{8,4},{9,5},{1... | collective-permute-start | bytes 393224 | tf_op jit(solution)/shard_map/ppermute | solution.py:271

commit v15 on v13

--- a/solution.py
+++ b/solution.py
@@ -370,11 +370,11 @@
     far_1, next_1 = send_on(pieces)
     near_1 = send_last(pieces, next_1, far_1)
 
-    keep_4, send = back(1, next_1, far_1)
-    own_2, *pieces = add_sides(after(keep_2, send), come_2, types)
-    (come_4,) = send_all([(send, side)], own_2)
+    own_2, *pieces = add_sides(keep_2, after(come_2, next_1, far_1), types)
     far_2, next_2 = send_on(pieces)
     near_2 = send_last(pieces, next_2, far_2, near_1)
+    keep_4, send = back(1, next_2, near_1)
+    (come_4,) = send_all([(send, side)], own_2)
 
     keep_5, send = back(2, next_2)
     own_3, *pieces = add_sides(after(keep_3, send), come_3, types)

time: 237 us -> 237 us (level)
  waiting for transfers between devices: 114 us -> 110 us
  starting transfers between devices: 59.6 us -> 63.1 us
    ppermute x43, waiting for transfers between devices: 114 us -> 110 us  [send_all(): lax.ppermute(v, 'expert', pairs)]
    ppermute x43, starting transfers between devices: 59.6 us -> 63.1 us  [send_all(): lax.ppermute(v, 'expert', pairs)]
where the time goes in v15:
time: 237 us; the launch traced here: 236 us
  waiting for transfers between devices  110 us (46%)
  starting transfers between devices  63.1 us (27%)
  Pallas kernels  55 us (23%)
  local copies, waits for them, and re-layouts  6.06 us (3%)
    ppermute x43, waiting for transfers between devices, send_all(): lax.ppermute(v, 'expert', pairs)  110 us
    ppermute x43, starting transfers between devices, send_all(): lax.ppermute(v, 'expert', pairs)  63.1 us
    pallas_call x6, Pallas kernels, sum_columns(): pl.pallas_call(kernel, grid=(2,), in_specs=[rows, rows] + weight_specs, o...  21.4 us
    pallas_call x2, Pallas kernels, hidden_forward(): pl.pallas_call(functools.partial(hidden_kernel, blocks, all_experts), gri...  20 us
    pallas_call x3, Pallas kernels, hidden_grads(): pl.pallas_call(functools.partial(grads_kernel, blocks, tuple(cuts), by is...  10.5 us
  transfers between devices with their start and end apart: 43, of which 25 were waited for; matrix products, arithmetic and copies ran while one was open for 1% of the time, Pallas kernels for 23%

profile of v15, /device:TPU:0, one launch (start us, length us, event | category | flops | bytes accessed | tf_op | source)
XLA Modules:
  0.0 236.2 jit_solution(14443776075128336354)
XLA Ops:
  0.6 0.7 select_reduce_fusion
  1.6 1.2 concatenate.3.refs_0_
  2.8 3.1 %collective-permute-start.3 = (bf16[128,2176]{1,0:T(8,128)(2,1)S(1)}, bf16[128,2176]{1,0:T(8,128)(2,1)S(1)}, u32[]{:S(2)}, u32[]{:S(2)}) collective-permute-start(bf16[128,2176]{1,0:T(8,128)(2,1)S(1)} %concatenate.3.refs_0_), channel_id=1, source_target_pairs={{0,4},{1,5},{2,6},{3,7},{4,8},{5,9},{6,10},{7,11},{8,12},{9,13},{1... | collective-permute-start | bytes 1671176 | tf_op jit(solution)/shard_map/ppermute | solution.py:271
  5.9 1.5 collective-permute-start.6
  7.4 1.5 collective-permute-start.8
  8.9 2.2 collective-permute-start
  11.7 9.3 %collective-permute-done.6.refs_6_.refs_7_ = bf16[128,2048]{1,0:T(8,128)(2,1)S(1)} collective-permute-done((bf16[128,2048]{1,0:T(8,128)(2,1)}, bf16[128,2048]{1,0:T(8,128)(2,1)S(1)}, u32[]{:S(2)}, u32[]{:S(2)}) %collective-permute-start.6) | collective-permute-done | bytes 524320 | tf_op jit(solution)/shard_map/ppermute | solution.py:271
  21.4 1.7 collective-permute-start.9
  23.2 9.3 %collective-permute-done.refs_1_ = bf16[128,2176]{1,0:T(8,128)(2,1)S(1)} collective-permute-done((bf16[128,2176]{1,0:T(8,128)(2,1)S(1)}, bf16[128,2176]{1,0:T(8,128)(2,1)S(1)}, u32[]{:S(2)}, u32[]{:S(2)}) %collective-permute-start) | collective-permute-done | bytes 557088 | tf_op jit(solution)/shard_map/ppermute | solution.py:271
  32.5 1.6 collective-permute-start.4
  34.1 3.3 %collective-permute-start.2 = (bf16[128,2176]{1,0:T(8,128)(2,1)S(1)}, bf16[128,2176]{1,0:T(8,128)(2,1)S(1)}, u32[]{:S(2)}, u32[]{:S(2)}) collective-permute-start(bf16[128,2176]{1,0:T(8,128)(2,1)S(1)} %collective-permute-done.refs_1_), channel_id=1, source_target_pairs={{0,12},{1,13},{2,14},{3,15},{4,0},{5,1},{6,2},{7,3},{8,4},{9,5},{1... | collective-permute-start | bytes 1671176 | tf_op jit(solution)/shard_map/ppermute | solution.py:271
  37.8 10.2 %collective-permute-done.4.refs_5_ = bf16[128,2176]{1,0:T(8,128)(2,1)S(1)} collective-permute-done((bf16[128,2176]{1,0:T(8,128)(2,1)S(1)}, bf16[128,2176]{1,0:T(8,128)(2,1)S(1)}, u32[]{:S(2)}, u32[]{:S(2)}) %collective-permute-start.4) | collective-permute-done | bytes 557088 | tf_op jit(solution)/shard_map/ppermute | solution.py:271
  48.3 1.4 collective-permute-start.5
  49.7 3.3 %collective-permute-start.11 = (bf16[128,2048]{1,0:T(8,128)(2,1)}, bf16[128,2048]{1,0:T(8,128)(2,1)S(1)}, u32[]{:S(2)}, u32[]{:S(2)}) collective-permute-start(bf16[128,2048]{1,0:T(8,128)(2,1)} %refs_3_), channel_id=1, source_target_pairs={{0,12},{1,13},{2,14},{3,15},{4,0},{5,1},{6,2},{7,3},{8,4},{9,5},{1... | collective-permute-start | bytes 1572872 | tf_op jit(solution)/shard_map/ppermute | solution.py:271
  53.0 7.0 %collective-permute-done.7.refs_7_ = bf16[128,2176]{1,0:T(8,128)(2,1)S(1)} collective-permute-done((bf16[128,2176]{1,0:T(8,128)(2,1)S(1)}, bf16[128,2176]{1,0:T(8,128)(2,1)S(1)}, u32[]{:S(2)}, u32[]{:S(2)}) %collective-permute-start.7) | collective-permute-done | bytes 557088 | tf_op jit(solution)/shard_map/ppermute | solution.py:271
  60.5 1.0 collective-permute-done.11.refs_3_.refs_4_
  61.5 9.4 %collective-permute-done.5.refs_6_ = bf16[128,2176]{1,0:T(8,128)(2,1)S(1)} collective-permute-done((bf16[128,2176]{1,0:T(8,128)(2,1)S(1)}, bf16[128,2176]{1,0:T(8,128)(2,1)S(1)}, u32[]{:S(2)}, u32[]{:S(2)}) %collective-permute-start.5) | collective-permute-done | bytes 557088 | tf_op jit(solution)/shard_map/ppermute | solution.py:271
  71.5 1.5 collective-permute-start.12
  73.0 1.9 slice.12
  74.9 1.5 collective-permute-start.10
  77.0 1.5 collective-permute-start.14
  78.5 10.1 %hidden_forward.2 = (bf16[1024,512]{1,0:T(8,128)(2,1)}, f32[1024,1024]{1,0:T(8,128)}) custom-call(s32[1]{0:T(128)} %bitcast.owner_ref, bf16[2,2048,256]{2,1,0:T(8,128)(2,1)} %refs_0_.5, bf16[2,2048,256]{2,1,0:T(8,128)(2,1)} %refs_1_.5, bf16[128,2176]{1,0:T(8,128)(2,1)} %copy-done.11, bf16[128,2176]{1,0:T(8,128)(2,1)} %copy-done.13, ...), custom_call_target="tpu_custom_call" | custom-call | flops 1 | bytes 1 | tf_op jit(solution)/shard_map/hidden_forward/pallas_call | solution.py:71
  89.2 1.0 fusion.1
  90.2 11.0 %collective-permute-done.9.up_ref.refs_3_ = bf16[2,2048,256]{2,1,0:T(8,128)(2,1)} collective-permute-done((bf16[2,2048,256]{2,1,0:T(8,128)(2,1)}, bf16[2,2048,256]{2,1,0:T(8,128)(2,1)}, u32[]{:S(2)}, u32[]{:S(2)}) %collective-permute-start.9) | collective-permute-done | bytes 2097184 | tf_op jit(solution)/shard_map/ppermute | solution.py:271
  101.2 9.9 %hidden_forward.3 = (bf16[1024,512]{1,0:T(8,128)(2,1)}, f32[1024,1024]{1,0:T(8,128)}) custom-call(s32[1]{0:T(128)} %bitcast.1.owner_ref, bf16[2,2048,256]{2,1,0:T(8,128)(2,1)} %copy-done.3, bf16[2,2048,256]{2,1,0:T(8,128)(2,1)} %collective-permute-done.9.up_ref.refs_3_, bf16[128,2176]{1,0:T(8,128)(2,1)} %copy-done.11, bf16[128,2176]{1,0:T(8,128)(2,1)} %copy-done.13, ...), custom_call_target="tpu_custom_call" | custom-call | flops 1 | bytes 1 | tf_op jit(solution)/shard_map/hidden_forward/pallas_call | solution.py:71
  111.2 1.6 collective-permute-start.17
  112.8 1.2 copy-done.6
  114.0 2.8 %mix_columns.3 = (f32[512,512]{1,0:T(8,128)S(1)}, bf16[512,512]{1,0:T(8,128)(2,1)S(1)}) custom-call(bf16[1024,512]{1,0:T(8,128)(2,1)S(1)} %copy-done.5, bf16[1024,512]{1,0:T(8,128)(2,1)S(1)} %copy-done.6, bf16[512,2048]{1,0:T(8,128)(2,1)S(1)} %bitcast.5, bf16[512,512]{1,0:T(8,128)(2,1)} %collective-permute-done.10.other_down_ref.refs_0_), custom_call_target="tpu_custom_call" | custom-call | flops 1 | bytes 1 | tf_op jit(solution)/shard_map/mix_columns/pallas_call | solution.py:179
  117.9 3.7 %hidden_grads.3.own_ref = bf16[1024,1024]{1,0:T(8,128)(2,1)S(1)} custom-call(f32[1024,1024]{1,0:T(8,128)S(1)} %copy-done.10, bf16[512,2048]{1,0:T(8,128)(2,1)S(1)} %bitcast.6, bf16[128,2048]{1,0:T(8,128)(2,1)S(1)} %copy-done.8, bf16[128,2048]{1,0:T(8,128)(2,1)S(1)} %collective-permute-done.11.refs_3_.refs_4_, ...), custom_call_target="tpu_custom_call" | custom-call | flops 1 | bytes 1 | tf_op jit(solution)/shard_map/hidden_grads/pallas_call | solution.py:127
  121.6 10.1 %collective-permute-done.17.other_down_ref.refs_1_ = bf16[512,768]{1,0:T(8,128)(2,1)S(1)} collective-permute-done((bf16[512,768]{1,0:T(8,128)(2,1)S(1)}, bf16[512,768]{1,0:T(8,128)(2,1)S(1)}, u32[]{:S(2)}, u32[]{:S(2)}) %collective-permute-start.17) | collective-permute-done | bytes 786464 | tf_op jit(solution)/shard_map/ppermute | solution.py:271
  131.7 2.2 mix_columns.4
  134.1 1.6 collective-permute-start.20
  135.7 2.2 collective-permute-start.19
  138.5 3.5 %collective-permute-done.20.come_ref = bf16[128,512]{1,0:T(8,128)(2,1)S(1)} collective-permute-done((bf16[128,512]{1,0:T(8,128)(2,1)S(1)}, bf16[128,512]{1,0:T(8,128)(2,1)S(1)}, u32[]{:S(2)}, u32[]{:S(2)}) %collective-permute-start.20) | collective-permute-done | bytes 131104 | tf_op jit(solution)/shard_map/ppermute | solution.py:271
  142.0 1.2 collective-permute-done.19.refs_1_
  143.8 4.0 %hidden_grads.4.refs_1_ = f32[1024,512]{1,0:T(8,128)S(1)} custom-call(bf16[512,512]{1,0:T(8,128)(2,1)} %collective-permute-done.10.other_down_ref.refs_0_, bf16[512,768]{1,0:T(8,128)(2,1)S(1)} %collective-permute-done.17.other_down_ref.refs_1_, bf16[128,2048]{1,0:T(8,128)(2,1)S(1)} %copy-done.8, ...), custom_call_target="tpu_custom_call" | custom-call | flops 1 | bytes 1 | tf_op jit(solution)/shard_map/hidden_grads/pallas_call | solution.py:127
  147.8 2.2 collective-permute-done.21.refs_2_
  150.0 2.2 mix_columns.5
  152.8 2.8 %hidden_grads.5.other_ref = bf16[1024,1024]{1,0:T(8,128)(2,1)S(1)} custom-call(f32[1024,1024]{1,0:T(8,128)S(1)} %copy-done.9, f32[1024,512]{1,0:T(8,128)S(1)} %hidden_grads.4.refs_1_, bf16[512,768]{1,0:T(8,128)(2,1)S(1)} %collective-permute-done.22.other_down_ref.refs_2_, bf16[128,2048]{1,0:T(8,128)(2,1)S(1)} %copy-done.8, ...), custom_call_target="tpu_custom_call" | custom-call | flops 1 | bytes 1 | tf_op jit(solution)/shard_map/hidden_grads/pallas_call | solution.py:127
  156.1 5.2 %back_columns.3 = (f32[512,768]{1,0:T(8,128)S(1)}, bf16[512,768]{1,0:T(8,128)(2,1)S(1)}) custom-call(bf16[1024,1024]{1,0:T(8,128)(2,1)S(1)} %hidden_grads.3.own_ref, bf16[1024,1024]{1,0:T(8,128)(2,1)S(1)} %hidden_grads.5.other_ref, bf16[2,2048,256]{2,1,0:T(8,128)(2,1)S(1)} %copy-done.1, bf16[2,2048,256]{2,1,0:T(8,128)(2,1)S(1)} %copy-done.2, ...), custom_call_target="tpu_custom_call" | custom-call | flops 1 | bytes 1 | tf_op jit(solution)/shard_map/back_columns/pallas_call | solution.py:179
  161.5 3.8 %collective-permute-start.24 = (bf16[128,768]{1,0:T(8,128)(2,1)S(1)}, bf16[128,768]{1,0:T(8,128)(2,1)S(1)}, u32[]{:S(2)}, u32[]{:S(2)}) collective-permute-start(bf16[128,768]{1,0:T(8,128)(2,1)S(1)} %get-tuple-element.129), channel_id=1, source_target_pairs={{0,12},{1,13},{2,14},{3,15},{4,0},{5,1},{6,2},{7,3},{8,4},{9,5},{1... | collective-permute-start | bytes 589832 | tf_op jit(solution)/shard_map/ppermute | solution.py:271
  165.3 1.5 collective-permute-start.31
  166.8 4.3 %collective-permute-done.25.come_ref = bf16[128,768]{1,0:T(8,128)(2,1)S(1)} collective-permute-done((bf16[128,768]{1,0:T(8,128)(2,1)S(1)}, bf16[128,768]{1,0:T(8,128)(2,1)S(1)}, u32[]{:S(2)}, u32[]{:S(2)}) %collective-permute-start.25) | collective-permute-done | bytes 196640 | tf_op jit(solution)/shard_map/ppermute | solution.py:271
  171.2 2.0 collective-permute-done.24.refs_4_
  173.4 2.7 %collective-permute-start.29 = (bf16[128,768]{1,0:T(8,128)(2,1)S(1)}, bf16[128,768]{1,0:T(8,128)(2,1)S(1)}, u32[]{:S(2)}, u32[]{:S(2)}) collective-permute-start(bf16[128,768]{1,0:T(8,128)(2,1)S(1)} %get-tuple-element.139), channel_id=1, source_target_pairs={{0,4},{1,5},{2,6},{3,7},{4,8},{5,9},{6,10},{7,11},{8,12},{9,13},{1... | collective-permute-start | bytes 589832 | tf_op jit(solution)/shard_map/ppermute | solution.py:271
  176.1 4.6 %collective-permute-done.26.refs_5_ = bf16[128,768]{1,0:T(8,128)(2,1)S(1)} collective-permute-done((bf16[128,768]{1,0:T(8,128)(2,1)S(1)}, bf16[128,768]{1,0:T(8,128)(2,1)S(1)}, u32[]{:S(2)}, u32[]{:S(2)}) %collective-permute-start.26) | collective-permute-done | bytes 196640 | tf_op jit(solution)/shard_map/ppermute | solution.py:271
  180.7 3.1 %collective-permute-done.29.come_ref = bf16[128,768]{1,0:T(8,128)(2,1)S(1)} collective-permute-done((bf16[128,768]{1,0:T(8,128)(2,1)S(1)}, bf16[128,768]{1,0:T(8,128)(2,1)S(1)}, u32[]{:S(2)}, u32[]{:S(2)}) %collective-permute-start.29) | collective-permute-done | bytes 196640 | tf_op jit(solution)/shard_map/ppermute | solution.py:271
  183.8 5.2 %back_columns.5 = (f32[512,768]{1,0:T(8,128)S(1)}, bf16[512,768]{1,0:T(8,128)(2,1)S(1)}) custom-call(bf16[1024,1024]{1,0:T(8,128)(2,1)S(1)} %hidden_grads.3.own_ref, bf16[1024,1024]{1,0:T(8,128)(2,1)S(1)} %hidden_grads.5.other_ref, bf16[2,2048,256]{2,1,0:T(8,128)(2,1)S(1)} %copy-done.1, bf16[2,2048,256]{2,1,0:T(8,128)(2,1)S(1)} %copy-done.2, ...), custom_call_target="tpu_custom_call" | custom-call | flops 1 | bytes 1 | tf_op jit(solution)/shard_map/back_columns/pallas_call | solution.py:179
  189.0 2.6 %collective-permute-start.35 = (bf16[512,768]{1,0:T(8,128)(2,1)S(1)}, bf16[512,768]{1,0:T(8,128)(2,1)S(1)}, u32[]{:S(2)}, u32[]{:S(2)}) collective-permute-start(bf16[512,768]{1,0:T(8,128)(2,1)S(1)} %get-tuple-element.155), channel_id=1, source_target_pairs={{0,2},{1,3},{2,0},{3,1},{4,6},{5,7},{6,4},{7,5},{8,10},{9,11},{10,... | collective-permute-start | bytes 2359304 | tf_op jit(solution)/shard_map/ppermute | solution.py:271
  191.7 3.9 %back_columns.4 = (f32[512,512]{1,0:T(8,128)S(1)}, bf16[512,512]{1,0:T(8,128)(2,1)S(1)}) custom-call(bf16[1024,1024]{1,0:T(8,128)(2,1)S(1)} %hidden_grads.3.own_ref, bf16[1024,1024]{1,0:T(8,128)(2,1)S(1)} %hidden_grads.5.other_ref, bf16[2,2048,256]{2,1,0:T(8,128)(2,1)S(1)} %copy-done.1, bf16[2,2048,256]{2,1,0:T(8,128)(2,1)S(1)} %copy-done.2, ...), custom_call_target="tpu_custom_call" | custom-call | flops 1 | bytes 1 | tf_op jit(solution)/shard_map/back_columns/pallas_call | solution.py:179
  195.9 1.6 collective-permute-done.28.refs_7_
  197.5 1.5 collective-permute-start.30
  199.0 3.8 %collective-permute-start.32 = (bf16[128,768]{1,0:T(8,128)(2,1)S(1)}, bf16[128,768]{1,0:T(8,128)(2,1)S(1)}, u32[]{:S(2)}, u32[]{:S(2)}) collective-permute-start(bf16[128,768]{1,0:T(8,128)(2,1)S(1)} %get-tuple-element.147), channel_id=1, source_target_pairs={{0,12},{1,13},{2,14},{3,15},{4,0},{5,1},{6,2},{7,3},{8,4},{9,5},{1... | collective-permute-start | bytes 589832 | tf_op jit(solution)/shard_map/ppermute | solution.py:271
  202.8 4.5 %collective-permute-done.30.refs_8_ = bf16[128,768]{1,0:T(8,128)(2,1)S(1)} collective-permute-done((bf16[128,768]{1,0:T(8,128)(2,1)S(1)}, bf16[128,768]{1,0:T(8,128)(2,1)S(1)}, u32[]{:S(2)}, u32[]{:S(2)}) %collective-permute-start.30) | collective-permute-done | bytes 196640 | tf_op jit(solution)/shard_map/ppermute | solution.py:271
  207.3 1.1 finish.2
  208.4 3.1 %collective-permute-done.33.come_ref = bf16[128,768]{1,0:T(8,128)(2,1)S(1)} collective-permute-done((bf16[128,768]{1,0:T(8,128)(2,1)S(1)}, bf16[128,768]{1,0:T(8,128)(2,1)S(1)}, u32[]{:S(2)}, u32[]{:S(2)}) %collective-permute-start.33) | collective-permute-done | bytes 196640 | tf_op jit(solution)/shard_map/ppermute | solution.py:271
  211.7 3.8 %collective-permute-start.36 = (bf16[128,768]{1,0:T(8,128)(2,1)S(1)}, bf16[128,768]{1,0:T(8,128)(2,1)S(1)}, u32[]{:S(2)}, u32[]{:S(2)}) collective-permute-start(bf16[128,768]{1,0:T(8,128)(2,1)S(1)} %get-tuple-element.158), channel_id=1, source_target_pairs={{0,12},{1,13},{2,14},{3,15},{4,0},{5,1},{6,2},{7,3},{8,4},{9,5},{1... | collective-permute-start | bytes 589832 | tf_op jit(solution)/shard_map/ppermute | solution.py:271
  215.6 5.5 %collective-permute-done.37.come_ref = bf16[128,768]{1,0:T(8,128)(2,1)S(1)} collective-permute-done((bf16[128,768]{1,0:T(8,128)(2,1)S(1)}, bf16[128,768]{1,0:T(8,128)(2,1)S(1)}, u32[]{:S(2)}, u32[]{:S(2)}) %collective-permute-start.37) | collective-permute-done | bytes 196640 | tf_op jit(solution)/shard_map/ppermute | solution.py:271
  221.2 1.0 collective-permute-done.36.refs_4_
  222.1 4.1 %collective-permute-start.38 = (bf16[128,768]{1,0:T(8,128)(2,1)S(1)}, bf16[128,768]{1,0:T(8,128)(2,1)S(1)}, u32[]{:S(2)}, u32[]{:S(2)}) collective-permute-start(bf16[128,768]{1,0:T(8,128)(2,1)S(1)} %add_piece.9), channel_id=1, source_target_pairs={{0,4},{1,5},{2,6},{3,7},{4,8},{5,9},{6,10},{7,11},{8,12},{9,13},{1... | collective-permute-start | bytes 589832 | tf_op jit(solution)/shard_map/ppermute | solution.py:271
  227.0 3.1 %collective-permute-start.42 = (bf16[128,512]{1,0:T(8,128)(2,1)S(1)}, bf16[128,512]{1,0:T(8,128)(2,1)S(1)}, u32[]{:S(2)}, u32[]{:S(2)}) collective-permute-start(bf16[128,512]{1,0:T(8,128)(2,1)S(1)} %get-tuple-element.171), channel_id=1, source_target_pairs={{0,12},{1,13},{2,14},{3,15},{4,0},{5,1},{6,2},{7,3},{8,4},{9,5},{1... | collective-permute-start | bytes 393224 | tf_op jit(solution)/shard_map/ppermute | solution.py:271
  230.2 3.1 %collective-permute-done.40.refs_7_ = bf16[128,512]{1,0:T(8,128)(2,1)S(1)} collective-permute-done((bf16[128,512]{1,0:T(8,128)(2,1)S(1)}, bf16[128,512]{1,0:T(8,128)(2,1)S(1)}, u32[]{:S(2)}, u32[]{:S(2)}) %collective-permute-start.40) | collective-permute-done | bytes 131104 | tf_op jit(solution)/shard_map/ppermute | solution.py:271
  233.3 1.8 collective-permute-done.41.refs_8_
  235.1 1.1 finish.3
  (93 shorter events, 9.5 us)
Async XLA Ops:
  2.8 45.5 %copy-start.11 = (bf16[128,2176]{1,0:T(8,128)(2,1)}, bf16[128,2176]{1,0:T(8,128)(2,1)S(1)}, u32[]{:S(2)}) copy-start(bf16[128,2176]{1,0:T(8,128)(2,1)S(1)} %concatenate.3.refs_0_) | copy-start | bytes 1671172
  2.8 18.6 %collective-permute-start.3 = (bf16[128,2176]{1,0:T(8,128)(2,1)S(1)}, bf16[128,2176]{1,0:T(8,128)(2,1)S(1)}, u32[]{:S(2)}, u32[]{:S(2)}) collective-permute-start(bf16[128,2176]{1,0:T(8,128)(2,1)S(1)} %concatenate.3.refs_0_), channel_id=1, source_target_pairs={{0,4},{1,5},{2,6},{3,7},{4,8},{5,9},{6,10},{7,11},{8,12},{9,13},{1... | collective-permute-start | bytes 1671176 | tf_op jit(solution)/shard_map/ppermute | solution.py:271
  5.9 15.1 %collective-permute-start.6 = (bf16[128,2048]{1,0:T(8,128)(2,1)}, bf16[128,2048]{1,0:T(8,128)(2,1)S(1)}, u32[]{:S(2)}, u32[]{:S(2)}) collective-permute-start(bf16[128,2048]{1,0:T(8,128)(2,1)} %refs_3_), channel_id=1, source_target_pairs={{0,2},{1,3},{2,0},{3,1},{4,6},{5,7},{6,4},{7,5},{8,10},{9,11},{10,... | collective-permute-start | bytes 1572872 | tf_op jit(solution)/shard_map/ppermute | solution.py:271
  7.4 67.5 %collective-permute-start.8 = (bf16[2,2048,256]{2,1,0:T(8,128)(2,1)}, bf16[2,2048,256]{2,1,0:T(8,128)(2,1)S(1)}, u32[]{:S(2)}, u32[]{:S(2)}) collective-permute-start(bf16[2,2048,256]{2,1,0:T(8,128)(2,1)} %refs_0_.5), channel_id=1, source_target_pairs={{0,1},{1,0},{2,3},{3,2},{4,5},{5,4},{6,7},{7,6},{8,9},{9,8},{10,11... | collective-permute-start | bytes 6291464 | tf_op jit(solution)/shard_map/ppermute | solution.py:271
  8.9 23.6 %collective-permute-start = (bf16[128,2176]{1,0:T(8,128)(2,1)S(1)}, bf16[128,2176]{1,0:T(8,128)(2,1)S(1)}, u32[]{:S(2)}, u32[]{:S(2)}) collective-permute-start(bf16[128,2176]{1,0:T(8,128)(2,1)S(1)} %concatenate.3.refs_0_), channel_id=1, source_target_pairs={{0,12},{1,13},{2,14},{3,15},{4,0},{5,1},{6,2},{7,3},{8,4},{9,5},{1... | collective-permute-start | bytes 1671176 | tf_op jit(solution)/shard_map/ppermute | solution.py:271
  11.2 21.3 %collective-permute-start.1 = (bf16[128,2176]{1,0:T(8,128)(2,1)S(1)}, bf16[128,2176]{1,0:T(8,128)(2,1)S(1)}, u32[]{:S(2)}, u32[]{:S(2)}) collective-permute-start(bf16[128,2176]{1,0:T(8,128)(2,1)S(1)} %concatenate.3.refs_0_), channel_id=1, source_target_pairs={{0,2},{1,3},{2,0},{3,1},{4,6},{5,7},{6,4},{7,5},{8,10},{9,11},{10,... | collective-permute-start | bytes 1671176 | tf_op jit(solution)/shard_map/ppermute | solution.py:271
  21.4 49.5 %copy-start.12 = (bf16[128,2176]{1,0:T(8,128)(2,1)}, bf16[128,2176]{1,0:T(8,128)(2,1)S(1)}, u32[]{:S(2)}) copy-start(bf16[128,2176]{1,0:T(8,128)(2,1)S(1)} %collective-permute-done.3.refs_3_) | copy-start | bytes 1671172
  21.4 79.8 %collective-permute-start.9 = (bf16[2,2048,256]{2,1,0:T(8,128)(2,1)}, bf16[2,2048,256]{2,1,0:T(8,128)(2,1)}, u32[]{:S(2)}, u32[]{:S(2)}) collective-permute-start(bf16[2,2048,256]{2,1,0:T(8,128)(2,1)} %refs_1_.5), channel_id=1, source_target_pairs={{0,1},{1,0},{2,3},{3,2},{4,5},{5,4},{6,7},{7,6},{8,9},{9,8},{10,11... | collective-permute-start | bytes 6291464 | tf_op jit(solution)/shard_map/ppermute | solution.py:271
  32.5 39.0 %copy-start.13 = (bf16[128,2176]{1,0:T(8,128)(2,1)}, bf16[128,2176]{1,0:T(8,128)(2,1)S(1)}, u32[]{:S(2)}) copy-start(bf16[128,2176]{1,0:T(8,128)(2,1)S(1)} %collective-permute-done.refs_1_) | copy-start | bytes 1671172
  32.5 40.5 %copy-start.14 = (bf16[128,2176]{1,0:T(8,128)(2,1)}, bf16[128,2176]{1,0:T(8,128)(2,1)S(1)}, u32[]{:S(2)}) copy-start(bf16[128,2176]{1,0:T(8,128)(2,1)S(1)} %collective-permute-done.1.refs_4_) | copy-start | bytes 1671172
  32.5 15.6 %collective-permute-start.4 = (bf16[128,2176]{1,0:T(8,128)(2,1)S(1)}, bf16[128,2176]{1,0:T(8,128)(2,1)S(1)}, u32[]{:S(2)}, u32[]{:S(2)}) collective-permute-start(bf16[128,2176]{1,0:T(8,128)(2,1)S(1)} %collective-permute-done.refs_1_), channel_id=1, source_target_pairs={{0,2},{1,3},{2,0},{3,1},{4,6},{5,7},{6,4},{7,5},{8,10},{9,11},{10,... | collective-permute-start | bytes 1671176 | tf_op jit(solution)/shard_map/ppermute | solution.py:271
  34.1 14.2 %collective-permute-start.2 = (bf16[128,2176]{1,0:T(8,128)(2,1)S(1)}, bf16[128,2176]{1,0:T(8,128)(2,1)S(1)}, u32[]{:S(2)}, u32[]{:S(2)}) collective-permute-start(bf16[128,2176]{1,0:T(8,128)(2,1)S(1)} %collective-permute-done.refs_1_), channel_id=1, source_target_pairs={{0,12},{1,13},{2,14},{3,15},{4,0},{5,1},{6,2},{7,3},{8,4},{9,5},{1... | collective-permute-start | bytes 1671176 | tf_op jit(solution)/shard_map/ppermute | solution.py:271
  37.3 22.7 %collective-permute-start.7 = (bf16[128,2176]{1,0:T(8,128)(2,1)S(1)}, bf16[128,2176]{1,0:T(8,128)(2,1)S(1)}, u32[]{:S(2)}, u32[]{:S(2)}) collective-permute-start(bf16[128,2176]{1,0:T(8,128)(2,1)S(1)} %collective-permute-done.3.refs_3_), channel_id=1, source_target_pairs={{0,2},{1,3},{2,0},{3,1},{4,6},{5,7},{6,4},{7,5},{8,10},{9,11},{10,... | collective-permute-start | bytes 1671176 | tf_op jit(solution)/shard_map/ppermute | solution.py:271
  48.1 25.0 %copy-start.15 = (bf16[128,2176]{1,0:T(8,128)(2,1)}, bf16[128,2176]{1,0:T(8,128)(2,1)S(1)}, u32[]{:S(2)}) copy-start(bf16[128,2176]{1,0:T(8,128)(2,1)S(1)} %collective-permute-done.4.refs_5_) | copy-start | bytes 1671172
  48.3 24.7 %copy-start.16 = (bf16[128,2176]{1,0:T(8,128)(2,1)}, bf16[128,2176]{1,0:T(8,128)(2,1)S(1)}, u32[]{:S(2)}) copy-start(bf16[128,2176]{1,0:T(8,128)(2,1)S(1)} %collective-permute-done.2.refs_2_) | copy-start | bytes 1671172
  48.3 22.6 %collective-permute-start.5 = (bf16[128,2176]{1,0:T(8,128)(2,1)S(1)}, bf16[128,2176]{1,0:T(8,128)(2,1)S(1)}, u32[]{:S(2)}, u32[]{:S(2)}) collective-permute-start(bf16[128,2176]{1,0:T(8,128)(2,1)S(1)} %collective-permute-done.2.refs_2_), channel_id=1, source_target_pairs={{0,2},{1,3},{2,0},{3,1},{4,6},{5,7},{6,4},{7,5},{8,10},{9,11},{10,... | collective-permute-start | bytes 1671176 | tf_op jit(solution)/shard_map/ppermute | solution.py:271
  49.7 11.9 %collective-permute-start.11 = (bf16[128,2048]{1,0:T(8,128)(2,1)}, bf16[128,2048]{1,0:T(8,128)(2,1)S(1)}, u32[]{:S(2)}, u32[]{:S(2)}) collective-permute-start(bf16[128,2048]{1,0:T(8,128)(2,1)} %refs_3_), channel_id=1, source_target_pairs={{0,12},{1,13},{2,14},{3,15},{4,0},{5,1},{6,2},{7,3},{8,4},{9,5},{1... | collective-permute-start | bytes 1572872 | tf_op jit(solution)/shard_map/ppermute | solution.py:271
  60.0 13.0 %copy-start.17 = (bf16[128,2176]{1,0:T(8,128)(2,1)}, bf16[128,2176]{1,0:T(8,128)(2,1)S(1)}, u32[]{:S(2)}) copy-start(bf16[128,2176]{1,0:T(8,128)(2,1)S(1)} %collective-permute-done.7.refs_7_) | copy-start | bytes 1671172
  60.0 17.0 %collective-permute-start.13 = (bf16[128,2048]{1,0:T(8,128)(2,1)}, bf16[128,2048]{1,0:T(8,128)(2,1)}, u32[]{:S(2)}, u32[]{:S(2)}) collective-permute-start(bf16[128,2048]{1,0:T(8,128)(2,1)} %refs_3_), channel_id=1, source_target_pairs={{0,4},{1,5},{2,6},{3,7},{4,8},{5,9},{6,10},{7,11},{8,12},{9,13},{1... | collective-permute-start | bytes 1572872 | tf_op jit(solution)/shard_map/ppermute | solution.py:271
  70.9 2.1 copy-start.18
  70.9 17.6 %collective-permute-start.15 = (bf16[128,2048]{1,0:T(8,128)(2,1)S(1)}, bf16[128,2048]{1,0:T(8,128)(2,1)}, u32[]{:S(2)}, u32[]{:S(2)}) collective-permute-start(bf16[128,2048]{1,0:T(8,128)(2,1)S(1)} %collective-permute-done.11.refs_3_.refs_4_), channel_id=1, source_target_pairs={{0,12},{1,13},{2,14},{3,15},{4,0},{5,1},{6,2},{7,3},{8,4},{9,5},{1... | collective-permute-start | bytes 1572872 | tf_op jit(solution)/shard_map/ppermute | solution.py:271
  71.5 17.1 %collective-permute-start.12 = (bf16[128,2048]{1,0:T(8,128)(2,1)S(1)}, bf16[128,2048]{1,0:T(8,128)(2,1)}, u32[]{:S(2)}, u32[]{:S(2)}) collective-permute-start(bf16[128,2048]{1,0:T(8,128)(2,1)S(1)} %collective-permute-done.11.refs_3_.refs_4_), channel_id=1, source_target_pairs={{0,2},{1,3},{2,0},{3,1},{4,6},{5,7},{6,4},{7,5},{8,10},{9,11},{10,... | collective-permute-start | bytes 1572872 | tf_op jit(solution)/shard_map/ppermute | solution.py:271
  74.9 13.7 %copy-start.3 = (bf16[2,2048,256]{2,1,0:T(8,128)(2,1)}, bf16[2,2048,256]{2,1,0:T(8,128)(2,1)S(1)}, u32[]{:S(2)}) copy-start(bf16[2,2048,256]{2,1,0:T(8,128)(2,1)S(1)} %collective-permute-done.8.gate_ref.refs_2_) | copy-start | bytes 6291460
  74.9 36.3 %collective-permute-start.10 = (bf16[512,512]{1,0:T(8,128)(2,1)}, bf16[512,512]{1,0:T(8,128)(2,1)}, u32[]{:S(2)}, u32[]{:S(2)}) collective-permute-start(bf16[512,512]{1,0:T(8,128)(2,1)} %slice.12), channel_id=1, source_target_pairs={{0,1},{1,0},{2,3},{3,2},{4,5},{5,4},{6,7},{7,6},{8,9},{9,8},{10,11... | collective-permute-start | bytes 1572872 | tf_op jit(solution)/shard_map/ppermute | solution.py:271
  77.0 35.8 %collective-permute-start.14 = (bf16[128,2048]{1,0:T(8,128)(2,1)}, bf16[128,2048]{1,0:T(8,128)(2,1)S(1)}, u32[]{:S(2)}, u32[]{:S(2)}) collective-permute-start(bf16[128,2048]{1,0:T(8,128)(2,1)} %collective-permute-done.13.refs_5_.refs_6_), channel_id=1, source_target_pairs={{0,2},{1,3},{2,0},{3,1},{4,6},{5,7},{6,4},{7,5},{8,10},{9,11},{10,... | collective-permute-start | bytes 1572872 | tf_op jit(solution)/shard_map/ppermute | solution.py:271
  78.5 10.7 %copy-start = (bf16[2,256,2048]{2,1,0:T(8,128)(2,1)S(1)}, bf16[2,256,2048]{2,1,0:T(8,128)(2,1)}, u32[]{:S(2)}) copy-start(bf16[2,256,2048]{2,1,0:T(8,128)(2,1)} %param.13) | copy-start | bytes 6291460
  88.6 24.1 %collective-permute-start.16 = (bf16[128,2048]{1,0:T(8,128)(2,1)}, bf16[128,2048]{1,0:T(8,128)(2,1)S(1)}, u32[]{:S(2)}, u32[]{:S(2)}) collective-permute-start(bf16[128,2048]{1,0:T(8,128)(2,1)} %collective-permute-done.15.refs_4_.refs_5_), channel_id=1, source_target_pairs={{0,2},{1,3},{2,0},{3,1},{4,6},{5,7},{6,4},{7,5},{8,10},{9,11},{10,... | collective-permute-start | bytes 1572872 | tf_op jit(solution)/shard_map/ppermute | solution.py:271
  101.2 11.5 %copy-start.5 = (bf16[1024,512]{1,0:T(8,128)(2,1)S(1)}, bf16[1024,512]{1,0:T(8,128)(2,1)}, u32[]{:S(2)}) copy-start(bf16[1024,512]{1,0:T(8,128)(2,1)} %get-tuple-element.94.own_ref) | copy-start | bytes 3145732
  111.2 20.5 %collective-permute-start.17 = (bf16[512,768]{1,0:T(8,128)(2,1)S(1)}, bf16[512,768]{1,0:T(8,128)(2,1)S(1)}, u32[]{:S(2)}, u32[]{:S(2)}) collective-permute-start(bf16[512,768]{1,0:T(8,128)(2,1)S(1)} %get-tuple-element.107), channel_id=1, source_target_pairs={{0,1},{1,0},{2,3},{3,2},{4,5},{5,4},{6,7},{7,6},{8,9},{9,8},{10,11... | collective-permute-start | bytes 2359304 | tf_op jit(solution)/shard_map/ppermute | solution.py:271
  112.8 1.2 copy-start.6
  114.0 3.9 %copy-start.8 = (bf16[128,2048]{1,0:T(8,128)(2,1)S(1)}, bf16[128,2048]{1,0:T(8,128)(2,1)}, u32[]{:S(2)}) copy-start(bf16[128,2048]{1,0:T(8,128)(2,1)} %refs_3_) | copy-start | bytes 1572868
  114.0 3.9 %copy-start.10 = (f32[1024,1024]{1,0:T(8,128)S(1)}, f32[1024,1024]{1,0:T(8,128)}, u32[]{:S(2)}) copy-start(f32[1024,1024]{1,0:T(8,128)} %get-tuple-element.109.refs_0_) | copy-start | bytes 12582916
  116.8 17.2 %collective-permute-start.18 = (bf16[512,512]{1,0:T(8,128)(2,1)S(1)}, bf16[512,512]{1,0:T(8,128)(2,1)S(1)}, u32[]{:S(2)}, u32[]{:S(2)}) collective-permute-start(bf16[512,512]{1,0:T(8,128)(2,1)S(1)} %get-tuple-element.113), channel_id=1, source_target_pairs={{0,2},{1,3},{2,0},{3,1},{4,6},{5,7},{6,4},{7,5},{8,10},{9,11},{10,... | collective-permute-start | bytes 1572872 | tf_op jit(solution)/shard_map/ppermute | solution.py:271
  117.4 30.5 %collective-permute-start.22 = (bf16[512,768]{1,0:T(8,128)(2,1)}, bf16[512,768]{1,0:T(8,128)(2,1)S(1)}, u32[]{:S(2)}, u32[]{:S(2)}) collective-permute-start(bf16[512,768]{1,0:T(8,128)(2,1)} %get-tuple-element.121), channel_id=1, source_target_pairs={{0,1},{1,0},{2,3},{3,2},{4,5},{5,4},{6,7},{7,6},{8,9},{9,8},{10,11... | collective-permute-start | bytes 2359304 | tf_op jit(solution)/shard_map/ppermute | solution.py:271
  117.9 13.8 %copy-start.7 = (bf16[1024,512]{1,0:T(8,128)(2,1)S(1)}, bf16[1024,512]{1,0:T(8,128)(2,1)}, u32[]{:S(2)}) copy-start(bf16[1024,512]{1,0:T(8,128)(2,1)} %get-tuple-element.98.other_ref) | copy-start | bytes 3145732
  134.1 7.9 %collective-permute-start.20 = (bf16[128,512]{1,0:T(8,128)(2,1)S(1)}, bf16[128,512]{1,0:T(8,128)(2,1)S(1)}, u32[]{:S(2)}, u32[]{:S(2)}) collective-permute-start(bf16[128,512]{1,0:T(8,128)(2,1)S(1)} %get-tuple-element.117), channel_id=1, source_target_pairs={{0,4},{1,5},{2,6},{3,7},{4,8},{5,9},{6,10},{7,11},{8,12},{9,13},{1... | collective-permute-start | bytes 393224 | tf_op jit(solution)/shard_map/ppermute | solution.py:271
  135.7 7.5 %collective-permute-start.19 = (bf16[128,512]{1,0:T(8,128)(2,1)S(1)}, bf16[128,512]{1,0:T(8,128)(2,1)S(1)}, u32[]{:S(2)}, u32[]{:S(2)}) collective-permute-start(bf16[128,512]{1,0:T(8,128)(2,1)S(1)} %get-tuple-element.115), channel_id=1, source_target_pairs={{0,12},{1,13},{2,14},{3,15},{4,0},{5,1},{6,2},{7,3},{8,4},{9,5},{1... | collective-permute-start | bytes 393224 | tf_op jit(solution)/shard_map/ppermute | solution.py:271
  138.0 23.3 %collective-permute-start.23 = (bf16[512,768]{1,0:T(8,128)(2,1)S(1)}, bf16[512,768]{1,0:T(8,128)(2,1)S(1)}, u32[]{:S(2)}, u32[]{:S(2)}) collective-permute-start(bf16[512,768]{1,0:T(8,128)(2,1)S(1)} %get-tuple-element.111), channel_id=1, source_target_pairs={{0,2},{1,3},{2,0},{3,1},{4,6},{5,7},{6,4},{7,5},{8,10},{9,11},{10,... | collective-permute-start | bytes 2359304 | tf_op jit(solution)/shard_map/ppermute | solution.py:271
  143.2 6.8 %collective-permute-start.21 = (bf16[128,512]{1,0:T(8,128)(2,1)S(1)}, bf16[128,512]{1,0:T(8,128)(2,1)S(1)}, u32[]{:S(2)}, u32[]{:S(2)}) collective-permute-start(bf16[128,512]{1,0:T(8,128)(2,1)S(1)} %add_piece.5), channel_id=1, source_target_pairs={{0,4},{1,5},{2,6},{3,7},{4,8},{5,9},{6,10},{7,11},{8,12},{9,13},{1... | collective-permute-start | bytes 393224 | tf_op jit(solution)/shard_map/ppermute | solution.py:271
  147.8 5.0 %copy-start.9 = (f32[1024,1024]{1,0:T(8,128)S(1)}, f32[1024,1024]{1,0:T(8,128)}, u32[]{:S(2)}) copy-start(f32[1024,1024]{1,0:T(8,128)} %get-tuple-element.125.refs_0_) | copy-start | bytes 12582916
  152.2 21.0 %collective-permute-start.27 = (bf16[512,768]{1,0:T(8,128)(2,1)S(1)}, bf16[512,768]{1,0:T(8,128)(2,1)S(1)}, u32[]{:S(2)}, u32[]{:S(2)}) collective-permute-start(bf16[512,768]{1,0:T(8,128)(2,1)S(1)} %get-tuple-element.134), channel_id=1, source_target_pairs={{0,2},{1,3},{2,0},{3,1},{4,6},{5,7},{6,4},{7,5},{8,10},{9,11},{10,... | collective-permute-start | bytes 2359304 | tf_op jit(solution)/shard_map/ppermute | solution.py:271
  152.8 2.8 %copy-start.1 = (bf16[2,2048,256]{2,1,0:T(8,128)(2,1)S(1)}, bf16[2,2048,256]{2,1,0:T(8,128)(2,1)}, u32[]{:S(2)}) copy-start(bf16[2,2048,256]{2,1,0:T(8,128)(2,1)} %refs_0_.5) | copy-start | bytes 6291460
  152.8 2.8 %copy-start.2 = (bf16[2,2048,256]{2,1,0:T(8,128)(2,1)S(1)}, bf16[2,2048,256]{2,1,0:T(8,128)(2,1)}, u32[]{:S(2)}) copy-start(bf16[2,2048,256]{2,1,0:T(8,128)(2,1)} %refs_1_.5) | copy-start | bytes 6291460
  152.8 3.3 %copy-start.4 = (bf16[2,2048,256]{2,1,0:T(8,128)(2,1)S(1)}, bf16[2,2048,256]{2,1,0:T(8,128)(2,1)}, u32[]{:S(2)}) copy-start(bf16[2,2048,256]{2,1,0:T(8,128)(2,1)} %copy-done.3) | copy-start | bytes 6291460
  161.4 9.7 %collective-permute-start.25 = (bf16[128,768]{1,0:T(8,128)(2,1)S(1)}, bf16[128,768]{1,0:T(8,128)(2,1)S(1)}, u32[]{:S(2)}, u32[]{:S(2)}) collective-permute-start(bf16[128,768]{1,0:T(8,128)(2,1)S(1)} %get-tuple-element.131), channel_id=1, source_target_pairs={{0,4},{1,5},{2,6},{3,7},{4,8},{5,9},{6,10},{7,11},{8,12},{9,13},{1... | collective-permute-start | bytes 589832 | tf_op jit(solution)/shard_map/ppermute | solution.py:271
  161.5 11.7 %collective-permute-start.24 = (bf16[128,768]{1,0:T(8,128)(2,1)S(1)}, bf16[128,768]{1,0:T(8,128)(2,1)S(1)}, u32[]{:S(2)}, u32[]{:S(2)}) collective-permute-start(bf16[128,768]{1,0:T(8,128)(2,1)S(1)} %get-tuple-element.129), channel_id=1, source_target_pairs={{0,12},{1,13},{2,14},{3,15},{4,0},{5,1},{6,2},{7,3},{8,4},{9,5},{1... | collective-permute-start | bytes 589832 | tf_op jit(solution)/shard_map/ppermute | solution.py:271
  165.3 30.2 %collective-permute-start.31 = (bf16[512,768]{1,0:T(8,128)(2,1)S(1)}, bf16[512,768]{1,0:T(8,128)(2,1)S(1)}, u32[]{:S(2)}, u32[]{:S(2)}) collective-permute-start(bf16[512,768]{1,0:T(8,128)(2,1)S(1)} %get-tuple-element.145), channel_id=1, source_target_pairs={{0,2},{1,3},{2,0},{3,1},{4,6},{5,7},{6,4},{7,5},{8,10},{9,11},{10,... | collective-permute-start | bytes 2359304 | tf_op jit(solution)/shard_map/ppermute | solution.py:271
  173.2 7.5 %collective-permute-start.26 = (bf16[128,768]{1,0:T(8,128)(2,1)S(1)}, bf16[128,768]{1,0:T(8,128)(2,1)S(1)}, u32[]{:S(2)}, u32[]{:S(2)}) collective-permute-start(bf16[128,768]{1,0:T(8,128)(2,1)S(1)} %add_piece.6), channel_id=1, source_target_pairs={{0,4},{1,5},{2,6},{3,7},{4,8},{5,9},{6,10},{7,11},{8,12},{9,13},{1... | collective-permute-start | bytes 589832 | tf_op jit(solution)/shard_map/ppermute | solution.py:271
  173.4 10.5 %collective-permute-start.29 = (bf16[128,768]{1,0:T(8,128)(2,1)S(1)}, bf16[128,768]{1,0:T(8,128)(2,1)S(1)}, u32[]{:S(2)}, u32[]{:S(2)}) collective-permute-start(bf16[128,768]{1,0:T(8,128)(2,1)S(1)} %get-tuple-element.139), channel_id=1, source_target_pairs={{0,4},{1,5},{2,6},{3,7},{4,8},{5,9},{6,10},{7,11},{8,12},{9,13},{1... | collective-permute-start | bytes 589832 | tf_op jit(solution)/shard_map/ppermute | solution.py:271
  189.0 22.5 %collective-permute-start.35 = (bf16[512,768]{1,0:T(8,128)(2,1)S(1)}, bf16[512,768]{1,0:T(8,128)(2,1)S(1)}, u32[]{:S(2)}, u32[]{:S(2)}) collective-permute-start(bf16[512,768]{1,0:T(8,128)(2,1)S(1)} %get-tuple-element.155), channel_id=1, source_target_pairs={{0,2},{1,3},{2,0},{3,1},{4,6},{5,7},{6,4},{7,5},{8,10},{9,11},{10,... | collective-permute-start | bytes 2359304 | tf_op jit(solution)/shard_map/ppermute | solution.py:271
  191.7 5.8 %collective-permute-start.28 = (bf16[128,768]{1,0:T(8,128)(2,1)S(1)}, bf16[128,768]{1,0:T(8,128)(2,1)S(1)}, u32[]{:S(2)}, u32[]{:S(2)}) collective-permute-start(bf16[128,768]{1,0:T(8,128)(2,1)S(1)} %get-tuple-element.137), channel_id=1, source_target_pairs={{0,12},{1,13},{2,14},{3,15},{4,0},{5,1},{6,2},{7,3},{8,4},{9,5},{1... | collective-permute-start | bytes 589832 | tf_op jit(solution)/shard_map/ppermute | solution.py:271
  195.7 30.5 %collective-permute-start.39 = (bf16[512,512]{1,0:T(8,128)(2,1)S(1)}, bf16[512,512]{1,0:T(8,128)(2,1)S(1)}, u32[]{:S(2)}, u32[]{:S(2)}) collective-permute-start(bf16[512,512]{1,0:T(8,128)(2,1)S(1)} %get-tuple-element.163), channel_id=1, source_target_pairs={{0,2},{1,3},{2,0},{3,1},{4,6},{5,7},{6,4},{7,5},{8,10},{9,11},{10,... | collective-permute-start | bytes 1572872 | tf_op jit(solution)/shard_map/ppermute | solution.py:271
  197.5 9.8 %collective-permute-start.30 = (bf16[128,768]{1,0:T(8,128)(2,1)S(1)}, bf16[128,768]{1,0:T(8,128)(2,1)S(1)}, u32[]{:S(2)}, u32[]{:S(2)}) collective-permute-start(bf16[128,768]{1,0:T(8,128)(2,1)S(1)} %add_piece.7), channel_id=1, source_target_pairs={{0,4},{1,5},{2,6},{3,7},{4,8},{5,9},{6,10},{7,11},{8,12},{9,13},{1... | collective-permute-start | bytes 589832 | tf_op jit(solution)/shard_map/ppermute | solution.py:271
  199.0 12.5 %collective-permute-start.33 = (bf16[128,768]{1,0:T(8,128)(2,1)S(1)}, bf16[128,768]{1,0:T(8,128)(2,1)S(1)}, u32[]{:S(2)}, u32[]{:S(2)}) collective-permute-start(bf16[128,768]{1,0:T(8,128)(2,1)S(1)} %get-tuple-element.149), channel_id=1, source_target_pairs={{0,4},{1,5},{2,6},{3,7},{4,8},{5,9},{6,10},{7,11},{8,12},{9,13},{1... | collective-permute-start | bytes 589832 | tf_op jit(solution)/shard_map/ppermute | solution.py:271
  199.0 16.5 %collective-permute-start.32 = (bf16[128,768]{1,0:T(8,128)(2,1)S(1)}, bf16[128,768]{1,0:T(8,128)(2,1)S(1)}, u32[]{:S(2)}, u32[]{:S(2)}) collective-permute-start(bf16[128,768]{1,0:T(8,128)(2,1)S(1)} %get-tuple-element.147), channel_id=1, source_target_pairs={{0,12},{1,13},{2,14},{3,15},{4,0},{5,1},{6,2},{7,3},{8,4},{9,5},{1... | collective-permute-start | bytes 589832 | tf_op jit(solution)/shard_map/ppermute | solution.py:271
  211.6 9.5 %collective-permute-start.37 = (bf16[128,768]{1,0:T(8,128)(2,1)S(1)}, bf16[128,768]{1,0:T(8,128)(2,1)S(1)}, u32[]{:S(2)}, u32[]{:S(2)}) collective-permute-start(bf16[128,768]{1,0:T(8,128)(2,1)S(1)} %get-tuple-element.160), channel_id=1, source_target_pairs={{0,4},{1,5},{2,6},{3,7},{4,8},{5,9},{6,10},{7,11},{8,12},{9,13},{1... | collective-permute-start | bytes 589832 | tf_op jit(solution)/shard_map/ppermute | solution.py:271
  211.7 10.4 %collective-permute-start.36 = (bf16[128,768]{1,0:T(8,128)(2,1)S(1)}, bf16[128,768]{1,0:T(8,128)(2,1)S(1)}, u32[]{:S(2)}, u32[]{:S(2)}) collective-permute-start(bf16[128,768]{1,0:T(8,128)(2,1)S(1)} %get-tuple-element.158), channel_id=1, source_target_pairs={{0,12},{1,13},{2,14},{3,15},{4,0},{5,1},{6,2},{7,3},{8,4},{9,5},{1... | collective-permute-start | bytes 589832 | tf_op jit(solution)/shard_map/ppermute | solution.py:271
  215.5 10.7 %collective-permute-start.34 = (bf16[128,768]{1,0:T(8,128)(2,1)S(1)}, bf16[128,768]{1,0:T(8,128)(2,1)S(1)}, u32[]{:S(2)}, u32[]{:S(2)}) collective-permute-start(bf16[128,768]{1,0:T(8,128)(2,1)S(1)} %add_piece.8), channel_id=1, source_target_pairs={{0,4},{1,5},{2,6},{3,7},{4,8},{5,9},{6,10},{7,11},{8,12},{9,13},{1... | collective-permute-start | bytes 589832 | tf_op jit(solution)/shard_map/ppermute | solution.py:271
  222.1 13.0 %collective-permute-start.38 = (bf16[128,768]{1,0:T(8,128)(2,1)S(1)}, bf16[128,768]{1,0:T(8,128)(2,1)S(1)}, u32[]{:S(2)}, u32[]{:S(2)}) collective-permute-start(bf16[128,768]{1,0:T(8,128)(2,1)S(1)} %add_piece.9), channel_id=1, source_target_pairs={{0,4},{1,5},{2,6},{3,7},{4,8},{5,9},{6,10},{7,11},{8,12},{9,13},{1... | collective-permute-start | bytes 589832 | tf_op jit(solution)/shard_map/ppermute | solution.py:271
  226.3 7.0 %collective-permute-start.40 = (bf16[128,512]{1,0:T(8,128)(2,1)S(1)}, bf16[128,512]{1,0:T(8,128)(2,1)S(1)}, u32[]{:S(2)}, u32[]{:S(2)}) collective-permute-start(bf16[128,512]{1,0:T(8,128)(2,1)S(1)} %get-tuple-element.169), channel_id=1, source_target_pairs={{0,4},{1,5},{2,6},{3,7},{4,8},{5,9},{6,10},{7,11},{8,12},{9,13},{1... | collective-permute-start | bytes 393224 | tf_op jit(solution)/shard_map/ppermute | solution.py:271
  226.4 8.7 %collective-permute-start.41 = (bf16[128,512]{1,0:T(8,128)(2,1)S(1)}, bf16[128,512]{1,0:T(8,128)(2,1)S(1)}, u32[]{:S(2)}, u32[]{:S(2)}) collective-permute-start(bf16[128,512]{1,0:T(8,128)(2,1)S(1)} %get-tuple-element.170), channel_id=1, source_target_pairs={{0,8},{1,9},{2,10},{3,11},{4,12},{5,13},{6,14},{7,15},{8,0},{9,1},... | collective-permute-start | bytes 393224 | tf_op jit(solution)/shard_map/ppermute | solution.py:271
  227.0 8.1 %collective-permute-start.42 = (bf16[128,512]{1,0:T(8,128)(2,1)S(1)}, bf16[128,512]{1,0:T(8,128)(2,1)S(1)}, u32[]{:S(2)}, u32[]{:S(2)}) collective-permute-start(bf16[128,512]{1,0:T(8,128)(2,1)S(1)} %get-tuple-element.171), channel_id=1, source_target_pairs={{0,12},{1,13},{2,14},{3,15},{4,0},{5,1},{6,2},{7,3},{8,4},{9,5},{1... | collective-permute-start | bytes 393224 | tf_op jit(solution)/shard_map/ppermute | solution.py:271

commit v16 on v15

--- a/solution.py
+++ b/solution.py
@@ -278,7 +278,7 @@
     experts = local_count * devices
     block = tokens.shape[0]
     chunks = cut_columns(width, ((6, 8), (0, 3), (3, 6)))
-    back_chunks = cut_columns(width, ((0, 3), (3, 6), (6, 8)))
+    back_chunks = cut_columns(width, ((0, 4), (4, 6), (6, 8)))
     me = lax.axis_index("expert")
     twin = [(d, d ^ 1) for d in range(devices)]
     side = [(d, d ^ 2) for d in range(devices)]

time: 237 us -> 257 us (1.084)
  waiting for transfers between devices: 110 us -> 129 us
    ppermute x43, waiting for transfers between devices: 110 us -> 129 us  [send_all(): lax.ppermute(v, 'expert', pairs)]
  transfers between devices with their start and end apart: 43 -> 43, of which waited for: 25 -> 27; matrix products, arithmetic and copies ran while one was open for 1% -> 1% of each run, Pallas kernels for 23% -> 22%
where the time goes in v16:
time: 257 us; the launch traced here: 254 us
  waiting for transfers between devices  129 us (50%)
  starting transfers between devices  61.1 us (24%)
  Pallas kernels  56.5 us (22%)
  local copies, waits for them, and re-layouts  6.27 us (2%)
    ppermute x43, waiting for transfers between devices, send_all(): lax.ppermute(v, 'expert', pairs)  129 us
    ppermute x43, starting transfers between devices, send_all(): lax.ppermute(v, 'expert', pairs)  61.1 us
    pallas_call x6, Pallas kernels, sum_columns(): pl.pallas_call(kernel, grid=(2,), in_specs=[rows, rows] + weight_specs, o...  21.9 us
    pallas_call x2, Pallas kernels, hidden_forward(): pl.pallas_call(functools.partial(hidden_kernel, blocks, all_experts), gri...  19.8 us
    pallas_call x3, Pallas kernels, hidden_grads(): pl.pallas_call(functools.partial(grads_kernel, blocks, tuple(cuts), by is...  11.7 us
  transfers between devices with their start and end apart: 43, of which 27 were waited for; matrix products, arithmetic and copies ran while one was open for 1% of the time, Pallas kernels for 22%

profile of v16, /device:TPU:0, one launch (start us, length us, event | category | flops | bytes accessed | tf_op | source)
XLA Modules:
  0.0 254.4 jit_solution(16259686389040191143)
XLA Ops:
  1.8 1.9 concatenate.3.refs_0_
  3.7 3.0 %collective-permute-start.3 = (bf16[128,2176]{1,0:T(8,128)(2,1)}, bf16[128,2176]{1,0:T(8,128)(2,1)S(1)}, u32[]{:S(2)}, u32[]{:S(2)}) collective-permute-start(bf16[128,2176]{1,0:T(8,128)(2,1)} %concatenate.3.refs_0_), channel_id=1, source_target_pairs={{0,4},{1,5},{2,6},{3,7},{4,8},{5,9},{6,10},{7,11},{8,12},{9,13},{1... | collective-permute-start | bytes 1671176 | tf_op jit(solution)/shard_map/ppermute | solution.py:271
  6.7 1.5 collective-permute-start.6
  8.2 1.5 collective-permute-start.8
  9.7 10.6 %collective-permute-done.6.refs_6_.refs_7_ = bf16[128,2048]{1,0:T(8,128)(2,1)S(1)} collective-permute-done((bf16[128,2048]{1,0:T(8,128)(2,1)}, bf16[128,2048]{1,0:T(8,128)(2,1)S(1)}, u32[]{:S(2)}, u32[]{:S(2)}) %collective-permute-start.6) | collective-permute-done | bytes 524320 | tf_op jit(solution)/shard_map/ppermute | solution.py:271
  20.3 1.3 collective-permute-done.3.refs_3_
  21.6 1.5 collective-permute-start.9
  23.0 1.7 collective-permute-start
  24.8 1.5 collective-permute-start.1
  26.3 10.2 %collective-permute-done.refs_1_ = bf16[128,2176]{1,0:T(8,128)(2,1)S(1)} collective-permute-done((bf16[128,2176]{1,0:T(8,128)(2,1)}, bf16[128,2176]{1,0:T(8,128)(2,1)S(1)}, u32[]{:S(2)}, u32[]{:S(2)}) %collective-permute-start) | collective-permute-done | bytes 557088 | tf_op jit(solution)/shard_map/ppermute | solution.py:271
  36.5 1.5 collective-permute-done.1.refs_4_
  38.0 1.5 collective-permute-start.4
  39.6 2.1 collective-permute-start.2
  42.5 11.2 %collective-permute-done.4.refs_5_ = bf16[128,2176]{1,0:T(8,128)(2,1)S(1)} collective-permute-done((bf16[128,2176]{1,0:T(8,128)(2,1)S(1)}, bf16[128,2176]{1,0:T(8,128)(2,1)S(1)}, u32[]{:S(2)}, u32[]{:S(2)}) %collective-permute-start.4) | collective-permute-done | bytes 557088 | tf_op jit(solution)/shard_map/ppermute | solution.py:271
  53.6 1.6 collective-permute-start.5
  55.2 2.1 collective-permute-start.11
  57.4 1.9 slice.12
  59.2 6.3 %collective-permute-done.7.refs_7_ = bf16[128,2176]{1,0:T(8,128)(2,1)S(1)} collective-permute-done((bf16[128,2176]{1,0:T(8,128)(2,1)S(1)}, bf16[128,2176]{1,0:T(8,128)(2,1)S(1)}, u32[]{:S(2)}, u32[]{:S(2)}) %collective-permute-start.7) | collective-permute-done | bytes 557088 | tf_op jit(solution)/shard_map/ppermute | solution.py:271
  66.7 2.7 %collective-permute-done.11.refs_3_.refs_4_ = bf16[128,2048]{1,0:T(8,128)(2,1)} collective-permute-done((bf16[128,2048]{1,0:T(8,128)(2,1)}, bf16[128,2048]{1,0:T(8,128)(2,1)}, u32[]{:S(2)}, u32[]{:S(2)}) %collective-permute-start.11) | collective-permute-done | bytes 524320 | tf_op jit(solution)/shard_map/ppermute | solution.py:271
  69.3 4.8 %collective-permute-done.5.refs_6_ = bf16[128,2176]{1,0:T(8,128)(2,1)S(1)} collective-permute-done((bf16[128,2176]{1,0:T(8,128)(2,1)S(1)}, bf16[128,2176]{1,0:T(8,128)(2,1)S(1)}, u32[]{:S(2)}, u32[]{:S(2)}) %collective-permute-start.5) | collective-permute-done | bytes 557088 | tf_op jit(solution)/shard_map/ppermute | solution.py:271
  74.1 2.3 collective-permute-start.15
  76.5 1.5 collective-permute-start.12
  79.0 9.9 %hidden_forward.2 = (bf16[1024,512]{1,0:T(8,128)(2,1)}, f32[1024,1024]{1,0:T(8,128)}) custom-call(s32[1]{0:T(128)} %bitcast.owner_ref, bf16[2,2048,256]{2,1,0:T(8,128)(2,1)} %refs_0_.5, bf16[2,2048,256]{2,1,0:T(8,128)(2,1)} %refs_1_.5, bf16[128,2176]{1,0:T(8,128)(2,1)} %concatenate.3.refs_0_, bf16[128,2176]{1,0:T(8,128)(2,1)} %copy-done.10, ...), custom_call_target="tpu_custom_call" | custom-call | flops 1 | bytes 1 | tf_op jit(solution)/shard_map/hidden_forward/pallas_call | solution.py:71
  88.9 13.1 %collective-permute-done.9.up_ref.refs_3_ = bf16[2,2048,256]{2,1,0:T(8,128)(2,1)} collective-permute-done((bf16[2,2048,256]{2,1,0:T(8,128)(2,1)}, bf16[2,2048,256]{2,1,0:T(8,128)(2,1)}, u32[]{:S(2)}, u32[]{:S(2)}) %collective-permute-start.9) | collective-permute-done | bytes 2097184 | tf_op jit(solution)/shard_map/ppermute | solution.py:271
  102.0 9.9 %hidden_forward.3 = (bf16[1024,512]{1,0:T(8,128)(2,1)}, f32[1024,1024]{1,0:T(8,128)}) custom-call(s32[1]{0:T(128)} %bitcast.1.owner_ref, bf16[2,2048,256]{2,1,0:T(8,128)(2,1)} %collective-permute-done.8.gate_ref.refs_2_, bf16[2,2048,256]{2,1,0:T(8,128)(2,1)} %collective-permute-done.9.up_ref.refs_3_, bf16[128,2176]{1,0:T(8,128)(2,1)} %concatenate.3.refs_0_, ...), custom_call_target="tpu_custom_call" | custom-call | flops 1 | bytes 1 | tf_op jit(solution)/shard_map/hidden_forward/pallas_call | solution.py:71
  112.0 1.6 collective-permute-start.17
  114.1 1.5 collective-permute-start.16
  115.6 13.0 %collective-permute-done.14.refs_9_.refs_10_ = bf16[128,2048]{1,0:T(8,128)(2,1)S(1)} collective-permute-done((bf16[128,2048]{1,0:T(8,128)(2,1)}, bf16[128,2048]{1,0:T(8,128)(2,1)S(1)}, u32[]{:S(2)}, u32[]{:S(2)}) %collective-permute-start.14) | collective-permute-done | bytes 524320 | tf_op jit(solution)/shard_map/ppermute | solution.py:271
  128.6 7.7 %collective-permute-done.16.refs_8_.refs_9_ = bf16[128,2048]{1,0:T(8,128)(2,1)S(1)} collective-permute-done((bf16[128,2048]{1,0:T(8,128)(2,1)}, bf16[128,2048]{1,0:T(8,128)(2,1)S(1)}, u32[]{:S(2)}, u32[]{:S(2)}) %collective-permute-start.16) | collective-permute-done | bytes 524320 | tf_op jit(solution)/shard_map/ppermute | solution.py:271
  136.4 1.2 copy-done.4
  137.6 2.8 %mix_columns.3 = (f32[512,512]{1,0:T(8,128)S(1)}, bf16[512,512]{1,0:T(8,128)(2,1)S(1)}) custom-call(bf16[1024,512]{1,0:T(8,128)(2,1)S(1)} %copy-done.3, bf16[1024,512]{1,0:T(8,128)(2,1)S(1)} %copy-done.4, bf16[512,2048]{1,0:T(8,128)(2,1)S(1)} %bitcast.5, bf16[512,512]{1,0:T(8,128)(2,1)} %collective-permute-done.10.other_down_ref.refs_0_), custom_call_target="tpu_custom_call" | custom-call | flops 1 | bytes 1 | tf_op jit(solution)/shard_map/mix_columns/pallas_call | solution.py:179
  141.5 4.3 %hidden_grads.3.own_ref = bf16[1024,1024]{1,0:T(8,128)(2,1)S(1)} custom-call(f32[1024,1024]{1,0:T(8,128)S(1)} %copy-done.8, bf16[512,2048]{1,0:T(8,128)(2,1)S(1)} %bitcast.6, bf16[128,2048]{1,0:T(8,128)(2,1)S(1)} %copy-done.6, bf16[128,2048]{1,0:T(8,128)(2,1)} %collective-permute-done.11.refs_3_.refs_4_, ...), custom_call_target="tpu_custom_call" | custom-call | flops 1 | bytes 1 | tf_op jit(solution)/shard_map/hidden_grads/pallas_call | solution.py:127
  145.8 2.2 mix_columns.4
  148.0 1.6 collective-permute-start.23
  149.6 5.4 %collective-permute-done.18.come_ref = bf16[512,512]{1,0:T(8,128)(2,1)S(1)} collective-permute-done((bf16[512,512]{1,0:T(8,128)(2,1)S(1)}, bf16[512,512]{1,0:T(8,128)(2,1)S(1)}, u32[]{:S(2)}, u32[]{:S(2)}) %collective-permute-start.18) | collective-permute-done | bytes 524320 | tf_op jit(solution)/shard_map/ppermute | solution.py:271
  155.1 1.6 collective-permute-start.20
  156.7 2.3 collective-permute-start.19
  158.9 3.1 %collective-permute-done.20.come_ref = bf16[128,512]{1,0:T(8,128)(2,1)S(1)} collective-permute-done((bf16[128,512]{1,0:T(8,128)(2,1)S(1)}, bf16[128,512]{1,0:T(8,128)(2,1)S(1)}, u32[]{:S(2)}, u32[]{:S(2)}) %collective-permute-start.20) | collective-permute-done | bytes 131104 | tf_op jit(solution)/shard_map/ppermute | solution.py:271
  163.9 4.4 %hidden_grads.4.refs_1_ = f32[1024,512]{1,0:T(8,128)S(1)} custom-call(bf16[512,512]{1,0:T(8,128)(2,1)} %collective-permute-done.10.other_down_ref.refs_0_, bf16[512,768]{1,0:T(8,128)(2,1)S(1)} %collective-permute-done.17.other_down_ref.refs_1_, bf16[128,2048]{1,0:T(8,128)(2,1)S(1)} %copy-done.6, bf16[128,2048]{1,0:T(8,128)(2,1)} %collective-permute-done.11.refs_3_.refs_4_, ...), custom_call_target="tpu_custom_call" | custom-call | flops 1 | bytes 1 | tf_op jit(solution)/shard_map/hidden_grads/pallas_call | solution.py:127
  168.3 1.6 collective-permute-done.21.refs_2_
  169.8 2.2 mix_columns.5
  172.2 3.0 %hidden_grads.5.other_ref = bf16[1024,1024]{1,0:T(8,128)(2,1)S(1)} custom-call(f32[1024,1024]{1,0:T(8,128)S(1)} %copy-done.7, f32[1024,512]{1,0:T(8,128)S(1)} %hidden_grads.4.refs_1_, bf16[512,768]{1,0:T(8,128)(2,1)S(1)} %collective-permute-done.22.other_down_ref.refs_2_, bf16[128,2048]{1,0:T(8,128)(2,1)S(1)} %copy-done.6, ...), custom_call_target="tpu_custom_call" | custom-call | flops 1 | bytes 1 | tf_op jit(solution)/shard_map/hidden_grads/pallas_call | solution.py:127
  175.2 6.7 %back_columns.3 = (f32[512,1024]{1,0:T(8,128)S(1)}, bf16[512,1024]{1,0:T(8,128)(2,1)S(1)}) custom-call(bf16[1024,1024]{1,0:T(8,128)(2,1)S(1)} %hidden_grads.3.own_ref, bf16[1024,1024]{1,0:T(8,128)(2,1)S(1)} %hidden_grads.5.other_ref, bf16[2,2048,256]{2,1,0:T(8,128)(2,1)S(1)} %copy-done.1, bf16[2,2048,256]{2,1,0:T(8,128)(2,1)S(1)} %copy-done.2, ...), custom_call_target="tpu_custom_call" | custom-call | flops 1 | bytes 1 | tf_op jit(solution)/shard_map/back_columns/pallas_call | solution.py:179
  182.1 2.0 collective-permute-start.31
  184.1 3.8 %collective-permute-start.24 = (bf16[128,768]{1,0:T(8,128)(2,1)S(1)}, bf16[128,768]{1,0:T(8,128)(2,1)S(1)}, u32[]{:S(2)}, u32[]{:S(2)}) collective-permute-start(bf16[128,768]{1,0:T(8,128)(2,1)S(1)} %get-tuple-element.129), channel_id=1, source_target_pairs={{0,12},{1,13},{2,14},{3,15},{4,0},{5,1},{6,2},{7,3},{8,4},{9,5},{1... | collective-permute-start | bytes 589832 | tf_op jit(solution)/shard_map/ppermute | solution.py:271
  187.9 3.8 %collective-permute-done.25.come_ref = bf16[128,768]{1,0:T(8,128)(2,1)S(1)} collective-permute-done((bf16[128,768]{1,0:T(8,128)(2,1)S(1)}, bf16[128,768]{1,0:T(8,128)(2,1)S(1)}, u32[]{:S(2)}, u32[]{:S(2)}) %collective-permute-start.25) | collective-permute-done | bytes 196640 | tf_op jit(solution)/shard_map/ppermute | solution.py:271
  193.5 1.8 collective-permute-start.29
  195.2 5.3 %collective-permute-done.26.refs_5_ = bf16[128,768]{1,0:T(8,128)(2,1)S(1)} collective-permute-done((bf16[128,768]{1,0:T(8,128)(2,1)S(1)}, bf16[128,768]{1,0:T(8,128)(2,1)S(1)}, u32[]{:S(2)}, u32[]{:S(2)}) %collective-permute-start.26) | collective-permute-done | bytes 196640 | tf_op jit(solution)/shard_map/ppermute | solution.py:271
  200.5 2.1 collective-permute-done.29.come_ref
  202.6 4.0 %back_columns.5 = (f32[512,512]{1,0:T(8,128)S(1)}, bf16[512,512]{1,0:T(8,128)(2,1)S(1)}) custom-call(bf16[1024,1024]{1,0:T(8,128)(2,1)S(1)} %hidden_grads.3.own_ref, bf16[1024,1024]{1,0:T(8,128)(2,1)S(1)} %hidden_grads.5.other_ref, bf16[2,2048,256]{2,1,0:T(8,128)(2,1)S(1)} %copy-done.1, bf16[2,2048,256]{2,1,0:T(8,128)(2,1)S(1)} %copy-done.2, ...), custom_call_target="tpu_custom_call" | custom-call | flops 1 | bytes 1 | tf_op jit(solution)/shard_map/back_columns/pallas_call | solution.py:179
  207.8 1.7 collective-permute-start.28
  209.4 4.0 %back_columns.4 = (f32[512,512]{1,0:T(8,128)S(1)}, bf16[512,512]{1,0:T(8,128)(2,1)S(1)}) custom-call(bf16[1024,1024]{1,0:T(8,128)(2,1)S(1)} %hidden_grads.3.own_ref, bf16[1024,1024]{1,0:T(8,128)(2,1)S(1)} %hidden_grads.5.other_ref, bf16[2,2048,256]{2,1,0:T(8,128)(2,1)S(1)} %copy-done.1, bf16[2,2048,256]{2,1,0:T(8,128)(2,1)S(1)} %copy-done.2, ...), custom_call_target="tpu_custom_call" | custom-call | flops 1 | bytes 1 | tf_op jit(solution)/shard_map/back_columns/pallas_call | solution.py:179
  213.4 1.6 collective-permute-done.31.come_ref
  215.7 3.8 %collective-permute-start.32 = (bf16[128,1024]{1,0:T(8,128)(2,1)S(1)}, bf16[128,1024]{1,0:T(8,128)(2,1)S(1)}, u32[]{:S(2)}, u32[]{:S(2)}) collective-permute-start(bf16[128,1024]{1,0:T(8,128)(2,1)S(1)} %get-tuple-element.147), channel_id=1, source_target_pairs={{0,12},{1,13},{2,14},{3,15},{4,0},{5,1},{6,2},{7,3},{8,4},{9,5},{1... | collective-permute-start | bytes 786440 | tf_op jit(solution)/shard_map/ppermute | solution.py:271
  219.6 6.4 %collective-permute-done.33.come_ref = bf16[128,1024]{1,0:T(8,128)(2,1)S(1)} collective-permute-done((bf16[128,1024]{1,0:T(8,128)(2,1)S(1)}, bf16[128,1024]{1,0:T(8,128)(2,1)S(1)}, u32[]{:S(2)}, u32[]{:S(2)}) %collective-permute-start.33) | collective-permute-done | bytes 262176 | tf_op jit(solution)/shard_map/ppermute | solution.py:271
  226.0 4.8 %collective-permute-done.30.refs_8_ = bf16[128,768]{1,0:T(8,128)(2,1)S(1)} collective-permute-done((bf16[128,768]{1,0:T(8,128)(2,1)S(1)}, bf16[128,768]{1,0:T(8,128)(2,1)S(1)}, u32[]{:S(2)}, u32[]{:S(2)}) %collective-permute-start.30) | collective-permute-done | bytes 196640 | tf_op jit(solution)/shard_map/ppermute | solution.py:271
  233.2 3.8 %collective-permute-start.36 = (bf16[128,512]{1,0:T(8,128)(2,1)S(1)}, bf16[128,512]{1,0:T(8,128)(2,1)S(1)}, u32[]{:S(2)}, u32[]{:S(2)}) collective-permute-start(bf16[128,512]{1,0:T(8,128)(2,1)S(1)} %get-tuple-element.158), channel_id=1, source_target_pairs={{0,12},{1,13},{2,14},{3,15},{4,0},{5,1},{6,2},{7,3},{8,4},{9,5},{1... | collective-permute-start | bytes 393224 | tf_op jit(solution)/shard_map/ppermute | solution.py:271
  237.0 4.1 %collective-permute-done.37.come_ref = bf16[128,512]{1,0:T(8,128)(2,1)S(1)} collective-permute-done((bf16[128,512]{1,0:T(8,128)(2,1)S(1)}, bf16[128,512]{1,0:T(8,128)(2,1)S(1)}, u32[]{:S(2)}, u32[]{:S(2)}) %collective-permute-start.37) | collective-permute-done | bytes 131104 | tf_op jit(solution)/shard_map/ppermute | solution.py:271
  241.1 1.2 collective-permute-done.36.refs_4_
  242.3 2.0 collective-permute-start.38
  244.4 2.4 collective-permute-start.41
  246.8 1.4 collective-permute-start.42
  249.1 2.3 collective-permute-done.40.refs_7_
  251.4 1.9 collective-permute-done.41.refs_8_
  (87 shorter events, 15.9 us)
Async XLA Ops:
  0.6 65.5 %copy-start.6 = (bf16[128,2048]{1,0:T(8,128)(2,1)S(1)}, bf16[128,2048]{1,0:T(8,128)(2,1)}, u32[]{:S(2)}) copy-start(bf16[128,2048]{1,0:T(8,128)(2,1)} %refs_3_) | copy-start | bytes 1572868
  0.6 77.3 %copy-start = (bf16[2,256,2048]{2,1,0:T(8,128)(2,1)S(1)}, bf16[2,256,2048]{2,1,0:T(8,128)(2,1)}, u32[]{:S(2)}) copy-start(bf16[2,256,2048]{2,1,0:T(8,128)(2,1)} %param.13) | copy-start | bytes 6291460
  3.7 17.9 %collective-permute-start.3 = (bf16[128,2176]{1,0:T(8,128)(2,1)}, bf16[128,2176]{1,0:T(8,128)(2,1)S(1)}, u32[]{:S(2)}, u32[]{:S(2)}) collective-permute-start(bf16[128,2176]{1,0:T(8,128)(2,1)} %concatenate.3.refs_0_), channel_id=1, source_target_pairs={{0,4},{1,5},{2,6},{3,7},{4,8},{5,9},{6,10},{7,11},{8,12},{9,13},{1... | collective-permute-start | bytes 1671176 | tf_op jit(solution)/shard_map/ppermute | solution.py:271
  6.7 13.6 %collective-permute-start.6 = (bf16[128,2048]{1,0:T(8,128)(2,1)}, bf16[128,2048]{1,0:T(8,128)(2,1)S(1)}, u32[]{:S(2)}, u32[]{:S(2)}) collective-permute-start(bf16[128,2048]{1,0:T(8,128)(2,1)} %refs_3_), channel_id=1, source_target_pairs={{0,2},{1,3},{2,0},{3,1},{4,6},{5,7},{6,4},{7,5},{8,10},{9,11},{10,... | collective-permute-start | bytes 1572872 | tf_op jit(solution)/shard_map/ppermute | solution.py:271
  8.2 57.3 %collective-permute-start.8 = (bf16[2,2048,256]{2,1,0:T(8,128)(2,1)}, bf16[2,2048,256]{2,1,0:T(8,128)(2,1)}, u32[]{:S(2)}, u32[]{:S(2)}) collective-permute-start(bf16[2,2048,256]{2,1,0:T(8,128)(2,1)} %refs_0_.5), channel_id=1, source_target_pairs={{0,1},{1,0},{2,3},{3,2},{4,5},{5,4},{6,7},{7,6},{8,9},{9,8},{10,11... | collective-permute-start | bytes 6291464 | tf_op jit(solution)/shard_map/ppermute | solution.py:271
  21.6 44.0 %copy-start.9 = (bf16[128,2176]{1,0:T(8,128)(2,1)}, bf16[128,2176]{1,0:T(8,128)(2,1)S(1)}, u32[]{:S(2)}) copy-start(bf16[128,2176]{1,0:T(8,128)(2,1)S(1)} %collective-permute-done.3.refs_3_) | copy-start | bytes 1671172
  21.6 80.5 %collective-permute-start.9 = (bf16[2,2048,256]{2,1,0:T(8,128)(2,1)}, bf16[2,2048,256]{2,1,0:T(8,128)(2,1)}, u32[]{:S(2)}, u32[]{:S(2)}) collective-permute-start(bf16[2,2048,256]{2,1,0:T(8,128)(2,1)} %refs_1_.5), channel_id=1, source_target_pairs={{0,1},{1,0},{2,3},{3,2},{4,5},{5,4},{6,7},{7,6},{8,9},{9,8},{10,11... | collective-permute-start | bytes 6291464 | tf_op jit(solution)/shard_map/ppermute | solution.py:271
  23.0 13.5 %collective-permute-start = (bf16[128,2176]{1,0:T(8,128)(2,1)}, bf16[128,2176]{1,0:T(8,128)(2,1)S(1)}, u32[]{:S(2)}, u32[]{:S(2)}) collective-permute-start(bf16[128,2176]{1,0:T(8,128)(2,1)} %concatenate.3.refs_0_), channel_id=1, source_target_pairs={{0,12},{1,13},{2,14},{3,15},{4,0},{5,1},{6,2},{7,3},{8,4},{9,5},{1... | collective-permute-start | bytes 1671176 | tf_op jit(solution)/shard_map/ppermute | solution.py:271
  24.8 13.2 %collective-permute-start.1 = (bf16[128,2176]{1,0:T(8,128)(2,1)}, bf16[128,2176]{1,0:T(8,128)(2,1)S(1)}, u32[]{:S(2)}, u32[]{:S(2)}) collective-permute-start(bf16[128,2176]{1,0:T(8,128)(2,1)} %concatenate.3.refs_0_), channel_id=1, source_target_pairs={{0,2},{1,3},{2,0},{3,1},{4,6},{5,7},{6,4},{7,5},{8,10},{9,11},{10,... | collective-permute-start | bytes 1671176 | tf_op jit(solution)/shard_map/ppermute | solution.py:271
  36.5 3.0 %copy-start.10 = (bf16[128,2176]{1,0:T(8,128)(2,1)}, bf16[128,2176]{1,0:T(8,128)(2,1)S(1)}, u32[]{:S(2)}) copy-start(bf16[128,2176]{1,0:T(8,128)(2,1)S(1)} %collective-permute-done.refs_1_) | copy-start | bytes 1671172
  38.0 15.6 %copy-start.11 = (bf16[128,2176]{1,0:T(8,128)(2,1)}, bf16[128,2176]{1,0:T(8,128)(2,1)S(1)}, u32[]{:S(2)}) copy-start(bf16[128,2176]{1,0:T(8,128)(2,1)S(1)} %collective-permute-done.1.refs_4_) | copy-start | bytes 1671172
  38.0 15.6 %collective-permute-start.4 = (bf16[128,2176]{1,0:T(8,128)(2,1)S(1)}, bf16[128,2176]{1,0:T(8,128)(2,1)S(1)}, u32[]{:S(2)}, u32[]{:S(2)}) collective-permute-start(bf16[128,2176]{1,0:T(8,128)(2,1)S(1)} %collective-permute-done.refs_1_), channel_id=1, source_target_pairs={{0,2},{1,3},{2,0},{3,1},{4,6},{5,7},{6,4},{7,5},{8,10},{9,11},{10,... | collective-permute-start | bytes 1671176 | tf_op jit(solution)/shard_map/ppermute | solution.py:271
  39.6 14.0 %collective-permute-start.2 = (bf16[128,2176]{1,0:T(8,128)(2,1)S(1)}, bf16[128,2176]{1,0:T(8,128)(2,1)S(1)}, u32[]{:S(2)}, u32[]{:S(2)}) collective-permute-start(bf16[128,2176]{1,0:T(8,128)(2,1)S(1)} %collective-permute-done.refs_1_), channel_id=1, source_target_pairs={{0,12},{1,13},{2,14},{3,15},{4,0},{5,1},{6,2},{7,3},{8,4},{9,5},{1... | collective-permute-start | bytes 1671176 | tf_op jit(solution)/shard_map/ppermute | solution.py:271
  41.7 23.8 %collective-permute-start.7 = (bf16[128,2176]{1,0:T(8,128)(2,1)S(1)}, bf16[128,2176]{1,0:T(8,128)(2,1)S(1)}, u32[]{:S(2)}, u32[]{:S(2)}) collective-permute-start(bf16[128,2176]{1,0:T(8,128)(2,1)S(1)} %collective-permute-done.3.refs_3_), channel_id=1, source_target_pairs={{0,2},{1,3},{2,0},{3,1},{4,6},{5,7},{6,4},{7,5},{8,10},{9,11},{10,... | collective-permute-start | bytes 1671176 | tf_op jit(solution)/shard_map/ppermute | solution.py:271
  53.6 1.6 copy-start.12
  53.6 12.5 %copy-start.13 = (bf16[128,2176]{1,0:T(8,128)(2,1)}, bf16[128,2176]{1,0:T(8,128)(2,1)S(1)}, u32[]{:S(2)}) copy-start(bf16[128,2176]{1,0:T(8,128)(2,1)S(1)} %collective-permute-done.2.refs_2_) | copy-start | bytes 1671172
  53.6 20.5 %collective-permute-start.5 = (bf16[128,2176]{1,0:T(8,128)(2,1)S(1)}, bf16[128,2176]{1,0:T(8,128)(2,1)S(1)}, u32[]{:S(2)}, u32[]{:S(2)}) collective-permute-start(bf16[128,2176]{1,0:T(8,128)(2,1)S(1)} %collective-permute-done.2.refs_2_), channel_id=1, source_target_pairs={{0,2},{1,3},{2,0},{3,1},{4,6},{5,7},{6,4},{7,5},{8,10},{9,11},{10,... | collective-permute-start | bytes 1671176 | tf_op jit(solution)/shard_map/ppermute | solution.py:271
  55.2 14.1 %collective-permute-start.11 = (bf16[128,2048]{1,0:T(8,128)(2,1)}, bf16[128,2048]{1,0:T(8,128)(2,1)}, u32[]{:S(2)}, u32[]{:S(2)}) collective-permute-start(bf16[128,2048]{1,0:T(8,128)(2,1)} %refs_3_), channel_id=1, source_target_pairs={{0,12},{1,13},{2,14},{3,15},{4,0},{5,1},{6,2},{7,3},{8,4},{9,5},{1... | collective-permute-start | bytes 1572872 | tf_op jit(solution)/shard_map/ppermute | solution.py:271
  65.5 8.6 %copy-start.14 = (bf16[128,2176]{1,0:T(8,128)(2,1)}, bf16[128,2176]{1,0:T(8,128)(2,1)S(1)}, u32[]{:S(2)}) copy-start(bf16[128,2176]{1,0:T(8,128)(2,1)S(1)} %collective-permute-done.7.refs_7_) | copy-start | bytes 1671172
  65.6 46.4 %collective-permute-start.10 = (bf16[512,512]{1,0:T(8,128)(2,1)}, bf16[512,512]{1,0:T(8,128)(2,1)}, u32[]{:S(2)}, u32[]{:S(2)}) collective-permute-start(bf16[512,512]{1,0:T(8,128)(2,1)} %slice.12), channel_id=1, source_target_pairs={{0,1},{1,0},{2,3},{3,2},{4,5},{5,4},{6,7},{7,6},{8,9},{9,8},{10,11... | collective-permute-start | bytes 1572872 | tf_op jit(solution)/shard_map/ppermute | solution.py:271
  66.2 47.4 %collective-permute-start.13 = (bf16[128,2048]{1,0:T(8,128)(2,1)S(1)}, bf16[128,2048]{1,0:T(8,128)(2,1)}, u32[]{:S(2)}, u32[]{:S(2)}) collective-permute-start(bf16[128,2048]{1,0:T(8,128)(2,1)S(1)} %copy-done.6), channel_id=1, source_target_pairs={{0,4},{1,5},{2,6},{3,7},{4,8},{5,9},{6,10},{7,11},{8,12},{9,13},{1... | collective-permute-start | bytes 1572872 | tf_op jit(solution)/shard_map/ppermute | solution.py:271
  74.1 2.3 copy-start.15
  74.1 39.9 %collective-permute-start.15 = (bf16[128,2048]{1,0:T(8,128)(2,1)}, bf16[128,2048]{1,0:T(8,128)(2,1)}, u32[]{:S(2)}, u32[]{:S(2)}) collective-permute-start(bf16[128,2048]{1,0:T(8,128)(2,1)} %collective-permute-done.11.refs_3_.refs_4_), channel_id=1, source_target_pairs={{0,12},{1,13},{2,14},{3,15},{4,0},{5,1},{6,2},{7,3},{8,4},{9,5},{1... | collective-permute-start | bytes 1572872 | tf_op jit(solution)/shard_map/ppermute | solution.py:271
  76.5 37.6 %collective-permute-start.12 = (bf16[128,2048]{1,0:T(8,128)(2,1)}, bf16[128,2048]{1,0:T(8,128)(2,1)}, u32[]{:S(2)}, u32[]{:S(2)}) collective-permute-start(bf16[128,2048]{1,0:T(8,128)(2,1)} %collective-permute-done.11.refs_3_.refs_4_), channel_id=1, source_target_pairs={{0,2},{1,3},{2,0},{3,1},{4,6},{5,7},{6,4},{7,5},{8,10},{9,11},{10,... | collective-permute-start | bytes 1572872 | tf_op jit(solution)/shard_map/ppermute | solution.py:271
  102.0 34.3 %copy-start.3 = (bf16[1024,512]{1,0:T(8,128)(2,1)S(1)}, bf16[1024,512]{1,0:T(8,128)(2,1)}, u32[]{:S(2)}) copy-start(bf16[1024,512]{1,0:T(8,128)(2,1)} %get-tuple-element.94.own_ref) | copy-start | bytes 3145732
  112.0 33.8 %collective-permute-start.17 = (bf16[512,768]{1,0:T(8,128)(2,1)S(1)}, bf16[512,768]{1,0:T(8,128)(2,1)S(1)}, u32[]{:S(2)}, u32[]{:S(2)}) collective-permute-start(bf16[512,768]{1,0:T(8,128)(2,1)S(1)} %get-tuple-element.107), channel_id=1, source_target_pairs={{0,1},{1,0},{2,3},{3,2},{4,5},{5,4},{6,7},{7,6},{8,9},{9,8},{10,11... | collective-permute-start | bytes 2359304 | tf_op jit(solution)/shard_map/ppermute | solution.py:271
  113.5 15.1 %collective-permute-start.14 = (bf16[128,2048]{1,0:T(8,128)(2,1)}, bf16[128,2048]{1,0:T(8,128)(2,1)S(1)}, u32[]{:S(2)}, u32[]{:S(2)}) collective-permute-start(bf16[128,2048]{1,0:T(8,128)(2,1)} %collective-permute-done.13.refs_5_.refs_6_), channel_id=1, source_target_pairs={{0,2},{1,3},{2,0},{3,1},{4,6},{5,7},{6,4},{7,5},{8,10},{9,11},{10,... | collective-permute-start | bytes 1572872 | tf_op jit(solution)/shard_map/ppermute | solution.py:271
  114.1 22.3 %collective-permute-start.16 = (bf16[128,2048]{1,0:T(8,128)(2,1)}, bf16[128,2048]{1,0:T(8,128)(2,1)S(1)}, u32[]{:S(2)}, u32[]{:S(2)}) collective-permute-start(bf16[128,2048]{1,0:T(8,128)(2,1)} %collective-permute-done.15.refs_4_.refs_5_), channel_id=1, source_target_pairs={{0,2},{1,3},{2,0},{3,1},{4,6},{5,7},{6,4},{7,5},{8,10},{9,11},{10,... | collective-permute-start | bytes 1572872 | tf_op jit(solution)/shard_map/ppermute | solution.py:271
  136.4 1.2 copy-start.4
  137.6 3.9 %copy-start.8 = (f32[1024,1024]{1,0:T(8,128)S(1)}, f32[1024,1024]{1,0:T(8,128)}, u32[]{:S(2)}) copy-start(f32[1024,1024]{1,0:T(8,128)} %get-tuple-element.109.refs_0_) | copy-start | bytes 12582916
  140.4 14.6 %collective-permute-start.18 = (bf16[512,512]{1,0:T(8,128)(2,1)S(1)}, bf16[512,512]{1,0:T(8,128)(2,1)S(1)}, u32[]{:S(2)}, u32[]{:S(2)}) collective-permute-start(bf16[512,512]{1,0:T(8,128)(2,1)S(1)} %get-tuple-element.113), channel_id=1, source_target_pairs={{0,2},{1,3},{2,0},{3,1},{4,6},{5,7},{6,4},{7,5},{8,10},{9,11},{10,... | collective-permute-start | bytes 1572872 | tf_op jit(solution)/shard_map/ppermute | solution.py:271
  141.0 27.3 %collective-permute-start.22 = (bf16[512,768]{1,0:T(8,128)(2,1)}, bf16[512,768]{1,0:T(8,128)(2,1)S(1)}, u32[]{:S(2)}, u32[]{:S(2)}) collective-permute-start(bf16[512,768]{1,0:T(8,128)(2,1)} %get-tuple-element.121), channel_id=1, source_target_pairs={{0,1},{1,0},{2,3},{3,2},{4,5},{5,4},{6,7},{7,6},{8,9},{9,8},{10,11... | collective-permute-start | bytes 2359304 | tf_op jit(solution)/shard_map/ppermute | solution.py:271
  141.5 4.3 %copy-start.5 = (bf16[1024,512]{1,0:T(8,128)(2,1)S(1)}, bf16[1024,512]{1,0:T(8,128)(2,1)}, u32[]{:S(2)}) copy-start(bf16[1024,512]{1,0:T(8,128)(2,1)} %get-tuple-element.98.other_ref) | copy-start | bytes 3145732
  148.0 33.9 %collective-permute-start.23 = (bf16[512,768]{1,0:T(8,128)(2,1)S(1)}, bf16[512,768]{1,0:T(8,128)(2,1)S(1)}, u32[]{:S(2)}, u32[]{:S(2)}) collective-permute-start(bf16[512,768]{1,0:T(8,128)(2,1)S(1)} %get-tuple-element.111), channel_id=1, source_target_pairs={{0,2},{1,3},{2,0},{3,1},{4,6},{5,7},{6,4},{7,5},{8,10},{9,11},{10,... | collective-permute-start | bytes 2359304 | tf_op jit(solution)/shard_map/ppermute | solution.py:271
  155.1 7.0 %collective-permute-start.20 = (bf16[128,512]{1,0:T(8,128)(2,1)S(1)}, bf16[128,512]{1,0:T(8,128)(2,1)S(1)}, u32[]{:S(2)}, u32[]{:S(2)}) collective-permute-start(bf16[128,512]{1,0:T(8,128)(2,1)S(1)} %get-tuple-element.117), channel_id=1, source_target_pairs={{0,4},{1,5},{2,6},{3,7},{4,8},{5,9},{6,10},{7,11},{8,12},{9,13},{1... | collective-permute-start | bytes 393224 | tf_op jit(solution)/shard_map/ppermute | solution.py:271
  156.7 6.4 %collective-permute-start.19 = (bf16[128,512]{1,0:T(8,128)(2,1)S(1)}, bf16[128,512]{1,0:T(8,128)(2,1)S(1)}, u32[]{:S(2)}, u32[]{:S(2)}) collective-permute-start(bf16[128,512]{1,0:T(8,128)(2,1)S(1)} %get-tuple-element.115), channel_id=1, source_target_pairs={{0,12},{1,13},{2,14},{3,15},{4,0},{5,1},{6,2},{7,3},{8,4},{9,5},{1... | collective-permute-start | bytes 393224 | tf_op jit(solution)/shard_map/ppermute | solution.py:271
  163.1 6.8 %collective-permute-start.21 = (bf16[128,512]{1,0:T(8,128)(2,1)S(1)}, bf16[128,512]{1,0:T(8,128)(2,1)S(1)}, u32[]{:S(2)}, u32[]{:S(2)}) collective-permute-start(bf16[128,512]{1,0:T(8,128)(2,1)S(1)} %add_piece.5), channel_id=1, source_target_pairs={{0,4},{1,5},{2,6},{3,7},{4,8},{5,9},{6,10},{7,11},{8,12},{9,13},{1... | collective-permute-start | bytes 393224 | tf_op jit(solution)/shard_map/ppermute | solution.py:271
  168.2 3.9 %copy-start.7 = (f32[1024,1024]{1,0:T(8,128)S(1)}, f32[1024,1024]{1,0:T(8,128)}, u32[]{:S(2)}) copy-start(f32[1024,1024]{1,0:T(8,128)} %get-tuple-element.125.refs_0_) | copy-start | bytes 12582916
  172.1 21.3 %collective-permute-start.27 = (bf16[512,768]{1,0:T(8,128)(2,1)S(1)}, bf16[512,768]{1,0:T(8,128)(2,1)S(1)}, u32[]{:S(2)}, u32[]{:S(2)}) collective-permute-start(bf16[512,768]{1,0:T(8,128)(2,1)S(1)} %get-tuple-element.134), channel_id=1, source_target_pairs={{0,2},{1,3},{2,0},{3,1},{4,6},{5,7},{6,4},{7,5},{8,10},{9,11},{10,... | collective-permute-start | bytes 2359304 | tf_op jit(solution)/shard_map/ppermute | solution.py:271
  172.1 3.1 %copy-start.1 = (bf16[2,2048,256]{2,1,0:T(8,128)(2,1)S(1)}, bf16[2,2048,256]{2,1,0:T(8,128)(2,1)}, u32[]{:S(2)}) copy-start(bf16[2,2048,256]{2,1,0:T(8,128)(2,1)} %refs_0_.5) | copy-start | bytes 6291460
  172.2 3.1 %copy-start.2 = (bf16[2,2048,256]{2,1,0:T(8,128)(2,1)S(1)}, bf16[2,2048,256]{2,1,0:T(8,128)(2,1)}, u32[]{:S(2)}) copy-start(bf16[2,2048,256]{2,1,0:T(8,128)(2,1)} %refs_1_.5) | copy-start | bytes 6291460
  182.1 33.0 %collective-permute-start.31 = (bf16[512,1024]{1,0:T(8,128)(2,1)S(1)}, bf16[512,1024]{1,0:T(8,128)(2,1)S(1)}, u32[]{:S(2)}, u32[]{:S(2)}) collective-permute-start(bf16[512,1024]{1,0:T(8,128)(2,1)S(1)} %get-tuple-element.145), channel_id=1, source_target_pairs={{0,2},{1,3},{2,0},{3,1},{4,6},{5,7},{6,4},{7,5},{8,10},{9,11},{10,... | collective-permute-start | bytes 3145736 | tf_op jit(solution)/shard_map/ppermute | solution.py:271
  184.1 7.6 %collective-permute-start.25 = (bf16[128,768]{1,0:T(8,128)(2,1)S(1)}, bf16[128,768]{1,0:T(8,128)(2,1)S(1)}, u32[]{:S(2)}, u32[]{:S(2)}) collective-permute-start(bf16[128,768]{1,0:T(8,128)(2,1)S(1)} %get-tuple-element.131), channel_id=1, source_target_pairs={{0,4},{1,5},{2,6},{3,7},{4,8},{5,9},{6,10},{7,11},{8,12},{9,13},{1... | collective-permute-start | bytes 589832 | tf_op jit(solution)/shard_map/ppermute | solution.py:271
  184.1 8.5 %collective-permute-start.24 = (bf16[128,768]{1,0:T(8,128)(2,1)S(1)}, bf16[128,768]{1,0:T(8,128)(2,1)S(1)}, u32[]{:S(2)}, u32[]{:S(2)}) collective-permute-start(bf16[128,768]{1,0:T(8,128)(2,1)S(1)} %get-tuple-element.129), channel_id=1, source_target_pairs={{0,12},{1,13},{2,14},{3,15},{4,0},{5,1},{6,2},{7,3},{8,4},{9,5},{1... | collective-permute-start | bytes 589832 | tf_op jit(solution)/shard_map/ppermute | solution.py:271
  192.6 7.9 %collective-permute-start.26 = (bf16[128,768]{1,0:T(8,128)(2,1)S(1)}, bf16[128,768]{1,0:T(8,128)(2,1)S(1)}, u32[]{:S(2)}, u32[]{:S(2)}) collective-permute-start(bf16[128,768]{1,0:T(8,128)(2,1)S(1)} %add_piece.6), channel_id=1, source_target_pairs={{0,4},{1,5},{2,6},{3,7},{4,8},{5,9},{6,10},{7,11},{8,12},{9,13},{1... | collective-permute-start | bytes 589832 | tf_op jit(solution)/shard_map/ppermute | solution.py:271
  193.5 9.1 %collective-permute-start.29 = (bf16[128,768]{1,0:T(8,128)(2,1)S(1)}, bf16[128,768]{1,0:T(8,128)(2,1)S(1)}, u32[]{:S(2)}, u32[]{:S(2)}) collective-permute-start(bf16[128,768]{1,0:T(8,128)(2,1)S(1)} %get-tuple-element.139), channel_id=1, source_target_pairs={{0,4},{1,5},{2,6},{3,7},{4,8},{5,9},{6,10},{7,11},{8,12},{9,13},{1... | collective-permute-start | bytes 589832 | tf_op jit(solution)/shard_map/ppermute | solution.py:271
  206.6 26.4 %collective-permute-start.35 = (bf16[512,512]{1,0:T(8,128)(2,1)S(1)}, bf16[512,512]{1,0:T(8,128)(2,1)S(1)}, u32[]{:S(2)}, u32[]{:S(2)}) collective-permute-start(bf16[512,512]{1,0:T(8,128)(2,1)S(1)} %get-tuple-element.155), channel_id=1, source_target_pairs={{0,2},{1,3},{2,0},{3,1},{4,6},{5,7},{6,4},{7,5},{8,10},{9,11},{10,... | collective-permute-start | bytes 1572872 | tf_op jit(solution)/shard_map/ppermute | solution.py:271
  207.8 11.8 %collective-permute-start.28 = (bf16[128,768]{1,0:T(8,128)(2,1)S(1)}, bf16[128,768]{1,0:T(8,128)(2,1)S(1)}, u32[]{:S(2)}, u32[]{:S(2)}) collective-permute-start(bf16[128,768]{1,0:T(8,128)(2,1)S(1)} %get-tuple-element.137), channel_id=1, source_target_pairs={{0,12},{1,13},{2,14},{3,15},{4,0},{5,1},{6,2},{7,3},{8,4},{9,5},{1... | collective-permute-start | bytes 589832 | tf_op jit(solution)/shard_map/ppermute | solution.py:271
  215.3 10.7 %collective-permute-start.33 = (bf16[128,1024]{1,0:T(8,128)(2,1)S(1)}, bf16[128,1024]{1,0:T(8,128)(2,1)S(1)}, u32[]{:S(2)}, u32[]{:S(2)}) collective-permute-start(bf16[128,1024]{1,0:T(8,128)(2,1)S(1)} %get-tuple-element.149), channel_id=1, source_target_pairs={{0,4},{1,5},{2,6},{3,7},{4,8},{5,9},{6,10},{7,11},{8,12},{9,13},{1... | collective-permute-start | bytes 786440 | tf_op jit(solution)/shard_map/ppermute | solution.py:271
  215.3 28.9 %collective-permute-start.39 = (bf16[512,512]{1,0:T(8,128)(2,1)S(1)}, bf16[512,512]{1,0:T(8,128)(2,1)S(1)}, u32[]{:S(2)}, u32[]{:S(2)}) collective-permute-start(bf16[512,512]{1,0:T(8,128)(2,1)S(1)} %get-tuple-element.163), channel_id=1, source_target_pairs={{0,2},{1,3},{2,0},{3,1},{4,6},{5,7},{6,4},{7,5},{8,10},{9,11},{10,... | collective-permute-start | bytes 1572872 | tf_op jit(solution)/shard_map/ppermute | solution.py:271
  215.7 15.1 %collective-permute-start.32 = (bf16[128,1024]{1,0:T(8,128)(2,1)S(1)}, bf16[128,1024]{1,0:T(8,128)(2,1)S(1)}, u32[]{:S(2)}, u32[]{:S(2)}) collective-permute-start(bf16[128,1024]{1,0:T(8,128)(2,1)S(1)} %get-tuple-element.147), channel_id=1, source_target_pairs={{0,12},{1,13},{2,14},{3,15},{4,0},{5,1},{6,2},{7,3},{8,4},{9,5},{1... | collective-permute-start | bytes 786440 | tf_op jit(solution)/shard_map/ppermute | solution.py:271
  219.5 11.3 %collective-permute-start.30 = (bf16[128,768]{1,0:T(8,128)(2,1)S(1)}, bf16[128,768]{1,0:T(8,128)(2,1)S(1)}, u32[]{:S(2)}, u32[]{:S(2)}) collective-permute-start(bf16[128,768]{1,0:T(8,128)(2,1)S(1)} %add_piece.7), channel_id=1, source_target_pairs={{0,4},{1,5},{2,6},{3,7},{4,8},{5,9},{6,10},{7,11},{8,12},{9,13},{1... | collective-permute-start | bytes 589832 | tf_op jit(solution)/shard_map/ppermute | solution.py:271
  230.8 13.5 %collective-permute-start.34 = (bf16[128,1024]{1,0:T(8,128)(2,1)S(1)}, bf16[128,1024]{1,0:T(8,128)(2,1)S(1)}, u32[]{:S(2)}, u32[]{:S(2)}) collective-permute-start(bf16[128,1024]{1,0:T(8,128)(2,1)S(1)} %add_piece.8), channel_id=1, source_target_pairs={{0,4},{1,5},{2,6},{3,7},{4,8},{5,9},{6,10},{7,11},{8,12},{9,13},{1... | collective-permute-start | bytes 786440 | tf_op jit(solution)/shard_map/ppermute | solution.py:271
  233.1 8.0 %collective-permute-start.37 = (bf16[128,512]{1,0:T(8,128)(2,1)S(1)}, bf16[128,512]{1,0:T(8,128)(2,1)S(1)}, u32[]{:S(2)}, u32[]{:S(2)}) collective-permute-start(bf16[128,512]{1,0:T(8,128)(2,1)S(1)} %get-tuple-element.160), channel_id=1, source_target_pairs={{0,4},{1,5},{2,6},{3,7},{4,8},{5,9},{6,10},{7,11},{8,12},{9,13},{1... | collective-permute-start | bytes 393224 | tf_op jit(solution)/shard_map/ppermute | solution.py:271
  233.2 9.1 %collective-permute-start.36 = (bf16[128,512]{1,0:T(8,128)(2,1)S(1)}, bf16[128,512]{1,0:T(8,128)(2,1)S(1)}, u32[]{:S(2)}, u32[]{:S(2)}) collective-permute-start(bf16[128,512]{1,0:T(8,128)(2,1)S(1)} %get-tuple-element.158), channel_id=1, source_target_pairs={{0,12},{1,13},{2,14},{3,15},{4,0},{5,1},{6,2},{7,3},{8,4},{9,5},{1... | collective-permute-start | bytes 393224 | tf_op jit(solution)/shard_map/ppermute | solution.py:271
  242.3 6.8 %collective-permute-start.38 = (bf16[128,512]{1,0:T(8,128)(2,1)S(1)}, bf16[128,512]{1,0:T(8,128)(2,1)S(1)}, u32[]{:S(2)}, u32[]{:S(2)}) collective-permute-start(bf16[128,512]{1,0:T(8,128)(2,1)S(1)} %add_piece.9), channel_id=1, source_target_pairs={{0,4},{1,5},{2,6},{3,7},{4,8},{5,9},{6,10},{7,11},{8,12},{9,13},{1... | collective-permute-start | bytes 393224 | tf_op jit(solution)/shard_map/ppermute | solution.py:271
  244.4 7.0 %collective-permute-start.40 = (bf16[128,512]{1,0:T(8,128)(2,1)S(1)}, bf16[128,512]{1,0:T(8,128)(2,1)S(1)}, u32[]{:S(2)}, u32[]{:S(2)}) collective-permute-start(bf16[128,512]{1,0:T(8,128)(2,1)S(1)} %get-tuple-element.169), channel_id=1, source_target_pairs={{0,4},{1,5},{2,6},{3,7},{4,8},{5,9},{6,10},{7,11},{8,12},{9,13},{1... | collective-permute-start | bytes 393224 | tf_op jit(solution)/shard_map/ppermute | solution.py:271
  244.4 8.8 %collective-permute-start.41 = (bf16[128,512]{1,0:T(8,128)(2,1)S(1)}, bf16[128,512]{1,0:T(8,128)(2,1)S(1)}, u32[]{:S(2)}, u32[]{:S(2)}) collective-permute-start(bf16[128,512]{1,0:T(8,128)(2,1)S(1)} %get-tuple-element.170), channel_id=1, source_target_pairs={{0,8},{1,9},{2,10},{3,11},{4,12},{5,13},{6,14},{7,15},{8,0},{9,1},... | collective-permute-start | bytes 393224 | tf_op jit(solution)/shard_map/ppermute | solution.py:271
  246.8 6.4 %collective-permute-start.42 = (bf16[128,512]{1,0:T(8,128)(2,1)S(1)}, bf16[128,512]{1,0:T(8,128)(2,1)S(1)}, u32[]{:S(2)}, u32[]{:S(2)}) collective-permute-start(bf16[128,512]{1,0:T(8,128)(2,1)S(1)} %get-tuple-element.171), channel_id=1, source_target_pairs={{0,12},{1,13},{2,14},{3,15},{4,0},{5,1},{6,2},{7,3},{8,4},{9,5},{1... | collective-permute-start | bytes 393224 | tf_op jit(solution)/shard_map/ppermute | solution.py:271
